TPU v7x, 32 devices: a whole 2x2x4 slice. The times are simulated.
32 devices in a mesh: groups: 2 (over y), space: 4 (over x, core), tm: 4 (over z).
Axes of the slice: x: 2, y: 2, z: 4, core: 2. Of those that a mesh axis runs over, the one named last changes fastest.
Arguments:
- couplings: float32 [9, 4, 4, 2, 4, 96, 192], P(None, 'tm', 'space'), may hold values from -0.15625 to 0.15625
- source: float32 [4, 4, 2, 4, 96, 256], P('tm', 'space'), may hold values from -6 to 6
- initial: float32 [4, 4, 2, 4, 96, 256], P('tm', 'space'), may hold values from -6 to 6
- vectors: float32 [512, 4, 4, 2, 4, 192], P(None, 'tm', 'space'), may hold values from -0.0390625 to 0.0390625
- inverse_eigen: float32 [2, 512], replicated, may hold values from -20 to 20
Outputs:
- solution: float32 [8, 4, 2, 4, 96, 256], P(('groups', 'tm'), 'space'), parts along dimension 0
- residual: float32 [8, 4, 2, 4, 96, 256], P(('groups', 'tm'), 'space'), parts along dimension 0
There are 2 independent parts, one for each index of `groups`. A program takes and returns all parts, laid end to end along the dimension named above; an argument that names none is the same for every part. Nothing has to cross between parts.
All inputs are finite; a program needn't handle non-finite values.
Results may differ from a plain program's by a relative error of at most 0.0001.
Values sent between devices are 32-bit elements; how exact they have to be, the bound alone decides.
No kernel may reach another device: no remote copies, remote signals or barrier semaphores. Data moves between devices by JAX's collectives and lax.ppermute only.
A program may use at most 64 MiB of HBM per device.

v0:
```python
import jax
import jax.numpy as jnp
from jax import lax
from jax.sharding import PartitionSpec as P

ITERS = 2


def with_halo(block, sides, width):
    for axis, dim in sides:
        count = lax.axis_size(axis)
        forward = [(i, i + 1) for i in range(count - 1)]
        forward.append((count - 1, 0))
        backward = [(target, source) for source, target in forward]
        low = lax.ppermute(
            lax.slice_in_dim(block, block.shape[dim] - width, None, axis=dim), axis, forward
        )
        high = lax.ppermute(lax.slice_in_dim(block, 0, width, axis=dim), axis, backward)
        block = jnp.concatenate([low, block, high], axis=dim)
    return block


def coupled(matrix, spinor):
    middle = spinor.shape[-1] // 2
    turned = jnp.concatenate([-spinor[..., middle:], spinor[..., :middle]], axis=-1)
    stacked = jnp.concatenate([spinor, turned], axis=-2)
    return jnp.einsum("tzyxij,tzyxjn->tzyxin", matrix, stacked, precision=lax.Precision.HIGHEST)


def layer_faces(spinor):
    time_padded = with_halo(spinor, (("tm", 0),), 1)
    space_padded = with_halo(spinor, (("space", 1),), 1)
    forward_t = time_padded[2:]
    backward_t = time_padded[:-2]
    forward_z = space_padded[:, 2:]
    backward_z = space_padded[:, :-2]
    return (forward_t, backward_t, forward_z, backward_z)


def apply_operator(spinor, couplings):
    forward_t, backward_t, forward_z, backward_z = layer_faces(spinor)
    at_last = lax.axis_index("tm") == lax.axis_size("tm") - 1
    at_first = lax.axis_index("tm") == 0
    sign_upper = jnp.where(at_last, -1.0, 1.0).astype(jnp.float32)
    sign_lower = jnp.where(at_first, -1.0, 1.0).astype(jnp.float32)
    forward_t = forward_t.at[-1].multiply(sign_upper)
    backward_t = backward_t.at[0].multiply(sign_lower)
    neighbours = [
        spinor,
        jnp.roll(spinor, -1, 3),
        jnp.roll(spinor, 1, 3),
        jnp.roll(spinor, -1, 2),
        jnp.roll(spinor, 1, 2),
        forward_z,
        backward_z,
        forward_t,
        backward_t,
    ]
    summed = jnp.zeros_like(spinor)
    for direction in range(9):
        summed = summed + coupled(couplings[direction], neighbours[direction])
    return summed


def scale_coeffs(coefficients, eigen_part):
    middle = coefficients.shape[-1] // 2
    eigen_real = eigen_part[0][:, None]
    eigen_imag = eigen_part[1][:, None]
    coef_real = coefficients[:, :middle]
    coef_imag = coefficients[:, middle:]
    scaled_real = eigen_real * coef_real - eigen_imag * coef_imag
    scaled_imag = eigen_real * coef_imag + eigen_imag * coef_real
    return jnp.concatenate([scaled_real, scaled_imag], axis=-1)


def deflate(residual, vectors, inverse_eigen):
    middle = residual.shape[-1] // 2
    number = vectors.shape[0]
    negated = jnp.concatenate([residual[..., middle:], -residual[..., :middle]], axis=-1)
    stacked = jnp.concatenate([residual, negated], axis=-2)
    partial_value = jnp.dot(
        vectors.reshape(number, -1),
        stacked.reshape(-1, stacked.shape[-1]),
        precision=lax.Precision.HIGHEST,
        preferred_element_type=jnp.float32,
    )
    over_time = lax.psum(partial_value, "tm")
    owned = lax.psum_scatter(over_time, "space", scatter_dimension=0, tiled=True)
    owned_rows = owned.shape[0]
    offset = lax.axis_index("space") * owned_rows
    eigen_part = lax.dynamic_slice_in_dim(inverse_eigen, offset, owned_rows, 1)
    scaled = lax.all_gather(scale_coeffs(owned, eigen_part), "space", axis=0, tiled=True)
    dstack = jnp.stack(
        [scaled, jnp.concatenate([-scaled[:, middle:], scaled[:, :middle]], axis=-1)]
    )
    halves = vectors.reshape(vectors.shape[:-1] + (2, vectors.shape[-1] // 2))
    return jnp.einsum("ktzyxci,ckn->tzyxin", halves, dstack, precision=lax.Precision.HIGHEST)


def shards(couplings, source, initial, vectors, inverse_eigen):
    iterate = initial
    residual = source
    for sweep in range(ITERS):
        residual = source - apply_operator(iterate, couplings)
        iterate = iterate + deflate(residual, vectors, inverse_eigen) + 0.5 * residual
    return (iterate, residual)


def solution(mesh):
    in_specs = (
        P(None, "tm", "space", None, None, None, None),
        P("tm", "space", None, None, None, None),
        P("tm", "space", None, None, None, None),
        P(None, "tm", "space", None, None, None),
        P(),
    )
    out_specs = (
        P(("groups", "tm"), "space", None, None, None, None),
        P(("groups", "tm"), "space", None, None, None, None),
    )
    return jax.shard_map(shards, mesh=mesh, in_specs=in_specs, out_specs=out_specs, check_vma=False)
```

profile of v0, /device:TPU:0, one launch (start us, length us, event | category | flops | bytes accessed | tf_op | source)
XLA Modules:
  0.0 262.6 jit_solution(13960371233287765386)
XLA Ops:
  7.2 5.1 %collective-permute-start.2 = (f32[1,1,2,4,96,256]{5,4,3,2,1,0:T(8,128)}, f32[1,1,2,4,96,256]{5,4,3,2,1,0:T(8,128)}, u32[]{:S(2)}, u32[]{:S(2)}) collective-permute-start(f32[1,1,2,4,96,256]{5,4,3,2,1,0:T(8,128)} %param.15), channel_id=1, source_target_pairs={{1,0},{2,1},{3,2},{0,3},{5,4},{6,5},{7,6},{4,7},{9,8},{10,9},{11,1... | collective-permute-start | bytes 2359304 | tf_op jit(solution)/shard_map/ppermute | solution.py:18
  12.3 1.7 collective-permute-start
  14.1 1.2 fusion.237
  15.3 3.0 %fusion.152 = f32[2,4,256,96]{2,3,1,0:T(8,128)} fusion(f32[1,1,1,4,96,256]{5,4,3,2,1,0:T(8,128)S(1)} %get-tuple-element.79, f32[1,1,1,4,96,256]{5,4,3,2,1,0:T(8,128)S(1)} %get-tuple-element.78, f32[1,1,2,4,96,128]{5,4,3,2,1,0:T(8,128)S(1)} %fusion.203, f32[9,1,1,2,4,96,192]{6,5,4,3,2,1,0:T(8,128)} %param.13), kind=kOutput, calls=%fused_computation.154 | convolution fusion | flops 454557696 | bytes 2752512 | tf_op jit(solution)/shard_map/tzyxij,tzyxjn->tzyxin/dot_general | solution.py:27
  18.3 3.1 %fusion.154 = f32[2,4,256,96]{2,3,1,0:T(8,128)} fusion(f32[1,1,1,4,96,256]{5,4,3,2,1,0:T(8,128)S(1)} %get-tuple-element.79, f32[1,1,1,4,96,256]{5,4,3,2,1,0:T(8,128)S(1)} %get-tuple-element.78, f32[1,1,2,4,96,128]{5,4,3,2,1,0:T(8,128)S(1)} %fusion.203, f32[9,1,1,2,4,96,192]{6,5,4,3,2,1,0:T(8,128)} %param.13), kind=kOutput, calls=%fused_computation.155 | convolution fusion | flops 454557696 | bytes 2752512 | tf_op jit(solution)/shard_map/tzyxij,tzyxjn->tzyxin/dot_general | solution.py:27
  21.4 0.9 fusion.236
  22.4 3.0 %fusion.31 = f32[2,4,256,96]{2,3,1,0:T(8,128)} fusion(f32[1,1,2,1,96,256]{5,4,3,2,1,0:T(8,128)S(1)} %get-tuple-element.73, f32[1,1,2,3,96,256]{5,4,3,2,1,0:T(8,128)S(1)} %get-tuple-element.75, f32[1,1,2,4,96,128]{5,4,3,2,1,0:T(8,128)S(1)} %fusion.207, f32[9,1,1,2,4,96,192]{6,5,4,3,2,1,0:T(8,128)} %param.13), kind=kOutput, calls=%fused_computation.34 | convolution fusion | flops 454557696 | bytes 2752512 | tf_op jit(solution)/shard_map/tzyxij,tzyxjn->tzyxin/dot_general | solution.py:27
  25.4 1.0 slice_negate_fusion.11
  26.4 1.1 fusion.205
  27.6 2.9 %fusion.111 = f32[2,4,256,96]{2,3,1,0:T(8,128)S(1)} fusion(f32[2,4,256,96]{2,3,1,0:T(8,128)} %fusion.31, f32[1,1,2,4,96,128]{5,4,3,2,1,0:T(8,128)} %get-tuple-element.77, f32[1,1,2,4,96,128]{5,4,3,2,1,0:T(8,128)} %get-tuple-element.76, f32[1,1,2,4,96,256]{5,4,3,2,1,0:T(8,128)S(1)} %copy-done.2, f32[9,1,1,2,4,96,192]{6,5,4,3,2,1,0:T(8,128)} %param.13), kind=kOutput, calls=%fused_computation.125 | convolution fusion | flops 453967872 | bytes 3932160 | tf_op jit(solution)/shard_map/tzyxij,tzyxjn->tzyxin/dot_general | solution.py:27
  30.5 2.2 fusion.127
  32.8 1.2 broadcast_multiply_fusion.3
  34.0 13.2 %collective-permute-done.3 = f32[1,1,2,4,96,256]{5,4,3,2,1,0:T(8,128)} collective-permute-done((f32[1,1,2,4,96,256]{5,4,3,2,1,0:T(8,128)}, f32[1,1,2,4,96,256]{5,4,3,2,1,0:T(8,128)}, u32[]{:S(2)}, u32[]{:S(2)}) %collective-permute-start.3) | collective-permute-done | bytes 786464 | tf_op jit(solution)/shard_map/ppermute | solution.py:15
  47.2 1.2 broadcast_multiply_fusion.1
  48.5 1.2 slice_negate_fusion.9
  49.7 2.2 fusion.57
  51.9 2.2 fusion.62
  54.1 1.2 slice_negate_fusion.10
  55.3 2.5 fusion.52
  57.9 2.7 %fusion.139 = f32[1,1,2,4,96,256]{5,4,3,2,1,0:T(8,128)S(1)} fusion(f32[1,1,2,4,96,256]{5,4,3,2,1,0:T(8,128)S(1)} %copy-done.10, f32[2,4,256,96]{2,3,1,0:T(8,128)S(1)} %fusion.62, f32[2,4,256,96]{2,3,1,0:T(8,128)S(1)} %fusion.57, f32[2,4,256,96]{2,3,1,0:T(8,128)S(1)} %fusion.52, f32[2,4,256,96]{2,3,1,0:T(8,128)S(1)} %fusion.127, ...), kind=kOutput, calls=%fused_computation.143 | convolution fusion | flops 454754304 | bytes 7077888 | tf_op jit(solution)/shard_map/tzyxij,tzyxjn->tzyxin/dot_general | solution.py:27
  60.6 0.8 copy-done.4
  61.4 4.0 %fusion.142 = f32[512,256]{0,1:T(8,128)} fusion(f32[512,1,1,2,4,192]{0,5,4,3,2,1:T(8,128)S(1)} %copy-done, f32[1,1,2,4,96,128]{5,4,3,2,1,0:T(8,128)S(1)} %get-tuple-element.69, f32[1,1,2,4,96,128]{5,4,3,2,1,0:T(8,128)S(1)} %get-tuple-element.68, f32[1,1,2,4,96,256]{5,4,3,2,1,0:T(8,128)S(1)} %fusion.139), kind=kOutput, calls=%fused_computation.146 | convolution fusion | flops 2416705536 | bytes 5242880 | tf_op jit(solution)/shard_map/dot_general | solution.py:81
  65.5 0.7 constant_dynamic-slice_fusion
  66.2 20.5 %reduce-scatter.3.cloned.1.call-done = f32[128,256]{0,1:T(8,128)} async-done(((f32[512,256]{0,1:T(8,128)}), f32[128,256]{0,1:T(8,128)}) %reduce-scatter.3.cloned.1.call-update) | async-done | bytes 131088 | tf_op jit(solution)/shard_map/reduce_scatter | solution.py:88
  86.7 36.8 %all-reduce.3.cloned.1.call-done = f32[128,256]{0,1:T(8,128)} async-done(((f32[128,256]{0,1:T(8,128)}), f32[128,256]{0,1:T(8,128)}) %all-reduce.3.cloned.1.call-update) | async-done | bytes 131088 | tf_op jit(solution)/shard_map/psum | solution.py:87
  123.5 0.9 multiply_subtract_fusion.1
  124.4 7.2 %all_gather.6 = f32[512,256]{0,1:T(8,128)S(1)} all-gather(f32[128,256]{0,1:T(8,128)S(1)} %pad_maximum_fusion.6), channel_id=1, replica_groups=mesh['groups'=2,'space'=4,'tm'=4] {'space'}, dimensions={0}, use_global_device_ids=true | all-gather | bytes 655360 | tf_op jit(solution)/shard_map/all_gather | solution.py:92
  131.8 3.6 %multiply_add_fusion.1 = (f32[1,1,2,4,96,256]{5,4,3,2,1,0:T(8,128)S(1)}, f32[1,1,2,4,96,256]{5,4,3,2,1,0:T(8,128)}) fusion(f32[1,1,2,4,96,256]{5,4,3,2,1,0:T(8,128)S(1)} %copy-done.5, f32[1,1,2,4,96,256]{5,4,3,2,1,0:T(8,128)S(1)} %copy-done.3, f32[512,2,4,2,96]{0,4,3,2,1:T(8,128)S(1)} %bitcast.221, f32[1,512,256]{1,2,0:T(8,128)S(1)} %maximum_bitcast_fusion.62, ...), kind=kOutput, calls=%fused_computation.189 | convolution fusion | flops 2416771072 | bytes 7340032 | tf_op jit(solution)/shard_map/ktzyxci,ckn->tzyxin/dot_general | solution.py:97
  135.7 1.0 fusion.158
  136.7 1.0 fusion.156
  138.2 2.1 collective-permute-start.6
  140.3 1.1 collective-permute-start.4
  141.4 1.0 fusion.16
  142.5 1.1 fusion.109
  143.6 1.1 fusion.121
  144.7 13.5 %collective-permute-done.6 = f32[1,1,2,4,96,256]{5,4,3,2,1,0:T(8,128)S(1)} collective-permute-done((f32[1,1,2,4,96,256]{5,4,3,2,1,0:T(8,128)S(1)}, f32[1,1,2,4,96,256]{5,4,3,2,1,0:T(8,128)S(1)}, u32[]{:S(2)}, u32[]{:S(2)}) %collective-permute-start.6) | collective-permute-done | bytes 786464 | tf_op jit(solution)/shard_map/ppermute | solution.py:18
  158.4 18.3 %collective-permute-done.7 = f32[1,1,2,4,96,256]{5,4,3,2,1,0:T(8,128)S(1)} collective-permute-done((f32[1,1,2,4,96,256]{5,4,3,2,1,0:T(8,128)S(1)}, f32[1,1,2,4,96,256]{5,4,3,2,1,0:T(8,128)S(1)}, u32[]{:S(2)}, u32[]{:S(2)}) %collective-permute-start.7) | collective-permute-done | bytes 786464 | tf_op jit(solution)/shard_map/ppermute | solution.py:15
  176.8 1.1 fusion.94
  178.0 1.1 fusion.99
  179.2 1.1 fusion.89
  180.3 1.3 fusion.138
  181.7 0.8 copy-done.7
  182.5 3.8 %fusion.145 = f32[512,256]{0,1:T(8,128)} fusion(f32[512,1,1,2,4,192]{0,5,4,3,2,1:T(8,128)S(1)} %copy-done, f32[1,1,2,4,96,128]{5,4,3,2,1,0:T(8,128)S(1)} %get-tuple-element.51, f32[1,1,2,4,96,128]{5,4,3,2,1,0:T(8,128)S(1)} %get-tuple-element.50, f32[1,1,2,4,96,256]{5,4,3,2,1,0:T(8,128)S(1)} %fusion.138), kind=kOutput, calls=%fused_computation.147 | convolution fusion | flops 2416705536 | bytes 5242880 | tf_op jit(solution)/shard_map/dot_general | solution.py:81
  186.4 20.8 %reduce-scatter.5.cloned.1.call-done = f32[128,256]{0,1:T(8,128)} async-done(((f32[512,256]{0,1:T(8,128)}), f32[128,256]{0,1:T(8,128)}) %reduce-scatter.5.cloned.1.call-update) | async-done | bytes 131088 | tf_op jit(solution)/shard_map/reduce_scatter | solution.py:88
  207.2 36.7 %all-reduce.5.cloned.1.call-done = f32[128,256]{0,1:T(8,128)} async-done(((f32[128,256]{0,1:T(8,128)}), f32[128,256]{0,1:T(8,128)}) %all-reduce.5.cloned.1.call-update) | async-done | bytes 131088 | tf_op jit(solution)/shard_map/psum | solution.py:87
  243.9 0.9 multiply_subtract_fusion
  244.9 7.5 %all_gather.7 = f32[512,256]{0,1:T(8,128)S(1)} all-gather(f32[128,256]{0,1:T(8,128)S(1)} %pad_maximum_fusion.7), channel_id=1, replica_groups=mesh['groups'=2,'space'=4,'tm'=4] {'space'}, dimensions={0}, use_global_device_ids=true | all-gather | bytes 655360 | tf_op jit(solution)/shard_map/all_gather | solution.py:92
  252.5 3.6 %multiply_add_fusion = f32[1,1,2,4,96,256]{5,4,3,2,1,0:T(8,128)} fusion(f32[1,1,2,4,96,256]{5,4,3,2,1,0:T(8,128)S(1)} %copy-done.8, f32[512,2,4,2,96]{0,4,3,2,1:T(8,128)S(1)} %bitcast.222, f32[1,512,256]{1,2,0:T(8,128)S(1)} %maximum_bitcast_fusion.63, f32[1,512,256]{1,2,0:T(8,128)S(1)} %bitcast.225, f32[1,1,2,4,96,256]{5,4,3,2,1,0:T(8,128)S(1)} %copy-done.12, ...), kind=kOutput, calls=%fused_computation.188 | convolution fusion | flops 2417164288 | bytes 7340032 | tf_op jit(solution)/shard_map/ktzyxci,ckn->tzyxin/dot_general | solution.py:97
  (77 shorter events, 2.1 us)
Async XLA Ops:
  7.2 54.3 %copy-start = (f32[512,1,1,2,4,192]{0,5,4,3,2,1:T(8,128)S(1)}, f32[512,1,1,2,4,192]{0,5,4,3,2,1:T(8,128)}, u32[]{:S(2)}) copy-start(f32[512,1,1,2,4,192]{0,5,4,3,2,1:T(8,128)} %param.16) | copy-start | bytes 9437188
  7.2 79.4 %reduce-scatter.3.cloned.1.call-start = ((), (), s32[]{:S(2)}) async-start(), calls=%async_computation.2 | async-start | bytes 655360 | tf_op jit(solution)/shard_map/reduce_scatter | solution.py:88
  7.2 25.5 %collective-permute-start.2 = (f32[1,1,2,4,96,256]{5,4,3,2,1,0:T(8,128)}, f32[1,1,2,4,96,256]{5,4,3,2,1,0:T(8,128)}, u32[]{:S(2)}, u32[]{:S(2)}) collective-permute-start(f32[1,1,2,4,96,256]{5,4,3,2,1,0:T(8,128)} %param.15), channel_id=1, source_target_pairs={{1,0},{2,1},{3,2},{0,3},{5,4},{6,5},{7,6},{4,7},{9,8},{10,9},{11,1... | collective-permute-start | bytes 2359304 | tf_op jit(solution)/shard_map/ppermute | solution.py:18
  12.3 34.9 %collective-permute-start.3 = (f32[1,1,2,4,96,256]{5,4,3,2,1,0:T(8,128)}, f32[1,1,2,4,96,256]{5,4,3,2,1,0:T(8,128)}, u32[]{:S(2)}, u32[]{:S(2)}) collective-permute-start(f32[1,1,2,4,96,256]{5,4,3,2,1,0:T(8,128)} %param.15), channel_id=1, source_target_pairs={{0,1},{1,2},{2,3},{3,0},{4,5},{5,6},{6,7},{7,4},{8,9},{9,10},{10,1... | collective-permute-start | bytes 2359304 | tf_op jit(solution)/shard_map/ppermute | solution.py:15
  12.3 36.2 %collective-permute-start.1 = (f32[1,1,2,4,96,256]{5,4,3,2,1,0:T(8,128)}, f32[1,1,2,4,96,256]{5,4,3,2,1,0:T(8,128)}, u32[]{:S(2)}, u32[]{:S(2)}) collective-permute-start(f32[1,1,2,4,96,256]{5,4,3,2,1,0:T(8,128)} %param.15), channel_id=1, source_target_pairs={{0,4},{4,8},{8,12},{12,0},{1,5},{5,9},{9,13},{13,1},{2,6},{6,10},{... | collective-permute-start | bytes 2359304 | tf_op jit(solution)/shard_map/ppermute | solution.py:15
  12.3 41.8 %collective-permute-start = (f32[1,1,2,4,96,256]{5,4,3,2,1,0:T(8,128)}, f32[1,1,2,4,96,256]{5,4,3,2,1,0:T(8,128)}, u32[]{:S(2)}, u32[]{:S(2)}) collective-permute-start(f32[1,1,2,4,96,256]{5,4,3,2,1,0:T(8,128)} %param.15), channel_id=1, source_target_pairs={{4,0},{8,4},{12,8},{0,12},{5,1},{9,5},{13,9},{1,13},{6,2},{10,6},{... | collective-permute-start | bytes 2359304 | tf_op jit(solution)/shard_map/ppermute | solution.py:18
  18.3 3.1 %copy-start.1 = (f32[1,1,2,4,96,256]{5,4,3,2,1,0:T(8,128)S(1)}, f32[1,1,2,4,96,256]{5,4,3,2,1,0:T(8,128)}, u32[]{:S(2)}) copy-start(f32[1,1,2,4,96,256]{5,4,3,2,1,0:T(8,128)} %param.15) | copy-start | bytes 2359300
  26.4 1.2 copy-start.2
  27.6 2.9 %copy-start.9 = (f32[1,1,2,3,96,256]{5,4,3,2,1,0:T(8,128)S(1)}, f32[1,1,2,3,96,256]{5,4,3,2,1,0:T(8,128)}, u32[]{:S(2)}) copy-start(f32[1,1,2,3,96,256]{5,4,3,2,1,0:T(8,128)} %get-tuple-element.74) | copy-start | bytes 1769476
  27.6 2.9 %copy-start.13 = (f32[2,4,256,96]{2,3,1,0:T(8,128)S(1)}, f32[2,4,256,96]{2,3,1,0:T(8,128)}, u32[]{:S(2)}) copy-start(f32[2,4,256,96]{2,3,1,0:T(8,128)} %fusion.152) | copy-start | bytes 2359300
  27.6 2.9 %copy-start.14 = (f32[2,4,256,96]{2,3,1,0:T(8,128)S(1)}, f32[2,4,256,96]{2,3,1,0:T(8,128)}, u32[]{:S(2)}) copy-start(f32[2,4,256,96]{2,3,1,0:T(8,128)} %fusion.154) | copy-start | bytes 2359300
  55.3 2.5 copy-start.10
  60.5 0.9 copy-start.4
  65.4 58.1 %all-reduce.3.cloned.1.call-start = ((), (), s32[]{:S(2)}) async-start(), calls=%async_computation.3 | async-start | bytes 262144 | tf_op jit(solution)/shard_map/psum | solution.py:87
  86.6 120.5 %reduce-scatter.5.cloned.1.call-start = ((), (), s32[]{:S(2)}) async-start(), calls=%async_computation.4 | async-start | bytes 655360 | tf_op jit(solution)/shard_map/reduce_scatter | solution.py:88
  124.4 7.4 %copy-start.3 = (f32[1,1,2,4,96,256]{5,4,3,2,1,0:T(8,128)S(1)}, f32[1,1,2,4,96,256]{5,4,3,2,1,0:T(8,128)}, u32[]{:S(2)}) copy-start(f32[1,1,2,4,96,256]{5,4,3,2,1,0:T(8,128)} %param.15) | copy-start | bytes 2359300
  124.4 7.4 %copy-start.5 = (f32[1,1,2,4,96,256]{5,4,3,2,1,0:T(8,128)S(1)}, f32[1,1,2,4,96,256]{5,4,3,2,1,0:T(8,128)}, u32[]{:S(2)}) copy-start(f32[1,1,2,4,96,256]{5,4,3,2,1,0:T(8,128)} %copy-done.4) | copy-start | bytes 2359300
  131.7 4.0 %slice-start = ((s8[7077888]{0:T(1024)(128)(4,1)}), s8[4194304]{0:T(1024)(128)(4,1)S(1)}, s32[]{:S(2)}) async-start(s8[7077888]{0:T(1024)(128)(4,1)} %bitcast.223), calls=%async_computation.6 | async-start | bytes 8388608
  131.8 3.9 %slice-start.1 = ((s8[7077888]{0:T(1024)(128)(4,1)}), s8[2883584]{0:T(1024)(128)(4,1)S(1)}, s32[]{:S(2)}) async-start(s8[7077888]{0:T(1024)(128)(4,1)} %bitcast.223), calls=%async_computation.7 | async-start | bytes 5767168
  137.8 39.0 %collective-permute-start.5 = (f32[1,1,2,4,96,256]{5,4,3,2,1,0:T(8,128)S(1)}, f32[1,1,2,4,96,256]{5,4,3,2,1,0:T(8,128)S(1)}, u32[]{:S(2)}, u32[]{:S(2)}) collective-permute-start(f32[1,1,2,4,96,256]{5,4,3,2,1,0:T(8,128)S(1)} %get-tuple-element.96), channel_id=1, source_target_pairs={{0,4},{4,8},{8,12},{12,0},{1,5},{5,9},{9,13},{13,1},{2,6},{6,10},{... | collective-permute-start | bytes 2359304 | tf_op jit(solution)/shard_map/ppermute | solution.py:15
  138.2 20.0 %collective-permute-start.6 = (f32[1,1,2,4,96,256]{5,4,3,2,1,0:T(8,128)S(1)}, f32[1,1,2,4,96,256]{5,4,3,2,1,0:T(8,128)S(1)}, u32[]{:S(2)}, u32[]{:S(2)}) collective-permute-start(f32[1,1,2,4,96,256]{5,4,3,2,1,0:T(8,128)S(1)} %get-tuple-element.96), channel_id=1, source_target_pairs={{1,0},{2,1},{3,2},{0,3},{5,4},{6,5},{7,6},{4,7},{9,8},{10,9},{11,1... | collective-permute-start | bytes 2359304 | tf_op jit(solution)/shard_map/ppermute | solution.py:18
  140.3 36.3 %collective-permute-start.7 = (f32[1,1,2,4,96,256]{5,4,3,2,1,0:T(8,128)S(1)}, f32[1,1,2,4,96,256]{5,4,3,2,1,0:T(8,128)S(1)}, u32[]{:S(2)}, u32[]{:S(2)}) collective-permute-start(f32[1,1,2,4,96,256]{5,4,3,2,1,0:T(8,128)S(1)} %get-tuple-element.96), channel_id=1, source_target_pairs={{0,1},{1,2},{2,3},{3,0},{4,5},{5,6},{6,7},{7,4},{8,9},{9,10},{10,1... | collective-permute-start | bytes 2359304 | tf_op jit(solution)/shard_map/ppermute | solution.py:15
  140.3 38.8 %collective-permute-start.4 = (f32[1,1,2,4,96,256]{5,4,3,2,1,0:T(8,128)S(1)}, f32[1,1,2,4,96,256]{5,4,3,2,1,0:T(8,128)S(1)}, u32[]{:S(2)}, u32[]{:S(2)}) collective-permute-start(f32[1,1,2,4,96,256]{5,4,3,2,1,0:T(8,128)S(1)} %get-tuple-element.96), channel_id=1, source_target_pairs={{4,0},{8,4},{12,8},{0,12},{5,1},{9,5},{13,9},{1,13},{6,2},{10,6},{... | collective-permute-start | bytes 2359304 | tf_op jit(solution)/shard_map/ppermute | solution.py:18
  179.2 1.1 copy-start.11
  181.6 0.9 copy-start.7
  186.3 57.6 %all-reduce.5.cloned.1.call-start = ((), (), s32[]{:S(2)}) async-start(), calls=%async_computation.5 | async-start | bytes 262144 | tf_op jit(solution)/shard_map/psum | solution.py:87
  244.8 7.6 %copy-start.6 = (f32[1,1,2,4,96,256]{5,4,3,2,1,0:T(8,128)S(1)}, f32[1,1,2,4,96,256]{5,4,3,2,1,0:T(8,128)}, u32[]{:S(2)}) copy-start(f32[1,1,2,4,96,256]{5,4,3,2,1,0:T(8,128)} %copy-done.4) | copy-start | bytes 2359300
  244.8 7.6 %copy-start.8 = (f32[1,1,2,4,96,256]{5,4,3,2,1,0:T(8,128)S(1)}, f32[1,1,2,4,96,256]{5,4,3,2,1,0:T(8,128)}, u32[]{:S(2)}) copy-start(f32[1,1,2,4,96,256]{5,4,3,2,1,0:T(8,128)} %copy-done.7) | copy-start | bytes 2359300
  244.8 7.6 %copy-start.12 = (f32[1,1,2,4,96,256]{5,4,3,2,1,0:T(8,128)S(1)}, f32[1,1,2,4,96,256]{5,4,3,2,1,0:T(8,128)}, u32[]{:S(2)}) copy-start(f32[1,1,2,4,96,256]{5,4,3,2,1,0:T(8,128)} %get-tuple-element.97) | copy-start | bytes 2359300
Sparse Core Ops, SparseCore 0:
  65.5 21.0 reduce-scatter.2
  89.0 34.4 all-reduce.2
  186.4 20.6 reduce-scatter.4
  209.4 34.4 all-reduce.4
where the time goes:
time: 263 us
  waiting for transfers between devices  160 us (61%)
  matrix products  48.7 us (19%)
  blocking collectives  14.7 us (6%)
  between operations  14.4 us (5%)
  starting transfers between devices  10.6 us (4%)
  other arithmetic  9.61 us (4%)
  local copies, waits for them, and re-layouts  4.8 us (2%)
    psum x2, waiting for transfers between devices, deflate(): over_time = lax.psum(partial_value, 'tm')  73.5 us
    reduce_scatter x2, waiting for transfers between devices, deflate(): lax.psum_scatter(over_time, 'space', scatter_dimension=0, tiled=True)  41.3 us
    dot_general x18, matrix products, coupled(): jnp.einsum('tzyxij,tzyxjn->tzyxin', matrix, stacked, precision=lax.Precis...  33.7 us
    ppermute x4, waiting for transfers between devices, with_halo(): lax.ppermute(lax.slice_in_dim(block, block.shape[dim] - width, None, axis...  31.4 us
    all_gather x2, blocking collectives, deflate(): lax.all_gather(scale_coeffs(owned, eigen_part), 'space', axis=0, tiled=True)  14.7 us
    ppermute x4, waiting for transfers between devices, with_halo(): lax.ppermute(lax.slice_in_dim(block, 0, width, axis=dim), axis, backward)  13.5 us
    ppermute x4, starting transfers between devices, with_halo(): lax.ppermute(lax.slice_in_dim(block, 0, width, axis=dim), axis, backward)  10.1 us
    dot_general x2, matrix products, deflate(): jnp.dot(vectors.reshape(number, -1), stacked.reshape(-1, stacked.shape[-1...  7.76 us
  transfers between devices with their start and end apart: 12, of which 7 were waited for; matrix products, arithmetic and copies ran while one was open for 13% of the time, Pallas kernels for 0%

commit v1 on v0

v1 whole, which is shorter than its diff:
```python
import functools

import jax
import jax.numpy as jnp
from jax import lax
from jax.experimental import pallas as pl
from jax.experimental.pallas import tpu as pltpu
from jax.sharding import PartitionSpec as P

ITERS = 2
F32 = jnp.float32
BF16 = jnp.bfloat16
VMEM_LIMIT = 48 * 1024 * 1024
LOCAL = 5


def params():
    return pltpu.CompilerParams(vmem_limit_bytes=VMEM_LIMIT)


def cost(flops, read):
    return pl.CostEstimate(flops=int(flops), bytes_accessed=int(read), transcendentals=0)


def low_lanes(value):
    lanes = lax.broadcasted_iota(jnp.int32, value.shape, value.ndim - 1)
    return lanes < value.shape[-1] // 2


def swap(value):
    return pltpu.roll(value, value.shape[-1] // 2, value.ndim - 1)


def turned(value):
    moved = swap(value)
    return jnp.where(low_lanes(value), -moved, moved)


def high_low(value):
    high = value.astype(BF16)
    low = (value - high.astype(F32)).astype(BF16)
    return high, low


def stack(value, sign):
    high, low = high_low(jnp.concatenate([value, sign * turned(value)], axis=0))
    return jnp.concatenate([high, low], axis=1)


def matmul(left, right):
    return jnp.dot(left, right, preferred_element_type=F32)


def fold(product):
    rows, lanes = product.shape[0] // 2, product.shape[1] // 2
    high = product[:rows, :lanes] + (product[:rows, lanes:] + product[rows:, :lanes])
    return high + product[rows:, lanes:]


def pick_half(value, group):
    middle = value.shape[-1] // 2
    real, imag = value[:, :middle], value[:, middle:]
    low = low_lanes(real)
    first = jnp.where(low, real, swap(imag))
    second = jnp.where(low, swap(real), imag)
    return jnp.where(group == 0, first, second)


def join_halves(own, other, group):
    first = jnp.where(group == 0, own, other)
    second = jnp.where(group == 0, other, own)
    low = low_lanes(own)
    real = jnp.where(low, first, swap(second))
    imag = jnp.where(low, swap(first), second)
    return jnp.concatenate([real, imag], axis=1)


def pack_kernel(place, full, half):
    for site in range(full.shape[0]):
        half[site] = pick_half(full[site], place[0])


def pack(place, full):
    sites, rows, lanes = full.shape
    return pl.pallas_call(
        pack_kernel,
        out_shape=jax.ShapeDtypeStruct((sites, rows, lanes // 2), F32),
        in_specs=[pl.BlockSpec(memory_space=pltpu.SMEM), pl.BlockSpec(memory_space=pltpu.VMEM)],
        out_specs=pl.BlockSpec(memory_space=pltpu.VMEM),
        compiler_params=params(),
        name="pack",
    )(place, full)


def around(site, ny, nx):
    y, x = site // nx, lax.rem(site, nx)
    right, left = lax.rem(x + 1, nx), lax.rem(x + nx - 1, nx)
    up, down = lax.rem(y + 1, ny), lax.rem(y + ny - 1, ny)
    return (site, y * nx + right, y * nx + left, up * nx + x, down * nx + x)


def local_sum(site, ny, nx, x_ref, stacks, matrix):
    @pl.when(site == 0)
    def _():
        for each in range(ny * nx):
            stacks[each] = stack(x_ref[each], 1.0)

    total = None
    for direction, neighbour in enumerate(around(site, ny, nx)):
        term = matmul(matrix(direction), stacks[neighbour])
        total = term if total is None else total + term
    return fold(total)


def first_kernel(ny, nx, place, x_ref, source, couplings, rest, half_source, local, halo, stacks):
    site = pl.program_id(0)
    own = pick_half(source[0], place[0])
    half_source[0] = own
    for direction in range(couplings.shape[0]):
        high, low = high_low(couplings[direction, 0])
        both = jnp.concatenate([high, low], axis=0)
        if direction < LOCAL:
            local[direction, 0] = both
        else:
            halo[direction - LOCAL, 0] = both
    rest[0] = own - local_sum(site, ny, nx, x_ref, stacks, lambda d: local[d, 0])


def first_local(place, x, source, couplings, ny, nx):
    sites, rows, lanes = x.shape
    directions, _, _, columns = couplings.shape
    outer = directions - LOCAL
    return pl.pallas_call(
        functools.partial(first_kernel, ny, nx),
        grid=(sites,),
        out_shape=(
            jax.ShapeDtypeStruct(x.shape, F32),
            jax.ShapeDtypeStruct(x.shape, F32),
            jax.ShapeDtypeStruct((LOCAL, sites, 2 * rows, columns), BF16),
            jax.ShapeDtypeStruct((outer, sites, 2 * rows, columns), BF16),
        ),
        in_specs=[
            pl.BlockSpec(memory_space=pltpu.SMEM),
            pl.BlockSpec((sites, rows, lanes), lambda s: (0, 0, 0)),
            pl.BlockSpec((1, rows, 2 * lanes), lambda s: (s, 0, 0)),
            pl.BlockSpec((directions, 1, rows, columns), lambda s: (0, s, 0, 0)),
        ],
        out_specs=(
            pl.BlockSpec((1, rows, lanes), lambda s: (s, 0, 0)),
            pl.BlockSpec((1, rows, lanes), lambda s: (s, 0, 0)),
            pl.BlockSpec((LOCAL, 1, 2 * rows, columns), lambda s: (0, s, 0, 0)),
            pl.BlockSpec((outer, 1, 2 * rows, columns), lambda s: (0, s, 0, 0)),
        ),
        scratch_shapes=[pltpu.VMEM((sites, 2 * rows, 2 * lanes), BF16)],
        compiler_params=params(),
        cost_estimate=cost(8e9, 16e6),
        name="first_local",
    )(place, x, source, couplings)


def local_kernel(ny, nx, x_ref, source, local, rest, stacks):
    site = pl.program_id(0)
    rest[0] = source[0] - local_sum(site, ny, nx, x_ref, stacks, lambda d: local[d, 0])


def local_part(x, source, local, ny, nx):
    sites, rows, lanes = x.shape
    columns = local.shape[-1]
    return pl.pallas_call(
        functools.partial(local_kernel, ny, nx),
        grid=(sites,),
        out_shape=jax.ShapeDtypeStruct(x.shape, F32),
        in_specs=[
            pl.BlockSpec((sites, rows, lanes), lambda s: (0, 0, 0)),
            pl.BlockSpec((1, rows, lanes), lambda s: (s, 0, 0)),
            pl.BlockSpec((LOCAL, 1, 2 * rows, columns), lambda s: (0, s, 0, 0)),
        ],
        out_specs=pl.BlockSpec((1, rows, lanes), lambda s: (s, 0, 0)),
        scratch_shapes=[pltpu.VMEM((sites, 2 * rows, 2 * lanes), BF16)],
        compiler_params=params(),
        cost_estimate=cost(8e9, 8e6),
        name="local_part",
    )(x, source, local)


def vectors_kernel(blocks, place, vectors, rows_out, columns_out, ordered):
    sites = rows_out.shape[0]
    rows = vectors.shape[1] // sites // 2
    size = vectors.shape[0] // blocks
    step = pl.program_id(0)

    @pl.when(step == 0)
    def _():
        for index in range(blocks):
            start = pl.multiple_of(place[1 + index] * size, size)
            ordered[index * size : (index + 1) * size] = vectors[pl.ds(start, size)]

    taken = rows_out.shape[2]
    part = ordered[pl.ds(pl.multiple_of(step * taken, taken), taken)]
    high, low = high_low(part)
    for site in range(sites):
        at = slice(site * 2 * rows, (site + 1) * 2 * rows)
        rows_out[site, 0] = high[:, at]
        rows_out[site, 1] = low[:, at]
    across = part.T
    for site in range(sites):
        for half in range(2):
            start = (2 * site + half) * rows
            high, low = high_low(across[start : start + rows])
            columns_out[0, site, half] = high
            columns_out[1, site, half] = low


def vectors_parts(place, vectors, blocks, sites):
    number, width = vectors.shape
    size = 128
    rows = width // sites // 2
    return pl.pallas_call(
        functools.partial(vectors_kernel, blocks),
        grid=(number // size,),
        out_shape=(
            jax.ShapeDtypeStruct((sites, 2, number, 2 * rows), BF16),
            jax.ShapeDtypeStruct((2, sites, 2, rows, number), BF16),
        ),
        in_specs=[
            pl.BlockSpec(memory_space=pltpu.SMEM),
            pl.BlockSpec((number, width), lambda b: (0, 0)),
        ],
        out_specs=(
            pl.BlockSpec((sites, 2, size, 2 * rows), lambda b: (0, 0, b, 0)),
            pl.BlockSpec((2, sites, 2, rows, size), lambda b: (0, 0, 0, 0, b)),
        ),
        scratch_shapes=[pltpu.VMEM((number, width), F32)],
        compiler_params=params(),
        cost_estimate=cost(1e9, 16e6),
        name="vectors_parts",
    )(place, vectors)


def halo_kernel(signs, rest, forward_z, backward_z, forward_t, backward_t, halo, vectors, residual, keep, send, total):
    site = pl.program_id(0)
    number, lanes = total.shape[0] // 2, total.shape[1] // 2
    fields = (forward_z[0], backward_z[0], signs[0] * forward_t[0], signs[1] * backward_t[0])
    summed = None
    for direction, field in enumerate(fields):
        term = matmul(halo[direction, 0], stack(field, 1.0))
        summed = term if summed is None else summed + term
    own = rest[0] - fold(summed)
    residual[0] = own
    rows = vectors.shape[3]
    left = vectors[0].reshape(2 * number, rows)
    product = matmul(left, stack(own, -1.0))

    @pl.when(site == 0)
    def _():
        total[...] = product

    @pl.when(site > 0)
    def _():
        total[...] += product

    @pl.when(site == pl.num_programs(0) - 1)
    def _():
        half = number // 2
        whole = fold(total[...])
        keep[...] = whole[:half]
        send[...] = whole[half:]


def halo_part(signs, rest, faces, halo, vectors):
    sites, rows, lanes = rest.shape
    outer, _, _, columns = halo.shape
    number = vectors.shape[2]
    field = pl.BlockSpec((1, rows, lanes), lambda s: (s, 0, 0))
    part = jax.ShapeDtypeStruct((number // 2, lanes), F32)
    whole = pl.BlockSpec((number // 2, lanes), lambda s: (0, 0))
    return pl.pallas_call(
        halo_kernel,
        grid=(sites,),
        out_shape=(jax.ShapeDtypeStruct(rest.shape, F32), part, part),
        in_specs=[
            pl.BlockSpec(memory_space=pltpu.SMEM),
            field,
            field,
            field,
            field,
            field,
            pl.BlockSpec((outer, 1, 2 * rows, columns), lambda s: (0, s, 0, 0)),
            pl.BlockSpec((1, 2, number, 2 * rows), lambda s: (s, 0, 0, 0)),
        ],
        out_specs=(field, whole, whole),
        scratch_shapes=[pltpu.VMEM((2 * number, 2 * lanes), F32)],
        compiler_params=params(),
        cost_estimate=cost(1e9, 8e6),
        name="halo_part",
    )(signs, rest, *faces, halo, vectors)


def scale_kernel(eigen, *refs):
    parts, out = refs[:-1], refs[-1]
    total = parts[0][...]
    for part in parts[1:]:
        total = total + part[...]
    out[...] = eigen[:, 0:1] * total + eigen[:, 1:2] * turned(total)


def scale(eigen, parts):
    return pl.pallas_call(
        scale_kernel,
        out_shape=jax.ShapeDtypeStruct(parts[0].shape, F32),
        compiler_params=params(),
        name="scale",
    )(eigen, *parts)


def update_kernel(x, residual, d, vectors, out, stacks):
    @pl.when(pl.program_id(0) == 0)
    def _():
        stacks[...] = stack(d[...], 1.0)

    rows = vectors.shape[3]
    number = vectors.shape[4]
    for site in range(vectors.shape[1]):
        total = None
        for half in range(2):
            left = vectors[:, site, half].reshape(2 * rows, number)
            term = matmul(left, stacks[half * number : (half + 1) * number, :])
            total = term if total is None else total + term
        out[site] = x[site] + 0.5 * residual[site] + fold(total)


def update(x, residual, d, vectors):
    sites, rows, lanes = x.shape
    number = vectors.shape[-1]
    step = 2
    field = pl.BlockSpec((step, rows, lanes), lambda s: (s, 0, 0))
    return pl.pallas_call(
        update_kernel,
        grid=(sites // step,),
        out_shape=jax.ShapeDtypeStruct(x.shape, F32),
        in_specs=[
            field,
            field,
            pl.BlockSpec((number, lanes), lambda s: (0, 0)),
            pl.BlockSpec((2, step, 2, rows, number), lambda s: (0, s, 0, 0, 0)),
        ],
        out_specs=field,
        scratch_shapes=[pltpu.VMEM((2 * number, 2 * lanes), BF16)],
        compiler_params=params(),
        cost_estimate=cost(1e9, 8e6),
        name="update",
    )(x, residual, d, vectors)


def join_kernel(place, x, other_x, residual, other_residual, base, full):
    own = x[0] + 0.5 * residual[0]
    other = other_x[0] + 0.5 * other_residual[0]
    base[0] = join_halves(own, other, place[0])
    full[0] = join_halves(residual[0], other_residual[0], place[0])


def join(place, x, other_x, residual, other_residual):
    sites, rows, lanes = x.shape
    field = pl.BlockSpec((1, rows, lanes), lambda s: (s, 0, 0))
    wide = pl.BlockSpec((1, rows, 2 * lanes), lambda s: (s, 0, 0))
    shape = jax.ShapeDtypeStruct((sites, rows, 2 * lanes), F32)
    return pl.pallas_call(
        join_kernel,
        grid=(sites,),
        out_shape=(shape, shape),
        in_specs=[pl.BlockSpec(memory_space=pltpu.SMEM), field, field, field, field],
        out_specs=(wide, wide),
        compiler_params=params(),
        cost_estimate=cost(1e6, 4e6),
        name="join",
    )(place, x, other_x, residual, other_residual)


def final_kernel(place, base, d, other_d, vectors, out, stacks):
    @pl.when(pl.program_id(0) == 0)
    def _():
        whole = join_halves(d[...], other_d[...], place[0])
        stacks[...] = stack(whole, 1.0)

    rows = vectors.shape[3]
    number = vectors.shape[4]
    for site in range(vectors.shape[1]):
        total = None
        for half in range(2):
            left = vectors[:, site, half].reshape(2 * rows, number)
            term = matmul(left, stacks[half * number : (half + 1) * number, :])
            total = term if total is None else total + term
        out[site] = base[site] + fold(total)


def final(place, base, d, other_d, vectors):
    sites, rows, lanes = base.shape
    number = vectors.shape[-1]
    step = 2
    field = pl.BlockSpec((step, rows, lanes), lambda s: (s, 0, 0))
    small = pl.BlockSpec((number, lanes // 2), lambda s: (0, 0))
    return pl.pallas_call(
        final_kernel,
        grid=(sites // step,),
        out_shape=jax.ShapeDtypeStruct(base.shape, F32),
        in_specs=[
            pl.BlockSpec(memory_space=pltpu.SMEM),
            field,
            small,
            small,
            pl.BlockSpec((2, step, 2, rows, number), lambda s: (0, s, 0, 0, 0)),
        ],
        out_specs=field,
        scratch_shapes=[pltpu.VMEM((2 * number, 2 * lanes), BF16)],
        compiler_params=params(),
        cost_estimate=cost(2e9, 8e6),
        name="final",
    )(place, base, d, other_d, vectors)


def shifted(value, axis, step):
    count = lax.axis_size(axis)
    return lax.ppermute(value, axis, [(i, (i + step) % count) for i in range(count)])


def crossed(value, axis, mask):
    count = lax.axis_size(axis)
    return lax.ppermute(value, axis, [(i, i ^ mask) for i in range(count)])


def faces_of(x):
    backward_t = shifted(x, "tm", 1)
    forward_t = shifted(x, "tm", -1)
    backward_z = shifted(x, "space", 1)
    forward_z = shifted(x, "space", -1)
    return forward_z, backward_z, forward_t, backward_t


def halving(keep, send):
    count = lax.axis_size("space")
    mask = 1
    while mask < count:
        part = keep + crossed(send, "space", mask)
        mask *= 2
        middle = part.shape[0] // 2
        keep, send = part[:middle], part[middle:]
    return part


def doubling(part):
    mask = lax.axis_size("space") // 2
    while mask:
        part = jnp.concatenate([part, crossed(part, "space", mask)], axis=0)
        mask //= 2
    return part


def over_time(part):
    count = lax.axis_size("tm")
    if count <= 4:
        return [part] + [shifted(part, "tm", step) for step in range(1, count)]
    mask = 1
    while mask < count:
        part = part + crossed(part, "tm", mask)
        mask *= 2
    return [part]


def block_order(count):
    bits = count.bit_length() - 1
    return [int(format(index, "b").zfill(bits)[::-1], 2) if bits else 0 for index in range(count)]


def shards(couplings, source, initial, vectors, inverse_eigen):
    directions = couplings.shape[0]
    ny, nx, rows, lanes = source.shape[2:]
    sites = ny * nx
    number = vectors.shape[0]
    width = vectors.shape[-1]
    group, space, time = (lax.axis_index(name) for name in ("groups", "space", "tm"))
    blocks, slices = lax.axis_size("space"), lax.axis_size("tm")

    order = jnp.array(block_order(blocks), jnp.int32) ^ space
    place = jnp.concatenate([jnp.full((1,), group, jnp.int32), order])
    signs = jnp.stack([jnp.where(time == slices - 1, -1.0, 1.0), jnp.where(time == 0, -1.0, 1.0)]).astype(F32)
    size = number // blocks
    eigen = lax.dynamic_slice_in_dim(inverse_eigen, space * size, size, 1).T

    x = pack(place, initial.reshape(sites, rows, lanes))
    faces = faces_of(x)
    matrices = couplings.reshape(directions, sites, rows, couplings.shape[-1])
    rest, half_source, local, halo = first_local(place, x, source.reshape(sites, rows, lanes), matrices, ny, nx)
    by_rows, by_columns = vectors_parts(place, vectors.reshape(number, sites * width), blocks, sites)

    for sweep in range(ITERS):
        if sweep:
            faces = faces_of(x)
            rest = local_part(x, half_source, local, ny, nx)
        residual, keep, send = halo_part(signs, rest, faces, halo, by_rows)
        part = halving(keep, send)
        d = scale(eigen, over_time(part))
        if sweep < ITERS - 1:
            x = update(x, residual, doubling(d), by_columns)
    other_x = crossed(x, "groups", 1)
    other_residual = crossed(residual, "groups", 1)
    other_d = crossed(d, "groups", 1)
    base, full_residual = join(place, x, other_x, residual, other_residual)
    whole = final(place, base, doubling(d), doubling(other_d), by_columns)
    shape = source.shape
    return whole.reshape(shape), full_residual.reshape(shape)


def solution(mesh):
    in_specs = (
        P(None, "tm", "space", None, None, None, None),
        P("tm", "space", None, None, None, None),
        P("tm", "space", None, None, None, None),
        P(None, "tm", "space", None, None, None),
        P(),
    )
    out_specs = (
        P(("groups", "tm"), "space", None, None, None, None),
        P(("groups", "tm"), "space", None, None, None, None),
    )
    return jax.shard_map(shards, mesh=mesh, in_specs=in_specs, out_specs=out_specs, check_vma=False)
```

time: 263 us -> 138 us (0.52)
  waiting for transfers between devices: 160 us -> 40.1 us
  matrix products: 48.7 us -> 0 us
  Pallas kernels: 0 us -> 47.8 us
  starting transfers between devices: 10.6 us -> 30.8 us
  blocking collectives: 14.7 us -> 0 us
  between operations: 14.4 us -> 0.91 us
  local copies, waits for them, and re-layouts: 4.8 us -> 15.4 us
  other arithmetic: 9.61 us -> 2.43 us
    psum x2 -> x0, waiting for transfers between devices: 73.5 us -> none  [deflate(): over_time = lax.psum(partial_value, 'tm')]
    dot_general x22 -> x0, matrix products: 48.7 us -> none  [the longest x18 33.7 us: coupled(): jnp.einsum('tzyxij,tzyxjn->tzyxin', matrix, stacked, precision=lax.Precis...]
    pallas_call x0 -> x11, Pallas kernels: none -> 47.8 us  [the longest x2 18.7 us: halo_part(): pl.pallas_call(halo_kernel, grid=(sites,), out_shape=(jax.ShapeDtypeStruc...]
    reduce_scatter x2 -> x0, waiting for transfers between devices: 41.3 us -> none  [deflate(): lax.psum_scatter(over_time, 'space', scatter_dimension=0, tiled=True)]
    ppermute x8 -> x27, starting transfers between devices: 10.5 us -> 30.8 us  [the longest x14 19.9 us: shifted(): lax.ppermute(value, axis, [(i, (i + step) % count) for i in range(count)])]
    all_gather x2 -> x0, blocking collectives: 14.7 us -> none  [deflate(): lax.all_gather(scale_coeffs(owned, eigen_part), 'space', axis=0, tiled=True)]
    unnamed x34 -> x33, local copies, waits for them, and re-layouts: 1.82 us -> 11.3 us
    neg x18 -> x0, other arithmetic: 5.09 us -> none  [the longest x16 5.02 us: coupled(): -spinor[..., middle:]]
  transfers between devices with their start and end apart: 12 -> 27, of which waited for: 7 -> 15; matrix products, arithmetic and copies ran while one was open for 13% -> 3% of each run, Pallas kernels for 0% -> 15%
where the time goes in v1:
time: 138 us
  Pallas kernels  47.8 us (35%)
  waiting for transfers between devices  40.1 us (29%)
  starting transfers between devices  30.8 us (22%)
  local copies, waits for them, and re-layouts  15.4 us (11%)
  other arithmetic  2.43 us (2%)
    ppermute x14, waiting for transfers between devices, shifted(): lax.ppermute(value, axis, [(i, (i + step) % count) for i in range(count)])  20.5 us
    ppermute x14, starting transfers between devices, shifted(): lax.ppermute(value, axis, [(i, (i + step) % count) for i in range(count)])  19.9 us
    ppermute x13, waiting for transfers between devices, crossed(): return lax.ppermute(value, axis, [(i, i ^ mask) for i in range(count)])  19.6 us
    pallas_call x2, Pallas kernels, halo_part(): pl.pallas_call(halo_kernel, grid=(sites,), out_shape=(jax.ShapeDtypeStruc...  18.7 us
    unnamed x33, local copies, waits for them, and re-layouts  11.3 us
    ppermute x13, starting transfers between devices, crossed(): return lax.ppermute(value, axis, [(i, i ^ mask) for i in range(count)])  10.9 us
    pallas_call x1, Pallas kernels, first_local(): pl.pallas_call(functools.partial(first_kernel, ny, nx), grid=(sites,), ou...  8.78 us
    pallas_call x1, Pallas kernels, vectors_parts(): pl.pallas_call(functools.partial(vectors_kernel, blocks), grid=(number //...  5.66 us
  transfers between devices with their start and end apart: 27, of which 15 were waited for; matrix products, arithmetic and copies ran while one was open for 3% of the time, Pallas kernels for 15%

profile of v1, /device:TPU:0, one launch (start us, length us, event | category | flops | bytes accessed | tf_op | source)
XLA Modules:
  0.0 137.6 jit_solution(12070206351707676635)
XLA Ops:
  1.4 1.1 copy-done.4
  2.5 0.8 pack.1.x_ref.x
  3.3 3.1 %collective-permute-start.3 = (f32[8,96,128]{2,1,0:T(8,128)S(1)}, f32[8,96,128]{2,1,0:T(8,128)}, u32[]{:S(2)}, u32[]{:S(2)}) collective-permute-start(f32[8,96,128]{2,1,0:T(8,128)S(1)} %pack.1.x_ref.x), channel_id=1, source_target_pairs={{0,1},{1,2},{2,3},{3,0},{4,5},{5,6},{6,7},{7,4},{8,9},{9,10},{10,1... | collective-permute-start | bytes 1179656 | tf_op jit(solution)/shard_map/ppermute | solution.py:423
  6.4 2.1 %collective-permute-start.2 = (f32[8,96,128]{2,1,0:T(8,128)S(1)}, f32[8,96,128]{2,1,0:T(8,128)}, u32[]{:S(2)}, u32[]{:S(2)}) collective-permute-start(f32[8,96,128]{2,1,0:T(8,128)S(1)} %pack.1.x_ref.x), channel_id=1, source_target_pairs={{0,3},{1,0},{2,1},{3,2},{4,7},{5,4},{6,5},{7,6},{8,11},{9,8},{10,9... | collective-permute-start | bytes 1179656 | tf_op jit(solution)/shard_map/ppermute | solution.py:423
  8.5 1.7 %collective-permute-start = (f32[8,96,128]{2,1,0:T(8,128)S(1)}, f32[8,96,128]{2,1,0:T(8,128)}, u32[]{:S(2)}, u32[]{:S(2)}) collective-permute-start(f32[8,96,128]{2,1,0:T(8,128)S(1)} %pack.1.x_ref.x), channel_id=1, source_target_pairs={{0,12},{4,0},{8,4},{12,8},{1,13},{5,1},{9,5},{13,9},{2,14},{6,2},{... | collective-permute-start | bytes 1179656 | tf_op jit(solution)/shard_map/ppermute | solution.py:423
  10.3 1.1 copy-done.11
  11.4 8.8 %first_local.1 = (f32[8,96,128]{2,1,0:T(8,128)S(1)}, f32[8,96,128]{2,1,0:T(8,128)S(1)}, bf16[5,8,192,192]{3,2,1,0:T(8,128)(2,1)}, bf16[4,8,192,192]{3,2,1,0:T(8,128)(2,1)S(1)}) custom-call(s32[5]{0:T(128)S(1)} %pad_add_fusion.place, f32[8,96,128]{2,1,0:T(8,128)S(1)} %pack.1.x_ref.x, f32[8,96,256]{2,1,0:T(8,128)S(1)} %bitcast.13, f32[9,8,96,192]{3,2,1,0:T(8,128)} %bitcast.15), custom_call_target="tpu_custom_call" | custom-call | flops 8000000000 | bytes 16000000 | tf_op jit(solution)/shard_map/first_local/pallas_call | solution.py:133
  20.2 0.7 copy-done.7
  21.7 3.5 %copy.10.vectors = f32[512,1536]{1,0:T(8,128)} copy(f32[512,1536]{0,1:T(8,128)} %bitcast.14) | data formatting | bytes 6291456 | tf_op jit(solution)/shard_map/reshape | solution.py:493
  25.2 5.7 %vectors_parts.1 = (bf16[8,2,512,192]{3,2,1,0:T(8,128)(2,1)}, bf16[2,8,2,96,512]{4,3,2,1,0:T(8,128)(2,1)S(1)}) custom-call(s32[5]{0:T(128)S(1)} %pad_add_fusion.place, f32[512,1536]{1,0:T(8,128)} %copy.10.vectors), custom_call_target="tpu_custom_call" | custom-call | flops 1000000000 | bytes 16000000 | tf_op jit(solution)/shard_map/vectors_parts/pallas_call | solution.py:218
  30.9 1.7 %copy-done.1 = bf16[2,8,2,96,512]{4,3,2,1,0:T(8,128)(2,1)} copy-done((bf16[2,8,2,96,512]{4,3,2,1,0:T(8,128)(2,1)}, bf16[2,8,2,96,512]{4,3,2,1,0:T(8,128)(2,1)S(1)}, u32[]{:S(2)}) %copy-start.1) | copy-done | bytes 3145752
  32.7 9.5 %halo_part.2 = (f32[8,96,128]{2,1,0:T(8,128)S(1)}, f32[256,128]{1,0:T(8,128)S(1)}, f32[256,128]{1,0:T(8,128)S(1)}) custom-call(f32[2]{0:T(128)S(1)} %pad_maximum_fusion.6.signs, f32[8,96,128]{2,1,0:T(8,128)S(1)} %copy-done.8, f32[8,96,128]{2,1,0:T(8,128)} %collective-permute-done.forward_z, f32[8,96,128]{2,1,0:T(8,128)} %collective-permute-done.1.backward_z, ...), custom_call_target="tpu_custom_call" | custom-call | flops 1000000000 | bytes 8000000 | tf_op jit(solution)/shard_map/halo_part/pallas_call | solution.py:277
  42.9 1.3 collective-permute-done.4
  45.5 1.6 %collective-permute-start.5 = (f32[128,128]{1,0:T(8,128)}, f32[128,128]{1,0:T(8,128)}, u32[]{:S(2)}, u32[]{:S(2)}) collective-permute-start(f32[128,128]{1,0:T(8,128)} %slice.17), channel_id=1, source_target_pairs={{0,8},{4,12},{8,0},{12,4},{1,9},{5,13},{9,1},{13,5},{2,10},{6,14},... | collective-permute-start | bytes 196616 | tf_op jit(solution)/shard_map/ppermute | solution.py:428
  47.2 2.9 %collective-permute-done.5 = f32[128,128]{1,0:T(8,128)} collective-permute-done((f32[128,128]{1,0:T(8,128)}, f32[128,128]{1,0:T(8,128)}, u32[]{:S(2)}, u32[]{:S(2)}) %collective-permute-start.5) | collective-permute-done | bytes 65568 | tf_op jit(solution)/shard_map/ppermute | solution.py:428
  50.1 1.5 %slice_add_fusion.1.refs_0_ = f32[128,128]{1,0:T(8,128)} fusion(f32[128,128]{1,0:T(8,128)} %collective-permute-done.5, f32[256,128]{1,0:T(8,128)} %copy-done.15), kind=kLoop, calls=%fused_computation.7 | loop fusion | flops 16384 | bytes 196608 | tf_op jit(solution)/shard_map/add | solution.py:443
  51.6 2.0 %collective-permute-start.8 = (f32[128,128]{1,0:T(8,128)}, f32[128,128]{1,0:T(8,128)}, u32[]{:S(2)}, u32[]{:S(2)}) collective-permute-start(f32[128,128]{1,0:T(8,128)} %slice_add_fusion.1.refs_0_), channel_id=1, source_target_pairs={{0,3},{1,0},{2,1},{3,2},{4,7},{5,4},{6,5},{7,6},{8,11},{9,8},{10,9... | collective-permute-start | bytes 196616 | tf_op jit(solution)/shard_map/ppermute | solution.py:423
  53.6 1.0 collective-permute-start.6
  55.3 1.0 collective-permute-done.8.refs_3_
  56.3 3.0 %collective-permute-done.7.refs_2_ = f32[128,128]{1,0:T(8,128)} collective-permute-done((f32[128,128]{1,0:T(8,128)}, f32[128,128]{1,0:T(8,128)}, u32[]{:S(2)}, u32[]{:S(2)}) %collective-permute-start.7) | collective-permute-done | bytes 65568 | tf_op jit(solution)/shard_map/ppermute | solution.py:423
  60.0 0.8 copy-done.5
  60.8 1.1 scale.2
  61.9 1.7 %collective-permute-start.9 = (f32[128,128]{1,0:T(8,128)S(1)}, f32[128,128]{1,0:T(8,128)S(1)}, u32[]{:S(2)}, u32[]{:S(2)}) collective-permute-start(f32[128,128]{1,0:T(8,128)S(1)} %scale.2), channel_id=1, source_target_pairs={{0,8},{4,12},{8,0},{12,4},{1,9},{5,13},{9,1},{13,5},{2,10},{6,14},... | collective-permute-start | bytes 196616 | tf_op jit(solution)/shard_map/ppermute | solution.py:428
  63.6 2.6 %collective-permute-done.9 = f32[128,128]{1,0:T(8,128)S(1)} collective-permute-done((f32[128,128]{1,0:T(8,128)S(1)}, f32[128,128]{1,0:T(8,128)S(1)}, u32[]{:S(2)}, u32[]{:S(2)}) %collective-permute-start.9) | collective-permute-done | bytes 65568 | tf_op jit(solution)/shard_map/ppermute | solution.py:428
  66.3 1.3 collective-permute-done.10
  67.7 1.9 %copy-done.2 = bf16[2,8,2,96,512]{4,3,2,1,0:T(8,128)(2,1)S(1)} copy-done((bf16[2,8,2,96,512]{4,3,2,1,0:T(8,128)(2,1)S(1)}, bf16[2,8,2,96,512]{4,3,2,1,0:T(8,128)(2,1)}, u32[]{:S(2)}) %copy-start.2) | copy-done | bytes 3145752
  69.6 1.0 copy-done.10
  70.6 1.9 %update.1.x_ref.x = f32[8,96,128]{2,1,0:T(8,128)S(1)} custom-call(f32[8,96,128]{2,1,0:T(8,128)S(1)} %pack.1.x_ref.x, f32[8,96,128]{2,1,0:T(8,128)S(1)} %copy-done.10, f32[512,128]{1,0:T(8,128)S(1)} %pad_maximum_fusion.d, bf16[2,8,2,96,512]{4,3,2,1,0:T(8,128)(2,1)S(1)} %copy-done.2), custom_call_target="tpu_custom_call" | custom-call | flops 1000000000 | bytes 8000000 | tf_op jit(solution)/shard_map/update/pallas_call | solution.py:337
  72.6 3.8 %collective-permute-start.14 = (f32[8,96,128]{2,1,0:T(8,128)S(1)}, f32[8,96,128]{2,1,0:T(8,128)S(1)}, u32[]{:S(2)}, u32[]{:S(2)}) collective-permute-start(f32[8,96,128]{2,1,0:T(8,128)S(1)} %update.1.x_ref.x), channel_id=1, source_target_pairs={{0,3},{1,0},{2,1},{3,2},{4,7},{5,4},{6,5},{7,6},{8,11},{9,8},{10,9... | collective-permute-start | bytes 1179656 | tf_op jit(solution)/shard_map/ppermute | solution.py:423
  76.4 1.7 %collective-permute-start.12 = (f32[8,96,128]{2,1,0:T(8,128)S(1)}, f32[8,96,128]{2,1,0:T(8,128)S(1)}, u32[]{:S(2)}, u32[]{:S(2)}) collective-permute-start(f32[8,96,128]{2,1,0:T(8,128)S(1)} %update.1.x_ref.x), channel_id=1, source_target_pairs={{0,12},{4,0},{8,4},{12,8},{1,13},{5,1},{9,5},{13,9},{2,14},{6,2},{... | collective-permute-start | bytes 1179656 | tf_op jit(solution)/shard_map/ppermute | solution.py:423
  78.1 3.0 %local_part.1.rest = f32[8,96,128]{2,1,0:T(8,128)S(1)} custom-call(f32[8,96,128]{2,1,0:T(8,128)S(1)} %update.1.x_ref.x, f32[8,96,128]{2,1,0:T(8,128)S(1)} %copy-done.14, bf16[5,8,192,192]{3,2,1,0:T(8,128)(2,1)S(1)} %copy-done.12), custom_call_target="tpu_custom_call" | custom-call | flops 8000000000 | bytes 8000000 | tf_op jit(solution)/shard_map/local_part/pallas_call | solution.py:169
  81.1 5.2 %collective-permute-done.15.backward_t = f32[8,96,128]{2,1,0:T(8,128)S(1)} collective-permute-done((f32[8,96,128]{2,1,0:T(8,128)S(1)}, f32[8,96,128]{2,1,0:T(8,128)S(1)}, u32[]{:S(2)}, u32[]{:S(2)}) %collective-permute-start.15) | collective-permute-done | bytes 393248 | tf_op jit(solution)/shard_map/ppermute | solution.py:423
  86.4 5.9 %collective-permute-done.14.forward_t = f32[8,96,128]{2,1,0:T(8,128)S(1)} collective-permute-done((f32[8,96,128]{2,1,0:T(8,128)S(1)}, f32[8,96,128]{2,1,0:T(8,128)S(1)}, u32[]{:S(2)}, u32[]{:S(2)}) %collective-permute-start.14) | collective-permute-done | bytes 393248 | tf_op jit(solution)/shard_map/ppermute | solution.py:423
  92.2 9.2 %halo_part.3 = (f32[8,96,128]{2,1,0:T(8,128)S(1)}, f32[256,128]{1,0:T(8,128)S(1)}, f32[256,128]{1,0:T(8,128)S(1)}) custom-call(f32[2]{0:T(128)S(1)} %pad_maximum_fusion.6.signs, f32[8,96,128]{2,1,0:T(8,128)S(1)} %local_part.1.rest, f32[8,96,128]{2,1,0:T(8,128)S(1)} %collective-permute-done.12.forward_z, ...), custom_call_target="tpu_custom_call" | custom-call | flops 1000000000 | bytes 8000000 | tf_op jit(solution)/shard_map/halo_part/pallas_call | solution.py:277
  101.5 1.3 collective-permute-done.17
  102.9 1.7 %collective-permute-start.18 = (f32[128,128]{1,0:T(8,128)S(1)}, f32[128,128]{1,0:T(8,128)S(1)}, u32[]{:S(2)}, u32[]{:S(2)}) collective-permute-start(f32[128,128]{1,0:T(8,128)S(1)} %slice.19), channel_id=1, source_target_pairs={{0,8},{4,12},{8,0},{12,4},{1,9},{5,13},{9,1},{13,5},{2,10},{6,14},... | collective-permute-start | bytes 196616 | tf_op jit(solution)/shard_map/ppermute | solution.py:428
  104.6 1.5 %collective-permute-start.11 = (f32[8,96,128]{2,1,0:T(8,128)S(1)}, f32[8,96,128]{2,1,0:T(8,128)S(1)}, u32[]{:S(2)}, u32[]{:S(2)}) collective-permute-start(f32[8,96,128]{2,1,0:T(8,128)S(1)} %update.1.x_ref.x), channel_id=1, source_target_pairs={{0,16},{16,0},{1,17},{17,1},{2,18},{18,2},{3,19},{19,3},{4,20},{20... | collective-permute-start | bytes 1179656 | tf_op jit(solution)/shard_map/ppermute | solution.py:428
  107.2 2.2 %collective-permute-start.21 = (f32[128,128]{1,0:T(8,128)S(1)}, f32[128,128]{1,0:T(8,128)S(1)}, u32[]{:S(2)}, u32[]{:S(2)}) collective-permute-start(f32[128,128]{1,0:T(8,128)S(1)} %slice_add_fusion.refs_0_), channel_id=1, source_target_pairs={{0,3},{1,0},{2,1},{3,2},{4,7},{5,4},{6,5},{7,6},{8,11},{9,8},{10,9... | collective-permute-start | bytes 196616 | tf_op jit(solution)/shard_map/ppermute | solution.py:423
  109.4 1.0 collective-permute-start.20
  110.3 1.3 collective-permute-start.19
  111.6 3.9 %collective-permute-done.20.refs_2_ = f32[128,128]{1,0:T(8,128)S(1)} collective-permute-done((f32[128,128]{1,0:T(8,128)S(1)}, f32[128,128]{1,0:T(8,128)S(1)}, u32[]{:S(2)}, u32[]{:S(2)}) %collective-permute-start.20) | collective-permute-done | bytes 65568 | tf_op jit(solution)/shard_map/ppermute | solution.py:423
  115.5 0.8 collective-permute-done.19.refs_1_
  116.5 1.6 %collective-permute-start.24 = (f32[128,128]{1,0:T(8,128)S(1)}, f32[128,128]{1,0:T(8,128)S(1)}, u32[]{:S(2)}, u32[]{:S(2)}) collective-permute-start(f32[128,128]{1,0:T(8,128)S(1)} %scale.3), channel_id=1, source_target_pairs={{0,16},{16,0},{1,17},{17,1},{2,18},{18,2},{3,19},{19,3},{4,20},{20... | collective-permute-start | bytes 196616 | tf_op jit(solution)/shard_map/ppermute | solution.py:428
  118.1 1.5 %collective-permute-start.22 = (f32[128,128]{1,0:T(8,128)S(1)}, f32[128,128]{1,0:T(8,128)S(1)}, u32[]{:S(2)}, u32[]{:S(2)}) collective-permute-start(f32[128,128]{1,0:T(8,128)S(1)} %scale.3), channel_id=1, source_target_pairs={{0,8},{4,12},{8,0},{12,4},{1,9},{5,13},{9,1},{13,5},{2,10},{6,14},... | collective-permute-start | bytes 196616 | tf_op jit(solution)/shard_map/ppermute | solution.py:428
  119.6 5.7 %collective-permute-done.24 = f32[128,128]{1,0:T(8,128)S(1)} collective-permute-done((f32[128,128]{1,0:T(8,128)S(1)}, f32[128,128]{1,0:T(8,128)S(1)}, u32[]{:S(2)}, u32[]{:S(2)}) %collective-permute-start.24) | collective-permute-done | bytes 65568 | tf_op jit(solution)/shard_map/ppermute | solution.py:428
  125.8 3.8 %collective-permute-done.25 = f32[128,128]{1,0:T(8,128)S(1)} collective-permute-done((f32[128,128]{1,0:T(8,128)S(1)}, f32[128,128]{1,0:T(8,128)S(1)}, u32[]{:S(2)}, u32[]{:S(2)}) %collective-permute-start.25) | collective-permute-done | bytes 65568 | tf_op jit(solution)/shard_map/ppermute | solution.py:428
  129.7 3.8 %join.1 = (f32[8,96,256]{2,1,0:T(8,128)S(1)}, f32[8,96,256]{2,1,0:T(8,128)}) custom-call(s32[5]{0:T(128)S(1)} %pad_add_fusion.place, f32[8,96,128]{2,1,0:T(8,128)S(1)} %update.1.x_ref.x, f32[8,96,128]{2,1,0:T(8,128)S(1)} %collective-permute-done.11.other_x, f32[8,96,128]{2,1,0:T(8,128)S(1)} %get-tuple-element.25.residual, ...), custom_call_target="tpu_custom_call" | custom-call | flops 1000000 | bytes 4000000 | tf_op jit(solution)/shard_map/join/pallas_call | solution.py:367
  133.5 4.0 %final.1 = f32[8,96,256]{2,1,0:T(8,128)} custom-call(s32[5]{0:T(128)S(1)} %pad_add_fusion.place, f32[8,96,256]{2,1,0:T(8,128)S(1)} %get-tuple-element.26.base, f32[512,128]{1,0:T(8,128)S(1)} %pad_maximum_fusion.1.d, f32[512,128]{1,0:T(8,128)S(1)} %pad_maximum_fusion.2.other_d, bf16[2,8,2,96,512]{4,3,2,1,0:T(8,128)(2,1)S(1)} %copy-done.3), custom_call_target="tpu_custom_call" | custom-call | flops 2000000000 | bytes 8000000 | tf_op jit(solution)/shard_map/final/pallas_call | solution.py:402
  (67 shorter events, 7.1 us)
Async XLA Ops:
  0.6 53.9 %copy-start = (f32[2,512]{1,0:T(2,128)S(1)}, f32[2,512]{1,0:T(2,128)}, u32[]{:S(2)}) copy-start(f32[2,512]{1,0:T(2,128)} %param.10) | copy-start | bytes 12292
  1.4 1.1 copy-start.4
  3.3 29.3 %collective-permute-start.3 = (f32[8,96,128]{2,1,0:T(8,128)S(1)}, f32[8,96,128]{2,1,0:T(8,128)}, u32[]{:S(2)}, u32[]{:S(2)}) collective-permute-start(f32[8,96,128]{2,1,0:T(8,128)S(1)} %pack.1.x_ref.x), channel_id=1, source_target_pairs={{0,1},{1,2},{2,3},{3,0},{4,5},{5,6},{6,7},{7,4},{8,9},{9,10},{10,1... | collective-permute-start | bytes 1179656 | tf_op jit(solution)/shard_map/ppermute | solution.py:423
  6.4 26.2 %collective-permute-start.2 = (f32[8,96,128]{2,1,0:T(8,128)S(1)}, f32[8,96,128]{2,1,0:T(8,128)}, u32[]{:S(2)}, u32[]{:S(2)}) collective-permute-start(f32[8,96,128]{2,1,0:T(8,128)S(1)} %pack.1.x_ref.x), channel_id=1, source_target_pairs={{0,3},{1,0},{2,1},{3,2},{4,7},{5,4},{6,5},{7,6},{8,11},{9,8},{10,9... | collective-permute-start | bytes 1179656 | tf_op jit(solution)/shard_map/ppermute | solution.py:423
  8.5 24.1 %collective-permute-start.1 = (f32[8,96,128]{2,1,0:T(8,128)S(1)}, f32[8,96,128]{2,1,0:T(8,128)}, u32[]{:S(2)}, u32[]{:S(2)}) collective-permute-start(f32[8,96,128]{2,1,0:T(8,128)S(1)} %pack.1.x_ref.x), channel_id=1, source_target_pairs={{0,4},{4,8},{8,12},{12,0},{1,5},{5,9},{9,13},{13,1},{2,6},{6,10},{... | collective-permute-start | bytes 1179656 | tf_op jit(solution)/shard_map/ppermute | solution.py:423
  8.5 24.1 %collective-permute-start = (f32[8,96,128]{2,1,0:T(8,128)S(1)}, f32[8,96,128]{2,1,0:T(8,128)}, u32[]{:S(2)}, u32[]{:S(2)}) collective-permute-start(f32[8,96,128]{2,1,0:T(8,128)S(1)} %pack.1.x_ref.x), channel_id=1, source_target_pairs={{0,12},{4,0},{8,4},{12,8},{1,13},{5,1},{9,5},{13,9},{2,14},{6,2},{... | collective-permute-start | bytes 1179656 | tf_op jit(solution)/shard_map/ppermute | solution.py:423
  10.3 1.1 copy-start.11
  20.2 0.7 copy-start.7
  20.9 0.7 copy-start.13
  25.2 7.4 %copy-start.8 = (f32[8,96,128]{2,1,0:T(8,128)S(1)}, f32[8,96,128]{2,1,0:T(8,128)}, u32[]{:S(2)}) copy-start(f32[8,96,128]{2,1,0:T(8,128)} %copy-done.7) | copy-start | bytes 1179652
  30.9 1.7 %copy-start.1 = (bf16[2,8,2,96,512]{4,3,2,1,0:T(8,128)(2,1)}, bf16[2,8,2,96,512]{4,3,2,1,0:T(8,128)(2,1)S(1)}, u32[]{:S(2)}) copy-start(bf16[2,8,2,96,512]{4,3,2,1,0:T(8,128)(2,1)S(1)} %get-tuple-element.22.vectors) | copy-start | bytes 9437188
  42.1 0.7 copy-start.9
  42.9 1.3 collective-permute-start.4
  44.3 0.6 copy-start.15
  45.5 4.6 %collective-permute-start.5 = (f32[128,128]{1,0:T(8,128)}, f32[128,128]{1,0:T(8,128)}, u32[]{:S(2)}, u32[]{:S(2)}) collective-permute-start(f32[128,128]{1,0:T(8,128)} %slice.17), channel_id=1, source_target_pairs={{0,8},{4,12},{8,0},{12,4},{1,9},{5,13},{9,1},{13,5},{2,10},{6,14},... | collective-permute-start | bytes 196616 | tf_op jit(solution)/shard_map/ppermute | solution.py:428
  51.6 4.7 %collective-permute-start.8 = (f32[128,128]{1,0:T(8,128)}, f32[128,128]{1,0:T(8,128)}, u32[]{:S(2)}, u32[]{:S(2)}) collective-permute-start(f32[128,128]{1,0:T(8,128)} %slice_add_fusion.1.refs_0_), channel_id=1, source_target_pairs={{0,3},{1,0},{2,1},{3,2},{4,7},{5,4},{6,5},{7,6},{8,11},{9,8},{10,9... | collective-permute-start | bytes 196616 | tf_op jit(solution)/shard_map/ppermute | solution.py:423
  53.6 5.7 %collective-permute-start.7 = (f32[128,128]{1,0:T(8,128)}, f32[128,128]{1,0:T(8,128)}, u32[]{:S(2)}, u32[]{:S(2)}) collective-permute-start(f32[128,128]{1,0:T(8,128)} %slice_add_fusion.1.refs_0_), channel_id=1, source_target_pairs={{0,2},{1,3},{2,0},{3,1},{4,6},{5,7},{6,4},{7,5},{8,10},{9,11},{10,... | collective-permute-start | bytes 196616 | tf_op jit(solution)/shard_map/ppermute | solution.py:423
  53.6 6.4 %collective-permute-start.6 = (f32[128,128]{1,0:T(8,128)}, f32[128,128]{1,0:T(8,128)}, u32[]{:S(2)}, u32[]{:S(2)}) collective-permute-start(f32[128,128]{1,0:T(8,128)} %slice_add_fusion.1.refs_0_), channel_id=1, source_target_pairs={{0,1},{1,2},{2,3},{3,0},{4,5},{5,6},{6,7},{7,4},{8,9},{9,10},{10,1... | collective-permute-start | bytes 196616 | tf_op jit(solution)/shard_map/ppermute | solution.py:423
  60.0 0.8 copy-start.5
  60.8 17.3 %copy-start.14 = (f32[8,96,128]{2,1,0:T(8,128)S(1)}, f32[8,96,128]{2,1,0:T(8,128)}, u32[]{:S(2)}) copy-start(f32[8,96,128]{2,1,0:T(8,128)} %copy-done.13) | copy-start | bytes 1179652
  61.9 4.3 %collective-permute-start.9 = (f32[128,128]{1,0:T(8,128)S(1)}, f32[128,128]{1,0:T(8,128)S(1)}, u32[]{:S(2)}, u32[]{:S(2)}) collective-permute-start(f32[128,128]{1,0:T(8,128)S(1)} %scale.2), channel_id=1, source_target_pairs={{0,8},{4,12},{8,0},{12,4},{1,9},{5,13},{9,1},{13,5},{2,10},{6,14},... | collective-permute-start | bytes 196616 | tf_op jit(solution)/shard_map/ppermute | solution.py:428
  66.2 1.4 %collective-permute-start.10 = (f32[256,128]{1,0:T(8,128)S(1)}, f32[256,128]{1,0:T(8,128)S(1)}, u32[]{:S(2)}, u32[]{:S(2)}) collective-permute-start(f32[256,128]{1,0:T(8,128)S(1)} %pad_maximum_fusion.3), channel_id=1, source_target_pairs={{0,4},{4,0},{8,12},{12,8},{1,5},{5,1},{9,13},{13,9},{2,6},{6,2},{1... | collective-permute-start | bytes 393224 | tf_op jit(solution)/shard_map/ppermute | solution.py:428
  67.7 1.9 %copy-start.2 = (bf16[2,8,2,96,512]{4,3,2,1,0:T(8,128)(2,1)S(1)}, bf16[2,8,2,96,512]{4,3,2,1,0:T(8,128)(2,1)}, u32[]{:S(2)}) copy-start(bf16[2,8,2,96,512]{4,3,2,1,0:T(8,128)(2,1)} %copy-done.1) | copy-start | bytes 9437188
  69.6 1.0 copy-start.10
  70.6 7.6 %copy-start.12 = (bf16[5,8,192,192]{3,2,1,0:T(8,128)(2,1)S(1)}, bf16[5,8,192,192]{3,2,1,0:T(8,128)(2,1)}, u32[]{:S(2)}) copy-start(bf16[5,8,192,192]{3,2,1,0:T(8,128)(2,1)} %get-tuple-element.24.local) | copy-start | bytes 8847364
  72.5 13.9 %collective-permute-start.15 = (f32[8,96,128]{2,1,0:T(8,128)S(1)}, f32[8,96,128]{2,1,0:T(8,128)S(1)}, u32[]{:S(2)}, u32[]{:S(2)}) collective-permute-start(f32[8,96,128]{2,1,0:T(8,128)S(1)} %update.1.x_ref.x), channel_id=1, source_target_pairs={{0,1},{1,2},{2,3},{3,0},{4,5},{5,6},{6,7},{7,4},{8,9},{9,10},{10,1... | collective-permute-start | bytes 1179656 | tf_op jit(solution)/shard_map/ppermute | solution.py:423
  72.6 19.6 %collective-permute-start.14 = (f32[8,96,128]{2,1,0:T(8,128)S(1)}, f32[8,96,128]{2,1,0:T(8,128)S(1)}, u32[]{:S(2)}, u32[]{:S(2)}) collective-permute-start(f32[8,96,128]{2,1,0:T(8,128)S(1)} %update.1.x_ref.x), channel_id=1, source_target_pairs={{0,3},{1,0},{2,1},{3,2},{4,7},{5,4},{6,5},{7,6},{8,11},{9,8},{10,9... | collective-permute-start | bytes 1179656 | tf_op jit(solution)/shard_map/ppermute | solution.py:423
  76.4 15.8 %collective-permute-start.13 = (f32[8,96,128]{2,1,0:T(8,128)S(1)}, f32[8,96,128]{2,1,0:T(8,128)S(1)}, u32[]{:S(2)}, u32[]{:S(2)}) collective-permute-start(f32[8,96,128]{2,1,0:T(8,128)S(1)} %update.1.x_ref.x), channel_id=1, source_target_pairs={{0,4},{4,8},{8,12},{12,0},{1,5},{5,9},{9,13},{13,1},{2,6},{6,10},{... | collective-permute-start | bytes 1179656 | tf_op jit(solution)/shard_map/ppermute | solution.py:423
  76.4 15.8 %collective-permute-start.12 = (f32[8,96,128]{2,1,0:T(8,128)S(1)}, f32[8,96,128]{2,1,0:T(8,128)S(1)}, u32[]{:S(2)}, u32[]{:S(2)}) collective-permute-start(f32[8,96,128]{2,1,0:T(8,128)S(1)} %update.1.x_ref.x), channel_id=1, source_target_pairs={{0,12},{4,0},{8,4},{12,8},{1,13},{5,1},{9,5},{13,9},{2,14},{6,2},{... | collective-permute-start | bytes 1179656 | tf_op jit(solution)/shard_map/ppermute | solution.py:423
  81.1 35.3 %copy-start.6 = (f32[2,128]{0,1:T(8,128)S(1)}, f32[2,128]{0,1:T(8,128)}, u32[]{:S(2)}) copy-start(f32[2,128]{0,1:T(8,128)} %copy.12) | copy-start | bytes 3076
  101.4 32.1 %copy-start.3 = (bf16[2,8,2,96,512]{4,3,2,1,0:T(8,128)(2,1)S(1)}, bf16[2,8,2,96,512]{4,3,2,1,0:T(8,128)(2,1)}, u32[]{:S(2)}) copy-start(bf16[2,8,2,96,512]{4,3,2,1,0:T(8,128)(2,1)} %copy-done.1) | copy-start | bytes 9437188
  101.4 1.4 %collective-permute-start.17 = (f32[256,128]{1,0:T(8,128)S(1)}, f32[256,128]{1,0:T(8,128)S(1)}, u32[]{:S(2)}, u32[]{:S(2)}) collective-permute-start(f32[256,128]{1,0:T(8,128)S(1)} %get-tuple-element.28), channel_id=1, source_target_pairs={{0,4},{4,0},{8,12},{12,8},{1,5},{5,1},{9,13},{13,9},{2,6},{6,2},{1... | collective-permute-start | bytes 393224 | tf_op jit(solution)/shard_map/ppermute | solution.py:428
  102.9 4.3 %collective-permute-start.18 = (f32[128,128]{1,0:T(8,128)S(1)}, f32[128,128]{1,0:T(8,128)S(1)}, u32[]{:S(2)}, u32[]{:S(2)}) collective-permute-start(f32[128,128]{1,0:T(8,128)S(1)} %slice.19), channel_id=1, source_target_pairs={{0,8},{4,12},{8,0},{12,4},{1,9},{5,13},{9,1},{13,5},{2,10},{6,14},... | collective-permute-start | bytes 196616 | tf_op jit(solution)/shard_map/ppermute | solution.py:428
  104.6 25.1 %collective-permute-start.11 = (f32[8,96,128]{2,1,0:T(8,128)S(1)}, f32[8,96,128]{2,1,0:T(8,128)S(1)}, u32[]{:S(2)}, u32[]{:S(2)}) collective-permute-start(f32[8,96,128]{2,1,0:T(8,128)S(1)} %update.1.x_ref.x), channel_id=1, source_target_pairs={{0,16},{16,0},{1,17},{17,1},{2,18},{18,2},{3,19},{19,3},{4,20},{20... | collective-permute-start | bytes 1179656 | tf_op jit(solution)/shard_map/ppermute | solution.py:428
  106.1 23.6 %collective-permute-start.16 = (f32[8,96,128]{2,1,0:T(8,128)S(1)}, f32[8,96,128]{2,1,0:T(8,128)S(1)}, u32[]{:S(2)}, u32[]{:S(2)}) collective-permute-start(f32[8,96,128]{2,1,0:T(8,128)S(1)} %get-tuple-element.25.residual), channel_id=1, source_target_pairs={{0,16},{16,0},{1,17},{17,1},{2,18},{18,2},{3,19},{19,3},{4,20},{20... | collective-permute-start | bytes 1179656 | tf_op jit(solution)/shard_map/ppermute | solution.py:428
  107.2 4.4 %collective-permute-start.21 = (f32[128,128]{1,0:T(8,128)S(1)}, f32[128,128]{1,0:T(8,128)S(1)}, u32[]{:S(2)}, u32[]{:S(2)}) collective-permute-start(f32[128,128]{1,0:T(8,128)S(1)} %slice_add_fusion.refs_0_), channel_id=1, source_target_pairs={{0,3},{1,0},{2,1},{3,2},{4,7},{5,4},{6,5},{7,6},{8,11},{9,8},{10,9... | collective-permute-start | bytes 196616 | tf_op jit(solution)/shard_map/ppermute | solution.py:423
  109.4 6.2 %collective-permute-start.20 = (f32[128,128]{1,0:T(8,128)S(1)}, f32[128,128]{1,0:T(8,128)S(1)}, u32[]{:S(2)}, u32[]{:S(2)}) collective-permute-start(f32[128,128]{1,0:T(8,128)S(1)} %slice_add_fusion.refs_0_), channel_id=1, source_target_pairs={{0,2},{1,3},{2,0},{3,1},{4,6},{5,7},{6,4},{7,5},{8,10},{9,11},{10,... | collective-permute-start | bytes 196616 | tf_op jit(solution)/shard_map/ppermute | solution.py:423
  110.3 6.1 %collective-permute-start.19 = (f32[128,128]{1,0:T(8,128)S(1)}, f32[128,128]{1,0:T(8,128)S(1)}, u32[]{:S(2)}, u32[]{:S(2)}) collective-permute-start(f32[128,128]{1,0:T(8,128)S(1)} %slice_add_fusion.refs_0_), channel_id=1, source_target_pairs={{0,1},{1,2},{2,3},{3,0},{4,5},{5,6},{6,7},{7,4},{8,9},{9,10},{10,1... | collective-permute-start | bytes 196616 | tf_op jit(solution)/shard_map/ppermute | solution.py:423
  116.5 8.8 %collective-permute-start.24 = (f32[128,128]{1,0:T(8,128)S(1)}, f32[128,128]{1,0:T(8,128)S(1)}, u32[]{:S(2)}, u32[]{:S(2)}) collective-permute-start(f32[128,128]{1,0:T(8,128)S(1)} %scale.3), channel_id=1, source_target_pairs={{0,16},{16,0},{1,17},{17,1},{2,18},{18,2},{3,19},{19,3},{4,20},{20... | collective-permute-start | bytes 196616 | tf_op jit(solution)/shard_map/ppermute | solution.py:428
  118.1 7.6 %collective-permute-start.22 = (f32[128,128]{1,0:T(8,128)S(1)}, f32[128,128]{1,0:T(8,128)S(1)}, u32[]{:S(2)}, u32[]{:S(2)}) collective-permute-start(f32[128,128]{1,0:T(8,128)S(1)} %scale.3), channel_id=1, source_target_pairs={{0,8},{4,12},{8,0},{12,4},{1,9},{5,13},{9,1},{13,5},{2,10},{6,14},... | collective-permute-start | bytes 196616 | tf_op jit(solution)/shard_map/ppermute | solution.py:428
  125.3 4.3 %collective-permute-start.25 = (f32[128,128]{1,0:T(8,128)S(1)}, f32[128,128]{1,0:T(8,128)S(1)}, u32[]{:S(2)}, u32[]{:S(2)}) collective-permute-start(f32[128,128]{1,0:T(8,128)S(1)} %collective-permute-done.24), channel_id=1, source_target_pairs={{0,8},{4,12},{8,0},{12,4},{1,9},{5,13},{9,1},{13,5},{2,10},{6,14},... | collective-permute-start | bytes 196616 | tf_op jit(solution)/shard_map/ppermute | solution.py:428
  125.7 7.7 %collective-permute-start.23 = (f32[256,128]{1,0:T(8,128)S(1)}, f32[256,128]{1,0:T(8,128)S(1)}, u32[]{:S(2)}, u32[]{:S(2)}) collective-permute-start(f32[256,128]{1,0:T(8,128)S(1)} %pad_maximum_fusion.4), channel_id=1, source_target_pairs={{0,4},{4,0},{8,12},{12,8},{1,5},{5,1},{9,13},{13,9},{2,6},{6,2},{1... | collective-permute-start | bytes 393224 | tf_op jit(solution)/shard_map/ppermute | solution.py:428
  129.6 3.9 %collective-permute-start.26 = (f32[256,128]{1,0:T(8,128)S(1)}, f32[256,128]{1,0:T(8,128)S(1)}, u32[]{:S(2)}, u32[]{:S(2)}) collective-permute-start(f32[256,128]{1,0:T(8,128)S(1)} %pad_maximum_fusion.5), channel_id=1, source_target_pairs={{0,4},{4,0},{8,12},{12,8},{1,5},{5,1},{9,13},{13,9},{2,6},{6,2},{1... | collective-permute-start | bytes 393224 | tf_op jit(solution)/shard_map/ppermute | solution.py:428

commit v2 on v1

v2 whole, which is shorter than its diff:
```python
import functools

import jax
import jax.numpy as jnp
from jax import lax
from jax.experimental import pallas as pl
from jax.experimental.pallas import tpu as pltpu
from jax.sharding import PartitionSpec as P

ITERS = 2
F32 = jnp.float32
BF16 = jnp.bfloat16
LOCAL = 5


def params(mebibytes=12):
    return pltpu.CompilerParams(vmem_limit_bytes=mebibytes * 1024 * 1024)


def cost(flops, read):
    return pl.CostEstimate(flops=int(flops), bytes_accessed=int(read), transcendentals=0)


def low_lanes(value):
    lanes = lax.broadcasted_iota(jnp.int32, value.shape, value.ndim - 1)
    return lanes < value.shape[-1] // 2


def swap(value):
    return pltpu.roll(value, value.shape[-1] // 2, value.ndim - 1)


def turned(value):
    moved = swap(value)
    return jnp.where(low_lanes(value), -moved, moved)


def high_low(value):
    high = value.astype(BF16)
    low = (value - high.astype(F32)).astype(BF16)
    return high, low


def stack(value, sign):
    high, low = high_low(jnp.concatenate([value, sign * turned(value)], axis=0))
    return jnp.concatenate([high, low], axis=1)


def matmul(left, right):
    return jnp.dot(left, right, preferred_element_type=F32)


def fold(product):
    rows, lanes = product.shape[0] // 2, product.shape[1] // 2
    high = product[:rows, :lanes] + (product[:rows, lanes:] + product[rows:, :lanes])
    return high + product[rows:, lanes:]


def pick_half(value, group):
    middle = value.shape[-1] // 2
    real, imag = value[:, :middle], value[:, middle:]
    low = low_lanes(real)
    first = jnp.where(low, real, swap(imag))
    second = jnp.where(low, swap(real), imag)
    return jnp.where(group == 0, first, second)


def join_halves(own, other, group):
    first = jnp.where(group == 0, own, other)
    second = jnp.where(group == 0, other, own)
    low = low_lanes(own)
    real = jnp.where(low, first, swap(second))
    imag = jnp.where(low, swap(first), second)
    return jnp.concatenate([real, imag], axis=1)


def vmem(count):
    return [pl.BlockSpec(memory_space=pltpu.VMEM)] * count


def pack_kernel(full, half):
    group = lax.axis_index("groups")
    for site in range(full.shape[0]):
        half[site] = pick_half(full[site], group)


def pack(full):
    sites, rows, lanes = full.shape
    step = 2
    return pl.pallas_call(
        pack_kernel,
        grid=(sites // step,),
        out_shape=jax.ShapeDtypeStruct((sites, rows, lanes // 2), F32),
        in_specs=[pl.BlockSpec((step, rows, lanes), lambda s: (s, 0, 0))],
        out_specs=pl.BlockSpec((step, rows, lanes // 2), lambda s: (s, 0, 0)),
        compiler_params=params(),
        cost_estimate=cost(1e6, 1e6),
        name="pack",
    )(full)


def around(site, ny, nx):
    y, x = site // nx, lax.rem(site, nx)
    right, left = lax.rem(x + 1, nx), lax.rem(x + nx - 1, nx)
    up, down = lax.rem(y + 1, ny), lax.rem(y + ny - 1, ny)
    return (site, y * nx + right, y * nx + left, up * nx + x, down * nx + x)


def local_sum(site, ny, nx, x_ref, stacks, matrix):
    @pl.when(site == 0)
    def _():
        for each in range(ny * nx):
            stacks[each] = stack(x_ref[each], 1.0)

    total = None
    for direction, neighbour in enumerate(around(site, ny, nx)):
        term = matmul(matrix(direction), stacks[neighbour])
        total = term if total is None else total + term
    return fold(total)


def first_kernel(ny, nx, x_ref, source, couplings, rest, half_source, local, halo, stacks):
    site = pl.program_id(0)
    own = pick_half(source[0], lax.axis_index("groups"))
    half_source[0] = own
    for direction in range(couplings.shape[0]):
        high, low = high_low(couplings[direction, 0])
        both = jnp.concatenate([high, low], axis=0)
        if direction < LOCAL:
            local[direction, 0] = both
        else:
            halo[direction - LOCAL, 0] = both
    rest[0] = own - local_sum(site, ny, nx, x_ref, stacks, lambda d: local[d, 0])


def first_local(x, source, couplings, ny, nx):
    sites, rows, lanes = x.shape
    directions, _, _, columns = couplings.shape
    outer = directions - LOCAL
    return pl.pallas_call(
        functools.partial(first_kernel, ny, nx),
        grid=(sites,),
        out_shape=(
            jax.ShapeDtypeStruct(x.shape, F32),
            jax.ShapeDtypeStruct(x.shape, F32),
            jax.ShapeDtypeStruct((LOCAL, sites, 2 * rows, columns), BF16),
            jax.ShapeDtypeStruct((outer, sites, 2 * rows, columns), BF16),
        ),
        in_specs=[
            pl.BlockSpec((sites, rows, lanes), lambda s: (0, 0, 0)),
            pl.BlockSpec((1, rows, 2 * lanes), lambda s: (s, 0, 0)),
            pl.BlockSpec((directions, 1, rows, columns), lambda s: (0, s, 0, 0)),
        ],
        out_specs=(
            pl.BlockSpec((1, rows, lanes), lambda s: (s, 0, 0)),
            pl.BlockSpec((1, rows, lanes), lambda s: (s, 0, 0)),
            pl.BlockSpec((LOCAL, 1, 2 * rows, columns), lambda s: (0, s, 0, 0)),
            pl.BlockSpec((outer, 1, 2 * rows, columns), lambda s: (0, s, 0, 0)),
        ),
        scratch_shapes=[pltpu.VMEM((sites, 2 * rows, 2 * lanes), BF16)],
        compiler_params=params(),
        cost_estimate=cost(8e9, 16e6),
        name="first_local",
    )(x, source, couplings)


def local_kernel(ny, nx, x_ref, source, local, rest, stacks):
    site = pl.program_id(0)
    rest[0] = source[0] - local_sum(site, ny, nx, x_ref, stacks, lambda d: local[d, 0])


def local_part(x, source, local, ny, nx):
    sites, rows, lanes = x.shape
    columns = local.shape[-1]
    return pl.pallas_call(
        functools.partial(local_kernel, ny, nx),
        grid=(sites,),
        out_shape=jax.ShapeDtypeStruct(x.shape, F32),
        in_specs=[
            pl.BlockSpec((sites, rows, lanes), lambda s: (0, 0, 0)),
            pl.BlockSpec((1, rows, lanes), lambda s: (s, 0, 0)),
            pl.BlockSpec((LOCAL, 1, 2 * rows, columns), lambda s: (0, s, 0, 0)),
        ],
        out_specs=pl.BlockSpec((1, rows, lanes), lambda s: (s, 0, 0)),
        scratch_shapes=[pltpu.VMEM((sites, 2 * rows, 2 * lanes), BF16)],
        compiler_params=params(),
        cost_estimate=cost(8e9, 8e6),
        name="local_part",
    )(x, source, local)


def block_order(count):
    bits = count.bit_length() - 1
    return [int(format(index, "b").zfill(bits)[::-1], 2) if bits else 0 for index in range(count)]


def ordered_rows(vectors, chunk, taken):
    blocks = lax.axis_size("space")
    space = lax.axis_index("space")
    size = vectors.shape[0] // blocks
    unit = min(size, taken)
    parts = []
    for start in range(chunk * taken, (chunk + 1) * taken, unit):
        block = space ^ block_order(blocks)[start // size]
        parts.append(vectors[pl.ds(pl.multiple_of(block * size + start % size, unit), unit)])
    return parts[0] if len(parts) == 1 else jnp.concatenate(parts, axis=0)


def by_rows_kernel(vectors, out):
    taken = 128
    number = vectors.shape[0]
    for chunk in range(number // taken):
        high, low = high_low(ordered_rows(vectors, chunk, taken))
        out[chunk * taken : (chunk + 1) * taken] = high
        out[number + chunk * taken : number + (chunk + 1) * taken] = low


def by_rows_of(vectors):
    number, width = vectors.shape
    return pl.pallas_call(
        by_rows_kernel,
        out_shape=jax.ShapeDtypeStruct((2 * number, width), BF16),
        in_specs=vmem(1),
        out_specs=vmem(1)[0],
        compiler_params=params(),
        cost_estimate=cost(1e6, 6e6),
        name="by_rows",
    )(vectors)


def by_columns_kernel(vectors, out):
    taken = 128
    sites, rows = out.shape[0], out.shape[2] // 2
    for chunk in range(vectors.shape[0] // taken):
        across = ordered_rows(vectors, chunk, taken).T
        at = slice(chunk * taken, (chunk + 1) * taken)
        for site in range(sites):
            for half in range(2):
                start = (2 * site + half) * rows
                high, low = high_low(across[start : start + rows])
                out[site, half, :rows, at] = high
                out[site, half, rows:, at] = low


def by_columns_of(vectors, sites):
    number, width = vectors.shape
    rows = width // sites // 2
    return pl.pallas_call(
        by_columns_kernel,
        out_shape=jax.ShapeDtypeStruct((sites, 2, 2 * rows, number), BF16),
        in_specs=vmem(1),
        out_specs=vmem(1)[0],
        compiler_params=params(),
        cost_estimate=cost(1e6, 6e6),
        name="by_columns",
    )(vectors)


def apply_faces(site, faces, matrices):
    summed = None
    for face, matrix in zip(faces, matrices):
        term = matmul(matrix[site], stack(face(site), 1.0))
        summed = term if summed is None else summed + term
    return fold(summed)


def z_faces_kernel(rest, forward, backward, matrix, out):
    faces = (lambda s: forward[s], lambda s: backward[s])
    for site in range(rest.shape[0]):
        out[site] = rest[site] - apply_faces(site, faces, (matrix.at[0], matrix.at[1]))


def z_faces(rest, forward, backward, matrix):
    return pl.pallas_call(
        z_faces_kernel,
        out_shape=jax.ShapeDtypeStruct(rest.shape, F32),
        in_specs=vmem(4),
        out_specs=vmem(1)[0],
        compiler_params=params(),
        cost_estimate=cost(1e9, 4e6),
        name="z_faces",
    )(rest, forward, backward, matrix)


def edge_sign(last):
    count = lax.axis_size("tm")
    return jnp.where(lax.axis_index("tm") == (count - 1 if last else 0), -1.0, 1.0).astype(F32)


def backward_kernel(rest, backward, matrix, out):
    sign = edge_sign(False)
    for site in range(rest.shape[0]):
        out[site] = rest[site] - apply_faces(site, (lambda s: sign * backward[s],), (matrix.at[3],))


def backward_face(rest, backward, matrix):
    return pl.pallas_call(
        backward_kernel,
        out_shape=jax.ShapeDtypeStruct(rest.shape, F32),
        in_specs=vmem(3),
        out_specs=vmem(1)[0],
        compiler_params=params(),
        cost_estimate=cost(1e9, 4e6),
        name="backward_face",
    )(rest, backward, matrix)


def forward_kernel(rest, forward, matrix, vectors, residual, keep, send, stacks):
    sign = edge_sign(True)
    rows = 2 * rest.shape[1]
    for site in range(rest.shape[0]):
        own = rest[site] - apply_faces(site, (lambda s: sign * forward[s],), (matrix.at[2],))
        residual[site] = own
        stacks[site * rows : (site + 1) * rows] = stack(own, -1.0)
    whole = fold(matmul(vectors[...], stacks[...]))
    half = whole.shape[0] // 2
    keep[...] = whole[:half]
    send[...] = whole[half:]


def forward_face(rest, forward, matrix, vectors):
    sites, rows, lanes = rest.shape
    part = jax.ShapeDtypeStruct((vectors.shape[0] // 4, lanes), F32)
    return pl.pallas_call(
        forward_kernel,
        out_shape=(jax.ShapeDtypeStruct(rest.shape, F32), part, part),
        in_specs=vmem(4),
        out_specs=tuple(vmem(3)),
        scratch_shapes=[pltpu.VMEM((sites * 2 * rows, 2 * lanes), BF16)],
        compiler_params=params(),
        cost_estimate=cost(2e9, 8e6),
        name="forward_face",
    )(rest, forward, matrix, vectors)


def split_kernel(keep, received, next_keep, next_send):
    half = next_keep.shape[0]
    next_keep[...] = keep[:half] + received[:half]
    next_send[...] = keep[half:] + received[half:]


def add_split(keep, received):
    rows, lanes = keep.shape
    part = jax.ShapeDtypeStruct((rows // 2, lanes), F32)
    return pl.pallas_call(
        split_kernel,
        out_shape=(part, part),
        in_specs=vmem(2),
        out_specs=tuple(vmem(2)),
        compiler_params=params(),
        name="add_split",
    )(keep, received)


def scale_kernel(eigen, *refs):
    parts, out = refs[:-1], refs[-1]
    total = parts[0][...]
    for part in parts[1:]:
        total = total + part[...]
    out[...] = eigen[0] * total + eigen[1] * turned(total)


def scale(eigen, parts):
    return pl.pallas_call(
        scale_kernel,
        out_shape=jax.ShapeDtypeStruct(parts[0].shape, F32),
        in_specs=vmem(1 + len(parts)),
        out_specs=vmem(1)[0],
        compiler_params=params(),
        name="scale",
    )(eigen, *parts)


def expand(site, vectors, stacks):
    number = vectors.shape[3]
    total = None
    for half in range(2):
        term = matmul(vectors[site, half], stacks[half * number : (half + 1) * number])
        total = term if total is None else total + term
    return fold(total)


def update_kernel(x, residual, d, vectors, out, stacks):
    stacks[...] = stack(d[...], 1.0)
    for site in range(x.shape[0]):
        out[site] = x[site] + 0.5 * residual[site] + expand(site, vectors, stacks)


def update(x, residual, d, vectors):
    number = vectors.shape[-1]
    return pl.pallas_call(
        update_kernel,
        out_shape=jax.ShapeDtypeStruct(x.shape, F32),
        in_specs=vmem(4),
        out_specs=vmem(1)[0],
        scratch_shapes=[pltpu.VMEM((2 * number, 2 * x.shape[-1]), BF16)],
        compiler_params=params(),
        cost_estimate=cost(1e9, 8e6),
        name="update",
    )(x, residual, d, vectors)


def join_kernel(x, other_x, residual, other_residual, base, full):
    group = lax.axis_index("groups")
    own = x[0] + 0.5 * residual[0]
    other = other_x[0] + 0.5 * other_residual[0]
    base[0] = join_halves(own, other, group)
    full[0] = join_halves(residual[0], other_residual[0], group)


def join(x, other_x, residual, other_residual):
    sites, rows, lanes = x.shape
    field = pl.BlockSpec((1, rows, lanes), lambda s: (s, 0, 0))
    wide = pl.BlockSpec((1, rows, 2 * lanes), lambda s: (s, 0, 0))
    shape = jax.ShapeDtypeStruct((sites, rows, 2 * lanes), F32)
    return pl.pallas_call(
        join_kernel,
        grid=(sites,),
        out_shape=(shape, shape),
        in_specs=[field, field, field, field],
        out_specs=(wide, wide),
        compiler_params=params(),
        cost_estimate=cost(1e6, 4e6),
        name="join",
    )(x, other_x, residual, other_residual)


def final_kernel(base, d, other_d, vectors, out, stacks):
    @pl.when(pl.program_id(0) == 0)
    def _():
        stacks[...] = stack(join_halves(d[...], other_d[...], lax.axis_index("groups")), 1.0)

    for site in range(vectors.shape[0]):
        out[site] = base[site] + expand(site, vectors, stacks)


def final(base, d, other_d, vectors):
    sites, rows, lanes = base.shape
    number = vectors.shape[-1]
    step = 2
    field = pl.BlockSpec((step, rows, lanes), lambda s: (s, 0, 0))
    small = pl.BlockSpec((number, lanes // 2), lambda s: (0, 0))
    return pl.pallas_call(
        final_kernel,
        grid=(sites // step,),
        out_shape=jax.ShapeDtypeStruct(base.shape, F32),
        in_specs=[field, small, small, pl.BlockSpec((step, 2, 2 * rows, number), lambda s: (s, 0, 0, 0))],
        out_specs=field,
        scratch_shapes=[pltpu.VMEM((2 * number, 2 * lanes), BF16)],
        compiler_params=params(),
        cost_estimate=cost(2e9, 8e6),
        name="final",
    )(base, d, other_d, vectors)


def shifted(value, axis, step):
    count = lax.axis_size(axis)
    return lax.ppermute(value, axis, [(i, (i + step) % count) for i in range(count)])


def crossed(value, axis, mask):
    count = lax.axis_size(axis)
    return lax.ppermute(value, axis, [(i, i ^ mask) for i in range(count)])


def faces_of(x):
    backward_t = shifted(x, "tm", 1)
    forward_t = shifted(x, "tm", -1)
    backward_z = shifted(x, "space", 1)
    forward_z = shifted(x, "space", -1)
    return forward_z, backward_z, forward_t, backward_t


def halving(keep, send):
    count = lax.axis_size("space")
    mask = 1
    while True:
        received = crossed(send, "space", mask)
        mask *= 2
        if mask >= count:
            return keep + received
        keep, send = add_split(keep, received)


def doubling(part, mask):
    while mask:
        part = jnp.concatenate([part, crossed(part, "space", mask)], axis=0)
        mask //= 2
    return part


def both_doubling(part):
    groups, count = lax.axis_size("groups"), lax.axis_size("space")
    mask = count // 2
    pairs = [(g * count + s, (g ^ 1) * count + (s ^ mask)) for g in range(groups) for s in range(count)]
    across = lax.ppermute(part, ("groups", "space"), pairs)
    other = jnp.concatenate([crossed(part, "groups", 1), across], axis=0)
    own = jnp.concatenate([part, crossed(part, "space", mask)], axis=0)
    mask //= 2
    while mask:
        rows = own.shape[0]
        received = crossed(jnp.concatenate([own, other], axis=0), "space", mask)
        own = jnp.concatenate([own, received[:rows]], axis=0)
        other = jnp.concatenate([other, received[rows:]], axis=0)
        mask //= 2
    return own, other


def over_time(part):
    count = lax.axis_size("tm")
    if count <= 4:
        return [part] + [shifted(part, "tm", step) for step in range(1, count)]
    mask = 1
    while mask < count:
        part = part + crossed(part, "tm", mask)
        mask *= 2
    return [part]


def shards(couplings, source, initial, vectors, inverse_eigen):
    directions = couplings.shape[0]
    ny, nx, rows, lanes = source.shape[2:]
    sites = ny * nx
    number = vectors.shape[0]
    blocks = lax.axis_size("space")

    x = pack(initial.reshape(sites, rows, lanes))
    faces = faces_of(x)
    matrices = couplings.reshape(directions, sites, rows, couplings.shape[-1])
    rest, half_source, local, halo = first_local(x, source.reshape(sites, rows, lanes), matrices, ny, nx)
    flat = vectors.reshape(number, sites * vectors.shape[-1])
    by_rows = by_rows_of(flat)
    size = number // blocks
    eigen = lax.dynamic_slice_in_dim(inverse_eigen, lax.axis_index("space") * size, size, 1)
    eigen = jnp.broadcast_to(eigen[:, :, None], (2, size, lanes // 2))

    for sweep in range(ITERS):
        last = sweep == ITERS - 1
        if sweep:
            faces = faces_of(x)
            if last:
                other_x = crossed(x, "groups", 1)
            rest = local_part(x, half_source, local, ny, nx)
        forward_z, backward_z, forward_t, backward_t = faces
        rest = z_faces(rest, forward_z, backward_z, halo)
        if sweep and last:
            rest, other_x = lax.optimization_barrier((rest, other_x))
        rest = backward_face(rest, backward_t, halo)
        residual, keep, send = forward_face(rest, forward_t, halo, by_rows)
        if sweep == 0:
            flat, send = lax.optimization_barrier((flat, send))
            by_columns = by_columns_of(flat, sites)
        d = scale(eigen, over_time(halving(keep, send)))
        if not last:
            x = update(x, residual, doubling(d, blocks // 2), by_columns)
    other_residual = crossed(residual, "groups", 1)
    base, full_residual = join(x, other_x, residual, other_residual)
    d, other_d = both_doubling(d)
    whole = final(base, d, other_d, by_columns)
    shape = source.shape
    return whole.reshape(shape), full_residual.reshape(shape)


def solution(mesh):
    in_specs = (
        P(None, "tm", "space", None, None, None, None),
        P("tm", "space", None, None, None, None),
        P("tm", "space", None, None, None, None),
        P(None, "tm", "space", None, None, None),
        P(),
    )
    out_specs = (
        P(("groups", "tm"), "space", None, None, None, None),
        P(("groups", "tm"), "space", None, None, None, None),
    )
    return jax.shard_map(shards, mesh=mesh, in_specs=in_specs, out_specs=out_specs, check_vma=False)
```

time: 138 us -> 126 us (0.913)
  Pallas kernels: 47.8 us -> 26.7 us
  local copies, waits for them, and re-layouts: 15.4 us -> 22.2 us
  waiting for transfers between devices: 40.1 us -> 43.4 us
  starting transfers between devices: 30.8 us -> 29.2 us
    pallas_call x5 -> x12, Pallas kernels: 27.1 us -> 12.4 us  [the longest x2 3.8 us: forward_face(): pl.pallas_call(forward_kernel, out_shape=(jax.ShapeDtypeStruct(rest.shape...]
    pallas_call x1, Pallas kernels: 8.78 us -> 4.61 us  [first_local(): pl.pallas_call(functools.partial(first_kernel, ny, nx), grid=(sites,), ou...]
    unnamed x33 -> x46, local copies, waits for them, and re-layouts: 11.3 us -> 15 us
    optimization_barrier x0 -> x1, local copies, waits for them, and re-layouts: none -> 3.64 us  [shards(): flat, send = lax.optimization_barrier((flat, send))]
    ppermute x14, waiting for transfers between devices: 20.5 us -> 23.1 us  [shifted(): lax.ppermute(value, axis, [(i, (i + step) % count) for i in range(count)])]
    ppermute x0 -> x1, starting transfers between devices: none -> 2.5 us  [both_doubling(): across = lax.ppermute(part, ('groups', 'space'), pairs)]
    ppermute x13 -> x11, starting transfers between devices: 10.9 us -> 8.76 us  [crossed(): return lax.ppermute(value, axis, [(i, i ^ mask) for i in range(count)])]
    ppermute x14, starting transfers between devices: 19.9 us -> 17.9 us  [shifted(): lax.ppermute(value, axis, [(i, (i + step) % count) for i in range(count)])]
  transfers between devices with their start and end apart: 27 -> 26, of which waited for: 15 -> 16; matrix products, arithmetic and copies ran while one was open for 3% -> 6% of each run, Pallas kernels for 15% -> 14%
where the time goes in v2:
time: 126 us; the launch traced here: 125 us
  waiting for transfers between devices  43.4 us (34%)
  starting transfers between devices  29.2 us (23%)
  Pallas kernels  26.7 us (21%)
  local copies, waits for them, and re-layouts  22.2 us (18%)
  other arithmetic  2.7 us (2%)
    ppermute x14, waiting for transfers between devices, shifted(): lax.ppermute(value, axis, [(i, (i + step) % count) for i in range(count)])  23.1 us
    ppermute x11, waiting for transfers between devices, crossed(): return lax.ppermute(value, axis, [(i, i ^ mask) for i in range(count)])  19.7 us
    ppermute x14, starting transfers between devices, shifted(): lax.ppermute(value, axis, [(i, (i + step) % count) for i in range(count)])  17.9 us
    unnamed x46, local copies, waits for them, and re-layouts  15 us
    ppermute x11, starting transfers between devices, crossed(): return lax.ppermute(value, axis, [(i, i ^ mask) for i in range(count)])  8.76 us
    pallas_call x1, Pallas kernels, first_local(): pl.pallas_call(functools.partial(first_kernel, ny, nx), grid=(sites,), ou...  4.61 us
    pallas_call x2, Pallas kernels, forward_face(): pl.pallas_call(forward_kernel, out_shape=(jax.ShapeDtypeStruct(rest.shape...  3.8 us
    optimization_barrier x1, local copies, waits for them, and re-layouts, shards(): flat, send = lax.optimization_barrier((flat, send))  3.64 us
  transfers between devices with their start and end apart: 26, of which 16 were waited for; matrix products, arithmetic and copies ran while one was open for 6% of the time, Pallas kernels for 14%

profile of v2, /device:TPU:0, one launch (start us, length us, event | category | flops | bytes accessed | tf_op | source)
XLA Modules:
  0.0 125.2 jit_solution(12517150801907866011)
XLA Ops:
  0.7 1.1 copy-done.7
  2.3 5.1 %collective-permute-start.3 = (f32[8,96,128]{2,1,0:T(8,128)S(1)}, f32[8,96,128]{2,1,0:T(8,128)}, u32[]{:S(2)}, u32[]{:S(2)}) collective-permute-start(f32[8,96,128]{2,1,0:T(8,128)S(1)} %pack.1.x_ref.x), channel_id=1, source_target_pairs={{0,3},{1,0},{2,1},{3,2},{4,7},{5,4},{6,5},{7,6},{8,11},{9,8},{10,9... | collective-permute-start | bytes 1179656 | tf_op jit(solution)/shard_map/ppermute | solution.py:458
  7.4 1.7 %collective-permute-start = (f32[8,96,128]{2,1,0:T(8,128)S(1)}, f32[8,96,128]{2,1,0:T(8,128)}, u32[]{:S(2)}, u32[]{:S(2)}) collective-permute-start(f32[8,96,128]{2,1,0:T(8,128)S(1)} %pack.1.x_ref.x), channel_id=1, source_target_pairs={{0,12},{4,0},{8,4},{12,8},{1,13},{5,1},{9,5},{13,9},{2,14},{6,2},{... | collective-permute-start | bytes 1179656 | tf_op jit(solution)/shard_map/ppermute | solution.py:458
  9.2 3.0 %copy-done.15 = f32[9,1,1,2,4,96,192]{6,5,4,3,2,1,0:T(8,128)S(1)} copy-done((f32[9,1,1,2,4,96,192]{6,5,4,3,2,1,0:T(8,128)S(1)}, f32[9,1,1,2,4,96,192]{6,5,4,3,2,1,0:T(8,128)}, u32[]{:S(2)}) %copy-start.15) | copy-done | bytes 5308440
  12.2 1.1 copy-done.16
  13.3 4.6 %first_local.1 = (f32[8,96,128]{2,1,0:T(8,128)S(1)}, f32[8,96,128]{2,1,0:T(8,128)S(1)}, bf16[5,8,192,192]{3,2,1,0:T(8,128)(2,1)S(1)}, bf16[4,8,192,192]{3,2,1,0:T(8,128)(2,1)S(1)}) custom-call(f32[8,96,128]{2,1,0:T(8,128)S(1)} %pack.1.x_ref.x, f32[8,96,256]{2,1,0:T(8,128)S(1)} %bitcast.8, f32[9,8,96,192]{3,2,1,0:T(8,128)S(1)} %bitcast.7), custom_call_target="tpu_custom_call" | custom-call | flops 8000000000 | bytes 16000000 | tf_op jit(solution)/shard_map/first_local/pallas_call | solution.py:140
  18.7 1.9 %copy-done.17 = bf16[5,8,192,192]{3,2,1,0:T(8,128)(2,1)} copy-done((bf16[5,8,192,192]{3,2,1,0:T(8,128)(2,1)}, bf16[5,8,192,192]{3,2,1,0:T(8,128)(2,1)S(1)}, u32[]{:S(2)}) %copy-start.17) | copy-done | bytes 2949144
  20.6 0.7 copy-done.19
  21.3 3.5 %copy.8.vectors = f32[512,1536]{1,0:T(8,128)} copy(f32[512,1536]{0,1:T(8,128)} %bitcast.9) | data formatting | bytes 6291456 | tf_op jit(solution)/shard_map/reshape | solution.py:531
  24.8 1.9 %copy-done.1 = f32[512,1536]{1,0:T(8,128)S(1)} copy-done((f32[512,1536]{1,0:T(8,128)S(1)}, f32[512,1536]{1,0:T(8,128)}, u32[]{:S(2)}) %copy-start.1) | copy-done | bytes 3145752
  27.7 2.4 %z_faces.2.rest = f32[8,96,128]{2,1,0:T(8,128)S(1)} custom-call(f32[8,96,128]{2,1,0:T(8,128)S(1)} %copy-done.13, f32[8,96,128]{2,1,0:T(8,128)} %collective-permute-done.forward, f32[8,96,128]{2,1,0:T(8,128)} %collective-permute-done.1.backward, bf16[4,8,192,192]{3,2,1,0:T(8,128)(2,1)S(1)} %get-tuple-element.23.matrix), custom_call_target="tpu_custom_call" | custom-call | flops 1000000000 | bytes 4000000 | tf_op jit(solution)/shard_map/z_faces/pallas_call | solution.py:274
  30.1 1.4 %backward_face.2.rest = f32[8,96,128]{2,1,0:T(8,128)S(1)} custom-call(f32[8,96,128]{2,1,0:T(8,128)S(1)} %z_faces.2.rest, f32[8,96,128]{2,1,0:T(8,128)} %collective-permute-done.2.backward, bf16[4,8,192,192]{3,2,1,0:T(8,128)(2,1)S(1)} %get-tuple-element.23.matrix), custom_call_target="tpu_custom_call" | custom-call | flops 1000000000 | bytes 4000000 | tf_op jit(solution)/shard_map/backward_face/pallas_call | solution.py:297
  31.6 2.4 %forward_face.2 = (f32[8,96,128]{2,1,0:T(8,128)S(1)}, f32[256,128]{1,0:T(8,128)S(1)}, f32[256,128]{1,0:T(8,128)S(1)}) custom-call(f32[8,96,128]{2,1,0:T(8,128)S(1)} %backward_face.2.rest, f32[8,96,128]{2,1,0:T(8,128)} %collective-permute-done.3.forward, bf16[4,8,192,192]{3,2,1,0:T(8,128)(2,1)S(1)} %get-tuple-element.23.matrix, ...), custom_call_target="tpu_custom_call" | custom-call | flops 2000000000 | bytes 8000000 | tf_op jit(solution)/shard_map/forward_face/pallas_call | solution.py:324
  34.7 1.3 %collective-permute-done.4.received = f32[256,128]{1,0:T(8,128)S(1)} collective-permute-done((f32[256,128]{1,0:T(8,128)S(1)}, f32[256,128]{1,0:T(8,128)S(1)}, u32[]{:S(2)}, u32[]{:S(2)}) %collective-permute-start.4) | collective-permute-done | bytes 131104 | tf_op jit(solution)/shard_map/ppermute | solution.py:463
  37.3 1.5 %collective-permute-start.5 = (f32[128,128]{1,0:T(8,128)}, f32[128,128]{1,0:T(8,128)}, u32[]{:S(2)}, u32[]{:S(2)}) collective-permute-start(f32[128,128]{1,0:T(8,128)} %get-tuple-element.29), channel_id=1, source_target_pairs={{0,8},{4,12},{8,0},{12,4},{1,9},{5,13},{9,1},{13,5},{2,10},{6,14},... | collective-permute-start | bytes 196616 | tf_op jit(solution)/shard_map/ppermute | solution.py:463
  38.8 3.1 %collective-permute-done.5 = f32[128,128]{1,0:T(8,128)} collective-permute-done((f32[128,128]{1,0:T(8,128)}, f32[128,128]{1,0:T(8,128)}, u32[]{:S(2)}, u32[]{:S(2)}) %collective-permute-start.5) | collective-permute-done | bytes 65568 | tf_op jit(solution)/shard_map/ppermute | solution.py:463
  41.9 0.9 add.10.refs_0_
  42.8 3.9 %collective-permute-start.8 = (f32[128,128]{1,0:T(8,128)S(1)}, f32[128,128]{1,0:T(8,128)S(1)}, u32[]{:S(2)}, u32[]{:S(2)}) collective-permute-start(f32[128,128]{1,0:T(8,128)S(1)} %add.10.refs_0_), channel_id=1, source_target_pairs={{0,3},{1,0},{2,1},{3,2},{4,7},{5,4},{6,5},{7,6},{8,11},{9,8},{10,9... | collective-permute-start | bytes 196616 | tf_op jit(solution)/shard_map/ppermute | solution.py:458
  47.3 1.3 %collective-permute-done.8.refs_3_ = f32[128,128]{1,0:T(8,128)S(1)} collective-permute-done((f32[128,128]{1,0:T(8,128)S(1)}, f32[128,128]{1,0:T(8,128)S(1)}, u32[]{:S(2)}, u32[]{:S(2)}) %collective-permute-start.8) | collective-permute-done | bytes 65568 | tf_op jit(solution)/shard_map/ppermute | solution.py:458
  48.6 3.2 %collective-permute-done.7.refs_2_ = f32[128,128]{1,0:T(8,128)S(1)} collective-permute-done((f32[128,128]{1,0:T(8,128)S(1)}, f32[128,128]{1,0:T(8,128)S(1)}, u32[]{:S(2)}, u32[]{:S(2)}) %collective-permute-start.7) | collective-permute-done | bytes 65568 | tf_op jit(solution)/shard_map/ppermute | solution.py:458
  51.8 0.9 collective-permute-done.6.refs_1_
  53.6 1.5 %collective-permute-start.9 = (f32[128,128]{1,0:T(8,128)S(1)}, f32[128,128]{1,0:T(8,128)S(1)}, u32[]{:S(2)}, u32[]{:S(2)}) collective-permute-start(f32[128,128]{1,0:T(8,128)S(1)} %scale.2), channel_id=1, source_target_pairs={{0,8},{4,12},{8,0},{12,4},{1,9},{5,13},{9,1},{13,5},{2,10},{6,14},... | collective-permute-start | bytes 196616 | tf_op jit(solution)/shard_map/ppermute | solution.py:463
  55.1 2.8 %collective-permute-done.9 = f32[128,128]{1,0:T(8,128)S(1)} collective-permute-done((f32[128,128]{1,0:T(8,128)S(1)}, f32[128,128]{1,0:T(8,128)S(1)}, u32[]{:S(2)}, u32[]{:S(2)}) %collective-permute-start.9) | collective-permute-done | bytes 65568 | tf_op jit(solution)/shard_map/ppermute | solution.py:463
  58.6 3.6 %copy.9.vectors = f32[512,1536]{1,0:T(8,128)} copy(f32[512,1536]{0,1:T(8,128)} %bitcast.10) | data formatting | bytes 6291456 | tf_op jit(solution)/shard_map/optimization_barrier | solution.py:551
  62.2 1.9 %copy-done.2 = f32[512,1536]{1,0:T(8,128)S(1)} copy-done((f32[512,1536]{1,0:T(8,128)S(1)}, f32[512,1536]{1,0:T(8,128)}, u32[]{:S(2)}) %copy-start.2) | copy-done | bytes 3145752
  64.1 0.9 by_columns.1.vectors
  65.0 1.1 pad_maximum_fusion.d
  66.1 1.1 update.1.x_ref.x
  67.2 1.5 %collective-permute-start.15 = (f32[8,96,128]{2,1,0:T(8,128)S(1)}, f32[8,96,128]{2,1,0:T(8,128)S(1)}, u32[]{:S(2)}, u32[]{:S(2)}) collective-permute-start(f32[8,96,128]{2,1,0:T(8,128)S(1)} %update.1.x_ref.x), channel_id=1, source_target_pairs={{0,3},{1,0},{2,1},{3,2},{4,7},{5,4},{6,5},{7,6},{8,11},{9,8},{10,9... | collective-permute-start | bytes 1179656 | tf_op jit(solution)/shard_map/ppermute | solution.py:458
  69.3 1.5 %collective-permute-start.13 = (f32[8,96,128]{2,1,0:T(8,128)S(1)}, f32[8,96,128]{2,1,0:T(8,128)S(1)}, u32[]{:S(2)}, u32[]{:S(2)}) collective-permute-start(f32[8,96,128]{2,1,0:T(8,128)S(1)} %update.1.x_ref.x), channel_id=1, source_target_pairs={{0,16},{16,0},{1,17},{17,1},{2,18},{18,2},{3,19},{19,3},{4,20},{20... | collective-permute-start | bytes 1179656 | tf_op jit(solution)/shard_map/ppermute | solution.py:463
  70.8 1.7 %collective-permute-start.11 = (f32[8,96,128]{2,1,0:T(8,128)S(1)}, f32[8,96,128]{2,1,0:T(8,128)S(1)}, u32[]{:S(2)}, u32[]{:S(2)}) collective-permute-start(f32[8,96,128]{2,1,0:T(8,128)S(1)} %update.1.x_ref.x), channel_id=1, source_target_pairs={{0,12},{4,0},{8,4},{12,8},{1,13},{5,1},{9,5},{13,9},{2,14},{6,2},{... | collective-permute-start | bytes 1179656 | tf_op jit(solution)/shard_map/ppermute | solution.py:458
  72.6 3.0 %local_part.1.rest = f32[8,96,128]{2,1,0:T(8,128)S(1)} custom-call(f32[8,96,128]{2,1,0:T(8,128)S(1)} %update.1.x_ref.x, f32[8,96,128]{2,1,0:T(8,128)S(1)} %copy-done.20, bf16[5,8,192,192]{3,2,1,0:T(8,128)(2,1)S(1)} %copy-done.18), custom_call_target="tpu_custom_call" | custom-call | flops 8000000000 | bytes 8000000 | tf_op jit(solution)/shard_map/local_part/pallas_call | solution.py:175
  75.5 4.8 %collective-permute-done.12.backward = f32[8,96,128]{2,1,0:T(8,128)S(1)} collective-permute-done((f32[8,96,128]{2,1,0:T(8,128)S(1)}, f32[8,96,128]{2,1,0:T(8,128)S(1)}, u32[]{:S(2)}, u32[]{:S(2)}) %collective-permute-start.12) | collective-permute-done | bytes 393248 | tf_op jit(solution)/shard_map/ppermute | solution.py:458
  80.4 0.9 collective-permute-done.11.forward
  82.0 6.1 %collective-permute-done.14.backward = f32[8,96,128]{2,1,0:T(8,128)S(1)} collective-permute-done((f32[8,96,128]{2,1,0:T(8,128)S(1)}, f32[8,96,128]{2,1,0:T(8,128)S(1)}, u32[]{:S(2)}, u32[]{:S(2)}) %collective-permute-start.14) | collective-permute-done | bytes 393248 | tf_op jit(solution)/shard_map/ppermute | solution.py:458
  88.5 1.4 %forward_face.3 = (f32[8,96,128]{2,1,0:T(8,128)S(1)}, f32[256,128]{1,0:T(8,128)S(1)}, f32[256,128]{1,0:T(8,128)S(1)}) custom-call(f32[8,96,128]{2,1,0:T(8,128)S(1)} %backward_face.3.rest, f32[8,96,128]{2,1,0:T(8,128)S(1)} %collective-permute-done.15.forward, bf16[4,8,192,192]{3,2,1,0:T(8,128)(2,1)S(1)} %get-tuple-element.23.matrix, ...), custom_call_target="tpu_custom_call" | custom-call | flops 2000000000 | bytes 8000000 | tf_op jit(solution)/shard_map/forward_face/pallas_call | solution.py:324
  90.0 1.3 %collective-permute-done.17.received = f32[256,128]{1,0:T(8,128)S(1)} collective-permute-done((f32[256,128]{1,0:T(8,128)S(1)}, f32[256,128]{1,0:T(8,128)S(1)}, u32[]{:S(2)}, u32[]{:S(2)}) %collective-permute-start.17) | collective-permute-done | bytes 131104 | tf_op jit(solution)/shard_map/ppermute | solution.py:463
  91.3 1.5 %collective-permute-start.18 = (f32[128,128]{1,0:T(8,128)S(1)}, f32[128,128]{1,0:T(8,128)S(1)}, u32[]{:S(2)}, u32[]{:S(2)}) collective-permute-start(f32[128,128]{1,0:T(8,128)S(1)} %get-tuple-element.40), channel_id=1, source_target_pairs={{0,8},{4,12},{8,0},{12,4},{1,9},{5,13},{9,1},{13,5},{2,10},{6,14},... | collective-permute-start | bytes 196616 | tf_op jit(solution)/shard_map/ppermute | solution.py:463
  92.9 2.8 %collective-permute-done.18 = f32[128,128]{1,0:T(8,128)S(1)} collective-permute-done((f32[128,128]{1,0:T(8,128)S(1)}, f32[128,128]{1,0:T(8,128)S(1)}, u32[]{:S(2)}, u32[]{:S(2)}) %collective-permute-start.18) | collective-permute-done | bytes 65568 | tf_op jit(solution)/shard_map/ppermute | solution.py:463
  95.7 1.8 %collective-permute-start.21 = (f32[128,128]{1,0:T(8,128)S(1)}, f32[128,128]{1,0:T(8,128)S(1)}, u32[]{:S(2)}, u32[]{:S(2)}) collective-permute-start(f32[128,128]{1,0:T(8,128)S(1)} %add.11.refs_0_), channel_id=1, source_target_pairs={{0,3},{1,0},{2,1},{3,2},{4,7},{5,4},{6,5},{7,6},{8,11},{9,8},{10,9... | collective-permute-start | bytes 196616 | tf_op jit(solution)/shard_map/ppermute | solution.py:458
  98.4 1.7 %collective-permute-done.21.refs_3_ = f32[128,128]{1,0:T(8,128)S(1)} collective-permute-done((f32[128,128]{1,0:T(8,128)S(1)}, f32[128,128]{1,0:T(8,128)S(1)}, u32[]{:S(2)}, u32[]{:S(2)}) %collective-permute-start.21) | collective-permute-done | bytes 65568 | tf_op jit(solution)/shard_map/ppermute | solution.py:458
  100.1 4.2 %collective-permute-done.20.refs_2_ = f32[128,128]{1,0:T(8,128)S(1)} collective-permute-done((f32[128,128]{1,0:T(8,128)S(1)}, f32[128,128]{1,0:T(8,128)S(1)}, u32[]{:S(2)}, u32[]{:S(2)}) %collective-permute-start.20) | collective-permute-done | bytes 65568 | tf_op jit(solution)/shard_map/ppermute | solution.py:458
  104.5 2.5 %collective-permute-start.24 = (f32[128,128]{1,0:T(8,128)S(1)}, f32[128,128]{1,0:T(8,128)S(1)}, u32[]{:S(2)}, u32[]{:S(2)}) collective-permute-start(f32[128,128]{1,0:T(8,128)S(1)} %scale.3), channel_id=1, source_target_pairs={{0,24},{4,28},{8,16},{12,20},{16,8},{20,12},{24,0},{28,4},{1,25},{... | collective-permute-start | bytes 196616 | tf_op jit(solution)/shard_map/ppermute | solution.py:496
  108.0 1.5 %collective-permute-start.16 = (f32[8,96,128]{2,1,0:T(8,128)S(1)}, f32[8,96,128]{2,1,0:T(8,128)S(1)}, u32[]{:S(2)}, u32[]{:S(2)}) collective-permute-start(f32[8,96,128]{2,1,0:T(8,128)S(1)} %get-tuple-element.35.residual), channel_id=1, source_target_pairs={{0,16},{16,0},{1,17},{17,1},{2,18},{18,2},{3,19},{19,3},{4,20},{20... | collective-permute-start | bytes 1179656 | tf_op jit(solution)/shard_map/ppermute | solution.py:463
  110.1 1.9 %collective-permute-done.23 = f32[128,128]{1,0:T(8,128)S(1)} collective-permute-done((f32[128,128]{1,0:T(8,128)S(1)}, f32[128,128]{1,0:T(8,128)S(1)}, u32[]{:S(2)}, u32[]{:S(2)}) %collective-permute-start.23) | collective-permute-done | bytes 65568 | tf_op jit(solution)/shard_map/ppermute | solution.py:463
  112.1 6.5 %collective-permute-done.16.other_residual = f32[8,96,128]{2,1,0:T(8,128)S(1)} collective-permute-done((f32[8,96,128]{2,1,0:T(8,128)S(1)}, f32[8,96,128]{2,1,0:T(8,128)S(1)}, u32[]{:S(2)}, u32[]{:S(2)}) %collective-permute-start.16) | collective-permute-done | bytes 393248 | tf_op jit(solution)/shard_map/ppermute | solution.py:463
  118.6 3.2 %join.1 = (f32[8,96,256]{2,1,0:T(8,128)S(1)}, f32[8,96,256]{2,1,0:T(8,128)}) custom-call(f32[8,96,128]{2,1,0:T(8,128)S(1)} %update.1.x_ref.x, f32[8,96,128]{2,1,0:T(8,128)S(1)} %collective-permute-done.13.other_x, f32[8,96,128]{2,1,0:T(8,128)S(1)} %get-tuple-element.35.residual, f32[8,96,128]{2,1,0:T(8,128)S(1)} %collective-permute-done.16.other_residual), custom_call_target="tpu_custom_call" | custom-call | flops 1000000 | bytes 4000000 | tf_op jit(solution)/shard_map/join/pallas_call | solution.py:416
  121.9 3.4 %final.1 = f32[8,96,256]{2,1,0:T(8,128)} custom-call(f32[8,96,256]{2,1,0:T(8,128)S(1)} %get-tuple-element.36.base, f32[512,128]{1,0:T(8,128)S(1)} %get-tuple-element.44.d, f32[512,128]{1,0:T(8,128)S(1)} %get-tuple-element.45.other_d, bf16[8,2,192,512]{3,2,1,0:T(8,128)(2,1)S(1)} %by_columns.1.vectors), custom_call_target="tpu_custom_call" | custom-call | flops 2000000000 | bytes 8000000 | tf_op jit(solution)/shard_map/final/pallas_call | solution.py:443
  (79 shorter events, 11.1 us)
Async XLA Ops:
  0.6 46.7 %copy-start = (f32[2,512]{1,0:T(2,128)S(1)}, f32[2,512]{1,0:T(2,128)}, u32[]{:S(2)}) copy-start(f32[2,512]{1,0:T(2,128)} %param.9) | copy-start | bytes 12292
  0.6 1.1 copy-start.7
  2.3 29.2 %collective-permute-start.3 = (f32[8,96,128]{2,1,0:T(8,128)S(1)}, f32[8,96,128]{2,1,0:T(8,128)}, u32[]{:S(2)}, u32[]{:S(2)}) collective-permute-start(f32[8,96,128]{2,1,0:T(8,128)S(1)} %pack.1.x_ref.x), channel_id=1, source_target_pairs={{0,3},{1,0},{2,1},{3,2},{4,7},{5,4},{6,5},{7,6},{8,11},{9,8},{10,9... | collective-permute-start | bytes 1179656 | tf_op jit(solution)/shard_map/ppermute | solution.py:458
  7.4 22.7 %collective-permute-start.2 = (f32[8,96,128]{2,1,0:T(8,128)S(1)}, f32[8,96,128]{2,1,0:T(8,128)}, u32[]{:S(2)}, u32[]{:S(2)}) collective-permute-start(f32[8,96,128]{2,1,0:T(8,128)S(1)} %pack.1.x_ref.x), channel_id=1, source_target_pairs={{0,1},{1,2},{2,3},{3,0},{4,5},{5,6},{6,7},{7,4},{8,9},{9,10},{10,1... | collective-permute-start | bytes 1179656 | tf_op jit(solution)/shard_map/ppermute | solution.py:458
  7.4 19.8 %collective-permute-start.1 = (f32[8,96,128]{2,1,0:T(8,128)S(1)}, f32[8,96,128]{2,1,0:T(8,128)}, u32[]{:S(2)}, u32[]{:S(2)}) collective-permute-start(f32[8,96,128]{2,1,0:T(8,128)S(1)} %pack.1.x_ref.x), channel_id=1, source_target_pairs={{0,4},{4,8},{8,12},{12,0},{1,5},{5,9},{9,13},{13,1},{2,6},{6,10},{... | collective-permute-start | bytes 1179656 | tf_op jit(solution)/shard_map/ppermute | solution.py:458
  7.4 19.8 %collective-permute-start = (f32[8,96,128]{2,1,0:T(8,128)S(1)}, f32[8,96,128]{2,1,0:T(8,128)}, u32[]{:S(2)}, u32[]{:S(2)}) collective-permute-start(f32[8,96,128]{2,1,0:T(8,128)S(1)} %pack.1.x_ref.x), channel_id=1, source_target_pairs={{0,12},{4,0},{8,4},{12,8},{1,13},{5,1},{9,5},{13,9},{2,14},{6,2},{... | collective-permute-start | bytes 1179656 | tf_op jit(solution)/shard_map/ppermute | solution.py:458
  9.2 3.0 %copy-start.15 = (f32[9,1,1,2,4,96,192]{6,5,4,3,2,1,0:T(8,128)S(1)}, f32[9,1,1,2,4,96,192]{6,5,4,3,2,1,0:T(8,128)}, u32[]{:S(2)}) copy-start(f32[9,1,1,2,4,96,192]{6,5,4,3,2,1,0:T(8,128)} %param.5) | copy-start | bytes 15925252
  12.2 1.1 copy-start.16
  17.9 0.7 copy-start.12
  18.7 1.9 %copy-start.17 = (bf16[5,8,192,192]{3,2,1,0:T(8,128)(2,1)}, bf16[5,8,192,192]{3,2,1,0:T(8,128)(2,1)S(1)}, u32[]{:S(2)}) copy-start(bf16[5,8,192,192]{3,2,1,0:T(8,128)(2,1)S(1)} %get-tuple-element.32.local) | copy-start | bytes 8847364
  20.6 0.7 copy-start.19
  24.8 1.9 %copy-start.1 = (f32[512,1536]{1,0:T(8,128)S(1)}, f32[512,1536]{1,0:T(8,128)}, u32[]{:S(2)}) copy-start(f32[512,1536]{1,0:T(8,128)} %copy.8.vectors) | copy-start | bytes 9437188
  26.7 1.0 copy-start.13
  27.2 4.3 %copy-start.3 = (bf16[1024,1536]{1,0:T(8,128)(2,1)}, bf16[1024,1536]{1,0:T(8,128)(2,1)S(1)}, u32[]{:S(2)}) copy-start(bf16[1024,1536]{1,0:T(8,128)(2,1)S(1)} %by_rows.1.vectors) | copy-start | bytes 9437188
  34.0 0.7 copy-start.10
  34.7 1.3 %collective-permute-start.4 = (f32[256,128]{1,0:T(8,128)S(1)}, f32[256,128]{1,0:T(8,128)S(1)}, u32[]{:S(2)}, u32[]{:S(2)}) collective-permute-start(f32[256,128]{1,0:T(8,128)S(1)} %get-tuple-element.27), channel_id=1, source_target_pairs={{0,4},{4,0},{8,12},{12,8},{1,5},{5,1},{9,13},{13,9},{2,6},{6,2},{1... | collective-permute-start | bytes 393224 | tf_op jit(solution)/shard_map/ppermute | solution.py:463
  37.3 4.6 %collective-permute-start.5 = (f32[128,128]{1,0:T(8,128)}, f32[128,128]{1,0:T(8,128)}, u32[]{:S(2)}, u32[]{:S(2)}) collective-permute-start(f32[128,128]{1,0:T(8,128)} %get-tuple-element.29), channel_id=1, source_target_pairs={{0,8},{4,12},{8,0},{12,4},{1,9},{5,13},{9,1},{13,5},{2,10},{6,14},... | collective-permute-start | bytes 196616 | tf_op jit(solution)/shard_map/ppermute | solution.py:463
  42.8 5.8 %collective-permute-start.8 = (f32[128,128]{1,0:T(8,128)S(1)}, f32[128,128]{1,0:T(8,128)S(1)}, u32[]{:S(2)}, u32[]{:S(2)}) collective-permute-start(f32[128,128]{1,0:T(8,128)S(1)} %add.10.refs_0_), channel_id=1, source_target_pairs={{0,3},{1,0},{2,1},{3,2},{4,7},{5,4},{6,5},{7,6},{8,11},{9,8},{10,9... | collective-permute-start | bytes 196616 | tf_op jit(solution)/shard_map/ppermute | solution.py:458
  46.7 5.2 %collective-permute-start.7 = (f32[128,128]{1,0:T(8,128)S(1)}, f32[128,128]{1,0:T(8,128)S(1)}, u32[]{:S(2)}, u32[]{:S(2)}) collective-permute-start(f32[128,128]{1,0:T(8,128)S(1)} %add.10.refs_0_), channel_id=1, source_target_pairs={{0,2},{1,3},{2,0},{3,1},{4,6},{5,7},{6,4},{7,5},{8,10},{9,11},{10,... | collective-permute-start | bytes 196616 | tf_op jit(solution)/shard_map/ppermute | solution.py:458
  46.7 6.1 %collective-permute-start.6 = (f32[128,128]{1,0:T(8,128)S(1)}, f32[128,128]{1,0:T(8,128)S(1)}, u32[]{:S(2)}, u32[]{:S(2)}) collective-permute-start(f32[128,128]{1,0:T(8,128)S(1)} %add.10.refs_0_), channel_id=1, source_target_pairs={{0,1},{1,2},{2,3},{3,0},{4,5},{5,6},{6,7},{7,4},{8,9},{9,10},{10,1... | collective-permute-start | bytes 196616 | tf_op jit(solution)/shard_map/ppermute | solution.py:458
  52.9 0.7 copy-start.5
  53.6 4.3 %copy-start.8 = (f32[128,128]{1,0:T(8,128)}, f32[128,128]{1,0:T(8,128)S(1)}, u32[]{:S(2)}) copy-start(f32[128,128]{1,0:T(8,128)S(1)} %scale.2) | copy-start | bytes 196612
  53.6 4.3 %collective-permute-start.9 = (f32[128,128]{1,0:T(8,128)S(1)}, f32[128,128]{1,0:T(8,128)S(1)}, u32[]{:S(2)}, u32[]{:S(2)}) collective-permute-start(f32[128,128]{1,0:T(8,128)S(1)} %scale.2), channel_id=1, source_target_pairs={{0,8},{4,12},{8,0},{12,4},{1,9},{5,13},{9,1},{13,5},{2,10},{6,14},... | collective-permute-start | bytes 196616 | tf_op jit(solution)/shard_map/ppermute | solution.py:463
  57.9 0.7 copy-start.21
  58.6 6.4 %collective-permute-start.10 = (f32[256,128]{1,0:T(8,128)}, f32[256,128]{1,0:T(8,128)}, u32[]{:S(2)}, u32[]{:S(2)}) collective-permute-start(f32[256,128]{1,0:T(8,128)} %pad_maximum_fusion.5), channel_id=1, source_target_pairs={{0,4},{4,0},{8,12},{12,8},{1,5},{5,1},{9,13},{13,9},{2,6},{6,2},{1... | collective-permute-start | bytes 393224 | tf_op jit(solution)/shard_map/ppermute | solution.py:463
  62.2 1.9 %copy-start.2 = (f32[512,1536]{1,0:T(8,128)S(1)}, f32[512,1536]{1,0:T(8,128)}, u32[]{:S(2)}) copy-start(f32[512,1536]{1,0:T(8,128)} %copy.9.vectors) | copy-start | bytes 9437188
  64.1 0.9 copy-start.9
  64.1 0.9 copy-start.22
  64.1 2.0 %copy-start.11 = (f32[8,96,128]{2,1,0:T(8,128)S(1)}, f32[8,96,128]{2,1,0:T(8,128)}, u32[]{:S(2)}) copy-start(f32[8,96,128]{2,1,0:T(8,128)} %copy-done.10) | copy-start | bytes 1179652
  65.0 7.6 %copy-start.18 = (bf16[5,8,192,192]{3,2,1,0:T(8,128)(2,1)S(1)}, bf16[5,8,192,192]{3,2,1,0:T(8,128)(2,1)}, u32[]{:S(2)}) copy-start(bf16[5,8,192,192]{3,2,1,0:T(8,128)(2,1)} %copy-done.17) | copy-start | bytes 8847364
  65.0 7.6 %copy-start.20 = (f32[8,96,128]{2,1,0:T(8,128)S(1)}, f32[8,96,128]{2,1,0:T(8,128)}, u32[]{:S(2)}) copy-start(f32[8,96,128]{2,1,0:T(8,128)} %copy-done.19) | copy-start | bytes 1179652
  67.2 21.3 %collective-permute-start.15 = (f32[8,96,128]{2,1,0:T(8,128)S(1)}, f32[8,96,128]{2,1,0:T(8,128)S(1)}, u32[]{:S(2)}, u32[]{:S(2)}) collective-permute-start(f32[8,96,128]{2,1,0:T(8,128)S(1)} %update.1.x_ref.x), channel_id=1, source_target_pairs={{0,3},{1,0},{2,1},{3,2},{4,7},{5,4},{6,5},{7,6},{8,11},{9,8},{10,9... | collective-permute-start | bytes 1179656 | tf_op jit(solution)/shard_map/ppermute | solution.py:458
  68.7 19.3 %collective-permute-start.14 = (f32[8,96,128]{2,1,0:T(8,128)S(1)}, f32[8,96,128]{2,1,0:T(8,128)S(1)}, u32[]{:S(2)}, u32[]{:S(2)}) collective-permute-start(f32[8,96,128]{2,1,0:T(8,128)S(1)} %update.1.x_ref.x), channel_id=1, source_target_pairs={{0,1},{1,2},{2,3},{3,0},{4,5},{5,6},{6,7},{7,4},{8,9},{9,10},{10,1... | collective-permute-start | bytes 1179656 | tf_op jit(solution)/shard_map/ppermute | solution.py:458
  69.3 12.6 %collective-permute-start.13 = (f32[8,96,128]{2,1,0:T(8,128)S(1)}, f32[8,96,128]{2,1,0:T(8,128)S(1)}, u32[]{:S(2)}, u32[]{:S(2)}) collective-permute-start(f32[8,96,128]{2,1,0:T(8,128)S(1)} %update.1.x_ref.x), channel_id=1, source_target_pairs={{0,16},{16,0},{1,17},{17,1},{2,18},{18,2},{3,19},{19,3},{4,20},{20... | collective-permute-start | bytes 1179656 | tf_op jit(solution)/shard_map/ppermute | solution.py:463
  70.8 9.6 %collective-permute-start.12 = (f32[8,96,128]{2,1,0:T(8,128)S(1)}, f32[8,96,128]{2,1,0:T(8,128)S(1)}, u32[]{:S(2)}, u32[]{:S(2)}) collective-permute-start(f32[8,96,128]{2,1,0:T(8,128)S(1)} %update.1.x_ref.x), channel_id=1, source_target_pairs={{0,4},{4,8},{8,12},{12,0},{1,5},{5,9},{9,13},{13,1},{2,6},{6,10},{... | collective-permute-start | bytes 1179656 | tf_op jit(solution)/shard_map/ppermute | solution.py:458
  70.8 10.4 %collective-permute-start.11 = (f32[8,96,128]{2,1,0:T(8,128)S(1)}, f32[8,96,128]{2,1,0:T(8,128)S(1)}, u32[]{:S(2)}, u32[]{:S(2)}) collective-permute-start(f32[8,96,128]{2,1,0:T(8,128)S(1)} %update.1.x_ref.x), channel_id=1, source_target_pairs={{0,12},{4,0},{8,4},{12,8},{1,13},{5,1},{9,5},{13,9},{2,14},{6,2},{... | collective-permute-start | bytes 1179656 | tf_op jit(solution)/shard_map/ppermute | solution.py:458
  81.9 6.6 %copy-start.4 = (bf16[1024,1536]{1,0:T(8,128)(2,1)S(1)}, bf16[1024,1536]{1,0:T(8,128)(2,1)}, u32[]{:S(2)}) copy-start(bf16[1024,1536]{1,0:T(8,128)(2,1)} %copy-done.3) | copy-start | bytes 9437188
  88.5 15.9 %copy-start.6 = (f32[2,128,128]{2,1,0:T(8,128)S(1)}, f32[2,128,128]{2,1,0:T(8,128)}, u32[]{:S(2)}) copy-start(f32[2,128,128]{2,1,0:T(8,128)} %copy-done.5) | copy-start | bytes 393220
  89.9 1.4 %collective-permute-start.17 = (f32[256,128]{1,0:T(8,128)S(1)}, f32[256,128]{1,0:T(8,128)S(1)}, u32[]{:S(2)}, u32[]{:S(2)}) collective-permute-start(f32[256,128]{1,0:T(8,128)S(1)} %get-tuple-element.38), channel_id=1, source_target_pairs={{0,4},{4,0},{8,12},{12,8},{1,5},{5,1},{9,13},{13,9},{2,6},{6,2},{1... | collective-permute-start | bytes 393224 | tf_op jit(solution)/shard_map/ppermute | solution.py:463
  91.3 4.3 %collective-permute-start.18 = (f32[128,128]{1,0:T(8,128)S(1)}, f32[128,128]{1,0:T(8,128)S(1)}, u32[]{:S(2)}, u32[]{:S(2)}) collective-permute-start(f32[128,128]{1,0:T(8,128)S(1)} %get-tuple-element.40), channel_id=1, source_target_pairs={{0,8},{4,12},{8,0},{12,4},{1,9},{5,13},{9,1},{13,5},{2,10},{6,14},... | collective-permute-start | bytes 196616 | tf_op jit(solution)/shard_map/ppermute | solution.py:463
  95.7 4.4 %collective-permute-start.21 = (f32[128,128]{1,0:T(8,128)S(1)}, f32[128,128]{1,0:T(8,128)S(1)}, u32[]{:S(2)}, u32[]{:S(2)}) collective-permute-start(f32[128,128]{1,0:T(8,128)S(1)} %add.11.refs_0_), channel_id=1, source_target_pairs={{0,3},{1,0},{2,1},{3,2},{4,7},{5,4},{6,5},{7,6},{8,11},{9,8},{10,9... | collective-permute-start | bytes 196616 | tf_op jit(solution)/shard_map/ppermute | solution.py:458
  97.5 6.9 %collective-permute-start.20 = (f32[128,128]{1,0:T(8,128)S(1)}, f32[128,128]{1,0:T(8,128)S(1)}, u32[]{:S(2)}, u32[]{:S(2)}) collective-permute-start(f32[128,128]{1,0:T(8,128)S(1)} %add.11.refs_0_), channel_id=1, source_target_pairs={{0,2},{1,3},{2,0},{3,1},{4,6},{5,7},{6,4},{7,5},{8,10},{9,11},{10,... | collective-permute-start | bytes 196616 | tf_op jit(solution)/shard_map/ppermute | solution.py:458
  97.9 6.4 %collective-permute-start.19 = (f32[128,128]{1,0:T(8,128)S(1)}, f32[128,128]{1,0:T(8,128)S(1)}, u32[]{:S(2)}, u32[]{:S(2)}) collective-permute-start(f32[128,128]{1,0:T(8,128)S(1)} %add.11.refs_0_), channel_id=1, source_target_pairs={{0,1},{1,2},{2,3},{3,0},{4,5},{5,6},{6,7},{7,4},{8,9},{9,10},{10,1... | collective-permute-start | bytes 196616 | tf_op jit(solution)/shard_map/ppermute | solution.py:458
  104.5 5.7 %collective-permute-start.24 = (f32[128,128]{1,0:T(8,128)S(1)}, f32[128,128]{1,0:T(8,128)S(1)}, u32[]{:S(2)}, u32[]{:S(2)}) collective-permute-start(f32[128,128]{1,0:T(8,128)S(1)} %scale.3), channel_id=1, source_target_pairs={{0,24},{4,28},{8,16},{12,20},{16,8},{20,12},{24,0},{28,4},{1,25},{... | collective-permute-start | bytes 196616 | tf_op jit(solution)/shard_map/ppermute | solution.py:496
  107.0 5.0 %collective-permute-start.23 = (f32[128,128]{1,0:T(8,128)S(1)}, f32[128,128]{1,0:T(8,128)S(1)}, u32[]{:S(2)}, u32[]{:S(2)}) collective-permute-start(f32[128,128]{1,0:T(8,128)S(1)} %scale.3), channel_id=1, source_target_pairs={{0,16},{16,0},{1,17},{17,1},{2,18},{18,2},{3,19},{19,3},{4,20},{20... | collective-permute-start | bytes 196616 | tf_op jit(solution)/shard_map/ppermute | solution.py:463
  107.5 4.5 %collective-permute-start.22 = (f32[128,128]{1,0:T(8,128)S(1)}, f32[128,128]{1,0:T(8,128)S(1)}, u32[]{:S(2)}, u32[]{:S(2)}) collective-permute-start(f32[128,128]{1,0:T(8,128)S(1)} %scale.3), channel_id=1, source_target_pairs={{0,8},{4,12},{8,0},{12,4},{1,9},{5,13},{9,1},{13,5},{2,10},{6,14},... | collective-permute-start | bytes 196616 | tf_op jit(solution)/shard_map/ppermute | solution.py:463
  108.0 10.6 %collective-permute-start.16 = (f32[8,96,128]{2,1,0:T(8,128)S(1)}, f32[8,96,128]{2,1,0:T(8,128)S(1)}, u32[]{:S(2)}, u32[]{:S(2)}) collective-permute-start(f32[8,96,128]{2,1,0:T(8,128)S(1)} %get-tuple-element.35.residual), channel_id=1, source_target_pairs={{0,16},{16,0},{1,17},{17,1},{2,18},{18,2},{3,19},{19,3},{4,20},{20... | collective-permute-start | bytes 1179656 | tf_op jit(solution)/shard_map/ppermute | solution.py:463
  112.0 9.8 %collective-permute-start.25 = (f32[512,128]{1,0:T(8,128)S(1)}, f32[512,128]{1,0:T(8,128)S(1)}, u32[]{:S(2)}, u32[]{:S(2)}) collective-permute-start(f32[512,128]{1,0:T(8,128)S(1)} %pad_maximum_fusion.1), channel_id=1, source_target_pairs={{0,4},{4,0},{8,12},{12,8},{1,5},{5,1},{9,13},{13,9},{2,6},{6,2},{1... | collective-permute-start | bytes 786440 | tf_op jit(solution)/shard_map/ppermute | solution.py:463
  (1 other events, 0.6 us)

commit v3 on v2

--- a/solution.py
+++ b/solution.py
@@ -78,6 +78,10 @@
     return [pl.BlockSpec(memory_space=pltpu.VMEM)] * count
 
 
+def in_hbm(value):
+    return pltpu.with_memory_space_constraint(value, pltpu.HBM)
+
+
 def pack_kernel(full, half):
     group = lax.axis_index("groups")
     for site in range(full.shape[0]):
@@ -90,13 +94,13 @@
     return pl.pallas_call(
         pack_kernel,
         grid=(sites // step,),
-        out_shape=jax.ShapeDtypeStruct((sites, rows, lanes // 2), F32),
+        out_shape=pltpu.VMEM((sites, rows, lanes // 2), F32),
         in_specs=[pl.BlockSpec((step, rows, lanes), lambda s: (s, 0, 0))],
         out_specs=pl.BlockSpec((step, rows, lanes // 2), lambda s: (s, 0, 0)),
         compiler_params=params(),
         cost_estimate=cost(1e6, 1e6),
         name="pack",
-    )(full)
+    )(in_hbm(full))
 
 
 def around(site, ny, nx):
@@ -141,10 +145,10 @@
         functools.partial(first_kernel, ny, nx),
         grid=(sites,),
         out_shape=(
-            jax.ShapeDtypeStruct(x.shape, F32),
-            jax.ShapeDtypeStruct(x.shape, F32),
-            jax.ShapeDtypeStruct((LOCAL, sites, 2 * rows, columns), BF16),
-            jax.ShapeDtypeStruct((outer, sites, 2 * rows, columns), BF16),
+            pltpu.VMEM(x.shape, F32),
+            pltpu.VMEM(x.shape, F32),
+            pltpu.VMEM((LOCAL, sites, 2 * rows, columns), BF16),
+            pltpu.VMEM((outer, sites, 2 * rows, columns), BF16),
         ),
         in_specs=[
             pl.BlockSpec((sites, rows, lanes), lambda s: (0, 0, 0)),
@@ -161,7 +165,7 @@
         compiler_params=params(),
         cost_estimate=cost(8e9, 16e6),
         name="first_local",
-    )(x, source, couplings)
+    )(x, in_hbm(source), in_hbm(couplings))
 
 
 def local_kernel(ny, nx, x_ref, source, local, rest, stacks):
@@ -175,7 +179,7 @@
     return pl.pallas_call(
         functools.partial(local_kernel, ny, nx),
         grid=(sites,),
-        out_shape=jax.ShapeDtypeStruct(x.shape, F32),
+        out_shape=pltpu.VMEM(x.shape, F32),
         in_specs=[
             pl.BlockSpec((sites, rows, lanes), lambda s: (0, 0, 0)),
             pl.BlockSpec((1, rows, lanes), lambda s: (s, 0, 0)),
@@ -219,7 +223,7 @@
     number, width = vectors.shape
     return pl.pallas_call(
         by_rows_kernel,
-        out_shape=jax.ShapeDtypeStruct((2 * number, width), BF16),
+        out_shape=pltpu.VMEM((2 * number, width), BF16),
         in_specs=vmem(1),
         out_specs=vmem(1)[0],
         compiler_params=params(),
@@ -228,32 +232,33 @@
     )(vectors)
 
 
-def by_columns_kernel(vectors, out):
+def by_columns_kernel(by_rows, out):
     taken = 128
+    number = by_rows.shape[0] // 2
     sites, rows = out.shape[0], out.shape[2] // 2
-    for chunk in range(vectors.shape[0] // taken):
-        across = ordered_rows(vectors, chunk, taken).T
-        at = slice(chunk * taken, (chunk + 1) * taken)
-        for site in range(sites):
-            for half in range(2):
-                start = (2 * site + half) * rows
-                high, low = high_low(across[start : start + rows])
-                out[site, half, :rows, at] = high
-                out[site, half, rows:, at] = low
-
-
-def by_columns_of(vectors, sites):
-    number, width = vectors.shape
+    for part in range(2):
+        for chunk in range(number // taken):
+            start = part * number + chunk * taken
+            across = by_rows[start : start + taken].astype(F32).T.astype(BF16)
+            at = slice(chunk * taken, (chunk + 1) * taken)
+            for site in range(sites):
+                for half in range(2):
+                    start = (2 * site + half) * rows
+                    out[site, half, part * rows : (part + 1) * rows, at] = across[start : start + rows]
+
+
+def by_columns_of(by_rows, sites):
+    number, width = by_rows.shape[0] // 2, by_rows.shape[1]
     rows = width // sites // 2
     return pl.pallas_call(
         by_columns_kernel,
-        out_shape=jax.ShapeDtypeStruct((sites, 2, 2 * rows, number), BF16),
+        out_shape=pltpu.VMEM((sites, 2, 2 * rows, number), BF16),
         in_specs=vmem(1),
         out_specs=vmem(1)[0],
         compiler_params=params(),
         cost_estimate=cost(1e6, 6e6),
         name="by_columns",
-    )(vectors)
+    )(by_rows)
 
 
 def apply_faces(site, faces, matrices):
@@ -273,7 +278,7 @@
 def z_faces(rest, forward, backward, matrix):
     return pl.pallas_call(
         z_faces_kernel,
-        out_shape=jax.ShapeDtypeStruct(rest.shape, F32),
+        out_shape=pltpu.VMEM(rest.shape, F32),
         in_specs=vmem(4),
         out_specs=vmem(1)[0],
         compiler_params=params(),
@@ -296,7 +301,7 @@
 def backward_face(rest, backward, matrix):
     return pl.pallas_call(
         backward_kernel,
-        out_shape=jax.ShapeDtypeStruct(rest.shape, F32),
+        out_shape=pltpu.VMEM(rest.shape, F32),
         in_specs=vmem(3),
         out_specs=vmem(1)[0],
         compiler_params=params(),
@@ -320,10 +325,10 @@
 
 def forward_face(rest, forward, matrix, vectors):
     sites, rows, lanes = rest.shape
-    part = jax.ShapeDtypeStruct((vectors.shape[0] // 4, lanes), F32)
+    part = pltpu.VMEM((vectors.shape[0] // 4, lanes), F32)
     return pl.pallas_call(
         forward_kernel,
-        out_shape=(jax.ShapeDtypeStruct(rest.shape, F32), part, part),
+        out_shape=(pltpu.VMEM(rest.shape, F32), part, part),
         in_specs=vmem(4),
         out_specs=tuple(vmem(3)),
         scratch_shapes=[pltpu.VMEM((sites * 2 * rows, 2 * lanes), BF16)],
@@ -341,7 +346,7 @@
 
 def add_split(keep, received):
     rows, lanes = keep.shape
-    part = jax.ShapeDtypeStruct((rows // 2, lanes), F32)
+    part = pltpu.VMEM((rows // 2, lanes), F32)
     return pl.pallas_call(
         split_kernel,
         out_shape=(part, part),
@@ -350,6 +355,21 @@
         compiler_params=params(),
         name="add_split",
     )(keep, received)
+
+
+def add_kernel(left, right, out):
+    out[...] = left[...] + right[...]
+
+
+def add(left, right):
+    return pl.pallas_call(
+        add_kernel,
+        out_shape=pltpu.VMEM(left.shape, F32),
+        in_specs=vmem(2),
+        out_specs=vmem(1)[0],
+        compiler_params=params(),
+        name="add",
+    )(left, right)
 
 
 def scale_kernel(eigen, *refs):
@@ -363,7 +383,7 @@
 def scale(eigen, parts):
     return pl.pallas_call(
         scale_kernel,
-        out_shape=jax.ShapeDtypeStruct(parts[0].shape, F32),
+        out_shape=pltpu.VMEM(parts[0].shape, F32),
         in_specs=vmem(1 + len(parts)),
         out_specs=vmem(1)[0],
         compiler_params=params(),
@@ -380,77 +400,81 @@
     return fold(total)
 
 
-def update_kernel(x, residual, d, vectors, out, stacks):
-    stacks[...] = stack(d[...], 1.0)
+def assemble(pieces):
+    return pieces[0][...] if len(pieces) == 1 else jnp.concatenate([piece[...] for piece in pieces], axis=0)
+
+
+def update_kernel(x, residual, vectors, *refs):
+    pieces, (out, stacks) = refs[:-2], refs[-2:]
+    stacks[...] = stack(assemble(pieces), 1.0)
     for site in range(x.shape[0]):
         out[site] = x[site] + 0.5 * residual[site] + expand(site, vectors, stacks)
 
 
-def update(x, residual, d, vectors):
+def update(x, residual, pieces, vectors):
     number = vectors.shape[-1]
     return pl.pallas_call(
         update_kernel,
-        out_shape=jax.ShapeDtypeStruct(x.shape, F32),
-        in_specs=vmem(4),
+        out_shape=pltpu.VMEM(x.shape, F32),
+        in_specs=vmem(3 + len(pieces)),
         out_specs=vmem(1)[0],
         scratch_shapes=[pltpu.VMEM((2 * number, 2 * x.shape[-1]), BF16)],
         compiler_params=params(),
         cost_estimate=cost(1e9, 8e6),
         name="update",
-    )(x, residual, d, vectors)
+    )(x, residual, vectors, *pieces)
 
 
 def join_kernel(x, other_x, residual, other_residual, base, full):
     group = lax.axis_index("groups")
-    own = x[0] + 0.5 * residual[0]
-    other = other_x[0] + 0.5 * other_residual[0]
-    base[0] = join_halves(own, other, group)
-    full[0] = join_halves(residual[0], other_residual[0], group)
+    for site in range(x.shape[0]):
+        own = x[site] + 0.5 * residual[site]
+        other = other_x[site] + 0.5 * other_residual[site]
+        base[site] = join_halves(own, other, group)
+        full[site] = join_halves(residual[site], other_residual[site], group)
 
 
 def join(x, other_x, residual, other_residual):
     sites, rows, lanes = x.shape
-    field = pl.BlockSpec((1, rows, lanes), lambda s: (s, 0, 0))
-    wide = pl.BlockSpec((1, rows, 2 * lanes), lambda s: (s, 0, 0))
-    shape = jax.ShapeDtypeStruct((sites, rows, 2 * lanes), F32)
+    shape = (sites, rows, 2 * lanes)
     return pl.pallas_call(
         join_kernel,
-        grid=(sites,),
-        out_shape=(shape, shape),
-        in_specs=[field, field, field, field],
-        out_specs=(wide, wide),
+        out_shape=(pltpu.VMEM(shape, F32), jax.ShapeDtypeStruct(shape, F32)),
+        in_specs=vmem(4),
+        out_specs=tuple(vmem(2)),
         compiler_params=params(),
         cost_estimate=cost(1e6, 4e6),
         name="join",
     )(x, other_x, residual, other_residual)
 
 
-def final_kernel(base, d, other_d, vectors, out, stacks):
+def final_kernel(count, base, vectors, *refs):
+    own, other, (out, stacks) = refs[:count], refs[count:-2], refs[-2:]
+
     @pl.when(pl.program_id(0) == 0)
     def _():
-        stacks[...] = stack(join_halves(d[...], other_d[...], lax.axis_index("groups")), 1.0)
+        stacks[...] = stack(join_halves(assemble(own), assemble(other), lax.axis_index("groups")), 1.0)
 
     for site in range(vectors.shape[0]):
         out[site] = base[site] + expand(site, vectors, stacks)
 
 
-def final(base, d, other_d, vectors):
+def final(base, own, other, vectors):
     sites, rows, lanes = base.shape
     number = vectors.shape[-1]
     step = 2
     field = pl.BlockSpec((step, rows, lanes), lambda s: (s, 0, 0))
-    small = pl.BlockSpec((number, lanes // 2), lambda s: (0, 0))
-    return pl.pallas_call(
-        final_kernel,
+    return pl.pallas_call(
+        functools.partial(final_kernel, len(own)),
         grid=(sites // step,),
         out_shape=jax.ShapeDtypeStruct(base.shape, F32),
-        in_specs=[field, small, small, pl.BlockSpec((step, 2, 2 * rows, number), lambda s: (s, 0, 0, 0))],
+        in_specs=[field, pl.BlockSpec((step, 2, 2 * rows, number), lambda s: (s, 0, 0, 0))] + vmem(len(own) + len(other)),
         out_specs=field,
         scratch_shapes=[pltpu.VMEM((2 * number, 2 * lanes), BF16)],
         compiler_params=params(),
         cost_estimate=cost(2e9, 8e6),
         name="final",
-    )(base, d, other_d, vectors)
+    )(base, vectors, *own, *other)
 
 
 def shifted(value, axis, step):
@@ -478,15 +502,17 @@
         received = crossed(send, "space", mask)
         mask *= 2
         if mask >= count:
-            return keep + received
+            return add(keep, received)
         keep, send = add_split(keep, received)
 
 
-def doubling(part, mask):
+def doubling(pieces, mask):
     while mask:
-        part = jnp.concatenate([part, crossed(part, "space", mask)], axis=0)
+        if len(pieces) > 2:
+            pieces = [jnp.concatenate(pieces, axis=0)]
+        pieces = pieces + [crossed(piece, "space", mask) for piece in pieces]
         mask //= 2
-    return part
+    return pieces
 
 
 def both_doubling(part):
@@ -494,16 +520,9 @@
     mask = count // 2
     pairs = [(g * count + s, (g ^ 1) * count + (s ^ mask)) for g in range(groups) for s in range(count)]
     across = lax.ppermute(part, ("groups", "space"), pairs)
-    other = jnp.concatenate([crossed(part, "groups", 1), across], axis=0)
-    own = jnp.concatenate([part, crossed(part, "space", mask)], axis=0)
-    mask //= 2
-    while mask:
-        rows = own.shape[0]
-        received = crossed(jnp.concatenate([own, other], axis=0), "space", mask)
-        own = jnp.concatenate([own, received[:rows]], axis=0)
-        other = jnp.concatenate([other, received[rows:]], axis=0)
-        mask //= 2
-    return own, other
+    other = [crossed(part, "groups", 1), across]
+    own = [part, crossed(part, "space", mask)]
+    return doubling(own, mask // 2), doubling(other, mask // 2)
 
 
 def over_time(part):
@@ -528,8 +547,7 @@
     faces = faces_of(x)
     matrices = couplings.reshape(directions, sites, rows, couplings.shape[-1])
     rest, half_source, local, halo = first_local(x, source.reshape(sites, rows, lanes), matrices, ny, nx)
-    flat = vectors.reshape(number, sites * vectors.shape[-1])
-    by_rows = by_rows_of(flat)
+    by_rows = by_rows_of(vectors.reshape(number, sites * vectors.shape[-1]))
     size = number // blocks
     eigen = lax.dynamic_slice_in_dim(inverse_eigen, lax.axis_index("space") * size, size, 1)
     eigen = jnp.broadcast_to(eigen[:, :, None], (2, size, lanes // 2))
@@ -548,15 +566,20 @@
         rest = backward_face(rest, backward_t, halo)
         residual, keep, send = forward_face(rest, forward_t, halo, by_rows)
         if sweep == 0:
-            flat, send = lax.optimization_barrier((flat, send))
-            by_columns = by_columns_of(flat, sites)
-        d = scale(eigen, over_time(halving(keep, send)))
+            by_rows, send = lax.optimization_barrier((by_rows, send))
+            by_columns = by_columns_of(by_rows, sites)
+        if last:
+            other_residual = crossed(residual, "groups", 1)
+        parts = over_time(halving(keep, send))
+        if sweep == 0:
+            parts, by_columns = lax.optimization_barrier((parts, by_columns))
+        if last:
+            parts, other_residual = lax.optimization_barrier((parts, other_residual))
+        d = scale(eigen, parts)
         if not last:
-            x = update(x, residual, doubling(d, blocks // 2), by_columns)
-    other_residual = crossed(residual, "groups", 1)
+            x = update(x, residual, doubling([d], blocks // 2), by_columns)
     base, full_residual = join(x, other_x, residual, other_residual)
-    d, other_d = both_doubling(d)
-    whole = final(base, d, other_d, by_columns)
+    whole = final(base, *both_doubling(d), by_columns)
     shape = source.shape
     return whole.reshape(shape), full_residual.reshape(shape)
 

time: 126 us -> 111 us (0.88)
  local copies, waits for them, and re-layouts: 22.2 us -> 13.5 us
  waiting for transfers between devices: 43.4 us -> 36.3 us
  Pallas kernels: 26.7 us -> 30.5 us
  other arithmetic: 2.7 us -> 0 us
    ppermute x11 -> x15, waiting for transfers between devices: 19.7 us -> 14.4 us  [crossed(): return lax.ppermute(value, axis, [(i, i ^ mask) for i in range(count)])]
    unnamed x46 -> x30, local copies, waits for them, and re-layouts: 15 us -> 9.9 us
    optimization_barrier x1 -> x0, local copies, waits for them, and re-layouts: 3.64 us -> none  [shards(): flat, send = lax.optimization_barrier((flat, send))]
    ppermute x14, waiting for transfers between devices: 23.1 us -> 20 us  [shifted(): lax.ppermute(value, axis, [(i, (i + step) % count) for i in range(count)])]
    pallas_call x1, Pallas kernels: 4.61 us -> 7.69 us  [first_local(): pl.pallas_call(functools.partial(first_kernel, ny, nx), grid=(sites,), ou...]
    concatenate x4 -> x0, other arithmetic: 1.82 us -> none  [the longest x2 1.76 us: doubling(): part = jnp.concatenate([part, crossed(part, 'space', mask)], axis=0)]
    ppermute x1, waiting for transfers between devices: 0.59 us -> 1.87 us  [both_doubling(): across = lax.ppermute(part, ('groups', 'space'), pairs)]
    ppermute x11 -> x15, starting transfers between devices: 8.76 us -> 9.79 us  [crossed(): return lax.ppermute(value, axis, [(i, i ^ mask) for i in range(count)])]
  transfers between devices with their start and end apart: 26 -> 30, of which waited for: 16 -> 16; matrix products, arithmetic and copies ran while one was open for 6% -> 3% of each run, Pallas kernels for 14% -> 17%
where the time goes in v3:
time: 111 us; the launch traced here: 110 us
  waiting for transfers between devices  36.3 us (33%)
  Pallas kernels  30.5 us (27%)
  starting transfers between devices  29.2 us (26%)
  local copies, waits for them, and re-layouts  13.5 us (12%)
    ppermute x14, waiting for transfers between devices, shifted(): lax.ppermute(value, axis, [(i, (i + step) % count) for i in range(count)])  20 us
    ppermute x14, starting transfers between devices, shifted(): lax.ppermute(value, axis, [(i, (i + step) % count) for i in range(count)])  18 us
    ppermute x15, waiting for transfers between devices, crossed(): return lax.ppermute(value, axis, [(i, i ^ mask) for i in range(count)])  14.4 us
    unnamed x30, local copies, waits for them, and re-layouts  9.9 us
    ppermute x15, starting transfers between devices, crossed(): return lax.ppermute(value, axis, [(i, i ^ mask) for i in range(count)])  9.79 us
    pallas_call x1, Pallas kernels, first_local(): pl.pallas_call(functools.partial(first_kernel, ny, nx), grid=(sites,), ou...  7.69 us
    pallas_call x2, Pallas kernels, forward_face(): pl.pallas_call(forward_kernel, out_shape=(pltpu.VMEM(rest.shape, F32), pa...  3.79 us
    reshape x1, local copies, waits for them, and re-layouts, shards(): by_rows = by_rows_of(vectors.reshape(number, sites * vectors.shape[-1]))  3.55 us
  transfers between devices with their start and end apart: 30, of which 16 were waited for; matrix products, arithmetic and copies ran while one was open for 3% of the time, Pallas kernels for 17%

profile of v3, /device:TPU:0, one launch (start us, length us, event | category | flops | bytes accessed | tf_op | source)
XLA Modules:
  0.0 110.5 jit_solution(13794957541138444682)
XLA Ops:
  0.6 2.3 %pack.1.x_ref.x = f32[8,96,128]{2,1,0:T(8,128)S(1)} custom-call(f32[8,96,256]{2,1,0:T(8,128)} %bitcast.7), custom_call_target="tpu_custom_call" | custom-call | flops 1000000 | bytes 1000000 | tf_op jit(solution)/shard_map/pack/pallas_call | solution.py:94
  2.9 5.1 %collective-permute-start.3 = (f32[8,96,128]{2,1,0:T(8,128)S(1)}, f32[8,96,128]{2,1,0:T(8,128)}, u32[]{:S(2)}, u32[]{:S(2)}) collective-permute-start(f32[8,96,128]{2,1,0:T(8,128)S(1)} %pack.1.x_ref.x), channel_id=1, source_target_pairs={{0,3},{1,0},{2,1},{3,2},{4,7},{5,4},{6,5},{7,6},{8,11},{9,8},{10,9... | collective-permute-start | bytes 1179656 | tf_op jit(solution)/shard_map/ppermute | solution.py:482
  8.0 1.7 %collective-permute-start = (f32[8,96,128]{2,1,0:T(8,128)S(1)}, f32[8,96,128]{2,1,0:T(8,128)}, u32[]{:S(2)}, u32[]{:S(2)}) collective-permute-start(f32[8,96,128]{2,1,0:T(8,128)S(1)} %pack.1.x_ref.x), channel_id=1, source_target_pairs={{0,12},{4,0},{8,4},{12,8},{1,13},{5,1},{9,5},{13,9},{2,14},{6,2},{... | collective-permute-start | bytes 1179656 | tf_op jit(solution)/shard_map/ppermute | solution.py:482
  9.8 7.7 %first_local.1 = (f32[8,96,128]{2,1,0:T(8,128)S(1)}, f32[8,96,128]{2,1,0:T(8,128)S(1)}, bf16[5,8,192,192]{3,2,1,0:T(8,128)(2,1)S(1)}, bf16[4,8,192,192]{3,2,1,0:T(8,128)(2,1)S(1)}) custom-call(f32[8,96,128]{2,1,0:T(8,128)S(1)} %pack.1.x_ref.x, f32[8,96,256]{2,1,0:T(8,128)} %bitcast.9, f32[9,8,96,192]{3,2,1,0:T(8,128)} %bitcast.8), custom_call_target="tpu_custom_call" | custom-call | flops 8000000000 | bytes 16000000 | tf_op jit(solution)/shard_map/first_local/pallas_call | solution.py:144
  17.5 0.7 copy-done.7
  18.2 1.9 %copy-done.11 = bf16[5,8,192,192]{3,2,1,0:T(8,128)(2,1)} copy-done((bf16[5,8,192,192]{3,2,1,0:T(8,128)(2,1)}, bf16[5,8,192,192]{3,2,1,0:T(8,128)(2,1)S(1)}, u32[]{:S(2)}) %copy-start.11) | copy-done | bytes 2949144
  20.1 0.7 copy-done.13
  20.9 3.5 %copy.8.vectors = f32[512,1536]{1,0:T(8,128)} copy(f32[512,1536]{0,1:T(8,128)} %bitcast.6) | data formatting | bytes 6291456 | tf_op jit(solution)/shard_map/reshape | solution.py:550
  24.4 1.9 %copy-done.4 = f32[512,1536]{1,0:T(8,128)S(1)} copy-done((f32[512,1536]{1,0:T(8,128)S(1)}, f32[512,1536]{1,0:T(8,128)}, u32[]{:S(2)}) %copy-start.4) | copy-done | bytes 3145752
  27.3 2.3 %z_faces.2.rest = f32[8,96,128]{2,1,0:T(8,128)S(1)} custom-call(f32[8,96,128]{2,1,0:T(8,128)S(1)} %copy-done.8, f32[8,96,128]{2,1,0:T(8,128)} %collective-permute-done.forward, f32[8,96,128]{2,1,0:T(8,128)} %collective-permute-done.1.backward, bf16[4,8,192,192]{3,2,1,0:T(8,128)(2,1)S(1)} %get-tuple-element.33.matrix), custom_call_target="tpu_custom_call" | custom-call | flops 1000000000 | bytes 4000000 | tf_op jit(solution)/shard_map/z_faces/pallas_call | solution.py:279
  29.7 1.4 %backward_face.2.rest = f32[8,96,128]{2,1,0:T(8,128)S(1)} custom-call(f32[8,96,128]{2,1,0:T(8,128)S(1)} %z_faces.2.rest, f32[8,96,128]{2,1,0:T(8,128)} %collective-permute-done.2.backward, bf16[4,8,192,192]{3,2,1,0:T(8,128)(2,1)S(1)} %get-tuple-element.33.matrix), custom_call_target="tpu_custom_call" | custom-call | flops 1000000000 | bytes 4000000 | tf_op jit(solution)/shard_map/backward_face/pallas_call | solution.py:302
  31.1 2.4 %forward_face.2 = (f32[8,96,128]{2,1,0:T(8,128)S(1)}, f32[256,128]{1,0:T(8,128)S(1)}, f32[256,128]{1,0:T(8,128)S(1)}) custom-call(f32[8,96,128]{2,1,0:T(8,128)S(1)} %backward_face.2.rest, f32[8,96,128]{2,1,0:T(8,128)} %collective-permute-done.3.forward, bf16[4,8,192,192]{3,2,1,0:T(8,128)(2,1)S(1)} %get-tuple-element.33.matrix, ...), custom_call_target="tpu_custom_call" | custom-call | flops 2000000000 | bytes 8000000 | tf_op jit(solution)/shard_map/forward_face/pallas_call | solution.py:329
  33.5 0.7 copy-done.5
  34.3 1.3 %collective-permute-done.4.received = f32[256,128]{1,0:T(8,128)S(1)} collective-permute-done((f32[256,128]{1,0:T(8,128)S(1)}, f32[256,128]{1,0:T(8,128)S(1)}, u32[]{:S(2)}, u32[]{:S(2)}) %collective-permute-start.4) | collective-permute-done | bytes 131104 | tf_op jit(solution)/shard_map/ppermute | solution.py:487
  36.9 1.5 %collective-permute-start.5 = (f32[128,128]{1,0:T(8,128)}, f32[128,128]{1,0:T(8,128)}, u32[]{:S(2)}, u32[]{:S(2)}) collective-permute-start(f32[128,128]{1,0:T(8,128)} %get-tuple-element.39), channel_id=1, source_target_pairs={{0,8},{4,12},{8,0},{12,4},{1,9},{5,13},{9,1},{13,5},{2,10},{6,14},... | collective-permute-start | bytes 196616 | tf_op jit(solution)/shard_map/ppermute | solution.py:487
  38.4 3.1 %collective-permute-done.5.right = f32[128,128]{1,0:T(8,128)} collective-permute-done((f32[128,128]{1,0:T(8,128)}, f32[128,128]{1,0:T(8,128)}, u32[]{:S(2)}, u32[]{:S(2)}) %collective-permute-start.5) | collective-permute-done | bytes 65568 | tf_op jit(solution)/shard_map/ppermute | solution.py:487
  41.5 0.8 copy-done.10
  42.3 0.8 add.6.refs_0_
  43.2 3.9 %collective-permute-start.8 = (f32[128,128]{1,0:T(8,128)S(1)}, f32[128,128]{1,0:T(8,128)S(1)}, u32[]{:S(2)}, u32[]{:S(2)}) collective-permute-start(f32[128,128]{1,0:T(8,128)S(1)} %add.6.refs_0_), channel_id=1, source_target_pairs={{0,3},{1,0},{2,1},{3,2},{4,7},{5,4},{6,5},{7,6},{8,11},{9,8},{10,9... | collective-permute-start | bytes 196616 | tf_op jit(solution)/shard_map/ppermute | solution.py:482
  47.7 1.9 %copy-done.2 = bf16[1024,1536]{1,0:T(8,128)(2,1)S(1)} copy-done((bf16[1024,1536]{1,0:T(8,128)(2,1)S(1)}, bf16[1024,1536]{1,0:T(8,128)(2,1)}, u32[]{:S(2)}) %copy-start.2) | copy-done | bytes 3145752
  49.6 0.9 by_columns.1.vectors
  50.5 1.7 %collective-permute-done.7.refs_2_ = f32[128,128]{1,0:T(8,128)S(1)} collective-permute-done((f32[128,128]{1,0:T(8,128)S(1)}, f32[128,128]{1,0:T(8,128)S(1)}, u32[]{:S(2)}, u32[]{:S(2)}) %collective-permute-start.7) | collective-permute-done | bytes 65568 | tf_op jit(solution)/shard_map/ppermute | solution.py:482
  52.2 0.9 collective-permute-done.6.refs_1_
  53.3 1.6 %collective-permute-start.9 = (f32[128,128]{1,0:T(8,128)S(1)}, f32[128,128]{1,0:T(8,128)S(1)}, u32[]{:S(2)}, u32[]{:S(2)}) collective-permute-start(f32[128,128]{1,0:T(8,128)S(1)} %scale.2.refs_0_), channel_id=1, source_target_pairs={{0,8},{4,12},{8,0},{12,4},{1,9},{5,13},{9,1},{13,5},{2,10},{6,14},... | collective-permute-start | bytes 196616 | tf_op jit(solution)/shard_map/ppermute | solution.py:487
  54.9 2.8 %collective-permute-done.9.refs_1_ = f32[128,128]{1,0:T(8,128)S(1)} collective-permute-done((f32[128,128]{1,0:T(8,128)S(1)}, f32[128,128]{1,0:T(8,128)S(1)}, u32[]{:S(2)}, u32[]{:S(2)}) %collective-permute-start.9) | collective-permute-done | bytes 65568 | tf_op jit(solution)/shard_map/ppermute | solution.py:487
  57.6 1.2 %collective-permute-done.11.refs_3_ = f32[128,128]{1,0:T(8,128)S(1)} collective-permute-done((f32[128,128]{1,0:T(8,128)S(1)}, f32[128,128]{1,0:T(8,128)S(1)}, u32[]{:S(2)}, u32[]{:S(2)}) %collective-permute-start.11) | collective-permute-done | bytes 65568 | tf_op jit(solution)/shard_map/ppermute | solution.py:487
  58.9 1.1 update.1.x_ref.x
  60.0 1.5 %collective-permute-start.16 = (f32[8,96,128]{2,1,0:T(8,128)S(1)}, f32[8,96,128]{2,1,0:T(8,128)S(1)}, u32[]{:S(2)}, u32[]{:S(2)}) collective-permute-start(f32[8,96,128]{2,1,0:T(8,128)S(1)} %update.1.x_ref.x), channel_id=1, source_target_pairs={{0,3},{1,0},{2,1},{3,2},{4,7},{5,4},{6,5},{7,6},{8,11},{9,8},{10,9... | collective-permute-start | bytes 1179656 | tf_op jit(solution)/shard_map/ppermute | solution.py:482
  62.1 1.5 %collective-permute-start.14 = (f32[8,96,128]{2,1,0:T(8,128)S(1)}, f32[8,96,128]{2,1,0:T(8,128)S(1)}, u32[]{:S(2)}, u32[]{:S(2)}) collective-permute-start(f32[8,96,128]{2,1,0:T(8,128)S(1)} %update.1.x_ref.x), channel_id=1, source_target_pairs={{0,16},{16,0},{1,17},{17,1},{2,18},{18,2},{3,19},{19,3},{4,20},{20... | collective-permute-start | bytes 1179656 | tf_op jit(solution)/shard_map/ppermute | solution.py:487
  63.6 1.7 %collective-permute-start.12 = (f32[8,96,128]{2,1,0:T(8,128)S(1)}, f32[8,96,128]{2,1,0:T(8,128)S(1)}, u32[]{:S(2)}, u32[]{:S(2)}) collective-permute-start(f32[8,96,128]{2,1,0:T(8,128)S(1)} %update.1.x_ref.x), channel_id=1, source_target_pairs={{0,12},{4,0},{8,4},{12,8},{1,13},{5,1},{9,5},{13,9},{2,14},{6,2},{... | collective-permute-start | bytes 1179656 | tf_op jit(solution)/shard_map/ppermute | solution.py:482
  65.3 3.0 %local_part.1.rest = f32[8,96,128]{2,1,0:T(8,128)S(1)} custom-call(f32[8,96,128]{2,1,0:T(8,128)S(1)} %update.1.x_ref.x, f32[8,96,128]{2,1,0:T(8,128)S(1)} %copy-done.14, bf16[5,8,192,192]{3,2,1,0:T(8,128)(2,1)S(1)} %copy-done.12), custom_call_target="tpu_custom_call" | custom-call | flops 8000000000 | bytes 8000000 | tf_op jit(solution)/shard_map/local_part/pallas_call | solution.py:179
  68.3 4.8 %collective-permute-done.13.backward = f32[8,96,128]{2,1,0:T(8,128)S(1)} collective-permute-done((f32[8,96,128]{2,1,0:T(8,128)S(1)}, f32[8,96,128]{2,1,0:T(8,128)S(1)}, u32[]{:S(2)}, u32[]{:S(2)}) %collective-permute-start.13) | collective-permute-done | bytes 393248 | tf_op jit(solution)/shard_map/ppermute | solution.py:482
  73.1 0.9 collective-permute-done.12.forward
  74.7 5.7 %collective-permute-done.15.backward = f32[8,96,128]{2,1,0:T(8,128)S(1)} collective-permute-done((f32[8,96,128]{2,1,0:T(8,128)S(1)}, f32[8,96,128]{2,1,0:T(8,128)S(1)}, u32[]{:S(2)}, u32[]{:S(2)}) %collective-permute-start.15) | collective-permute-done | bytes 393248 | tf_op jit(solution)/shard_map/ppermute | solution.py:482
  80.9 1.4 %forward_face.3 = (f32[8,96,128]{2,1,0:T(8,128)S(1)}, f32[256,128]{1,0:T(8,128)S(1)}, f32[256,128]{1,0:T(8,128)S(1)}) custom-call(f32[8,96,128]{2,1,0:T(8,128)S(1)} %backward_face.3.rest, f32[8,96,128]{2,1,0:T(8,128)S(1)} %collective-permute-done.16.forward, bf16[4,8,192,192]{3,2,1,0:T(8,128)(2,1)S(1)} %get-tuple-element.33.matrix, ...), custom_call_target="tpu_custom_call" | custom-call | flops 2000000000 | bytes 8000000 | tf_op jit(solution)/shard_map/forward_face/pallas_call | solution.py:329
  82.3 1.6 %collective-permute-start.22 = (f32[8,96,128]{2,1,0:T(8,128)S(1)}, f32[8,96,128]{2,1,0:T(8,128)S(1)}, u32[]{:S(2)}, u32[]{:S(2)}) collective-permute-start(f32[8,96,128]{2,1,0:T(8,128)S(1)} %get-tuple-element.50.residual), channel_id=1, source_target_pairs={{0,16},{16,0},{1,17},{17,1},{2,18},{18,2},{3,19},{19,3},{4,20},{20... | collective-permute-start | bytes 1179656 | tf_op jit(solution)/shard_map/ppermute | solution.py:487
  83.9 1.3 %collective-permute-done.17.received = f32[256,128]{1,0:T(8,128)S(1)} collective-permute-done((f32[256,128]{1,0:T(8,128)S(1)}, f32[256,128]{1,0:T(8,128)S(1)}, u32[]{:S(2)}, u32[]{:S(2)}) %collective-permute-start.17) | collective-permute-done | bytes 131104 | tf_op jit(solution)/shard_map/ppermute | solution.py:487
  85.3 1.6 %collective-permute-start.18 = (f32[128,128]{1,0:T(8,128)S(1)}, f32[128,128]{1,0:T(8,128)S(1)}, u32[]{:S(2)}, u32[]{:S(2)}) collective-permute-start(f32[128,128]{1,0:T(8,128)S(1)} %get-tuple-element.54), channel_id=1, source_target_pairs={{0,8},{4,12},{8,0},{12,4},{1,9},{5,13},{9,1},{13,5},{2,10},{6,14},... | collective-permute-start | bytes 196616 | tf_op jit(solution)/shard_map/ppermute | solution.py:487
  86.8 2.8 %collective-permute-done.18.right = f32[128,128]{1,0:T(8,128)S(1)} collective-permute-done((f32[128,128]{1,0:T(8,128)S(1)}, f32[128,128]{1,0:T(8,128)S(1)}, u32[]{:S(2)}, u32[]{:S(2)}) %collective-permute-start.18) | collective-permute-done | bytes 65568 | tf_op jit(solution)/shard_map/ppermute | solution.py:487
  89.6 1.8 %collective-permute-start.21 = (f32[128,128]{1,0:T(8,128)S(1)}, f32[128,128]{1,0:T(8,128)S(1)}, u32[]{:S(2)}, u32[]{:S(2)}) collective-permute-start(f32[128,128]{1,0:T(8,128)S(1)} %add.7.refs_0_), channel_id=1, source_target_pairs={{0,3},{1,0},{2,1},{3,2},{4,7},{5,4},{6,5},{7,6},{8,11},{9,8},{10,9... | collective-permute-start | bytes 196616 | tf_op jit(solution)/shard_map/ppermute | solution.py:482
  92.4 1.6 %collective-permute-done.21.refs_3_ = f32[128,128]{1,0:T(8,128)S(1)} collective-permute-done((f32[128,128]{1,0:T(8,128)S(1)}, f32[128,128]{1,0:T(8,128)S(1)}, u32[]{:S(2)}, u32[]{:S(2)}) %collective-permute-start.21) | collective-permute-done | bytes 65568 | tf_op jit(solution)/shard_map/ppermute | solution.py:482
  93.9 4.4 %collective-permute-done.20.refs_2_ = f32[128,128]{1,0:T(8,128)S(1)} collective-permute-done((f32[128,128]{1,0:T(8,128)S(1)}, f32[128,128]{1,0:T(8,128)S(1)}, u32[]{:S(2)}, u32[]{:S(2)}) %collective-permute-start.20) | collective-permute-done | bytes 65568 | tf_op jit(solution)/shard_map/ppermute | solution.py:482
  98.4 1.5 %collective-permute-start.27 = (f32[128,128]{1,0:T(8,128)S(1)}, f32[128,128]{1,0:T(8,128)S(1)}, u32[]{:S(2)}, u32[]{:S(2)}) collective-permute-start(f32[128,128]{1,0:T(8,128)S(1)} %scale.3.refs_0_), channel_id=1, source_target_pairs={{0,24},{4,28},{8,16},{12,20},{16,8},{20,12},{24,0},{28,4},{1,25},{... | collective-permute-start | bytes 196616 | tf_op jit(solution)/shard_map/ppermute | solution.py:522
  99.9 1.5 %collective-permute-start.26 = (f32[128,128]{1,0:T(8,128)S(1)}, f32[128,128]{1,0:T(8,128)S(1)}, u32[]{:S(2)}, u32[]{:S(2)}) collective-permute-start(f32[128,128]{1,0:T(8,128)S(1)} %scale.3.refs_0_), channel_id=1, source_target_pairs={{0,16},{16,0},{1,17},{17,1},{2,18},{18,2},{3,19},{19,3},{4,20},{20... | collective-permute-start | bytes 196616 | tf_op jit(solution)/shard_map/ppermute | solution.py:487
  102.0 1.9 %collective-permute-done.27.refs_5_ = f32[128,128]{1,0:T(8,128)S(1)} collective-permute-done((f32[128,128]{1,0:T(8,128)S(1)}, f32[128,128]{1,0:T(8,128)S(1)}, u32[]{:S(2)}, u32[]{:S(2)}) %collective-permute-start.27) | collective-permute-done | bytes 65568 | tf_op jit(solution)/shard_map/ppermute | solution.py:522
  104.5 1.2 %collective-permute-done.23.refs_1_ = f32[128,128]{1,0:T(8,128)S(1)} collective-permute-done((f32[128,128]{1,0:T(8,128)S(1)}, f32[128,128]{1,0:T(8,128)S(1)}, u32[]{:S(2)}, u32[]{:S(2)}) %collective-permute-start.23) | collective-permute-done | bytes 65568 | tf_op jit(solution)/shard_map/ppermute | solution.py:487
  105.7 1.4 %join.1 = (f32[8,96,256]{2,1,0:T(8,128)S(1)}, f32[8,96,256]{2,1,0:T(8,128)}) custom-call(f32[8,96,128]{2,1,0:T(8,128)S(1)} %update.1.x_ref.x, f32[8,96,128]{2,1,0:T(8,128)S(1)} %collective-permute-done.14.other_x, f32[8,96,128]{2,1,0:T(8,128)S(1)} %get-tuple-element.50.residual, f32[8,96,128]{2,1,0:T(8,128)S(1)} %collective-permute-done.22.other_residual), custom_call_target="tpu_custom_call" | custom-call | flops 1000000 | bytes 4000000 | tf_op jit(solution)/shard_map/join/pallas_call | solution.py:440
  107.1 3.4 %final.1 = f32[8,96,256]{2,1,0:T(8,128)} custom-call(f32[8,96,256]{2,1,0:T(8,128)S(1)} %get-tuple-element.56.base, bf16[8,2,192,512]{3,2,1,0:T(8,128)(2,1)S(1)} %by_columns.1.vectors, f32[128,128]{1,0:T(8,128)S(1)} %scale.3.refs_0_, f32[128,128]{1,0:T(8,128)S(1)} %collective-permute-done.23.refs_1_, f32[128,128]{1,0:T(8,128)S(1)} %collective-permute-done.24.refs_2_, ...), custom_call_target="tpu_custom_call" | custom-call | flops 2000000000 | bytes 8000000 | tf_op jit(solution)/shard_map/final/pallas_call | solution.py:467
  (65 shorter events, 7.1 us)
Async XLA Ops:
  0.6 47.1 %copy-start = (f32[2,512]{1,0:T(2,128)S(1)}, f32[2,512]{1,0:T(2,128)}, u32[]{:S(2)}) copy-start(f32[2,512]{1,0:T(2,128)} %param.9) | copy-start | bytes 12292
  2.9 28.2 %collective-permute-start.3 = (f32[8,96,128]{2,1,0:T(8,128)S(1)}, f32[8,96,128]{2,1,0:T(8,128)}, u32[]{:S(2)}, u32[]{:S(2)}) collective-permute-start(f32[8,96,128]{2,1,0:T(8,128)S(1)} %pack.1.x_ref.x), channel_id=1, source_target_pairs={{0,3},{1,0},{2,1},{3,2},{4,7},{5,4},{6,5},{7,6},{8,11},{9,8},{10,9... | collective-permute-start | bytes 1179656 | tf_op jit(solution)/shard_map/ppermute | solution.py:482
  8.0 21.6 %collective-permute-start.2 = (f32[8,96,128]{2,1,0:T(8,128)S(1)}, f32[8,96,128]{2,1,0:T(8,128)}, u32[]{:S(2)}, u32[]{:S(2)}) collective-permute-start(f32[8,96,128]{2,1,0:T(8,128)S(1)} %pack.1.x_ref.x), channel_id=1, source_target_pairs={{0,1},{1,2},{2,3},{3,0},{4,5},{5,6},{6,7},{7,4},{8,9},{9,10},{10,1... | collective-permute-start | bytes 1179656 | tf_op jit(solution)/shard_map/ppermute | solution.py:482
  8.0 18.7 %collective-permute-start.1 = (f32[8,96,128]{2,1,0:T(8,128)S(1)}, f32[8,96,128]{2,1,0:T(8,128)}, u32[]{:S(2)}, u32[]{:S(2)}) collective-permute-start(f32[8,96,128]{2,1,0:T(8,128)S(1)} %pack.1.x_ref.x), channel_id=1, source_target_pairs={{0,4},{4,8},{8,12},{12,0},{1,5},{5,9},{9,13},{13,1},{2,6},{6,10},{... | collective-permute-start | bytes 1179656 | tf_op jit(solution)/shard_map/ppermute | solution.py:482
  8.0 18.7 %collective-permute-start = (f32[8,96,128]{2,1,0:T(8,128)S(1)}, f32[8,96,128]{2,1,0:T(8,128)}, u32[]{:S(2)}, u32[]{:S(2)}) collective-permute-start(f32[8,96,128]{2,1,0:T(8,128)S(1)} %pack.1.x_ref.x), channel_id=1, source_target_pairs={{0,12},{4,0},{8,4},{12,8},{1,13},{5,1},{9,5},{13,9},{2,14},{6,2},{... | collective-permute-start | bytes 1179656 | tf_op jit(solution)/shard_map/ppermute | solution.py:482
  17.5 0.7 copy-start.7
  18.2 1.9 %copy-start.11 = (bf16[5,8,192,192]{3,2,1,0:T(8,128)(2,1)}, bf16[5,8,192,192]{3,2,1,0:T(8,128)(2,1)S(1)}, u32[]{:S(2)}) copy-start(bf16[5,8,192,192]{3,2,1,0:T(8,128)(2,1)S(1)} %get-tuple-element.47.local) | copy-start | bytes 8847364
  20.1 0.7 copy-start.13
  24.4 1.9 %copy-start.4 = (f32[512,1536]{1,0:T(8,128)S(1)}, f32[512,1536]{1,0:T(8,128)}, u32[]{:S(2)}) copy-start(f32[512,1536]{1,0:T(8,128)} %copy.8.vectors) | copy-start | bytes 9437188
  26.3 1.0 copy-start.8
  26.7 4.4 %copy-start.1 = (bf16[1024,1536]{1,0:T(8,128)(2,1)}, bf16[1024,1536]{1,0:T(8,128)(2,1)S(1)}, u32[]{:S(2)}) copy-start(bf16[1024,1536]{1,0:T(8,128)(2,1)S(1)} %by_rows.1.vectors) | copy-start | bytes 9437188
  33.5 0.7 copy-start.5
  34.3 1.3 %collective-permute-start.4 = (f32[256,128]{1,0:T(8,128)S(1)}, f32[256,128]{1,0:T(8,128)S(1)}, u32[]{:S(2)}, u32[]{:S(2)}) collective-permute-start(f32[256,128]{1,0:T(8,128)S(1)} %get-tuple-element.37), channel_id=1, source_target_pairs={{0,4},{4,0},{8,12},{12,8},{1,5},{5,1},{9,13},{13,9},{2,6},{6,2},{1... | collective-permute-start | bytes 393224 | tf_op jit(solution)/shard_map/ppermute | solution.py:487
  36.3 0.6 copy-start.9
  36.9 4.6 %collective-permute-start.5 = (f32[128,128]{1,0:T(8,128)}, f32[128,128]{1,0:T(8,128)}, u32[]{:S(2)}, u32[]{:S(2)}) collective-permute-start(f32[128,128]{1,0:T(8,128)} %get-tuple-element.39), channel_id=1, source_target_pairs={{0,8},{4,12},{8,0},{12,4},{1,9},{5,13},{9,1},{13,5},{2,10},{6,14},... | collective-permute-start | bytes 196616 | tf_op jit(solution)/shard_map/ppermute | solution.py:487
  41.5 0.8 copy-start.10
  43.2 7.3 %collective-permute-start.8 = (f32[128,128]{1,0:T(8,128)S(1)}, f32[128,128]{1,0:T(8,128)S(1)}, u32[]{:S(2)}, u32[]{:S(2)}) collective-permute-start(f32[128,128]{1,0:T(8,128)S(1)} %add.6.refs_0_), channel_id=1, source_target_pairs={{0,3},{1,0},{2,1},{3,2},{4,7},{5,4},{6,5},{7,6},{8,11},{9,8},{10,9... | collective-permute-start | bytes 196616 | tf_op jit(solution)/shard_map/ppermute | solution.py:482
  47.0 5.2 %collective-permute-start.7 = (f32[128,128]{1,0:T(8,128)S(1)}, f32[128,128]{1,0:T(8,128)S(1)}, u32[]{:S(2)}, u32[]{:S(2)}) collective-permute-start(f32[128,128]{1,0:T(8,128)S(1)} %add.6.refs_0_), channel_id=1, source_target_pairs={{0,2},{1,3},{2,0},{3,1},{4,6},{5,7},{6,4},{7,5},{8,10},{9,11},{10,... | collective-permute-start | bytes 196616 | tf_op jit(solution)/shard_map/ppermute | solution.py:482
  47.0 6.1 %collective-permute-start.6 = (f32[128,128]{1,0:T(8,128)S(1)}, f32[128,128]{1,0:T(8,128)S(1)}, u32[]{:S(2)}, u32[]{:S(2)}) collective-permute-start(f32[128,128]{1,0:T(8,128)S(1)} %add.6.refs_0_), channel_id=1, source_target_pairs={{0,1},{1,2},{2,3},{3,0},{4,5},{5,6},{6,7},{7,4},{8,9},{9,10},{10,1... | collective-permute-start | bytes 196616 | tf_op jit(solution)/shard_map/ppermute | solution.py:482
  47.7 1.9 %copy-start.2 = (bf16[1024,1536]{1,0:T(8,128)(2,1)S(1)}, bf16[1024,1536]{1,0:T(8,128)(2,1)}, u32[]{:S(2)}) copy-start(bf16[1024,1536]{1,0:T(8,128)(2,1)} %copy-done.1) | copy-start | bytes 9437188
  49.6 9.3 %copy-start.6 = (f32[8,96,128]{2,1,0:T(8,128)S(1)}, f32[8,96,128]{2,1,0:T(8,128)}, u32[]{:S(2)}) copy-start(f32[8,96,128]{2,1,0:T(8,128)} %copy-done.5) | copy-start | bytes 1179652
  50.5 14.9 %copy-start.12 = (bf16[5,8,192,192]{3,2,1,0:T(8,128)(2,1)S(1)}, bf16[5,8,192,192]{3,2,1,0:T(8,128)(2,1)}, u32[]{:S(2)}) copy-start(bf16[5,8,192,192]{3,2,1,0:T(8,128)(2,1)} %copy-done.11) | copy-start | bytes 8847364
  50.5 14.9 %copy-start.14 = (f32[8,96,128]{2,1,0:T(8,128)S(1)}, f32[8,96,128]{2,1,0:T(8,128)}, u32[]{:S(2)}) copy-start(f32[8,96,128]{2,1,0:T(8,128)} %copy-done.13) | copy-start | bytes 1179652
  53.3 4.3 %collective-permute-start.9 = (f32[128,128]{1,0:T(8,128)S(1)}, f32[128,128]{1,0:T(8,128)S(1)}, u32[]{:S(2)}, u32[]{:S(2)}) collective-permute-start(f32[128,128]{1,0:T(8,128)S(1)} %scale.2.refs_0_), channel_id=1, source_target_pairs={{0,8},{4,12},{8,0},{12,4},{1,9},{5,13},{9,1},{13,5},{2,10},{6,14},... | collective-permute-start | bytes 196616 | tf_op jit(solution)/shard_map/ppermute | solution.py:487
  54.8 2.8 %collective-permute-start.10 = (f32[128,128]{1,0:T(8,128)S(1)}, f32[128,128]{1,0:T(8,128)S(1)}, u32[]{:S(2)}, u32[]{:S(2)}) collective-permute-start(f32[128,128]{1,0:T(8,128)S(1)} %scale.2.refs_0_), channel_id=1, source_target_pairs={{0,4},{4,0},{8,12},{12,8},{1,5},{5,1},{9,13},{13,9},{2,6},{6,2},{1... | collective-permute-start | bytes 196616 | tf_op jit(solution)/shard_map/ppermute | solution.py:487
  57.6 1.3 %collective-permute-start.11 = (f32[128,128]{1,0:T(8,128)S(1)}, f32[128,128]{1,0:T(8,128)S(1)}, u32[]{:S(2)}, u32[]{:S(2)}) collective-permute-start(f32[128,128]{1,0:T(8,128)S(1)} %collective-permute-done.9.refs_1_), channel_id=1, source_target_pairs={{0,4},{4,0},{8,12},{12,8},{1,5},{5,1},{9,13},{13,9},{2,6},{6,2},{1... | collective-permute-start | bytes 196616 | tf_op jit(solution)/shard_map/ppermute | solution.py:487
  60.0 20.9 %collective-permute-start.16 = (f32[8,96,128]{2,1,0:T(8,128)S(1)}, f32[8,96,128]{2,1,0:T(8,128)S(1)}, u32[]{:S(2)}, u32[]{:S(2)}) collective-permute-start(f32[8,96,128]{2,1,0:T(8,128)S(1)} %update.1.x_ref.x), channel_id=1, source_target_pairs={{0,3},{1,0},{2,1},{3,2},{4,7},{5,4},{6,5},{7,6},{8,11},{9,8},{10,9... | collective-permute-start | bytes 1179656 | tf_op jit(solution)/shard_map/ppermute | solution.py:482
  61.5 18.9 %collective-permute-start.15 = (f32[8,96,128]{2,1,0:T(8,128)S(1)}, f32[8,96,128]{2,1,0:T(8,128)S(1)}, u32[]{:S(2)}, u32[]{:S(2)}) collective-permute-start(f32[8,96,128]{2,1,0:T(8,128)S(1)} %update.1.x_ref.x), channel_id=1, source_target_pairs={{0,1},{1,2},{2,3},{3,0},{4,5},{5,6},{6,7},{7,4},{8,9},{9,10},{10,1... | collective-permute-start | bytes 1179656 | tf_op jit(solution)/shard_map/ppermute | solution.py:482
  62.1 12.6 %collective-permute-start.14 = (f32[8,96,128]{2,1,0:T(8,128)S(1)}, f32[8,96,128]{2,1,0:T(8,128)S(1)}, u32[]{:S(2)}, u32[]{:S(2)}) collective-permute-start(f32[8,96,128]{2,1,0:T(8,128)S(1)} %update.1.x_ref.x), channel_id=1, source_target_pairs={{0,16},{16,0},{1,17},{17,1},{2,18},{18,2},{3,19},{19,3},{4,20},{20... | collective-permute-start | bytes 1179656 | tf_op jit(solution)/shard_map/ppermute | solution.py:487
  63.6 9.6 %collective-permute-start.13 = (f32[8,96,128]{2,1,0:T(8,128)S(1)}, f32[8,96,128]{2,1,0:T(8,128)S(1)}, u32[]{:S(2)}, u32[]{:S(2)}) collective-permute-start(f32[8,96,128]{2,1,0:T(8,128)S(1)} %update.1.x_ref.x), channel_id=1, source_target_pairs={{0,4},{4,8},{8,12},{12,0},{1,5},{5,9},{9,13},{13,1},{2,6},{6,10},{... | collective-permute-start | bytes 1179656 | tf_op jit(solution)/shard_map/ppermute | solution.py:482
  63.6 10.4 %collective-permute-start.12 = (f32[8,96,128]{2,1,0:T(8,128)S(1)}, f32[8,96,128]{2,1,0:T(8,128)S(1)}, u32[]{:S(2)}, u32[]{:S(2)}) collective-permute-start(f32[8,96,128]{2,1,0:T(8,128)S(1)} %update.1.x_ref.x), channel_id=1, source_target_pairs={{0,12},{4,0},{8,4},{12,8},{1,13},{5,1},{9,5},{13,9},{2,14},{6,2},{... | collective-permute-start | bytes 1179656 | tf_op jit(solution)/shard_map/ppermute | solution.py:482
  74.7 6.2 %copy-start.3 = (bf16[1024,1536]{1,0:T(8,128)(2,1)S(1)}, bf16[1024,1536]{1,0:T(8,128)(2,1)}, u32[]{:S(2)}) copy-start(bf16[1024,1536]{1,0:T(8,128)(2,1)} %copy-done.1) | copy-start | bytes 9437188
  82.3 16.0 %collective-permute-start.22 = (f32[8,96,128]{2,1,0:T(8,128)S(1)}, f32[8,96,128]{2,1,0:T(8,128)S(1)}, u32[]{:S(2)}, u32[]{:S(2)}) collective-permute-start(f32[8,96,128]{2,1,0:T(8,128)S(1)} %get-tuple-element.50.residual), channel_id=1, source_target_pairs={{0,16},{16,0},{1,17},{17,1},{2,18},{18,2},{3,19},{19,3},{4,20},{20... | collective-permute-start | bytes 1179656 | tf_op jit(solution)/shard_map/ppermute | solution.py:487
  83.9 1.3 %collective-permute-start.17 = (f32[256,128]{1,0:T(8,128)S(1)}, f32[256,128]{1,0:T(8,128)S(1)}, u32[]{:S(2)}, u32[]{:S(2)}) collective-permute-start(f32[256,128]{1,0:T(8,128)S(1)} %get-tuple-element.52), channel_id=1, source_target_pairs={{0,4},{4,0},{8,12},{12,8},{1,5},{5,1},{9,13},{13,9},{2,6},{6,2},{1... | collective-permute-start | bytes 393224 | tf_op jit(solution)/shard_map/ppermute | solution.py:487
  85.3 4.3 %collective-permute-start.18 = (f32[128,128]{1,0:T(8,128)S(1)}, f32[128,128]{1,0:T(8,128)S(1)}, u32[]{:S(2)}, u32[]{:S(2)}) collective-permute-start(f32[128,128]{1,0:T(8,128)S(1)} %get-tuple-element.54), channel_id=1, source_target_pairs={{0,8},{4,12},{8,0},{12,4},{1,9},{5,13},{9,1},{13,5},{2,10},{6,14},... | collective-permute-start | bytes 196616 | tf_op jit(solution)/shard_map/ppermute | solution.py:487
  89.6 4.3 %collective-permute-start.21 = (f32[128,128]{1,0:T(8,128)S(1)}, f32[128,128]{1,0:T(8,128)S(1)}, u32[]{:S(2)}, u32[]{:S(2)}) collective-permute-start(f32[128,128]{1,0:T(8,128)S(1)} %add.7.refs_0_), channel_id=1, source_target_pairs={{0,3},{1,0},{2,1},{3,2},{4,7},{5,4},{6,5},{7,6},{8,11},{9,8},{10,9... | collective-permute-start | bytes 196616 | tf_op jit(solution)/shard_map/ppermute | solution.py:482
  91.4 6.9 %collective-permute-start.20 = (f32[128,128]{1,0:T(8,128)S(1)}, f32[128,128]{1,0:T(8,128)S(1)}, u32[]{:S(2)}, u32[]{:S(2)}) collective-permute-start(f32[128,128]{1,0:T(8,128)S(1)} %add.7.refs_0_), channel_id=1, source_target_pairs={{0,2},{1,3},{2,0},{3,1},{4,6},{5,7},{6,4},{7,5},{8,10},{9,11},{10,... | collective-permute-start | bytes 196616 | tf_op jit(solution)/shard_map/ppermute | solution.py:482
  91.9 6.5 %collective-permute-start.19 = (f32[128,128]{1,0:T(8,128)S(1)}, f32[128,128]{1,0:T(8,128)S(1)}, u32[]{:S(2)}, u32[]{:S(2)}) collective-permute-start(f32[128,128]{1,0:T(8,128)S(1)} %add.7.refs_0_), channel_id=1, source_target_pairs={{0,1},{1,2},{2,3},{3,0},{4,5},{5,6},{6,7},{7,4},{8,9},{9,10},{10,1... | collective-permute-start | bytes 196616 | tf_op jit(solution)/shard_map/ppermute | solution.py:482
  98.4 5.4 %collective-permute-start.27 = (f32[128,128]{1,0:T(8,128)S(1)}, f32[128,128]{1,0:T(8,128)S(1)}, u32[]{:S(2)}, u32[]{:S(2)}) collective-permute-start(f32[128,128]{1,0:T(8,128)S(1)} %scale.3.refs_0_), channel_id=1, source_target_pairs={{0,24},{4,28},{8,16},{12,20},{16,8},{20,12},{24,0},{28,4},{1,25},{... | collective-permute-start | bytes 196616 | tf_op jit(solution)/shard_map/ppermute | solution.py:522
  99.9 4.6 %collective-permute-start.26 = (f32[128,128]{1,0:T(8,128)S(1)}, f32[128,128]{1,0:T(8,128)S(1)}, u32[]{:S(2)}, u32[]{:S(2)}) collective-permute-start(f32[128,128]{1,0:T(8,128)S(1)} %scale.3.refs_0_), channel_id=1, source_target_pairs={{0,16},{16,0},{1,17},{17,1},{2,18},{18,2},{3,19},{19,3},{4,20},{20... | collective-permute-start | bytes 196616 | tf_op jit(solution)/shard_map/ppermute | solution.py:487
  101.4 4.3 %collective-permute-start.23 = (f32[128,128]{1,0:T(8,128)S(1)}, f32[128,128]{1,0:T(8,128)S(1)}, u32[]{:S(2)}, u32[]{:S(2)}) collective-permute-start(f32[128,128]{1,0:T(8,128)S(1)} %scale.3.refs_0_), channel_id=1, source_target_pairs={{0,8},{4,12},{8,0},{12,4},{1,9},{5,13},{9,1},{13,5},{2,10},{6,14},... | collective-permute-start | bytes 196616 | tf_op jit(solution)/shard_map/ppermute | solution.py:487
  102.0 5.1 %collective-permute-start.24 = (f32[128,128]{1,0:T(8,128)S(1)}, f32[128,128]{1,0:T(8,128)S(1)}, u32[]{:S(2)}, u32[]{:S(2)}) collective-permute-start(f32[128,128]{1,0:T(8,128)S(1)} %scale.3.refs_0_), channel_id=1, source_target_pairs={{0,4},{4,0},{8,12},{12,8},{1,5},{5,1},{9,13},{13,9},{2,6},{6,2},{1... | collective-permute-start | bytes 196616 | tf_op jit(solution)/shard_map/ppermute | solution.py:487
  103.8 3.2 %collective-permute-start.29 = (f32[128,128]{1,0:T(8,128)S(1)}, f32[128,128]{1,0:T(8,128)S(1)}, u32[]{:S(2)}, u32[]{:S(2)}) collective-permute-start(f32[128,128]{1,0:T(8,128)S(1)} %collective-permute-done.27.refs_5_), channel_id=1, source_target_pairs={{0,4},{4,0},{8,12},{12,8},{1,5},{5,1},{9,13},{13,9},{2,6},{6,2},{1... | collective-permute-start | bytes 196616 | tf_op jit(solution)/shard_map/ppermute | solution.py:487
  104.5 2.6 %collective-permute-start.28 = (f32[128,128]{1,0:T(8,128)S(1)}, f32[128,128]{1,0:T(8,128)S(1)}, u32[]{:S(2)}, u32[]{:S(2)}) collective-permute-start(f32[128,128]{1,0:T(8,128)S(1)} %collective-permute-done.26.refs_4_), channel_id=1, source_target_pairs={{0,4},{4,0},{8,12},{12,8},{1,5},{5,1},{9,13},{13,9},{2,6},{6,2},{1... | collective-permute-start | bytes 196616 | tf_op jit(solution)/shard_map/ppermute | solution.py:487
  105.7 1.4 %collective-permute-start.25 = (f32[128,128]{1,0:T(8,128)S(1)}, f32[128,128]{1,0:T(8,128)S(1)}, u32[]{:S(2)}, u32[]{:S(2)}) collective-permute-start(f32[128,128]{1,0:T(8,128)S(1)} %collective-permute-done.23.refs_1_), channel_id=1, source_target_pairs={{0,4},{4,0},{8,12},{12,8},{1,5},{5,1},{9,13},{13,9},{2,6},{6,2},{1... | collective-permute-start | bytes 196616 | tf_op jit(solution)/shard_map/ppermute | solution.py:487

commit v4 on v3

--- a/solution.py
+++ b/solution.py
@@ -90,17 +90,15 @@
 
 def pack(full):
     sites, rows, lanes = full.shape
-    step = 2
     return pl.pallas_call(
         pack_kernel,
-        grid=(sites // step,),
         out_shape=pltpu.VMEM((sites, rows, lanes // 2), F32),
-        in_specs=[pl.BlockSpec((step, rows, lanes), lambda s: (s, 0, 0))],
-        out_specs=pl.BlockSpec((step, rows, lanes // 2), lambda s: (s, 0, 0)),
+        in_specs=vmem(1),
+        out_specs=vmem(1)[0],
         compiler_params=params(),
         cost_estimate=cost(1e6, 1e6),
         name="pack",
-    )(in_hbm(full))
+    )(full)
 
 
 def around(site, ny, nx):
@@ -198,67 +196,65 @@
     return [int(format(index, "b").zfill(bits)[::-1], 2) if bits else 0 for index in range(count)]
 
 
-def ordered_rows(vectors, chunk, taken):
-    blocks = lax.axis_size("space")
+def block_starts(size):
     space = lax.axis_index("space")
-    size = vectors.shape[0] // blocks
-    unit = min(size, taken)
-    parts = []
-    for start in range(chunk * taken, (chunk + 1) * taken, unit):
-        block = space ^ block_order(blocks)[start // size]
-        parts.append(vectors[pl.ds(pl.multiple_of(block * size + start % size, unit), unit)])
-    return parts[0] if len(parts) == 1 else jnp.concatenate(parts, axis=0)
-
-
-def by_rows_kernel(vectors, out):
-    taken = 128
-    number = vectors.shape[0]
-    for chunk in range(number // taken):
-        high, low = high_low(ordered_rows(vectors, chunk, taken))
-        out[chunk * taken : (chunk + 1) * taken] = high
-        out[number + chunk * taken : number + (chunk + 1) * taken] = low
-
-
-def by_rows_of(vectors):
-    number, width = vectors.shape
-    return pl.pallas_call(
-        by_rows_kernel,
-        out_shape=pltpu.VMEM((2 * number, width), BF16),
+    return [pl.multiple_of((space ^ block) * size, size) for block in block_order(lax.axis_size("space"))]
+
+
+def vectors_kernel(across, by_rows, by_columns):
+    sites, _, double, number = by_columns.shape
+    rows = double // 2
+    high, low = high_low(across[...].T)
+    by_rows[:number] = high
+    by_rows[number:] = low
+    for site in range(sites):
+        for half in range(2):
+            start = (2 * site + half) * rows
+            high, low = high_low(across[start : start + rows])
+            by_columns[site, half, :rows] = high
+            by_columns[site, half, rows:] = low
+
+
+def vectors_parts(across, sites):
+    width, number = across.shape
+    rows = width // sites // 2
+    step = 2
+    return pl.pallas_call(
+        vectors_kernel,
+        grid=(sites // step,),
+        out_shape=(pltpu.VMEM((2 * number, width), BF16), pltpu.VMEM((sites, 2, 2 * rows, number), BF16)),
+        in_specs=[pl.BlockSpec((step * 2 * rows, number), lambda s: (s, 0))],
+        out_specs=(
+            pl.BlockSpec((2 * number, step * 2 * rows), lambda s: (0, s)),
+            pl.BlockSpec((step, 2, 2 * rows, number), lambda s: (s, 0, 0, 0)),
+        ),
+        compiler_params=params(16),
+        cost_estimate=cost(1e6, 9e6),
+        name="vectors_parts",
+    )(in_hbm(across))
+
+
+def eigen_kernel(inverse, out):
+    size, lanes = out.shape[1:]
+    number = inverse.shape[1]
+    start = lax.axis_index("space") * size
+    row = lax.broadcasted_iota(jnp.int32, (size, number), 0) + start
+    chosen = lax.broadcasted_iota(jnp.int32, (size, number), 1) == row
+    for part in range(2):
+        value = jnp.where(chosen, inverse[part : part + 1], 0.0)
+        out[part] = jnp.broadcast_to(jnp.sum(value, axis=1, keepdims=True), (size, lanes))
+
+
+def eigen_of(inverse, size, lanes):
+    return pl.pallas_call(
+        eigen_kernel,
+        out_shape=pltpu.VMEM((2, size, lanes), F32),
         in_specs=vmem(1),
         out_specs=vmem(1)[0],
         compiler_params=params(),
-        cost_estimate=cost(1e6, 6e6),
-        name="by_rows",
-    )(vectors)
-
-
-def by_columns_kernel(by_rows, out):
-    taken = 128
-    number = by_rows.shape[0] // 2
-    sites, rows = out.shape[0], out.shape[2] // 2
-    for part in range(2):
-        for chunk in range(number // taken):
-            start = part * number + chunk * taken
-            across = by_rows[start : start + taken].astype(F32).T.astype(BF16)
-            at = slice(chunk * taken, (chunk + 1) * taken)
-            for site in range(sites):
-                for half in range(2):
-                    start = (2 * site + half) * rows
-                    out[site, half, part * rows : (part + 1) * rows, at] = across[start : start + rows]
-
-
-def by_columns_of(by_rows, sites):
-    number, width = by_rows.shape[0] // 2, by_rows.shape[1]
-    rows = width // sites // 2
-    return pl.pallas_call(
-        by_columns_kernel,
-        out_shape=pltpu.VMEM((sites, 2, 2 * rows, number), BF16),
-        in_specs=vmem(1),
-        out_specs=vmem(1)[0],
-        compiler_params=params(),
-        cost_estimate=cost(1e6, 6e6),
-        name="by_columns",
-    )(by_rows)
+        cost_estimate=cost(1e6, 1e6),
+        name="eigen",
+    )(inverse)
 
 
 def apply_faces(site, faces, matrices):
@@ -310,17 +306,20 @@
     )(rest, backward, matrix)
 
 
-def forward_kernel(rest, forward, matrix, vectors, residual, keep, send, stacks):
+def forward_kernel(rest, forward, matrix, vectors, residual, keep, send, stacks, whole):
     sign = edge_sign(True)
     rows = 2 * rest.shape[1]
     for site in range(rest.shape[0]):
         own = rest[site] - apply_faces(site, (lambda s: sign * forward[s],), (matrix.at[2],))
         residual[site] = own
         stacks[site * rows : (site + 1) * rows] = stack(own, -1.0)
-    whole = fold(matmul(vectors[...], stacks[...]))
-    half = whole.shape[0] // 2
-    keep[...] = whole[:half]
-    send[...] = whole[half:]
+    whole[...] = fold(matmul(vectors[...], stacks[...]))
+    starts = block_starts(whole.shape[0] // lax.axis_size("space"))
+    half = len(starts) // 2
+    size = whole.shape[0] // len(starts)
+    for index, start in enumerate(starts):
+        part, at = (keep, index) if index < half else (send, index - half)
+        part[at * size : (at + 1) * size] = whole[pl.ds(start, size)]
 
 
 def forward_face(rest, forward, matrix, vectors):
@@ -331,7 +330,10 @@
         out_shape=(pltpu.VMEM(rest.shape, F32), part, part),
         in_specs=vmem(4),
         out_specs=tuple(vmem(3)),
-        scratch_shapes=[pltpu.VMEM((sites * 2 * rows, 2 * lanes), BF16)],
+        scratch_shapes=[
+            pltpu.VMEM((sites * 2 * rows, 2 * lanes), BF16),
+            pltpu.VMEM((vectors.shape[0] // 2, lanes), F32),
+        ],
         compiler_params=params(),
         cost_estimate=cost(2e9, 8e6),
         name="forward_face",
@@ -400,13 +402,22 @@
     return fold(total)
 
 
-def assemble(pieces):
-    return pieces[0][...] if len(pieces) == 1 else jnp.concatenate([piece[...] for piece in pieces], axis=0)
+def place_pieces(values, stacks):
+    number = stacks.shape[0] // 2
+    size = number // lax.axis_size("space")
+    starts = iter(block_starts(size))
+    for value in values:
+        both = stack(value, 1.0)
+        rows = value.shape[0]
+        for at in range(0, rows, size):
+            start = next(starts)
+            stacks[pl.ds(start, size)] = both[at : at + size]
+            stacks[pl.ds(start + number, size)] = both[rows + at : rows + at + size]
 
 
 def update_kernel(x, residual, vectors, *refs):
     pieces, (out, stacks) = refs[:-2], refs[-2:]
-    stacks[...] = stack(assemble(pieces), 1.0)
+    place_pieces([piece[...] for piece in pieces], stacks)
     for site in range(x.shape[0]):
         out[site] = x[site] + 0.5 * residual[site] + expand(site, vectors, stacks)
 
@@ -450,26 +461,28 @@
 
 def final_kernel(count, base, vectors, *refs):
     own, other, (out, stacks) = refs[:count], refs[count:-2], refs[-2:]
-
-    @pl.when(pl.program_id(0) == 0)
+    step = out.shape[0]
+    first = pl.program_id(0) * step
+
+    @pl.when(first == 0)
     def _():
-        stacks[...] = stack(join_halves(assemble(own), assemble(other), lax.axis_index("groups")), 1.0)
-
-    for site in range(vectors.shape[0]):
-        out[site] = base[site] + expand(site, vectors, stacks)
+        group = lax.axis_index("groups")
+        place_pieces([join_halves(a[...], b[...], group) for a, b in zip(own, other)], stacks)
+
+    for index in range(step):
+        out[index] = base[first + index] + expand(first + index, vectors, stacks)
 
 
 def final(base, own, other, vectors):
     sites, rows, lanes = base.shape
     number = vectors.shape[-1]
     step = 2
-    field = pl.BlockSpec((step, rows, lanes), lambda s: (s, 0, 0))
     return pl.pallas_call(
         functools.partial(final_kernel, len(own)),
         grid=(sites // step,),
         out_shape=jax.ShapeDtypeStruct(base.shape, F32),
-        in_specs=[field, pl.BlockSpec((step, 2, 2 * rows, number), lambda s: (s, 0, 0, 0))] + vmem(len(own) + len(other)),
-        out_specs=field,
+        in_specs=vmem(2 + len(own) + len(other)),
+        out_specs=pl.BlockSpec((step, rows, lanes), lambda s: (s, 0, 0)),
         scratch_shapes=[pltpu.VMEM((2 * number, 2 * lanes), BF16)],
         compiler_params=params(),
         cost_estimate=cost(2e9, 8e6),
@@ -547,10 +560,9 @@
     faces = faces_of(x)
     matrices = couplings.reshape(directions, sites, rows, couplings.shape[-1])
     rest, half_source, local, halo = first_local(x, source.reshape(sites, rows, lanes), matrices, ny, nx)
-    by_rows = by_rows_of(vectors.reshape(number, sites * vectors.shape[-1]))
-    size = number // blocks
-    eigen = lax.dynamic_slice_in_dim(inverse_eigen, lax.axis_index("space") * size, size, 1)
-    eigen = jnp.broadcast_to(eigen[:, :, None], (2, size, lanes // 2))
+    across = jnp.transpose(vectors, (1, 2, 3, 4, 5, 0)).reshape(sites * vectors.shape[-1], number)
+    by_rows, by_columns = vectors_parts(across, sites)
+    eigen = eigen_of(inverse_eigen, number // blocks, lanes // 2)
 
     for sweep in range(ITERS):
         last = sweep == ITERS - 1
@@ -565,14 +577,11 @@
             rest, other_x = lax.optimization_barrier((rest, other_x))
         rest = backward_face(rest, backward_t, halo)
         residual, keep, send = forward_face(rest, forward_t, halo, by_rows)
-        if sweep == 0:
-            by_rows, send = lax.optimization_barrier((by_rows, send))
-            by_columns = by_columns_of(by_rows, sites)
+        part = halving(keep, send)
         if last:
+            part, residual = lax.optimization_barrier((part, residual))
             other_residual = crossed(residual, "groups", 1)
-        parts = over_time(halving(keep, send))
-        if sweep == 0:
-            parts, by_columns = lax.optimization_barrier((parts, by_columns))
+        parts = over_time(part)
         if last:
             parts, other_residual = lax.optimization_barrier((parts, other_residual))
         d = scale(eigen, parts)

time: 111 us -> 101 us (0.910)
  local copies, waits for them, and re-layouts: 13.5 us -> 1.13 us
  waiting for transfers between devices: 36.3 us -> 43.1 us
  Pallas kernels: 30.5 us -> 25.9 us
    unnamed x30 -> x4, local copies, waits for them, and re-layouts: 9.9 us -> 1.13 us
    ppermute x14, waiting for transfers between devices: 20 us -> 24.4 us  [shifted(): lax.ppermute(value, axis, [(i, (i + step) % count) for i in range(count)])]
    reshape x1 -> x0, local copies, waits for them, and re-layouts: 3.55 us -> none  [shards(): by_rows = by_rows_of(vectors.reshape(number, sites * vectors.shape[-1]))]
    ppermute x15, waiting for transfers between devices: 14.4 us -> 17.3 us  [crossed(): return lax.ppermute(value, axis, [(i, i ^ mask) for i in range(count)])]
    ppermute x14, starting transfers between devices: 18 us -> 20.2 us  [shifted(): lax.ppermute(value, axis, [(i, (i + step) % count) for i in range(count)])]
    ppermute x15, starting transfers between devices: 9.79 us -> 8.09 us  [crossed(): return lax.ppermute(value, axis, [(i, i ^ mask) for i in range(count)])]
    pallas_call x2, Pallas kernels: 3.01 us -> 1.32 us  [z_faces(): pl.pallas_call(z_faces_kernel, out_shape=pltpu.VMEM(rest.shape, F32), in_...]
  transfers between devices with their start and end apart: 30 -> 30, of which waited for: 16 -> 20; matrix products, arithmetic and copies ran while one was open for 3% -> 0% of each run, Pallas kernels for 17% -> 18%
where the time goes in v4:
time: 101 us
  waiting for transfers between devices  43.1 us (43%)
  starting transfers between devices  30.1 us (30%)
  Pallas kernels  25.9 us (26%)
  local copies, waits for them, and re-layouts  1.13 us (1%)
    ppermute x14, waiting for transfers between devices, shifted(): lax.ppermute(value, axis, [(i, (i + step) % count) for i in range(count)])  24.4 us
    ppermute x14, starting transfers between devices, shifted(): lax.ppermute(value, axis, [(i, (i + step) % count) for i in range(count)])  20.2 us
    ppermute x15, waiting for transfers between devices, crossed(): return lax.ppermute(value, axis, [(i, i ^ mask) for i in range(count)])  17.3 us
    ppermute x15, starting transfers between devices, crossed(): return lax.ppermute(value, axis, [(i, i ^ mask) for i in range(count)])  8.09 us
    pallas_call x1, Pallas kernels, first_local(): pl.pallas_call(functools.partial(first_kernel, ny, nx), grid=(sites,), ou...  7.69 us
    pallas_call x1, Pallas kernels, vectors_parts(): pl.pallas_call(vectors_kernel, grid=(sites // step,), out_shape=(pltpu.VM...  3.72 us
    pallas_call x1, Pallas kernels, final(): pl.pallas_call(functools.partial(final_kernel, len(own)), grid=(sites //...  3.38 us
    pallas_call x1, Pallas kernels, local_part(): pl.pallas_call(functools.partial(local_kernel, ny, nx), grid=(sites,), ou...  2.97 us
  transfers between devices with their start and end apart: 30, of which 20 were waited for; matrix products, arithmetic and copies ran while one was open for 0% of the time, Pallas kernels for 18%

profile of v4, /device:TPU:0, one launch (start us, length us, event | category | flops | bytes accessed | tf_op | source)
XLA Modules:
  0.0 101.0 jit_solution(3766199218972213751)
XLA Ops:
  0.6 1.1 %copy-done = f32[1,1,2,4,96,256]{5,4,3,2,1,0:T(8,128)S(1)} copy-done((f32[1,1,2,4,96,256]{5,4,3,2,1,0:T(8,128)S(1)}, f32[1,1,2,4,96,256]{5,4,3,2,1,0:T(8,128)}, u32[]{:S(2)}) %copy-start) | copy-done | bytes 786456
  2.0 2.4 %collective-permute-start = (f32[8,96,128]{2,1,0:T(8,128)S(1)}, f32[8,96,128]{2,1,0:T(8,128)S(1)}, u32[]{:S(2)}, u32[]{:S(2)}) collective-permute-start(f32[8,96,128]{2,1,0:T(8,128)S(1)} %pack.1.x_ref.x), channel_id=1, source_target_pairs={{0,12},{4,0},{8,4},{12,8},{1,13},{5,1},{9,5},{13,9},{2,14},{6,2},{... | collective-permute-start | bytes 1179656 | tf_op jit(solution)/shard_map/ppermute | solution.py:495
  4.5 1.6 %collective-permute-start.2 = (f32[8,96,128]{2,1,0:T(8,128)S(1)}, f32[8,96,128]{2,1,0:T(8,128)S(1)}, u32[]{:S(2)}, u32[]{:S(2)}) collective-permute-start(f32[8,96,128]{2,1,0:T(8,128)S(1)} %pack.1.x_ref.x), channel_id=1, source_target_pairs={{0,1},{1,2},{2,3},{3,0},{4,5},{5,6},{6,7},{7,4},{8,9},{9,10},{10,1... | collective-permute-start | bytes 1179656 | tf_op jit(solution)/shard_map/ppermute | solution.py:495
  6.0 2.2 %collective-permute-start.3 = (f32[8,96,128]{2,1,0:T(8,128)S(1)}, f32[8,96,128]{2,1,0:T(8,128)S(1)}, u32[]{:S(2)}, u32[]{:S(2)}) collective-permute-start(f32[8,96,128]{2,1,0:T(8,128)S(1)} %pack.1.x_ref.x), channel_id=1, source_target_pairs={{0,3},{1,0},{2,1},{3,2},{4,7},{5,4},{6,5},{7,6},{8,11},{9,8},{10,9... | collective-permute-start | bytes 1179656 | tf_op jit(solution)/shard_map/ppermute | solution.py:495
  8.3 7.7 %first_local.1 = (f32[8,96,128]{2,1,0:T(8,128)S(1)}, f32[8,96,128]{2,1,0:T(8,128)S(1)}, bf16[5,8,192,192]{3,2,1,0:T(8,128)(2,1)S(1)}, bf16[4,8,192,192]{3,2,1,0:T(8,128)(2,1)S(1)}) custom-call(f32[8,96,128]{2,1,0:T(8,128)S(1)} %pack.1.x_ref.x, f32[8,96,256]{2,1,0:T(8,128)} %bitcast.11, f32[9,8,96,192]{3,2,1,0:T(8,128)} %bitcast.10), custom_call_target="tpu_custom_call" | custom-call | flops 8000000000 | bytes 16000000 | tf_op jit(solution)/shard_map/first_local/pallas_call | solution.py:142
  16.0 3.7 %vectors_parts.1 = (bf16[1024,1536]{1,0:T(8,128)(2,1)S(1)}, bf16[8,2,192,512]{3,2,1,0:T(8,128)(2,1)S(1)}) custom-call(f32[1536,512]{1,0:T(8,128)} %bitcast.9), custom_call_target="tpu_custom_call" | custom-call | flops 1000000 | bytes 9000000 | tf_op jit(solution)/shard_map/vectors_parts/pallas_call | solution.py:222
  19.7 0.7 z_faces.2.rest
  20.9 5.1 %collective-permute-done.3.forward = f32[8,96,128]{2,1,0:T(8,128)S(1)} collective-permute-done((f32[8,96,128]{2,1,0:T(8,128)S(1)}, f32[8,96,128]{2,1,0:T(8,128)S(1)}, u32[]{:S(2)}, u32[]{:S(2)}) %collective-permute-start.3) | collective-permute-done | bytes 393248 | tf_op jit(solution)/shard_map/ppermute | solution.py:495
  26.0 1.4 %forward_face.2 = (f32[8,96,128]{2,1,0:T(8,128)S(1)}, f32[256,128]{1,0:T(8,128)S(1)}, f32[256,128]{1,0:T(8,128)S(1)}) custom-call(f32[8,96,128]{2,1,0:T(8,128)S(1)} %backward_face.2.rest, f32[8,96,128]{2,1,0:T(8,128)S(1)} %collective-permute-done.3.forward, bf16[4,8,192,192]{3,2,1,0:T(8,128)(2,1)S(1)} %get-tuple-element.30.matrix, ...), custom_call_target="tpu_custom_call" | custom-call | flops 2000000000 | bytes 8000000 | tf_op jit(solution)/shard_map/forward_face/pallas_call | solution.py:328
  27.5 1.3 %collective-permute-done.4.received = f32[256,128]{1,0:T(8,128)S(1)} collective-permute-done((f32[256,128]{1,0:T(8,128)S(1)}, f32[256,128]{1,0:T(8,128)S(1)}, u32[]{:S(2)}, u32[]{:S(2)}) %collective-permute-start.4) | collective-permute-done | bytes 131104 | tf_op jit(solution)/shard_map/ppermute | solution.py:500
  28.8 1.5 %collective-permute-start.5 = (f32[128,128]{1,0:T(8,128)S(1)}, f32[128,128]{1,0:T(8,128)S(1)}, u32[]{:S(2)}, u32[]{:S(2)}) collective-permute-start(f32[128,128]{1,0:T(8,128)S(1)} %get-tuple-element.37), channel_id=1, source_target_pairs={{0,8},{4,12},{8,0},{12,4},{1,9},{5,13},{9,1},{13,5},{2,10},{6,14},... | collective-permute-start | bytes 196616 | tf_op jit(solution)/shard_map/ppermute | solution.py:500
  30.3 2.9 %collective-permute-done.5.right = f32[128,128]{1,0:T(8,128)S(1)} collective-permute-done((f32[128,128]{1,0:T(8,128)S(1)}, f32[128,128]{1,0:T(8,128)S(1)}, u32[]{:S(2)}, u32[]{:S(2)}) %collective-permute-start.5) | collective-permute-done | bytes 65568 | tf_op jit(solution)/shard_map/ppermute | solution.py:500
  33.2 1.2 %collective-permute-start.6 = (f32[128,128]{1,0:T(8,128)S(1)}, f32[128,128]{1,0:T(8,128)S(1)}, u32[]{:S(2)}, u32[]{:S(2)}) collective-permute-start(f32[128,128]{1,0:T(8,128)S(1)} %add.2.refs_0_), channel_id=1, source_target_pairs={{0,1},{1,2},{2,3},{3,0},{4,5},{5,6},{6,7},{7,4},{8,9},{9,10},{10,1... | collective-permute-start | bytes 196616 | tf_op jit(solution)/shard_map/ppermute | solution.py:495
  34.3 2.2 %collective-permute-start.7 = (f32[128,128]{1,0:T(8,128)S(1)}, f32[128,128]{1,0:T(8,128)S(1)}, u32[]{:S(2)}, u32[]{:S(2)}) collective-permute-start(f32[128,128]{1,0:T(8,128)S(1)} %add.2.refs_0_), channel_id=1, source_target_pairs={{0,2},{1,3},{2,0},{3,1},{4,6},{5,7},{6,4},{7,5},{8,10},{9,11},{10,... | collective-permute-start | bytes 196616 | tf_op jit(solution)/shard_map/ppermute | solution.py:495
  36.6 1.3 %collective-permute-start.8 = (f32[128,128]{1,0:T(8,128)S(1)}, f32[128,128]{1,0:T(8,128)S(1)}, u32[]{:S(2)}, u32[]{:S(2)}) collective-permute-start(f32[128,128]{1,0:T(8,128)S(1)} %add.2.refs_0_), channel_id=1, source_target_pairs={{0,3},{1,0},{2,1},{3,2},{4,7},{5,4},{6,5},{7,6},{8,11},{9,8},{10,9... | collective-permute-start | bytes 196616 | tf_op jit(solution)/shard_map/ppermute | solution.py:495
  38.1 1.5 %collective-permute-done.6.refs_1_ = f32[128,128]{1,0:T(8,128)S(1)} collective-permute-done((f32[128,128]{1,0:T(8,128)S(1)}, f32[128,128]{1,0:T(8,128)S(1)}, u32[]{:S(2)}, u32[]{:S(2)}) %collective-permute-start.6) | collective-permute-done | bytes 65568 | tf_op jit(solution)/shard_map/ppermute | solution.py:495
  39.6 1.9 %collective-permute-done.7.refs_2_ = f32[128,128]{1,0:T(8,128)S(1)} collective-permute-done((f32[128,128]{1,0:T(8,128)S(1)}, f32[128,128]{1,0:T(8,128)S(1)}, u32[]{:S(2)}, u32[]{:S(2)}) %collective-permute-start.7) | collective-permute-done | bytes 65568 | tf_op jit(solution)/shard_map/ppermute | solution.py:495
  41.6 1.3 %collective-permute-start.9 = (f32[128,128]{1,0:T(8,128)S(1)}, f32[128,128]{1,0:T(8,128)S(1)}, u32[]{:S(2)}, u32[]{:S(2)}) collective-permute-start(f32[128,128]{1,0:T(8,128)S(1)} %scale.2.refs_0_), channel_id=1, source_target_pairs={{0,8},{4,12},{8,0},{12,4},{1,9},{5,13},{9,1},{13,5},{2,10},{6,14},... | collective-permute-start | bytes 196616 | tf_op jit(solution)/shard_map/ppermute | solution.py:500
  42.9 3.1 %collective-permute-done.9.refs_1_ = f32[128,128]{1,0:T(8,128)S(1)} collective-permute-done((f32[128,128]{1,0:T(8,128)S(1)}, f32[128,128]{1,0:T(8,128)S(1)}, u32[]{:S(2)}, u32[]{:S(2)}) %collective-permute-start.9) | collective-permute-done | bytes 65568 | tf_op jit(solution)/shard_map/ppermute | solution.py:500
  45.9 1.2 %collective-permute-done.11.refs_3_ = f32[128,128]{1,0:T(8,128)S(1)} collective-permute-done((f32[128,128]{1,0:T(8,128)S(1)}, f32[128,128]{1,0:T(8,128)S(1)}, u32[]{:S(2)}, u32[]{:S(2)}) %collective-permute-start.11) | collective-permute-done | bytes 65568 | tf_op jit(solution)/shard_map/ppermute | solution.py:500
  47.2 1.1 %update.1.x_ref.x = f32[8,96,128]{2,1,0:T(8,128)S(1)} custom-call(f32[8,96,128]{2,1,0:T(8,128)S(1)} %pack.1.x_ref.x, f32[8,96,128]{2,1,0:T(8,128)S(1)} %get-tuple-element.32.residual, bf16[8,2,192,512]{3,2,1,0:T(8,128)(2,1)S(1)} %get-tuple-element.33.vectors, f32[128,128]{1,0:T(8,128)S(1)} %scale.2.refs_0_, f32[128,128]{1,0:T(8,128)S(1)} %collective-permute-done.9.refs_1_, ...), custom_call_target="tpu_custom_call" | custom-call | flops 1000000000 | bytes 8000000 | tf_op jit(solution)/shard_map/update/pallas_call | solution.py:427
  48.3 1.0 %collective-permute-start.12 = (f32[8,96,128]{2,1,0:T(8,128)S(1)}, f32[8,96,128]{2,1,0:T(8,128)S(1)}, u32[]{:S(2)}, u32[]{:S(2)}) collective-permute-start(f32[8,96,128]{2,1,0:T(8,128)S(1)} %update.1.x_ref.x), channel_id=1, source_target_pairs={{0,12},{4,0},{8,4},{12,8},{1,13},{5,1},{9,5},{13,9},{2,14},{6,2},{... | collective-permute-start | bytes 1179656 | tf_op jit(solution)/shard_map/ppermute | solution.py:495
  49.3 1.5 %collective-permute-start.14 = (f32[8,96,128]{2,1,0:T(8,128)S(1)}, f32[8,96,128]{2,1,0:T(8,128)S(1)}, u32[]{:S(2)}, u32[]{:S(2)}) collective-permute-start(f32[8,96,128]{2,1,0:T(8,128)S(1)} %update.1.x_ref.x), channel_id=1, source_target_pairs={{0,16},{16,0},{1,17},{17,1},{2,18},{18,2},{3,19},{19,3},{4,20},{20... | collective-permute-start | bytes 1179656 | tf_op jit(solution)/shard_map/ppermute | solution.py:500
  50.9 1.3 %collective-permute-start.15 = (f32[8,96,128]{2,1,0:T(8,128)S(1)}, f32[8,96,128]{2,1,0:T(8,128)S(1)}, u32[]{:S(2)}, u32[]{:S(2)}) collective-permute-start(f32[8,96,128]{2,1,0:T(8,128)S(1)} %update.1.x_ref.x), channel_id=1, source_target_pairs={{0,1},{1,2},{2,3},{3,0},{4,5},{5,6},{6,7},{7,4},{8,9},{9,10},{10,1... | collective-permute-start | bytes 1179656 | tf_op jit(solution)/shard_map/ppermute | solution.py:495
  52.1 2.6 %collective-permute-start.16 = (f32[8,96,128]{2,1,0:T(8,128)S(1)}, f32[8,96,128]{2,1,0:T(8,128)S(1)}, u32[]{:S(2)}, u32[]{:S(2)}) collective-permute-start(f32[8,96,128]{2,1,0:T(8,128)S(1)} %update.1.x_ref.x), channel_id=1, source_target_pairs={{0,3},{1,0},{2,1},{3,2},{4,7},{5,4},{6,5},{7,6},{8,11},{9,8},{10,9... | collective-permute-start | bytes 1179656 | tf_op jit(solution)/shard_map/ppermute | solution.py:495
  54.7 3.0 %local_part.1.rest = f32[8,96,128]{2,1,0:T(8,128)S(1)} custom-call(f32[8,96,128]{2,1,0:T(8,128)S(1)} %update.1.x_ref.x, f32[8,96,128]{2,1,0:T(8,128)S(1)} %get-tuple-element.38.source, bf16[5,8,192,192]{3,2,1,0:T(8,128)(2,1)S(1)} %get-tuple-element.39.local), custom_call_target="tpu_custom_call" | custom-call | flops 8000000000 | bytes 8000000 | tf_op jit(solution)/shard_map/local_part/pallas_call | solution.py:177
  57.7 0.9 collective-permute-done.12.forward
  58.6 1.5 %collective-permute-done.13.backward = f32[8,96,128]{2,1,0:T(8,128)S(1)} collective-permute-done((f32[8,96,128]{2,1,0:T(8,128)S(1)}, f32[8,96,128]{2,1,0:T(8,128)S(1)}, u32[]{:S(2)}, u32[]{:S(2)}) %collective-permute-start.13) | collective-permute-done | bytes 393248 | tf_op jit(solution)/shard_map/ppermute | solution.py:495
  60.1 0.7 z_faces.3.rest
  61.3 3.4 %collective-permute-done.15.backward = f32[8,96,128]{2,1,0:T(8,128)S(1)} collective-permute-done((f32[8,96,128]{2,1,0:T(8,128)S(1)}, f32[8,96,128]{2,1,0:T(8,128)S(1)}, u32[]{:S(2)}, u32[]{:S(2)}) %collective-permute-start.15) | collective-permute-done | bytes 393248 | tf_op jit(solution)/shard_map/ppermute | solution.py:495
  65.1 6.8 %collective-permute-done.16.forward = f32[8,96,128]{2,1,0:T(8,128)S(1)} collective-permute-done((f32[8,96,128]{2,1,0:T(8,128)S(1)}, f32[8,96,128]{2,1,0:T(8,128)S(1)}, u32[]{:S(2)}, u32[]{:S(2)}) %collective-permute-start.16) | collective-permute-done | bytes 393248 | tf_op jit(solution)/shard_map/ppermute | solution.py:495
  71.9 1.4 %forward_face.3 = (f32[8,96,128]{2,1,0:T(8,128)S(1)}, f32[256,128]{1,0:T(8,128)S(1)}, f32[256,128]{1,0:T(8,128)S(1)}) custom-call(f32[8,96,128]{2,1,0:T(8,128)S(1)} %backward_face.3.rest, f32[8,96,128]{2,1,0:T(8,128)S(1)} %collective-permute-done.16.forward, bf16[4,8,192,192]{3,2,1,0:T(8,128)(2,1)S(1)} %get-tuple-element.30.matrix, ...), custom_call_target="tpu_custom_call" | custom-call | flops 2000000000 | bytes 8000000 | tf_op jit(solution)/shard_map/forward_face/pallas_call | solution.py:328
  73.4 1.3 %collective-permute-done.17.received = f32[256,128]{1,0:T(8,128)S(1)} collective-permute-done((f32[256,128]{1,0:T(8,128)S(1)}, f32[256,128]{1,0:T(8,128)S(1)}, u32[]{:S(2)}, u32[]{:S(2)}) %collective-permute-start.17) | collective-permute-done | bytes 131104 | tf_op jit(solution)/shard_map/ppermute | solution.py:500
  74.8 1.3 %collective-permute-start.18 = (f32[128,128]{1,0:T(8,128)S(1)}, f32[128,128]{1,0:T(8,128)S(1)}, u32[]{:S(2)}, u32[]{:S(2)}) collective-permute-start(f32[128,128]{1,0:T(8,128)S(1)} %get-tuple-element.45), channel_id=1, source_target_pairs={{0,8},{4,12},{8,0},{12,4},{1,9},{5,13},{9,1},{13,5},{2,10},{6,14},... | collective-permute-start | bytes 196616 | tf_op jit(solution)/shard_map/ppermute | solution.py:500
  76.1 3.0 %collective-permute-done.18.right = f32[128,128]{1,0:T(8,128)S(1)} collective-permute-done((f32[128,128]{1,0:T(8,128)S(1)}, f32[128,128]{1,0:T(8,128)S(1)}, u32[]{:S(2)}, u32[]{:S(2)}) %collective-permute-start.18) | collective-permute-done | bytes 65568 | tf_op jit(solution)/shard_map/ppermute | solution.py:500
  79.7 0.8 collective-permute-start.19
  80.5 1.8 %collective-permute-start.20 = (f32[128,128]{1,0:T(8,128)S(1)}, f32[128,128]{1,0:T(8,128)S(1)}, u32[]{:S(2)}, u32[]{:S(2)}) collective-permute-start(f32[128,128]{1,0:T(8,128)S(1)} %add.3.refs_0_), channel_id=1, source_target_pairs={{0,2},{1,3},{2,0},{3,1},{4,6},{5,7},{6,4},{7,5},{8,10},{9,11},{10,... | collective-permute-start | bytes 196616 | tf_op jit(solution)/shard_map/ppermute | solution.py:495
  82.3 1.7 %collective-permute-start.21 = (f32[128,128]{1,0:T(8,128)S(1)}, f32[128,128]{1,0:T(8,128)S(1)}, u32[]{:S(2)}, u32[]{:S(2)}) collective-permute-start(f32[128,128]{1,0:T(8,128)S(1)} %add.3.refs_0_), channel_id=1, source_target_pairs={{0,3},{1,0},{2,1},{3,2},{4,7},{5,4},{6,5},{7,6},{8,11},{9,8},{10,9... | collective-permute-start | bytes 196616 | tf_op jit(solution)/shard_map/ppermute | solution.py:495
  84.1 1.8 %collective-permute-done.19.refs_1_ = f32[128,128]{1,0:T(8,128)S(1)} collective-permute-done((f32[128,128]{1,0:T(8,128)S(1)}, f32[128,128]{1,0:T(8,128)S(1)}, u32[]{:S(2)}, u32[]{:S(2)}) %collective-permute-start.19) | collective-permute-done | bytes 65568 | tf_op jit(solution)/shard_map/ppermute | solution.py:495
  85.8 1.5 %collective-permute-done.20.refs_2_ = f32[128,128]{1,0:T(8,128)S(1)} collective-permute-done((f32[128,128]{1,0:T(8,128)S(1)}, f32[128,128]{1,0:T(8,128)S(1)}, u32[]{:S(2)}, u32[]{:S(2)}) %collective-permute-start.20) | collective-permute-done | bytes 65568 | tf_op jit(solution)/shard_map/ppermute | solution.py:495
  87.3 1.8 %collective-permute-done.22.other_residual = f32[8,96,128]{2,1,0:T(8,128)S(1)} collective-permute-done((f32[8,96,128]{2,1,0:T(8,128)S(1)}, f32[8,96,128]{2,1,0:T(8,128)S(1)}, u32[]{:S(2)}, u32[]{:S(2)}) %collective-permute-start.22) | collective-permute-done | bytes 393248 | tf_op jit(solution)/shard_map/ppermute | solution.py:500
  89.3 1.3 %collective-permute-start.23 = (f32[128,128]{1,0:T(8,128)S(1)}, f32[128,128]{1,0:T(8,128)S(1)}, u32[]{:S(2)}, u32[]{:S(2)}) collective-permute-start(f32[128,128]{1,0:T(8,128)S(1)} %scale.3.refs_0_), channel_id=1, source_target_pairs={{0,8},{4,12},{8,0},{12,4},{1,9},{5,13},{9,1},{13,5},{2,10},{6,14},... | collective-permute-start | bytes 196616 | tf_op jit(solution)/shard_map/ppermute | solution.py:500
  91.1 1.7 %collective-permute-start.27 = (f32[128,128]{1,0:T(8,128)S(1)}, f32[128,128]{1,0:T(8,128)S(1)}, u32[]{:S(2)}, u32[]{:S(2)}) collective-permute-start(f32[128,128]{1,0:T(8,128)S(1)} %scale.3.refs_0_), channel_id=1, source_target_pairs={{0,24},{4,28},{8,16},{12,20},{16,8},{20,12},{24,0},{28,4},{1,25},{... | collective-permute-start | bytes 196616 | tf_op jit(solution)/shard_map/ppermute | solution.py:535
  92.8 0.8 collective-permute-done.23.refs_1_
  93.6 1.2 %collective-permute-done.26.refs_4_ = f32[128,128]{1,0:T(8,128)S(1)} collective-permute-done((f32[128,128]{1,0:T(8,128)S(1)}, f32[128,128]{1,0:T(8,128)S(1)}, u32[]{:S(2)}, u32[]{:S(2)}) %collective-permute-start.26) | collective-permute-done | bytes 65568 | tf_op jit(solution)/shard_map/ppermute | solution.py:500
  94.9 1.4 %collective-permute-done.27.refs_5_ = f32[128,128]{1,0:T(8,128)S(1)} collective-permute-done((f32[128,128]{1,0:T(8,128)S(1)}, f32[128,128]{1,0:T(8,128)S(1)}, u32[]{:S(2)}, u32[]{:S(2)}) %collective-permute-start.27) | collective-permute-done | bytes 65568 | tf_op jit(solution)/shard_map/ppermute | solution.py:535
  96.3 1.4 %join.1 = (f32[8,96,256]{2,1,0:T(8,128)S(1)}, f32[8,96,256]{2,1,0:T(8,128)}) custom-call(f32[8,96,128]{2,1,0:T(8,128)S(1)} %update.1.x_ref.x, f32[8,96,128]{2,1,0:T(8,128)S(1)} %collective-permute-done.14.other_x, f32[8,96,128]{2,1,0:T(8,128)S(1)} %get-tuple-element.47.residual, f32[8,96,128]{2,1,0:T(8,128)S(1)} %collective-permute-done.22.other_residual), custom_call_target="tpu_custom_call" | custom-call | flops 1000000 | bytes 4000000 | tf_op jit(solution)/shard_map/join/pallas_call | solution.py:451
  97.6 3.4 %final.1 = f32[8,96,256]{2,1,0:T(8,128)} custom-call(f32[8,96,256]{2,1,0:T(8,128)S(1)} %get-tuple-element.50.base, bf16[8,2,192,512]{3,2,1,0:T(8,128)(2,1)S(1)} %get-tuple-element.33.vectors, f32[128,128]{1,0:T(8,128)S(1)} %scale.3.refs_0_, f32[128,128]{1,0:T(8,128)S(1)} %collective-permute-done.23.refs_1_, f32[128,128]{1,0:T(8,128)S(1)} %collective-permute-done.24.refs_2_, ...), custom_call_target="tpu_custom_call" | custom-call | flops 2000000000 | bytes 8000000 | tf_op jit(solution)/shard_map/final/pallas_call | solution.py:480
  (36 shorter events, 3.3 us)
Async XLA Ops:
  0.6 1.1 %copy-start = (f32[1,1,2,4,96,256]{5,4,3,2,1,0:T(8,128)S(1)}, f32[1,1,2,4,96,256]{5,4,3,2,1,0:T(8,128)}, u32[]{:S(2)}) copy-start(f32[1,1,2,4,96,256]{5,4,3,2,1,0:T(8,128)} %param.7) | copy-start | bytes 2359300
  2.0 17.7 %collective-permute-start = (f32[8,96,128]{2,1,0:T(8,128)S(1)}, f32[8,96,128]{2,1,0:T(8,128)S(1)}, u32[]{:S(2)}, u32[]{:S(2)}) collective-permute-start(f32[8,96,128]{2,1,0:T(8,128)S(1)} %pack.1.x_ref.x), channel_id=1, source_target_pairs={{0,12},{4,0},{8,4},{12,8},{1,13},{5,1},{9,5},{13,9},{2,14},{6,2},{... | collective-permute-start | bytes 1179656 | tf_op jit(solution)/shard_map/ppermute | solution.py:495
  4.5 15.3 %collective-permute-start.1 = (f32[8,96,128]{2,1,0:T(8,128)S(1)}, f32[8,96,128]{2,1,0:T(8,128)S(1)}, u32[]{:S(2)}, u32[]{:S(2)}) collective-permute-start(f32[8,96,128]{2,1,0:T(8,128)S(1)} %pack.1.x_ref.x), channel_id=1, source_target_pairs={{0,4},{4,8},{8,12},{12,0},{1,5},{5,9},{9,13},{13,1},{2,6},{6,10},{... | collective-permute-start | bytes 1179656 | tf_op jit(solution)/shard_map/ppermute | solution.py:495
  4.5 15.9 %collective-permute-start.2 = (f32[8,96,128]{2,1,0:T(8,128)S(1)}, f32[8,96,128]{2,1,0:T(8,128)S(1)}, u32[]{:S(2)}, u32[]{:S(2)}) collective-permute-start(f32[8,96,128]{2,1,0:T(8,128)S(1)} %pack.1.x_ref.x), channel_id=1, source_target_pairs={{0,1},{1,2},{2,3},{3,0},{4,5},{5,6},{6,7},{7,4},{8,9},{9,10},{10,1... | collective-permute-start | bytes 1179656 | tf_op jit(solution)/shard_map/ppermute | solution.py:495
  6.0 19.9 %collective-permute-start.3 = (f32[8,96,128]{2,1,0:T(8,128)S(1)}, f32[8,96,128]{2,1,0:T(8,128)S(1)}, u32[]{:S(2)}, u32[]{:S(2)}) collective-permute-start(f32[8,96,128]{2,1,0:T(8,128)S(1)} %pack.1.x_ref.x), channel_id=1, source_target_pairs={{0,3},{1,0},{2,1},{3,2},{4,7},{5,4},{6,5},{7,6},{8,11},{9,8},{10,9... | collective-permute-start | bytes 1179656 | tf_op jit(solution)/shard_map/ppermute | solution.py:495
  26.0 12.0 %copy-start.1 = (f32[2,512]{1,0:T(2,128)S(1)}, f32[2,512]{1,0:T(2,128)}, u32[]{:S(2)}) copy-start(f32[2,512]{1,0:T(2,128)} %inverse.1) | copy-start | bytes 12292
  27.4 1.4 %collective-permute-start.4 = (f32[256,128]{1,0:T(8,128)S(1)}, f32[256,128]{1,0:T(8,128)S(1)}, u32[]{:S(2)}, u32[]{:S(2)}) collective-permute-start(f32[256,128]{1,0:T(8,128)S(1)} %get-tuple-element.35), channel_id=1, source_target_pairs={{0,4},{4,0},{8,12},{12,8},{1,5},{5,1},{9,13},{13,9},{2,6},{6,2},{1... | collective-permute-start | bytes 393224 | tf_op jit(solution)/shard_map/ppermute | solution.py:500
  28.8 4.3 %collective-permute-start.5 = (f32[128,128]{1,0:T(8,128)S(1)}, f32[128,128]{1,0:T(8,128)S(1)}, u32[]{:S(2)}, u32[]{:S(2)}) collective-permute-start(f32[128,128]{1,0:T(8,128)S(1)} %get-tuple-element.37), channel_id=1, source_target_pairs={{0,8},{4,12},{8,0},{12,4},{1,9},{5,13},{9,1},{13,5},{2,10},{6,14},... | collective-permute-start | bytes 196616 | tf_op jit(solution)/shard_map/ppermute | solution.py:500
  33.2 6.4 %collective-permute-start.6 = (f32[128,128]{1,0:T(8,128)S(1)}, f32[128,128]{1,0:T(8,128)S(1)}, u32[]{:S(2)}, u32[]{:S(2)}) collective-permute-start(f32[128,128]{1,0:T(8,128)S(1)} %add.2.refs_0_), channel_id=1, source_target_pairs={{0,1},{1,2},{2,3},{3,0},{4,5},{5,6},{6,7},{7,4},{8,9},{9,10},{10,1... | collective-permute-start | bytes 196616 | tf_op jit(solution)/shard_map/ppermute | solution.py:495
  34.3 7.2 %collective-permute-start.7 = (f32[128,128]{1,0:T(8,128)S(1)}, f32[128,128]{1,0:T(8,128)S(1)}, u32[]{:S(2)}, u32[]{:S(2)}) collective-permute-start(f32[128,128]{1,0:T(8,128)S(1)} %add.2.refs_0_), channel_id=1, source_target_pairs={{0,2},{1,3},{2,0},{3,1},{4,6},{5,7},{6,4},{7,5},{8,10},{9,11},{10,... | collective-permute-start | bytes 196616 | tf_op jit(solution)/shard_map/ppermute | solution.py:495
  36.6 4.9 %collective-permute-start.8 = (f32[128,128]{1,0:T(8,128)S(1)}, f32[128,128]{1,0:T(8,128)S(1)}, u32[]{:S(2)}, u32[]{:S(2)}) collective-permute-start(f32[128,128]{1,0:T(8,128)S(1)} %add.2.refs_0_), channel_id=1, source_target_pairs={{0,3},{1,0},{2,1},{3,2},{4,7},{5,4},{6,5},{7,6},{8,11},{9,8},{10,9... | collective-permute-start | bytes 196616 | tf_op jit(solution)/shard_map/ppermute | solution.py:495
  41.6 4.3 %collective-permute-start.9 = (f32[128,128]{1,0:T(8,128)S(1)}, f32[128,128]{1,0:T(8,128)S(1)}, u32[]{:S(2)}, u32[]{:S(2)}) collective-permute-start(f32[128,128]{1,0:T(8,128)S(1)} %scale.2.refs_0_), channel_id=1, source_target_pairs={{0,8},{4,12},{8,0},{12,4},{1,9},{5,13},{9,1},{13,5},{2,10},{6,14},... | collective-permute-start | bytes 196616 | tf_op jit(solution)/shard_map/ppermute | solution.py:500
  42.9 3.1 %collective-permute-start.10 = (f32[128,128]{1,0:T(8,128)S(1)}, f32[128,128]{1,0:T(8,128)S(1)}, u32[]{:S(2)}, u32[]{:S(2)}) collective-permute-start(f32[128,128]{1,0:T(8,128)S(1)} %scale.2.refs_0_), channel_id=1, source_target_pairs={{0,4},{4,0},{8,12},{12,8},{1,5},{5,1},{9,13},{13,9},{2,6},{6,2},{1... | collective-permute-start | bytes 196616 | tf_op jit(solution)/shard_map/ppermute | solution.py:500
  45.9 1.3 %collective-permute-start.11 = (f32[128,128]{1,0:T(8,128)S(1)}, f32[128,128]{1,0:T(8,128)S(1)}, u32[]{:S(2)}, u32[]{:S(2)}) collective-permute-start(f32[128,128]{1,0:T(8,128)S(1)} %collective-permute-done.9.refs_1_), channel_id=1, source_target_pairs={{0,4},{4,0},{8,12},{12,8},{1,5},{5,1},{9,13},{13,9},{2,6},{6,2},{1... | collective-permute-start | bytes 196616 | tf_op jit(solution)/shard_map/ppermute | solution.py:500
  48.3 10.3 %collective-permute-start.12 = (f32[8,96,128]{2,1,0:T(8,128)S(1)}, f32[8,96,128]{2,1,0:T(8,128)S(1)}, u32[]{:S(2)}, u32[]{:S(2)}) collective-permute-start(f32[8,96,128]{2,1,0:T(8,128)S(1)} %update.1.x_ref.x), channel_id=1, source_target_pairs={{0,12},{4,0},{8,4},{12,8},{1,13},{5,1},{9,5},{13,9},{2,14},{6,2},{... | collective-permute-start | bytes 1179656 | tf_op jit(solution)/shard_map/ppermute | solution.py:495
  49.3 10.8 %collective-permute-start.13 = (f32[8,96,128]{2,1,0:T(8,128)S(1)}, f32[8,96,128]{2,1,0:T(8,128)S(1)}, u32[]{:S(2)}, u32[]{:S(2)}) collective-permute-start(f32[8,96,128]{2,1,0:T(8,128)S(1)} %update.1.x_ref.x), channel_id=1, source_target_pairs={{0,4},{4,8},{8,12},{12,0},{1,5},{5,9},{9,13},{13,1},{2,6},{6,10},{... | collective-permute-start | bytes 1179656 | tf_op jit(solution)/shard_map/ppermute | solution.py:495
  49.3 12.0 %collective-permute-start.14 = (f32[8,96,128]{2,1,0:T(8,128)S(1)}, f32[8,96,128]{2,1,0:T(8,128)S(1)}, u32[]{:S(2)}, u32[]{:S(2)}) collective-permute-start(f32[8,96,128]{2,1,0:T(8,128)S(1)} %update.1.x_ref.x), channel_id=1, source_target_pairs={{0,16},{16,0},{1,17},{17,1},{2,18},{18,2},{3,19},{19,3},{4,20},{20... | collective-permute-start | bytes 1179656 | tf_op jit(solution)/shard_map/ppermute | solution.py:500
  50.9 13.8 %collective-permute-start.15 = (f32[8,96,128]{2,1,0:T(8,128)S(1)}, f32[8,96,128]{2,1,0:T(8,128)S(1)}, u32[]{:S(2)}, u32[]{:S(2)}) collective-permute-start(f32[8,96,128]{2,1,0:T(8,128)S(1)} %update.1.x_ref.x), channel_id=1, source_target_pairs={{0,1},{1,2},{2,3},{3,0},{4,5},{5,6},{6,7},{7,4},{8,9},{9,10},{10,1... | collective-permute-start | bytes 1179656 | tf_op jit(solution)/shard_map/ppermute | solution.py:495
  52.1 19.8 %collective-permute-start.16 = (f32[8,96,128]{2,1,0:T(8,128)S(1)}, f32[8,96,128]{2,1,0:T(8,128)S(1)}, u32[]{:S(2)}, u32[]{:S(2)}) collective-permute-start(f32[8,96,128]{2,1,0:T(8,128)S(1)} %update.1.x_ref.x), channel_id=1, source_target_pairs={{0,3},{1,0},{2,1},{3,2},{4,7},{5,4},{6,5},{7,6},{8,11},{9,8},{10,9... | collective-permute-start | bytes 1179656 | tf_op jit(solution)/shard_map/ppermute | solution.py:495
  73.3 1.4 %collective-permute-start.17 = (f32[256,128]{1,0:T(8,128)S(1)}, f32[256,128]{1,0:T(8,128)S(1)}, u32[]{:S(2)}, u32[]{:S(2)}) collective-permute-start(f32[256,128]{1,0:T(8,128)S(1)} %get-tuple-element.43), channel_id=1, source_target_pairs={{0,4},{4,0},{8,12},{12,8},{1,5},{5,1},{9,13},{13,9},{2,6},{6,2},{1... | collective-permute-start | bytes 393224 | tf_op jit(solution)/shard_map/ppermute | solution.py:500
  74.8 4.3 %collective-permute-start.18 = (f32[128,128]{1,0:T(8,128)S(1)}, f32[128,128]{1,0:T(8,128)S(1)}, u32[]{:S(2)}, u32[]{:S(2)}) collective-permute-start(f32[128,128]{1,0:T(8,128)S(1)} %get-tuple-element.45), channel_id=1, source_target_pairs={{0,8},{4,12},{8,0},{12,4},{1,9},{5,13},{9,1},{13,5},{2,10},{6,14},... | collective-permute-start | bytes 196616 | tf_op jit(solution)/shard_map/ppermute | solution.py:500
  79.1 10.1 %collective-permute-start.22 = (f32[8,96,128]{2,1,0:T(8,128)S(1)}, f32[8,96,128]{2,1,0:T(8,128)S(1)}, u32[]{:S(2)}, u32[]{:S(2)}) collective-permute-start(f32[8,96,128]{2,1,0:T(8,128)S(1)} %get-tuple-element.47.residual), channel_id=1, source_target_pairs={{0,16},{16,0},{1,17},{17,1},{2,18},{18,2},{3,19},{19,3},{4,20},{20... | collective-permute-start | bytes 1179656 | tf_op jit(solution)/shard_map/ppermute | solution.py:500
  79.7 6.2 %collective-permute-start.19 = (f32[128,128]{1,0:T(8,128)S(1)}, f32[128,128]{1,0:T(8,128)S(1)}, u32[]{:S(2)}, u32[]{:S(2)}) collective-permute-start(f32[128,128]{1,0:T(8,128)S(1)} %add.3.refs_0_), channel_id=1, source_target_pairs={{0,1},{1,2},{2,3},{3,0},{4,5},{5,6},{6,7},{7,4},{8,9},{9,10},{10,1... | collective-permute-start | bytes 196616 | tf_op jit(solution)/shard_map/ppermute | solution.py:495
  80.5 6.8 %collective-permute-start.20 = (f32[128,128]{1,0:T(8,128)S(1)}, f32[128,128]{1,0:T(8,128)S(1)}, u32[]{:S(2)}, u32[]{:S(2)}) collective-permute-start(f32[128,128]{1,0:T(8,128)S(1)} %add.3.refs_0_), channel_id=1, source_target_pairs={{0,2},{1,3},{2,0},{3,1},{4,6},{5,7},{6,4},{7,5},{8,10},{9,11},{10,... | collective-permute-start | bytes 196616 | tf_op jit(solution)/shard_map/ppermute | solution.py:495
  82.3 5.0 %collective-permute-start.21 = (f32[128,128]{1,0:T(8,128)S(1)}, f32[128,128]{1,0:T(8,128)S(1)}, u32[]{:S(2)}, u32[]{:S(2)}) collective-permute-start(f32[128,128]{1,0:T(8,128)S(1)} %add.3.refs_0_), channel_id=1, source_target_pairs={{0,3},{1,0},{2,1},{3,2},{4,7},{5,4},{6,5},{7,6},{8,11},{9,8},{10,9... | collective-permute-start | bytes 196616 | tf_op jit(solution)/shard_map/ppermute | solution.py:495
  89.3 4.3 %collective-permute-start.23 = (f32[128,128]{1,0:T(8,128)S(1)}, f32[128,128]{1,0:T(8,128)S(1)}, u32[]{:S(2)}, u32[]{:S(2)}) collective-permute-start(f32[128,128]{1,0:T(8,128)S(1)} %scale.3.refs_0_), channel_id=1, source_target_pairs={{0,8},{4,12},{8,0},{12,4},{1,9},{5,13},{9,1},{13,5},{2,10},{6,14},... | collective-permute-start | bytes 196616 | tf_op jit(solution)/shard_map/ppermute | solution.py:500
  90.6 4.3 %collective-permute-start.26 = (f32[128,128]{1,0:T(8,128)S(1)}, f32[128,128]{1,0:T(8,128)S(1)}, u32[]{:S(2)}, u32[]{:S(2)}) collective-permute-start(f32[128,128]{1,0:T(8,128)S(1)} %scale.3.refs_0_), channel_id=1, source_target_pairs={{0,16},{16,0},{1,17},{17,1},{2,18},{18,2},{3,19},{19,3},{4,20},{20... | collective-permute-start | bytes 196616 | tf_op jit(solution)/shard_map/ppermute | solution.py:500
  91.1 5.2 %collective-permute-start.27 = (f32[128,128]{1,0:T(8,128)S(1)}, f32[128,128]{1,0:T(8,128)S(1)}, u32[]{:S(2)}, u32[]{:S(2)}) collective-permute-start(f32[128,128]{1,0:T(8,128)S(1)} %scale.3.refs_0_), channel_id=1, source_target_pairs={{0,24},{4,28},{8,16},{12,20},{16,8},{20,12},{24,0},{28,4},{1,25},{... | collective-permute-start | bytes 196616 | tf_op jit(solution)/shard_map/ppermute | solution.py:535
  92.8 4.8 %collective-permute-start.24 = (f32[128,128]{1,0:T(8,128)S(1)}, f32[128,128]{1,0:T(8,128)S(1)}, u32[]{:S(2)}, u32[]{:S(2)}) collective-permute-start(f32[128,128]{1,0:T(8,128)S(1)} %scale.3.refs_0_), channel_id=1, source_target_pairs={{0,4},{4,0},{8,12},{12,8},{1,5},{5,1},{9,13},{13,9},{2,6},{6,2},{1... | collective-permute-start | bytes 196616 | tf_op jit(solution)/shard_map/ppermute | solution.py:500
  93.6 4.0 %collective-permute-start.25 = (f32[128,128]{1,0:T(8,128)S(1)}, f32[128,128]{1,0:T(8,128)S(1)}, u32[]{:S(2)}, u32[]{:S(2)}) collective-permute-start(f32[128,128]{1,0:T(8,128)S(1)} %collective-permute-done.23.refs_1_), channel_id=1, source_target_pairs={{0,4},{4,0},{8,12},{12,8},{1,5},{5,1},{9,13},{13,9},{2,6},{6,2},{1... | collective-permute-start | bytes 196616 | tf_op jit(solution)/shard_map/ppermute | solution.py:500
  94.9 2.8 %collective-permute-start.28 = (f32[128,128]{1,0:T(8,128)S(1)}, f32[128,128]{1,0:T(8,128)S(1)}, u32[]{:S(2)}, u32[]{:S(2)}) collective-permute-start(f32[128,128]{1,0:T(8,128)S(1)} %collective-permute-done.26.refs_4_), channel_id=1, source_target_pairs={{0,4},{4,0},{8,12},{12,8},{1,5},{5,1},{9,13},{13,9},{2,6},{6,2},{1... | collective-permute-start | bytes 196616 | tf_op jit(solution)/shard_map/ppermute | solution.py:500
  96.3 1.4 %collective-permute-start.29 = (f32[128,128]{1,0:T(8,128)S(1)}, f32[128,128]{1,0:T(8,128)S(1)}, u32[]{:S(2)}, u32[]{:S(2)}) collective-permute-start(f32[128,128]{1,0:T(8,128)S(1)} %collective-permute-done.27.refs_5_), channel_id=1, source_target_pairs={{0,4},{4,0},{8,12},{12,8},{1,5},{5,1},{9,13},{13,9},{2,6},{6,2},{1... | collective-permute-start | bytes 196616 | tf_op jit(solution)/shard_map/ppermute | solution.py:500

commit v5 on v4

--- a/solution.py
+++ b/solution.py
@@ -161,7 +161,7 @@
         ),
         scratch_shapes=[pltpu.VMEM((sites, 2 * rows, 2 * lanes), BF16)],
         compiler_params=params(),
-        cost_estimate=cost(8e9, 16e6),
+        cost_estimate=cost(1e11, 16e6),
         name="first_local",
     )(x, in_hbm(source), in_hbm(couplings))
 
@@ -186,7 +186,7 @@
         out_specs=pl.BlockSpec((1, rows, lanes), lambda s: (s, 0, 0)),
         scratch_shapes=[pltpu.VMEM((sites, 2 * rows, 2 * lanes), BF16)],
         compiler_params=params(),
-        cost_estimate=cost(8e9, 8e6),
+        cost_estimate=cost(1e11, 8e6),
         name="local_part",
     )(x, source, local)
 
@@ -461,7 +461,7 @@
 
 def final_kernel(count, base, vectors, *refs):
     own, other, (out, stacks) = refs[:count], refs[count:-2], refs[-2:]
-    step = out.shape[0]
+    step, _, lanes = out.shape
     first = pl.program_id(0) * step
 
     @pl.when(first == 0)
@@ -469,8 +469,14 @@
         group = lax.axis_index("groups")
         place_pieces([join_halves(a[...], b[...], group) for a, b in zip(own, other)], stacks)
 
+    number, rows = vectors.shape[3], out.shape[1]
     for index in range(step):
-        out[index] = base[first + index] + expand(first + index, vectors, stacks)
+        total = base[first + index]
+        for half in range(2):
+            left = vectors[first + index, half]
+            right = stacks[half * number : (half + 1) * number]
+            total = total + (matmul(left[:rows], right[:, :lanes]) + (matmul(left[:rows], right[:, lanes:]) + matmul(left[rows:], right[:, :lanes])))
+        out[index] = total
 
 
 def final(base, own, other, vectors):
@@ -528,20 +534,16 @@
     return pieces
 
 
-def both_doubling(part):
+def across_groups(part, mask):
     groups, count = lax.axis_size("groups"), lax.axis_size("space")
-    mask = count // 2
     pairs = [(g * count + s, (g ^ 1) * count + (s ^ mask)) for g in range(groups) for s in range(count)]
-    across = lax.ppermute(part, ("groups", "space"), pairs)
-    other = [crossed(part, "groups", 1), across]
-    own = [part, crossed(part, "space", mask)]
-    return doubling(own, mask // 2), doubling(other, mask // 2)
+    return [crossed(part, "groups", 1), lax.ppermute(part, ("groups", "space"), pairs)]
 
 
 def over_time(part):
     count = lax.axis_size("tm")
     if count <= 4:
-        return [part] + [shifted(part, "tm", step) for step in range(1, count)]
+        return [part] + [crossed(part, "tm", mask) for mask in range(1, count)]
     mask = 1
     while mask < count:
         part = part + crossed(part, "tm", mask)
@@ -572,10 +574,10 @@
                 other_x = crossed(x, "groups", 1)
             rest = local_part(x, half_source, local, ny, nx)
         forward_z, backward_z, forward_t, backward_t = faces
+        rest = backward_face(rest, backward_t, halo)
         rest = z_faces(rest, forward_z, backward_z, halo)
         if sweep and last:
             rest, other_x = lax.optimization_barrier((rest, other_x))
-        rest = backward_face(rest, backward_t, halo)
         residual, keep, send = forward_face(rest, forward_t, halo, by_rows)
         part = halving(keep, send)
         if last:
@@ -588,7 +590,11 @@
         if not last:
             x = update(x, residual, doubling([d], blocks // 2), by_columns)
     base, full_residual = join(x, other_x, residual, other_residual)
-    whole = final(base, *both_doubling(d), by_columns)
+    mask = blocks // 2
+    other = across_groups(d, mask)
+    own = [d, crossed(d, "space", mask)]
+    other[1], base = lax.optimization_barrier((other[1], base))
+    whole = final(base, doubling(own, mask // 2), doubling(other, mask // 2), by_columns)
     shape = source.shape
     return whole.reshape(shape), full_residual.reshape(shape)
 

time: 101 us -> 99.6 us (0.986)
  waiting for transfers between devices: 43.1 us -> 39.6 us
  starting transfers between devices: 30.1 us -> 31.6 us
    ppermute x15 -> x21, starting transfers between devices: 8.09 us -> 18.2 us  [crossed(): return lax.ppermute(value, axis, [(i, i ^ mask) for i in range(count)])]
    ppermute x14 -> x8, waiting for transfers between devices: 24.4 us -> 14.9 us  [shifted(): lax.ppermute(value, axis, [(i, (i + step) % count) for i in range(count)])]
    ppermute x14 -> x8, starting transfers between devices: 20.2 us -> 11 us  [shifted(): lax.ppermute(value, axis, [(i, (i + step) % count) for i in range(count)])]
    ppermute x15 -> x21, waiting for transfers between devices: 17.3 us -> 24.3 us  [crossed(): return lax.ppermute(value, axis, [(i, i ^ mask) for i in range(count)])]
    ppermute x1, waiting for transfers between devices: 1.41 us -> 0.32 us  [across_groups(): lax.ppermute(part, ('groups', 'space'), pairs)]
  transfers between devices with their start and end apart: 30 -> 30, of which waited for: 20 -> 18; matrix products, arithmetic and copies ran while one was open for 0% -> 0% of each run, Pallas kernels for 18% -> 18%
where the time goes in v5:
time: 99.6 us; the launch traced here: 99.2 us
  waiting for transfers between devices  39.6 us (40%)
  starting transfers between devices  31.6 us (32%)
  Pallas kernels  26.1 us (26%)
  local copies, waits for them, and re-layouts  1.13 us (1%)
    ppermute x21, waiting for transfers between devices, crossed(): return lax.ppermute(value, axis, [(i, i ^ mask) for i in range(count)])  24.3 us
    ppermute x21, starting transfers between devices, crossed(): return lax.ppermute(value, axis, [(i, i ^ mask) for i in range(count)])  18.2 us
    ppermute x8, waiting for transfers between devices, shifted(): lax.ppermute(value, axis, [(i, (i + step) % count) for i in range(count)])  14.9 us
    ppermute x8, starting transfers between devices, shifted(): lax.ppermute(value, axis, [(i, (i + step) % count) for i in range(count)])  11 us
    pallas_call x1, Pallas kernels, first_local(): pl.pallas_call(functools.partial(first_kernel, ny, nx), grid=(sites,), ou...  7.69 us
    pallas_call x1, Pallas kernels, vectors_parts(): pl.pallas_call(vectors_kernel, grid=(sites // step,), out_shape=(pltpu.VM...  3.72 us
    pallas_call x1, Pallas kernels, final(): pl.pallas_call(functools.partial(final_kernel, len(own)), grid=(sites //...  3.52 us
    pallas_call x1, Pallas kernels, local_part(): pl.pallas_call(functools.partial(local_kernel, ny, nx), grid=(sites,), ou...  2.97 us
  transfers between devices with their start and end apart: 30, of which 18 were waited for; matrix products, arithmetic and copies ran while one was open for 0% of the time, Pallas kernels for 18%

profile of v5, /device:TPU:0, one launch (start us, length us, event | category | flops | bytes accessed | tf_op | source)
XLA Modules:
  0.0 99.2 jit_solution(11019994561309701053)
XLA Ops:
  0.6 1.1 %copy-done = f32[1,1,2,4,96,256]{5,4,3,2,1,0:T(8,128)S(1)} copy-done((f32[1,1,2,4,96,256]{5,4,3,2,1,0:T(8,128)S(1)}, f32[1,1,2,4,96,256]{5,4,3,2,1,0:T(8,128)}, u32[]{:S(2)}) %copy-start) | copy-done | bytes 786456
  2.0 3.1 %collective-permute-start = (f32[8,96,128]{2,1,0:T(8,128)S(1)}, f32[8,96,128]{2,1,0:T(8,128)S(1)}, u32[]{:S(2)}, u32[]{:S(2)}) collective-permute-start(f32[8,96,128]{2,1,0:T(8,128)S(1)} %pack.1.x_ref.x), channel_id=1, source_target_pairs={{0,1},{1,2},{2,3},{3,0},{4,5},{5,6},{6,7},{7,4},{8,9},{9,10},{10,1... | collective-permute-start | bytes 1179656 | tf_op jit(solution)/shard_map/ppermute | solution.py:501
  5.1 0.7 collective-permute-start.1
  5.8 2.4 %collective-permute-start.3 = (f32[8,96,128]{2,1,0:T(8,128)S(1)}, f32[8,96,128]{2,1,0:T(8,128)S(1)}, u32[]{:S(2)}, u32[]{:S(2)}) collective-permute-start(f32[8,96,128]{2,1,0:T(8,128)S(1)} %pack.1.x_ref.x), channel_id=1, source_target_pairs={{0,3},{1,0},{2,1},{3,2},{4,7},{5,4},{6,5},{7,6},{8,11},{9,8},{10,9... | collective-permute-start | bytes 1179656 | tf_op jit(solution)/shard_map/ppermute | solution.py:501
  8.1 7.7 %first_local.1 = (f32[8,96,128]{2,1,0:T(8,128)S(1)}, f32[8,96,128]{2,1,0:T(8,128)S(1)}, bf16[5,8,192,192]{3,2,1,0:T(8,128)(2,1)S(1)}, bf16[4,8,192,192]{3,2,1,0:T(8,128)(2,1)S(1)}) custom-call(f32[8,96,128]{2,1,0:T(8,128)S(1)} %pack.1.x_ref.x, f32[8,96,256]{2,1,0:T(8,128)} %bitcast.11, f32[9,8,96,192]{3,2,1,0:T(8,128)} %bitcast.10), custom_call_target="tpu_custom_call" | custom-call | flops 99999997952 | bytes 16000000 | tf_op jit(solution)/shard_map/first_local/pallas_call | solution.py:142
  15.8 3.7 %vectors_parts.1 = (bf16[1024,1536]{1,0:T(8,128)(2,1)S(1)}, bf16[8,2,192,512]{3,2,1,0:T(8,128)(2,1)S(1)}) custom-call(f32[1536,512]{1,0:T(8,128)} %bitcast.9), custom_call_target="tpu_custom_call" | custom-call | flops 1000000 | bytes 9000000 | tf_op jit(solution)/shard_map/vectors_parts/pallas_call | solution.py:222
  19.6 0.5 backward_face.2.rest
  20.1 0.7 z_faces.2.rest
  20.7 4.0 %collective-permute-done.3.forward = f32[8,96,128]{2,1,0:T(8,128)S(1)} collective-permute-done((f32[8,96,128]{2,1,0:T(8,128)S(1)}, f32[8,96,128]{2,1,0:T(8,128)S(1)}, u32[]{:S(2)}, u32[]{:S(2)}) %collective-permute-start.3) | collective-permute-done | bytes 393248 | tf_op jit(solution)/shard_map/ppermute | solution.py:501
  24.7 1.4 %forward_face.2 = (f32[8,96,128]{2,1,0:T(8,128)S(1)}, f32[256,128]{1,0:T(8,128)S(1)}, f32[256,128]{1,0:T(8,128)S(1)}) custom-call(f32[8,96,128]{2,1,0:T(8,128)S(1)} %z_faces.2.rest, f32[8,96,128]{2,1,0:T(8,128)S(1)} %collective-permute-done.3.forward, bf16[4,8,192,192]{3,2,1,0:T(8,128)(2,1)S(1)} %get-tuple-element.32.matrix, ...), custom_call_target="tpu_custom_call" | custom-call | flops 2000000000 | bytes 8000000 | tf_op jit(solution)/shard_map/forward_face/pallas_call | solution.py:328
  26.3 1.2 %collective-permute-done.4.received = f32[256,128]{1,0:T(8,128)S(1)} collective-permute-done((f32[256,128]{1,0:T(8,128)S(1)}, f32[256,128]{1,0:T(8,128)S(1)}, u32[]{:S(2)}, u32[]{:S(2)}) %collective-permute-start.4) | collective-permute-done | bytes 131104 | tf_op jit(solution)/shard_map/ppermute | solution.py:506
  27.5 1.6 %collective-permute-start.5 = (f32[128,128]{1,0:T(8,128)S(1)}, f32[128,128]{1,0:T(8,128)S(1)}, u32[]{:S(2)}, u32[]{:S(2)}) collective-permute-start(f32[128,128]{1,0:T(8,128)S(1)} %get-tuple-element.39), channel_id=1, source_target_pairs={{0,8},{4,12},{8,0},{12,4},{1,9},{5,13},{9,1},{13,5},{2,10},{6,14},... | collective-permute-start | bytes 196616 | tf_op jit(solution)/shard_map/ppermute | solution.py:506
  29.1 2.8 %collective-permute-done.5.right = f32[128,128]{1,0:T(8,128)S(1)} collective-permute-done((f32[128,128]{1,0:T(8,128)S(1)}, f32[128,128]{1,0:T(8,128)S(1)}, u32[]{:S(2)}, u32[]{:S(2)}) %collective-permute-start.5) | collective-permute-done | bytes 65568 | tf_op jit(solution)/shard_map/ppermute | solution.py:506
  31.9 0.6 collective-permute-start.6
  32.5 2.9 %collective-permute-start.7 = (f32[128,128]{1,0:T(8,128)S(1)}, f32[128,128]{1,0:T(8,128)S(1)}, u32[]{:S(2)}, u32[]{:S(2)}) collective-permute-start(f32[128,128]{1,0:T(8,128)S(1)} %add.2.refs_0_), channel_id=1, source_target_pairs={{0,2},{1,3},{2,0},{3,1},{4,6},{5,7},{6,4},{7,5},{8,10},{9,11},{10,... | collective-permute-start | bytes 196616 | tf_op jit(solution)/shard_map/ppermute | solution.py:506
  35.4 0.9 collective-permute-start.8
  36.5 1.3 %collective-permute-done.7.refs_2_ = f32[128,128]{1,0:T(8,128)S(1)} collective-permute-done((f32[128,128]{1,0:T(8,128)S(1)}, f32[128,128]{1,0:T(8,128)S(1)}, u32[]{:S(2)}, u32[]{:S(2)}) %collective-permute-start.7) | collective-permute-done | bytes 65568 | tf_op jit(solution)/shard_map/ppermute | solution.py:506
  37.8 3.7 %collective-permute-done.8.refs_3_ = f32[128,128]{1,0:T(8,128)S(1)} collective-permute-done((f32[128,128]{1,0:T(8,128)S(1)}, f32[128,128]{1,0:T(8,128)S(1)}, u32[]{:S(2)}, u32[]{:S(2)}) %collective-permute-start.8) | collective-permute-done | bytes 65568 | tf_op jit(solution)/shard_map/ppermute | solution.py:506
  41.6 1.6 %collective-permute-start.9 = (f32[128,128]{1,0:T(8,128)S(1)}, f32[128,128]{1,0:T(8,128)S(1)}, u32[]{:S(2)}, u32[]{:S(2)}) collective-permute-start(f32[128,128]{1,0:T(8,128)S(1)} %scale.2.refs_0_), channel_id=1, source_target_pairs={{0,8},{4,12},{8,0},{12,4},{1,9},{5,13},{9,1},{13,5},{2,10},{6,14},... | collective-permute-start | bytes 196616 | tf_op jit(solution)/shard_map/ppermute | solution.py:506
  43.1 2.8 %collective-permute-done.9.refs_1_ = f32[128,128]{1,0:T(8,128)S(1)} collective-permute-done((f32[128,128]{1,0:T(8,128)S(1)}, f32[128,128]{1,0:T(8,128)S(1)}, u32[]{:S(2)}, u32[]{:S(2)}) %collective-permute-start.9) | collective-permute-done | bytes 65568 | tf_op jit(solution)/shard_map/ppermute | solution.py:506
  45.9 1.2 %collective-permute-done.11.refs_3_ = f32[128,128]{1,0:T(8,128)S(1)} collective-permute-done((f32[128,128]{1,0:T(8,128)S(1)}, f32[128,128]{1,0:T(8,128)S(1)}, u32[]{:S(2)}, u32[]{:S(2)}) %collective-permute-start.11) | collective-permute-done | bytes 65568 | tf_op jit(solution)/shard_map/ppermute | solution.py:506
  47.2 1.1 %update.1.x_ref.x = f32[8,96,128]{2,1,0:T(8,128)S(1)} custom-call(f32[8,96,128]{2,1,0:T(8,128)S(1)} %pack.1.x_ref.x, f32[8,96,128]{2,1,0:T(8,128)S(1)} %get-tuple-element.34.residual, bf16[8,2,192,512]{3,2,1,0:T(8,128)(2,1)S(1)} %get-tuple-element.35.vectors, f32[128,128]{1,0:T(8,128)S(1)} %scale.2.refs_0_, f32[128,128]{1,0:T(8,128)S(1)} %collective-permute-done.9.refs_1_, ...), custom_call_target="tpu_custom_call" | custom-call | flops 1000000000 | bytes 8000000 | tf_op jit(solution)/shard_map/update/pallas_call | solution.py:427
  48.4 1.3 %collective-permute-start.13 = (f32[8,96,128]{2,1,0:T(8,128)S(1)}, f32[8,96,128]{2,1,0:T(8,128)S(1)}, u32[]{:S(2)}, u32[]{:S(2)}) collective-permute-start(f32[8,96,128]{2,1,0:T(8,128)S(1)} %update.1.x_ref.x), channel_id=1, source_target_pairs={{0,12},{4,0},{8,4},{12,8},{1,13},{5,1},{9,5},{13,9},{2,14},{6,2},{... | collective-permute-start | bytes 1179656 | tf_op jit(solution)/shard_map/ppermute | solution.py:501
  49.7 1.5 %collective-permute-start.15 = (f32[8,96,128]{2,1,0:T(8,128)S(1)}, f32[8,96,128]{2,1,0:T(8,128)S(1)}, u32[]{:S(2)}, u32[]{:S(2)}) collective-permute-start(f32[8,96,128]{2,1,0:T(8,128)S(1)} %update.1.x_ref.x), channel_id=1, source_target_pairs={{0,16},{16,0},{1,17},{17,1},{2,18},{18,2},{3,19},{19,3},{4,20},{20... | collective-permute-start | bytes 1179656 | tf_op jit(solution)/shard_map/ppermute | solution.py:506
  51.2 3.5 %collective-permute-start.16 = (f32[8,96,128]{2,1,0:T(8,128)S(1)}, f32[8,96,128]{2,1,0:T(8,128)S(1)}, u32[]{:S(2)}, u32[]{:S(2)}) collective-permute-start(f32[8,96,128]{2,1,0:T(8,128)S(1)} %update.1.x_ref.x), channel_id=1, source_target_pairs={{0,3},{1,0},{2,1},{3,2},{4,7},{5,4},{6,5},{7,6},{8,11},{9,8},{10,9... | collective-permute-start | bytes 1179656 | tf_op jit(solution)/shard_map/ppermute | solution.py:501
  54.7 3.0 %local_part.1.rest = f32[8,96,128]{2,1,0:T(8,128)S(1)} custom-call(f32[8,96,128]{2,1,0:T(8,128)S(1)} %update.1.x_ref.x, f32[8,96,128]{2,1,0:T(8,128)S(1)} %get-tuple-element.40.source, bf16[5,8,192,192]{3,2,1,0:T(8,128)(2,1)S(1)} %get-tuple-element.41.local), custom_call_target="tpu_custom_call" | custom-call | flops 99999997952 | bytes 8000000 | tf_op jit(solution)/shard_map/local_part/pallas_call | solution.py:177
  57.7 4.5 %collective-permute-done.12.backward = f32[8,96,128]{2,1,0:T(8,128)S(1)} collective-permute-done((f32[8,96,128]{2,1,0:T(8,128)S(1)}, f32[8,96,128]{2,1,0:T(8,128)S(1)}, u32[]{:S(2)}, u32[]{:S(2)}) %collective-permute-start.12) | collective-permute-done | bytes 393248 | tf_op jit(solution)/shard_map/ppermute | solution.py:501
  62.2 0.5 backward_face.3.rest
  62.6 0.7 z_faces.3.rest
  63.3 6.4 %collective-permute-done.16.forward = f32[8,96,128]{2,1,0:T(8,128)S(1)} collective-permute-done((f32[8,96,128]{2,1,0:T(8,128)S(1)}, f32[8,96,128]{2,1,0:T(8,128)S(1)}, u32[]{:S(2)}, u32[]{:S(2)}) %collective-permute-start.16) | collective-permute-done | bytes 393248 | tf_op jit(solution)/shard_map/ppermute | solution.py:501
  69.8 1.4 %forward_face.3 = (f32[8,96,128]{2,1,0:T(8,128)S(1)}, f32[256,128]{1,0:T(8,128)S(1)}, f32[256,128]{1,0:T(8,128)S(1)}) custom-call(f32[8,96,128]{2,1,0:T(8,128)S(1)} %z_faces.3.rest, f32[8,96,128]{2,1,0:T(8,128)S(1)} %collective-permute-done.16.forward, bf16[4,8,192,192]{3,2,1,0:T(8,128)(2,1)S(1)} %get-tuple-element.32.matrix, ...), custom_call_target="tpu_custom_call" | custom-call | flops 2000000000 | bytes 8000000 | tf_op jit(solution)/shard_map/forward_face/pallas_call | solution.py:328
  71.3 1.3 %collective-permute-done.17.received = f32[256,128]{1,0:T(8,128)S(1)} collective-permute-done((f32[256,128]{1,0:T(8,128)S(1)}, f32[256,128]{1,0:T(8,128)S(1)}, u32[]{:S(2)}, u32[]{:S(2)}) %collective-permute-start.17) | collective-permute-done | bytes 131104 | tf_op jit(solution)/shard_map/ppermute | solution.py:506
  72.6 1.6 %collective-permute-start.18 = (f32[128,128]{1,0:T(8,128)S(1)}, f32[128,128]{1,0:T(8,128)S(1)}, u32[]{:S(2)}, u32[]{:S(2)}) collective-permute-start(f32[128,128]{1,0:T(8,128)S(1)} %get-tuple-element.46), channel_id=1, source_target_pairs={{0,8},{4,12},{8,0},{12,4},{1,9},{5,13},{9,1},{13,5},{2,10},{6,14},... | collective-permute-start | bytes 196616 | tf_op jit(solution)/shard_map/ppermute | solution.py:506
  74.2 2.8 %collective-permute-done.18.right = f32[128,128]{1,0:T(8,128)S(1)} collective-permute-done((f32[128,128]{1,0:T(8,128)S(1)}, f32[128,128]{1,0:T(8,128)S(1)}, u32[]{:S(2)}, u32[]{:S(2)}) %collective-permute-start.18) | collective-permute-done | bytes 65568 | tf_op jit(solution)/shard_map/ppermute | solution.py:506
  77.0 1.6 %collective-permute-start.22 = (f32[8,96,128]{2,1,0:T(8,128)S(1)}, f32[8,96,128]{2,1,0:T(8,128)S(1)}, u32[]{:S(2)}, u32[]{:S(2)}) collective-permute-start(f32[8,96,128]{2,1,0:T(8,128)S(1)} %get-tuple-element.49.residual), channel_id=1, source_target_pairs={{0,16},{16,0},{1,17},{17,1},{2,18},{18,2},{3,19},{19,3},{4,20},{20... | collective-permute-start | bytes 1179656 | tf_op jit(solution)/shard_map/ppermute | solution.py:506
  78.5 0.6 collective-permute-start.19
  79.4 3.5 %collective-permute-start.21 = (f32[128,128]{1,0:T(8,128)S(1)}, f32[128,128]{1,0:T(8,128)S(1)}, u32[]{:S(2)}, u32[]{:S(2)}) collective-permute-start(f32[128,128]{1,0:T(8,128)S(1)} %add.3.refs_0_), channel_id=1, source_target_pairs={{0,3},{1,2},{2,1},{3,0},{4,7},{5,6},{6,5},{7,4},{8,11},{9,10},{10,... | collective-permute-start | bytes 196616 | tf_op jit(solution)/shard_map/ppermute | solution.py:506
  82.9 3.2 %collective-permute-done.20.refs_2_ = f32[128,128]{1,0:T(8,128)S(1)} collective-permute-done((f32[128,128]{1,0:T(8,128)S(1)}, f32[128,128]{1,0:T(8,128)S(1)}, u32[]{:S(2)}, u32[]{:S(2)}) %collective-permute-start.20) | collective-permute-done | bytes 65568 | tf_op jit(solution)/shard_map/ppermute | solution.py:506
  86.2 0.9 collective-permute-done.22.other_residual
  87.1 2.5 %collective-permute-start.23 = (f32[128,128]{1,0:T(8,128)S(1)}, f32[128,128]{1,0:T(8,128)S(1)}, u32[]{:S(2)}, u32[]{:S(2)}) collective-permute-start(f32[128,128]{1,0:T(8,128)S(1)} %scale.3.refs_0_), channel_id=1, source_target_pairs={{0,24},{4,28},{8,16},{12,20},{16,8},{20,12},{24,0},{28,4},{1,25},{... | collective-permute-start | bytes 196616 | tf_op jit(solution)/shard_map/ppermute | solution.py:540
  89.6 0.5 collective-permute-start.24
  90.2 0.5 collective-permute-start.27
  90.7 1.4 %join.1 = (f32[8,96,256]{2,1,0:T(8,128)S(1)}, f32[8,96,256]{2,1,0:T(8,128)}) custom-call(f32[8,96,128]{2,1,0:T(8,128)S(1)} %update.1.x_ref.x, f32[8,96,128]{2,1,0:T(8,128)S(1)} %collective-permute-done.15.other_x, f32[8,96,128]{2,1,0:T(8,128)S(1)} %get-tuple-element.49.residual, f32[8,96,128]{2,1,0:T(8,128)S(1)} %collective-permute-done.22.other_residual), custom_call_target="tpu_custom_call" | custom-call | flops 1000000 | bytes 4000000 | tf_op jit(solution)/shard_map/join/pallas_call | solution.py:451
  92.6 1.3 %collective-permute-done.24.refs_1_ = f32[128,128]{1,0:T(8,128)S(1)} collective-permute-done((f32[128,128]{1,0:T(8,128)S(1)}, f32[128,128]{1,0:T(8,128)S(1)}, u32[]{:S(2)}, u32[]{:S(2)}) %collective-permute-start.24) | collective-permute-done | bytes 65568 | tf_op jit(solution)/shard_map/ppermute | solution.py:506
  93.9 0.5 collective-permute-done.27.refs_4_
  94.5 0.7 collective-permute-done.26.refs_3_
  95.2 0.5 collective-permute-done.28.refs_6_
  95.7 3.5 %final.1 = f32[8,96,256]{2,1,0:T(8,128)} custom-call(f32[8,96,256]{2,1,0:T(8,128)S(1)} %get-tuple-element.57.base, bf16[8,2,192,512]{3,2,1,0:T(8,128)(2,1)S(1)} %get-tuple-element.35.vectors, f32[128,128]{1,0:T(8,128)S(1)} %scale.3.refs_0_, f32[128,128]{1,0:T(8,128)S(1)} %collective-permute-done.24.refs_1_, f32[128,128]{1,0:T(8,128)S(1)} %collective-permute-done.25.refs_2_, ...), custom_call_target="tpu_custom_call" | custom-call | flops 2000000000 | bytes 8000000 | tf_op jit(solution)/shard_map/final/pallas_call | solution.py:486
  (36 shorter events, 1.8 us)
Async XLA Ops:
  0.6 1.1 %copy-start = (f32[1,1,2,4,96,256]{5,4,3,2,1,0:T(8,128)S(1)}, f32[1,1,2,4,96,256]{5,4,3,2,1,0:T(8,128)}, u32[]{:S(2)}) copy-start(f32[1,1,2,4,96,256]{5,4,3,2,1,0:T(8,128)} %param.7) | copy-start | bytes 2359300
  2.0 17.5 %collective-permute-start = (f32[8,96,128]{2,1,0:T(8,128)S(1)}, f32[8,96,128]{2,1,0:T(8,128)S(1)}, u32[]{:S(2)}, u32[]{:S(2)}) collective-permute-start(f32[8,96,128]{2,1,0:T(8,128)S(1)} %pack.1.x_ref.x), channel_id=1, source_target_pairs={{0,1},{1,2},{2,3},{3,0},{4,5},{5,6},{6,7},{7,4},{8,9},{9,10},{10,1... | collective-permute-start | bytes 1179656 | tf_op jit(solution)/shard_map/ppermute | solution.py:501
  5.1 14.9 %collective-permute-start.1 = (f32[8,96,128]{2,1,0:T(8,128)S(1)}, f32[8,96,128]{2,1,0:T(8,128)S(1)}, u32[]{:S(2)}, u32[]{:S(2)}) collective-permute-start(f32[8,96,128]{2,1,0:T(8,128)S(1)} %pack.1.x_ref.x), channel_id=1, source_target_pairs={{0,12},{4,0},{8,4},{12,8},{1,13},{5,1},{9,5},{13,9},{2,14},{6,2},{... | collective-permute-start | bytes 1179656 | tf_op jit(solution)/shard_map/ppermute | solution.py:501
  5.8 14.3 %collective-permute-start.2 = (f32[8,96,128]{2,1,0:T(8,128)S(1)}, f32[8,96,128]{2,1,0:T(8,128)S(1)}, u32[]{:S(2)}, u32[]{:S(2)}) collective-permute-start(f32[8,96,128]{2,1,0:T(8,128)S(1)} %pack.1.x_ref.x), channel_id=1, source_target_pairs={{0,4},{4,8},{8,12},{12,0},{1,5},{5,9},{9,13},{13,1},{2,6},{6,10},{... | collective-permute-start | bytes 1179656 | tf_op jit(solution)/shard_map/ppermute | solution.py:501
  5.8 18.9 %collective-permute-start.3 = (f32[8,96,128]{2,1,0:T(8,128)S(1)}, f32[8,96,128]{2,1,0:T(8,128)S(1)}, u32[]{:S(2)}, u32[]{:S(2)}) collective-permute-start(f32[8,96,128]{2,1,0:T(8,128)S(1)} %pack.1.x_ref.x), channel_id=1, source_target_pairs={{0,3},{1,0},{2,1},{3,2},{4,7},{5,4},{6,5},{7,6},{8,11},{9,8},{10,9... | collective-permute-start | bytes 1179656 | tf_op jit(solution)/shard_map/ppermute | solution.py:501
  24.7 11.7 %copy-start.1 = (f32[2,512]{1,0:T(2,128)S(1)}, f32[2,512]{1,0:T(2,128)}, u32[]{:S(2)}) copy-start(f32[2,512]{1,0:T(2,128)} %inverse.1) | copy-start | bytes 12292
  26.1 1.4 %collective-permute-start.4 = (f32[256,128]{1,0:T(8,128)S(1)}, f32[256,128]{1,0:T(8,128)S(1)}, u32[]{:S(2)}, u32[]{:S(2)}) collective-permute-start(f32[256,128]{1,0:T(8,128)S(1)} %get-tuple-element.37), channel_id=1, source_target_pairs={{0,4},{4,0},{8,12},{12,8},{1,5},{5,1},{9,13},{13,9},{2,6},{6,2},{1... | collective-permute-start | bytes 393224 | tf_op jit(solution)/shard_map/ppermute | solution.py:506
  27.5 4.3 %collective-permute-start.5 = (f32[128,128]{1,0:T(8,128)S(1)}, f32[128,128]{1,0:T(8,128)S(1)}, u32[]{:S(2)}, u32[]{:S(2)}) collective-permute-start(f32[128,128]{1,0:T(8,128)S(1)} %get-tuple-element.39), channel_id=1, source_target_pairs={{0,8},{4,12},{8,0},{12,4},{1,9},{5,13},{9,1},{13,5},{2,10},{6,14},... | collective-permute-start | bytes 196616 | tf_op jit(solution)/shard_map/ppermute | solution.py:506
  31.9 4.6 %collective-permute-start.6 = (f32[128,128]{1,0:T(8,128)S(1)}, f32[128,128]{1,0:T(8,128)S(1)}, u32[]{:S(2)}, u32[]{:S(2)}) collective-permute-start(f32[128,128]{1,0:T(8,128)S(1)} %add.2.refs_0_), channel_id=1, source_target_pairs={{0,1},{1,0},{2,3},{3,2},{4,5},{5,4},{6,7},{7,6},{8,9},{9,8},{10,11... | collective-permute-start | bytes 196616 | tf_op jit(solution)/shard_map/ppermute | solution.py:506
  32.5 5.3 %collective-permute-start.7 = (f32[128,128]{1,0:T(8,128)S(1)}, f32[128,128]{1,0:T(8,128)S(1)}, u32[]{:S(2)}, u32[]{:S(2)}) collective-permute-start(f32[128,128]{1,0:T(8,128)S(1)} %add.2.refs_0_), channel_id=1, source_target_pairs={{0,2},{1,3},{2,0},{3,1},{4,6},{5,7},{6,4},{7,5},{8,10},{9,11},{10,... | collective-permute-start | bytes 196616 | tf_op jit(solution)/shard_map/ppermute | solution.py:506
  35.4 6.1 %collective-permute-start.8 = (f32[128,128]{1,0:T(8,128)S(1)}, f32[128,128]{1,0:T(8,128)S(1)}, u32[]{:S(2)}, u32[]{:S(2)}) collective-permute-start(f32[128,128]{1,0:T(8,128)S(1)} %add.2.refs_0_), channel_id=1, source_target_pairs={{0,3},{1,2},{2,1},{3,0},{4,7},{5,6},{6,5},{7,4},{8,11},{9,10},{10,... | collective-permute-start | bytes 196616 | tf_op jit(solution)/shard_map/ppermute | solution.py:506
  41.6 4.3 %collective-permute-start.9 = (f32[128,128]{1,0:T(8,128)S(1)}, f32[128,128]{1,0:T(8,128)S(1)}, u32[]{:S(2)}, u32[]{:S(2)}) collective-permute-start(f32[128,128]{1,0:T(8,128)S(1)} %scale.2.refs_0_), channel_id=1, source_target_pairs={{0,8},{4,12},{8,0},{12,4},{1,9},{5,13},{9,1},{13,5},{2,10},{6,14},... | collective-permute-start | bytes 196616 | tf_op jit(solution)/shard_map/ppermute | solution.py:506
  43.1 2.8 %collective-permute-start.10 = (f32[128,128]{1,0:T(8,128)S(1)}, f32[128,128]{1,0:T(8,128)S(1)}, u32[]{:S(2)}, u32[]{:S(2)}) collective-permute-start(f32[128,128]{1,0:T(8,128)S(1)} %scale.2.refs_0_), channel_id=1, source_target_pairs={{0,4},{4,0},{8,12},{12,8},{1,5},{5,1},{9,13},{13,9},{2,6},{6,2},{1... | collective-permute-start | bytes 196616 | tf_op jit(solution)/shard_map/ppermute | solution.py:506
  45.9 1.3 %collective-permute-start.11 = (f32[128,128]{1,0:T(8,128)S(1)}, f32[128,128]{1,0:T(8,128)S(1)}, u32[]{:S(2)}, u32[]{:S(2)}) collective-permute-start(f32[128,128]{1,0:T(8,128)S(1)} %collective-permute-done.9.refs_1_), channel_id=1, source_target_pairs={{0,4},{4,0},{8,12},{12,8},{1,5},{5,1},{9,13},{13,9},{2,6},{6,2},{1... | collective-permute-start | bytes 196616 | tf_op jit(solution)/shard_map/ppermute | solution.py:506
  48.3 13.9 %collective-permute-start.12 = (f32[8,96,128]{2,1,0:T(8,128)S(1)}, f32[8,96,128]{2,1,0:T(8,128)S(1)}, u32[]{:S(2)}, u32[]{:S(2)}) collective-permute-start(f32[8,96,128]{2,1,0:T(8,128)S(1)} %update.1.x_ref.x), channel_id=1, source_target_pairs={{0,1},{1,2},{2,3},{3,0},{4,5},{5,6},{6,7},{7,4},{8,9},{9,10},{10,1... | collective-permute-start | bytes 1179656 | tf_op jit(solution)/shard_map/ppermute | solution.py:501
  48.4 14.2 %collective-permute-start.13 = (f32[8,96,128]{2,1,0:T(8,128)S(1)}, f32[8,96,128]{2,1,0:T(8,128)S(1)}, u32[]{:S(2)}, u32[]{:S(2)}) collective-permute-start(f32[8,96,128]{2,1,0:T(8,128)S(1)} %update.1.x_ref.x), channel_id=1, source_target_pairs={{0,12},{4,0},{8,4},{12,8},{1,13},{5,1},{9,5},{13,9},{2,14},{6,2},{... | collective-permute-start | bytes 1179656 | tf_op jit(solution)/shard_map/ppermute | solution.py:501
  49.7 12.9 %collective-permute-start.14 = (f32[8,96,128]{2,1,0:T(8,128)S(1)}, f32[8,96,128]{2,1,0:T(8,128)S(1)}, u32[]{:S(2)}, u32[]{:S(2)}) collective-permute-start(f32[8,96,128]{2,1,0:T(8,128)S(1)} %update.1.x_ref.x), channel_id=1, source_target_pairs={{0,4},{4,8},{8,12},{12,0},{1,5},{5,9},{9,13},{13,1},{2,6},{6,10},{... | collective-permute-start | bytes 1179656 | tf_op jit(solution)/shard_map/ppermute | solution.py:501
  49.7 13.6 %collective-permute-start.15 = (f32[8,96,128]{2,1,0:T(8,128)S(1)}, f32[8,96,128]{2,1,0:T(8,128)S(1)}, u32[]{:S(2)}, u32[]{:S(2)}) collective-permute-start(f32[8,96,128]{2,1,0:T(8,128)S(1)} %update.1.x_ref.x), channel_id=1, source_target_pairs={{0,16},{16,0},{1,17},{17,1},{2,18},{18,2},{3,19},{19,3},{4,20},{20... | collective-permute-start | bytes 1179656 | tf_op jit(solution)/shard_map/ppermute | solution.py:506
  51.2 18.6 %collective-permute-start.16 = (f32[8,96,128]{2,1,0:T(8,128)S(1)}, f32[8,96,128]{2,1,0:T(8,128)S(1)}, u32[]{:S(2)}, u32[]{:S(2)}) collective-permute-start(f32[8,96,128]{2,1,0:T(8,128)S(1)} %update.1.x_ref.x), channel_id=1, source_target_pairs={{0,3},{1,0},{2,1},{3,2},{4,7},{5,4},{6,5},{7,6},{8,11},{9,8},{10,9... | collective-permute-start | bytes 1179656 | tf_op jit(solution)/shard_map/ppermute | solution.py:501
  71.2 1.4 %collective-permute-start.17 = (f32[256,128]{1,0:T(8,128)S(1)}, f32[256,128]{1,0:T(8,128)S(1)}, u32[]{:S(2)}, u32[]{:S(2)}) collective-permute-start(f32[256,128]{1,0:T(8,128)S(1)} %get-tuple-element.44), channel_id=1, source_target_pairs={{0,4},{4,0},{8,12},{12,8},{1,5},{5,1},{9,13},{13,9},{2,6},{6,2},{1... | collective-permute-start | bytes 393224 | tf_op jit(solution)/shard_map/ppermute | solution.py:506
  72.6 4.3 %collective-permute-start.18 = (f32[128,128]{1,0:T(8,128)S(1)}, f32[128,128]{1,0:T(8,128)S(1)}, u32[]{:S(2)}, u32[]{:S(2)}) collective-permute-start(f32[128,128]{1,0:T(8,128)S(1)} %get-tuple-element.46), channel_id=1, source_target_pairs={{0,8},{4,12},{8,0},{12,4},{1,9},{5,13},{9,1},{13,5},{2,10},{6,14},... | collective-permute-start | bytes 196616 | tf_op jit(solution)/shard_map/ppermute | solution.py:506
  77.0 10.1 %collective-permute-start.22 = (f32[8,96,128]{2,1,0:T(8,128)S(1)}, f32[8,96,128]{2,1,0:T(8,128)S(1)}, u32[]{:S(2)}, u32[]{:S(2)}) collective-permute-start(f32[8,96,128]{2,1,0:T(8,128)S(1)} %get-tuple-element.49.residual), channel_id=1, source_target_pairs={{0,16},{16,0},{1,17},{17,1},{2,18},{18,2},{3,19},{19,3},{4,20},{20... | collective-permute-start | bytes 1179656 | tf_op jit(solution)/shard_map/ppermute | solution.py:506
  78.5 4.4 %collective-permute-start.19 = (f32[128,128]{1,0:T(8,128)S(1)}, f32[128,128]{1,0:T(8,128)S(1)}, u32[]{:S(2)}, u32[]{:S(2)}) collective-permute-start(f32[128,128]{1,0:T(8,128)S(1)} %add.3.refs_0_), channel_id=1, source_target_pairs={{0,1},{1,0},{2,3},{3,2},{4,5},{5,4},{6,7},{7,6},{8,9},{9,8},{10,11... | collective-permute-start | bytes 196616 | tf_op jit(solution)/shard_map/ppermute | solution.py:506
  79.1 7.0 %collective-permute-start.20 = (f32[128,128]{1,0:T(8,128)S(1)}, f32[128,128]{1,0:T(8,128)S(1)}, u32[]{:S(2)}, u32[]{:S(2)}) collective-permute-start(f32[128,128]{1,0:T(8,128)S(1)} %add.3.refs_0_), channel_id=1, source_target_pairs={{0,2},{1,3},{2,0},{3,1},{4,6},{5,7},{6,4},{7,5},{8,10},{9,11},{10,... | collective-permute-start | bytes 196616 | tf_op jit(solution)/shard_map/ppermute | solution.py:506
  79.4 6.8 %collective-permute-start.21 = (f32[128,128]{1,0:T(8,128)S(1)}, f32[128,128]{1,0:T(8,128)S(1)}, u32[]{:S(2)}, u32[]{:S(2)}) collective-permute-start(f32[128,128]{1,0:T(8,128)S(1)} %add.3.refs_0_), channel_id=1, source_target_pairs={{0,3},{1,2},{2,1},{3,0},{4,7},{5,6},{6,5},{7,4},{8,11},{9,10},{10,... | collective-permute-start | bytes 196616 | tf_op jit(solution)/shard_map/ppermute | solution.py:506
  87.1 5.2 %collective-permute-start.23 = (f32[128,128]{1,0:T(8,128)S(1)}, f32[128,128]{1,0:T(8,128)S(1)}, u32[]{:S(2)}, u32[]{:S(2)}) collective-permute-start(f32[128,128]{1,0:T(8,128)S(1)} %scale.3.refs_0_), channel_id=1, source_target_pairs={{0,24},{4,28},{8,16},{12,20},{16,8},{20,12},{24,0},{28,4},{1,25},{... | collective-permute-start | bytes 196616 | tf_op jit(solution)/shard_map/ppermute | solution.py:540
  89.6 4.3 %collective-permute-start.24 = (f32[128,128]{1,0:T(8,128)S(1)}, f32[128,128]{1,0:T(8,128)S(1)}, u32[]{:S(2)}, u32[]{:S(2)}) collective-permute-start(f32[128,128]{1,0:T(8,128)S(1)} %scale.3.refs_0_), channel_id=1, source_target_pairs={{0,8},{4,12},{8,0},{12,4},{1,9},{5,13},{9,1},{13,5},{2,10},{6,14},... | collective-permute-start | bytes 196616 | tf_op jit(solution)/shard_map/ppermute | solution.py:506
  90.2 4.3 %collective-permute-start.27 = (f32[128,128]{1,0:T(8,128)S(1)}, f32[128,128]{1,0:T(8,128)S(1)}, u32[]{:S(2)}, u32[]{:S(2)}) collective-permute-start(f32[128,128]{1,0:T(8,128)S(1)} %scale.3.refs_0_), channel_id=1, source_target_pairs={{0,16},{16,0},{1,17},{17,1},{2,18},{18,2},{3,19},{19,3},{4,20},{20... | collective-permute-start | bytes 196616 | tf_op jit(solution)/shard_map/ppermute | solution.py:506
  90.7 3.8 %collective-permute-start.25 = (f32[128,128]{1,0:T(8,128)S(1)}, f32[128,128]{1,0:T(8,128)S(1)}, u32[]{:S(2)}, u32[]{:S(2)}) collective-permute-start(f32[128,128]{1,0:T(8,128)S(1)} %scale.3.refs_0_), channel_id=1, source_target_pairs={{0,4},{4,0},{8,12},{12,8},{1,5},{5,1},{9,13},{13,9},{2,6},{6,2},{1... | collective-permute-start | bytes 196616 | tf_op jit(solution)/shard_map/ppermute | solution.py:506
  92.4 2.1 %collective-permute-start.29 = (f32[128,128]{1,0:T(8,128)S(1)}, f32[128,128]{1,0:T(8,128)S(1)}, u32[]{:S(2)}, u32[]{:S(2)}) collective-permute-start(f32[128,128]{1,0:T(8,128)S(1)} %collective-permute-done.23.refs_5_), channel_id=1, source_target_pairs={{0,4},{4,0},{8,12},{12,8},{1,5},{5,1},{9,13},{13,9},{2,6},{6,2},{1... | collective-permute-start | bytes 196616 | tf_op jit(solution)/shard_map/ppermute | solution.py:506
  93.9 1.3 %collective-permute-start.26 = (f32[128,128]{1,0:T(8,128)S(1)}, f32[128,128]{1,0:T(8,128)S(1)}, u32[]{:S(2)}, u32[]{:S(2)}) collective-permute-start(f32[128,128]{1,0:T(8,128)S(1)} %collective-permute-done.24.refs_1_), channel_id=1, source_target_pairs={{0,4},{4,0},{8,12},{12,8},{1,5},{5,1},{9,13},{13,9},{2,6},{6,2},{1... | collective-permute-start | bytes 196616 | tf_op jit(solution)/shard_map/ppermute | solution.py:506
  94.4 1.3 %collective-permute-start.28 = (f32[128,128]{1,0:T(8,128)S(1)}, f32[128,128]{1,0:T(8,128)S(1)}, u32[]{:S(2)}, u32[]{:S(2)}) collective-permute-start(f32[128,128]{1,0:T(8,128)S(1)} %collective-permute-done.27.refs_4_), channel_id=1, source_target_pairs={{0,4},{4,0},{8,12},{12,8},{1,5},{5,1},{9,13},{13,9},{2,6},{6,2},{1... | collective-permute-start | bytes 196616 | tf_op jit(solution)/shard_map/ppermute | solution.py:506

commit v6 on v5

--- a/solution.py
+++ b/solution.py
@@ -161,7 +161,7 @@
         ),
         scratch_shapes=[pltpu.VMEM((sites, 2 * rows, 2 * lanes), BF16)],
         compiler_params=params(),
-        cost_estimate=cost(1e11, 16e6),
+        cost_estimate=cost(8e9, 16e6),
         name="first_local",
     )(x, in_hbm(source), in_hbm(couplings))
 
@@ -186,7 +186,7 @@
         out_specs=pl.BlockSpec((1, rows, lanes), lambda s: (s, 0, 0)),
         scratch_shapes=[pltpu.VMEM((sites, 2 * rows, 2 * lanes), BF16)],
         compiler_params=params(),
-        cost_estimate=cost(1e11, 8e6),
+        cost_estimate=cost(8e9, 8e6),
         name="local_part",
     )(x, source, local)
 
@@ -436,64 +436,62 @@
     )(x, residual, vectors, *pieces)
 
 
-def join_kernel(x, other_x, residual, other_residual, base, full):
+def join_kernel(own, other, out):
     group = lax.axis_index("groups")
-    for site in range(x.shape[0]):
-        own = x[site] + 0.5 * residual[site]
-        other = other_x[site] + 0.5 * other_residual[site]
-        base[site] = join_halves(own, other, group)
-        full[site] = join_halves(residual[site], other_residual[site], group)
-
-
-def join(x, other_x, residual, other_residual):
-    sites, rows, lanes = x.shape
-    shape = (sites, rows, 2 * lanes)
+    for site in range(own.shape[0]):
+        out[site] = join_halves(own[site], other[site], group)
+
+
+def join(own, other):
+    sites, rows, lanes = own.shape
     return pl.pallas_call(
         join_kernel,
-        out_shape=(pltpu.VMEM(shape, F32), jax.ShapeDtypeStruct(shape, F32)),
-        in_specs=vmem(4),
-        out_specs=tuple(vmem(2)),
-        compiler_params=params(),
-        cost_estimate=cost(1e6, 4e6),
+        out_shape=pltpu.VMEM((sites, rows, 2 * lanes), F32),
+        in_specs=vmem(2),
+        out_specs=vmem(1)[0],
+        compiler_params=params(),
+        cost_estimate=cost(1e6, 2e6),
         name="join",
-    )(x, other_x, residual, other_residual)
-
-
-def final_kernel(count, base, vectors, *refs):
-    own, other, (out, stacks) = refs[:count], refs[count:-2], refs[-2:]
-    step, _, lanes = out.shape
-    first = pl.program_id(0) * step
-
-    @pl.when(first == 0)
-    def _():
-        group = lax.axis_index("groups")
-        place_pieces([join_halves(a[...], b[...], group) for a, b in zip(own, other)], stacks)
-
-    number, rows = vectors.shape[3], out.shape[1]
-    for index in range(step):
-        total = base[first + index]
-        for half in range(2):
-            left = vectors[first + index, half]
-            right = stacks[half * number : (half + 1) * number]
-            total = total + (matmul(left[:rows], right[:, :lanes]) + (matmul(left[:rows], right[:, lanes:]) + matmul(left[rows:], right[:, :lanes])))
-        out[index] = total
-
-
-def final(base, own, other, vectors):
-    sites, rows, lanes = base.shape
+    )(own, other)
+
+
+def final_kernel(count, base, residual, other_residual, vectors, *refs):
+    own, other = refs[:count], refs[count : 2 * count]
+    out, full, stacks, held, held_full, sems = refs[2 * count :]
+    group = lax.axis_index("groups")
+    copies = []
+    for site in range(base.shape[0]):
+        held_full[site] = join_halves(residual[site], other_residual[site], group)
+        copies.append(pltpu.make_async_copy(held_full.at[site], full.at[site], sems.at[0, site]))
+        copies[-1].start()
+    place_pieces([join_halves(a[...], b[...], group) for a, b in zip(own, other)], stacks)
+    for site in range(base.shape[0]):
+        held[site] = base[site] + 0.5 * held_full[site] + expand(site, vectors, stacks)
+        copies.append(pltpu.make_async_copy(held.at[site], out.at[site], sems.at[1, site]))
+        copies[-1].start()
+    for copy in copies:
+        copy.wait()
+
+
+def final(base, residual, other_residual, own, other, vectors):
+    sites, _, lanes = base.shape
     number = vectors.shape[-1]
-    step = 2
+    shape = jax.ShapeDtypeStruct(base.shape, F32)
     return pl.pallas_call(
         functools.partial(final_kernel, len(own)),
-        grid=(sites // step,),
-        out_shape=jax.ShapeDtypeStruct(base.shape, F32),
-        in_specs=vmem(2 + len(own) + len(other)),
-        out_specs=pl.BlockSpec((step, rows, lanes), lambda s: (s, 0, 0)),
-        scratch_shapes=[pltpu.VMEM((2 * number, 2 * lanes), BF16)],
+        out_shape=(shape, shape),
+        in_specs=vmem(4 + len(own) + len(other)),
+        out_specs=(pl.BlockSpec(memory_space=pl.ANY),) * 2,
+        scratch_shapes=[
+            pltpu.VMEM((2 * number, 2 * lanes), BF16),
+            pltpu.VMEM(base.shape, F32),
+            pltpu.VMEM(base.shape, F32),
+            pltpu.SemaphoreType.DMA((2, sites)),
+        ],
         compiler_params=params(),
         cost_estimate=cost(2e9, 8e6),
         name="final",
-    )(base, vectors, *own, *other)
+    )(base, residual, other_residual, vectors, *own, *other)
 
 
 def shifted(value, axis, step):
@@ -577,24 +575,20 @@
         rest = backward_face(rest, backward_t, halo)
         rest = z_faces(rest, forward_z, backward_z, halo)
         if sweep and last:
-            rest, other_x = lax.optimization_barrier((rest, other_x))
+            base, rest = lax.optimization_barrier((join(x, other_x), rest))
         residual, keep, send = forward_face(rest, forward_t, halo, by_rows)
         part = halving(keep, send)
         if last:
             part, residual = lax.optimization_barrier((part, residual))
             other_residual = crossed(residual, "groups", 1)
         parts = over_time(part)
-        if last:
-            parts, other_residual = lax.optimization_barrier((parts, other_residual))
         d = scale(eigen, parts)
         if not last:
             x = update(x, residual, doubling([d], blocks // 2), by_columns)
-    base, full_residual = join(x, other_x, residual, other_residual)
     mask = blocks // 2
     other = across_groups(d, mask)
     own = [d, crossed(d, "space", mask)]
-    other[1], base = lax.optimization_barrier((other[1], base))
-    whole = final(base, doubling(own, mask // 2), doubling(other, mask // 2), by_columns)
+    whole, full_residual = final(base, residual, other_residual, doubling(own, mask // 2), doubling(other, mask // 2), by_columns)
     shape = source.shape
     return whole.reshape(shape), full_residual.reshape(shape)
 

time: 99.6 us -> 98 us (0.984)
  Pallas kernels: 26.1 us -> 24.3 us
    ppermute x8, waiting for transfers between devices: 14.9 us -> 11 us  [shifted(): lax.ppermute(value, axis, [(i, (i + step) % count) for i in range(count)])]
    ppermute x21, waiting for transfers between devices: 24.3 us -> 27.5 us  [crossed(): return lax.ppermute(value, axis, [(i, i ^ mask) for i in range(count)])]
    pallas_call x2, Pallas kernels: 4.87 us -> 3.16 us  [the longest x1 2.89 us: final(): pl.pallas_call(functools.partial(final_kernel, len(own)), out_shape=(shap...]
    ppermute x1, waiting for transfers between devices: 0.32 us -> 1.41 us  [across_groups(): lax.ppermute(part, ('groups', 'space'), pairs)]
    ppermute x1, starting transfers between devices: 2.5 us -> 1.49 us  [across_groups(): lax.ppermute(part, ('groups', 'space'), pairs)]
  transfers between devices with their start and end apart: 30 -> 30, of which waited for: 18 -> 17; matrix products, arithmetic and copies ran while one was open for 0% -> 0% of each run, Pallas kernels for 18% -> 18%
where the time goes in v6:
time: 98 us; the launch traced here: 97.6 us
  waiting for transfers between devices  39.9 us (41%)
  starting transfers between devices  31.4 us (32%)
  Pallas kernels  24.3 us (25%)
  local copies, waits for them, and re-layouts  1.13 us (1%)
    ppermute x21, waiting for transfers between devices, crossed(): return lax.ppermute(value, axis, [(i, i ^ mask) for i in range(count)])  27.5 us
    ppermute x21, starting transfers between devices, crossed(): return lax.ppermute(value, axis, [(i, i ^ mask) for i in range(count)])  19 us
    ppermute x8, starting transfers between devices, shifted(): lax.ppermute(value, axis, [(i, (i + step) % count) for i in range(count)])  11 us
    ppermute x8, waiting for transfers between devices, shifted(): lax.ppermute(value, axis, [(i, (i + step) % count) for i in range(count)])  11 us
    pallas_call x1, Pallas kernels, first_local(): pl.pallas_call(functools.partial(first_kernel, ny, nx), grid=(sites,), ou...  7.69 us
    pallas_call x1, Pallas kernels, vectors_parts(): pl.pallas_call(vectors_kernel, grid=(sites // step,), out_shape=(pltpu.VM...  3.72 us
    pallas_call x1, Pallas kernels, local_part(): pl.pallas_call(functools.partial(local_kernel, ny, nx), grid=(sites,), ou...  2.97 us
    pallas_call x1, Pallas kernels, final(): pl.pallas_call(functools.partial(final_kernel, len(own)), out_shape=(shap...  2.89 us
  transfers between devices with their start and end apart: 30, of which 17 were waited for; matrix products, arithmetic and copies ran while one was open for 0% of the time, Pallas kernels for 18%

profile of v6, /device:TPU:0, one launch (start us, length us, event | category | flops | bytes accessed | tf_op | source)
XLA Modules:
  0.0 97.6 jit_solution(14931306086232548308)
XLA Ops:
  0.6 1.1 %copy-done = f32[1,1,2,4,96,256]{5,4,3,2,1,0:T(8,128)S(1)} copy-done((f32[1,1,2,4,96,256]{5,4,3,2,1,0:T(8,128)S(1)}, f32[1,1,2,4,96,256]{5,4,3,2,1,0:T(8,128)}, u32[]{:S(2)}) %copy-start) | copy-done | bytes 786456
  2.0 3.1 %collective-permute-start = (f32[8,96,128]{2,1,0:T(8,128)S(1)}, f32[8,96,128]{2,1,0:T(8,128)S(1)}, u32[]{:S(2)}, u32[]{:S(2)}) collective-permute-start(f32[8,96,128]{2,1,0:T(8,128)S(1)} %pack.1.x_ref.x), channel_id=1, source_target_pairs={{0,1},{1,2},{2,3},{3,0},{4,5},{5,6},{6,7},{7,4},{8,9},{9,10},{10,1... | collective-permute-start | bytes 1179656 | tf_op jit(solution)/shard_map/ppermute | solution.py:499
  5.1 0.7 collective-permute-start.1
  5.8 2.4 %collective-permute-start.3 = (f32[8,96,128]{2,1,0:T(8,128)S(1)}, f32[8,96,128]{2,1,0:T(8,128)S(1)}, u32[]{:S(2)}, u32[]{:S(2)}) collective-permute-start(f32[8,96,128]{2,1,0:T(8,128)S(1)} %pack.1.x_ref.x), channel_id=1, source_target_pairs={{0,3},{1,0},{2,1},{3,2},{4,7},{5,4},{6,5},{7,6},{8,11},{9,8},{10,9... | collective-permute-start | bytes 1179656 | tf_op jit(solution)/shard_map/ppermute | solution.py:499
  8.1 7.7 %first_local.1 = (f32[8,96,128]{2,1,0:T(8,128)S(1)}, f32[8,96,128]{2,1,0:T(8,128)S(1)}, bf16[5,8,192,192]{3,2,1,0:T(8,128)(2,1)S(1)}, bf16[4,8,192,192]{3,2,1,0:T(8,128)(2,1)S(1)}) custom-call(f32[8,96,128]{2,1,0:T(8,128)S(1)} %pack.1.x_ref.x, f32[8,96,256]{2,1,0:T(8,128)} %bitcast.11, f32[9,8,96,192]{3,2,1,0:T(8,128)} %bitcast.10), custom_call_target="tpu_custom_call" | custom-call | flops 8000000000 | bytes 16000000 | tf_op jit(solution)/shard_map/first_local/pallas_call | solution.py:142
  15.8 3.7 %vectors_parts.1 = (bf16[1024,1536]{1,0:T(8,128)(2,1)S(1)}, bf16[8,2,192,512]{3,2,1,0:T(8,128)(2,1)S(1)}) custom-call(f32[1536,512]{1,0:T(8,128)} %bitcast.9), custom_call_target="tpu_custom_call" | custom-call | flops 1000000 | bytes 9000000 | tf_op jit(solution)/shard_map/vectors_parts/pallas_call | solution.py:222
  19.6 0.5 backward_face.2.rest
  20.1 0.7 z_faces.2.rest
  20.7 4.0 %collective-permute-done.3.forward = f32[8,96,128]{2,1,0:T(8,128)S(1)} collective-permute-done((f32[8,96,128]{2,1,0:T(8,128)S(1)}, f32[8,96,128]{2,1,0:T(8,128)S(1)}, u32[]{:S(2)}, u32[]{:S(2)}) %collective-permute-start.3) | collective-permute-done | bytes 393248 | tf_op jit(solution)/shard_map/ppermute | solution.py:499
  24.7 1.4 %forward_face.2 = (f32[8,96,128]{2,1,0:T(8,128)S(1)}, f32[256,128]{1,0:T(8,128)S(1)}, f32[256,128]{1,0:T(8,128)S(1)}) custom-call(f32[8,96,128]{2,1,0:T(8,128)S(1)} %z_faces.2.rest, f32[8,96,128]{2,1,0:T(8,128)S(1)} %collective-permute-done.3.forward, bf16[4,8,192,192]{3,2,1,0:T(8,128)(2,1)S(1)} %get-tuple-element.25.matrix, ...), custom_call_target="tpu_custom_call" | custom-call | flops 2000000000 | bytes 8000000 | tf_op jit(solution)/shard_map/forward_face/pallas_call | solution.py:328
  26.3 1.2 %collective-permute-done.4.received = f32[256,128]{1,0:T(8,128)S(1)} collective-permute-done((f32[256,128]{1,0:T(8,128)S(1)}, f32[256,128]{1,0:T(8,128)S(1)}, u32[]{:S(2)}, u32[]{:S(2)}) %collective-permute-start.4) | collective-permute-done | bytes 131104 | tf_op jit(solution)/shard_map/ppermute | solution.py:504
  27.5 1.6 %collective-permute-start.5 = (f32[128,128]{1,0:T(8,128)S(1)}, f32[128,128]{1,0:T(8,128)S(1)}, u32[]{:S(2)}, u32[]{:S(2)}) collective-permute-start(f32[128,128]{1,0:T(8,128)S(1)} %get-tuple-element.32), channel_id=1, source_target_pairs={{0,8},{4,12},{8,0},{12,4},{1,9},{5,13},{9,1},{13,5},{2,10},{6,14},... | collective-permute-start | bytes 196616 | tf_op jit(solution)/shard_map/ppermute | solution.py:504
  29.1 2.8 %collective-permute-done.5.right = f32[128,128]{1,0:T(8,128)S(1)} collective-permute-done((f32[128,128]{1,0:T(8,128)S(1)}, f32[128,128]{1,0:T(8,128)S(1)}, u32[]{:S(2)}, u32[]{:S(2)}) %collective-permute-start.5) | collective-permute-done | bytes 65568 | tf_op jit(solution)/shard_map/ppermute | solution.py:504
  31.9 0.6 collective-permute-start.6
  32.5 2.9 %collective-permute-start.7 = (f32[128,128]{1,0:T(8,128)S(1)}, f32[128,128]{1,0:T(8,128)S(1)}, u32[]{:S(2)}, u32[]{:S(2)}) collective-permute-start(f32[128,128]{1,0:T(8,128)S(1)} %add.2.refs_0_), channel_id=1, source_target_pairs={{0,2},{1,3},{2,0},{3,1},{4,6},{5,7},{6,4},{7,5},{8,10},{9,11},{10,... | collective-permute-start | bytes 196616 | tf_op jit(solution)/shard_map/ppermute | solution.py:504
  35.4 0.9 collective-permute-start.8
  36.5 1.3 %collective-permute-done.7.refs_2_ = f32[128,128]{1,0:T(8,128)S(1)} collective-permute-done((f32[128,128]{1,0:T(8,128)S(1)}, f32[128,128]{1,0:T(8,128)S(1)}, u32[]{:S(2)}, u32[]{:S(2)}) %collective-permute-start.7) | collective-permute-done | bytes 65568 | tf_op jit(solution)/shard_map/ppermute | solution.py:504
  37.8 3.7 %collective-permute-done.8.refs_3_ = f32[128,128]{1,0:T(8,128)S(1)} collective-permute-done((f32[128,128]{1,0:T(8,128)S(1)}, f32[128,128]{1,0:T(8,128)S(1)}, u32[]{:S(2)}, u32[]{:S(2)}) %collective-permute-start.8) | collective-permute-done | bytes 65568 | tf_op jit(solution)/shard_map/ppermute | solution.py:504
  41.6 1.6 %collective-permute-start.9 = (f32[128,128]{1,0:T(8,128)S(1)}, f32[128,128]{1,0:T(8,128)S(1)}, u32[]{:S(2)}, u32[]{:S(2)}) collective-permute-start(f32[128,128]{1,0:T(8,128)S(1)} %scale.2.refs_0_), channel_id=1, source_target_pairs={{0,8},{4,12},{8,0},{12,4},{1,9},{5,13},{9,1},{13,5},{2,10},{6,14},... | collective-permute-start | bytes 196616 | tf_op jit(solution)/shard_map/ppermute | solution.py:504
  43.1 2.8 %collective-permute-done.9.refs_1_ = f32[128,128]{1,0:T(8,128)S(1)} collective-permute-done((f32[128,128]{1,0:T(8,128)S(1)}, f32[128,128]{1,0:T(8,128)S(1)}, u32[]{:S(2)}, u32[]{:S(2)}) %collective-permute-start.9) | collective-permute-done | bytes 65568 | tf_op jit(solution)/shard_map/ppermute | solution.py:504
  45.9 1.2 %collective-permute-done.11.refs_3_ = f32[128,128]{1,0:T(8,128)S(1)} collective-permute-done((f32[128,128]{1,0:T(8,128)S(1)}, f32[128,128]{1,0:T(8,128)S(1)}, u32[]{:S(2)}, u32[]{:S(2)}) %collective-permute-start.11) | collective-permute-done | bytes 65568 | tf_op jit(solution)/shard_map/ppermute | solution.py:504
  47.2 1.1 %update.1.own.x_ref = f32[8,96,128]{2,1,0:T(8,128)S(1)} custom-call(f32[8,96,128]{2,1,0:T(8,128)S(1)} %pack.1.x_ref.x, f32[8,96,128]{2,1,0:T(8,128)S(1)} %get-tuple-element.27.residual, bf16[8,2,192,512]{3,2,1,0:T(8,128)(2,1)S(1)} %get-tuple-element.28.vectors, f32[128,128]{1,0:T(8,128)S(1)} %scale.2.refs_0_, f32[128,128]{1,0:T(8,128)S(1)} %collective-permute-done.9.refs_1_, ...), custom_call_target="tpu_custom_call" | custom-call | flops 1000000000 | bytes 8000000 | tf_op jit(solution)/shard_map/update/pallas_call | solution.py:427
  48.4 1.3 %collective-permute-start.14 = (f32[8,96,128]{2,1,0:T(8,128)S(1)}, f32[8,96,128]{2,1,0:T(8,128)S(1)}, u32[]{:S(2)}, u32[]{:S(2)}) collective-permute-start(f32[8,96,128]{2,1,0:T(8,128)S(1)} %update.1.own.x_ref), channel_id=1, source_target_pairs={{0,12},{4,0},{8,4},{12,8},{1,13},{5,1},{9,5},{13,9},{2,14},{6,2},{... | collective-permute-start | bytes 1179656 | tf_op jit(solution)/shard_map/ppermute | solution.py:499
  49.7 1.5 %collective-permute-start.12 = (f32[8,96,128]{2,1,0:T(8,128)S(1)}, f32[8,96,128]{2,1,0:T(8,128)S(1)}, u32[]{:S(2)}, u32[]{:S(2)}) collective-permute-start(f32[8,96,128]{2,1,0:T(8,128)S(1)} %update.1.own.x_ref), channel_id=1, source_target_pairs={{0,16},{16,0},{1,17},{17,1},{2,18},{18,2},{3,19},{19,3},{4,20},{20... | collective-permute-start | bytes 1179656 | tf_op jit(solution)/shard_map/ppermute | solution.py:504
  51.2 3.5 %collective-permute-start.16 = (f32[8,96,128]{2,1,0:T(8,128)S(1)}, f32[8,96,128]{2,1,0:T(8,128)S(1)}, u32[]{:S(2)}, u32[]{:S(2)}) collective-permute-start(f32[8,96,128]{2,1,0:T(8,128)S(1)} %update.1.own.x_ref), channel_id=1, source_target_pairs={{0,3},{1,0},{2,1},{3,2},{4,7},{5,4},{6,5},{7,6},{8,11},{9,8},{10,9... | collective-permute-start | bytes 1179656 | tf_op jit(solution)/shard_map/ppermute | solution.py:499
  54.7 3.0 %local_part.1.rest = f32[8,96,128]{2,1,0:T(8,128)S(1)} custom-call(f32[8,96,128]{2,1,0:T(8,128)S(1)} %update.1.own.x_ref, f32[8,96,128]{2,1,0:T(8,128)S(1)} %get-tuple-element.33.source, bf16[5,8,192,192]{3,2,1,0:T(8,128)(2,1)S(1)} %get-tuple-element.34.local), custom_call_target="tpu_custom_call" | custom-call | flops 8000000000 | bytes 8000000 | tf_op jit(solution)/shard_map/local_part/pallas_call | solution.py:177
  57.7 3.7 %collective-permute-done.12.other = f32[8,96,128]{2,1,0:T(8,128)S(1)} collective-permute-done((f32[8,96,128]{2,1,0:T(8,128)S(1)}, f32[8,96,128]{2,1,0:T(8,128)S(1)}, u32[]{:S(2)}, u32[]{:S(2)}) %collective-permute-start.12) | collective-permute-done | bytes 393248 | tf_op jit(solution)/shard_map/ppermute | solution.py:504
  61.6 0.5 collective-permute-done.13.backward
  62.2 0.5 backward_face.3.rest
  62.6 0.7 z_faces.3.rest
  63.3 6.5 %collective-permute-done.16.forward = f32[8,96,128]{2,1,0:T(8,128)S(1)} collective-permute-done((f32[8,96,128]{2,1,0:T(8,128)S(1)}, f32[8,96,128]{2,1,0:T(8,128)S(1)}, u32[]{:S(2)}, u32[]{:S(2)}) %collective-permute-start.16) | collective-permute-done | bytes 393248 | tf_op jit(solution)/shard_map/ppermute | solution.py:499
  69.8 1.4 %forward_face.3 = (f32[8,96,128]{2,1,0:T(8,128)S(1)}, f32[256,128]{1,0:T(8,128)S(1)}, f32[256,128]{1,0:T(8,128)S(1)}) custom-call(f32[8,96,128]{2,1,0:T(8,128)S(1)} %z_faces.3.rest, f32[8,96,128]{2,1,0:T(8,128)S(1)} %collective-permute-done.16.forward, bf16[4,8,192,192]{3,2,1,0:T(8,128)(2,1)S(1)} %get-tuple-element.25.matrix, ...), custom_call_target="tpu_custom_call" | custom-call | flops 2000000000 | bytes 8000000 | tf_op jit(solution)/shard_map/forward_face/pallas_call | solution.py:328
  71.3 1.3 %collective-permute-done.17.received = f32[256,128]{1,0:T(8,128)S(1)} collective-permute-done((f32[256,128]{1,0:T(8,128)S(1)}, f32[256,128]{1,0:T(8,128)S(1)}, u32[]{:S(2)}, u32[]{:S(2)}) %collective-permute-start.17) | collective-permute-done | bytes 131104 | tf_op jit(solution)/shard_map/ppermute | solution.py:504
  72.6 1.6 %collective-permute-start.18 = (f32[128,128]{1,0:T(8,128)S(1)}, f32[128,128]{1,0:T(8,128)S(1)}, u32[]{:S(2)}, u32[]{:S(2)}) collective-permute-start(f32[128,128]{1,0:T(8,128)S(1)} %get-tuple-element.40), channel_id=1, source_target_pairs={{0,8},{4,12},{8,0},{12,4},{1,9},{5,13},{9,1},{13,5},{2,10},{6,14},... | collective-permute-start | bytes 196616 | tf_op jit(solution)/shard_map/ppermute | solution.py:504
  74.2 2.8 %collective-permute-done.18.right = f32[128,128]{1,0:T(8,128)S(1)} collective-permute-done((f32[128,128]{1,0:T(8,128)S(1)}, f32[128,128]{1,0:T(8,128)S(1)}, u32[]{:S(2)}, u32[]{:S(2)}) %collective-permute-start.18) | collective-permute-done | bytes 65568 | tf_op jit(solution)/shard_map/ppermute | solution.py:504
  77.0 1.6 %collective-permute-start.19 = (f32[8,96,128]{2,1,0:T(8,128)S(1)}, f32[8,96,128]{2,1,0:T(8,128)S(1)}, u32[]{:S(2)}, u32[]{:S(2)}) collective-permute-start(f32[8,96,128]{2,1,0:T(8,128)S(1)} %get-tuple-element.42.residual), channel_id=1, source_target_pairs={{0,16},{16,0},{1,17},{17,1},{2,18},{18,2},{3,19},{19,3},{4,20},{20... | collective-permute-start | bytes 1179656 | tf_op jit(solution)/shard_map/ppermute | solution.py:504
  78.5 0.6 collective-permute-start.20
  79.1 0.3 collective-permute-start.21
  79.4 3.5 %collective-permute-start.22 = (f32[128,128]{1,0:T(8,128)S(1)}, f32[128,128]{1,0:T(8,128)S(1)}, u32[]{:S(2)}, u32[]{:S(2)}) collective-permute-start(f32[128,128]{1,0:T(8,128)S(1)} %add.3.refs_0_), channel_id=1, source_target_pairs={{0,3},{1,2},{2,1},{3,0},{4,7},{5,6},{6,5},{7,4},{8,11},{9,10},{10,... | collective-permute-start | bytes 196616 | tf_op jit(solution)/shard_map/ppermute | solution.py:504
  82.9 3.2 %collective-permute-done.21.refs_2_ = f32[128,128]{1,0:T(8,128)S(1)} collective-permute-done((f32[128,128]{1,0:T(8,128)S(1)}, f32[128,128]{1,0:T(8,128)S(1)}, u32[]{:S(2)}, u32[]{:S(2)}) %collective-permute-start.21) | collective-permute-done | bytes 65568 | tf_op jit(solution)/shard_map/ppermute | solution.py:504
  86.2 1.5 %collective-permute-start.23 = (f32[128,128]{1,0:T(8,128)S(1)}, f32[128,128]{1,0:T(8,128)S(1)}, u32[]{:S(2)}, u32[]{:S(2)}) collective-permute-start(f32[128,128]{1,0:T(8,128)S(1)} %scale.3.refs_0_), channel_id=1, source_target_pairs={{0,8},{4,12},{8,0},{12,4},{1,9},{5,13},{9,1},{13,5},{2,10},{6,14},... | collective-permute-start | bytes 196616 | tf_op jit(solution)/shard_map/ppermute | solution.py:504
  87.8 0.5 collective-permute-start.26
  88.3 1.5 %collective-permute-start.27 = (f32[128,128]{1,0:T(8,128)S(1)}, f32[128,128]{1,0:T(8,128)S(1)}, u32[]{:S(2)}, u32[]{:S(2)}) collective-permute-start(f32[128,128]{1,0:T(8,128)S(1)} %scale.3.refs_0_), channel_id=1, source_target_pairs={{0,24},{4,28},{8,16},{12,20},{16,8},{20,12},{24,0},{28,4},{1,25},{... | collective-permute-start | bytes 196616 | tf_op jit(solution)/shard_map/ppermute | solution.py:538
  89.8 0.8 collective-permute-done.23.refs_1_
  90.6 1.5 %collective-permute-done.26.refs_4_ = f32[128,128]{1,0:T(8,128)S(1)} collective-permute-done((f32[128,128]{1,0:T(8,128)S(1)}, f32[128,128]{1,0:T(8,128)S(1)}, u32[]{:S(2)}, u32[]{:S(2)}) %collective-permute-start.26) | collective-permute-done | bytes 65568 | tf_op jit(solution)/shard_map/ppermute | solution.py:504
  92.1 1.4 %collective-permute-done.27.refs_5_ = f32[128,128]{1,0:T(8,128)S(1)} collective-permute-done((f32[128,128]{1,0:T(8,128)S(1)}, f32[128,128]{1,0:T(8,128)S(1)}, u32[]{:S(2)}, u32[]{:S(2)}) %collective-permute-start.27) | collective-permute-done | bytes 65568 | tf_op jit(solution)/shard_map/ppermute | solution.py:538
  93.5 1.2 %collective-permute-done.29.refs_7_ = f32[128,128]{1,0:T(8,128)S(1)} collective-permute-done((f32[128,128]{1,0:T(8,128)S(1)}, f32[128,128]{1,0:T(8,128)S(1)}, u32[]{:S(2)}, u32[]{:S(2)}) %collective-permute-start.29) | collective-permute-done | bytes 65568 | tf_op jit(solution)/shard_map/ppermute | solution.py:504
  94.7 2.9 %final.1 = (f32[8,96,256]{2,1,0:T(8,128)}, f32[8,96,256]{2,1,0:T(8,128)}) custom-call(f32[8,96,256]{2,1,0:T(8,128)S(1)} %join.1.base, f32[8,96,128]{2,1,0:T(8,128)S(1)} %get-tuple-element.42.residual, f32[8,96,128]{2,1,0:T(8,128)S(1)} %collective-permute-done.19.other_residual, bf16[8,2,192,512]{3,2,1,0:T(8,128)(2,1)S(1)} %get-tuple-element.28.vectors, ...), custom_call_target="tpu_custom_call" | custom-call | flops 2000000000 | bytes 8000000 | tf_op jit(solution)/shard_map/final/pallas_call | solution.py:480
  (36 shorter events, 1.3 us)
Async XLA Ops:
  0.6 1.1 %copy-start = (f32[1,1,2,4,96,256]{5,4,3,2,1,0:T(8,128)S(1)}, f32[1,1,2,4,96,256]{5,4,3,2,1,0:T(8,128)}, u32[]{:S(2)}) copy-start(f32[1,1,2,4,96,256]{5,4,3,2,1,0:T(8,128)} %param.7) | copy-start | bytes 2359300
  2.0 17.5 %collective-permute-start = (f32[8,96,128]{2,1,0:T(8,128)S(1)}, f32[8,96,128]{2,1,0:T(8,128)S(1)}, u32[]{:S(2)}, u32[]{:S(2)}) collective-permute-start(f32[8,96,128]{2,1,0:T(8,128)S(1)} %pack.1.x_ref.x), channel_id=1, source_target_pairs={{0,1},{1,2},{2,3},{3,0},{4,5},{5,6},{6,7},{7,4},{8,9},{9,10},{10,1... | collective-permute-start | bytes 1179656 | tf_op jit(solution)/shard_map/ppermute | solution.py:499
  5.1 14.9 %collective-permute-start.1 = (f32[8,96,128]{2,1,0:T(8,128)S(1)}, f32[8,96,128]{2,1,0:T(8,128)S(1)}, u32[]{:S(2)}, u32[]{:S(2)}) collective-permute-start(f32[8,96,128]{2,1,0:T(8,128)S(1)} %pack.1.x_ref.x), channel_id=1, source_target_pairs={{0,12},{4,0},{8,4},{12,8},{1,13},{5,1},{9,5},{13,9},{2,14},{6,2},{... | collective-permute-start | bytes 1179656 | tf_op jit(solution)/shard_map/ppermute | solution.py:499
  5.8 14.3 %collective-permute-start.2 = (f32[8,96,128]{2,1,0:T(8,128)S(1)}, f32[8,96,128]{2,1,0:T(8,128)S(1)}, u32[]{:S(2)}, u32[]{:S(2)}) collective-permute-start(f32[8,96,128]{2,1,0:T(8,128)S(1)} %pack.1.x_ref.x), channel_id=1, source_target_pairs={{0,4},{4,8},{8,12},{12,0},{1,5},{5,9},{9,13},{13,1},{2,6},{6,10},{... | collective-permute-start | bytes 1179656 | tf_op jit(solution)/shard_map/ppermute | solution.py:499
  5.8 18.9 %collective-permute-start.3 = (f32[8,96,128]{2,1,0:T(8,128)S(1)}, f32[8,96,128]{2,1,0:T(8,128)S(1)}, u32[]{:S(2)}, u32[]{:S(2)}) collective-permute-start(f32[8,96,128]{2,1,0:T(8,128)S(1)} %pack.1.x_ref.x), channel_id=1, source_target_pairs={{0,3},{1,0},{2,1},{3,2},{4,7},{5,4},{6,5},{7,6},{8,11},{9,8},{10,9... | collective-permute-start | bytes 1179656 | tf_op jit(solution)/shard_map/ppermute | solution.py:499
  24.7 11.7 %copy-start.1 = (f32[2,512]{1,0:T(2,128)S(1)}, f32[2,512]{1,0:T(2,128)}, u32[]{:S(2)}) copy-start(f32[2,512]{1,0:T(2,128)} %inverse.1) | copy-start | bytes 12292
  26.1 1.4 %collective-permute-start.4 = (f32[256,128]{1,0:T(8,128)S(1)}, f32[256,128]{1,0:T(8,128)S(1)}, u32[]{:S(2)}, u32[]{:S(2)}) collective-permute-start(f32[256,128]{1,0:T(8,128)S(1)} %get-tuple-element.30), channel_id=1, source_target_pairs={{0,4},{4,0},{8,12},{12,8},{1,5},{5,1},{9,13},{13,9},{2,6},{6,2},{1... | collective-permute-start | bytes 393224 | tf_op jit(solution)/shard_map/ppermute | solution.py:504
  27.5 4.3 %collective-permute-start.5 = (f32[128,128]{1,0:T(8,128)S(1)}, f32[128,128]{1,0:T(8,128)S(1)}, u32[]{:S(2)}, u32[]{:S(2)}) collective-permute-start(f32[128,128]{1,0:T(8,128)S(1)} %get-tuple-element.32), channel_id=1, source_target_pairs={{0,8},{4,12},{8,0},{12,4},{1,9},{5,13},{9,1},{13,5},{2,10},{6,14},... | collective-permute-start | bytes 196616 | tf_op jit(solution)/shard_map/ppermute | solution.py:504
  31.9 4.6 %collective-permute-start.6 = (f32[128,128]{1,0:T(8,128)S(1)}, f32[128,128]{1,0:T(8,128)S(1)}, u32[]{:S(2)}, u32[]{:S(2)}) collective-permute-start(f32[128,128]{1,0:T(8,128)S(1)} %add.2.refs_0_), channel_id=1, source_target_pairs={{0,1},{1,0},{2,3},{3,2},{4,5},{5,4},{6,7},{7,6},{8,9},{9,8},{10,11... | collective-permute-start | bytes 196616 | tf_op jit(solution)/shard_map/ppermute | solution.py:504
  32.5 5.3 %collective-permute-start.7 = (f32[128,128]{1,0:T(8,128)S(1)}, f32[128,128]{1,0:T(8,128)S(1)}, u32[]{:S(2)}, u32[]{:S(2)}) collective-permute-start(f32[128,128]{1,0:T(8,128)S(1)} %add.2.refs_0_), channel_id=1, source_target_pairs={{0,2},{1,3},{2,0},{3,1},{4,6},{5,7},{6,4},{7,5},{8,10},{9,11},{10,... | collective-permute-start | bytes 196616 | tf_op jit(solution)/shard_map/ppermute | solution.py:504
  35.4 6.1 %collective-permute-start.8 = (f32[128,128]{1,0:T(8,128)S(1)}, f32[128,128]{1,0:T(8,128)S(1)}, u32[]{:S(2)}, u32[]{:S(2)}) collective-permute-start(f32[128,128]{1,0:T(8,128)S(1)} %add.2.refs_0_), channel_id=1, source_target_pairs={{0,3},{1,2},{2,1},{3,0},{4,7},{5,6},{6,5},{7,4},{8,11},{9,10},{10,... | collective-permute-start | bytes 196616 | tf_op jit(solution)/shard_map/ppermute | solution.py:504
  41.6 4.3 %collective-permute-start.9 = (f32[128,128]{1,0:T(8,128)S(1)}, f32[128,128]{1,0:T(8,128)S(1)}, u32[]{:S(2)}, u32[]{:S(2)}) collective-permute-start(f32[128,128]{1,0:T(8,128)S(1)} %scale.2.refs_0_), channel_id=1, source_target_pairs={{0,8},{4,12},{8,0},{12,4},{1,9},{5,13},{9,1},{13,5},{2,10},{6,14},... | collective-permute-start | bytes 196616 | tf_op jit(solution)/shard_map/ppermute | solution.py:504
  43.1 2.8 %collective-permute-start.10 = (f32[128,128]{1,0:T(8,128)S(1)}, f32[128,128]{1,0:T(8,128)S(1)}, u32[]{:S(2)}, u32[]{:S(2)}) collective-permute-start(f32[128,128]{1,0:T(8,128)S(1)} %scale.2.refs_0_), channel_id=1, source_target_pairs={{0,4},{4,0},{8,12},{12,8},{1,5},{5,1},{9,13},{13,9},{2,6},{6,2},{1... | collective-permute-start | bytes 196616 | tf_op jit(solution)/shard_map/ppermute | solution.py:504
  45.9 1.3 %collective-permute-start.11 = (f32[128,128]{1,0:T(8,128)S(1)}, f32[128,128]{1,0:T(8,128)S(1)}, u32[]{:S(2)}, u32[]{:S(2)}) collective-permute-start(f32[128,128]{1,0:T(8,128)S(1)} %collective-permute-done.9.refs_1_), channel_id=1, source_target_pairs={{0,4},{4,0},{8,12},{12,8},{1,5},{5,1},{9,13},{13,9},{2,6},{6,2},{1... | collective-permute-start | bytes 196616 | tf_op jit(solution)/shard_map/ppermute | solution.py:504
  48.3 13.9 %collective-permute-start.13 = (f32[8,96,128]{2,1,0:T(8,128)S(1)}, f32[8,96,128]{2,1,0:T(8,128)S(1)}, u32[]{:S(2)}, u32[]{:S(2)}) collective-permute-start(f32[8,96,128]{2,1,0:T(8,128)S(1)} %update.1.own.x_ref), channel_id=1, source_target_pairs={{0,1},{1,2},{2,3},{3,0},{4,5},{5,6},{6,7},{7,4},{8,9},{9,10},{10,1... | collective-permute-start | bytes 1179656 | tf_op jit(solution)/shard_map/ppermute | solution.py:499
  48.4 14.2 %collective-permute-start.14 = (f32[8,96,128]{2,1,0:T(8,128)S(1)}, f32[8,96,128]{2,1,0:T(8,128)S(1)}, u32[]{:S(2)}, u32[]{:S(2)}) collective-permute-start(f32[8,96,128]{2,1,0:T(8,128)S(1)} %update.1.own.x_ref), channel_id=1, source_target_pairs={{0,12},{4,0},{8,4},{12,8},{1,13},{5,1},{9,5},{13,9},{2,14},{6,2},{... | collective-permute-start | bytes 1179656 | tf_op jit(solution)/shard_map/ppermute | solution.py:499
  49.7 12.9 %collective-permute-start.15 = (f32[8,96,128]{2,1,0:T(8,128)S(1)}, f32[8,96,128]{2,1,0:T(8,128)S(1)}, u32[]{:S(2)}, u32[]{:S(2)}) collective-permute-start(f32[8,96,128]{2,1,0:T(8,128)S(1)} %update.1.own.x_ref), channel_id=1, source_target_pairs={{0,4},{4,8},{8,12},{12,0},{1,5},{5,9},{9,13},{13,1},{2,6},{6,10},{... | collective-permute-start | bytes 1179656 | tf_op jit(solution)/shard_map/ppermute | solution.py:499
  49.7 11.7 %collective-permute-start.12 = (f32[8,96,128]{2,1,0:T(8,128)S(1)}, f32[8,96,128]{2,1,0:T(8,128)S(1)}, u32[]{:S(2)}, u32[]{:S(2)}) collective-permute-start(f32[8,96,128]{2,1,0:T(8,128)S(1)} %update.1.own.x_ref), channel_id=1, source_target_pairs={{0,16},{16,0},{1,17},{17,1},{2,18},{18,2},{3,19},{19,3},{4,20},{20... | collective-permute-start | bytes 1179656 | tf_op jit(solution)/shard_map/ppermute | solution.py:504
  51.2 18.6 %collective-permute-start.16 = (f32[8,96,128]{2,1,0:T(8,128)S(1)}, f32[8,96,128]{2,1,0:T(8,128)S(1)}, u32[]{:S(2)}, u32[]{:S(2)}) collective-permute-start(f32[8,96,128]{2,1,0:T(8,128)S(1)} %update.1.own.x_ref), channel_id=1, source_target_pairs={{0,3},{1,0},{2,1},{3,2},{4,7},{5,4},{6,5},{7,6},{8,11},{9,8},{10,9... | collective-permute-start | bytes 1179656 | tf_op jit(solution)/shard_map/ppermute | solution.py:499
  71.2 1.4 %collective-permute-start.17 = (f32[256,128]{1,0:T(8,128)S(1)}, f32[256,128]{1,0:T(8,128)S(1)}, u32[]{:S(2)}, u32[]{:S(2)}) collective-permute-start(f32[256,128]{1,0:T(8,128)S(1)} %get-tuple-element.38), channel_id=1, source_target_pairs={{0,4},{4,0},{8,12},{12,8},{1,5},{5,1},{9,13},{13,9},{2,6},{6,2},{1... | collective-permute-start | bytes 393224 | tf_op jit(solution)/shard_map/ppermute | solution.py:504
  72.6 4.3 %collective-permute-start.18 = (f32[128,128]{1,0:T(8,128)S(1)}, f32[128,128]{1,0:T(8,128)S(1)}, u32[]{:S(2)}, u32[]{:S(2)}) collective-permute-start(f32[128,128]{1,0:T(8,128)S(1)} %get-tuple-element.40), channel_id=1, source_target_pairs={{0,8},{4,12},{8,0},{12,4},{1,9},{5,13},{9,1},{13,5},{2,10},{6,14},... | collective-permute-start | bytes 196616 | tf_op jit(solution)/shard_map/ppermute | solution.py:504
  77.0 17.8 %collective-permute-start.19 = (f32[8,96,128]{2,1,0:T(8,128)S(1)}, f32[8,96,128]{2,1,0:T(8,128)S(1)}, u32[]{:S(2)}, u32[]{:S(2)}) collective-permute-start(f32[8,96,128]{2,1,0:T(8,128)S(1)} %get-tuple-element.42.residual), channel_id=1, source_target_pairs={{0,16},{16,0},{1,17},{17,1},{2,18},{18,2},{3,19},{19,3},{4,20},{20... | collective-permute-start | bytes 1179656 | tf_op jit(solution)/shard_map/ppermute | solution.py:504
  78.5 4.4 %collective-permute-start.20 = (f32[128,128]{1,0:T(8,128)S(1)}, f32[128,128]{1,0:T(8,128)S(1)}, u32[]{:S(2)}, u32[]{:S(2)}) collective-permute-start(f32[128,128]{1,0:T(8,128)S(1)} %add.3.refs_0_), channel_id=1, source_target_pairs={{0,1},{1,0},{2,3},{3,2},{4,5},{5,4},{6,7},{7,6},{8,9},{9,8},{10,11... | collective-permute-start | bytes 196616 | tf_op jit(solution)/shard_map/ppermute | solution.py:504
  79.1 7.0 %collective-permute-start.21 = (f32[128,128]{1,0:T(8,128)S(1)}, f32[128,128]{1,0:T(8,128)S(1)}, u32[]{:S(2)}, u32[]{:S(2)}) collective-permute-start(f32[128,128]{1,0:T(8,128)S(1)} %add.3.refs_0_), channel_id=1, source_target_pairs={{0,2},{1,3},{2,0},{3,1},{4,6},{5,7},{6,4},{7,5},{8,10},{9,11},{10,... | collective-permute-start | bytes 196616 | tf_op jit(solution)/shard_map/ppermute | solution.py:504
  79.4 6.8 %collective-permute-start.22 = (f32[128,128]{1,0:T(8,128)S(1)}, f32[128,128]{1,0:T(8,128)S(1)}, u32[]{:S(2)}, u32[]{:S(2)}) collective-permute-start(f32[128,128]{1,0:T(8,128)S(1)} %add.3.refs_0_), channel_id=1, source_target_pairs={{0,3},{1,2},{2,1},{3,0},{4,7},{5,6},{6,5},{7,4},{8,11},{9,10},{10,... | collective-permute-start | bytes 196616 | tf_op jit(solution)/shard_map/ppermute | solution.py:504
  86.2 4.3 %collective-permute-start.23 = (f32[128,128]{1,0:T(8,128)S(1)}, f32[128,128]{1,0:T(8,128)S(1)}, u32[]{:S(2)}, u32[]{:S(2)}) collective-permute-start(f32[128,128]{1,0:T(8,128)S(1)} %scale.3.refs_0_), channel_id=1, source_target_pairs={{0,8},{4,12},{8,0},{12,4},{1,9},{5,13},{9,1},{13,5},{2,10},{6,14},... | collective-permute-start | bytes 196616 | tf_op jit(solution)/shard_map/ppermute | solution.py:504
  87.8 4.3 %collective-permute-start.26 = (f32[128,128]{1,0:T(8,128)S(1)}, f32[128,128]{1,0:T(8,128)S(1)}, u32[]{:S(2)}, u32[]{:S(2)}) collective-permute-start(f32[128,128]{1,0:T(8,128)S(1)} %scale.3.refs_0_), channel_id=1, source_target_pairs={{0,16},{16,0},{1,17},{17,1},{2,18},{18,2},{3,19},{19,3},{4,20},{20... | collective-permute-start | bytes 196616 | tf_op jit(solution)/shard_map/ppermute | solution.py:504
  88.3 5.2 %collective-permute-start.27 = (f32[128,128]{1,0:T(8,128)S(1)}, f32[128,128]{1,0:T(8,128)S(1)}, u32[]{:S(2)}, u32[]{:S(2)}) collective-permute-start(f32[128,128]{1,0:T(8,128)S(1)} %scale.3.refs_0_), channel_id=1, source_target_pairs={{0,24},{4,28},{8,16},{12,20},{16,8},{20,12},{24,0},{28,4},{1,25},{... | collective-permute-start | bytes 196616 | tf_op jit(solution)/shard_map/ppermute | solution.py:538
  89.8 3.7 %collective-permute-start.24 = (f32[128,128]{1,0:T(8,128)S(1)}, f32[128,128]{1,0:T(8,128)S(1)}, u32[]{:S(2)}, u32[]{:S(2)}) collective-permute-start(f32[128,128]{1,0:T(8,128)S(1)} %scale.3.refs_0_), channel_id=1, source_target_pairs={{0,4},{4,0},{8,12},{12,8},{1,5},{5,1},{9,13},{13,9},{2,6},{6,2},{1... | collective-permute-start | bytes 196616 | tf_op jit(solution)/shard_map/ppermute | solution.py:504
  90.6 2.9 %collective-permute-start.25 = (f32[128,128]{1,0:T(8,128)S(1)}, f32[128,128]{1,0:T(8,128)S(1)}, u32[]{:S(2)}, u32[]{:S(2)}) collective-permute-start(f32[128,128]{1,0:T(8,128)S(1)} %collective-permute-done.23.refs_1_), channel_id=1, source_target_pairs={{0,4},{4,0},{8,12},{12,8},{1,5},{5,1},{9,13},{13,9},{2,6},{6,2},{1... | collective-permute-start | bytes 196616 | tf_op jit(solution)/shard_map/ppermute | solution.py:504
  92.1 1.4 %collective-permute-start.28 = (f32[128,128]{1,0:T(8,128)S(1)}, f32[128,128]{1,0:T(8,128)S(1)}, u32[]{:S(2)}, u32[]{:S(2)}) collective-permute-start(f32[128,128]{1,0:T(8,128)S(1)} %collective-permute-done.26.refs_4_), channel_id=1, source_target_pairs={{0,4},{4,0},{8,12},{12,8},{1,5},{5,1},{9,13},{13,9},{2,6},{6,2},{1... | collective-permute-start | bytes 196616 | tf_op jit(solution)/shard_map/ppermute | solution.py:504
  93.5 1.3 %collective-permute-start.29 = (f32[128,128]{1,0:T(8,128)S(1)}, f32[128,128]{1,0:T(8,128)S(1)}, u32[]{:S(2)}, u32[]{:S(2)}) collective-permute-start(f32[128,128]{1,0:T(8,128)S(1)} %collective-permute-done.27.refs_5_), channel_id=1, source_target_pairs={{0,4},{4,0},{8,12},{12,8},{1,5},{5,1},{9,13},{13,9},{2,6},{6,2},{1... | collective-permute-start | bytes 196616 | tf_op jit(solution)/shard_map/ppermute | solution.py:504

commit v7 on v6

--- a/solution.py
+++ b/solution.py
@@ -82,10 +82,14 @@
     return pltpu.with_memory_space_constraint(value, pltpu.HBM)
 
 
-def pack_kernel(full, half):
+def pack_kernel(full, half, held, sems):
     group = lax.axis_index("groups")
-    for site in range(full.shape[0]):
-        half[site] = pick_half(full[site], group)
+    copies = [pltpu.make_async_copy(full.at[site], held.at[site], sems.at[site]) for site in range(half.shape[0])]
+    for copy in copies:
+        copy.start()
+    for site, copy in enumerate(copies):
+        copy.wait()
+        half[site] = pick_half(held[site], group)
 
 
 def pack(full):
@@ -93,12 +97,13 @@
     return pl.pallas_call(
         pack_kernel,
         out_shape=pltpu.VMEM((sites, rows, lanes // 2), F32),
-        in_specs=vmem(1),
-        out_specs=vmem(1)[0],
+        in_specs=[pl.BlockSpec(memory_space=pl.ANY)],
+        out_specs=vmem(1)[0],
+        scratch_shapes=[pltpu.VMEM(full.shape, F32), pltpu.SemaphoreType.DMA((sites,))],
         compiler_params=params(),
         cost_estimate=cost(1e6, 1e6),
         name="pack",
-    )(full)
+    )(in_hbm(full))
 
 
 def around(site, ny, nx):
@@ -196,23 +201,36 @@
     return [int(format(index, "b").zfill(bits)[::-1], 2) if bits else 0 for index in range(count)]
 
 
-def block_starts(size):
+def ordered_rows(rows, chunk, taken):
+    blocks = lax.axis_size("space")
     space = lax.axis_index("space")
-    return [pl.multiple_of((space ^ block) * size, size) for block in block_order(lax.axis_size("space"))]
-
-
-def vectors_kernel(across, by_rows, by_columns):
+    size = rows.shape[0] // blocks
+    unit = min(size, taken)
+    parts = []
+    for start in range(chunk * taken, (chunk + 1) * taken, unit):
+        block = space ^ block_order(blocks)[start // size]
+        parts.append(rows[pl.ds(pl.multiple_of(block * size + start % size, unit), unit)])
+    return parts[0] if len(parts) == 1 else jnp.concatenate(parts, axis=0)
+
+
+def vectors_kernel(across, by_rows, by_columns, turned_rows):
     sites, _, double, number = by_columns.shape
     rows = double // 2
-    high, low = high_low(across[...].T)
-    by_rows[:number] = high
-    by_rows[number:] = low
-    for site in range(sites):
-        for half in range(2):
-            start = (2 * site + half) * rows
-            high, low = high_low(across[start : start + rows])
-            by_columns[site, half, :rows] = high
-            by_columns[site, half, rows:] = low
+    taken = 128
+    turned_rows[...] = across[...].T
+    for chunk in range(number // taken):
+        part = ordered_rows(turned_rows, chunk, taken)
+        high, low = high_low(part)
+        at = slice(chunk * taken, (chunk + 1) * taken)
+        by_rows[at] = high
+        by_rows[number + chunk * taken : number + (chunk + 1) * taken] = low
+        back = part.T
+        for site in range(sites):
+            for half in range(2):
+                start = (2 * site + half) * rows
+                high, low = high_low(back[start : start + rows])
+                by_columns[site, half, :rows, at] = high
+                by_columns[site, half, rows:, at] = low
 
 
 def vectors_parts(across, sites):
@@ -228,6 +246,7 @@
             pl.BlockSpec((2 * number, step * 2 * rows), lambda s: (0, s)),
             pl.BlockSpec((step, 2, 2 * rows, number), lambda s: (s, 0, 0, 0)),
         ),
+        scratch_shapes=[pltpu.VMEM((number, step * 2 * rows), F32)],
         compiler_params=params(16),
         cost_estimate=cost(1e6, 9e6),
         name="vectors_parts",
@@ -306,20 +325,17 @@
     )(rest, backward, matrix)
 
 
-def forward_kernel(rest, forward, matrix, vectors, residual, keep, send, stacks, whole):
+def forward_kernel(rest, forward, matrix, vectors, residual, keep, send, stacks):
     sign = edge_sign(True)
     rows = 2 * rest.shape[1]
     for site in range(rest.shape[0]):
         own = rest[site] - apply_faces(site, (lambda s: sign * forward[s],), (matrix.at[2],))
         residual[site] = own
         stacks[site * rows : (site + 1) * rows] = stack(own, -1.0)
-    whole[...] = fold(matmul(vectors[...], stacks[...]))
-    starts = block_starts(whole.shape[0] // lax.axis_size("space"))
-    half = len(starts) // 2
-    size = whole.shape[0] // len(starts)
-    for index, start in enumerate(starts):
-        part, at = (keep, index) if index < half else (send, index - half)
-        part[at * size : (at + 1) * size] = whole[pl.ds(start, size)]
+    whole = fold(matmul(vectors[...], stacks[...]))
+    half = whole.shape[0] // 2
+    keep[...] = whole[:half]
+    send[...] = whole[half:]
 
 
 def forward_face(rest, forward, matrix, vectors):
@@ -330,10 +346,7 @@
         out_shape=(pltpu.VMEM(rest.shape, F32), part, part),
         in_specs=vmem(4),
         out_specs=tuple(vmem(3)),
-        scratch_shapes=[
-            pltpu.VMEM((sites * 2 * rows, 2 * lanes), BF16),
-            pltpu.VMEM((vectors.shape[0] // 2, lanes), F32),
-        ],
+        scratch_shapes=[pltpu.VMEM((sites * 2 * rows, 2 * lanes), BF16)],
         compiler_params=params(),
         cost_estimate=cost(2e9, 8e6),
         name="forward_face",
@@ -393,105 +406,117 @@
     )(eigen, *parts)
 
 
-def expand(site, vectors, stacks):
-    number = vectors.shape[3]
+def expand(site, vectors, part, stacks):
+    depth = stacks.shape[0] // 2
     total = None
     for half in range(2):
-        term = matmul(vectors[site, half], stacks[half * number : (half + 1) * number])
+        left = vectors[site, half, :, part * depth : (part + 1) * depth]
+        term = matmul(left, stacks[half * depth : (half + 1) * depth])
         total = term if total is None else total + term
     return fold(total)
 
 
-def place_pieces(values, stacks):
-    number = stacks.shape[0] // 2
-    size = number // lax.axis_size("space")
-    starts = iter(block_starts(size))
-    for value in values:
-        both = stack(value, 1.0)
-        rows = value.shape[0]
-        for at in range(0, rows, size):
-            start = next(starts)
-            stacks[pl.ds(start, size)] = both[at : at + size]
-            stacks[pl.ds(start + number, size)] = both[rows + at : rows + at + size]
-
-
-def update_kernel(x, residual, vectors, *refs):
+def place_pieces(pieces, stacks):
+    values = [piece[...] for piece in pieces]
+    stacks[...] = stack(values[0] if len(values) == 1 else jnp.concatenate(values, axis=0), 1.0)
+
+
+def first_half_kernel(x, residual, vectors, *refs):
     pieces, (out, stacks) = refs[:-2], refs[-2:]
-    place_pieces([piece[...] for piece in pieces], stacks)
+    place_pieces(pieces, stacks)
     for site in range(x.shape[0]):
-        out[site] = x[site] + 0.5 * residual[site] + expand(site, vectors, stacks)
-
-
-def update(x, residual, pieces, vectors):
-    number = vectors.shape[-1]
-    return pl.pallas_call(
-        update_kernel,
+        out[site] = x[site] + 0.5 * residual[site] + expand(site, vectors, 0, stacks)
+
+
+def first_half(x, residual, pieces, vectors):
+    return pl.pallas_call(
+        first_half_kernel,
         out_shape=pltpu.VMEM(x.shape, F32),
         in_specs=vmem(3 + len(pieces)),
         out_specs=vmem(1)[0],
-        scratch_shapes=[pltpu.VMEM((2 * number, 2 * x.shape[-1]), BF16)],
-        compiler_params=params(),
-        cost_estimate=cost(1e9, 8e6),
-        name="update",
+        scratch_shapes=[pltpu.VMEM((vectors.shape[-1], 2 * x.shape[-1]), BF16)],
+        compiler_params=params(),
+        cost_estimate=cost(1e9, 4e6),
+        name="first_half",
     )(x, residual, vectors, *pieces)
 
 
-def join_kernel(own, other, out):
+def second_half_kernel(base, vectors, *refs):
+    pieces, (out, stacks) = refs[:-2], refs[-2:]
+    place_pieces(pieces, stacks)
+    for site in range(base.shape[0]):
+        out[site] = base[site] + expand(site, vectors, 1, stacks)
+
+
+def second_half(base, pieces, vectors):
+    return pl.pallas_call(
+        second_half_kernel,
+        out_shape=pltpu.VMEM(base.shape, F32),
+        in_specs=vmem(2 + len(pieces)),
+        out_specs=vmem(1)[0],
+        scratch_shapes=[pltpu.VMEM((vectors.shape[-1], 2 * base.shape[-1]), BF16)],
+        compiler_params=params(),
+        cost_estimate=cost(1e9, 4e6),
+        name="second_half",
+    )(base, vectors, *pieces)
+
+
+def join_kernel(own, other, full, held, sems):
     group = lax.axis_index("groups")
+    copies = []
     for site in range(own.shape[0]):
-        out[site] = join_halves(own[site], other[site], group)
+        held[site] = join_halves(own[site], other[site], group)
+        copies.append(pltpu.make_async_copy(held.at[site], full.at[site], sems.at[site]))
+        copies[-1].start()
+    for copy in copies:
+        copy.wait()
 
 
 def join(own, other):
     sites, rows, lanes = own.shape
+    shape = (sites, rows, 2 * lanes)
     return pl.pallas_call(
         join_kernel,
-        out_shape=pltpu.VMEM((sites, rows, 2 * lanes), F32),
+        out_shape=jax.ShapeDtypeStruct(shape, F32),
         in_specs=vmem(2),
-        out_specs=vmem(1)[0],
+        out_specs=pl.BlockSpec(memory_space=pl.ANY),
+        scratch_shapes=[pltpu.VMEM(shape, F32), pltpu.SemaphoreType.DMA((sites,))],
         compiler_params=params(),
         cost_estimate=cost(1e6, 2e6),
         name="join",
     )(own, other)
 
 
-def final_kernel(count, base, residual, other_residual, vectors, *refs):
-    own, other = refs[:count], refs[count : 2 * count]
-    out, full, stacks, held, held_full, sems = refs[2 * count :]
+def final_kernel(own, other, vectors, *refs):
+    pieces, (full, stacks, held, sems) = refs[:-4], refs[-4:]
     group = lax.axis_index("groups")
+    place_pieces(pieces, stacks)
     copies = []
-    for site in range(base.shape[0]):
-        held_full[site] = join_halves(residual[site], other_residual[site], group)
-        copies.append(pltpu.make_async_copy(held_full.at[site], full.at[site], sems.at[0, site]))
-        copies[-1].start()
-    place_pieces([join_halves(a[...], b[...], group) for a, b in zip(own, other)], stacks)
-    for site in range(base.shape[0]):
-        held[site] = base[site] + 0.5 * held_full[site] + expand(site, vectors, stacks)
-        copies.append(pltpu.make_async_copy(held.at[site], out.at[site], sems.at[1, site]))
+    for site in range(own.shape[0]):
+        held[site] = join_halves(own[site], other[site] + expand(site, vectors, 1, stacks), group)
+        copies.append(pltpu.make_async_copy(held.at[site], full.at[site], sems.at[site]))
         copies[-1].start()
     for copy in copies:
         copy.wait()
 
 
-def final(base, residual, other_residual, own, other, vectors):
-    sites, _, lanes = base.shape
-    number = vectors.shape[-1]
-    shape = jax.ShapeDtypeStruct(base.shape, F32)
-    return pl.pallas_call(
-        functools.partial(final_kernel, len(own)),
-        out_shape=(shape, shape),
-        in_specs=vmem(4 + len(own) + len(other)),
-        out_specs=(pl.BlockSpec(memory_space=pl.ANY),) * 2,
+def final(own, other, pieces, vectors):
+    sites, rows, lanes = own.shape
+    shape = (sites, rows, 2 * lanes)
+    return pl.pallas_call(
+        final_kernel,
+        out_shape=jax.ShapeDtypeStruct(shape, F32),
+        in_specs=vmem(3 + len(pieces)),
+        out_specs=pl.BlockSpec(memory_space=pl.ANY),
         scratch_shapes=[
-            pltpu.VMEM((2 * number, 2 * lanes), BF16),
-            pltpu.VMEM(base.shape, F32),
-            pltpu.VMEM(base.shape, F32),
-            pltpu.SemaphoreType.DMA((2, sites)),
+            pltpu.VMEM((vectors.shape[-1], 2 * lanes), BF16),
+            pltpu.VMEM(shape, F32),
+            pltpu.SemaphoreType.DMA((sites,)),
         ],
         compiler_params=params(),
-        cost_estimate=cost(2e9, 8e6),
+        cost_estimate=cost(1e9, 4e6),
         name="final",
-    )(base, residual, other_residual, vectors, *own, *other)
+    )(own, other, vectors, *pieces)
 
 
 def shifted(value, axis, step):
@@ -524,12 +549,16 @@
 
 
 def doubling(pieces, mask):
-    while mask:
+    while mask > 1:
         if len(pieces) > 2:
             pieces = [jnp.concatenate(pieces, axis=0)]
         pieces = pieces + [crossed(piece, "space", mask) for piece in pieces]
         mask //= 2
     return pieces
+
+
+def paired(pieces):
+    return [crossed(piece, "space", 1) for piece in pieces]
 
 
 def across_groups(part, mask):
@@ -575,7 +604,7 @@
         rest = backward_face(rest, backward_t, halo)
         rest = z_faces(rest, forward_z, backward_z, halo)
         if sweep and last:
-            base, rest = lax.optimization_barrier((join(x, other_x), rest))
+            rest, other_x = lax.optimization_barrier((rest, other_x))
         residual, keep, send = forward_face(rest, forward_t, halo, by_rows)
         part = halving(keep, send)
         if last:
@@ -584,11 +613,22 @@
         parts = over_time(part)
         d = scale(eigen, parts)
         if not last:
-            x = update(x, residual, doubling([d], blocks // 2), by_columns)
+            pieces = doubling([d], blocks // 2)
+            base = first_half(x, residual, pieces, by_columns)
+            x = second_half(base, paired(pieces), by_columns)
     mask = blocks // 2
     other = across_groups(d, mask)
     own = [d, crossed(d, "space", mask)]
-    whole, full_residual = final(base, residual, other_residual, doubling(own, mask // 2), doubling(other, mask // 2), by_columns)
+    other, own = doubling(other, mask // 2), doubling(own, mask // 2)
+    full_residual = join(residual, other_residual)
+    own[-1], full_residual = lax.optimization_barrier((own[-1], full_residual))
+    own_x = first_half(x, residual, own, by_columns)
+    other[0], own_x = lax.optimization_barrier((other[0], own_x))
+    own_x = second_half(own_x, paired(own), by_columns)
+    other[-1], own_x = lax.optimization_barrier((other[-1], own_x))
+    other_second = paired(other)
+    other_x = first_half(other_x, other_residual, other, by_columns)
+    whole = final(own_x, other_x, other_second, by_columns)
     shape = source.shape
     return whole.reshape(shape), full_residual.reshape(shape)
 

time: 98 us -> 96.8 us (0.988)
  waiting for transfers between devices: 39.9 us -> 35.7 us
  Pallas kernels: 24.3 us -> 27.8 us
  local copies, waits for them, and re-layouts: 1.13 us -> 0.01 us
    ppermute x21, waiting for transfers between devices: 27.5 us -> 20.5 us  [crossed(): return lax.ppermute(value, axis, [(i, i ^ mask) for i in range(count)])]
    ppermute x8, waiting for transfers between devices: 11 us -> 14.4 us  [shifted(): lax.ppermute(value, axis, [(i, (i + step) % count) for i in range(count)])]
    pallas_call x3 -> x7, Pallas kernels: 4.29 us -> 5.85 us  [the longest x3 1.99 us: first_half(): pl.pallas_call(first_half_kernel, out_shape=pltpu.VMEM(x.shape, F32), in_...]
    pallas_call x1, Pallas kernels: 0.27 us -> 1.72 us  [pack(): pl.pallas_call(pack_kernel, out_shape=pltpu.VMEM((sites, rows, lanes // 2...]
    unnamed x4 -> x2, local copies, waits for them, and re-layouts: 1.13 us -> 0.01 us
  transfers between devices with their start and end apart: 30 -> 30, of which waited for: 17 -> 15; matrix products, arithmetic and copies ran while one was open for 0% -> 0% of each run, Pallas kernels for 18% -> 22%
where the time goes in v7:
time: 96.8 us; the launch traced here: 96.4 us
  waiting for transfers between devices  35.7 us (37%)
  starting transfers between devices  31.8 us (33%)
  Pallas kernels  27.8 us (29%)
  between operations  1.04 us (1%)
    ppermute x21, waiting for transfers between devices, crossed(): return lax.ppermute(value, axis, [(i, i ^ mask) for i in range(count)])  20.5 us
    ppermute x21, starting transfers between devices, crossed(): return lax.ppermute(value, axis, [(i, i ^ mask) for i in range(count)])  19.4 us
    ppermute x8, waiting for transfers between devices, shifted(): lax.ppermute(value, axis, [(i, (i + step) % count) for i in range(count)])  14.4 us
    ppermute x8, starting transfers between devices, shifted(): lax.ppermute(value, axis, [(i, (i + step) % count) for i in range(count)])  11 us
    pallas_call x1, Pallas kernels, first_local(): pl.pallas_call(functools.partial(first_kernel, ny, nx), grid=(sites,), ou...  7.69 us
    pallas_call x1, Pallas kernels, vectors_parts(): pl.pallas_call(vectors_kernel, grid=(sites // step,), out_shape=(pltpu.VM...  4.24 us
    pallas_call x1, Pallas kernels, local_part(): pl.pallas_call(functools.partial(local_kernel, ny, nx), grid=(sites,), ou...  2.97 us
    pallas_call x2, Pallas kernels, forward_face(): pl.pallas_call(forward_kernel, out_shape=(pltpu.VMEM(rest.shape, F32), pa...  2.79 us
  transfers between devices with their start and end apart: 30, of which 15 were waited for; matrix products, arithmetic and copies ran while one was open for 0% of the time, Pallas kernels for 22%

profile of v7, /device:TPU:0, one launch (start us, length us, event | category | flops | bytes accessed | tf_op | source)
XLA Modules:
  0.0 96.4 jit_solution(11489558743483345516)
XLA Ops:
  0.6 1.7 %pack.1.x_ref.x = f32[8,96,128]{2,1,0:T(8,128)S(1)} custom-call(f32[8,96,256]{2,1,0:T(8,128)} %bitcast.10), custom_call_target="tpu_custom_call" | custom-call | flops 1000000 | bytes 1000000 | tf_op jit(solution)/shard_map/pack/pallas_call | solution.py:97
  2.4 3.1 %collective-permute-start = (f32[8,96,128]{2,1,0:T(8,128)S(1)}, f32[8,96,128]{2,1,0:T(8,128)S(1)}, u32[]{:S(2)}, u32[]{:S(2)}) collective-permute-start(f32[8,96,128]{2,1,0:T(8,128)S(1)} %pack.1.x_ref.x), channel_id=1, source_target_pairs={{0,1},{1,2},{2,3},{3,0},{4,5},{5,6},{6,7},{7,4},{8,9},{9,10},{10,1... | collective-permute-start | bytes 1179656 | tf_op jit(solution)/shard_map/ppermute | solution.py:524
  5.4 0.7 collective-permute-start.1
  6.1 2.4 %collective-permute-start.3 = (f32[8,96,128]{2,1,0:T(8,128)S(1)}, f32[8,96,128]{2,1,0:T(8,128)S(1)}, u32[]{:S(2)}, u32[]{:S(2)}) collective-permute-start(f32[8,96,128]{2,1,0:T(8,128)S(1)} %pack.1.x_ref.x), channel_id=1, source_target_pairs={{0,3},{1,0},{2,1},{3,2},{4,7},{5,4},{6,5},{7,6},{8,11},{9,8},{10,9... | collective-permute-start | bytes 1179656 | tf_op jit(solution)/shard_map/ppermute | solution.py:524
  8.5 7.7 %first_local.1 = (f32[8,96,128]{2,1,0:T(8,128)S(1)}, f32[8,96,128]{2,1,0:T(8,128)S(1)}, bf16[5,8,192,192]{3,2,1,0:T(8,128)(2,1)S(1)}, bf16[4,8,192,192]{3,2,1,0:T(8,128)(2,1)S(1)}) custom-call(f32[8,96,128]{2,1,0:T(8,128)S(1)} %pack.1.x_ref.x, f32[8,96,256]{2,1,0:T(8,128)} %bitcast.13, f32[9,8,96,192]{3,2,1,0:T(8,128)} %bitcast.12), custom_call_target="tpu_custom_call" | custom-call | flops 8000000000 | bytes 16000000 | tf_op jit(solution)/shard_map/first_local/pallas_call | solution.py:147
  16.2 4.2 %vectors_parts.1 = (bf16[1024,1536]{1,0:T(8,128)(2,1)S(1)}, bf16[8,2,192,512]{3,2,1,0:T(8,128)(2,1)S(1)}) custom-call(f32[1536,512]{1,0:T(8,128)} %bitcast.8), custom_call_target="tpu_custom_call" | custom-call | flops 1000000 | bytes 9000000 | tf_op jit(solution)/shard_map/vectors_parts/pallas_call | solution.py:240
  20.4 0.5 backward_face.2.rest
  20.9 0.7 z_faces.2.rest
  21.6 3.4 %collective-permute-done.3.forward = f32[8,96,128]{2,1,0:T(8,128)S(1)} collective-permute-done((f32[8,96,128]{2,1,0:T(8,128)S(1)}, f32[8,96,128]{2,1,0:T(8,128)S(1)}, u32[]{:S(2)}, u32[]{:S(2)}) %collective-permute-start.3) | collective-permute-done | bytes 393248 | tf_op jit(solution)/shard_map/ppermute | solution.py:524
  25.0 1.4 %forward_face.2 = (f32[8,96,128]{2,1,0:T(8,128)S(1)}, f32[256,128]{1,0:T(8,128)S(1)}, f32[256,128]{1,0:T(8,128)S(1)}) custom-call(f32[8,96,128]{2,1,0:T(8,128)S(1)} %z_faces.2.rest, f32[8,96,128]{2,1,0:T(8,128)S(1)} %collective-permute-done.3.forward, bf16[4,8,192,192]{3,2,1,0:T(8,128)(2,1)S(1)} %get-tuple-element.29.matrix, ...), custom_call_target="tpu_custom_call" | custom-call | flops 2000000000 | bytes 8000000 | tf_op jit(solution)/shard_map/forward_face/pallas_call | solution.py:344
  26.6 1.2 %collective-permute-done.4.received = f32[256,128]{1,0:T(8,128)S(1)} collective-permute-done((f32[256,128]{1,0:T(8,128)S(1)}, f32[256,128]{1,0:T(8,128)S(1)}, u32[]{:S(2)}, u32[]{:S(2)}) %collective-permute-start.4) | collective-permute-done | bytes 131104 | tf_op jit(solution)/shard_map/ppermute | solution.py:529
  27.8 1.6 %collective-permute-start.5 = (f32[128,128]{1,0:T(8,128)S(1)}, f32[128,128]{1,0:T(8,128)S(1)}, u32[]{:S(2)}, u32[]{:S(2)}) collective-permute-start(f32[128,128]{1,0:T(8,128)S(1)} %get-tuple-element.36), channel_id=1, source_target_pairs={{0,8},{4,12},{8,0},{12,4},{1,9},{5,13},{9,1},{13,5},{2,10},{6,14},... | collective-permute-start | bytes 196616 | tf_op jit(solution)/shard_map/ppermute | solution.py:529
  29.4 2.8 %collective-permute-done.5.right = f32[128,128]{1,0:T(8,128)S(1)} collective-permute-done((f32[128,128]{1,0:T(8,128)S(1)}, f32[128,128]{1,0:T(8,128)S(1)}, u32[]{:S(2)}, u32[]{:S(2)}) %collective-permute-start.5) | collective-permute-done | bytes 65568 | tf_op jit(solution)/shard_map/ppermute | solution.py:529
  32.2 0.6 collective-permute-start.6
  32.8 2.9 %collective-permute-start.7 = (f32[128,128]{1,0:T(8,128)S(1)}, f32[128,128]{1,0:T(8,128)S(1)}, u32[]{:S(2)}, u32[]{:S(2)}) collective-permute-start(f32[128,128]{1,0:T(8,128)S(1)} %add.2.refs_0_), channel_id=1, source_target_pairs={{0,2},{1,3},{2,0},{3,1},{4,6},{5,7},{6,4},{7,5},{8,10},{9,11},{10,... | collective-permute-start | bytes 196616 | tf_op jit(solution)/shard_map/ppermute | solution.py:529
  35.7 0.9 collective-permute-start.8
  36.8 1.3 %collective-permute-done.7.refs_2_ = f32[128,128]{1,0:T(8,128)S(1)} collective-permute-done((f32[128,128]{1,0:T(8,128)S(1)}, f32[128,128]{1,0:T(8,128)S(1)}, u32[]{:S(2)}, u32[]{:S(2)}) %collective-permute-start.7) | collective-permute-done | bytes 65568 | tf_op jit(solution)/shard_map/ppermute | solution.py:529
  38.1 3.7 %collective-permute-done.8.refs_3_ = f32[128,128]{1,0:T(8,128)S(1)} collective-permute-done((f32[128,128]{1,0:T(8,128)S(1)}, f32[128,128]{1,0:T(8,128)S(1)}, u32[]{:S(2)}, u32[]{:S(2)}) %collective-permute-start.8) | collective-permute-done | bytes 65568 | tf_op jit(solution)/shard_map/ppermute | solution.py:529
  41.9 1.6 %collective-permute-start.9 = (f32[128,128]{1,0:T(8,128)S(1)}, f32[128,128]{1,0:T(8,128)S(1)}, u32[]{:S(2)}, u32[]{:S(2)}) collective-permute-start(f32[128,128]{1,0:T(8,128)S(1)} %scale.2.refs_0_), channel_id=1, source_target_pairs={{0,8},{4,12},{8,0},{12,4},{1,9},{5,13},{9,1},{13,5},{2,10},{6,14},... | collective-permute-start | bytes 196616 | tf_op jit(solution)/shard_map/ppermute | solution.py:529
  43.4 2.8 %collective-permute-done.9.refs_1_ = f32[128,128]{1,0:T(8,128)S(1)} collective-permute-done((f32[128,128]{1,0:T(8,128)S(1)}, f32[128,128]{1,0:T(8,128)S(1)}, u32[]{:S(2)}, u32[]{:S(2)}) %collective-permute-start.9) | collective-permute-done | bytes 65568 | tf_op jit(solution)/shard_map/ppermute | solution.py:529
  46.2 0.7 first_half.3.base
  46.9 0.6 collective-permute-done.11.refs_1_
  47.5 0.7 second_half.2.x_ref.x
  48.2 1.3 %collective-permute-start.13 = (f32[8,96,128]{2,1,0:T(8,128)S(1)}, f32[8,96,128]{2,1,0:T(8,128)S(1)}, u32[]{:S(2)}, u32[]{:S(2)}) collective-permute-start(f32[8,96,128]{2,1,0:T(8,128)S(1)} %second_half.2.x_ref.x), channel_id=1, source_target_pairs={{0,12},{4,0},{8,4},{12,8},{1,13},{5,1},{9,5},{13,9},{2,14},{6,2},{... | collective-permute-start | bytes 1179656 | tf_op jit(solution)/shard_map/ppermute | solution.py:524
  49.5 1.5 %collective-permute-start.15 = (f32[8,96,128]{2,1,0:T(8,128)S(1)}, f32[8,96,128]{2,1,0:T(8,128)S(1)}, u32[]{:S(2)}, u32[]{:S(2)}) collective-permute-start(f32[8,96,128]{2,1,0:T(8,128)S(1)} %second_half.2.x_ref.x), channel_id=1, source_target_pairs={{0,16},{16,0},{1,17},{17,1},{2,18},{18,2},{3,19},{19,3},{4,20},{20... | collective-permute-start | bytes 1179656 | tf_op jit(solution)/shard_map/ppermute | solution.py:529
  51.0 3.5 %collective-permute-start.16 = (f32[8,96,128]{2,1,0:T(8,128)S(1)}, f32[8,96,128]{2,1,0:T(8,128)S(1)}, u32[]{:S(2)}, u32[]{:S(2)}) collective-permute-start(f32[8,96,128]{2,1,0:T(8,128)S(1)} %second_half.2.x_ref.x), channel_id=1, source_target_pairs={{0,3},{1,0},{2,1},{3,2},{4,7},{5,4},{6,5},{7,6},{8,11},{9,8},{10,9... | collective-permute-start | bytes 1179656 | tf_op jit(solution)/shard_map/ppermute | solution.py:524
  54.5 3.0 %local_part.1.rest = f32[8,96,128]{2,1,0:T(8,128)S(1)} custom-call(f32[8,96,128]{2,1,0:T(8,128)S(1)} %second_half.2.x_ref.x, f32[8,96,128]{2,1,0:T(8,128)S(1)} %get-tuple-element.37.source, bf16[5,8,192,192]{3,2,1,0:T(8,128)(2,1)S(1)} %get-tuple-element.38.local), custom_call_target="tpu_custom_call" | custom-call | flops 8000000000 | bytes 8000000 | tf_op jit(solution)/shard_map/local_part/pallas_call | solution.py:182
  57.5 4.5 %collective-permute-done.12.backward = f32[8,96,128]{2,1,0:T(8,128)S(1)} collective-permute-done((f32[8,96,128]{2,1,0:T(8,128)S(1)}, f32[8,96,128]{2,1,0:T(8,128)S(1)}, u32[]{:S(2)}, u32[]{:S(2)}) %collective-permute-start.12) | collective-permute-done | bytes 393248 | tf_op jit(solution)/shard_map/ppermute | solution.py:524
  62.5 0.7 z_faces.3.rest
  63.1 6.5 %collective-permute-done.16.forward = f32[8,96,128]{2,1,0:T(8,128)S(1)} collective-permute-done((f32[8,96,128]{2,1,0:T(8,128)S(1)}, f32[8,96,128]{2,1,0:T(8,128)S(1)}, u32[]{:S(2)}, u32[]{:S(2)}) %collective-permute-start.16) | collective-permute-done | bytes 393248 | tf_op jit(solution)/shard_map/ppermute | solution.py:524
  69.6 1.4 %forward_face.3 = (f32[8,96,128]{2,1,0:T(8,128)S(1)}, f32[256,128]{1,0:T(8,128)S(1)}, f32[256,128]{1,0:T(8,128)S(1)}) custom-call(f32[8,96,128]{2,1,0:T(8,128)S(1)} %z_faces.3.rest, f32[8,96,128]{2,1,0:T(8,128)S(1)} %collective-permute-done.16.forward, bf16[4,8,192,192]{3,2,1,0:T(8,128)(2,1)S(1)} %get-tuple-element.29.matrix, ...), custom_call_target="tpu_custom_call" | custom-call | flops 2000000000 | bytes 8000000 | tf_op jit(solution)/shard_map/forward_face/pallas_call | solution.py:344
  71.1 1.3 %collective-permute-done.17.received = f32[256,128]{1,0:T(8,128)S(1)} collective-permute-done((f32[256,128]{1,0:T(8,128)S(1)}, f32[256,128]{1,0:T(8,128)S(1)}, u32[]{:S(2)}, u32[]{:S(2)}) %collective-permute-start.17) | collective-permute-done | bytes 131104 | tf_op jit(solution)/shard_map/ppermute | solution.py:529
  72.4 1.5 %collective-permute-start.18 = (f32[128,128]{1,0:T(8,128)S(1)}, f32[128,128]{1,0:T(8,128)S(1)}, u32[]{:S(2)}, u32[]{:S(2)}) collective-permute-start(f32[128,128]{1,0:T(8,128)S(1)} %get-tuple-element.43), channel_id=1, source_target_pairs={{0,8},{4,12},{8,0},{12,4},{1,9},{5,13},{9,1},{13,5},{2,10},{6,14},... | collective-permute-start | bytes 196616 | tf_op jit(solution)/shard_map/ppermute | solution.py:529
  74.0 2.8 %collective-permute-done.18.right = f32[128,128]{1,0:T(8,128)S(1)} collective-permute-done((f32[128,128]{1,0:T(8,128)S(1)}, f32[128,128]{1,0:T(8,128)S(1)}, u32[]{:S(2)}, u32[]{:S(2)}) %collective-permute-start.18) | collective-permute-done | bytes 65568 | tf_op jit(solution)/shard_map/ppermute | solution.py:529
  76.8 1.6 %collective-permute-start.25 = (f32[8,96,128]{2,1,0:T(8,128)S(1)}, f32[8,96,128]{2,1,0:T(8,128)S(1)}, u32[]{:S(2)}, u32[]{:S(2)}) collective-permute-start(f32[8,96,128]{2,1,0:T(8,128)S(1)} %get-tuple-element.46.own.residual), channel_id=1, source_target_pairs={{0,16},{16,0},{1,17},{17,1},{2,18},{18,2},{3,19},{19,3},{4,20},{20... | collective-permute-start | bytes 1179656 | tf_op jit(solution)/shard_map/ppermute | solution.py:529
  78.3 0.6 collective-permute-start.19
  79.2 3.5 %collective-permute-start.21 = (f32[128,128]{1,0:T(8,128)S(1)}, f32[128,128]{1,0:T(8,128)S(1)}, u32[]{:S(2)}, u32[]{:S(2)}) collective-permute-start(f32[128,128]{1,0:T(8,128)S(1)} %add.3.refs_0_), channel_id=1, source_target_pairs={{0,3},{1,2},{2,1},{3,0},{4,7},{5,6},{6,5},{7,4},{8,11},{9,10},{10,... | collective-permute-start | bytes 196616 | tf_op jit(solution)/shard_map/ppermute | solution.py:529
  82.7 3.2 %collective-permute-done.20.refs_2_ = f32[128,128]{1,0:T(8,128)S(1)} collective-permute-done((f32[128,128]{1,0:T(8,128)S(1)}, f32[128,128]{1,0:T(8,128)S(1)}, u32[]{:S(2)}, u32[]{:S(2)}) %collective-permute-start.20) | collective-permute-done | bytes 65568 | tf_op jit(solution)/shard_map/ppermute | solution.py:529
  86.0 1.5 %collective-permute-start.24 = (f32[128,128]{1,0:T(8,128)S(1)}, f32[128,128]{1,0:T(8,128)S(1)}, u32[]{:S(2)}, u32[]{:S(2)}) collective-permute-start(f32[128,128]{1,0:T(8,128)S(1)} %scale.3.refs_0_), channel_id=1, source_target_pairs={{0,8},{4,12},{8,0},{12,4},{1,9},{5,13},{9,1},{13,5},{2,10},{6,14},... | collective-permute-start | bytes 196616 | tf_op jit(solution)/shard_map/ppermute | solution.py:529
  87.6 0.5 collective-permute-start.23
  88.1 1.5 %collective-permute-start.22 = (f32[128,128]{1,0:T(8,128)S(1)}, f32[128,128]{1,0:T(8,128)S(1)}, u32[]{:S(2)}, u32[]{:S(2)}) collective-permute-start(f32[128,128]{1,0:T(8,128)S(1)} %scale.3.refs_0_), channel_id=1, source_target_pairs={{0,24},{4,28},{8,16},{12,20},{16,8},{20,12},{24,0},{28,4},{1,25},{... | collective-permute-start | bytes 196616 | tf_op jit(solution)/shard_map/ppermute | solution.py:567
  89.6 1.0 %join.1 = f32[8,96,256]{2,1,0:T(8,128)} custom-call(f32[8,96,128]{2,1,0:T(8,128)S(1)} %get-tuple-element.46.own.residual, f32[8,96,128]{2,1,0:T(8,128)S(1)} %collective-permute-done.25.other.residual), custom_call_target="tpu_custom_call" | custom-call | flops 1000000 | bytes 2000000 | tf_op jit(solution)/shard_map/join/pallas_call | solution.py:478
  91.0 0.7 first_half.4.base
  92.0 0.7 second_half.3.own
  92.7 0.8 collective-permute-done.22.refs_1_
  93.5 0.7 first_half.5.other
  94.2 0.6 collective-permute-done.29.refs_1_
  94.8 1.5 %final.1 = f32[8,96,256]{2,1,0:T(8,128)} custom-call(f32[8,96,128]{2,1,0:T(8,128)S(1)} %second_half.3.own, f32[8,96,128]{2,1,0:T(8,128)S(1)} %first_half.5.other, bf16[8,2,192,512]{3,2,1,0:T(8,128)(2,1)S(1)} %get-tuple-element.32.vectors, f32[128,128]{1,0:T(8,128)S(1)} %collective-permute-done.28.refs_0_, f32[128,128]{1,0:T(8,128)S(1)} %collective-permute-done.29.refs_1_), custom_call_target="tpu_custom_call" | custom-call | flops 1000000000 | bytes 4000000 | tf_op jit(solution)/shard_map/final/pallas_call | solution.py:506
  (38 shorter events, 2.2 us)
Async XLA Ops:
  2.4 18.1 %collective-permute-start = (f32[8,96,128]{2,1,0:T(8,128)S(1)}, f32[8,96,128]{2,1,0:T(8,128)S(1)}, u32[]{:S(2)}, u32[]{:S(2)}) collective-permute-start(f32[8,96,128]{2,1,0:T(8,128)S(1)} %pack.1.x_ref.x), channel_id=1, source_target_pairs={{0,1},{1,2},{2,3},{3,0},{4,5},{5,6},{6,7},{7,4},{8,9},{9,10},{10,1... | collective-permute-start | bytes 1179656 | tf_op jit(solution)/shard_map/ppermute | solution.py:524
  5.4 15.4 %collective-permute-start.1 = (f32[8,96,128]{2,1,0:T(8,128)S(1)}, f32[8,96,128]{2,1,0:T(8,128)S(1)}, u32[]{:S(2)}, u32[]{:S(2)}) collective-permute-start(f32[8,96,128]{2,1,0:T(8,128)S(1)} %pack.1.x_ref.x), channel_id=1, source_target_pairs={{0,12},{4,0},{8,4},{12,8},{1,13},{5,1},{9,5},{13,9},{2,14},{6,2},{... | collective-permute-start | bytes 1179656 | tf_op jit(solution)/shard_map/ppermute | solution.py:524
  6.1 14.8 %collective-permute-start.2 = (f32[8,96,128]{2,1,0:T(8,128)S(1)}, f32[8,96,128]{2,1,0:T(8,128)S(1)}, u32[]{:S(2)}, u32[]{:S(2)}) collective-permute-start(f32[8,96,128]{2,1,0:T(8,128)S(1)} %pack.1.x_ref.x), channel_id=1, source_target_pairs={{0,4},{4,8},{8,12},{12,0},{1,5},{5,9},{9,13},{13,1},{2,6},{6,10},{... | collective-permute-start | bytes 1179656 | tf_op jit(solution)/shard_map/ppermute | solution.py:524
  6.1 18.9 %collective-permute-start.3 = (f32[8,96,128]{2,1,0:T(8,128)S(1)}, f32[8,96,128]{2,1,0:T(8,128)S(1)}, u32[]{:S(2)}, u32[]{:S(2)}) collective-permute-start(f32[8,96,128]{2,1,0:T(8,128)S(1)} %pack.1.x_ref.x), channel_id=1, source_target_pairs={{0,3},{1,0},{2,1},{3,2},{4,7},{5,4},{6,5},{7,6},{8,11},{9,8},{10,9... | collective-permute-start | bytes 1179656 | tf_op jit(solution)/shard_map/ppermute | solution.py:524
  25.0 11.6 %copy-start = (f32[2,512]{1,0:T(2,128)S(1)}, f32[2,512]{1,0:T(2,128)}, u32[]{:S(2)}) copy-start(f32[2,512]{1,0:T(2,128)} %inverse.1) | copy-start | bytes 12292
  26.4 1.4 %collective-permute-start.4 = (f32[256,128]{1,0:T(8,128)S(1)}, f32[256,128]{1,0:T(8,128)S(1)}, u32[]{:S(2)}, u32[]{:S(2)}) collective-permute-start(f32[256,128]{1,0:T(8,128)S(1)} %get-tuple-element.34), channel_id=1, source_target_pairs={{0,4},{4,0},{8,12},{12,8},{1,5},{5,1},{9,13},{13,9},{2,6},{6,2},{1... | collective-permute-start | bytes 393224 | tf_op jit(solution)/shard_map/ppermute | solution.py:529
  27.8 4.3 %collective-permute-start.5 = (f32[128,128]{1,0:T(8,128)S(1)}, f32[128,128]{1,0:T(8,128)S(1)}, u32[]{:S(2)}, u32[]{:S(2)}) collective-permute-start(f32[128,128]{1,0:T(8,128)S(1)} %get-tuple-element.36), channel_id=1, source_target_pairs={{0,8},{4,12},{8,0},{12,4},{1,9},{5,13},{9,1},{13,5},{2,10},{6,14},... | collective-permute-start | bytes 196616 | tf_op jit(solution)/shard_map/ppermute | solution.py:529
  32.2 4.6 %collective-permute-start.6 = (f32[128,128]{1,0:T(8,128)S(1)}, f32[128,128]{1,0:T(8,128)S(1)}, u32[]{:S(2)}, u32[]{:S(2)}) collective-permute-start(f32[128,128]{1,0:T(8,128)S(1)} %add.2.refs_0_), channel_id=1, source_target_pairs={{0,1},{1,0},{2,3},{3,2},{4,5},{5,4},{6,7},{7,6},{8,9},{9,8},{10,11... | collective-permute-start | bytes 196616 | tf_op jit(solution)/shard_map/ppermute | solution.py:529
  32.8 5.3 %collective-permute-start.7 = (f32[128,128]{1,0:T(8,128)S(1)}, f32[128,128]{1,0:T(8,128)S(1)}, u32[]{:S(2)}, u32[]{:S(2)}) collective-permute-start(f32[128,128]{1,0:T(8,128)S(1)} %add.2.refs_0_), channel_id=1, source_target_pairs={{0,2},{1,3},{2,0},{3,1},{4,6},{5,7},{6,4},{7,5},{8,10},{9,11},{10,... | collective-permute-start | bytes 196616 | tf_op jit(solution)/shard_map/ppermute | solution.py:529
  35.7 6.1 %collective-permute-start.8 = (f32[128,128]{1,0:T(8,128)S(1)}, f32[128,128]{1,0:T(8,128)S(1)}, u32[]{:S(2)}, u32[]{:S(2)}) collective-permute-start(f32[128,128]{1,0:T(8,128)S(1)} %add.2.refs_0_), channel_id=1, source_target_pairs={{0,3},{1,2},{2,1},{3,0},{4,7},{5,6},{6,5},{7,4},{8,11},{9,10},{10,... | collective-permute-start | bytes 196616 | tf_op jit(solution)/shard_map/ppermute | solution.py:529
  41.9 4.3 %collective-permute-start.9 = (f32[128,128]{1,0:T(8,128)S(1)}, f32[128,128]{1,0:T(8,128)S(1)}, u32[]{:S(2)}, u32[]{:S(2)}) collective-permute-start(f32[128,128]{1,0:T(8,128)S(1)} %scale.2.refs_0_), channel_id=1, source_target_pairs={{0,8},{4,12},{8,0},{12,4},{1,9},{5,13},{9,1},{13,5},{2,10},{6,14},... | collective-permute-start | bytes 196616 | tf_op jit(solution)/shard_map/ppermute | solution.py:529
  43.4 3.4 %collective-permute-start.10 = (f32[128,128]{1,0:T(8,128)S(1)}, f32[128,128]{1,0:T(8,128)S(1)}, u32[]{:S(2)}, u32[]{:S(2)}) collective-permute-start(f32[128,128]{1,0:T(8,128)S(1)} %scale.2.refs_0_), channel_id=1, source_target_pairs={{0,4},{4,0},{8,12},{12,8},{1,5},{5,1},{9,13},{13,9},{2,6},{6,2},{1... | collective-permute-start | bytes 196616 | tf_op jit(solution)/shard_map/ppermute | solution.py:529
  46.2 1.3 %collective-permute-start.11 = (f32[128,128]{1,0:T(8,128)S(1)}, f32[128,128]{1,0:T(8,128)S(1)}, u32[]{:S(2)}, u32[]{:S(2)}) collective-permute-start(f32[128,128]{1,0:T(8,128)S(1)} %collective-permute-done.9.refs_1_), channel_id=1, source_target_pairs={{0,4},{4,0},{8,12},{12,8},{1,5},{5,1},{9,13},{13,9},{2,6},{6,2},{1... | collective-permute-start | bytes 196616 | tf_op jit(solution)/shard_map/ppermute | solution.py:529
  48.1 13.9 %collective-permute-start.12 = (f32[8,96,128]{2,1,0:T(8,128)S(1)}, f32[8,96,128]{2,1,0:T(8,128)S(1)}, u32[]{:S(2)}, u32[]{:S(2)}) collective-permute-start(f32[8,96,128]{2,1,0:T(8,128)S(1)} %second_half.2.x_ref.x), channel_id=1, source_target_pairs={{0,1},{1,2},{2,3},{3,0},{4,5},{5,6},{6,7},{7,4},{8,9},{9,10},{10,1... | collective-permute-start | bytes 1179656 | tf_op jit(solution)/shard_map/ppermute | solution.py:524
  48.2 14.2 %collective-permute-start.13 = (f32[8,96,128]{2,1,0:T(8,128)S(1)}, f32[8,96,128]{2,1,0:T(8,128)S(1)}, u32[]{:S(2)}, u32[]{:S(2)}) collective-permute-start(f32[8,96,128]{2,1,0:T(8,128)S(1)} %second_half.2.x_ref.x), channel_id=1, source_target_pairs={{0,12},{4,0},{8,4},{12,8},{1,13},{5,1},{9,5},{13,9},{2,14},{6,2},{... | collective-permute-start | bytes 1179656 | tf_op jit(solution)/shard_map/ppermute | solution.py:524
  49.5 13.0 %collective-permute-start.14 = (f32[8,96,128]{2,1,0:T(8,128)S(1)}, f32[8,96,128]{2,1,0:T(8,128)S(1)}, u32[]{:S(2)}, u32[]{:S(2)}) collective-permute-start(f32[8,96,128]{2,1,0:T(8,128)S(1)} %second_half.2.x_ref.x), channel_id=1, source_target_pairs={{0,4},{4,8},{8,12},{12,0},{1,5},{5,9},{9,13},{13,1},{2,6},{6,10},{... | collective-permute-start | bytes 1179656 | tf_op jit(solution)/shard_map/ppermute | solution.py:524
  49.5 13.6 %collective-permute-start.15 = (f32[8,96,128]{2,1,0:T(8,128)S(1)}, f32[8,96,128]{2,1,0:T(8,128)S(1)}, u32[]{:S(2)}, u32[]{:S(2)}) collective-permute-start(f32[8,96,128]{2,1,0:T(8,128)S(1)} %second_half.2.x_ref.x), channel_id=1, source_target_pairs={{0,16},{16,0},{1,17},{17,1},{2,18},{18,2},{3,19},{19,3},{4,20},{20... | collective-permute-start | bytes 1179656 | tf_op jit(solution)/shard_map/ppermute | solution.py:529
  51.0 18.6 %collective-permute-start.16 = (f32[8,96,128]{2,1,0:T(8,128)S(1)}, f32[8,96,128]{2,1,0:T(8,128)S(1)}, u32[]{:S(2)}, u32[]{:S(2)}) collective-permute-start(f32[8,96,128]{2,1,0:T(8,128)S(1)} %second_half.2.x_ref.x), channel_id=1, source_target_pairs={{0,3},{1,0},{2,1},{3,2},{4,7},{5,4},{6,5},{7,6},{8,11},{9,8},{10,9... | collective-permute-start | bytes 1179656 | tf_op jit(solution)/shard_map/ppermute | solution.py:524
  71.0 1.4 %collective-permute-start.17 = (f32[256,128]{1,0:T(8,128)S(1)}, f32[256,128]{1,0:T(8,128)S(1)}, u32[]{:S(2)}, u32[]{:S(2)}) collective-permute-start(f32[256,128]{1,0:T(8,128)S(1)} %get-tuple-element.41), channel_id=1, source_target_pairs={{0,4},{4,0},{8,12},{12,8},{1,5},{5,1},{9,13},{13,9},{2,6},{6,2},{1... | collective-permute-start | bytes 393224 | tf_op jit(solution)/shard_map/ppermute | solution.py:529
  72.4 4.3 %collective-permute-start.18 = (f32[128,128]{1,0:T(8,128)S(1)}, f32[128,128]{1,0:T(8,128)S(1)}, u32[]{:S(2)}, u32[]{:S(2)}) collective-permute-start(f32[128,128]{1,0:T(8,128)S(1)} %get-tuple-element.43), channel_id=1, source_target_pairs={{0,8},{4,12},{8,0},{12,4},{1,9},{5,13},{9,1},{13,5},{2,10},{6,14},... | collective-permute-start | bytes 196616 | tf_op jit(solution)/shard_map/ppermute | solution.py:529
  76.8 12.8 %collective-permute-start.25 = (f32[8,96,128]{2,1,0:T(8,128)S(1)}, f32[8,96,128]{2,1,0:T(8,128)S(1)}, u32[]{:S(2)}, u32[]{:S(2)}) collective-permute-start(f32[8,96,128]{2,1,0:T(8,128)S(1)} %get-tuple-element.46.own.residual), channel_id=1, source_target_pairs={{0,16},{16,0},{1,17},{17,1},{2,18},{18,2},{3,19},{19,3},{4,20},{20... | collective-permute-start | bytes 1179656 | tf_op jit(solution)/shard_map/ppermute | solution.py:529
  78.3 4.4 %collective-permute-start.19 = (f32[128,128]{1,0:T(8,128)S(1)}, f32[128,128]{1,0:T(8,128)S(1)}, u32[]{:S(2)}, u32[]{:S(2)}) collective-permute-start(f32[128,128]{1,0:T(8,128)S(1)} %add.3.refs_0_), channel_id=1, source_target_pairs={{0,1},{1,0},{2,3},{3,2},{4,5},{5,4},{6,7},{7,6},{8,9},{9,8},{10,11... | collective-permute-start | bytes 196616 | tf_op jit(solution)/shard_map/ppermute | solution.py:529
  78.9 7.0 %collective-permute-start.20 = (f32[128,128]{1,0:T(8,128)S(1)}, f32[128,128]{1,0:T(8,128)S(1)}, u32[]{:S(2)}, u32[]{:S(2)}) collective-permute-start(f32[128,128]{1,0:T(8,128)S(1)} %add.3.refs_0_), channel_id=1, source_target_pairs={{0,2},{1,3},{2,0},{3,1},{4,6},{5,7},{6,4},{7,5},{8,10},{9,11},{10,... | collective-permute-start | bytes 196616 | tf_op jit(solution)/shard_map/ppermute | solution.py:529
  79.2 6.8 %collective-permute-start.21 = (f32[128,128]{1,0:T(8,128)S(1)}, f32[128,128]{1,0:T(8,128)S(1)}, u32[]{:S(2)}, u32[]{:S(2)}) collective-permute-start(f32[128,128]{1,0:T(8,128)S(1)} %add.3.refs_0_), channel_id=1, source_target_pairs={{0,3},{1,2},{2,1},{3,0},{4,7},{5,6},{6,5},{7,4},{8,11},{9,10},{10,... | collective-permute-start | bytes 196616 | tf_op jit(solution)/shard_map/ppermute | solution.py:529
  86.0 4.6 %collective-permute-start.24 = (f32[128,128]{1,0:T(8,128)S(1)}, f32[128,128]{1,0:T(8,128)S(1)}, u32[]{:S(2)}, u32[]{:S(2)}) collective-permute-start(f32[128,128]{1,0:T(8,128)S(1)} %scale.3.refs_0_), channel_id=1, source_target_pairs={{0,8},{4,12},{8,0},{12,4},{1,9},{5,13},{9,1},{13,5},{2,10},{6,14},... | collective-permute-start | bytes 196616 | tf_op jit(solution)/shard_map/ppermute | solution.py:529
  87.6 4.3 %collective-permute-start.23 = (f32[128,128]{1,0:T(8,128)S(1)}, f32[128,128]{1,0:T(8,128)S(1)}, u32[]{:S(2)}, u32[]{:S(2)}) collective-permute-start(f32[128,128]{1,0:T(8,128)S(1)} %scale.3.refs_0_), channel_id=1, source_target_pairs={{0,16},{16,0},{1,17},{17,1},{2,18},{18,2},{3,19},{19,3},{4,20},{20... | collective-permute-start | bytes 196616 | tf_op jit(solution)/shard_map/ppermute | solution.py:529
  88.1 3.9 %collective-permute-start.26 = (f32[128,128]{1,0:T(8,128)S(1)}, f32[128,128]{1,0:T(8,128)S(1)}, u32[]{:S(2)}, u32[]{:S(2)}) collective-permute-start(f32[128,128]{1,0:T(8,128)S(1)} %scale.3.refs_0_), channel_id=1, source_target_pairs={{0,4},{4,0},{8,12},{12,8},{1,5},{5,1},{9,13},{13,9},{2,6},{6,2},{1... | collective-permute-start | bytes 196616 | tf_op jit(solution)/shard_map/ppermute | solution.py:529
  88.1 5.4 %collective-permute-start.22 = (f32[128,128]{1,0:T(8,128)S(1)}, f32[128,128]{1,0:T(8,128)S(1)}, u32[]{:S(2)}, u32[]{:S(2)}) collective-permute-start(f32[128,128]{1,0:T(8,128)S(1)} %scale.3.refs_0_), channel_id=1, source_target_pairs={{0,24},{4,28},{8,16},{12,20},{16,8},{20,12},{24,0},{28,4},{1,25},{... | collective-permute-start | bytes 196616 | tf_op jit(solution)/shard_map/ppermute | solution.py:567
  90.7 1.3 %collective-permute-start.27 = (f32[128,128]{1,0:T(8,128)S(1)}, f32[128,128]{1,0:T(8,128)S(1)}, u32[]{:S(2)}, u32[]{:S(2)}) collective-permute-start(f32[128,128]{1,0:T(8,128)S(1)} %collective-permute-done.24.refs_1_), channel_id=1, source_target_pairs={{0,4},{4,0},{8,12},{12,8},{1,5},{5,1},{9,13},{13,9},{2,6},{6,2},{1... | collective-permute-start | bytes 196616 | tf_op jit(solution)/shard_map/ppermute | solution.py:529
  91.9 2.3 %collective-permute-start.28 = (f32[128,128]{1,0:T(8,128)S(1)}, f32[128,128]{1,0:T(8,128)S(1)}, u32[]{:S(2)}, u32[]{:S(2)}) collective-permute-start(f32[128,128]{1,0:T(8,128)S(1)} %collective-permute-done.23.refs_0_), channel_id=1, source_target_pairs={{0,4},{4,0},{8,12},{12,8},{1,5},{5,1},{9,13},{13,9},{2,6},{6,2},{1... | collective-permute-start | bytes 196616 | tf_op jit(solution)/shard_map/ppermute | solution.py:529
  93.5 1.3 %collective-permute-start.29 = (f32[128,128]{1,0:T(8,128)S(1)}, f32[128,128]{1,0:T(8,128)S(1)}, u32[]{:S(2)}, u32[]{:S(2)}) collective-permute-start(f32[128,128]{1,0:T(8,128)S(1)} %collective-permute-done.22.refs_1_), channel_id=1, source_target_pairs={{0,4},{4,0},{8,12},{12,8},{1,5},{5,1},{9,13},{13,9},{2,6},{6,2},{1... | collective-permute-start | bytes 196616 | tf_op jit(solution)/shard_map/ppermute | solution.py:529

commit v8 on v7

--- a/solution.py
+++ b/solution.py
@@ -82,14 +82,10 @@
     return pltpu.with_memory_space_constraint(value, pltpu.HBM)
 
 
-def pack_kernel(full, half, held, sems):
+def pack_kernel(full, half):
     group = lax.axis_index("groups")
-    copies = [pltpu.make_async_copy(full.at[site], held.at[site], sems.at[site]) for site in range(half.shape[0])]
-    for copy in copies:
-        copy.start()
-    for site, copy in enumerate(copies):
-        copy.wait()
-        half[site] = pick_half(held[site], group)
+    for site in range(full.shape[0]):
+        half[site] = pick_half(full[site], group)
 
 
 def pack(full):
@@ -97,13 +93,12 @@
     return pl.pallas_call(
         pack_kernel,
         out_shape=pltpu.VMEM((sites, rows, lanes // 2), F32),
-        in_specs=[pl.BlockSpec(memory_space=pl.ANY)],
-        out_specs=vmem(1)[0],
-        scratch_shapes=[pltpu.VMEM(full.shape, F32), pltpu.SemaphoreType.DMA((sites,))],
+        in_specs=vmem(1),
+        out_specs=vmem(1)[0],
         compiler_params=params(),
         cost_estimate=cost(1e6, 1e6),
         name="pack",
-    )(in_hbm(full))
+    )(full)
 
 
 def around(site, ny, nx):
@@ -284,13 +279,14 @@
     return fold(summed)
 
 
-def z_faces_kernel(rest, forward, backward, matrix, out):
-    faces = (lambda s: forward[s], lambda s: backward[s])
+def z_faces_kernel(rest, near, far, matrix, out):
+    parity = lax.rem(lax.axis_index("space"), 2)
+    faces = (lambda s: near[s], lambda s: far[s])
     for site in range(rest.shape[0]):
-        out[site] = rest[site] - apply_faces(site, faces, (matrix.at[0], matrix.at[1]))
-
-
-def z_faces(rest, forward, backward, matrix):
+        out[site] = rest[site] - apply_faces(site, faces, (matrix.at[parity], matrix.at[1 - parity]))
+
+
+def z_faces(rest, near, far, matrix):
     return pl.pallas_call(
         z_faces_kernel,
         out_shape=pltpu.VMEM(rest.shape, F32),
@@ -299,7 +295,7 @@
         compiler_params=params(),
         cost_estimate=cost(1e9, 4e6),
         name="z_faces",
-    )(rest, forward, backward, matrix)
+    )(rest, near, far, matrix)
 
 
 def edge_sign(last):
@@ -387,6 +383,17 @@
     )(left, right)
 
 
+def scaled_sum(keep, send, eigen):
+    blocks, slices = lax.axis_size("space"), lax.axis_size("tm")
+    if blocks != 4 or slices != 4:
+        return doubling([scale(eigen, over_time(halving(keep, send)))], blocks // 2)
+    keep, send = add_split(keep, crossed(send, "space", 1))
+    parts = [crossed(send, "space", 2), crossed(keep, "tm", 2), crossed_both(send, "space", 2, "tm", 2)]
+    d = scale(eigen, [keep] + parts)
+    moved, across = crossed(d, "space", 2), crossed_both(d, "space", 2, "tm", 1)
+    return [add(d, crossed(d, "tm", 1)), add(moved, across)]
+
+
 def scale_kernel(eigen, *refs):
     parts, out = refs[:-1], refs[-1]
     total = parts[0][...]
@@ -529,12 +536,17 @@
     return lax.ppermute(value, axis, [(i, i ^ mask) for i in range(count)])
 
 
+def crossed_both(value, first, first_mask, second, second_mask):
+    count, inner = lax.axis_size(first), lax.axis_size(second)
+    pairs = [(i * inner + j, (i ^ first_mask) * inner + (j ^ second_mask)) for i in range(count) for j in range(inner)]
+    return lax.ppermute(value, (first, second), pairs)
+
+
 def faces_of(x):
-    backward_t = shifted(x, "tm", 1)
-    forward_t = shifted(x, "tm", -1)
-    backward_z = shifted(x, "space", 1)
-    forward_z = shifted(x, "space", -1)
-    return forward_z, backward_z, forward_t, backward_t
+    count = lax.axis_size("space")
+    near = crossed(x, "space", 1)
+    far = lax.ppermute(x, "space", [(i, (i + 1 if i % 2 else i - 1) % count) for i in range(count)])
+    return near, far, shifted(x, "tm", -1), shifted(x, "tm", 1)
 
 
 def halving(keep, send):
@@ -562,9 +574,7 @@
 
 
 def across_groups(part, mask):
-    groups, count = lax.axis_size("groups"), lax.axis_size("space")
-    pairs = [(g * count + s, (g ^ 1) * count + (s ^ mask)) for g in range(groups) for s in range(count)]
-    return [crossed(part, "groups", 1), lax.ppermute(part, ("groups", "space"), pairs)]
+    return [crossed(part, "groups", 1), crossed_both(part, "groups", 1, "space", mask)]
 
 
 def over_time(part):
@@ -597,25 +607,23 @@
         last = sweep == ITERS - 1
         if sweep:
             faces = faces_of(x)
-            if last:
-                other_x = crossed(x, "groups", 1)
             rest = local_part(x, half_source, local, ny, nx)
-        forward_z, backward_z, forward_t, backward_t = faces
+        near, far, forward_t, backward_t = faces
+        if last:
+            near, x = lax.optimization_barrier((near, x))
+            other_x = crossed(x, "groups", 1)
         rest = backward_face(rest, backward_t, halo)
-        rest = z_faces(rest, forward_z, backward_z, halo)
-        if sweep and last:
+        rest = z_faces(rest, near, far, halo)
+        if last:
             rest, other_x = lax.optimization_barrier((rest, other_x))
         residual, keep, send = forward_face(rest, forward_t, halo, by_rows)
-        part = halving(keep, send)
-        if last:
-            part, residual = lax.optimization_barrier((part, residual))
-            other_residual = crossed(residual, "groups", 1)
-        parts = over_time(part)
-        d = scale(eigen, parts)
         if not last:
-            pieces = doubling([d], blocks // 2)
+            pieces = scaled_sum(keep, send, eigen)
             base = first_half(x, residual, pieces, by_columns)
             x = second_half(base, paired(pieces), by_columns)
+    part, residual = lax.optimization_barrier((halving(keep, send), residual))
+    other_residual = crossed(residual, "groups", 1)
+    d = scale(eigen, over_time(part))
     mask = blocks // 2
     other = across_groups(d, mask)
     own = [d, crossed(d, "space", mask)]

time: 96.8 us -> 96.2 us (level)
  Pallas kernels: 27.8 us -> 26.4 us
  local copies, waits for them, and re-layouts: 0.01 us -> 1.13 us
  waiting for transfers between devices: 35.7 us -> 34.7 us
    ppermute x1 -> x5, starting transfers between devices: 1.5 us -> 6.72 us  [the longest x3 3.87 us: crossed_both(): return lax.ppermute(value, (first, second), pairs)]
    ppermute x1 -> x5, waiting for transfers between devices: 0.84 us -> 3.61 us  [the longest x3 3.61 us: crossed_both(): return lax.ppermute(value, (first, second), pairs)]
    ppermute x21 -> x22, waiting for transfers between devices: 20.5 us -> 17.9 us  [crossed(): return lax.ppermute(value, axis, [(i, i ^ mask) for i in range(count)])]
    ppermute x8 -> x4, starting transfers between devices: 11 us -> 8.51 us  [shifted(): lax.ppermute(value, axis, [(i, (i + step) % count) for i in range(count)])]
    ppermute x21 -> x22, starting transfers between devices: 19.4 us -> 17.3 us  [crossed(): return lax.ppermute(value, axis, [(i, i ^ mask) for i in range(count)])]
    pallas_call x1, Pallas kernels: 1.72 us -> 0.27 us  [pack(): pl.pallas_call(pack_kernel, out_shape=pltpu.VMEM((sites, rows, lanes // 2...]
    ppermute x8 -> x4, waiting for transfers between devices: 14.4 us -> 13.2 us  [shifted(): lax.ppermute(value, axis, [(i, (i + step) % count) for i in range(count)])]
    unnamed x2 -> x4, local copies, waits for them, and re-layouts: 0.01 us -> 1.13 us
  transfers between devices with their start and end apart: 30 -> 31, of which waited for: 15 -> 18; matrix products, arithmetic and copies ran while one was open for 0% -> 0% of each run, Pallas kernels for 22% -> 22%
where the time goes in v8:
time: 96.2 us; the launch traced here: 95.8 us
  waiting for transfers between devices  34.7 us (36%)
  starting transfers between devices  32.6 us (34%)
  Pallas kernels  26.4 us (27%)
  local copies, waits for them, and re-layouts  1.13 us (1%)
  between operations  1.05 us (1%)
    ppermute x22, waiting for transfers between devices, crossed(): return lax.ppermute(value, axis, [(i, i ^ mask) for i in range(count)])  17.9 us
    ppermute x22, starting transfers between devices, crossed(): return lax.ppermute(value, axis, [(i, i ^ mask) for i in range(count)])  17.3 us
    ppermute x4, waiting for transfers between devices, shifted(): lax.ppermute(value, axis, [(i, (i + step) % count) for i in range(count)])  13.2 us
    ppermute x4, starting transfers between devices, shifted(): lax.ppermute(value, axis, [(i, (i + step) % count) for i in range(count)])  8.51 us
    pallas_call x1, Pallas kernels, first_local(): pl.pallas_call(functools.partial(first_kernel, ny, nx), grid=(sites,), ou...  7.69 us
    pallas_call x1, Pallas kernels, vectors_parts(): pl.pallas_call(vectors_kernel, grid=(sites // step,), out_shape=(pltpu.VM...  4.24 us
    ppermute x3, starting transfers between devices, crossed_both(): return lax.ppermute(value, (first, second), pairs)  3.87 us
    ppermute x3, waiting for transfers between devices, crossed_both(): return lax.ppermute(value, (first, second), pairs)  3.61 us
  transfers between devices with their start and end apart: 31, of which 18 were waited for; matrix products, arithmetic and copies ran while one was open for 0% of the time, Pallas kernels for 22%

profile of v8, /device:TPU:0, one launch (start us, length us, event | category | flops | bytes accessed | tf_op | source)
XLA Modules:
  0.0 95.8 jit_solution(447988830309276637)
XLA Ops:
  0.6 1.1 %copy-done = f32[1,1,2,4,96,256]{5,4,3,2,1,0:T(8,128)S(1)} copy-done((f32[1,1,2,4,96,256]{5,4,3,2,1,0:T(8,128)S(1)}, f32[1,1,2,4,96,256]{5,4,3,2,1,0:T(8,128)}, u32[]{:S(2)}) %copy-start) | copy-done | bytes 786456
  2.0 3.1 %collective-permute-start = (f32[8,96,128]{2,1,0:T(8,128)S(1)}, f32[8,96,128]{2,1,0:T(8,128)S(1)}, u32[]{:S(2)}, u32[]{:S(2)}) collective-permute-start(f32[8,96,128]{2,1,0:T(8,128)S(1)} %pack.1.x_ref.x), channel_id=1, source_target_pairs={{0,1},{1,2},{2,3},{3,0},{4,5},{5,6},{6,7},{7,4},{8,9},{9,10},{10,1... | collective-permute-start | bytes 1179656 | tf_op jit(solution)/shard_map/ppermute | solution.py:531
  5.1 1.6 %collective-permute-start.2 = (f32[8,96,128]{2,1,0:T(8,128)S(1)}, f32[8,96,128]{2,1,0:T(8,128)S(1)}, u32[]{:S(2)}, u32[]{:S(2)}) collective-permute-start(f32[8,96,128]{2,1,0:T(8,128)S(1)} %pack.1.x_ref.x), channel_id=1, source_target_pairs={{0,12},{4,8},{8,4},{12,0},{1,13},{5,9},{9,5},{13,1},{2,14},{6,10},... | collective-permute-start | bytes 1179656 | tf_op jit(solution)/shard_map/ppermute | solution.py:548
  6.7 2.2 %collective-permute-start.3 = (f32[8,96,128]{2,1,0:T(8,128)S(1)}, f32[8,96,128]{2,1,0:T(8,128)S(1)}, u32[]{:S(2)}, u32[]{:S(2)}) collective-permute-start(f32[8,96,128]{2,1,0:T(8,128)S(1)} %pack.1.x_ref.x), channel_id=1, source_target_pairs={{0,3},{1,0},{2,1},{3,2},{4,7},{5,4},{6,5},{7,6},{8,11},{9,8},{10,9... | collective-permute-start | bytes 1179656 | tf_op jit(solution)/shard_map/ppermute | solution.py:531
  9.0 7.7 %first_local.1 = (f32[8,96,128]{2,1,0:T(8,128)S(1)}, f32[8,96,128]{2,1,0:T(8,128)S(1)}, bf16[5,8,192,192]{3,2,1,0:T(8,128)(2,1)S(1)}, bf16[4,8,192,192]{3,2,1,0:T(8,128)(2,1)S(1)}) custom-call(f32[8,96,128]{2,1,0:T(8,128)S(1)} %pack.1.x_ref.x, f32[8,96,256]{2,1,0:T(8,128)} %bitcast.13, f32[9,8,96,192]{3,2,1,0:T(8,128)} %bitcast.12), custom_call_target="tpu_custom_call" | custom-call | flops 8000000000 | bytes 16000000 | tf_op jit(solution)/shard_map/first_local/pallas_call | solution.py:142
  16.7 4.2 %vectors_parts.1 = (bf16[1024,1536]{1,0:T(8,128)(2,1)S(1)}, bf16[8,2,192,512]{3,2,1,0:T(8,128)(2,1)S(1)}) custom-call(f32[1536,512]{1,0:T(8,128)} %bitcast.9), custom_call_target="tpu_custom_call" | custom-call | flops 1000000 | bytes 9000000 | tf_op jit(solution)/shard_map/vectors_parts/pallas_call | solution.py:235
  21.4 0.7 z_faces.2.rest
  22.1 2.6 %collective-permute-done.3.forward = f32[8,96,128]{2,1,0:T(8,128)S(1)} collective-permute-done((f32[8,96,128]{2,1,0:T(8,128)S(1)}, f32[8,96,128]{2,1,0:T(8,128)S(1)}, u32[]{:S(2)}, u32[]{:S(2)}) %collective-permute-start.3) | collective-permute-done | bytes 393248 | tf_op jit(solution)/shard_map/ppermute | solution.py:531
  24.7 1.4 %forward_face.2 = (f32[8,96,128]{2,1,0:T(8,128)S(1)}, f32[256,128]{1,0:T(8,128)S(1)}, f32[256,128]{1,0:T(8,128)S(1)}) custom-call(f32[8,96,128]{2,1,0:T(8,128)S(1)} %z_faces.2.rest, f32[8,96,128]{2,1,0:T(8,128)S(1)} %collective-permute-done.3.forward, bf16[4,8,192,192]{3,2,1,0:T(8,128)(2,1)S(1)} %get-tuple-element.31.matrix, ...), custom_call_target="tpu_custom_call" | custom-call | flops 2000000000 | bytes 8000000 | tf_op jit(solution)/shard_map/forward_face/pallas_call | solution.py:340
  26.2 1.3 %collective-permute-done.4.received = f32[256,128]{1,0:T(8,128)S(1)} collective-permute-done((f32[256,128]{1,0:T(8,128)S(1)}, f32[256,128]{1,0:T(8,128)S(1)}, u32[]{:S(2)}, u32[]{:S(2)}) %collective-permute-start.4) | collective-permute-done | bytes 131104 | tf_op jit(solution)/shard_map/ppermute | solution.py:536
  27.5 1.6 %collective-permute-start.5 = (f32[128,128]{1,0:T(8,128)S(1)}, f32[128,128]{1,0:T(8,128)S(1)}, u32[]{:S(2)}, u32[]{:S(2)}) collective-permute-start(f32[128,128]{1,0:T(8,128)S(1)} %get-tuple-element.38), channel_id=1, source_target_pairs={{0,8},{4,12},{8,0},{12,4},{1,9},{5,13},{9,1},{13,5},{2,10},{6,14},... | collective-permute-start | bytes 196616 | tf_op jit(solution)/shard_map/ppermute | solution.py:536
  29.1 1.9 %collective-permute-start.6 = (f32[128,128]{1,0:T(8,128)S(1)}, f32[128,128]{1,0:T(8,128)S(1)}, u32[]{:S(2)}, u32[]{:S(2)}) collective-permute-start(f32[128,128]{1,0:T(8,128)S(1)} %get-tuple-element.37.refs_0_), channel_id=1, source_target_pairs={{0,2},{1,3},{2,0},{3,1},{4,6},{5,7},{6,4},{7,5},{8,10},{9,11},{10,... | collective-permute-start | bytes 196616 | tf_op jit(solution)/shard_map/ppermute | solution.py:536
  31.0 1.0 %collective-permute-start.7 = (f32[128,128]{1,0:T(8,128)S(1)}, f32[128,128]{1,0:T(8,128)S(1)}, u32[]{:S(2)}, u32[]{:S(2)}) collective-permute-start(f32[128,128]{1,0:T(8,128)S(1)} %get-tuple-element.38), channel_id=1, source_target_pairs={{0,10},{1,11},{2,8},{3,9},{4,14},{5,15},{6,12},{7,13},{8,2},{9,3},... | collective-permute-start | bytes 196616 | tf_op jit(solution)/shard_map/ppermute | solution.py:542
  32.1 4.2 %collective-permute-done.6.refs_2_ = f32[128,128]{1,0:T(8,128)S(1)} collective-permute-done((f32[128,128]{1,0:T(8,128)S(1)}, f32[128,128]{1,0:T(8,128)S(1)}, u32[]{:S(2)}, u32[]{:S(2)}) %collective-permute-start.6) | collective-permute-done | bytes 65568 | tf_op jit(solution)/shard_map/ppermute | solution.py:536
  36.3 1.0 %collective-permute-done.7.refs_3_ = f32[128,128]{1,0:T(8,128)S(1)} collective-permute-done((f32[128,128]{1,0:T(8,128)S(1)}, f32[128,128]{1,0:T(8,128)S(1)}, u32[]{:S(2)}, u32[]{:S(2)}) %collective-permute-start.7) | collective-permute-done | bytes 65568 | tf_op jit(solution)/shard_map/ppermute | solution.py:542
  37.5 1.4 %collective-permute-start.10 = (f32[128,128]{1,0:T(8,128)S(1)}, f32[128,128]{1,0:T(8,128)S(1)}, u32[]{:S(2)}, u32[]{:S(2)}) collective-permute-start(f32[128,128]{1,0:T(8,128)S(1)} %scale.2.left), channel_id=1, source_target_pairs={{0,9},{1,8},{2,11},{3,10},{4,13},{5,12},{6,15},{7,14},{8,1},{9,0},... | collective-permute-start | bytes 196616 | tf_op jit(solution)/shard_map/ppermute | solution.py:542
  38.8 1.4 %collective-permute-start.9 = (f32[128,128]{1,0:T(8,128)S(1)}, f32[128,128]{1,0:T(8,128)S(1)}, u32[]{:S(2)}, u32[]{:S(2)}) collective-permute-start(f32[128,128]{1,0:T(8,128)S(1)} %scale.2.left), channel_id=1, source_target_pairs={{0,8},{4,12},{8,0},{12,4},{1,9},{5,13},{9,1},{13,5},{2,10},{6,14},... | collective-permute-start | bytes 196616 | tf_op jit(solution)/shard_map/ppermute | solution.py:536
  40.3 0.9 collective-permute-start.8
  41.1 1.7 %collective-permute-done.10.right = f32[128,128]{1,0:T(8,128)S(1)} collective-permute-done((f32[128,128]{1,0:T(8,128)S(1)}, f32[128,128]{1,0:T(8,128)S(1)}, u32[]{:S(2)}, u32[]{:S(2)}) %collective-permute-start.10) | collective-permute-done | bytes 65568 | tf_op jit(solution)/shard_map/ppermute | solution.py:542
  43.5 1.0 %collective-permute-done.8.right = f32[128,128]{1,0:T(8,128)S(1)} collective-permute-done((f32[128,128]{1,0:T(8,128)S(1)}, f32[128,128]{1,0:T(8,128)S(1)}, u32[]{:S(2)}, u32[]{:S(2)}) %collective-permute-start.8) | collective-permute-done | bytes 65568 | tf_op jit(solution)/shard_map/ppermute | solution.py:536
  44.6 0.7 first_half.3.base
  45.9 0.7 second_half.2.x_ref.x
  46.7 1.3 %collective-permute-start.13 = (f32[8,96,128]{2,1,0:T(8,128)S(1)}, f32[8,96,128]{2,1,0:T(8,128)S(1)}, u32[]{:S(2)}, u32[]{:S(2)}) collective-permute-start(f32[8,96,128]{2,1,0:T(8,128)S(1)} %second_half.2.x_ref.x), channel_id=1, source_target_pairs={{0,1},{1,2},{2,3},{3,0},{4,5},{5,6},{6,7},{7,4},{8,9},{9,10},{10,1... | collective-permute-start | bytes 1179656 | tf_op jit(solution)/shard_map/ppermute | solution.py:531
  48.1 1.3 %collective-permute-start.15 = (f32[8,96,128]{2,1,0:T(8,128)S(1)}, f32[8,96,128]{2,1,0:T(8,128)S(1)}, u32[]{:S(2)}, u32[]{:S(2)}) collective-permute-start(f32[8,96,128]{2,1,0:T(8,128)S(1)} %second_half.2.x_ref.x), channel_id=1, source_target_pairs={{0,12},{4,8},{8,4},{12,0},{1,13},{5,9},{9,5},{13,1},{2,14},{6,10},... | collective-permute-start | bytes 1179656 | tf_op jit(solution)/shard_map/ppermute | solution.py:548
  49.3 1.9 %collective-permute-start.17 = (f32[8,96,128]{2,1,0:T(8,128)S(1)}, f32[8,96,128]{2,1,0:T(8,128)S(1)}, u32[]{:S(2)}, u32[]{:S(2)}) collective-permute-start(f32[8,96,128]{2,1,0:T(8,128)S(1)} %second_half.2.x_ref.x), channel_id=1, source_target_pairs={{0,3},{1,0},{2,1},{3,2},{4,7},{5,4},{6,5},{7,6},{8,11},{9,8},{10,9... | collective-permute-start | bytes 1179656 | tf_op jit(solution)/shard_map/ppermute | solution.py:531
  51.2 1.5 %collective-permute-start.16 = (f32[8,96,128]{2,1,0:T(8,128)S(1)}, f32[8,96,128]{2,1,0:T(8,128)S(1)}, u32[]{:S(2)}, u32[]{:S(2)}) collective-permute-start(f32[8,96,128]{2,1,0:T(8,128)S(1)} %second_half.2.x_ref.x), channel_id=1, source_target_pairs={{0,16},{16,0},{1,17},{17,1},{2,18},{18,2},{3,19},{19,3},{4,20},{20... | collective-permute-start | bytes 1179656 | tf_op jit(solution)/shard_map/ppermute | solution.py:536
  52.7 3.0 %local_part.1.rest = f32[8,96,128]{2,1,0:T(8,128)S(1)} custom-call(f32[8,96,128]{2,1,0:T(8,128)S(1)} %second_half.2.x_ref.x, f32[8,96,128]{2,1,0:T(8,128)S(1)} %get-tuple-element.39.source, bf16[5,8,192,192]{3,2,1,0:T(8,128)(2,1)S(1)} %get-tuple-element.40.local), custom_call_target="tpu_custom_call" | custom-call | flops 8000000000 | bytes 8000000 | tf_op jit(solution)/shard_map/local_part/pallas_call | solution.py:177
  55.7 4.8 %collective-permute-done.13.backward = f32[8,96,128]{2,1,0:T(8,128)S(1)} collective-permute-done((f32[8,96,128]{2,1,0:T(8,128)S(1)}, f32[8,96,128]{2,1,0:T(8,128)S(1)}, u32[]{:S(2)}, u32[]{:S(2)}) %collective-permute-start.13) | collective-permute-done | bytes 393248 | tf_op jit(solution)/shard_map/ppermute | solution.py:531
  61.0 0.7 z_faces.3.rest
  61.6 0.9 collective-permute-done.16.x
  62.6 5.8 %collective-permute-done.17.forward = f32[8,96,128]{2,1,0:T(8,128)S(1)} collective-permute-done((f32[8,96,128]{2,1,0:T(8,128)S(1)}, f32[8,96,128]{2,1,0:T(8,128)S(1)}, u32[]{:S(2)}, u32[]{:S(2)}) %collective-permute-start.17) | collective-permute-done | bytes 393248 | tf_op jit(solution)/shard_map/ppermute | solution.py:531
  68.3 1.4 %forward_face.3 = (f32[8,96,128]{2,1,0:T(8,128)S(1)}, f32[256,128]{1,0:T(8,128)S(1)}, f32[256,128]{1,0:T(8,128)S(1)}) custom-call(f32[8,96,128]{2,1,0:T(8,128)S(1)} %z_faces.3.rest, f32[8,96,128]{2,1,0:T(8,128)S(1)} %collective-permute-done.17.forward, bf16[4,8,192,192]{3,2,1,0:T(8,128)(2,1)S(1)} %get-tuple-element.31.matrix, ...), custom_call_target="tpu_custom_call" | custom-call | flops 2000000000 | bytes 8000000 | tf_op jit(solution)/shard_map/forward_face/pallas_call | solution.py:340
  69.9 1.3 %collective-permute-done.18.received = f32[256,128]{1,0:T(8,128)S(1)} collective-permute-done((f32[256,128]{1,0:T(8,128)S(1)}, f32[256,128]{1,0:T(8,128)S(1)}, u32[]{:S(2)}, u32[]{:S(2)}) %collective-permute-start.18) | collective-permute-done | bytes 131104 | tf_op jit(solution)/shard_map/ppermute | solution.py:536
  71.2 1.0 %collective-permute-start.19 = (f32[128,128]{1,0:T(8,128)S(1)}, f32[128,128]{1,0:T(8,128)S(1)}, u32[]{:S(2)}, u32[]{:S(2)}) collective-permute-start(f32[128,128]{1,0:T(8,128)S(1)} %get-tuple-element.47), channel_id=1, source_target_pairs={{0,8},{4,12},{8,0},{12,4},{1,9},{5,13},{9,1},{13,5},{2,10},{6,14},... | collective-permute-start | bytes 196616 | tf_op jit(solution)/shard_map/ppermute | solution.py:536
  72.2 3.3 %collective-permute-done.19.right = f32[128,128]{1,0:T(8,128)S(1)} collective-permute-done((f32[128,128]{1,0:T(8,128)S(1)}, f32[128,128]{1,0:T(8,128)S(1)}, u32[]{:S(2)}, u32[]{:S(2)}) %collective-permute-start.19) | collective-permute-done | bytes 65568 | tf_op jit(solution)/shard_map/ppermute | solution.py:536
  75.5 1.6 %collective-permute-start.26 = (f32[8,96,128]{2,1,0:T(8,128)S(1)}, f32[8,96,128]{2,1,0:T(8,128)S(1)}, u32[]{:S(2)}, u32[]{:S(2)}) collective-permute-start(f32[8,96,128]{2,1,0:T(8,128)S(1)} %get-tuple-element.50.own.residual), channel_id=1, source_target_pairs={{0,16},{16,0},{1,17},{17,1},{2,18},{18,2},{3,19},{19,3},{4,20},{20... | collective-permute-start | bytes 1179656 | tf_op jit(solution)/shard_map/ppermute | solution.py:536
  77.7 1.6 %collective-permute-start.21 = (f32[128,128]{1,0:T(8,128)S(1)}, f32[128,128]{1,0:T(8,128)S(1)}, u32[]{:S(2)}, u32[]{:S(2)}) collective-permute-start(f32[128,128]{1,0:T(8,128)S(1)} %add.5.refs_0_), channel_id=1, source_target_pairs={{0,2},{1,3},{2,0},{3,1},{4,6},{5,7},{6,4},{7,5},{8,10},{9,11},{10,... | collective-permute-start | bytes 196616 | tf_op jit(solution)/shard_map/ppermute | solution.py:536
  79.2 2.3 %collective-permute-start.22 = (f32[128,128]{1,0:T(8,128)S(1)}, f32[128,128]{1,0:T(8,128)S(1)}, u32[]{:S(2)}, u32[]{:S(2)}) collective-permute-start(f32[128,128]{1,0:T(8,128)S(1)} %add.5.refs_0_), channel_id=1, source_target_pairs={{0,3},{1,2},{2,1},{3,0},{4,7},{5,6},{6,5},{7,4},{8,11},{9,10},{10,... | collective-permute-start | bytes 196616 | tf_op jit(solution)/shard_map/ppermute | solution.py:536
  81.5 2.8 %collective-permute-done.21.refs_2_ = f32[128,128]{1,0:T(8,128)S(1)} collective-permute-done((f32[128,128]{1,0:T(8,128)S(1)}, f32[128,128]{1,0:T(8,128)S(1)}, u32[]{:S(2)}, u32[]{:S(2)}) %collective-permute-start.21) | collective-permute-done | bytes 65568 | tf_op jit(solution)/shard_map/ppermute | solution.py:536
  84.2 1.1 %collective-permute-done.22.refs_3_ = f32[128,128]{1,0:T(8,128)S(1)} collective-permute-done((f32[128,128]{1,0:T(8,128)S(1)}, f32[128,128]{1,0:T(8,128)S(1)}, u32[]{:S(2)}, u32[]{:S(2)}) %collective-permute-start.22) | collective-permute-done | bytes 65568 | tf_op jit(solution)/shard_map/ppermute | solution.py:536
  85.4 1.6 %collective-permute-start.25 = (f32[128,128]{1,0:T(8,128)S(1)}, f32[128,128]{1,0:T(8,128)S(1)}, u32[]{:S(2)}, u32[]{:S(2)}) collective-permute-start(f32[128,128]{1,0:T(8,128)S(1)} %scale.3.refs_0_), channel_id=1, source_target_pairs={{0,8},{4,12},{8,0},{12,4},{1,9},{5,13},{9,1},{13,5},{2,10},{6,14},... | collective-permute-start | bytes 196616 | tf_op jit(solution)/shard_map/ppermute | solution.py:536
  87.5 1.5 %collective-permute-start.23 = (f32[128,128]{1,0:T(8,128)S(1)}, f32[128,128]{1,0:T(8,128)S(1)}, u32[]{:S(2)}, u32[]{:S(2)}) collective-permute-start(f32[128,128]{1,0:T(8,128)S(1)} %scale.3.refs_0_), channel_id=1, source_target_pairs={{0,24},{4,28},{8,16},{12,20},{16,8},{20,12},{24,0},{28,4},{1,25},{... | collective-permute-start | bytes 196616 | tf_op jit(solution)/shard_map/ppermute | solution.py:542
  89.0 1.0 %join.1 = f32[8,96,256]{2,1,0:T(8,128)} custom-call(f32[8,96,128]{2,1,0:T(8,128)S(1)} %get-tuple-element.50.own.residual, f32[8,96,128]{2,1,0:T(8,128)S(1)} %collective-permute-done.26.other.residual), custom_call_target="tpu_custom_call" | custom-call | flops 1000000 | bytes 2000000 | tf_op jit(solution)/shard_map/join/pallas_call | solution.py:485
  90.3 0.7 first_half.4.base
  91.4 0.7 second_half.3.own
  92.1 0.8 collective-permute-done.23.refs_1_
  92.9 0.7 first_half.5.other
  94.2 1.5 %final.1 = f32[8,96,256]{2,1,0:T(8,128)} custom-call(f32[8,96,128]{2,1,0:T(8,128)S(1)} %second_half.3.own, f32[8,96,128]{2,1,0:T(8,128)S(1)} %first_half.5.other, bf16[8,2,192,512]{3,2,1,0:T(8,128)(2,1)S(1)} %get-tuple-element.34.vectors, f32[128,128]{1,0:T(8,128)S(1)} %collective-permute-done.29.refs_0_, f32[128,128]{1,0:T(8,128)S(1)} %collective-permute-done.30.refs_1_), custom_call_target="tpu_custom_call" | custom-call | flops 1000000000 | bytes 4000000 | tf_op jit(solution)/shard_map/final/pallas_call | solution.py:513
  (43 shorter events, 5.6 us)
Async XLA Ops:
  0.6 1.1 %copy-start = (f32[1,1,2,4,96,256]{5,4,3,2,1,0:T(8,128)S(1)}, f32[1,1,2,4,96,256]{5,4,3,2,1,0:T(8,128)}, u32[]{:S(2)}) copy-start(f32[1,1,2,4,96,256]{5,4,3,2,1,0:T(8,128)} %param.7) | copy-start | bytes 2359300
  2.0 18.9 %collective-permute-start = (f32[8,96,128]{2,1,0:T(8,128)S(1)}, f32[8,96,128]{2,1,0:T(8,128)S(1)}, u32[]{:S(2)}, u32[]{:S(2)}) collective-permute-start(f32[8,96,128]{2,1,0:T(8,128)S(1)} %pack.1.x_ref.x), channel_id=1, source_target_pairs={{0,1},{1,2},{2,3},{3,0},{4,5},{5,6},{6,7},{7,4},{8,9},{9,10},{10,1... | collective-permute-start | bytes 1179656 | tf_op jit(solution)/shard_map/ppermute | solution.py:531
  5.1 16.3 %collective-permute-start.1 = (f32[8,96,128]{2,1,0:T(8,128)S(1)}, f32[8,96,128]{2,1,0:T(8,128)S(1)}, u32[]{:S(2)}, u32[]{:S(2)}) collective-permute-start(f32[8,96,128]{2,1,0:T(8,128)S(1)} %pack.1.x_ref.x), channel_id=1, source_target_pairs={{0,4},{4,0},{8,12},{12,8},{1,5},{5,1},{9,13},{13,9},{2,6},{6,2},{1... | collective-permute-start | bytes 1179656 | tf_op jit(solution)/shard_map/ppermute | solution.py:536
  5.1 16.3 %collective-permute-start.2 = (f32[8,96,128]{2,1,0:T(8,128)S(1)}, f32[8,96,128]{2,1,0:T(8,128)S(1)}, u32[]{:S(2)}, u32[]{:S(2)}) collective-permute-start(f32[8,96,128]{2,1,0:T(8,128)S(1)} %pack.1.x_ref.x), channel_id=1, source_target_pairs={{0,12},{4,8},{8,4},{12,0},{1,13},{5,9},{9,5},{13,1},{2,14},{6,10},... | collective-permute-start | bytes 1179656 | tf_op jit(solution)/shard_map/ppermute | solution.py:548
  6.7 18.0 %collective-permute-start.3 = (f32[8,96,128]{2,1,0:T(8,128)S(1)}, f32[8,96,128]{2,1,0:T(8,128)S(1)}, u32[]{:S(2)}, u32[]{:S(2)}) collective-permute-start(f32[8,96,128]{2,1,0:T(8,128)S(1)} %pack.1.x_ref.x), channel_id=1, source_target_pairs={{0,3},{1,0},{2,1},{3,2},{4,7},{5,4},{6,5},{7,6},{8,11},{9,8},{10,9... | collective-permute-start | bytes 1179656 | tf_op jit(solution)/shard_map/ppermute | solution.py:531
  24.7 7.3 %copy-start.1 = (f32[2,512]{1,0:T(2,128)S(1)}, f32[2,512]{1,0:T(2,128)}, u32[]{:S(2)}) copy-start(f32[2,512]{1,0:T(2,128)} %inverse.1) | copy-start | bytes 12292
  26.1 1.4 %collective-permute-start.4 = (f32[256,128]{1,0:T(8,128)S(1)}, f32[256,128]{1,0:T(8,128)S(1)}, u32[]{:S(2)}, u32[]{:S(2)}) collective-permute-start(f32[256,128]{1,0:T(8,128)S(1)} %get-tuple-element.36), channel_id=1, source_target_pairs={{0,4},{4,0},{8,12},{12,8},{1,5},{5,1},{9,13},{13,9},{2,6},{6,2},{1... | collective-permute-start | bytes 393224 | tf_op jit(solution)/shard_map/ppermute | solution.py:536
  27.5 4.6 %collective-permute-start.5 = (f32[128,128]{1,0:T(8,128)S(1)}, f32[128,128]{1,0:T(8,128)S(1)}, u32[]{:S(2)}, u32[]{:S(2)}) collective-permute-start(f32[128,128]{1,0:T(8,128)S(1)} %get-tuple-element.38), channel_id=1, source_target_pairs={{0,8},{4,12},{8,0},{12,4},{1,9},{5,13},{9,1},{13,5},{2,10},{6,14},... | collective-permute-start | bytes 196616 | tf_op jit(solution)/shard_map/ppermute | solution.py:536
  29.1 7.3 %collective-permute-start.6 = (f32[128,128]{1,0:T(8,128)S(1)}, f32[128,128]{1,0:T(8,128)S(1)}, u32[]{:S(2)}, u32[]{:S(2)}) collective-permute-start(f32[128,128]{1,0:T(8,128)S(1)} %get-tuple-element.37.refs_0_), channel_id=1, source_target_pairs={{0,2},{1,3},{2,0},{3,1},{4,6},{5,7},{6,4},{7,5},{8,10},{9,11},{10,... | collective-permute-start | bytes 196616 | tf_op jit(solution)/shard_map/ppermute | solution.py:536
  31.0 6.4 %collective-permute-start.7 = (f32[128,128]{1,0:T(8,128)S(1)}, f32[128,128]{1,0:T(8,128)S(1)}, u32[]{:S(2)}, u32[]{:S(2)}) collective-permute-start(f32[128,128]{1,0:T(8,128)S(1)} %get-tuple-element.38), channel_id=1, source_target_pairs={{0,10},{1,11},{2,8},{3,9},{4,14},{5,15},{6,12},{7,13},{8,2},{9,3},... | collective-permute-start | bytes 196616 | tf_op jit(solution)/shard_map/ppermute | solution.py:542
  37.5 5.4 %collective-permute-start.10 = (f32[128,128]{1,0:T(8,128)S(1)}, f32[128,128]{1,0:T(8,128)S(1)}, u32[]{:S(2)}, u32[]{:S(2)}) collective-permute-start(f32[128,128]{1,0:T(8,128)S(1)} %scale.2.left), channel_id=1, source_target_pairs={{0,9},{1,8},{2,11},{3,10},{4,13},{5,12},{6,15},{7,14},{8,1},{9,0},... | collective-permute-start | bytes 196616 | tf_op jit(solution)/shard_map/ppermute | solution.py:542
  38.8 4.6 %collective-permute-start.9 = (f32[128,128]{1,0:T(8,128)S(1)}, f32[128,128]{1,0:T(8,128)S(1)}, u32[]{:S(2)}, u32[]{:S(2)}) collective-permute-start(f32[128,128]{1,0:T(8,128)S(1)} %scale.2.left), channel_id=1, source_target_pairs={{0,8},{4,12},{8,0},{12,4},{1,9},{5,13},{9,1},{13,5},{2,10},{6,14},... | collective-permute-start | bytes 196616 | tf_op jit(solution)/shard_map/ppermute | solution.py:536
  40.3 4.3 %collective-permute-start.8 = (f32[128,128]{1,0:T(8,128)S(1)}, f32[128,128]{1,0:T(8,128)S(1)}, u32[]{:S(2)}, u32[]{:S(2)}) collective-permute-start(f32[128,128]{1,0:T(8,128)S(1)} %scale.2.left), channel_id=1, source_target_pairs={{0,1},{1,0},{2,3},{3,2},{4,5},{5,4},{6,7},{7,6},{8,9},{9,8},{10,11... | collective-permute-start | bytes 196616 | tf_op jit(solution)/shard_map/ppermute | solution.py:536
  43.4 1.9 %collective-permute-start.12 = (f32[128,128]{1,0:T(8,128)S(1)}, f32[128,128]{1,0:T(8,128)S(1)}, u32[]{:S(2)}, u32[]{:S(2)}) collective-permute-start(f32[128,128]{1,0:T(8,128)S(1)} %add.4.refs_1_), channel_id=1, source_target_pairs={{0,4},{4,0},{8,12},{12,8},{1,5},{5,1},{9,13},{13,9},{2,6},{6,2},{1... | collective-permute-start | bytes 196616 | tf_op jit(solution)/shard_map/ppermute | solution.py:536
  44.5 1.3 %collective-permute-start.11 = (f32[128,128]{1,0:T(8,128)S(1)}, f32[128,128]{1,0:T(8,128)S(1)}, u32[]{:S(2)}, u32[]{:S(2)}) collective-permute-start(f32[128,128]{1,0:T(8,128)S(1)} %add.3.refs_0_), channel_id=1, source_target_pairs={{0,4},{4,0},{8,12},{12,8},{1,5},{5,1},{9,13},{13,9},{2,6},{6,2},{1... | collective-permute-start | bytes 196616 | tf_op jit(solution)/shard_map/ppermute | solution.py:536
  46.5 4.7 %collective-permute-start.14 = (f32[8,96,128]{2,1,0:T(8,128)S(1)}, f32[8,96,128]{2,1,0:T(8,128)S(1)}, u32[]{:S(2)}, u32[]{:S(2)}) collective-permute-start(f32[8,96,128]{2,1,0:T(8,128)S(1)} %second_half.2.x_ref.x), channel_id=1, source_target_pairs={{0,4},{4,0},{8,12},{12,8},{1,5},{5,1},{9,13},{13,9},{2,6},{6,2},{1... | collective-permute-start | bytes 1179656 | tf_op jit(solution)/shard_map/ppermute | solution.py:536
  46.7 13.8 %collective-permute-start.13 = (f32[8,96,128]{2,1,0:T(8,128)S(1)}, f32[8,96,128]{2,1,0:T(8,128)S(1)}, u32[]{:S(2)}, u32[]{:S(2)}) collective-permute-start(f32[8,96,128]{2,1,0:T(8,128)S(1)} %second_half.2.x_ref.x), channel_id=1, source_target_pairs={{0,1},{1,2},{2,3},{3,0},{4,5},{5,6},{6,7},{7,4},{8,9},{9,10},{10,1... | collective-permute-start | bytes 1179656 | tf_op jit(solution)/shard_map/ppermute | solution.py:531
  48.1 12.9 %collective-permute-start.15 = (f32[8,96,128]{2,1,0:T(8,128)S(1)}, f32[8,96,128]{2,1,0:T(8,128)S(1)}, u32[]{:S(2)}, u32[]{:S(2)}) collective-permute-start(f32[8,96,128]{2,1,0:T(8,128)S(1)} %second_half.2.x_ref.x), channel_id=1, source_target_pairs={{0,12},{4,8},{8,4},{12,0},{1,13},{5,9},{9,5},{13,1},{2,14},{6,10},... | collective-permute-start | bytes 1179656 | tf_op jit(solution)/shard_map/ppermute | solution.py:548
  49.3 19.0 %collective-permute-start.17 = (f32[8,96,128]{2,1,0:T(8,128)S(1)}, f32[8,96,128]{2,1,0:T(8,128)S(1)}, u32[]{:S(2)}, u32[]{:S(2)}) collective-permute-start(f32[8,96,128]{2,1,0:T(8,128)S(1)} %second_half.2.x_ref.x), channel_id=1, source_target_pairs={{0,3},{1,0},{2,1},{3,2},{4,7},{5,4},{6,5},{7,6},{8,11},{9,8},{10,9... | collective-permute-start | bytes 1179656 | tf_op jit(solution)/shard_map/ppermute | solution.py:531
  51.2 11.4 %collective-permute-start.16 = (f32[8,96,128]{2,1,0:T(8,128)S(1)}, f32[8,96,128]{2,1,0:T(8,128)S(1)}, u32[]{:S(2)}, u32[]{:S(2)}) collective-permute-start(f32[8,96,128]{2,1,0:T(8,128)S(1)} %second_half.2.x_ref.x), channel_id=1, source_target_pairs={{0,16},{16,0},{1,17},{17,1},{2,18},{18,2},{3,19},{19,3},{4,20},{20... | collective-permute-start | bytes 1179656 | tf_op jit(solution)/shard_map/ppermute | solution.py:536
  69.7 1.4 %collective-permute-start.18 = (f32[256,128]{1,0:T(8,128)S(1)}, f32[256,128]{1,0:T(8,128)S(1)}, u32[]{:S(2)}, u32[]{:S(2)}) collective-permute-start(f32[256,128]{1,0:T(8,128)S(1)} %get-tuple-element.45), channel_id=1, source_target_pairs={{0,4},{4,0},{8,12},{12,8},{1,5},{5,1},{9,13},{13,9},{2,6},{6,2},{1... | collective-permute-start | bytes 393224 | tf_op jit(solution)/shard_map/ppermute | solution.py:536
  71.2 4.3 %collective-permute-start.19 = (f32[128,128]{1,0:T(8,128)S(1)}, f32[128,128]{1,0:T(8,128)S(1)}, u32[]{:S(2)}, u32[]{:S(2)}) collective-permute-start(f32[128,128]{1,0:T(8,128)S(1)} %get-tuple-element.47), channel_id=1, source_target_pairs={{0,8},{4,12},{8,0},{12,4},{1,9},{5,13},{9,1},{13,5},{2,10},{6,14},... | collective-permute-start | bytes 196616 | tf_op jit(solution)/shard_map/ppermute | solution.py:536
  75.5 13.5 %collective-permute-start.26 = (f32[8,96,128]{2,1,0:T(8,128)S(1)}, f32[8,96,128]{2,1,0:T(8,128)S(1)}, u32[]{:S(2)}, u32[]{:S(2)}) collective-permute-start(f32[8,96,128]{2,1,0:T(8,128)S(1)} %get-tuple-element.50.own.residual), channel_id=1, source_target_pairs={{0,16},{16,0},{1,17},{17,1},{2,18},{18,2},{3,19},{19,3},{4,20},{20... | collective-permute-start | bytes 1179656 | tf_op jit(solution)/shard_map/ppermute | solution.py:536
  77.1 4.4 %collective-permute-start.20 = (f32[128,128]{1,0:T(8,128)S(1)}, f32[128,128]{1,0:T(8,128)S(1)}, u32[]{:S(2)}, u32[]{:S(2)}) collective-permute-start(f32[128,128]{1,0:T(8,128)S(1)} %add.5.refs_0_), channel_id=1, source_target_pairs={{0,1},{1,0},{2,3},{3,2},{4,5},{5,4},{6,7},{7,6},{8,9},{9,8},{10,11... | collective-permute-start | bytes 196616 | tf_op jit(solution)/shard_map/ppermute | solution.py:536
  77.7 6.6 %collective-permute-start.21 = (f32[128,128]{1,0:T(8,128)S(1)}, f32[128,128]{1,0:T(8,128)S(1)}, u32[]{:S(2)}, u32[]{:S(2)}) collective-permute-start(f32[128,128]{1,0:T(8,128)S(1)} %add.5.refs_0_), channel_id=1, source_target_pairs={{0,2},{1,3},{2,0},{3,1},{4,6},{5,7},{6,4},{7,5},{8,10},{9,11},{10,... | collective-permute-start | bytes 196616 | tf_op jit(solution)/shard_map/ppermute | solution.py:536
  79.2 6.1 %collective-permute-start.22 = (f32[128,128]{1,0:T(8,128)S(1)}, f32[128,128]{1,0:T(8,128)S(1)}, u32[]{:S(2)}, u32[]{:S(2)}) collective-permute-start(f32[128,128]{1,0:T(8,128)S(1)} %add.5.refs_0_), channel_id=1, source_target_pairs={{0,3},{1,2},{2,1},{3,0},{4,7},{5,6},{6,5},{7,4},{8,11},{9,10},{10,... | collective-permute-start | bytes 196616 | tf_op jit(solution)/shard_map/ppermute | solution.py:536
  85.4 4.6 %collective-permute-start.25 = (f32[128,128]{1,0:T(8,128)S(1)}, f32[128,128]{1,0:T(8,128)S(1)}, u32[]{:S(2)}, u32[]{:S(2)}) collective-permute-start(f32[128,128]{1,0:T(8,128)S(1)} %scale.3.refs_0_), channel_id=1, source_target_pairs={{0,8},{4,12},{8,0},{12,4},{1,9},{5,13},{9,1},{13,5},{2,10},{6,14},... | collective-permute-start | bytes 196616 | tf_op jit(solution)/shard_map/ppermute | solution.py:536
  87.0 4.3 %collective-permute-start.24 = (f32[128,128]{1,0:T(8,128)S(1)}, f32[128,128]{1,0:T(8,128)S(1)}, u32[]{:S(2)}, u32[]{:S(2)}) collective-permute-start(f32[128,128]{1,0:T(8,128)S(1)} %scale.3.refs_0_), channel_id=1, source_target_pairs={{0,16},{16,0},{1,17},{17,1},{2,18},{18,2},{3,19},{19,3},{4,20},{20... | collective-permute-start | bytes 196616 | tf_op jit(solution)/shard_map/ppermute | solution.py:536
  87.5 3.9 %collective-permute-start.27 = (f32[128,128]{1,0:T(8,128)S(1)}, f32[128,128]{1,0:T(8,128)S(1)}, u32[]{:S(2)}, u32[]{:S(2)}) collective-permute-start(f32[128,128]{1,0:T(8,128)S(1)} %scale.3.refs_0_), channel_id=1, source_target_pairs={{0,4},{4,0},{8,12},{12,8},{1,5},{5,1},{9,13},{13,9},{2,6},{6,2},{1... | collective-permute-start | bytes 196616 | tf_op jit(solution)/shard_map/ppermute | solution.py:536
  87.5 5.4 %collective-permute-start.23 = (f32[128,128]{1,0:T(8,128)S(1)}, f32[128,128]{1,0:T(8,128)S(1)}, u32[]{:S(2)}, u32[]{:S(2)}) collective-permute-start(f32[128,128]{1,0:T(8,128)S(1)} %scale.3.refs_0_), channel_id=1, source_target_pairs={{0,24},{4,28},{8,16},{12,20},{16,8},{20,12},{24,0},{28,4},{1,25},{... | collective-permute-start | bytes 196616 | tf_op jit(solution)/shard_map/ppermute | solution.py:542
  90.0 1.3 %collective-permute-start.28 = (f32[128,128]{1,0:T(8,128)S(1)}, f32[128,128]{1,0:T(8,128)S(1)}, u32[]{:S(2)}, u32[]{:S(2)}) collective-permute-start(f32[128,128]{1,0:T(8,128)S(1)} %collective-permute-done.25.refs_1_), channel_id=1, source_target_pairs={{0,4},{4,0},{8,12},{12,8},{1,5},{5,1},{9,13},{13,9},{2,6},{6,2},{1... | collective-permute-start | bytes 196616 | tf_op jit(solution)/shard_map/ppermute | solution.py:536
  91.3 2.3 %collective-permute-start.29 = (f32[128,128]{1,0:T(8,128)S(1)}, f32[128,128]{1,0:T(8,128)S(1)}, u32[]{:S(2)}, u32[]{:S(2)}) collective-permute-start(f32[128,128]{1,0:T(8,128)S(1)} %collective-permute-done.24.refs_0_), channel_id=1, source_target_pairs={{0,4},{4,0},{8,12},{12,8},{1,5},{5,1},{9,13},{13,9},{2,6},{6,2},{1... | collective-permute-start | bytes 196616 | tf_op jit(solution)/shard_map/ppermute | solution.py:536
  92.9 1.3 %collective-permute-start.30 = (f32[128,128]{1,0:T(8,128)S(1)}, f32[128,128]{1,0:T(8,128)S(1)}, u32[]{:S(2)}, u32[]{:S(2)}) collective-permute-start(f32[128,128]{1,0:T(8,128)S(1)} %collective-permute-done.23.refs_1_), channel_id=1, source_target_pairs={{0,4},{4,0},{8,12},{12,8},{1,5},{5,1},{9,13},{13,9},{2,6},{6,2},{1... | collective-permute-start | bytes 196616 | tf_op jit(solution)/shard_map/ppermute | solution.py:536

commit v9 on v8

--- a/solution.py
+++ b/solution.py
@@ -544,9 +544,10 @@
 
 def faces_of(x):
     count = lax.axis_size("space")
-    near = crossed(x, "space", 1)
+    backward_t, forward_t = shifted(x, "tm", 1), shifted(x, "tm", -1)
+    near, x = lax.optimization_barrier((crossed(x, "space", 1), x))
     far = lax.ppermute(x, "space", [(i, (i + 1 if i % 2 else i - 1) % count) for i in range(count)])
-    return near, far, shifted(x, "tm", -1), shifted(x, "tm", 1)
+    return near, far, forward_t, backward_t
 
 
 def halving(keep, send):
@@ -612,8 +613,8 @@
         if last:
             near, x = lax.optimization_barrier((near, x))
             other_x = crossed(x, "groups", 1)
+        rest = z_faces(rest, near, far, halo)
         rest = backward_face(rest, backward_t, halo)
-        rest = z_faces(rest, near, far, halo)
         if last:
             rest, other_x = lax.optimization_barrier((rest, other_x))
         residual, keep, send = forward_face(rest, forward_t, halo, by_rows)

time: 96.2 us -> 96.2 us (level)
    ppermute x2, waiting for transfers between devices: 0.01 us -> 6.55 us  [faces_of(): lax.ppermute(x, 'space', [(i, (i + 1 if i % 2 else i - 1) % count) for i...]
    ppermute x4, waiting for transfers between devices: 13.2 us -> 7.89 us  [shifted(): lax.ppermute(value, axis, [(i, (i + step) % count) for i in range(count)])]
    ppermute x2, starting transfers between devices: 2.86 us -> 1.51 us  [faces_of(): lax.ppermute(x, 'space', [(i, (i + 1 if i % 2 else i - 1) % count) for i...]
    ppermute x22, starting transfers between devices: 17.3 us -> 18.4 us  [crossed(): return lax.ppermute(value, axis, [(i, i ^ mask) for i in range(count)])]
  transfers between devices with their start and end apart: 31 -> 31, of which waited for: 18 -> 16; matrix products, arithmetic and copies ran while one was open for 0% -> 0% of each run, Pallas kernels for 22% -> 22%
where the time goes in v9:
time: 96.2 us; the launch traced here: 95.9 us
  waiting for transfers between devices  35.1 us (36%)
  starting transfers between devices  32.2 us (33%)
  Pallas kernels  26.4 us (27%)
  local copies, waits for them, and re-layouts  1.13 us (1%)
  between operations  1.07 us (1%)
    ppermute x22, starting transfers between devices, crossed(): return lax.ppermute(value, axis, [(i, i ^ mask) for i in range(count)])  18.4 us
    ppermute x22, waiting for transfers between devices, crossed(): return lax.ppermute(value, axis, [(i, i ^ mask) for i in range(count)])  17.8 us
    ppermute x4, starting transfers between devices, shifted(): lax.ppermute(value, axis, [(i, (i + step) % count) for i in range(count)])  8.57 us
    ppermute x4, waiting for transfers between devices, shifted(): lax.ppermute(value, axis, [(i, (i + step) % count) for i in range(count)])  7.89 us
    pallas_call x1, Pallas kernels, first_local(): pl.pallas_call(functools.partial(first_kernel, ny, nx), grid=(sites,), ou...  7.69 us
    ppermute x2, waiting for transfers between devices, faces_of(): lax.ppermute(x, 'space', [(i, (i + 1 if i % 2 else i - 1) % count) for i...  6.55 us
    pallas_call x1, Pallas kernels, vectors_parts(): pl.pallas_call(vectors_kernel, grid=(sites // step,), out_shape=(pltpu.VM...  4.24 us
    ppermute x3, starting transfers between devices, crossed_both(): return lax.ppermute(value, (first, second), pairs)  3.71 us
  transfers between devices with their start and end apart: 31, of which 16 were waited for; matrix products, arithmetic and copies ran while one was open for 0% of the time, Pallas kernels for 22%

profile of v9, /device:TPU:0, one launch (start us, length us, event | category | flops | bytes accessed | tf_op | source)
XLA Modules:
  0.0 95.9 jit_solution(13204819684960504772)
XLA Ops:
  0.6 1.1 %copy-done = f32[1,1,2,4,96,256]{5,4,3,2,1,0:T(8,128)S(1)} copy-done((f32[1,1,2,4,96,256]{5,4,3,2,1,0:T(8,128)S(1)}, f32[1,1,2,4,96,256]{5,4,3,2,1,0:T(8,128)}, u32[]{:S(2)}) %copy-start) | copy-done | bytes 786456
  2.6 2.6 %collective-permute-start.2 = (f32[8,96,128]{2,1,0:T(8,128)S(1)}, f32[8,96,128]{2,1,0:T(8,128)S(1)}, u32[]{:S(2)}, u32[]{:S(2)}) collective-permute-start(f32[8,96,128]{2,1,0:T(8,128)S(1)} %pack.1.x_ref.x), channel_id=1, source_target_pairs={{0,1},{1,2},{2,3},{3,0},{4,5},{5,6},{6,7},{7,4},{8,9},{9,10},{10,1... | collective-permute-start | bytes 1179656 | tf_op jit(solution)/shard_map/ppermute | solution.py:531
  5.2 2.1 %collective-permute-start.3 = (f32[8,96,128]{2,1,0:T(8,128)S(1)}, f32[8,96,128]{2,1,0:T(8,128)S(1)}, u32[]{:S(2)}, u32[]{:S(2)}) collective-permute-start(f32[8,96,128]{2,1,0:T(8,128)S(1)} %pack.1.x_ref.x), channel_id=1, source_target_pairs={{0,3},{1,0},{2,1},{3,2},{4,7},{5,4},{6,5},{7,6},{8,11},{9,8},{10,9... | collective-permute-start | bytes 1179656 | tf_op jit(solution)/shard_map/ppermute | solution.py:531
  7.3 1.2 %collective-permute-start.1 = (f32[8,96,128]{2,1,0:T(8,128)S(1)}, f32[8,96,128]{2,1,0:T(8,128)S(1)}, u32[]{:S(2)}, u32[]{:S(2)}) collective-permute-start(f32[8,96,128]{2,1,0:T(8,128)S(1)} %pack.1.x_ref.x), channel_id=1, source_target_pairs={{0,12},{4,8},{8,4},{12,0},{1,13},{5,9},{9,5},{13,1},{2,14},{6,10},... | collective-permute-start | bytes 1179656 | tf_op jit(solution)/shard_map/ppermute | solution.py:549
  8.5 7.7 %first_local.1 = (f32[8,96,128]{2,1,0:T(8,128)S(1)}, f32[8,96,128]{2,1,0:T(8,128)S(1)}, bf16[5,8,192,192]{3,2,1,0:T(8,128)(2,1)S(1)}, bf16[4,8,192,192]{3,2,1,0:T(8,128)(2,1)S(1)}) custom-call(f32[8,96,128]{2,1,0:T(8,128)S(1)} %pack.1.x_ref.x, f32[8,96,256]{2,1,0:T(8,128)} %bitcast.13, f32[9,8,96,192]{3,2,1,0:T(8,128)} %bitcast.12), custom_call_target="tpu_custom_call" | custom-call | flops 8000000000 | bytes 16000000 | tf_op jit(solution)/shard_map/first_local/pallas_call | solution.py:142
  16.2 4.2 %vectors_parts.1 = (bf16[1024,1536]{1,0:T(8,128)(2,1)S(1)}, bf16[8,2,192,512]{3,2,1,0:T(8,128)(2,1)S(1)}) custom-call(f32[1536,512]{1,0:T(8,128)} %bitcast.9), custom_call_target="tpu_custom_call" | custom-call | flops 1000000 | bytes 9000000 | tf_op jit(solution)/shard_map/vectors_parts/pallas_call | solution.py:235
  20.4 0.7 z_faces.2.rest
  21.6 3.2 %collective-permute-done.3.forward = f32[8,96,128]{2,1,0:T(8,128)S(1)} collective-permute-done((f32[8,96,128]{2,1,0:T(8,128)S(1)}, f32[8,96,128]{2,1,0:T(8,128)S(1)}, u32[]{:S(2)}, u32[]{:S(2)}) %collective-permute-start.3) | collective-permute-done | bytes 393248 | tf_op jit(solution)/shard_map/ppermute | solution.py:531
  24.8 1.4 %forward_face.2 = (f32[8,96,128]{2,1,0:T(8,128)S(1)}, f32[256,128]{1,0:T(8,128)S(1)}, f32[256,128]{1,0:T(8,128)S(1)}) custom-call(f32[8,96,128]{2,1,0:T(8,128)S(1)} %backward_face.2.rest, f32[8,96,128]{2,1,0:T(8,128)S(1)} %collective-permute-done.3.forward, bf16[4,8,192,192]{3,2,1,0:T(8,128)(2,1)S(1)} %get-tuple-element.37.matrix, ...), custom_call_target="tpu_custom_call" | custom-call | flops 2000000000 | bytes 8000000 | tf_op jit(solution)/shard_map/forward_face/pallas_call | solution.py:340
  26.3 1.3 %collective-permute-done.4.received = f32[256,128]{1,0:T(8,128)S(1)} collective-permute-done((f32[256,128]{1,0:T(8,128)S(1)}, f32[256,128]{1,0:T(8,128)S(1)}, u32[]{:S(2)}, u32[]{:S(2)}) %collective-permute-start.4) | collective-permute-done | bytes 131104 | tf_op jit(solution)/shard_map/ppermute | solution.py:536
  27.6 1.6 %collective-permute-start.5 = (f32[128,128]{1,0:T(8,128)S(1)}, f32[128,128]{1,0:T(8,128)S(1)}, u32[]{:S(2)}, u32[]{:S(2)}) collective-permute-start(f32[128,128]{1,0:T(8,128)S(1)} %get-tuple-element.44), channel_id=1, source_target_pairs={{0,8},{4,12},{8,0},{12,4},{1,9},{5,13},{9,1},{13,5},{2,10},{6,14},... | collective-permute-start | bytes 196616 | tf_op jit(solution)/shard_map/ppermute | solution.py:536
  29.2 1.8 %collective-permute-start.6 = (f32[128,128]{1,0:T(8,128)S(1)}, f32[128,128]{1,0:T(8,128)S(1)}, u32[]{:S(2)}, u32[]{:S(2)}) collective-permute-start(f32[128,128]{1,0:T(8,128)S(1)} %get-tuple-element.43.refs_0_), channel_id=1, source_target_pairs={{0,2},{1,3},{2,0},{3,1},{4,6},{5,7},{6,4},{7,5},{8,10},{9,11},{10,... | collective-permute-start | bytes 196616 | tf_op jit(solution)/shard_map/ppermute | solution.py:536
  31.0 1.1 %collective-permute-start.7 = (f32[128,128]{1,0:T(8,128)S(1)}, f32[128,128]{1,0:T(8,128)S(1)}, u32[]{:S(2)}, u32[]{:S(2)}) collective-permute-start(f32[128,128]{1,0:T(8,128)S(1)} %get-tuple-element.44), channel_id=1, source_target_pairs={{0,10},{1,11},{2,8},{3,9},{4,14},{5,15},{6,12},{7,13},{8,2},{9,3},... | collective-permute-start | bytes 196616 | tf_op jit(solution)/shard_map/ppermute | solution.py:542
  32.2 5.2 %collective-permute-done.6.refs_2_ = f32[128,128]{1,0:T(8,128)S(1)} collective-permute-done((f32[128,128]{1,0:T(8,128)S(1)}, f32[128,128]{1,0:T(8,128)S(1)}, u32[]{:S(2)}, u32[]{:S(2)}) %collective-permute-start.6) | collective-permute-done | bytes 65568 | tf_op jit(solution)/shard_map/ppermute | solution.py:536
  37.6 1.3 %collective-permute-start.10 = (f32[128,128]{1,0:T(8,128)S(1)}, f32[128,128]{1,0:T(8,128)S(1)}, u32[]{:S(2)}, u32[]{:S(2)}) collective-permute-start(f32[128,128]{1,0:T(8,128)S(1)} %scale.2.left), channel_id=1, source_target_pairs={{0,9},{1,8},{2,11},{3,10},{4,13},{5,12},{6,15},{7,14},{8,1},{9,0},... | collective-permute-start | bytes 196616 | tf_op jit(solution)/shard_map/ppermute | solution.py:542
  38.8 1.5 %collective-permute-start.9 = (f32[128,128]{1,0:T(8,128)S(1)}, f32[128,128]{1,0:T(8,128)S(1)}, u32[]{:S(2)}, u32[]{:S(2)}) collective-permute-start(f32[128,128]{1,0:T(8,128)S(1)} %scale.2.left), channel_id=1, source_target_pairs={{0,8},{4,12},{8,0},{12,4},{1,9},{5,13},{9,1},{13,5},{2,10},{6,14},... | collective-permute-start | bytes 196616 | tf_op jit(solution)/shard_map/ppermute | solution.py:536
  40.3 0.9 collective-permute-start.8
  41.3 1.9 %collective-permute-done.10.right = f32[128,128]{1,0:T(8,128)S(1)} collective-permute-done((f32[128,128]{1,0:T(8,128)S(1)}, f32[128,128]{1,0:T(8,128)S(1)}, u32[]{:S(2)}, u32[]{:S(2)}) %collective-permute-start.10) | collective-permute-done | bytes 65568 | tf_op jit(solution)/shard_map/ppermute | solution.py:542
  43.6 1.0 %collective-permute-done.8.right = f32[128,128]{1,0:T(8,128)S(1)} collective-permute-done((f32[128,128]{1,0:T(8,128)S(1)}, f32[128,128]{1,0:T(8,128)S(1)}, u32[]{:S(2)}, u32[]{:S(2)}) %collective-permute-start.8) | collective-permute-done | bytes 65568 | tf_op jit(solution)/shard_map/ppermute | solution.py:536
  44.7 0.7 first_half.3.base
  45.4 0.6 collective-permute-done.11.refs_0_
  45.9 0.7 second_half.2.x_ref.x
  46.8 1.4 %collective-permute-start.15 = (f32[8,96,128]{2,1,0:T(8,128)S(1)}, f32[8,96,128]{2,1,0:T(8,128)S(1)}, u32[]{:S(2)}, u32[]{:S(2)}) collective-permute-start(f32[8,96,128]{2,1,0:T(8,128)S(1)} %second_half.2.x_ref.x), channel_id=1, source_target_pairs={{0,1},{1,2},{2,3},{3,0},{4,5},{5,6},{6,7},{7,4},{8,9},{9,10},{10,1... | collective-permute-start | bytes 1179656 | tf_op jit(solution)/shard_map/ppermute | solution.py:531
  48.2 2.5 %collective-permute-start.17 = (f32[8,96,128]{2,1,0:T(8,128)S(1)}, f32[8,96,128]{2,1,0:T(8,128)S(1)}, u32[]{:S(2)}, u32[]{:S(2)}) collective-permute-start(f32[8,96,128]{2,1,0:T(8,128)S(1)} %second_half.2.x_ref.x), channel_id=1, source_target_pairs={{0,3},{1,0},{2,1},{3,2},{4,7},{5,4},{6,5},{7,6},{8,11},{9,8},{10,9... | collective-permute-start | bytes 1179656 | tf_op jit(solution)/shard_map/ppermute | solution.py:531
  51.0 1.5 %collective-permute-start.16 = (f32[8,96,128]{2,1,0:T(8,128)S(1)}, f32[8,96,128]{2,1,0:T(8,128)S(1)}, u32[]{:S(2)}, u32[]{:S(2)}) collective-permute-start(f32[8,96,128]{2,1,0:T(8,128)S(1)} %second_half.2.x_ref.x), channel_id=1, source_target_pairs={{0,16},{16,0},{1,17},{17,1},{2,18},{18,2},{3,19},{19,3},{4,20},{20... | collective-permute-start | bytes 1179656 | tf_op jit(solution)/shard_map/ppermute | solution.py:536
  52.5 3.0 %local_part.1.rest = f32[8,96,128]{2,1,0:T(8,128)S(1)} custom-call(f32[8,96,128]{2,1,0:T(8,128)S(1)} %second_half.2.x_ref.x, f32[8,96,128]{2,1,0:T(8,128)S(1)} %get-tuple-element.45.source, bf16[5,8,192,192]{3,2,1,0:T(8,128)(2,1)S(1)} %get-tuple-element.46.local), custom_call_target="tpu_custom_call" | custom-call | flops 8000000000 | bytes 8000000 | tf_op jit(solution)/shard_map/local_part/pallas_call | solution.py:177
  55.5 6.5 %collective-permute-done.14.far = f32[8,96,128]{2,1,0:T(8,128)S(1)} collective-permute-done((f32[8,96,128]{2,1,0:T(8,128)S(1)}, f32[8,96,128]{2,1,0:T(8,128)S(1)}, u32[]{:S(2)}, u32[]{:S(2)}) %collective-permute-start.14) | collective-permute-done | bytes 393248 | tf_op jit(solution)/shard_map/ppermute | solution.py:549
  62.0 0.7 z_faces.3.rest
  63.2 4.7 %collective-permute-done.17.forward = f32[8,96,128]{2,1,0:T(8,128)S(1)} collective-permute-done((f32[8,96,128]{2,1,0:T(8,128)S(1)}, f32[8,96,128]{2,1,0:T(8,128)S(1)}, u32[]{:S(2)}, u32[]{:S(2)}) %collective-permute-start.17) | collective-permute-done | bytes 393248 | tf_op jit(solution)/shard_map/ppermute | solution.py:531
  67.8 1.4 %forward_face.3 = (f32[8,96,128]{2,1,0:T(8,128)S(1)}, f32[256,128]{1,0:T(8,128)S(1)}, f32[256,128]{1,0:T(8,128)S(1)}) custom-call(f32[8,96,128]{2,1,0:T(8,128)S(1)} %backward_face.3.rest, f32[8,96,128]{2,1,0:T(8,128)S(1)} %collective-permute-done.17.forward, bf16[4,8,192,192]{3,2,1,0:T(8,128)(2,1)S(1)} %get-tuple-element.37.matrix, ...), custom_call_target="tpu_custom_call" | custom-call | flops 2000000000 | bytes 8000000 | tf_op jit(solution)/shard_map/forward_face/pallas_call | solution.py:340
  69.3 1.3 %collective-permute-done.18.received = f32[256,128]{1,0:T(8,128)S(1)} collective-permute-done((f32[256,128]{1,0:T(8,128)S(1)}, f32[256,128]{1,0:T(8,128)S(1)}, u32[]{:S(2)}, u32[]{:S(2)}) %collective-permute-start.18) | collective-permute-done | bytes 131104 | tf_op jit(solution)/shard_map/ppermute | solution.py:536
  70.7 1.5 %collective-permute-start.19 = (f32[128,128]{1,0:T(8,128)S(1)}, f32[128,128]{1,0:T(8,128)S(1)}, u32[]{:S(2)}, u32[]{:S(2)}) collective-permute-start(f32[128,128]{1,0:T(8,128)S(1)} %get-tuple-element.55), channel_id=1, source_target_pairs={{0,8},{4,12},{8,0},{12,4},{1,9},{5,13},{9,1},{13,5},{2,10},{6,14},... | collective-permute-start | bytes 196616 | tf_op jit(solution)/shard_map/ppermute | solution.py:536
  72.2 2.8 %collective-permute-done.19.right = f32[128,128]{1,0:T(8,128)S(1)} collective-permute-done((f32[128,128]{1,0:T(8,128)S(1)}, f32[128,128]{1,0:T(8,128)S(1)}, u32[]{:S(2)}, u32[]{:S(2)}) %collective-permute-start.19) | collective-permute-done | bytes 65568 | tf_op jit(solution)/shard_map/ppermute | solution.py:536
  75.0 1.6 %collective-permute-start.26 = (f32[8,96,128]{2,1,0:T(8,128)S(1)}, f32[8,96,128]{2,1,0:T(8,128)S(1)}, u32[]{:S(2)}, u32[]{:S(2)}) collective-permute-start(f32[8,96,128]{2,1,0:T(8,128)S(1)} %get-tuple-element.58.own.residual), channel_id=1, source_target_pairs={{0,16},{16,0},{1,17},{17,1},{2,18},{18,2},{3,19},{19,3},{4,20},{20... | collective-permute-start | bytes 1179656 | tf_op jit(solution)/shard_map/ppermute | solution.py:536
  76.6 1.2 %collective-permute-start.20 = (f32[128,128]{1,0:T(8,128)S(1)}, f32[128,128]{1,0:T(8,128)S(1)}, u32[]{:S(2)}, u32[]{:S(2)}) collective-permute-start(f32[128,128]{1,0:T(8,128)S(1)} %add.5.refs_0_), channel_id=1, source_target_pairs={{0,1},{1,0},{2,3},{3,2},{4,5},{5,4},{6,7},{7,6},{8,9},{9,8},{10,11... | collective-permute-start | bytes 196616 | tf_op jit(solution)/shard_map/ppermute | solution.py:536
  77.7 1.3 %collective-permute-start.21 = (f32[128,128]{1,0:T(8,128)S(1)}, f32[128,128]{1,0:T(8,128)S(1)}, u32[]{:S(2)}, u32[]{:S(2)}) collective-permute-start(f32[128,128]{1,0:T(8,128)S(1)} %add.5.refs_0_), channel_id=1, source_target_pairs={{0,2},{1,3},{2,0},{3,1},{4,6},{5,7},{6,4},{7,5},{8,10},{9,11},{10,... | collective-permute-start | bytes 196616 | tf_op jit(solution)/shard_map/ppermute | solution.py:536
  79.0 2.0 %collective-permute-start.22 = (f32[128,128]{1,0:T(8,128)S(1)}, f32[128,128]{1,0:T(8,128)S(1)}, u32[]{:S(2)}, u32[]{:S(2)}) collective-permute-start(f32[128,128]{1,0:T(8,128)S(1)} %add.5.refs_0_), channel_id=1, source_target_pairs={{0,3},{1,2},{2,1},{3,0},{4,7},{5,6},{6,5},{7,4},{8,11},{9,10},{10,... | collective-permute-start | bytes 196616 | tf_op jit(solution)/shard_map/ppermute | solution.py:536
  81.0 3.0 %collective-permute-done.21.refs_2_ = f32[128,128]{1,0:T(8,128)S(1)} collective-permute-done((f32[128,128]{1,0:T(8,128)S(1)}, f32[128,128]{1,0:T(8,128)S(1)}, u32[]{:S(2)}, u32[]{:S(2)}) %collective-permute-start.21) | collective-permute-done | bytes 65568 | tf_op jit(solution)/shard_map/ppermute | solution.py:536
  84.0 1.2 %collective-permute-done.22.refs_3_ = f32[128,128]{1,0:T(8,128)S(1)} collective-permute-done((f32[128,128]{1,0:T(8,128)S(1)}, f32[128,128]{1,0:T(8,128)S(1)}, u32[]{:S(2)}, u32[]{:S(2)}) %collective-permute-start.22) | collective-permute-done | bytes 65568 | tf_op jit(solution)/shard_map/ppermute | solution.py:536
  85.3 1.8 %collective-permute-start.25 = (f32[128,128]{1,0:T(8,128)S(1)}, f32[128,128]{1,0:T(8,128)S(1)}, u32[]{:S(2)}, u32[]{:S(2)}) collective-permute-start(f32[128,128]{1,0:T(8,128)S(1)} %scale.3.refs_0_), channel_id=1, source_target_pairs={{0,8},{4,12},{8,0},{12,4},{1,9},{5,13},{9,1},{13,5},{2,10},{6,14},... | collective-permute-start | bytes 196616 | tf_op jit(solution)/shard_map/ppermute | solution.py:536
  87.5 1.3 %collective-permute-start.23 = (f32[128,128]{1,0:T(8,128)S(1)}, f32[128,128]{1,0:T(8,128)S(1)}, u32[]{:S(2)}, u32[]{:S(2)}) collective-permute-start(f32[128,128]{1,0:T(8,128)S(1)} %scale.3.refs_0_), channel_id=1, source_target_pairs={{0,24},{4,28},{8,16},{12,20},{16,8},{20,12},{24,0},{28,4},{1,25},{... | collective-permute-start | bytes 196616 | tf_op jit(solution)/shard_map/ppermute | solution.py:542
  88.8 1.0 %join.1 = f32[8,96,256]{2,1,0:T(8,128)} custom-call(f32[8,96,128]{2,1,0:T(8,128)S(1)} %get-tuple-element.58.own.residual, f32[8,96,128]{2,1,0:T(8,128)S(1)} %collective-permute-done.26.other.residual), custom_call_target="tpu_custom_call" | custom-call | flops 1000000 | bytes 2000000 | tf_op jit(solution)/shard_map/join/pallas_call | solution.py:485
  90.2 0.7 first_half.4.base
  91.3 0.7 second_half.3.own
  92.0 1.0 %collective-permute-done.23.refs_1_ = f32[128,128]{1,0:T(8,128)S(1)} collective-permute-done((f32[128,128]{1,0:T(8,128)S(1)}, f32[128,128]{1,0:T(8,128)S(1)}, u32[]{:S(2)}, u32[]{:S(2)}) %collective-permute-start.23) | collective-permute-done | bytes 65568 | tf_op jit(solution)/shard_map/ppermute | solution.py:542
  93.0 0.7 first_half.5.other
  93.6 0.6 collective-permute-done.30.refs_1_
  94.2 1.5 %final.1 = f32[8,96,256]{2,1,0:T(8,128)} custom-call(f32[8,96,128]{2,1,0:T(8,128)S(1)} %second_half.3.own, f32[8,96,128]{2,1,0:T(8,128)S(1)} %first_half.5.other, bf16[8,2,192,512]{3,2,1,0:T(8,128)(2,1)S(1)} %get-tuple-element.40.vectors, f32[128,128]{1,0:T(8,128)S(1)} %collective-permute-done.29.refs_0_, f32[128,128]{1,0:T(8,128)S(1)} %collective-permute-done.30.refs_1_), custom_call_target="tpu_custom_call" | custom-call | flops 1000000000 | bytes 4000000 | tf_op jit(solution)/shard_map/final/pallas_call | solution.py:513
  (43 shorter events, 4.6 us)
Async XLA Ops:
  0.6 1.1 %copy-start = (f32[1,1,2,4,96,256]{5,4,3,2,1,0:T(8,128)S(1)}, f32[1,1,2,4,96,256]{5,4,3,2,1,0:T(8,128)}, u32[]{:S(2)}) copy-start(f32[1,1,2,4,96,256]{5,4,3,2,1,0:T(8,128)} %param.7) | copy-start | bytes 2359300
  2.0 5.3 %collective-permute-start = (f32[8,96,128]{2,1,0:T(8,128)S(1)}, f32[8,96,128]{2,1,0:T(8,128)S(1)}, u32[]{:S(2)}, u32[]{:S(2)}) collective-permute-start(f32[8,96,128]{2,1,0:T(8,128)S(1)} %pack.1.x_ref.x), channel_id=1, source_target_pairs={{0,4},{4,0},{8,12},{12,8},{1,5},{5,1},{9,13},{13,9},{2,6},{6,2},{1... | collective-permute-start | bytes 1179656 | tf_op jit(solution)/shard_map/ppermute | solution.py:536
  2.6 18.6 %collective-permute-start.2 = (f32[8,96,128]{2,1,0:T(8,128)S(1)}, f32[8,96,128]{2,1,0:T(8,128)S(1)}, u32[]{:S(2)}, u32[]{:S(2)}) collective-permute-start(f32[8,96,128]{2,1,0:T(8,128)S(1)} %pack.1.x_ref.x), channel_id=1, source_target_pairs={{0,1},{1,2},{2,3},{3,0},{4,5},{5,6},{6,7},{7,4},{8,9},{9,10},{10,1... | collective-permute-start | bytes 1179656 | tf_op jit(solution)/shard_map/ppermute | solution.py:531
  5.2 19.6 %collective-permute-start.3 = (f32[8,96,128]{2,1,0:T(8,128)S(1)}, f32[8,96,128]{2,1,0:T(8,128)S(1)}, u32[]{:S(2)}, u32[]{:S(2)}) collective-permute-start(f32[8,96,128]{2,1,0:T(8,128)S(1)} %pack.1.x_ref.x), channel_id=1, source_target_pairs={{0,3},{1,0},{2,1},{3,2},{4,7},{5,4},{6,5},{7,6},{8,11},{9,8},{10,9... | collective-permute-start | bytes 1179656 | tf_op jit(solution)/shard_map/ppermute | solution.py:531
  7.3 13.1 %collective-permute-start.1 = (f32[8,96,128]{2,1,0:T(8,128)S(1)}, f32[8,96,128]{2,1,0:T(8,128)S(1)}, u32[]{:S(2)}, u32[]{:S(2)}) collective-permute-start(f32[8,96,128]{2,1,0:T(8,128)S(1)} %pack.1.x_ref.x), channel_id=1, source_target_pairs={{0,12},{4,8},{8,4},{12,0},{1,13},{5,9},{9,5},{13,1},{2,14},{6,10},... | collective-permute-start | bytes 1179656 | tf_op jit(solution)/shard_map/ppermute | solution.py:549
  24.8 7.3 %copy-start.1 = (f32[2,512]{1,0:T(2,128)S(1)}, f32[2,512]{1,0:T(2,128)}, u32[]{:S(2)}) copy-start(f32[2,512]{1,0:T(2,128)} %inverse.1) | copy-start | bytes 12292
  26.2 1.4 %collective-permute-start.4 = (f32[256,128]{1,0:T(8,128)S(1)}, f32[256,128]{1,0:T(8,128)S(1)}, u32[]{:S(2)}, u32[]{:S(2)}) collective-permute-start(f32[256,128]{1,0:T(8,128)S(1)} %get-tuple-element.42), channel_id=1, source_target_pairs={{0,4},{4,0},{8,12},{12,8},{1,5},{5,1},{9,13},{13,9},{2,6},{6,2},{1... | collective-permute-start | bytes 393224 | tf_op jit(solution)/shard_map/ppermute | solution.py:536
  27.6 4.6 %collective-permute-start.5 = (f32[128,128]{1,0:T(8,128)S(1)}, f32[128,128]{1,0:T(8,128)S(1)}, u32[]{:S(2)}, u32[]{:S(2)}) collective-permute-start(f32[128,128]{1,0:T(8,128)S(1)} %get-tuple-element.44), channel_id=1, source_target_pairs={{0,8},{4,12},{8,0},{12,4},{1,9},{5,13},{9,1},{13,5},{2,10},{6,14},... | collective-permute-start | bytes 196616 | tf_op jit(solution)/shard_map/ppermute | solution.py:536
  29.2 8.2 %collective-permute-start.6 = (f32[128,128]{1,0:T(8,128)S(1)}, f32[128,128]{1,0:T(8,128)S(1)}, u32[]{:S(2)}, u32[]{:S(2)}) collective-permute-start(f32[128,128]{1,0:T(8,128)S(1)} %get-tuple-element.43.refs_0_), channel_id=1, source_target_pairs={{0,2},{1,3},{2,0},{3,1},{4,6},{5,7},{6,4},{7,5},{8,10},{9,11},{10,... | collective-permute-start | bytes 196616 | tf_op jit(solution)/shard_map/ppermute | solution.py:536
  31.0 6.5 %collective-permute-start.7 = (f32[128,128]{1,0:T(8,128)S(1)}, f32[128,128]{1,0:T(8,128)S(1)}, u32[]{:S(2)}, u32[]{:S(2)}) collective-permute-start(f32[128,128]{1,0:T(8,128)S(1)} %get-tuple-element.44), channel_id=1, source_target_pairs={{0,10},{1,11},{2,8},{3,9},{4,14},{5,15},{6,12},{7,13},{8,2},{9,3},... | collective-permute-start | bytes 196616 | tf_op jit(solution)/shard_map/ppermute | solution.py:542
  37.6 5.6 %collective-permute-start.10 = (f32[128,128]{1,0:T(8,128)S(1)}, f32[128,128]{1,0:T(8,128)S(1)}, u32[]{:S(2)}, u32[]{:S(2)}) collective-permute-start(f32[128,128]{1,0:T(8,128)S(1)} %scale.2.left), channel_id=1, source_target_pairs={{0,9},{1,8},{2,11},{3,10},{4,13},{5,12},{6,15},{7,14},{8,1},{9,0},... | collective-permute-start | bytes 196616 | tf_op jit(solution)/shard_map/ppermute | solution.py:542
  38.8 4.6 %collective-permute-start.9 = (f32[128,128]{1,0:T(8,128)S(1)}, f32[128,128]{1,0:T(8,128)S(1)}, u32[]{:S(2)}, u32[]{:S(2)}) collective-permute-start(f32[128,128]{1,0:T(8,128)S(1)} %scale.2.left), channel_id=1, source_target_pairs={{0,8},{4,12},{8,0},{12,4},{1,9},{5,13},{9,1},{13,5},{2,10},{6,14},... | collective-permute-start | bytes 196616 | tf_op jit(solution)/shard_map/ppermute | solution.py:536
  40.3 4.3 %collective-permute-start.8 = (f32[128,128]{1,0:T(8,128)S(1)}, f32[128,128]{1,0:T(8,128)S(1)}, u32[]{:S(2)}, u32[]{:S(2)}) collective-permute-start(f32[128,128]{1,0:T(8,128)S(1)} %scale.2.left), channel_id=1, source_target_pairs={{0,1},{1,0},{2,3},{3,2},{4,5},{5,4},{6,7},{7,6},{8,9},{9,8},{10,11... | collective-permute-start | bytes 196616 | tf_op jit(solution)/shard_map/ppermute | solution.py:536
  43.5 1.9 %collective-permute-start.12 = (f32[128,128]{1,0:T(8,128)S(1)}, f32[128,128]{1,0:T(8,128)S(1)}, u32[]{:S(2)}, u32[]{:S(2)}) collective-permute-start(f32[128,128]{1,0:T(8,128)S(1)} %add.4.refs_1_), channel_id=1, source_target_pairs={{0,4},{4,0},{8,12},{12,8},{1,5},{5,1},{9,13},{13,9},{2,6},{6,2},{1... | collective-permute-start | bytes 196616 | tf_op jit(solution)/shard_map/ppermute | solution.py:536
  44.6 1.3 %collective-permute-start.11 = (f32[128,128]{1,0:T(8,128)S(1)}, f32[128,128]{1,0:T(8,128)S(1)}, u32[]{:S(2)}, u32[]{:S(2)}) collective-permute-start(f32[128,128]{1,0:T(8,128)S(1)} %add.3.refs_0_), channel_id=1, source_target_pairs={{0,4},{4,0},{8,12},{12,8},{1,5},{5,1},{9,13},{13,9},{2,6},{6,2},{1... | collective-permute-start | bytes 196616 | tf_op jit(solution)/shard_map/ppermute | solution.py:536
  46.6 4.1 %collective-permute-start.13 = (f32[8,96,128]{2,1,0:T(8,128)S(1)}, f32[8,96,128]{2,1,0:T(8,128)S(1)}, u32[]{:S(2)}, u32[]{:S(2)}) collective-permute-start(f32[8,96,128]{2,1,0:T(8,128)S(1)} %second_half.2.x_ref.x), channel_id=1, source_target_pairs={{0,4},{4,0},{8,12},{12,8},{1,5},{5,1},{9,13},{13,9},{2,6},{6,2},{1... | collective-permute-start | bytes 1179656 | tf_op jit(solution)/shard_map/ppermute | solution.py:536
  46.8 15.9 %collective-permute-start.15 = (f32[8,96,128]{2,1,0:T(8,128)S(1)}, f32[8,96,128]{2,1,0:T(8,128)S(1)}, u32[]{:S(2)}, u32[]{:S(2)}) collective-permute-start(f32[8,96,128]{2,1,0:T(8,128)S(1)} %second_half.2.x_ref.x), channel_id=1, source_target_pairs={{0,1},{1,2},{2,3},{3,0},{4,5},{5,6},{6,7},{7,4},{8,9},{9,10},{10,1... | collective-permute-start | bytes 1179656 | tf_op jit(solution)/shard_map/ppermute | solution.py:531
  48.2 19.7 %collective-permute-start.17 = (f32[8,96,128]{2,1,0:T(8,128)S(1)}, f32[8,96,128]{2,1,0:T(8,128)S(1)}, u32[]{:S(2)}, u32[]{:S(2)}) collective-permute-start(f32[8,96,128]{2,1,0:T(8,128)S(1)} %second_half.2.x_ref.x), channel_id=1, source_target_pairs={{0,3},{1,0},{2,1},{3,2},{4,7},{5,4},{6,5},{7,6},{8,11},{9,8},{10,9... | collective-permute-start | bytes 1179656 | tf_op jit(solution)/shard_map/ppermute | solution.py:531
  50.7 11.4 %collective-permute-start.14 = (f32[8,96,128]{2,1,0:T(8,128)S(1)}, f32[8,96,128]{2,1,0:T(8,128)S(1)}, u32[]{:S(2)}, u32[]{:S(2)}) collective-permute-start(f32[8,96,128]{2,1,0:T(8,128)S(1)} %second_half.2.x_ref.x), channel_id=1, source_target_pairs={{0,12},{4,8},{8,4},{12,0},{1,13},{5,9},{9,5},{13,1},{2,14},{6,10},... | collective-permute-start | bytes 1179656 | tf_op jit(solution)/shard_map/ppermute | solution.py:549
  51.0 12.2 %collective-permute-start.16 = (f32[8,96,128]{2,1,0:T(8,128)S(1)}, f32[8,96,128]{2,1,0:T(8,128)S(1)}, u32[]{:S(2)}, u32[]{:S(2)}) collective-permute-start(f32[8,96,128]{2,1,0:T(8,128)S(1)} %second_half.2.x_ref.x), channel_id=1, source_target_pairs={{0,16},{16,0},{1,17},{17,1},{2,18},{18,2},{3,19},{19,3},{4,20},{20... | collective-permute-start | bytes 1179656 | tf_op jit(solution)/shard_map/ppermute | solution.py:536
  69.2 1.4 %collective-permute-start.18 = (f32[256,128]{1,0:T(8,128)S(1)}, f32[256,128]{1,0:T(8,128)S(1)}, u32[]{:S(2)}, u32[]{:S(2)}) collective-permute-start(f32[256,128]{1,0:T(8,128)S(1)} %get-tuple-element.53), channel_id=1, source_target_pairs={{0,4},{4,0},{8,12},{12,8},{1,5},{5,1},{9,13},{13,9},{2,6},{6,2},{1... | collective-permute-start | bytes 393224 | tf_op jit(solution)/shard_map/ppermute | solution.py:536
  70.7 4.3 %collective-permute-start.19 = (f32[128,128]{1,0:T(8,128)S(1)}, f32[128,128]{1,0:T(8,128)S(1)}, u32[]{:S(2)}, u32[]{:S(2)}) collective-permute-start(f32[128,128]{1,0:T(8,128)S(1)} %get-tuple-element.55), channel_id=1, source_target_pairs={{0,8},{4,12},{8,0},{12,4},{1,9},{5,13},{9,1},{13,5},{2,10},{6,14},... | collective-permute-start | bytes 196616 | tf_op jit(solution)/shard_map/ppermute | solution.py:536
  75.0 13.8 %collective-permute-start.26 = (f32[8,96,128]{2,1,0:T(8,128)S(1)}, f32[8,96,128]{2,1,0:T(8,128)S(1)}, u32[]{:S(2)}, u32[]{:S(2)}) collective-permute-start(f32[8,96,128]{2,1,0:T(8,128)S(1)} %get-tuple-element.58.own.residual), channel_id=1, source_target_pairs={{0,16},{16,0},{1,17},{17,1},{2,18},{18,2},{3,19},{19,3},{4,20},{20... | collective-permute-start | bytes 1179656 | tf_op jit(solution)/shard_map/ppermute | solution.py:536
  76.6 4.4 %collective-permute-start.20 = (f32[128,128]{1,0:T(8,128)S(1)}, f32[128,128]{1,0:T(8,128)S(1)}, u32[]{:S(2)}, u32[]{:S(2)}) collective-permute-start(f32[128,128]{1,0:T(8,128)S(1)} %add.5.refs_0_), channel_id=1, source_target_pairs={{0,1},{1,0},{2,3},{3,2},{4,5},{5,4},{6,7},{7,6},{8,9},{9,8},{10,11... | collective-permute-start | bytes 196616 | tf_op jit(solution)/shard_map/ppermute | solution.py:536
  77.7 6.3 %collective-permute-start.21 = (f32[128,128]{1,0:T(8,128)S(1)}, f32[128,128]{1,0:T(8,128)S(1)}, u32[]{:S(2)}, u32[]{:S(2)}) collective-permute-start(f32[128,128]{1,0:T(8,128)S(1)} %add.5.refs_0_), channel_id=1, source_target_pairs={{0,2},{1,3},{2,0},{3,1},{4,6},{5,7},{6,4},{7,5},{8,10},{9,11},{10,... | collective-permute-start | bytes 196616 | tf_op jit(solution)/shard_map/ppermute | solution.py:536
  79.0 6.2 %collective-permute-start.22 = (f32[128,128]{1,0:T(8,128)S(1)}, f32[128,128]{1,0:T(8,128)S(1)}, u32[]{:S(2)}, u32[]{:S(2)}) collective-permute-start(f32[128,128]{1,0:T(8,128)S(1)} %add.5.refs_0_), channel_id=1, source_target_pairs={{0,3},{1,2},{2,1},{3,0},{4,7},{5,6},{6,5},{7,4},{8,11},{9,10},{10,... | collective-permute-start | bytes 196616 | tf_op jit(solution)/shard_map/ppermute | solution.py:536
  85.3 4.6 %collective-permute-start.25 = (f32[128,128]{1,0:T(8,128)S(1)}, f32[128,128]{1,0:T(8,128)S(1)}, u32[]{:S(2)}, u32[]{:S(2)}) collective-permute-start(f32[128,128]{1,0:T(8,128)S(1)} %scale.3.refs_0_), channel_id=1, source_target_pairs={{0,8},{4,12},{8,0},{12,4},{1,9},{5,13},{9,1},{13,5},{2,10},{6,14},... | collective-permute-start | bytes 196616 | tf_op jit(solution)/shard_map/ppermute | solution.py:536
  87.0 4.3 %collective-permute-start.24 = (f32[128,128]{1,0:T(8,128)S(1)}, f32[128,128]{1,0:T(8,128)S(1)}, u32[]{:S(2)}, u32[]{:S(2)}) collective-permute-start(f32[128,128]{1,0:T(8,128)S(1)} %scale.3.refs_0_), channel_id=1, source_target_pairs={{0,16},{16,0},{1,17},{17,1},{2,18},{18,2},{3,19},{19,3},{4,20},{20... | collective-permute-start | bytes 196616 | tf_op jit(solution)/shard_map/ppermute | solution.py:536
  87.5 3.8 %collective-permute-start.27 = (f32[128,128]{1,0:T(8,128)S(1)}, f32[128,128]{1,0:T(8,128)S(1)}, u32[]{:S(2)}, u32[]{:S(2)}) collective-permute-start(f32[128,128]{1,0:T(8,128)S(1)} %scale.3.refs_0_), channel_id=1, source_target_pairs={{0,4},{4,0},{8,12},{12,8},{1,5},{5,1},{9,13},{13,9},{2,6},{6,2},{1... | collective-permute-start | bytes 196616 | tf_op jit(solution)/shard_map/ppermute | solution.py:536
  87.5 5.4 %collective-permute-start.23 = (f32[128,128]{1,0:T(8,128)S(1)}, f32[128,128]{1,0:T(8,128)S(1)}, u32[]{:S(2)}, u32[]{:S(2)}) collective-permute-start(f32[128,128]{1,0:T(8,128)S(1)} %scale.3.refs_0_), channel_id=1, source_target_pairs={{0,24},{4,28},{8,16},{12,20},{16,8},{20,12},{24,0},{28,4},{1,25},{... | collective-permute-start | bytes 196616 | tf_op jit(solution)/shard_map/ppermute | solution.py:542
  89.9 1.4 %collective-permute-start.28 = (f32[128,128]{1,0:T(8,128)S(1)}, f32[128,128]{1,0:T(8,128)S(1)}, u32[]{:S(2)}, u32[]{:S(2)}) collective-permute-start(f32[128,128]{1,0:T(8,128)S(1)} %collective-permute-done.25.refs_1_), channel_id=1, source_target_pairs={{0,4},{4,0},{8,12},{12,8},{1,5},{5,1},{9,13},{13,9},{2,6},{6,2},{1... | collective-permute-start | bytes 196616 | tf_op jit(solution)/shard_map/ppermute | solution.py:536
  91.3 2.3 %collective-permute-start.29 = (f32[128,128]{1,0:T(8,128)S(1)}, f32[128,128]{1,0:T(8,128)S(1)}, u32[]{:S(2)}, u32[]{:S(2)}) collective-permute-start(f32[128,128]{1,0:T(8,128)S(1)} %collective-permute-done.24.refs_0_), channel_id=1, source_target_pairs={{0,4},{4,0},{8,12},{12,8},{1,5},{5,1},{9,13},{13,9},{2,6},{6,2},{1... | collective-permute-start | bytes 196616 | tf_op jit(solution)/shard_map/ppermute | solution.py:536
  92.9 1.3 %collective-permute-start.30 = (f32[128,128]{1,0:T(8,128)S(1)}, f32[128,128]{1,0:T(8,128)S(1)}, u32[]{:S(2)}, u32[]{:S(2)}) collective-permute-start(f32[128,128]{1,0:T(8,128)S(1)} %collective-permute-done.23.refs_1_), channel_id=1, source_target_pairs={{0,4},{4,0},{8,12},{12,8},{1,5},{5,1},{9,13},{13,9},{2,6},{6,2},{1... | collective-permute-start | bytes 196616 | tf_op jit(solution)/shard_map/ppermute | solution.py:536

commit v10 on v8

--- a/solution.py
+++ b/solution.py
@@ -82,19 +82,33 @@
     return pltpu.with_memory_space_constraint(value, pltpu.HBM)
 
 
-def pack_kernel(full, half):
+def put(site, value, whole, front, back):
+    count = front.shape[0]
+    whole[site] = value
+    if site < count:
+        front[site] = value
+    else:
+        back[site - count] = value
+
+
+def with_halves(shape):
+    part = pltpu.VMEM((shape[0] // 2,) + tuple(shape[1:]), F32)
+    return pltpu.VMEM(shape, F32), part, part
+
+
+def pack_kernel(full, half, front, back):
     group = lax.axis_index("groups")
     for site in range(full.shape[0]):
-        half[site] = pick_half(full[site], group)
+        put(site, pick_half(full[site], group), half, front, back)
 
 
 def pack(full):
     sites, rows, lanes = full.shape
     return pl.pallas_call(
         pack_kernel,
-        out_shape=pltpu.VMEM((sites, rows, lanes // 2), F32),
+        out_shape=with_halves((sites, rows, lanes // 2)),
         in_specs=vmem(1),
-        out_specs=vmem(1)[0],
+        out_specs=tuple(vmem(3)),
         compiler_params=params(),
         cost_estimate=cost(1e6, 1e6),
         name="pack",
@@ -271,31 +285,12 @@
     )(inverse)
 
 
-def apply_faces(site, faces, matrices):
+def apply_faces(*pairs):
     summed = None
-    for face, matrix in zip(faces, matrices):
-        term = matmul(matrix[site], stack(face(site), 1.0))
+    for matrix, face in pairs:
+        term = matmul(matrix, stack(face, 1.0))
         summed = term if summed is None else summed + term
     return fold(summed)
-
-
-def z_faces_kernel(rest, near, far, matrix, out):
-    parity = lax.rem(lax.axis_index("space"), 2)
-    faces = (lambda s: near[s], lambda s: far[s])
-    for site in range(rest.shape[0]):
-        out[site] = rest[site] - apply_faces(site, faces, (matrix.at[parity], matrix.at[1 - parity]))
-
-
-def z_faces(rest, near, far, matrix):
-    return pl.pallas_call(
-        z_faces_kernel,
-        out_shape=pltpu.VMEM(rest.shape, F32),
-        in_specs=vmem(4),
-        out_specs=vmem(1)[0],
-        compiler_params=params(),
-        cost_estimate=cost(1e9, 4e6),
-        name="z_faces",
-    )(rest, near, far, matrix)
 
 
 def edge_sign(last):
@@ -303,50 +298,99 @@
     return jnp.where(lax.axis_index("tm") == (count - 1 if last else 0), -1.0, 1.0).astype(F32)
 
 
+def front_kernel(backward, forward, matrix, out):
+    behind, ahead = edge_sign(False), edge_sign(True)
+    for site in range(out.shape[0]):
+        out[site] = apply_faces((matrix[2, site], ahead * forward[site]), (matrix[3, site], behind * backward[site]))
+
+
+def front_faces(backward, forward, matrix):
+    return pl.pallas_call(
+        front_kernel,
+        out_shape=pltpu.VMEM(forward.shape, F32),
+        in_specs=vmem(3),
+        out_specs=vmem(1)[0],
+        compiler_params=params(),
+        cost_estimate=cost(1e3, 1e3),
+        name="front_faces",
+    )(backward, forward, matrix)
+
+
+def middle_kernel(rest, near, far, front, matrix, vectors, back, residual, partial, stacks):
+    parity = lax.rem(lax.axis_index("space"), 2)
+    sites, rows, _ = front.shape
+    for site in range(rest.shape[0]):
+        own = rest[site] - apply_faces((matrix[parity, site], near[site]), (matrix[1 - parity, site], far[site]))
+        if site < sites:
+            own = own - front[site]
+            residual[site] = own
+            stacks[site * 2 * rows : (site + 1) * 2 * rows] = stack(own, -1.0)
+        else:
+            back[site - sites] = own
+    partial[...] = fold(matmul(vectors[:, : stacks.shape[0]], stacks[...]))
+
+
+def middle(rest, near, far, front, matrix, vectors):
+    sites, rows, lanes = front.shape
+    half = pltpu.VMEM(front.shape, F32)
+    return pl.pallas_call(
+        middle_kernel,
+        out_shape=(half, half, pltpu.VMEM((vectors.shape[0] // 2, lanes), F32)),
+        in_specs=vmem(6),
+        out_specs=tuple(vmem(3)),
+        scratch_shapes=[pltpu.VMEM((sites * 2 * rows, 2 * lanes), BF16)],
+        compiler_params=params(),
+        cost_estimate=cost(1e3, 1e3),
+        name="middle",
+    )(rest, near, far, front, matrix, vectors)
+
+
 def backward_kernel(rest, backward, matrix, out):
     sign = edge_sign(False)
-    for site in range(rest.shape[0]):
-        out[site] = rest[site] - apply_faces(site, (lambda s: sign * backward[s],), (matrix.at[3],))
+    sites = backward.shape[0]
+    for site in range(sites):
+        out[site] = rest[site] - apply_faces((matrix[3, sites + site], sign * backward[site]))
 
 
 def backward_face(rest, backward, matrix):
     return pl.pallas_call(
         backward_kernel,
-        out_shape=pltpu.VMEM(rest.shape, F32),
+        out_shape=pltpu.VMEM(backward.shape, F32),
         in_specs=vmem(3),
         out_specs=vmem(1)[0],
         compiler_params=params(),
-        cost_estimate=cost(1e9, 4e6),
+        cost_estimate=cost(1e3, 1e3),
         name="backward_face",
     )(rest, backward, matrix)
 
 
-def forward_kernel(rest, forward, matrix, vectors, residual, keep, send, stacks):
+def forward_kernel(front, partial, rest, forward, matrix, vectors, residual, keep, send, stacks):
     sign = edge_sign(True)
-    rows = 2 * rest.shape[1]
-    for site in range(rest.shape[0]):
-        own = rest[site] - apply_faces(site, (lambda s: sign * forward[s],), (matrix.at[2],))
-        residual[site] = own
-        stacks[site * rows : (site + 1) * rows] = stack(own, -1.0)
-    whole = fold(matmul(vectors[...], stacks[...]))
+    sites, rows, _ = forward.shape
+    for site in range(sites):
+        own = rest[site] - apply_faces((matrix[2, sites + site], sign * forward[site]))
+        residual[site] = front[site]
+        residual[sites + site] = own
+        stacks[site * 2 * rows : (site + 1) * 2 * rows] = stack(own, -1.0)
+    whole = partial[...] + fold(matmul(vectors[:, stacks.shape[0] :], stacks[...]))
     half = whole.shape[0] // 2
     keep[...] = whole[:half]
     send[...] = whole[half:]
 
 
-def forward_face(rest, forward, matrix, vectors):
-    sites, rows, lanes = rest.shape
+def forward_face(front, partial, rest, forward, matrix, vectors):
+    sites, rows, lanes = forward.shape
     part = pltpu.VMEM((vectors.shape[0] // 4, lanes), F32)
     return pl.pallas_call(
         forward_kernel,
-        out_shape=(pltpu.VMEM(rest.shape, F32), part, part),
-        in_specs=vmem(4),
+        out_shape=(pltpu.VMEM((2 * sites, rows, lanes), F32), part, part),
+        in_specs=vmem(6),
         out_specs=tuple(vmem(3)),
         scratch_shapes=[pltpu.VMEM((sites * 2 * rows, 2 * lanes), BF16)],
         compiler_params=params(),
         cost_estimate=cost(2e9, 8e6),
         name="forward_face",
-    )(rest, forward, matrix, vectors)
+    )(front, partial, rest, forward, matrix, vectors)
 
 
 def split_kernel(keep, received, next_keep, next_send):
@@ -449,18 +493,18 @@
 
 
 def second_half_kernel(base, vectors, *refs):
-    pieces, (out, stacks) = refs[:-2], refs[-2:]
+    pieces, (out, front, back, stacks) = refs[:-4], refs[-4:]
     place_pieces(pieces, stacks)
     for site in range(base.shape[0]):
-        out[site] = base[site] + expand(site, vectors, 1, stacks)
+        put(site, base[site] + expand(site, vectors, 1, stacks), out, front, back)
 
 
 def second_half(base, pieces, vectors):
     return pl.pallas_call(
         second_half_kernel,
-        out_shape=pltpu.VMEM(base.shape, F32),
+        out_shape=with_halves(base.shape),
         in_specs=vmem(2 + len(pieces)),
-        out_specs=vmem(1)[0],
+        out_specs=tuple(vmem(3)),
         scratch_shapes=[pltpu.VMEM((vectors.shape[-1], 2 * base.shape[-1]), BF16)],
         compiler_params=params(),
         cost_estimate=cost(1e9, 4e6),
@@ -542,11 +586,13 @@
     return lax.ppermute(value, (first, second), pairs)
 
 
-def faces_of(x):
+def faces_of(x, front, back):
     count = lax.axis_size("space")
-    near = crossed(x, "space", 1)
+    early = shifted(front, "tm", 1), shifted(front, "tm", -1)
+    near, back = lax.optimization_barrier((crossed(x, "space", 1), back))
     far = lax.ppermute(x, "space", [(i, (i + 1 if i % 2 else i - 1) % count) for i in range(count)])
-    return near, far, shifted(x, "tm", -1), shifted(x, "tm", 1)
+    late = shifted(back, "tm", 1), shifted(back, "tm", -1)
+    return near, far, early, late
 
 
 def halving(keep, send):
@@ -595,8 +641,8 @@
     number = vectors.shape[0]
     blocks = lax.axis_size("space")
 
-    x = pack(initial.reshape(sites, rows, lanes))
-    faces = faces_of(x)
+    x, front, back = pack(initial.reshape(sites, rows, lanes))
+    faces = faces_of(x, front, back)
     matrices = couplings.reshape(directions, sites, rows, couplings.shape[-1])
     rest, half_source, local, halo = first_local(x, source.reshape(sites, rows, lanes), matrices, ny, nx)
     across = jnp.transpose(vectors, (1, 2, 3, 4, 5, 0)).reshape(sites * vectors.shape[-1], number)
@@ -606,22 +652,20 @@
     for sweep in range(ITERS):
         last = sweep == ITERS - 1
         if sweep:
-            faces = faces_of(x)
+            faces = faces_of(x, front, back)
             rest = local_part(x, half_source, local, ny, nx)
-        near, far, forward_t, backward_t = faces
+        near, far, early, late = faces
+        back_rest, own, partial = middle(rest, near, far, front_faces(*early, halo), halo, by_rows)
         if last:
-            near, x = lax.optimization_barrier((near, x))
+            partial, x = lax.optimization_barrier((partial, x))
             other_x = crossed(x, "groups", 1)
-        rest = backward_face(rest, backward_t, halo)
-        rest = z_faces(rest, near, far, halo)
-        if last:
-            rest, other_x = lax.optimization_barrier((rest, other_x))
-        residual, keep, send = forward_face(rest, forward_t, halo, by_rows)
+        back_rest = backward_face(back_rest, late[0], halo)
+        residual, keep, send = forward_face(own, partial, back_rest, late[1], halo, by_rows)
         if not last:
             pieces = scaled_sum(keep, send, eigen)
             base = first_half(x, residual, pieces, by_columns)
-            x = second_half(base, paired(pieces), by_columns)
-    part, residual = lax.optimization_barrier((halving(keep, send), residual))
+            x, front, back = second_half(base, paired(pieces), by_columns)
+    part, residual, other_x = lax.optimization_barrier((halving(keep, send), residual, other_x))
     other_residual = crossed(residual, "groups", 1)
     d = scale(eigen, over_time(part))
     mask = blocks // 2
@@ -632,7 +676,7 @@
     own[-1], full_residual = lax.optimization_barrier((own[-1], full_residual))
     own_x = first_half(x, residual, own, by_columns)
     other[0], own_x = lax.optimization_barrier((other[0], own_x))
-    own_x = second_half(own_x, paired(own), by_columns)
+    own_x, _, _ = second_half(own_x, paired(own), by_columns)
     other[-1], own_x = lax.optimization_barrier((other[-1], own_x))
     other_second = paired(other)
     other_x = first_half(other_x, other_residual, other, by_columns)

time: 96.2 us -> 95.8 us (level)
  waiting for transfers between devices: 34.7 us -> 24.9 us
  starting transfers between devices: 32.6 us -> 40.6 us
  Pallas kernels: 26.4 us -> 27.7 us
    ppermute x4 -> x8, waiting for transfers between devices: 13.2 us -> 5.06 us  [shifted(): lax.ppermute(value, axis, [(i, (i + step) % count) for i in range(count)])]
    ppermute x4 -> x8, starting transfers between devices: 8.51 us -> 16.2 us  [shifted(): lax.ppermute(value, axis, [(i, (i + step) % count) for i in range(count)])]
    ppermute x22, waiting for transfers between devices: 17.9 us -> 16.2 us  [crossed(): return lax.ppermute(value, axis, [(i, i ^ mask) for i in range(count)])]
    ppermute x2, starting transfers between devices: 2.86 us -> 1.42 us  [faces_of(): lax.ppermute(x, 'space', [(i, (i + 1 if i % 2 else i - 1) % count) for i...]
    pallas_call x9 -> x11, Pallas kernels: 6.59 us -> 7.89 us  [the longest x2 2.15 us: middle(): pl.pallas_call(middle_kernel, out_shape=(half, half, pltpu.VMEM((vectors....]
    ppermute x2, waiting for transfers between devices: 0.01 us -> 1.04 us  [faces_of(): lax.ppermute(x, 'space', [(i, (i + 1 if i % 2 else i - 1) % count) for i...]
    ppermute x3, starting transfers between devices: 3.87 us -> 4.9 us  [crossed_both(): return lax.ppermute(value, (first, second), pairs)]
  transfers between devices with their start and end apart: 31 -> 35, of which waited for: 18 -> 15; matrix products, arithmetic and copies ran while one was open for 0% -> 0% of each run, Pallas kernels for 22% -> 25%
where the time goes in v10:
time: 95.8 us; the launch traced here: 95.5 us
  starting transfers between devices  40.6 us (42%)
  Pallas kernels  27.7 us (29%)
  waiting for transfers between devices  24.9 us (26%)
  local copies, waits for them, and re-layouts  1.13 us (1%)
  between operations  1.11 us (1%)
    ppermute x22, starting transfers between devices, crossed(): return lax.ppermute(value, axis, [(i, i ^ mask) for i in range(count)])  18.1 us
    ppermute x8, starting transfers between devices, shifted(): lax.ppermute(value, axis, [(i, (i + step) % count) for i in range(count)])  16.2 us
    ppermute x22, waiting for transfers between devices, crossed(): return lax.ppermute(value, axis, [(i, i ^ mask) for i in range(count)])  16.2 us
    pallas_call x1, Pallas kernels, first_local(): pl.pallas_call(functools.partial(first_kernel, ny, nx), grid=(sites,), ou...  7.69 us
    ppermute x8, waiting for transfers between devices, shifted(): lax.ppermute(value, axis, [(i, (i + step) % count) for i in range(count)])  5.06 us
    ppermute x3, starting transfers between devices, crossed_both(): return lax.ppermute(value, (first, second), pairs)  4.9 us
    pallas_call x1, Pallas kernels, vectors_parts(): pl.pallas_call(vectors_kernel, grid=(sites // step,), out_shape=(pltpu.VM...  4.24 us
    pallas_call x1, Pallas kernels, local_part(): pl.pallas_call(functools.partial(local_kernel, ny, nx), grid=(sites,), ou...  2.97 us
  transfers between devices with their start and end apart: 35, of which 15 were waited for; matrix products, arithmetic and copies ran while one was open for 0% of the time, Pallas kernels for 25%

profile of v10, /device:TPU:0, one launch (start us, length us, event | category | flops | bytes accessed | tf_op | source)
XLA Modules:
  0.0 95.5 jit_solution(4989274263920995521)
XLA Ops:
  0.6 1.1 %copy-done = f32[1,1,2,4,96,256]{5,4,3,2,1,0:T(8,128)S(1)} copy-done((f32[1,1,2,4,96,256]{5,4,3,2,1,0:T(8,128)S(1)}, f32[1,1,2,4,96,256]{5,4,3,2,1,0:T(8,128)}, u32[]{:S(2)}) %copy-start) | copy-done | bytes 786456
  2.6 2.6 %collective-permute-start.2 = (f32[4,96,128]{2,1,0:T(8,128)S(1)}, f32[4,96,128]{2,1,0:T(8,128)S(1)}, u32[]{:S(2)}, u32[]{:S(2)}) collective-permute-start(f32[4,96,128]{2,1,0:T(8,128)S(1)} %get-tuple-element.50), channel_id=1, source_target_pairs={{0,1},{1,2},{2,3},{3,0},{4,5},{5,6},{6,7},{7,4},{8,9},{9,10},{10,1... | collective-permute-start | bytes 589832 | tf_op jit(solution)/shard_map/ppermute | solution.py:575
  5.2 2.1 %collective-permute-start.3 = (f32[4,96,128]{2,1,0:T(8,128)S(1)}, f32[4,96,128]{2,1,0:T(8,128)S(1)}, u32[]{:S(2)}, u32[]{:S(2)}) collective-permute-start(f32[4,96,128]{2,1,0:T(8,128)S(1)} %get-tuple-element.50), channel_id=1, source_target_pairs={{0,3},{1,0},{2,1},{3,2},{4,7},{5,4},{6,5},{7,6},{8,11},{9,8},{10,9... | collective-permute-start | bytes 589832 | tf_op jit(solution)/shard_map/ppermute | solution.py:575
  7.3 1.2 %collective-permute-start.1 = (f32[8,96,128]{2,1,0:T(8,128)S(1)}, f32[8,96,128]{2,1,0:T(8,128)S(1)}, u32[]{:S(2)}, u32[]{:S(2)}) collective-permute-start(f32[8,96,128]{2,1,0:T(8,128)S(1)} %get-tuple-element.46.x_ref.x), channel_id=1, source_target_pairs={{0,12},{4,8},{8,4},{12,0},{1,13},{5,9},{9,5},{13,1},{2,14},{6,10},... | collective-permute-start | bytes 1179656 | tf_op jit(solution)/shard_map/ppermute | solution.py:593
  8.5 3.8 %collective-permute-start.5 = (f32[4,96,128]{2,1,0:T(8,128)S(1)}, f32[4,96,128]{2,1,0:T(8,128)S(1)}, u32[]{:S(2)}, u32[]{:S(2)}) collective-permute-start(f32[4,96,128]{2,1,0:T(8,128)S(1)} %get-tuple-element.56), channel_id=1, source_target_pairs={{0,3},{1,0},{2,1},{3,2},{4,7},{5,4},{6,5},{7,6},{8,11},{9,8},{10,9... | collective-permute-start | bytes 589832 | tf_op jit(solution)/shard_map/ppermute | solution.py:575
  12.3 7.7 %first_local.1 = (f32[8,96,128]{2,1,0:T(8,128)S(1)}, f32[8,96,128]{2,1,0:T(8,128)S(1)}, bf16[5,8,192,192]{3,2,1,0:T(8,128)(2,1)S(1)}, bf16[4,8,192,192]{3,2,1,0:T(8,128)(2,1)S(1)}) custom-call(f32[8,96,128]{2,1,0:T(8,128)S(1)} %get-tuple-element.46.x_ref.x, f32[8,96,256]{2,1,0:T(8,128)} %bitcast.13, f32[9,8,96,192]{3,2,1,0:T(8,128)} %bitcast.12), custom_call_target="tpu_custom_call" | custom-call | flops 8000000000 | bytes 16000000 | tf_op jit(solution)/shard_map/first_local/pallas_call | solution.py:156
  20.0 4.2 %vectors_parts.1 = (bf16[1024,1536]{1,0:T(8,128)(2,1)S(1)}, bf16[8,2,192,512]{3,2,1,0:T(8,128)(2,1)S(1)}) custom-call(f32[1536,512]{1,0:T(8,128)} %bitcast.9), custom_call_target="tpu_custom_call" | custom-call | flops 1000000 | bytes 9000000 | tf_op jit(solution)/shard_map/vectors_parts/pallas_call | solution.py:249
  24.8 1.1 %middle.2 = (f32[4,96,128]{2,1,0:T(8,128)S(1)}, f32[4,96,128]{2,1,0:T(8,128)S(1)}, f32[512,128]{1,0:T(8,128)S(1)}) custom-call(f32[8,96,128]{2,1,0:T(8,128)S(1)} %get-tuple-element.47.rest, f32[8,96,128]{2,1,0:T(8,128)S(1)} %collective-permute-done.near, f32[8,96,128]{2,1,0:T(8,128)S(1)} %collective-permute-done.1.far, f32[4,96,128]{2,1,0:T(8,128)S(1)} %front_faces.2.front, ...), custom_call_target="tpu_custom_call" | custom-call | flops 1000 | bytes 1000 | tf_op jit(solution)/shard_map/middle/pallas_call | solution.py:336
  26.2 0.9 forward_face.2
  27.2 1.3 %collective-permute-done.6.received = f32[256,128]{1,0:T(8,128)S(1)} collective-permute-done((f32[256,128]{1,0:T(8,128)S(1)}, f32[256,128]{1,0:T(8,128)S(1)}, u32[]{:S(2)}, u32[]{:S(2)}) %collective-permute-start.6) | collective-permute-done | bytes 131104 | tf_op jit(solution)/shard_map/ppermute | solution.py:580
  28.6 0.6 collective-permute-start.7
  29.2 0.8 collective-permute-start.8
  30.0 3.1 %collective-permute-start.9 = (f32[128,128]{1,0:T(8,128)S(1)}, f32[128,128]{1,0:T(8,128)S(1)}, u32[]{:S(2)}, u32[]{:S(2)}) collective-permute-start(f32[128,128]{1,0:T(8,128)S(1)} %get-tuple-element.62), channel_id=1, source_target_pairs={{0,10},{1,11},{2,8},{3,9},{4,14},{5,15},{6,12},{7,13},{8,2},{9,3},... | collective-permute-start | bytes 196616 | tf_op jit(solution)/shard_map/ppermute | solution.py:586
  33.2 4.0 %collective-permute-done.8.refs_2_ = f32[128,128]{1,0:T(8,128)S(1)} collective-permute-done((f32[128,128]{1,0:T(8,128)S(1)}, f32[128,128]{1,0:T(8,128)S(1)}, u32[]{:S(2)}, u32[]{:S(2)}) %collective-permute-start.8) | collective-permute-done | bytes 65568 | tf_op jit(solution)/shard_map/ppermute | solution.py:580
  37.2 1.2 %collective-permute-done.9.refs_3_ = f32[128,128]{1,0:T(8,128)S(1)} collective-permute-done((f32[128,128]{1,0:T(8,128)S(1)}, f32[128,128]{1,0:T(8,128)S(1)}, u32[]{:S(2)}, u32[]{:S(2)}) %collective-permute-start.9) | collective-permute-done | bytes 65568 | tf_op jit(solution)/shard_map/ppermute | solution.py:586
  38.5 1.3 %collective-permute-start.11 = (f32[128,128]{1,0:T(8,128)S(1)}, f32[128,128]{1,0:T(8,128)S(1)}, u32[]{:S(2)}, u32[]{:S(2)}) collective-permute-start(f32[128,128]{1,0:T(8,128)S(1)} %scale.2.left), channel_id=1, source_target_pairs={{0,8},{4,12},{8,0},{12,4},{1,9},{5,13},{9,1},{13,5},{2,10},{6,14},... | collective-permute-start | bytes 196616 | tf_op jit(solution)/shard_map/ppermute | solution.py:580
  39.8 2.2 %collective-permute-start.10 = (f32[128,128]{1,0:T(8,128)S(1)}, f32[128,128]{1,0:T(8,128)S(1)}, u32[]{:S(2)}, u32[]{:S(2)}) collective-permute-start(f32[128,128]{1,0:T(8,128)S(1)} %scale.2.left), channel_id=1, source_target_pairs={{0,1},{1,0},{2,3},{3,2},{4,5},{5,4},{6,7},{7,6},{8,9},{9,8},{10,11... | collective-permute-start | bytes 196616 | tf_op jit(solution)/shard_map/ppermute | solution.py:580
  42.0 1.5 %collective-permute-done.11.left = f32[128,128]{1,0:T(8,128)S(1)} collective-permute-done((f32[128,128]{1,0:T(8,128)S(1)}, f32[128,128]{1,0:T(8,128)S(1)}, u32[]{:S(2)}, u32[]{:S(2)}) %collective-permute-start.11) | collective-permute-done | bytes 65568 | tf_op jit(solution)/shard_map/ppermute | solution.py:580
  43.5 1.4 %collective-permute-done.12.right = f32[128,128]{1,0:T(8,128)S(1)} collective-permute-done((f32[128,128]{1,0:T(8,128)S(1)}, f32[128,128]{1,0:T(8,128)S(1)}, u32[]{:S(2)}, u32[]{:S(2)}) %collective-permute-start.12) | collective-permute-done | bytes 65568 | tf_op jit(solution)/shard_map/ppermute | solution.py:586
  45.1 0.5 collective-permute-start.13
  45.6 0.7 first_half.3.base
  46.5 0.7 second_half.2
  47.6 0.9 collective-permute-start.17
  48.5 2.9 %collective-permute-start.18 = (f32[4,96,128]{2,1,0:T(8,128)S(1)}, f32[4,96,128]{2,1,0:T(8,128)S(1)}, u32[]{:S(2)}, u32[]{:S(2)}) collective-permute-start(f32[4,96,128]{2,1,0:T(8,128)S(1)} %get-tuple-element.68), channel_id=1, source_target_pairs={{0,3},{1,0},{2,1},{3,2},{4,7},{5,4},{6,5},{7,6},{8,11},{9,8},{10,9... | collective-permute-start | bytes 589832 | tf_op jit(solution)/shard_map/ppermute | solution.py:575
  51.7 3.8 %collective-permute-start.20 = (f32[4,96,128]{2,1,0:T(8,128)S(1)}, f32[4,96,128]{2,1,0:T(8,128)S(1)}, u32[]{:S(2)}, u32[]{:S(2)}) collective-permute-start(f32[4,96,128]{2,1,0:T(8,128)S(1)} %get-tuple-element.73), channel_id=1, source_target_pairs={{0,3},{1,0},{2,1},{3,2},{4,7},{5,4},{6,5},{7,6},{8,11},{9,8},{10,9... | collective-permute-start | bytes 589832 | tf_op jit(solution)/shard_map/ppermute | solution.py:575
  55.5 3.0 %local_part.1.rest = f32[8,96,128]{2,1,0:T(8,128)S(1)} custom-call(f32[8,96,128]{2,1,0:T(8,128)S(1)} %get-tuple-element.79.x_ref.x, f32[8,96,128]{2,1,0:T(8,128)S(1)} %get-tuple-element.64.source, bf16[5,8,192,192]{3,2,1,0:T(8,128)(2,1)S(1)} %get-tuple-element.65.local), custom_call_target="tpu_custom_call" | custom-call | flops 8000000000 | bytes 8000000 | tf_op jit(solution)/shard_map/local_part/pallas_call | solution.py:191
  58.5 2.6 %collective-permute-done.18.forward = f32[4,96,128]{2,1,0:T(8,128)S(1)} collective-permute-done((f32[4,96,128]{2,1,0:T(8,128)S(1)}, f32[4,96,128]{2,1,0:T(8,128)S(1)}, u32[]{:S(2)}, u32[]{:S(2)}) %collective-permute-start.18) | collective-permute-done | bytes 196640 | tf_op jit(solution)/shard_map/ppermute | solution.py:575
  61.6 1.0 %collective-permute-done.16.far = f32[8,96,128]{2,1,0:T(8,128)S(1)} collective-permute-done((f32[8,96,128]{2,1,0:T(8,128)S(1)}, f32[8,96,128]{2,1,0:T(8,128)S(1)}, u32[]{:S(2)}, u32[]{:S(2)}) %collective-permute-start.16) | collective-permute-done | bytes 393248 | tf_op jit(solution)/shard_map/ppermute | solution.py:593
  62.7 1.1 %middle.3 = (f32[4,96,128]{2,1,0:T(8,128)S(1)}, f32[4,96,128]{2,1,0:T(8,128)S(1)}, f32[512,128]{1,0:T(8,128)S(1)}) custom-call(f32[8,96,128]{2,1,0:T(8,128)S(1)} %local_part.1.rest, f32[8,96,128]{2,1,0:T(8,128)S(1)} %collective-permute-done.15.near, f32[8,96,128]{2,1,0:T(8,128)S(1)} %collective-permute-done.16.far, f32[4,96,128]{2,1,0:T(8,128)S(1)} %front_faces.3.front, ...), custom_call_target="tpu_custom_call" | custom-call | flops 1000 | bytes 1000 | tf_op jit(solution)/shard_map/middle/pallas_call | solution.py:336
  63.7 1.6 %collective-permute-start.23 = (f32[8,96,128]{2,1,0:T(8,128)S(1)}, f32[8,96,128]{2,1,0:T(8,128)S(1)}, u32[]{:S(2)}, u32[]{:S(2)}) collective-permute-start(f32[8,96,128]{2,1,0:T(8,128)S(1)} %get-tuple-element.79.x_ref.x), channel_id=1, source_target_pairs={{0,16},{16,0},{1,17},{17,1},{2,18},{18,2},{3,19},{19,3},{4,20},{20... | collective-permute-start | bytes 1179656 | tf_op jit(solution)/shard_map/ppermute | solution.py:580
  66.0 2.0 %collective-permute-done.20.forward = f32[4,96,128]{2,1,0:T(8,128)S(1)} collective-permute-done((f32[4,96,128]{2,1,0:T(8,128)S(1)}, f32[4,96,128]{2,1,0:T(8,128)S(1)}, u32[]{:S(2)}, u32[]{:S(2)}) %collective-permute-start.20) | collective-permute-done | bytes 196640 | tf_op jit(solution)/shard_map/ppermute | solution.py:575
  68.1 0.9 forward_face.3
  69.1 1.3 %collective-permute-done.21.received = f32[256,128]{1,0:T(8,128)S(1)} collective-permute-done((f32[256,128]{1,0:T(8,128)S(1)}, f32[256,128]{1,0:T(8,128)S(1)}, u32[]{:S(2)}, u32[]{:S(2)}) %collective-permute-start.21) | collective-permute-done | bytes 131104 | tf_op jit(solution)/shard_map/ppermute | solution.py:580
  70.4 1.3 %collective-permute-start.22 = (f32[128,128]{1,0:T(8,128)S(1)}, f32[128,128]{1,0:T(8,128)S(1)}, u32[]{:S(2)}, u32[]{:S(2)}) collective-permute-start(f32[128,128]{1,0:T(8,128)S(1)} %get-tuple-element.77), channel_id=1, source_target_pairs={{0,8},{4,12},{8,0},{12,4},{1,9},{5,13},{9,1},{13,5},{2,10},{6,14},... | collective-permute-start | bytes 196616 | tf_op jit(solution)/shard_map/ppermute | solution.py:580
  71.8 3.0 %collective-permute-done.22.right = f32[128,128]{1,0:T(8,128)S(1)} collective-permute-done((f32[128,128]{1,0:T(8,128)S(1)}, f32[128,128]{1,0:T(8,128)S(1)}, u32[]{:S(2)}, u32[]{:S(2)}) %collective-permute-start.22) | collective-permute-done | bytes 65568 | tf_op jit(solution)/shard_map/ppermute | solution.py:580
  74.8 1.6 %collective-permute-start.30 = (f32[8,96,128]{2,1,0:T(8,128)S(1)}, f32[8,96,128]{2,1,0:T(8,128)S(1)}, u32[]{:S(2)}, u32[]{:S(2)}) collective-permute-start(f32[8,96,128]{2,1,0:T(8,128)S(1)} %get-tuple-element.81.own.residual), channel_id=1, source_target_pairs={{0,16},{16,0},{1,17},{17,1},{2,18},{18,2},{3,19},{19,3},{4,20},{20... | collective-permute-start | bytes 1179656 | tf_op jit(solution)/shard_map/ppermute | solution.py:580
  76.4 1.0 %collective-permute-start.24 = (f32[128,128]{1,0:T(8,128)S(1)}, f32[128,128]{1,0:T(8,128)S(1)}, u32[]{:S(2)}, u32[]{:S(2)}) collective-permute-start(f32[128,128]{1,0:T(8,128)S(1)} %add.5.refs_0_), channel_id=1, source_target_pairs={{0,1},{1,0},{2,3},{3,2},{4,5},{5,4},{6,7},{7,6},{8,9},{9,8},{10,11... | collective-permute-start | bytes 196616 | tf_op jit(solution)/shard_map/ppermute | solution.py:580
  77.4 1.7 %collective-permute-start.25 = (f32[128,128]{1,0:T(8,128)S(1)}, f32[128,128]{1,0:T(8,128)S(1)}, u32[]{:S(2)}, u32[]{:S(2)}) collective-permute-start(f32[128,128]{1,0:T(8,128)S(1)} %add.5.refs_0_), channel_id=1, source_target_pairs={{0,2},{1,3},{2,0},{3,1},{4,6},{5,7},{6,4},{7,5},{8,10},{9,11},{10,... | collective-permute-start | bytes 196616 | tf_op jit(solution)/shard_map/ppermute | solution.py:580
  79.1 1.7 %collective-permute-start.26 = (f32[128,128]{1,0:T(8,128)S(1)}, f32[128,128]{1,0:T(8,128)S(1)}, u32[]{:S(2)}, u32[]{:S(2)}) collective-permute-start(f32[128,128]{1,0:T(8,128)S(1)} %add.5.refs_0_), channel_id=1, source_target_pairs={{0,3},{1,2},{2,1},{3,0},{4,7},{5,6},{6,5},{7,4},{8,11},{9,10},{10,... | collective-permute-start | bytes 196616 | tf_op jit(solution)/shard_map/ppermute | solution.py:580
  80.8 3.0 %collective-permute-done.25.refs_2_ = f32[128,128]{1,0:T(8,128)S(1)} collective-permute-done((f32[128,128]{1,0:T(8,128)S(1)}, f32[128,128]{1,0:T(8,128)S(1)}, u32[]{:S(2)}, u32[]{:S(2)}) %collective-permute-start.25) | collective-permute-done | bytes 65568 | tf_op jit(solution)/shard_map/ppermute | solution.py:580
  83.8 1.4 %collective-permute-done.26.refs_3_ = f32[128,128]{1,0:T(8,128)S(1)} collective-permute-done((f32[128,128]{1,0:T(8,128)S(1)}, f32[128,128]{1,0:T(8,128)S(1)}, u32[]{:S(2)}, u32[]{:S(2)}) %collective-permute-start.26) | collective-permute-done | bytes 65568 | tf_op jit(solution)/shard_map/ppermute | solution.py:580
  85.3 1.2 %collective-permute-start.29 = (f32[128,128]{1,0:T(8,128)S(1)}, f32[128,128]{1,0:T(8,128)S(1)}, u32[]{:S(2)}, u32[]{:S(2)}) collective-permute-start(f32[128,128]{1,0:T(8,128)S(1)} %scale.3.refs_0_), channel_id=1, source_target_pairs={{0,8},{4,12},{8,0},{12,4},{1,9},{5,13},{9,1},{13,5},{2,10},{6,14},... | collective-permute-start | bytes 196616 | tf_op jit(solution)/shard_map/ppermute | solution.py:580
  87.0 1.8 %collective-permute-start.27 = (f32[128,128]{1,0:T(8,128)S(1)}, f32[128,128]{1,0:T(8,128)S(1)}, u32[]{:S(2)}, u32[]{:S(2)}) collective-permute-start(f32[128,128]{1,0:T(8,128)S(1)} %scale.3.refs_0_), channel_id=1, source_target_pairs={{0,24},{4,28},{8,16},{12,20},{16,8},{20,12},{24,0},{28,4},{1,25},{... | collective-permute-start | bytes 196616 | tf_op jit(solution)/shard_map/ppermute | solution.py:586
  88.9 1.0 %join.1 = f32[8,96,256]{2,1,0:T(8,128)} custom-call(f32[8,96,128]{2,1,0:T(8,128)S(1)} %get-tuple-element.81.own.residual, f32[8,96,128]{2,1,0:T(8,128)S(1)} %collective-permute-done.30.other.residual), custom_call_target="tpu_custom_call" | custom-call | flops 1000000 | bytes 2000000 | tf_op jit(solution)/shard_map/join/pallas_call | solution.py:529
  90.2 0.7 first_half.4.base
  91.2 1.3 %second_half.3 = (f32[8,96,128]{2,1,0:T(8,128)S(1)}, f32[4,96,128]{2,1,0:T(8,128)}, f32[4,96,128]{2,1,0:T(8,128)}) custom-call(f32[8,96,128]{2,1,0:T(8,128)S(1)} %first_half.4.base, bf16[8,2,192,512]{3,2,1,0:T(8,128)(2,1)S(1)} %get-tuple-element.58.vectors, f32[128,128]{1,0:T(8,128)S(1)} %collective-permute-done.31.refs_0_, ...), custom_call_target="tpu_custom_call" | custom-call | flops 1000000000 | bytes 4000000 | tf_op jit(solution)/shard_map/second_half/pallas_call | solution.py:503
  92.8 0.7 first_half.5.other
  93.8 1.5 %final.1 = f32[8,96,256]{2,1,0:T(8,128)} custom-call(f32[8,96,128]{2,1,0:T(8,128)S(1)} %get-tuple-element.85.own, f32[8,96,128]{2,1,0:T(8,128)S(1)} %first_half.5.other, bf16[8,2,192,512]{3,2,1,0:T(8,128)(2,1)S(1)} %get-tuple-element.58.vectors, f32[128,128]{1,0:T(8,128)S(1)} %collective-permute-done.33.refs_0_, f32[128,128]{1,0:T(8,128)S(1)} %collective-permute-done.34.refs_1_), custom_call_target="tpu_custom_call" | custom-call | flops 1000000000 | bytes 4000000 | tf_op jit(solution)/shard_map/final/pallas_call | solution.py:557
  (53 shorter events, 6.0 us)
Async XLA Ops:
  0.6 1.1 %copy-start = (f32[1,1,2,4,96,256]{5,4,3,2,1,0:T(8,128)S(1)}, f32[1,1,2,4,96,256]{5,4,3,2,1,0:T(8,128)}, u32[]{:S(2)}) copy-start(f32[1,1,2,4,96,256]{5,4,3,2,1,0:T(8,128)} %param.7) | copy-start | bytes 2359300
  2.0 6.4 %collective-permute-start = (f32[8,96,128]{2,1,0:T(8,128)S(1)}, f32[8,96,128]{2,1,0:T(8,128)S(1)}, u32[]{:S(2)}, u32[]{:S(2)}) collective-permute-start(f32[8,96,128]{2,1,0:T(8,128)S(1)} %get-tuple-element.46.x_ref.x), channel_id=1, source_target_pairs={{0,4},{4,0},{8,12},{12,8},{1,5},{5,1},{9,13},{13,9},{2,6},{6,2},{1... | collective-permute-start | bytes 1179656 | tf_op jit(solution)/shard_map/ppermute | solution.py:580
  2.6 21.7 %collective-permute-start.2 = (f32[4,96,128]{2,1,0:T(8,128)S(1)}, f32[4,96,128]{2,1,0:T(8,128)S(1)}, u32[]{:S(2)}, u32[]{:S(2)}) collective-permute-start(f32[4,96,128]{2,1,0:T(8,128)S(1)} %get-tuple-element.50), channel_id=1, source_target_pairs={{0,1},{1,2},{2,3},{3,0},{4,5},{5,6},{6,7},{7,4},{8,9},{9,10},{10,1... | collective-permute-start | bytes 589832 | tf_op jit(solution)/shard_map/ppermute | solution.py:575
  5.2 19.1 %collective-permute-start.3 = (f32[4,96,128]{2,1,0:T(8,128)S(1)}, f32[4,96,128]{2,1,0:T(8,128)S(1)}, u32[]{:S(2)}, u32[]{:S(2)}) collective-permute-start(f32[4,96,128]{2,1,0:T(8,128)S(1)} %get-tuple-element.50), channel_id=1, source_target_pairs={{0,3},{1,0},{2,1},{3,2},{4,7},{5,4},{6,5},{7,6},{8,11},{9,8},{10,9... | collective-permute-start | bytes 589832 | tf_op jit(solution)/shard_map/ppermute | solution.py:575
  7.3 17.4 %collective-permute-start.1 = (f32[8,96,128]{2,1,0:T(8,128)S(1)}, f32[8,96,128]{2,1,0:T(8,128)S(1)}, u32[]{:S(2)}, u32[]{:S(2)}) collective-permute-start(f32[8,96,128]{2,1,0:T(8,128)S(1)} %get-tuple-element.46.x_ref.x), channel_id=1, source_target_pairs={{0,12},{4,8},{8,4},{12,0},{1,13},{5,9},{9,5},{13,1},{2,14},{6,10},... | collective-permute-start | bytes 1179656 | tf_op jit(solution)/shard_map/ppermute | solution.py:593
  8.5 17.4 %collective-permute-start.4 = (f32[4,96,128]{2,1,0:T(8,128)S(1)}, f32[4,96,128]{2,1,0:T(8,128)S(1)}, u32[]{:S(2)}, u32[]{:S(2)}) collective-permute-start(f32[4,96,128]{2,1,0:T(8,128)S(1)} %get-tuple-element.56), channel_id=1, source_target_pairs={{0,1},{1,2},{2,3},{3,0},{4,5},{5,6},{6,7},{7,4},{8,9},{9,10},{10,1... | collective-permute-start | bytes 589832 | tf_op jit(solution)/shard_map/ppermute | solution.py:575
  8.5 17.7 %collective-permute-start.5 = (f32[4,96,128]{2,1,0:T(8,128)S(1)}, f32[4,96,128]{2,1,0:T(8,128)S(1)}, u32[]{:S(2)}, u32[]{:S(2)}) collective-permute-start(f32[4,96,128]{2,1,0:T(8,128)S(1)} %get-tuple-element.56), channel_id=1, source_target_pairs={{0,3},{1,0},{2,1},{3,2},{4,7},{5,4},{6,5},{7,6},{8,11},{9,8},{10,9... | collective-permute-start | bytes 589832 | tf_op jit(solution)/shard_map/ppermute | solution.py:575
  26.2 6.8 %copy-start.1 = (f32[2,512]{1,0:T(2,128)S(1)}, f32[2,512]{1,0:T(2,128)}, u32[]{:S(2)}) copy-start(f32[2,512]{1,0:T(2,128)} %inverse.1) | copy-start | bytes 12292
  27.2 1.4 %collective-permute-start.6 = (f32[256,128]{1,0:T(8,128)S(1)}, f32[256,128]{1,0:T(8,128)S(1)}, u32[]{:S(2)}, u32[]{:S(2)}) collective-permute-start(f32[256,128]{1,0:T(8,128)S(1)} %get-tuple-element.60), channel_id=1, source_target_pairs={{0,4},{4,0},{8,12},{12,8},{1,5},{5,1},{9,13},{13,9},{2,6},{6,2},{1... | collective-permute-start | bytes 393224 | tf_op jit(solution)/shard_map/ppermute | solution.py:580
  28.6 4.6 %collective-permute-start.7 = (f32[128,128]{1,0:T(8,128)S(1)}, f32[128,128]{1,0:T(8,128)S(1)}, u32[]{:S(2)}, u32[]{:S(2)}) collective-permute-start(f32[128,128]{1,0:T(8,128)S(1)} %get-tuple-element.62), channel_id=1, source_target_pairs={{0,8},{4,12},{8,0},{12,4},{1,9},{5,13},{9,1},{13,5},{2,10},{6,14},... | collective-permute-start | bytes 196616 | tf_op jit(solution)/shard_map/ppermute | solution.py:580
  29.2 8.0 %collective-permute-start.8 = (f32[128,128]{1,0:T(8,128)S(1)}, f32[128,128]{1,0:T(8,128)S(1)}, u32[]{:S(2)}, u32[]{:S(2)}) collective-permute-start(f32[128,128]{1,0:T(8,128)S(1)} %get-tuple-element.61.refs_0_), channel_id=1, source_target_pairs={{0,2},{1,3},{2,0},{3,1},{4,6},{5,7},{6,4},{7,5},{8,10},{9,11},{10,... | collective-permute-start | bytes 196616 | tf_op jit(solution)/shard_map/ppermute | solution.py:580
  30.0 8.4 %collective-permute-start.9 = (f32[128,128]{1,0:T(8,128)S(1)}, f32[128,128]{1,0:T(8,128)S(1)}, u32[]{:S(2)}, u32[]{:S(2)}) collective-permute-start(f32[128,128]{1,0:T(8,128)S(1)} %get-tuple-element.62), channel_id=1, source_target_pairs={{0,10},{1,11},{2,8},{3,9},{4,14},{5,15},{6,12},{7,13},{8,2},{9,3},... | collective-permute-start | bytes 196616 | tf_op jit(solution)/shard_map/ppermute | solution.py:586
  38.5 5.0 %collective-permute-start.11 = (f32[128,128]{1,0:T(8,128)S(1)}, f32[128,128]{1,0:T(8,128)S(1)}, u32[]{:S(2)}, u32[]{:S(2)}) collective-permute-start(f32[128,128]{1,0:T(8,128)S(1)} %scale.2.left), channel_id=1, source_target_pairs={{0,8},{4,12},{8,0},{12,4},{1,9},{5,13},{9,1},{13,5},{2,10},{6,14},... | collective-permute-start | bytes 196616 | tf_op jit(solution)/shard_map/ppermute | solution.py:580
  39.8 5.2 %collective-permute-start.12 = (f32[128,128]{1,0:T(8,128)S(1)}, f32[128,128]{1,0:T(8,128)S(1)}, u32[]{:S(2)}, u32[]{:S(2)}) collective-permute-start(f32[128,128]{1,0:T(8,128)S(1)} %scale.2.left), channel_id=1, source_target_pairs={{0,9},{1,8},{2,11},{3,10},{4,13},{5,12},{6,15},{7,14},{8,1},{9,0},... | collective-permute-start | bytes 196616 | tf_op jit(solution)/shard_map/ppermute | solution.py:586
  39.8 5.3 %collective-permute-start.10 = (f32[128,128]{1,0:T(8,128)S(1)}, f32[128,128]{1,0:T(8,128)S(1)}, u32[]{:S(2)}, u32[]{:S(2)}) collective-permute-start(f32[128,128]{1,0:T(8,128)S(1)} %scale.2.left), channel_id=1, source_target_pairs={{0,1},{1,0},{2,3},{3,2},{4,5},{5,4},{6,7},{7,6},{8,9},{9,8},{10,11... | collective-permute-start | bytes 196616 | tf_op jit(solution)/shard_map/ppermute | solution.py:580
  45.0 1.3 %collective-permute-start.14 = (f32[128,128]{1,0:T(8,128)S(1)}, f32[128,128]{1,0:T(8,128)S(1)}, u32[]{:S(2)}, u32[]{:S(2)}) collective-permute-start(f32[128,128]{1,0:T(8,128)S(1)} %add.4.refs_1_), channel_id=1, source_target_pairs={{0,4},{4,0},{8,12},{12,8},{1,5},{5,1},{9,13},{13,9},{2,6},{6,2},{1... | collective-permute-start | bytes 196616 | tf_op jit(solution)/shard_map/ppermute | solution.py:580
  45.1 1.5 %collective-permute-start.13 = (f32[128,128]{1,0:T(8,128)S(1)}, f32[128,128]{1,0:T(8,128)S(1)}, u32[]{:S(2)}, u32[]{:S(2)}) collective-permute-start(f32[128,128]{1,0:T(8,128)S(1)} %add.3.refs_0_), channel_id=1, source_target_pairs={{0,4},{4,0},{8,12},{12,8},{1,5},{5,1},{9,13},{13,9},{2,6},{6,2},{1... | collective-permute-start | bytes 196616 | tf_op jit(solution)/shard_map/ppermute | solution.py:580
  47.2 4.5 %collective-permute-start.15 = (f32[8,96,128]{2,1,0:T(8,128)S(1)}, f32[8,96,128]{2,1,0:T(8,128)S(1)}, u32[]{:S(2)}, u32[]{:S(2)}) collective-permute-start(f32[8,96,128]{2,1,0:T(8,128)S(1)} %get-tuple-element.79.x_ref.x), channel_id=1, source_target_pairs={{0,4},{4,0},{8,12},{12,8},{1,5},{5,1},{9,13},{13,9},{2,6},{6,2},{1... | collective-permute-start | bytes 1179656 | tf_op jit(solution)/shard_map/ppermute | solution.py:580
  47.6 10.9 %collective-permute-start.17 = (f32[4,96,128]{2,1,0:T(8,128)S(1)}, f32[4,96,128]{2,1,0:T(8,128)S(1)}, u32[]{:S(2)}, u32[]{:S(2)}) collective-permute-start(f32[4,96,128]{2,1,0:T(8,128)S(1)} %get-tuple-element.68), channel_id=1, source_target_pairs={{0,1},{1,2},{2,3},{3,0},{4,5},{5,6},{6,7},{7,4},{8,9},{9,10},{10,1... | collective-permute-start | bytes 589832 | tf_op jit(solution)/shard_map/ppermute | solution.py:575
  48.5 12.6 %collective-permute-start.18 = (f32[4,96,128]{2,1,0:T(8,128)S(1)}, f32[4,96,128]{2,1,0:T(8,128)S(1)}, u32[]{:S(2)}, u32[]{:S(2)}) collective-permute-start(f32[4,96,128]{2,1,0:T(8,128)S(1)} %get-tuple-element.68), channel_id=1, source_target_pairs={{0,3},{1,0},{2,1},{3,2},{4,7},{5,4},{6,5},{7,6},{8,11},{9,8},{10,9... | collective-permute-start | bytes 589832 | tf_op jit(solution)/shard_map/ppermute | solution.py:575
  51.5 11.2 %collective-permute-start.16 = (f32[8,96,128]{2,1,0:T(8,128)S(1)}, f32[8,96,128]{2,1,0:T(8,128)S(1)}, u32[]{:S(2)}, u32[]{:S(2)}) collective-permute-start(f32[8,96,128]{2,1,0:T(8,128)S(1)} %get-tuple-element.79.x_ref.x), channel_id=1, source_target_pairs={{0,12},{4,8},{8,4},{12,0},{1,13},{5,9},{9,5},{13,1},{2,14},{6,10},... | collective-permute-start | bytes 1179656 | tf_op jit(solution)/shard_map/ppermute | solution.py:593
  51.7 14.0 %collective-permute-start.19 = (f32[4,96,128]{2,1,0:T(8,128)S(1)}, f32[4,96,128]{2,1,0:T(8,128)S(1)}, u32[]{:S(2)}, u32[]{:S(2)}) collective-permute-start(f32[4,96,128]{2,1,0:T(8,128)S(1)} %get-tuple-element.73), channel_id=1, source_target_pairs={{0,1},{1,2},{2,3},{3,0},{4,5},{5,6},{6,7},{7,4},{8,9},{9,10},{10,1... | collective-permute-start | bytes 589832 | tf_op jit(solution)/shard_map/ppermute | solution.py:575
  51.7 16.4 %collective-permute-start.20 = (f32[4,96,128]{2,1,0:T(8,128)S(1)}, f32[4,96,128]{2,1,0:T(8,128)S(1)}, u32[]{:S(2)}, u32[]{:S(2)}) collective-permute-start(f32[4,96,128]{2,1,0:T(8,128)S(1)} %get-tuple-element.73), channel_id=1, source_target_pairs={{0,3},{1,0},{2,1},{3,2},{4,7},{5,4},{6,5},{7,6},{8,11},{9,8},{10,9... | collective-permute-start | bytes 589832 | tf_op jit(solution)/shard_map/ppermute | solution.py:575
  63.7 11.1 %collective-permute-start.23 = (f32[8,96,128]{2,1,0:T(8,128)S(1)}, f32[8,96,128]{2,1,0:T(8,128)S(1)}, u32[]{:S(2)}, u32[]{:S(2)}) collective-permute-start(f32[8,96,128]{2,1,0:T(8,128)S(1)} %get-tuple-element.79.x_ref.x), channel_id=1, source_target_pairs={{0,16},{16,0},{1,17},{17,1},{2,18},{18,2},{3,19},{19,3},{4,20},{20... | collective-permute-start | bytes 1179656 | tf_op jit(solution)/shard_map/ppermute | solution.py:580
  69.0 1.4 %collective-permute-start.21 = (f32[256,128]{1,0:T(8,128)S(1)}, f32[256,128]{1,0:T(8,128)S(1)}, u32[]{:S(2)}, u32[]{:S(2)}) collective-permute-start(f32[256,128]{1,0:T(8,128)S(1)} %get-tuple-element.75), channel_id=1, source_target_pairs={{0,4},{4,0},{8,12},{12,8},{1,5},{5,1},{9,13},{13,9},{2,6},{6,2},{1... | collective-permute-start | bytes 393224 | tf_op jit(solution)/shard_map/ppermute | solution.py:580
  70.4 4.3 %collective-permute-start.22 = (f32[128,128]{1,0:T(8,128)S(1)}, f32[128,128]{1,0:T(8,128)S(1)}, u32[]{:S(2)}, u32[]{:S(2)}) collective-permute-start(f32[128,128]{1,0:T(8,128)S(1)} %get-tuple-element.77), channel_id=1, source_target_pairs={{0,8},{4,12},{8,0},{12,4},{1,9},{5,13},{9,1},{13,5},{2,10},{6,14},... | collective-permute-start | bytes 196616 | tf_op jit(solution)/shard_map/ppermute | solution.py:580
  74.8 14.1 %collective-permute-start.30 = (f32[8,96,128]{2,1,0:T(8,128)S(1)}, f32[8,96,128]{2,1,0:T(8,128)S(1)}, u32[]{:S(2)}, u32[]{:S(2)}) collective-permute-start(f32[8,96,128]{2,1,0:T(8,128)S(1)} %get-tuple-element.81.own.residual), channel_id=1, source_target_pairs={{0,16},{16,0},{1,17},{17,1},{2,18},{18,2},{3,19},{19,3},{4,20},{20... | collective-permute-start | bytes 1179656 | tf_op jit(solution)/shard_map/ppermute | solution.py:580
  76.4 4.4 %collective-permute-start.24 = (f32[128,128]{1,0:T(8,128)S(1)}, f32[128,128]{1,0:T(8,128)S(1)}, u32[]{:S(2)}, u32[]{:S(2)}) collective-permute-start(f32[128,128]{1,0:T(8,128)S(1)} %add.5.refs_0_), channel_id=1, source_target_pairs={{0,1},{1,0},{2,3},{3,2},{4,5},{5,4},{6,7},{7,6},{8,9},{9,8},{10,11... | collective-permute-start | bytes 196616 | tf_op jit(solution)/shard_map/ppermute | solution.py:580
  77.4 6.4 %collective-permute-start.25 = (f32[128,128]{1,0:T(8,128)S(1)}, f32[128,128]{1,0:T(8,128)S(1)}, u32[]{:S(2)}, u32[]{:S(2)}) collective-permute-start(f32[128,128]{1,0:T(8,128)S(1)} %add.5.refs_0_), channel_id=1, source_target_pairs={{0,2},{1,3},{2,0},{3,1},{4,6},{5,7},{6,4},{7,5},{8,10},{9,11},{10,... | collective-permute-start | bytes 196616 | tf_op jit(solution)/shard_map/ppermute | solution.py:580
  79.1 6.1 %collective-permute-start.26 = (f32[128,128]{1,0:T(8,128)S(1)}, f32[128,128]{1,0:T(8,128)S(1)}, u32[]{:S(2)}, u32[]{:S(2)}) collective-permute-start(f32[128,128]{1,0:T(8,128)S(1)} %add.5.refs_0_), channel_id=1, source_target_pairs={{0,3},{1,2},{2,1},{3,0},{4,7},{5,6},{6,5},{7,4},{8,11},{9,10},{10,... | collective-permute-start | bytes 196616 | tf_op jit(solution)/shard_map/ppermute | solution.py:580
  85.3 4.6 %collective-permute-start.29 = (f32[128,128]{1,0:T(8,128)S(1)}, f32[128,128]{1,0:T(8,128)S(1)}, u32[]{:S(2)}, u32[]{:S(2)}) collective-permute-start(f32[128,128]{1,0:T(8,128)S(1)} %scale.3.refs_0_), channel_id=1, source_target_pairs={{0,8},{4,12},{8,0},{12,4},{1,9},{5,13},{9,1},{13,5},{2,10},{6,14},... | collective-permute-start | bytes 196616 | tf_op jit(solution)/shard_map/ppermute | solution.py:580
  86.5 4.3 %collective-permute-start.28 = (f32[128,128]{1,0:T(8,128)S(1)}, f32[128,128]{1,0:T(8,128)S(1)}, u32[]{:S(2)}, u32[]{:S(2)}) collective-permute-start(f32[128,128]{1,0:T(8,128)S(1)} %scale.3.refs_0_), channel_id=1, source_target_pairs={{0,16},{16,0},{1,17},{17,1},{2,18},{18,2},{3,19},{19,3},{4,20},{20... | collective-permute-start | bytes 196616 | tf_op jit(solution)/shard_map/ppermute | solution.py:580
  87.0 4.2 %collective-permute-start.31 = (f32[128,128]{1,0:T(8,128)S(1)}, f32[128,128]{1,0:T(8,128)S(1)}, u32[]{:S(2)}, u32[]{:S(2)}) collective-permute-start(f32[128,128]{1,0:T(8,128)S(1)} %scale.3.refs_0_), channel_id=1, source_target_pairs={{0,4},{4,0},{8,12},{12,8},{1,5},{5,1},{9,13},{13,9},{2,6},{6,2},{1... | collective-permute-start | bytes 196616 | tf_op jit(solution)/shard_map/ppermute | solution.py:580
  87.0 5.5 %collective-permute-start.27 = (f32[128,128]{1,0:T(8,128)S(1)}, f32[128,128]{1,0:T(8,128)S(1)}, u32[]{:S(2)}, u32[]{:S(2)}) collective-permute-start(f32[128,128]{1,0:T(8,128)S(1)} %scale.3.refs_0_), channel_id=1, source_target_pairs={{0,24},{4,28},{8,16},{12,20},{16,8},{20,12},{24,0},{28,4},{1,25},{... | collective-permute-start | bytes 196616 | tf_op jit(solution)/shard_map/ppermute | solution.py:586
  89.9 1.3 %collective-permute-start.32 = (f32[128,128]{1,0:T(8,128)S(1)}, f32[128,128]{1,0:T(8,128)S(1)}, u32[]{:S(2)}, u32[]{:S(2)}) collective-permute-start(f32[128,128]{1,0:T(8,128)S(1)} %collective-permute-done.29.refs_1_), channel_id=1, source_target_pairs={{0,4},{4,0},{8,12},{12,8},{1,5},{5,1},{9,13},{13,9},{2,6},{6,2},{1... | collective-permute-start | bytes 196616 | tf_op jit(solution)/shard_map/ppermute | solution.py:580
  90.9 2.6 %collective-permute-start.33 = (f32[128,128]{1,0:T(8,128)S(1)}, f32[128,128]{1,0:T(8,128)S(1)}, u32[]{:S(2)}, u32[]{:S(2)}) collective-permute-start(f32[128,128]{1,0:T(8,128)S(1)} %collective-permute-done.28.refs_0_), channel_id=1, source_target_pairs={{0,4},{4,0},{8,12},{12,8},{1,5},{5,1},{9,13},{13,9},{2,6},{6,2},{1... | collective-permute-start | bytes 196616 | tf_op jit(solution)/shard_map/ppermute | solution.py:580
  92.6 1.3 %collective-permute-start.34 = (f32[128,128]{1,0:T(8,128)S(1)}, f32[128,128]{1,0:T(8,128)S(1)}, u32[]{:S(2)}, u32[]{:S(2)}) collective-permute-start(f32[128,128]{1,0:T(8,128)S(1)} %collective-permute-done.27.refs_1_), channel_id=1, source_target_pairs={{0,4},{4,0},{8,12},{12,8},{1,5},{5,1},{9,13},{13,9},{2,6},{6,2},{1... | collective-permute-start | bytes 196616 | tf_op jit(solution)/shard_map/ppermute | solution.py:580

commit v11 on v10

--- a/solution.py
+++ b/solution.py
@@ -116,88 +116,87 @@
 
 
 def around(site, ny, nx):
-    y, x = site // nx, lax.rem(site, nx)
-    right, left = lax.rem(x + 1, nx), lax.rem(x + nx - 1, nx)
-    up, down = lax.rem(y + 1, ny), lax.rem(y + ny - 1, ny)
+    y, x = site // nx, site % nx
+    right, left = (x + 1) % nx, (x - 1) % nx
+    up, down = (y + 1) % ny, (y - 1) % ny
     return (site, y * nx + right, y * nx + left, up * nx + x, down * nx + x)
 
 
-def local_sum(site, ny, nx, x_ref, stacks, matrix):
-    @pl.when(site == 0)
-    def _():
-        for each in range(ny * nx):
-            stacks[each] = stack(x_ref[each], 1.0)
-
+def local_sum(site, ny, nx, stacks, local):
     total = None
     for direction, neighbour in enumerate(around(site, ny, nx)):
-        term = matmul(matrix(direction), stacks[neighbour])
+        term = matmul(local[direction, site], stacks[neighbour])
         total = term if total is None else total + term
     return fold(total)
 
 
-def first_kernel(ny, nx, x_ref, source, couplings, rest, half_source, local, halo, stacks):
-    site = pl.program_id(0)
-    own = pick_half(source[0], lax.axis_index("groups"))
-    half_source[0] = own
-    for direction in range(couplings.shape[0]):
-        high, low = high_low(couplings[direction, 0])
-        both = jnp.concatenate([high, low], axis=0)
-        if direction < LOCAL:
-            local[direction, 0] = both
-        else:
-            halo[direction - LOCAL, 0] = both
-    rest[0] = own - local_sum(site, ny, nx, x_ref, stacks, lambda d: local[d, 0])
+def first_kernel(ny, nx, x_ref, source, couplings, rest, half_source, local, halo, stacks, held, held_source, sems):
+    group = lax.axis_index("groups")
+    sites = x_ref.shape[0]
+    copies = []
+    for site in range(sites):
+        copies.append(pltpu.make_async_copy(couplings.at[:, site], held.at[site], sems.at[site]))
+        copies[-1].start()
+    bring = pltpu.make_async_copy(source, held_source, sems.at[sites])
+    bring.start()
+    for site in range(sites):
+        stacks[site] = stack(x_ref[site], 1.0)
+    bring.wait()
+    for site in range(sites):
+        half_source[site] = pick_half(held_source[site], group)
+    for site in range(sites):
+        copies[site].wait()
+        for direction in range(couplings.shape[0]):
+            high, low = high_low(held[site, direction])
+            both = jnp.concatenate([high, low], axis=0)
+            if direction < LOCAL:
+                local[direction, site] = both
+            else:
+                halo[direction - LOCAL, site] = both
+        rest[site] = half_source[site] - local_sum(site, ny, nx, stacks, local)
 
 
 def first_local(x, source, couplings, ny, nx):
     sites, rows, lanes = x.shape
     directions, _, _, columns = couplings.shape
     outer = directions - LOCAL
+    in_place = pl.BlockSpec(memory_space=pl.ANY)
     return pl.pallas_call(
         functools.partial(first_kernel, ny, nx),
-        grid=(sites,),
         out_shape=(
             pltpu.VMEM(x.shape, F32),
             pltpu.VMEM(x.shape, F32),
             pltpu.VMEM((LOCAL, sites, 2 * rows, columns), BF16),
             pltpu.VMEM((outer, sites, 2 * rows, columns), BF16),
         ),
-        in_specs=[
-            pl.BlockSpec((sites, rows, lanes), lambda s: (0, 0, 0)),
-            pl.BlockSpec((1, rows, 2 * lanes), lambda s: (s, 0, 0)),
-            pl.BlockSpec((directions, 1, rows, columns), lambda s: (0, s, 0, 0)),
+        in_specs=vmem(1) + [in_place, in_place],
+        out_specs=tuple(vmem(4)),
+        scratch_shapes=[
+            pltpu.VMEM((sites, 2 * rows, 2 * lanes), BF16),
+            pltpu.VMEM((sites, directions, rows, columns), F32),
+            pltpu.VMEM(source.shape, F32),
+            pltpu.SemaphoreType.DMA((sites + 1,)),
         ],
-        out_specs=(
-            pl.BlockSpec((1, rows, lanes), lambda s: (s, 0, 0)),
-            pl.BlockSpec((1, rows, lanes), lambda s: (s, 0, 0)),
-            pl.BlockSpec((LOCAL, 1, 2 * rows, columns), lambda s: (0, s, 0, 0)),
-            pl.BlockSpec((outer, 1, 2 * rows, columns), lambda s: (0, s, 0, 0)),
-        ),
-        scratch_shapes=[pltpu.VMEM((sites, 2 * rows, 2 * lanes), BF16)],
-        compiler_params=params(),
+        compiler_params=params(20),
         cost_estimate=cost(8e9, 16e6),
         name="first_local",
     )(x, in_hbm(source), in_hbm(couplings))
 
 
 def local_kernel(ny, nx, x_ref, source, local, rest, stacks):
-    site = pl.program_id(0)
-    rest[0] = source[0] - local_sum(site, ny, nx, x_ref, stacks, lambda d: local[d, 0])
+    for site in range(x_ref.shape[0]):
+        stacks[site] = stack(x_ref[site], 1.0)
+    for site in range(x_ref.shape[0]):
+        rest[site] = source[site] - local_sum(site, ny, nx, stacks, local)
 
 
 def local_part(x, source, local, ny, nx):
     sites, rows, lanes = x.shape
-    columns = local.shape[-1]
     return pl.pallas_call(
         functools.partial(local_kernel, ny, nx),
-        grid=(sites,),
         out_shape=pltpu.VMEM(x.shape, F32),
-        in_specs=[
-            pl.BlockSpec((sites, rows, lanes), lambda s: (0, 0, 0)),
-            pl.BlockSpec((1, rows, lanes), lambda s: (s, 0, 0)),
-            pl.BlockSpec((LOCAL, 1, 2 * rows, columns), lambda s: (0, s, 0, 0)),
-        ],
-        out_specs=pl.BlockSpec((1, rows, lanes), lambda s: (s, 0, 0)),
+        in_specs=vmem(3),
+        out_specs=vmem(1)[0],
         scratch_shapes=[pltpu.VMEM((sites, 2 * rows, 2 * lanes), BF16)],
         compiler_params=params(),
         cost_estimate=cost(8e9, 8e6),
@@ -222,44 +221,70 @@
     return parts[0] if len(parts) == 1 else jnp.concatenate(parts, axis=0)
 
 
-def vectors_kernel(across, by_rows, by_columns, turned_rows):
+def by_rows_kernel(across, by_rows, held, turned_rows, sems):
+    number = held.shape[1]
+    taken = 128
+    step = turned_rows.shape[1]
+    copies = []
+    for index in range(across.shape[0] // step):
+        at = pl.ds(index * step, step)
+        copies.append(pltpu.make_async_copy(across.at[at], held.at[at], sems.at[index]))
+        copies[-1].start()
+    for index, copy in enumerate(copies):
+        copy.wait()
+        at = slice(index * step, (index + 1) * step)
+        turned_rows[...] = held[at].T
+        for chunk in range(number // taken):
+            high, low = high_low(ordered_rows(turned_rows, chunk, taken))
+            by_rows[chunk * taken : (chunk + 1) * taken, at] = high
+            by_rows[number + chunk * taken : number + (chunk + 1) * taken, at] = low
+
+
+def by_rows_of(across, sites):
+    width, number = across.shape
+    step = width // (sites // 2)
+    return pl.pallas_call(
+        by_rows_kernel,
+        out_shape=pltpu.VMEM((2 * number, width), BF16),
+        in_specs=[pl.BlockSpec(memory_space=pl.ANY)],
+        out_specs=vmem(1)[0],
+        scratch_shapes=[
+            pltpu.VMEM((width, number), F32),
+            pltpu.VMEM((number, step), F32),
+            pltpu.SemaphoreType.DMA((width // step,)),
+        ],
+        compiler_params=params(),
+        cost_estimate=cost(1e6, 9e6),
+        name="by_rows",
+    )(in_hbm(across))
+
+
+def by_columns_kernel(by_rows, by_columns):
     sites, _, double, number = by_columns.shape
     rows = double // 2
     taken = 128
-    turned_rows[...] = across[...].T
-    for chunk in range(number // taken):
-        part = ordered_rows(turned_rows, chunk, taken)
-        high, low = high_low(part)
-        at = slice(chunk * taken, (chunk + 1) * taken)
-        by_rows[at] = high
-        by_rows[number + chunk * taken : number + (chunk + 1) * taken] = low
-        back = part.T
-        for site in range(sites):
-            for half in range(2):
-                start = (2 * site + half) * rows
-                high, low = high_low(back[start : start + rows])
-                by_columns[site, half, :rows, at] = high
-                by_columns[site, half, rows:, at] = low
-
-
-def vectors_parts(across, sites):
-    width, number = across.shape
-    rows = width // sites // 2
-    step = 2
-    return pl.pallas_call(
-        vectors_kernel,
-        grid=(sites // step,),
-        out_shape=(pltpu.VMEM((2 * number, width), BF16), pltpu.VMEM((sites, 2, 2 * rows, number), BF16)),
-        in_specs=[pl.BlockSpec((step * 2 * rows, number), lambda s: (s, 0))],
-        out_specs=(
-            pl.BlockSpec((2 * number, step * 2 * rows), lambda s: (0, s)),
-            pl.BlockSpec((step, 2, 2 * rows, number), lambda s: (s, 0, 0, 0)),
-        ),
-        scratch_shapes=[pltpu.VMEM((number, step * 2 * rows), F32)],
-        compiler_params=params(16),
-        cost_estimate=cost(1e6, 9e6),
-        name="vectors_parts",
-    )(in_hbm(across))
+    for part in range(2):
+        for chunk in range(number // taken):
+            start = part * number + chunk * taken
+            back = by_rows[start : start + taken].astype(F32).T.astype(BF16)
+            at = slice(chunk * taken, (chunk + 1) * taken)
+            for site in range(sites):
+                for half in range(2):
+                    start = (2 * site + half) * rows
+                    by_columns[site, half, part * rows : (part + 1) * rows, at] = back[start : start + rows]
+
+
+def by_columns_of(by_rows, sites):
+    number, width = by_rows.shape[0] // 2, by_rows.shape[1]
+    return pl.pallas_call(
+        by_columns_kernel,
+        out_shape=pltpu.VMEM((sites, 2, width // sites, number), BF16),
+        in_specs=vmem(1),
+        out_specs=vmem(1)[0],
+        compiler_params=params(),
+        cost_estimate=cost(1e6, 6e6),
+        name="by_columns",
+    )(by_rows)
 
 
 def eigen_kernel(inverse, out):
@@ -427,15 +452,18 @@
     )(left, right)
 
 
-def scaled_sum(keep, send, eigen):
+def scaled_sum(keep, send, eigen, by_rows, sites):
     blocks, slices = lax.axis_size("space"), lax.axis_size("tm")
+    by_rows, send = lax.optimization_barrier((by_rows, send))
+    by_columns = by_columns_of(by_rows, sites)
     if blocks != 4 or slices != 4:
-        return doubling([scale(eigen, over_time(halving(keep, send)))], blocks // 2)
+        return doubling([scale(eigen, over_time(halving(keep, send)))], blocks // 2), by_columns
     keep, send = add_split(keep, crossed(send, "space", 1))
     parts = [crossed(send, "space", 2), crossed(keep, "tm", 2), crossed_both(send, "space", 2, "tm", 2)]
+    parts[-1], by_columns = lax.optimization_barrier((parts[-1], by_columns))
     d = scale(eigen, [keep] + parts)
     moved, across = crossed(d, "space", 2), crossed_both(d, "space", 2, "tm", 1)
-    return [add(d, crossed(d, "tm", 1)), add(moved, across)]
+    return [add(d, crossed(d, "tm", 1)), add(moved, across)], by_columns
 
 
 def scale_kernel(eigen, *refs):
@@ -589,7 +617,7 @@
 def faces_of(x, front, back):
     count = lax.axis_size("space")
     early = shifted(front, "tm", 1), shifted(front, "tm", -1)
-    near, back = lax.optimization_barrier((crossed(x, "space", 1), back))
+    near, back, x = lax.optimization_barrier((crossed(x, "space", 1), back, x))
     far = lax.ppermute(x, "space", [(i, (i + 1 if i % 2 else i - 1) % count) for i in range(count)])
     late = shifted(back, "tm", 1), shifted(back, "tm", -1)
     return near, far, early, late
@@ -641,18 +669,18 @@
     number = vectors.shape[0]
     blocks = lax.axis_size("space")
 
-    x, front, back = pack(initial.reshape(sites, rows, lanes))
-    faces = faces_of(x, front, back)
+    x, early_x, late_x = pack(initial.reshape(sites, rows, lanes))
+    faces = faces_of(x, early_x, late_x)
     matrices = couplings.reshape(directions, sites, rows, couplings.shape[-1])
     rest, half_source, local, halo = first_local(x, source.reshape(sites, rows, lanes), matrices, ny, nx)
     across = jnp.transpose(vectors, (1, 2, 3, 4, 5, 0)).reshape(sites * vectors.shape[-1], number)
-    by_rows, by_columns = vectors_parts(across, sites)
+    by_rows = by_rows_of(across, sites)
     eigen = eigen_of(inverse_eigen, number // blocks, lanes // 2)
 
     for sweep in range(ITERS):
         last = sweep == ITERS - 1
         if sweep:
-            faces = faces_of(x, front, back)
+            faces = faces_of(x, early_x, late_x)
             rest = local_part(x, half_source, local, ny, nx)
         near, far, early, late = faces
         back_rest, own, partial = middle(rest, near, far, front_faces(*early, halo), halo, by_rows)
@@ -662,9 +690,9 @@
         back_rest = backward_face(back_rest, late[0], halo)
         residual, keep, send = forward_face(own, partial, back_rest, late[1], halo, by_rows)
         if not last:
-            pieces = scaled_sum(keep, send, eigen)
+            pieces, by_columns = scaled_sum(keep, send, eigen, by_rows, sites)
             base = first_half(x, residual, pieces, by_columns)
-            x, front, back = second_half(base, paired(pieces), by_columns)
+            x, early_x, late_x = second_half(base, paired(pieces), by_columns)
     part, residual, other_x = lax.optimization_barrier((halving(keep, send), residual, other_x))
     other_residual = crossed(residual, "groups", 1)
     d = scale(eigen, over_time(part))

time: 95.8 us -> 97.2 us (1.015)
  waiting for transfers between devices: 24.9 us -> 30.6 us
  Pallas kernels: 27.7 us -> 25 us
  starting transfers between devices: 40.6 us -> 39.3 us
    ppermute x2, waiting for transfers between devices: 1.04 us -> 4.31 us  [faces_of(): lax.ppermute(x, 'space', [(i, (i + 1 if i % 2 else i - 1) % count) for i...]
    pallas_call x3 -> x4, Pallas kernels: 14.9 us -> 12.2 us  [the longest x1 7.11 us: first_local(): pl.pallas_call(functools.partial(first_kernel, ny, nx), out_shape=(pltpu....]
    ppermute x3, waiting for transfers between devices: 2.67 us -> 4.06 us  [crossed_both(): return lax.ppermute(value, (first, second), pairs)]
  transfers between devices with their start and end apart: 35 -> 35, of which waited for: 15 -> 18; matrix products, arithmetic and copies ran while one was open for 0% -> 0% of each run, Pallas kernels for 25% -> 22%
where the time goes in v11:
time: 97.2 us; the launch traced here: 97 us
  starting transfers between devices  39.3 us (40%)
  waiting for transfers between devices  30.6 us (31%)
  Pallas kernels  25 us (26%)
  local copies, waits for them, and re-layouts  1.13 us (1%)
  between operations  1.08 us (1%)
    ppermute x22, starting transfers between devices, crossed(): return lax.ppermute(value, axis, [(i, i ^ mask) for i in range(count)])  17.1 us
    ppermute x22, waiting for transfers between devices, crossed(): return lax.ppermute(value, axis, [(i, i ^ mask) for i in range(count)])  16.3 us
    ppermute x8, starting transfers between devices, shifted(): lax.ppermute(value, axis, [(i, (i + step) % count) for i in range(count)])  16.2 us
    pallas_call x1, Pallas kernels, first_local(): pl.pallas_call(functools.partial(first_kernel, ny, nx), out_shape=(pltpu....  7.11 us
    ppermute x8, waiting for transfers between devices, shifted(): lax.ppermute(value, axis, [(i, (i + step) % count) for i in range(count)])  5.94 us
    ppermute x3, starting transfers between devices, crossed_both(): return lax.ppermute(value, (first, second), pairs)  5.26 us
    ppermute x2, waiting for transfers between devices, faces_of(): lax.ppermute(x, 'space', [(i, (i + 1 if i % 2 else i - 1) % count) for i...  4.31 us
    ppermute x3, waiting for transfers between devices, crossed_both(): return lax.ppermute(value, (first, second), pairs)  4.06 us
  transfers between devices with their start and end apart: 35, of which 18 were waited for; matrix products, arithmetic and copies ran while one was open for 0% of the time, Pallas kernels for 22%

profile of v11, /device:TPU:0, one launch (start us, length us, event | category | flops | bytes accessed | tf_op | source)
XLA Modules:
  0.0 97.0 jit_solution(14794935687098115684)
XLA Ops:
  0.6 1.1 %copy-done = f32[1,1,2,4,96,256]{5,4,3,2,1,0:T(8,128)S(1)} copy-done((f32[1,1,2,4,96,256]{5,4,3,2,1,0:T(8,128)S(1)}, f32[1,1,2,4,96,256]{5,4,3,2,1,0:T(8,128)}, u32[]{:S(2)}) %copy-start) | copy-done | bytes 786456
  2.6 2.6 %collective-permute-start.2 = (f32[4,96,128]{2,1,0:T(8,128)S(1)}, f32[4,96,128]{2,1,0:T(8,128)S(1)}, u32[]{:S(2)}, u32[]{:S(2)}) collective-permute-start(f32[4,96,128]{2,1,0:T(8,128)S(1)} %get-tuple-element.55), channel_id=1, source_target_pairs={{0,1},{1,2},{2,3},{3,0},{4,5},{5,6},{6,7},{7,4},{8,9},{9,10},{10,1... | collective-permute-start | bytes 589832 | tf_op jit(solution)/shard_map/ppermute | solution.py:603
  5.2 2.1 %collective-permute-start.3 = (f32[4,96,128]{2,1,0:T(8,128)S(1)}, f32[4,96,128]{2,1,0:T(8,128)S(1)}, u32[]{:S(2)}, u32[]{:S(2)}) collective-permute-start(f32[4,96,128]{2,1,0:T(8,128)S(1)} %get-tuple-element.55), channel_id=1, source_target_pairs={{0,3},{1,0},{2,1},{3,2},{4,7},{5,4},{6,5},{7,6},{8,11},{9,8},{10,9... | collective-permute-start | bytes 589832 | tf_op jit(solution)/shard_map/ppermute | solution.py:603
  7.3 3.8 %collective-permute-start.5 = (f32[4,96,128]{2,1,0:T(8,128)S(1)}, f32[4,96,128]{2,1,0:T(8,128)S(1)}, u32[]{:S(2)}, u32[]{:S(2)}) collective-permute-start(f32[4,96,128]{2,1,0:T(8,128)S(1)} %get-tuple-element.60), channel_id=1, source_target_pairs={{0,3},{1,0},{2,1},{3,2},{4,7},{5,4},{6,5},{7,6},{8,11},{9,8},{10,9... | collective-permute-start | bytes 589832 | tf_op jit(solution)/shard_map/ppermute | solution.py:603
  11.8 7.1 %first_local.1 = (f32[8,96,128]{2,1,0:T(8,128)S(1)}, f32[8,96,128]{2,1,0:T(8,128)S(1)}, bf16[5,8,192,192]{3,2,1,0:T(8,128)(2,1)S(1)}, bf16[4,8,192,192]{3,2,1,0:T(8,128)(2,1)S(1)}) custom-call(f32[8,96,128]{2,1,0:T(8,128)S(1)} %get-tuple-element.54.x_ref.x, f32[8,96,256]{2,1,0:T(8,128)} %bitcast.13, f32[9,8,96,192]{3,2,1,0:T(8,128)} %bitcast.12), custom_call_target="tpu_custom_call" | custom-call | flops 8000000000 | bytes 16000000 | tf_op jit(solution)/shard_map/first_local/pallas_call | solution.py:164
  18.9 2.9 %by_rows.1.vectors = bf16[1024,1536]{1,0:T(8,128)(2,1)S(1)} custom-call(f32[1536,512]{1,0:T(8,128)} %bitcast.9), custom_call_target="tpu_custom_call" | custom-call | flops 1000000 | bytes 9000000 | tf_op jit(solution)/shard_map/by_rows/pallas_call | solution.py:246
  22.4 1.1 %middle.2 = (f32[4,96,128]{2,1,0:T(8,128)S(1)}, f32[4,96,128]{2,1,0:T(8,128)S(1)}, f32[512,128]{1,0:T(8,128)S(1)}) custom-call(f32[8,96,128]{2,1,0:T(8,128)S(1)} %get-tuple-element.51.rest, f32[8,96,128]{2,1,0:T(8,128)S(1)} %collective-permute-done.near, f32[8,96,128]{2,1,0:T(8,128)S(1)} %collective-permute-done.1.far, f32[4,96,128]{2,1,0:T(8,128)S(1)} %front_faces.2.front, ...), custom_call_target="tpu_custom_call" | custom-call | flops 1000 | bytes 1000 | tf_op jit(solution)/shard_map/middle/pallas_call | solution.py:361
  23.8 1.0 %collective-permute-done.5.forward = f32[4,96,128]{2,1,0:T(8,128)S(1)} collective-permute-done((f32[4,96,128]{2,1,0:T(8,128)S(1)}, f32[4,96,128]{2,1,0:T(8,128)S(1)}, u32[]{:S(2)}, u32[]{:S(2)}) %collective-permute-start.5) | collective-permute-done | bytes 196640 | tf_op jit(solution)/shard_map/ppermute | solution.py:603
  24.8 0.9 forward_face.2
  25.9 1.2 %collective-permute-done.6.received = f32[256,128]{1,0:T(8,128)S(1)} collective-permute-done((f32[256,128]{1,0:T(8,128)S(1)}, f32[256,128]{1,0:T(8,128)S(1)}, u32[]{:S(2)}, u32[]{:S(2)}) %collective-permute-start.6) | collective-permute-done | bytes 131104 | tf_op jit(solution)/shard_map/ppermute | solution.py:608
  27.2 2.2 %collective-permute-start.7 = (f32[128,128]{1,0:T(8,128)S(1)}, f32[128,128]{1,0:T(8,128)S(1)}, u32[]{:S(2)}, u32[]{:S(2)}) collective-permute-start(f32[128,128]{1,0:T(8,128)S(1)} %get-tuple-element.65), channel_id=1, source_target_pairs={{0,10},{1,11},{2,8},{3,9},{4,14},{5,15},{6,12},{7,13},{8,2},{9,3},... | collective-permute-start | bytes 196616 | tf_op jit(solution)/shard_map/ppermute | solution.py:614
  29.9 1.7 %collective-permute-start.9 = (f32[128,128]{1,0:T(8,128)S(1)}, f32[128,128]{1,0:T(8,128)S(1)}, u32[]{:S(2)}, u32[]{:S(2)}) collective-permute-start(f32[128,128]{1,0:T(8,128)S(1)} %get-tuple-element.68.refs_0_), channel_id=1, source_target_pairs={{0,2},{1,3},{2,0},{3,1},{4,6},{5,7},{6,4},{7,5},{8,10},{9,11},{10,... | collective-permute-start | bytes 196616 | tf_op jit(solution)/shard_map/ppermute | solution.py:608
  31.8 0.9 by_columns.1.vectors
  32.7 2.6 %collective-permute-done.7.refs_3_ = f32[128,128]{1,0:T(8,128)S(1)} collective-permute-done((f32[128,128]{1,0:T(8,128)S(1)}, f32[128,128]{1,0:T(8,128)S(1)}, u32[]{:S(2)}, u32[]{:S(2)}) %collective-permute-start.7) | collective-permute-done | bytes 65568 | tf_op jit(solution)/shard_map/ppermute | solution.py:614
  35.2 2.2 %collective-permute-done.9.refs_2_ = f32[128,128]{1,0:T(8,128)S(1)} collective-permute-done((f32[128,128]{1,0:T(8,128)S(1)}, f32[128,128]{1,0:T(8,128)S(1)}, u32[]{:S(2)}, u32[]{:S(2)}) %collective-permute-start.9) | collective-permute-done | bytes 65568 | tf_op jit(solution)/shard_map/ppermute | solution.py:608
  37.6 1.2 %collective-permute-start.11 = (f32[128,128]{1,0:T(8,128)S(1)}, f32[128,128]{1,0:T(8,128)S(1)}, u32[]{:S(2)}, u32[]{:S(2)}) collective-permute-start(f32[128,128]{1,0:T(8,128)S(1)} %scale.2.left), channel_id=1, source_target_pairs={{0,8},{4,12},{8,0},{12,4},{1,9},{5,13},{9,1},{13,5},{2,10},{6,14},... | collective-permute-start | bytes 196616 | tf_op jit(solution)/shard_map/ppermute | solution.py:608
  38.8 2.3 %collective-permute-start.12 = (f32[128,128]{1,0:T(8,128)S(1)}, f32[128,128]{1,0:T(8,128)S(1)}, u32[]{:S(2)}, u32[]{:S(2)}) collective-permute-start(f32[128,128]{1,0:T(8,128)S(1)} %scale.2.left), channel_id=1, source_target_pairs={{0,9},{1,8},{2,11},{3,10},{4,13},{5,12},{6,15},{7,14},{8,1},{9,0},... | collective-permute-start | bytes 196616 | tf_op jit(solution)/shard_map/ppermute | solution.py:614
  41.1 1.2 %collective-permute-done.10.right = f32[128,128]{1,0:T(8,128)S(1)} collective-permute-done((f32[128,128]{1,0:T(8,128)S(1)}, f32[128,128]{1,0:T(8,128)S(1)}, u32[]{:S(2)}, u32[]{:S(2)}) %collective-permute-start.10) | collective-permute-done | bytes 65568 | tf_op jit(solution)/shard_map/ppermute | solution.py:608
  42.4 1.5 %collective-permute-done.12.right = f32[128,128]{1,0:T(8,128)S(1)} collective-permute-done((f32[128,128]{1,0:T(8,128)S(1)}, f32[128,128]{1,0:T(8,128)S(1)}, u32[]{:S(2)}, u32[]{:S(2)}) %collective-permute-start.12) | collective-permute-done | bytes 65568 | tf_op jit(solution)/shard_map/ppermute | solution.py:614
  44.0 0.7 first_half.3.base
  45.3 0.7 second_half.2
  46.2 1.5 %collective-permute-start.17 = (f32[4,96,128]{2,1,0:T(8,128)S(1)}, f32[4,96,128]{2,1,0:T(8,128)S(1)}, u32[]{:S(2)}, u32[]{:S(2)}) collective-permute-start(f32[4,96,128]{2,1,0:T(8,128)S(1)} %get-tuple-element.76), channel_id=1, source_target_pairs={{0,1},{1,2},{2,3},{3,0},{4,5},{5,6},{6,7},{7,4},{8,9},{9,10},{10,1... | collective-permute-start | bytes 589832 | tf_op jit(solution)/shard_map/ppermute | solution.py:603
  47.7 2.3 %collective-permute-start.18 = (f32[4,96,128]{2,1,0:T(8,128)S(1)}, f32[4,96,128]{2,1,0:T(8,128)S(1)}, u32[]{:S(2)}, u32[]{:S(2)}) collective-permute-start(f32[4,96,128]{2,1,0:T(8,128)S(1)} %get-tuple-element.76), channel_id=1, source_target_pairs={{0,3},{1,0},{2,1},{3,2},{4,7},{5,4},{6,5},{7,6},{8,11},{9,8},{10,9... | collective-permute-start | bytes 589832 | tf_op jit(solution)/shard_map/ppermute | solution.py:603
  50.0 3.8 %collective-permute-start.20 = (f32[4,96,128]{2,1,0:T(8,128)S(1)}, f32[4,96,128]{2,1,0:T(8,128)S(1)}, u32[]{:S(2)}, u32[]{:S(2)}) collective-permute-start(f32[4,96,128]{2,1,0:T(8,128)S(1)} %get-tuple-element.81), channel_id=1, source_target_pairs={{0,3},{1,0},{2,1},{3,2},{4,7},{5,4},{6,5},{7,6},{8,11},{9,8},{10,9... | collective-permute-start | bytes 589832 | tf_op jit(solution)/shard_map/ppermute | solution.py:603
  53.8 1.3 %local_part.1.rest = f32[8,96,128]{2,1,0:T(8,128)S(1)} custom-call(f32[8,96,128]{2,1,0:T(8,128)S(1)} %get-tuple-element.87.x_ref.x, f32[8,96,128]{2,1,0:T(8,128)S(1)} %get-tuple-element.71.source, bf16[5,8,192,192]{3,2,1,0:T(8,128)(2,1)S(1)} %get-tuple-element.72.local), custom_call_target="tpu_custom_call" | custom-call | flops 8000000000 | bytes 8000000 | tf_op jit(solution)/shard_map/local_part/pallas_call | solution.py:195
  55.7 4.3 %collective-permute-done.18.forward = f32[4,96,128]{2,1,0:T(8,128)S(1)} collective-permute-done((f32[4,96,128]{2,1,0:T(8,128)S(1)}, f32[4,96,128]{2,1,0:T(8,128)S(1)}, u32[]{:S(2)}, u32[]{:S(2)}) %collective-permute-start.18) | collective-permute-done | bytes 196640 | tf_op jit(solution)/shard_map/ppermute | solution.py:603
  60.5 4.2 %collective-permute-done.16.far = f32[8,96,128]{2,1,0:T(8,128)S(1)} collective-permute-done((f32[8,96,128]{2,1,0:T(8,128)S(1)}, f32[8,96,128]{2,1,0:T(8,128)S(1)}, u32[]{:S(2)}, u32[]{:S(2)}) %collective-permute-start.16) | collective-permute-done | bytes 393248 | tf_op jit(solution)/shard_map/ppermute | solution.py:621
  64.7 1.1 %middle.3 = (f32[4,96,128]{2,1,0:T(8,128)S(1)}, f32[4,96,128]{2,1,0:T(8,128)S(1)}, f32[512,128]{1,0:T(8,128)S(1)}) custom-call(f32[8,96,128]{2,1,0:T(8,128)S(1)} %local_part.1.rest, f32[8,96,128]{2,1,0:T(8,128)S(1)} %collective-permute-done.15.near, f32[8,96,128]{2,1,0:T(8,128)S(1)} %collective-permute-done.16.far, f32[4,96,128]{2,1,0:T(8,128)S(1)} %front_faces.3.front, ...), custom_call_target="tpu_custom_call" | custom-call | flops 1000 | bytes 1000 | tf_op jit(solution)/shard_map/middle/pallas_call | solution.py:361
  65.8 1.6 %collective-permute-start.23 = (f32[8,96,128]{2,1,0:T(8,128)S(1)}, f32[8,96,128]{2,1,0:T(8,128)S(1)}, u32[]{:S(2)}, u32[]{:S(2)}) collective-permute-start(f32[8,96,128]{2,1,0:T(8,128)S(1)} %get-tuple-element.87.x_ref.x), channel_id=1, source_target_pairs={{0,16},{16,0},{1,17},{17,1},{2,18},{18,2},{3,19},{19,3},{4,20},{20... | collective-permute-start | bytes 1179656 | tf_op jit(solution)/shard_map/ppermute | solution.py:608
  67.7 0.9 forward_face.3
  68.8 1.3 %collective-permute-done.21.received = f32[256,128]{1,0:T(8,128)S(1)} collective-permute-done((f32[256,128]{1,0:T(8,128)S(1)}, f32[256,128]{1,0:T(8,128)S(1)}, u32[]{:S(2)}, u32[]{:S(2)}) %collective-permute-start.21) | collective-permute-done | bytes 131104 | tf_op jit(solution)/shard_map/ppermute | solution.py:608
  70.1 1.2 %collective-permute-start.22 = (f32[128,128]{1,0:T(8,128)S(1)}, f32[128,128]{1,0:T(8,128)S(1)}, u32[]{:S(2)}, u32[]{:S(2)}) collective-permute-start(f32[128,128]{1,0:T(8,128)S(1)} %get-tuple-element.85), channel_id=1, source_target_pairs={{0,8},{4,12},{8,0},{12,4},{1,9},{5,13},{9,1},{13,5},{2,10},{6,14},... | collective-permute-start | bytes 196616 | tf_op jit(solution)/shard_map/ppermute | solution.py:608
  71.3 3.2 %collective-permute-done.22.right = f32[128,128]{1,0:T(8,128)S(1)} collective-permute-done((f32[128,128]{1,0:T(8,128)S(1)}, f32[128,128]{1,0:T(8,128)S(1)}, u32[]{:S(2)}, u32[]{:S(2)}) %collective-permute-start.22) | collective-permute-done | bytes 65568 | tf_op jit(solution)/shard_map/ppermute | solution.py:608
  74.5 2.1 %collective-permute-done.23.x = f32[8,96,128]{2,1,0:T(8,128)S(1)} collective-permute-done((f32[8,96,128]{2,1,0:T(8,128)S(1)}, f32[8,96,128]{2,1,0:T(8,128)S(1)}, u32[]{:S(2)}, u32[]{:S(2)}) %collective-permute-start.23) | collective-permute-done | bytes 393248 | tf_op jit(solution)/shard_map/ppermute | solution.py:608
  76.5 1.5 %collective-permute-start.30 = (f32[8,96,128]{2,1,0:T(8,128)S(1)}, f32[8,96,128]{2,1,0:T(8,128)S(1)}, u32[]{:S(2)}, u32[]{:S(2)}) collective-permute-start(f32[8,96,128]{2,1,0:T(8,128)S(1)} %get-tuple-element.89.own.residual), channel_id=1, source_target_pairs={{0,16},{16,0},{1,17},{17,1},{2,18},{18,2},{3,19},{19,3},{4,20},{20... | collective-permute-start | bytes 1179656 | tf_op jit(solution)/shard_map/ppermute | solution.py:608
  78.1 0.9 collective-permute-start.25
  79.0 3.5 %collective-permute-start.26 = (f32[128,128]{1,0:T(8,128)S(1)}, f32[128,128]{1,0:T(8,128)S(1)}, u32[]{:S(2)}, u32[]{:S(2)}) collective-permute-start(f32[128,128]{1,0:T(8,128)S(1)} %add.5.refs_0_), channel_id=1, source_target_pairs={{0,3},{1,2},{2,1},{3,0},{4,7},{5,6},{6,5},{7,4},{8,11},{9,10},{10,... | collective-permute-start | bytes 196616 | tf_op jit(solution)/shard_map/ppermute | solution.py:608
  82.5 1.3 %collective-permute-done.24.refs_1_ = f32[128,128]{1,0:T(8,128)S(1)} collective-permute-done((f32[128,128]{1,0:T(8,128)S(1)}, f32[128,128]{1,0:T(8,128)S(1)}, u32[]{:S(2)}, u32[]{:S(2)}) %collective-permute-start.24) | collective-permute-done | bytes 65568 | tf_op jit(solution)/shard_map/ppermute | solution.py:608
  83.7 1.8 %collective-permute-done.26.refs_3_ = f32[128,128]{1,0:T(8,128)S(1)} collective-permute-done((f32[128,128]{1,0:T(8,128)S(1)}, f32[128,128]{1,0:T(8,128)S(1)}, u32[]{:S(2)}, u32[]{:S(2)}) %collective-permute-start.26) | collective-permute-done | bytes 65568 | tf_op jit(solution)/shard_map/ppermute | solution.py:608
  85.6 1.3 %collective-permute-start.29 = (f32[128,128]{1,0:T(8,128)S(1)}, f32[128,128]{1,0:T(8,128)S(1)}, u32[]{:S(2)}, u32[]{:S(2)}) collective-permute-start(f32[128,128]{1,0:T(8,128)S(1)} %scale.3.refs_0_), channel_id=1, source_target_pairs={{0,8},{4,12},{8,0},{12,4},{1,9},{5,13},{9,1},{13,5},{2,10},{6,14},... | collective-permute-start | bytes 196616 | tf_op jit(solution)/shard_map/ppermute | solution.py:608
  86.9 0.7 collective-permute-start.27
  87.6 1.5 %collective-permute-start.28 = (f32[128,128]{1,0:T(8,128)S(1)}, f32[128,128]{1,0:T(8,128)S(1)}, u32[]{:S(2)}, u32[]{:S(2)}) collective-permute-start(f32[128,128]{1,0:T(8,128)S(1)} %scale.3.refs_0_), channel_id=1, source_target_pairs={{0,16},{16,0},{1,17},{17,1},{2,18},{18,2},{3,19},{19,3},{4,20},{20... | collective-permute-start | bytes 196616 | tf_op jit(solution)/shard_map/ppermute | solution.py:608
  89.2 1.0 %join.1 = f32[8,96,256]{2,1,0:T(8,128)} custom-call(f32[8,96,128]{2,1,0:T(8,128)S(1)} %get-tuple-element.89.own.residual, f32[8,96,128]{2,1,0:T(8,128)S(1)} %collective-permute-done.30.other.residual), custom_call_target="tpu_custom_call" | custom-call | flops 1000000 | bytes 2000000 | tf_op jit(solution)/shard_map/join/pallas_call | solution.py:557
  90.8 0.7 first_half.4.base
  91.4 1.1 %collective-permute-done.28.refs_0_ = f32[128,128]{1,0:T(8,128)S(1)} collective-permute-done((f32[128,128]{1,0:T(8,128)S(1)}, f32[128,128]{1,0:T(8,128)S(1)}, u32[]{:S(2)}, u32[]{:S(2)}) %collective-permute-start.28) | collective-permute-done | bytes 65568 | tf_op jit(solution)/shard_map/ppermute | solution.py:608
  92.6 1.4 %second_half.3 = (f32[8,96,128]{2,1,0:T(8,128)S(1)}, f32[4,96,128]{2,1,0:T(8,128)}, f32[4,96,128]{2,1,0:T(8,128)}) custom-call(f32[8,96,128]{2,1,0:T(8,128)S(1)} %first_half.4.base, bf16[8,2,192,512]{3,2,1,0:T(8,128)(2,1)S(1)} %by_columns.1.vectors, f32[128,128]{1,0:T(8,128)S(1)} %collective-permute-done.31.refs_0_, ...), custom_call_target="tpu_custom_call" | custom-call | flops 1000000000 | bytes 4000000 | tf_op jit(solution)/shard_map/second_half/pallas_call | solution.py:531
  94.4 0.7 first_half.5.other
  95.3 1.5 %final.1 = f32[8,96,256]{2,1,0:T(8,128)} custom-call(f32[8,96,128]{2,1,0:T(8,128)S(1)} %get-tuple-element.93.own, f32[8,96,128]{2,1,0:T(8,128)S(1)} %first_half.5.other, bf16[8,2,192,512]{3,2,1,0:T(8,128)(2,1)S(1)} %by_columns.1.vectors, f32[128,128]{1,0:T(8,128)S(1)} %collective-permute-done.33.refs_0_, f32[128,128]{1,0:T(8,128)S(1)} %collective-permute-done.34.refs_1_), custom_call_target="tpu_custom_call" | custom-call | flops 1000000000 | bytes 4000000 | tf_op jit(solution)/shard_map/final/pallas_call | solution.py:585
  (54 shorter events, 7.2 us)
Async XLA Ops:
  0.6 1.1 %copy-start = (f32[1,1,2,4,96,256]{5,4,3,2,1,0:T(8,128)S(1)}, f32[1,1,2,4,96,256]{5,4,3,2,1,0:T(8,128)}, u32[]{:S(2)}) copy-start(f32[1,1,2,4,96,256]{5,4,3,2,1,0:T(8,128)} %param.7) | copy-start | bytes 2359300
  2.0 5.3 %collective-permute-start = (f32[8,96,128]{2,1,0:T(8,128)S(1)}, f32[8,96,128]{2,1,0:T(8,128)S(1)}, u32[]{:S(2)}, u32[]{:S(2)}) collective-permute-start(f32[8,96,128]{2,1,0:T(8,128)S(1)} %get-tuple-element.54.x_ref.x), channel_id=1, source_target_pairs={{0,4},{4,0},{8,12},{12,8},{1,5},{5,1},{9,13},{13,9},{2,6},{6,2},{1... | collective-permute-start | bytes 1179656 | tf_op jit(solution)/shard_map/ppermute | solution.py:608
  2.6 19.3 %collective-permute-start.2 = (f32[4,96,128]{2,1,0:T(8,128)S(1)}, f32[4,96,128]{2,1,0:T(8,128)S(1)}, u32[]{:S(2)}, u32[]{:S(2)}) collective-permute-start(f32[4,96,128]{2,1,0:T(8,128)S(1)} %get-tuple-element.55), channel_id=1, source_target_pairs={{0,1},{1,2},{2,3},{3,0},{4,5},{5,6},{6,7},{7,4},{8,9},{9,10},{10,1... | collective-permute-start | bytes 589832 | tf_op jit(solution)/shard_map/ppermute | solution.py:603
  5.2 16.6 %collective-permute-start.3 = (f32[4,96,128]{2,1,0:T(8,128)S(1)}, f32[4,96,128]{2,1,0:T(8,128)S(1)}, u32[]{:S(2)}, u32[]{:S(2)}) collective-permute-start(f32[4,96,128]{2,1,0:T(8,128)S(1)} %get-tuple-element.55), channel_id=1, source_target_pairs={{0,3},{1,0},{2,1},{3,2},{4,7},{5,4},{6,5},{7,6},{8,11},{9,8},{10,9... | collective-permute-start | bytes 589832 | tf_op jit(solution)/shard_map/ppermute | solution.py:603
  7.3 16.1 %collective-permute-start.4 = (f32[4,96,128]{2,1,0:T(8,128)S(1)}, f32[4,96,128]{2,1,0:T(8,128)S(1)}, u32[]{:S(2)}, u32[]{:S(2)}) collective-permute-start(f32[4,96,128]{2,1,0:T(8,128)S(1)} %get-tuple-element.60), channel_id=1, source_target_pairs={{0,1},{1,2},{2,3},{3,0},{4,5},{5,6},{6,7},{7,4},{8,9},{9,10},{10,1... | collective-permute-start | bytes 589832 | tf_op jit(solution)/shard_map/ppermute | solution.py:603
  7.3 17.5 %collective-permute-start.5 = (f32[4,96,128]{2,1,0:T(8,128)S(1)}, f32[4,96,128]{2,1,0:T(8,128)S(1)}, u32[]{:S(2)}, u32[]{:S(2)}) collective-permute-start(f32[4,96,128]{2,1,0:T(8,128)S(1)} %get-tuple-element.60), channel_id=1, source_target_pairs={{0,3},{1,0},{2,1},{3,2},{4,7},{5,4},{6,5},{7,6},{8,11},{9,8},{10,9... | collective-permute-start | bytes 589832 | tf_op jit(solution)/shard_map/ppermute | solution.py:603
  11.1 11.2 %collective-permute-start.1 = (f32[8,96,128]{2,1,0:T(8,128)S(1)}, f32[8,96,128]{2,1,0:T(8,128)S(1)}, u32[]{:S(2)}, u32[]{:S(2)}) collective-permute-start(f32[8,96,128]{2,1,0:T(8,128)S(1)} %get-tuple-element.54.x_ref.x), channel_id=1, source_target_pairs={{0,12},{4,8},{8,4},{12,0},{1,13},{5,9},{9,5},{13,1},{2,14},{6,10},... | collective-permute-start | bytes 1179656 | tf_op jit(solution)/shard_map/ppermute | solution.py:621
  24.8 6.8 %copy-start.1 = (f32[2,512]{1,0:T(2,128)S(1)}, f32[2,512]{1,0:T(2,128)}, u32[]{:S(2)}) copy-start(f32[2,512]{1,0:T(2,128)} %inverse.1) | copy-start | bytes 12292
  25.8 1.4 %collective-permute-start.6 = (f32[256,128]{1,0:T(8,128)S(1)}, f32[256,128]{1,0:T(8,128)S(1)}, u32[]{:S(2)}, u32[]{:S(2)}) collective-permute-start(f32[256,128]{1,0:T(8,128)S(1)} %get-tuple-element.64), channel_id=1, source_target_pairs={{0,4},{4,0},{8,12},{12,8},{1,5},{5,1},{9,13},{13,9},{2,6},{6,2},{1... | collective-permute-start | bytes 393224 | tf_op jit(solution)/shard_map/ppermute | solution.py:608
  27.2 8.0 %collective-permute-start.7 = (f32[128,128]{1,0:T(8,128)S(1)}, f32[128,128]{1,0:T(8,128)S(1)}, u32[]{:S(2)}, u32[]{:S(2)}) collective-permute-start(f32[128,128]{1,0:T(8,128)S(1)} %get-tuple-element.65), channel_id=1, source_target_pairs={{0,10},{1,11},{2,8},{3,9},{4,14},{5,15},{6,12},{7,13},{8,2},{9,3},... | collective-permute-start | bytes 196616 | tf_op jit(solution)/shard_map/ppermute | solution.py:614
  29.4 5.8 %collective-permute-start.8 = (f32[128,128]{1,0:T(8,128)S(1)}, f32[128,128]{1,0:T(8,128)S(1)}, u32[]{:S(2)}, u32[]{:S(2)}) collective-permute-start(f32[128,128]{1,0:T(8,128)S(1)} %get-tuple-element.65), channel_id=1, source_target_pairs={{0,8},{4,12},{8,0},{12,4},{1,9},{5,13},{9,1},{13,5},{2,10},{6,14},... | collective-permute-start | bytes 196616 | tf_op jit(solution)/shard_map/ppermute | solution.py:608
  29.9 7.5 %collective-permute-start.9 = (f32[128,128]{1,0:T(8,128)S(1)}, f32[128,128]{1,0:T(8,128)S(1)}, u32[]{:S(2)}, u32[]{:S(2)}) collective-permute-start(f32[128,128]{1,0:T(8,128)S(1)} %get-tuple-element.68.refs_0_), channel_id=1, source_target_pairs={{0,2},{1,3},{2,0},{3,1},{4,6},{5,7},{6,4},{7,5},{8,10},{9,11},{10,... | collective-permute-start | bytes 196616 | tf_op jit(solution)/shard_map/ppermute | solution.py:608
  37.5 4.8 %collective-permute-start.10 = (f32[128,128]{1,0:T(8,128)S(1)}, f32[128,128]{1,0:T(8,128)S(1)}, u32[]{:S(2)}, u32[]{:S(2)}) collective-permute-start(f32[128,128]{1,0:T(8,128)S(1)} %scale.2.left), channel_id=1, source_target_pairs={{0,1},{1,0},{2,3},{3,2},{4,5},{5,4},{6,7},{7,6},{8,9},{9,8},{10,11... | collective-permute-start | bytes 196616 | tf_op jit(solution)/shard_map/ppermute | solution.py:608
  37.6 4.8 %collective-permute-start.11 = (f32[128,128]{1,0:T(8,128)S(1)}, f32[128,128]{1,0:T(8,128)S(1)}, u32[]{:S(2)}, u32[]{:S(2)}) collective-permute-start(f32[128,128]{1,0:T(8,128)S(1)} %scale.2.left), channel_id=1, source_target_pairs={{0,8},{4,12},{8,0},{12,4},{1,9},{5,13},{9,1},{13,5},{2,10},{6,14},... | collective-permute-start | bytes 196616 | tf_op jit(solution)/shard_map/ppermute | solution.py:608
  38.8 5.2 %collective-permute-start.12 = (f32[128,128]{1,0:T(8,128)S(1)}, f32[128,128]{1,0:T(8,128)S(1)}, u32[]{:S(2)}, u32[]{:S(2)}) collective-permute-start(f32[128,128]{1,0:T(8,128)S(1)} %scale.2.left), channel_id=1, source_target_pairs={{0,9},{1,8},{2,11},{3,10},{4,13},{5,12},{6,15},{7,14},{8,1},{9,0},... | collective-permute-start | bytes 196616 | tf_op jit(solution)/shard_map/ppermute | solution.py:614
  42.3 2.3 %collective-permute-start.13 = (f32[128,128]{1,0:T(8,128)S(1)}, f32[128,128]{1,0:T(8,128)S(1)}, u32[]{:S(2)}, u32[]{:S(2)}) collective-permute-start(f32[128,128]{1,0:T(8,128)S(1)} %add.3.refs_0_), channel_id=1, source_target_pairs={{0,4},{4,0},{8,12},{12,8},{1,5},{5,1},{9,13},{13,9},{2,6},{6,2},{1... | collective-permute-start | bytes 196616 | tf_op jit(solution)/shard_map/ppermute | solution.py:608
  43.9 1.3 %collective-permute-start.14 = (f32[128,128]{1,0:T(8,128)S(1)}, f32[128,128]{1,0:T(8,128)S(1)}, u32[]{:S(2)}, u32[]{:S(2)}) collective-permute-start(f32[128,128]{1,0:T(8,128)S(1)} %add.4.refs_1_), channel_id=1, source_target_pairs={{0,4},{4,0},{8,12},{12,8},{1,5},{5,1},{9,13},{13,9},{2,6},{6,2},{1... | collective-permute-start | bytes 196616 | tf_op jit(solution)/shard_map/ppermute | solution.py:608
  45.9 4.1 %collective-permute-start.15 = (f32[8,96,128]{2,1,0:T(8,128)S(1)}, f32[8,96,128]{2,1,0:T(8,128)S(1)}, u32[]{:S(2)}, u32[]{:S(2)}) collective-permute-start(f32[8,96,128]{2,1,0:T(8,128)S(1)} %get-tuple-element.87.x_ref.x), channel_id=1, source_target_pairs={{0,4},{4,0},{8,12},{12,8},{1,5},{5,1},{9,13},{13,9},{2,6},{6,2},{1... | collective-permute-start | bytes 1179656 | tf_op jit(solution)/shard_map/ppermute | solution.py:608
  46.2 9.6 %collective-permute-start.17 = (f32[4,96,128]{2,1,0:T(8,128)S(1)}, f32[4,96,128]{2,1,0:T(8,128)S(1)}, u32[]{:S(2)}, u32[]{:S(2)}) collective-permute-start(f32[4,96,128]{2,1,0:T(8,128)S(1)} %get-tuple-element.76), channel_id=1, source_target_pairs={{0,1},{1,2},{2,3},{3,0},{4,5},{5,6},{6,7},{7,4},{8,9},{9,10},{10,1... | collective-permute-start | bytes 589832 | tf_op jit(solution)/shard_map/ppermute | solution.py:603
  47.7 12.3 %collective-permute-start.18 = (f32[4,96,128]{2,1,0:T(8,128)S(1)}, f32[4,96,128]{2,1,0:T(8,128)S(1)}, u32[]{:S(2)}, u32[]{:S(2)}) collective-permute-start(f32[4,96,128]{2,1,0:T(8,128)S(1)} %get-tuple-element.76), channel_id=1, source_target_pairs={{0,3},{1,0},{2,1},{3,2},{4,7},{5,4},{6,5},{7,6},{8,11},{9,8},{10,9... | collective-permute-start | bytes 589832 | tf_op jit(solution)/shard_map/ppermute | solution.py:603
  50.0 17.4 %collective-permute-start.19 = (f32[4,96,128]{2,1,0:T(8,128)S(1)}, f32[4,96,128]{2,1,0:T(8,128)S(1)}, u32[]{:S(2)}, u32[]{:S(2)}) collective-permute-start(f32[4,96,128]{2,1,0:T(8,128)S(1)} %get-tuple-element.81), channel_id=1, source_target_pairs={{0,1},{1,2},{2,3},{3,0},{4,5},{5,6},{6,7},{7,4},{8,9},{9,10},{10,1... | collective-permute-start | bytes 589832 | tf_op jit(solution)/shard_map/ppermute | solution.py:603
  50.0 17.7 %collective-permute-start.20 = (f32[4,96,128]{2,1,0:T(8,128)S(1)}, f32[4,96,128]{2,1,0:T(8,128)S(1)}, u32[]{:S(2)}, u32[]{:S(2)}) collective-permute-start(f32[4,96,128]{2,1,0:T(8,128)S(1)} %get-tuple-element.81), channel_id=1, source_target_pairs={{0,3},{1,0},{2,1},{3,2},{4,7},{5,4},{6,5},{7,6},{8,11},{9,8},{10,9... | collective-permute-start | bytes 589832 | tf_op jit(solution)/shard_map/ppermute | solution.py:603
  53.8 10.9 %collective-permute-start.16 = (f32[8,96,128]{2,1,0:T(8,128)S(1)}, f32[8,96,128]{2,1,0:T(8,128)S(1)}, u32[]{:S(2)}, u32[]{:S(2)}) collective-permute-start(f32[8,96,128]{2,1,0:T(8,128)S(1)} %get-tuple-element.87.x_ref.x), channel_id=1, source_target_pairs={{0,12},{4,8},{8,4},{12,0},{1,13},{5,9},{9,5},{13,1},{2,14},{6,10},... | collective-permute-start | bytes 1179656 | tf_op jit(solution)/shard_map/ppermute | solution.py:621
  65.8 10.7 %collective-permute-start.23 = (f32[8,96,128]{2,1,0:T(8,128)S(1)}, f32[8,96,128]{2,1,0:T(8,128)S(1)}, u32[]{:S(2)}, u32[]{:S(2)}) collective-permute-start(f32[8,96,128]{2,1,0:T(8,128)S(1)} %get-tuple-element.87.x_ref.x), channel_id=1, source_target_pairs={{0,16},{16,0},{1,17},{17,1},{2,18},{18,2},{3,19},{19,3},{4,20},{20... | collective-permute-start | bytes 1179656 | tf_op jit(solution)/shard_map/ppermute | solution.py:608
  68.7 1.4 %collective-permute-start.21 = (f32[256,128]{1,0:T(8,128)S(1)}, f32[256,128]{1,0:T(8,128)S(1)}, u32[]{:S(2)}, u32[]{:S(2)}) collective-permute-start(f32[256,128]{1,0:T(8,128)S(1)} %get-tuple-element.83), channel_id=1, source_target_pairs={{0,4},{4,0},{8,12},{12,8},{1,5},{5,1},{9,13},{13,9},{2,6},{6,2},{1... | collective-permute-start | bytes 393224 | tf_op jit(solution)/shard_map/ppermute | solution.py:608
  70.1 4.3 %collective-permute-start.22 = (f32[128,128]{1,0:T(8,128)S(1)}, f32[128,128]{1,0:T(8,128)S(1)}, u32[]{:S(2)}, u32[]{:S(2)}) collective-permute-start(f32[128,128]{1,0:T(8,128)S(1)} %get-tuple-element.85), channel_id=1, source_target_pairs={{0,8},{4,12},{8,0},{12,4},{1,9},{5,13},{9,1},{13,5},{2,10},{6,14},... | collective-permute-start | bytes 196616 | tf_op jit(solution)/shard_map/ppermute | solution.py:608
  76.5 12.6 %collective-permute-start.30 = (f32[8,96,128]{2,1,0:T(8,128)S(1)}, f32[8,96,128]{2,1,0:T(8,128)S(1)}, u32[]{:S(2)}, u32[]{:S(2)}) collective-permute-start(f32[8,96,128]{2,1,0:T(8,128)S(1)} %get-tuple-element.89.own.residual), channel_id=1, source_target_pairs={{0,16},{16,0},{1,17},{17,1},{2,18},{18,2},{3,19},{19,3},{4,20},{20... | collective-permute-start | bytes 1179656 | tf_op jit(solution)/shard_map/ppermute | solution.py:608
  78.1 5.7 %collective-permute-start.24 = (f32[128,128]{1,0:T(8,128)S(1)}, f32[128,128]{1,0:T(8,128)S(1)}, u32[]{:S(2)}, u32[]{:S(2)}) collective-permute-start(f32[128,128]{1,0:T(8,128)S(1)} %add.5.refs_0_), channel_id=1, source_target_pairs={{0,1},{1,0},{2,3},{3,2},{4,5},{5,4},{6,7},{7,6},{8,9},{9,8},{10,11... | collective-permute-start | bytes 196616 | tf_op jit(solution)/shard_map/ppermute | solution.py:608
  78.1 5.7 %collective-permute-start.25 = (f32[128,128]{1,0:T(8,128)S(1)}, f32[128,128]{1,0:T(8,128)S(1)}, u32[]{:S(2)}, u32[]{:S(2)}) collective-permute-start(f32[128,128]{1,0:T(8,128)S(1)} %add.5.refs_0_), channel_id=1, source_target_pairs={{0,2},{1,3},{2,0},{3,1},{4,6},{5,7},{6,4},{7,5},{8,10},{9,11},{10,... | collective-permute-start | bytes 196616 | tf_op jit(solution)/shard_map/ppermute | solution.py:608
  79.0 6.5 %collective-permute-start.26 = (f32[128,128]{1,0:T(8,128)S(1)}, f32[128,128]{1,0:T(8,128)S(1)}, u32[]{:S(2)}, u32[]{:S(2)}) collective-permute-start(f32[128,128]{1,0:T(8,128)S(1)} %add.5.refs_0_), channel_id=1, source_target_pairs={{0,3},{1,2},{2,1},{3,0},{4,7},{5,6},{6,5},{7,4},{8,11},{9,10},{10,... | collective-permute-start | bytes 196616 | tf_op jit(solution)/shard_map/ppermute | solution.py:608
  85.6 4.6 %collective-permute-start.29 = (f32[128,128]{1,0:T(8,128)S(1)}, f32[128,128]{1,0:T(8,128)S(1)}, u32[]{:S(2)}, u32[]{:S(2)}) collective-permute-start(f32[128,128]{1,0:T(8,128)S(1)} %scale.3.refs_0_), channel_id=1, source_target_pairs={{0,8},{4,12},{8,0},{12,4},{1,9},{5,13},{9,1},{13,5},{2,10},{6,14},... | collective-permute-start | bytes 196616 | tf_op jit(solution)/shard_map/ppermute | solution.py:608
  86.9 7.1 %collective-permute-start.27 = (f32[128,128]{1,0:T(8,128)S(1)}, f32[128,128]{1,0:T(8,128)S(1)}, u32[]{:S(2)}, u32[]{:S(2)}) collective-permute-start(f32[128,128]{1,0:T(8,128)S(1)} %scale.3.refs_0_), channel_id=1, source_target_pairs={{0,24},{4,28},{8,16},{12,20},{16,8},{20,12},{24,0},{28,4},{1,25},{... | collective-permute-start | bytes 196616 | tf_op jit(solution)/shard_map/ppermute | solution.py:614
  87.6 5.0 %collective-permute-start.28 = (f32[128,128]{1,0:T(8,128)S(1)}, f32[128,128]{1,0:T(8,128)S(1)}, u32[]{:S(2)}, u32[]{:S(2)}) collective-permute-start(f32[128,128]{1,0:T(8,128)S(1)} %scale.3.refs_0_), channel_id=1, source_target_pairs={{0,16},{16,0},{1,17},{17,1},{2,18},{18,2},{3,19},{19,3},{4,20},{20... | collective-permute-start | bytes 196616 | tf_op jit(solution)/shard_map/ppermute | solution.py:608
  89.1 3.4 %collective-permute-start.31 = (f32[128,128]{1,0:T(8,128)S(1)}, f32[128,128]{1,0:T(8,128)S(1)}, u32[]{:S(2)}, u32[]{:S(2)}) collective-permute-start(f32[128,128]{1,0:T(8,128)S(1)} %scale.3.refs_0_), channel_id=1, source_target_pairs={{0,4},{4,0},{8,12},{12,8},{1,5},{5,1},{9,13},{13,9},{2,6},{6,2},{1... | collective-permute-start | bytes 196616 | tf_op jit(solution)/shard_map/ppermute | solution.py:608
  90.2 2.4 %collective-permute-start.32 = (f32[128,128]{1,0:T(8,128)S(1)}, f32[128,128]{1,0:T(8,128)S(1)}, u32[]{:S(2)}, u32[]{:S(2)}) collective-permute-start(f32[128,128]{1,0:T(8,128)S(1)} %collective-permute-done.29.refs_1_), channel_id=1, source_target_pairs={{0,4},{4,0},{8,12},{12,8},{1,5},{5,1},{9,13},{13,9},{2,6},{6,2},{1... | collective-permute-start | bytes 196616 | tf_op jit(solution)/shard_map/ppermute | solution.py:608
  92.6 2.5 %collective-permute-start.33 = (f32[128,128]{1,0:T(8,128)S(1)}, f32[128,128]{1,0:T(8,128)S(1)}, u32[]{:S(2)}, u32[]{:S(2)}) collective-permute-start(f32[128,128]{1,0:T(8,128)S(1)} %collective-permute-done.28.refs_0_), channel_id=1, source_target_pairs={{0,4},{4,0},{8,12},{12,8},{1,5},{5,1},{9,13},{13,9},{2,6},{6,2},{1... | collective-permute-start | bytes 196616 | tf_op jit(solution)/shard_map/ppermute | solution.py:608
  94.0 1.4 %collective-permute-start.34 = (f32[128,128]{1,0:T(8,128)S(1)}, f32[128,128]{1,0:T(8,128)S(1)}, u32[]{:S(2)}, u32[]{:S(2)}) collective-permute-start(f32[128,128]{1,0:T(8,128)S(1)} %collective-permute-done.27.refs_1_), channel_id=1, source_target_pairs={{0,4},{4,0},{8,12},{12,8},{1,5},{5,1},{9,13},{13,9},{2,6},{6,2},{1... | collective-permute-start | bytes 196616 | tf_op jit(solution)/shard_map/ppermute | solution.py:608

commit v12 on v10

--- a/solution.py
+++ b/solution.py
@@ -116,88 +116,87 @@
 
 
 def around(site, ny, nx):
-    y, x = site // nx, lax.rem(site, nx)
-    right, left = lax.rem(x + 1, nx), lax.rem(x + nx - 1, nx)
-    up, down = lax.rem(y + 1, ny), lax.rem(y + ny - 1, ny)
+    y, x = site // nx, site % nx
+    right, left = (x + 1) % nx, (x - 1) % nx
+    up, down = (y + 1) % ny, (y - 1) % ny
     return (site, y * nx + right, y * nx + left, up * nx + x, down * nx + x)
 
 
-def local_sum(site, ny, nx, x_ref, stacks, matrix):
-    @pl.when(site == 0)
-    def _():
-        for each in range(ny * nx):
-            stacks[each] = stack(x_ref[each], 1.0)
-
+def local_sum(site, ny, nx, stacks, local):
     total = None
     for direction, neighbour in enumerate(around(site, ny, nx)):
-        term = matmul(matrix(direction), stacks[neighbour])
+        term = matmul(local[direction, site], stacks[neighbour])
         total = term if total is None else total + term
     return fold(total)
 
 
-def first_kernel(ny, nx, x_ref, source, couplings, rest, half_source, local, halo, stacks):
-    site = pl.program_id(0)
-    own = pick_half(source[0], lax.axis_index("groups"))
-    half_source[0] = own
-    for direction in range(couplings.shape[0]):
-        high, low = high_low(couplings[direction, 0])
-        both = jnp.concatenate([high, low], axis=0)
-        if direction < LOCAL:
-            local[direction, 0] = both
-        else:
-            halo[direction - LOCAL, 0] = both
-    rest[0] = own - local_sum(site, ny, nx, x_ref, stacks, lambda d: local[d, 0])
+def first_kernel(ny, nx, x_ref, source, couplings, rest, half_source, local, halo, stacks, held, held_source, sems):
+    group = lax.axis_index("groups")
+    sites = x_ref.shape[0]
+    copies = []
+    for site in range(sites):
+        copies.append(pltpu.make_async_copy(couplings.at[:, site], held.at[site], sems.at[site]))
+        copies[-1].start()
+    bring = pltpu.make_async_copy(source, held_source, sems.at[sites])
+    bring.start()
+    for site in range(sites):
+        stacks[site] = stack(x_ref[site], 1.0)
+    bring.wait()
+    for site in range(sites):
+        half_source[site] = pick_half(held_source[site], group)
+    for site in range(sites):
+        copies[site].wait()
+        for direction in range(couplings.shape[0]):
+            high, low = high_low(held[site, direction])
+            both = jnp.concatenate([high, low], axis=0)
+            if direction < LOCAL:
+                local[direction, site] = both
+            else:
+                halo[direction - LOCAL, site] = both
+        rest[site] = half_source[site] - local_sum(site, ny, nx, stacks, local)
 
 
 def first_local(x, source, couplings, ny, nx):
     sites, rows, lanes = x.shape
     directions, _, _, columns = couplings.shape
     outer = directions - LOCAL
+    in_place = pl.BlockSpec(memory_space=pl.ANY)
     return pl.pallas_call(
         functools.partial(first_kernel, ny, nx),
-        grid=(sites,),
         out_shape=(
             pltpu.VMEM(x.shape, F32),
             pltpu.VMEM(x.shape, F32),
             pltpu.VMEM((LOCAL, sites, 2 * rows, columns), BF16),
             pltpu.VMEM((outer, sites, 2 * rows, columns), BF16),
         ),
-        in_specs=[
-            pl.BlockSpec((sites, rows, lanes), lambda s: (0, 0, 0)),
-            pl.BlockSpec((1, rows, 2 * lanes), lambda s: (s, 0, 0)),
-            pl.BlockSpec((directions, 1, rows, columns), lambda s: (0, s, 0, 0)),
+        in_specs=vmem(1) + [in_place, in_place],
+        out_specs=tuple(vmem(4)),
+        scratch_shapes=[
+            pltpu.VMEM((sites, 2 * rows, 2 * lanes), BF16),
+            pltpu.VMEM((sites, directions, rows, columns), F32),
+            pltpu.VMEM(source.shape, F32),
+            pltpu.SemaphoreType.DMA((sites + 1,)),
         ],
-        out_specs=(
-            pl.BlockSpec((1, rows, lanes), lambda s: (s, 0, 0)),
-            pl.BlockSpec((1, rows, lanes), lambda s: (s, 0, 0)),
-            pl.BlockSpec((LOCAL, 1, 2 * rows, columns), lambda s: (0, s, 0, 0)),
-            pl.BlockSpec((outer, 1, 2 * rows, columns), lambda s: (0, s, 0, 0)),
-        ),
-        scratch_shapes=[pltpu.VMEM((sites, 2 * rows, 2 * lanes), BF16)],
-        compiler_params=params(),
+        compiler_params=params(20),
         cost_estimate=cost(8e9, 16e6),
         name="first_local",
     )(x, in_hbm(source), in_hbm(couplings))
 
 
 def local_kernel(ny, nx, x_ref, source, local, rest, stacks):
-    site = pl.program_id(0)
-    rest[0] = source[0] - local_sum(site, ny, nx, x_ref, stacks, lambda d: local[d, 0])
+    for site in range(x_ref.shape[0]):
+        stacks[site] = stack(x_ref[site], 1.0)
+    for site in range(x_ref.shape[0]):
+        rest[site] = source[site] - local_sum(site, ny, nx, stacks, local)
 
 
 def local_part(x, source, local, ny, nx):
     sites, rows, lanes = x.shape
-    columns = local.shape[-1]
     return pl.pallas_call(
         functools.partial(local_kernel, ny, nx),
-        grid=(sites,),
         out_shape=pltpu.VMEM(x.shape, F32),
-        in_specs=[
-            pl.BlockSpec((sites, rows, lanes), lambda s: (0, 0, 0)),
-            pl.BlockSpec((1, rows, lanes), lambda s: (s, 0, 0)),
-            pl.BlockSpec((LOCAL, 1, 2 * rows, columns), lambda s: (0, s, 0, 0)),
-        ],
-        out_specs=pl.BlockSpec((1, rows, lanes), lambda s: (s, 0, 0)),
+        in_specs=vmem(3),
+        out_specs=vmem(1)[0],
         scratch_shapes=[pltpu.VMEM((sites, 2 * rows, 2 * lanes), BF16)],
         compiler_params=params(),
         cost_estimate=cost(8e9, 8e6),
@@ -492,19 +491,23 @@
     )(x, residual, vectors, *pieces)
 
 
-def second_half_kernel(base, vectors, *refs):
-    pieces, (out, front, back, stacks) = refs[:-4], refs[-4:]
+def second_half_kernel(count, base, vectors, *refs):
+    pieces, (outs, stacks) = refs[:count], (refs[count:-1], refs[-1])
     place_pieces(pieces, stacks)
     for site in range(base.shape[0]):
-        put(site, base[site] + expand(site, vectors, 1, stacks), out, front, back)
-
-
-def second_half(base, pieces, vectors):
-    return pl.pallas_call(
-        second_half_kernel,
-        out_shape=with_halves(base.shape),
+        value = base[site] + expand(site, vectors, 1, stacks)
+        if len(outs) == 1:
+            outs[0][site] = value
+        else:
+            put(site, value, *outs)
+
+
+def second_half(base, pieces, vectors, halves):
+    return pl.pallas_call(
+        functools.partial(second_half_kernel, len(pieces)),
+        out_shape=with_halves(base.shape) if halves else pltpu.VMEM(base.shape, F32),
         in_specs=vmem(2 + len(pieces)),
-        out_specs=tuple(vmem(3)),
+        out_specs=tuple(vmem(3)) if halves else vmem(1)[0],
         scratch_shapes=[pltpu.VMEM((vectors.shape[-1], 2 * base.shape[-1]), BF16)],
         compiler_params=params(),
         cost_estimate=cost(1e9, 4e6),
@@ -641,8 +644,8 @@
     number = vectors.shape[0]
     blocks = lax.axis_size("space")
 
-    x, front, back = pack(initial.reshape(sites, rows, lanes))
-    faces = faces_of(x, front, back)
+    x, early_x, late_x = pack(initial.reshape(sites, rows, lanes))
+    faces = faces_of(x, early_x, late_x)
     matrices = couplings.reshape(directions, sites, rows, couplings.shape[-1])
     rest, half_source, local, halo = first_local(x, source.reshape(sites, rows, lanes), matrices, ny, nx)
     across = jnp.transpose(vectors, (1, 2, 3, 4, 5, 0)).reshape(sites * vectors.shape[-1], number)
@@ -652,19 +655,19 @@
     for sweep in range(ITERS):
         last = sweep == ITERS - 1
         if sweep:
-            faces = faces_of(x, front, back)
+            faces = faces_of(x, early_x, late_x)
             rest = local_part(x, half_source, local, ny, nx)
+        if last:
+            rest, x = lax.optimization_barrier((rest, x))
+            other_x = crossed(x, "groups", 1)
         near, far, early, late = faces
         back_rest, own, partial = middle(rest, near, far, front_faces(*early, halo), halo, by_rows)
-        if last:
-            partial, x = lax.optimization_barrier((partial, x))
-            other_x = crossed(x, "groups", 1)
         back_rest = backward_face(back_rest, late[0], halo)
         residual, keep, send = forward_face(own, partial, back_rest, late[1], halo, by_rows)
         if not last:
             pieces = scaled_sum(keep, send, eigen)
             base = first_half(x, residual, pieces, by_columns)
-            x, front, back = second_half(base, paired(pieces), by_columns)
+            x, early_x, late_x = second_half(base, paired(pieces), by_columns, True)
     part, residual, other_x = lax.optimization_barrier((halving(keep, send), residual, other_x))
     other_residual = crossed(residual, "groups", 1)
     d = scale(eigen, over_time(part))
@@ -676,7 +679,7 @@
     own[-1], full_residual = lax.optimization_barrier((own[-1], full_residual))
     own_x = first_half(x, residual, own, by_columns)
     other[0], own_x = lax.optimization_barrier((other[0], own_x))
-    own_x, _, _ = second_half(own_x, paired(own), by_columns)
+    own_x = second_half(own_x, paired(own), by_columns, False)
     other[-1], own_x = lax.optimization_barrier((other[-1], own_x))
     other_second = paired(other)
     other_x = first_half(other_x, other_residual, other, by_columns)

time: 95.8 us -> 95.1 us (level)
  waiting for transfers between devices: 24.9 us -> 28.2 us
  Pallas kernels: 27.7 us -> 24.7 us
    pallas_call x4, Pallas kernels: 12.7 us -> 9.68 us  [the longest x1 7.11 us: first_local(): pl.pallas_call(functools.partial(first_kernel, ny, nx), out_shape=(pltpu....]
    ppermute x8, waiting for transfers between devices: 5.06 us -> 7.32 us  [shifted(): lax.ppermute(value, axis, [(i, (i + step) % count) for i in range(count)])]
    ppermute x22, waiting for transfers between devices: 16.2 us -> 17.4 us  [crossed(): return lax.ppermute(value, axis, [(i, i ^ mask) for i in range(count)])]
    ppermute x22, starting transfers between devices: 18.1 us -> 17.1 us  [crossed(): return lax.ppermute(value, axis, [(i, i ^ mask) for i in range(count)])]
  transfers between devices with their start and end apart: 35 -> 35, of which waited for: 15 -> 18; matrix products, arithmetic and copies ran while one was open for 0% -> 0% of each run, Pallas kernels for 25% -> 22%
where the time goes in v12:
time: 95.1 us; the launch traced here: 94.9 us
  starting transfers between devices  39.8 us (42%)
  waiting for transfers between devices  28.2 us (30%)
  Pallas kernels  24.7 us (26%)
  local copies, waits for them, and re-layouts  1.13 us (1%)
  between operations  1.1 us (1%)
    ppermute x22, waiting for transfers between devices, crossed(): return lax.ppermute(value, axis, [(i, i ^ mask) for i in range(count)])  17.4 us
    ppermute x22, starting transfers between devices, crossed(): return lax.ppermute(value, axis, [(i, i ^ mask) for i in range(count)])  17.1 us
    ppermute x8, starting transfers between devices, shifted(): lax.ppermute(value, axis, [(i, (i + step) % count) for i in range(count)])  16.2 us
    ppermute x8, waiting for transfers between devices, shifted(): lax.ppermute(value, axis, [(i, (i + step) % count) for i in range(count)])  7.32 us
    pallas_call x1, Pallas kernels, first_local(): pl.pallas_call(functools.partial(first_kernel, ny, nx), out_shape=(pltpu....  7.11 us
    ppermute x3, starting transfers between devices, crossed_both(): return lax.ppermute(value, (first, second), pairs)  4.98 us
    pallas_call x1, Pallas kernels, vectors_parts(): pl.pallas_call(vectors_kernel, grid=(sites // step,), out_shape=(pltpu.VM...  4.24 us
    ppermute x3, waiting for transfers between devices, crossed_both(): return lax.ppermute(value, (first, second), pairs)  2.72 us
  transfers between devices with their start and end apart: 35, of which 18 were waited for; matrix products, arithmetic and copies ran while one was open for 0% of the time, Pallas kernels for 22%

profile of v12, /device:TPU:0, one launch (start us, length us, event | category | flops | bytes accessed | tf_op | source)
XLA Modules:
  0.0 94.9 jit_solution(15064826418781867428)
XLA Ops:
  0.6 1.1 %copy-done = f32[1,1,2,4,96,256]{5,4,3,2,1,0:T(8,128)S(1)} copy-done((f32[1,1,2,4,96,256]{5,4,3,2,1,0:T(8,128)S(1)}, f32[1,1,2,4,96,256]{5,4,3,2,1,0:T(8,128)}, u32[]{:S(2)}) %copy-start) | copy-done | bytes 786456
  2.6 2.6 %collective-permute-start.2 = (f32[4,96,128]{2,1,0:T(8,128)S(1)}, f32[4,96,128]{2,1,0:T(8,128)S(1)}, u32[]{:S(2)}, u32[]{:S(2)}) collective-permute-start(f32[4,96,128]{2,1,0:T(8,128)S(1)} %get-tuple-element.49), channel_id=1, source_target_pairs={{0,1},{1,2},{2,3},{3,0},{4,5},{5,6},{6,7},{7,4},{8,9},{9,10},{10,1... | collective-permute-start | bytes 589832 | tf_op jit(solution)/shard_map/ppermute | solution.py:578
  5.2 2.1 %collective-permute-start.3 = (f32[4,96,128]{2,1,0:T(8,128)S(1)}, f32[4,96,128]{2,1,0:T(8,128)S(1)}, u32[]{:S(2)}, u32[]{:S(2)}) collective-permute-start(f32[4,96,128]{2,1,0:T(8,128)S(1)} %get-tuple-element.49), channel_id=1, source_target_pairs={{0,3},{1,0},{2,1},{3,2},{4,7},{5,4},{6,5},{7,6},{8,11},{9,8},{10,9... | collective-permute-start | bytes 589832 | tf_op jit(solution)/shard_map/ppermute | solution.py:578
  7.3 1.2 %collective-permute-start.1 = (f32[8,96,128]{2,1,0:T(8,128)S(1)}, f32[8,96,128]{2,1,0:T(8,128)S(1)}, u32[]{:S(2)}, u32[]{:S(2)}) collective-permute-start(f32[8,96,128]{2,1,0:T(8,128)S(1)} %get-tuple-element.45.x_ref.x), channel_id=1, source_target_pairs={{0,12},{4,8},{8,4},{12,0},{1,13},{5,9},{9,5},{13,1},{2,14},{6,10},... | collective-permute-start | bytes 1179656 | tf_op jit(solution)/shard_map/ppermute | solution.py:596
  8.5 3.8 %collective-permute-start.5 = (f32[4,96,128]{2,1,0:T(8,128)S(1)}, f32[4,96,128]{2,1,0:T(8,128)S(1)}, u32[]{:S(2)}, u32[]{:S(2)}) collective-permute-start(f32[4,96,128]{2,1,0:T(8,128)S(1)} %get-tuple-element.55), channel_id=1, source_target_pairs={{0,3},{1,0},{2,1},{3,2},{4,7},{5,4},{6,5},{7,6},{8,11},{9,8},{10,9... | collective-permute-start | bytes 589832 | tf_op jit(solution)/shard_map/ppermute | solution.py:578
  12.3 7.1 %first_local.1 = (f32[8,96,128]{2,1,0:T(8,128)S(1)}, f32[8,96,128]{2,1,0:T(8,128)S(1)}, bf16[5,8,192,192]{3,2,1,0:T(8,128)(2,1)S(1)}, bf16[4,8,192,192]{3,2,1,0:T(8,128)(2,1)S(1)}) custom-call(f32[8,96,128]{2,1,0:T(8,128)S(1)} %get-tuple-element.45.x_ref.x, f32[8,96,256]{2,1,0:T(8,128)} %bitcast.13, f32[9,8,96,192]{3,2,1,0:T(8,128)} %bitcast.12), custom_call_target="tpu_custom_call" | custom-call | flops 8000000000 | bytes 16000000 | tf_op jit(solution)/shard_map/first_local/pallas_call | solution.py:164
  19.4 4.2 %vectors_parts.1 = (bf16[1024,1536]{1,0:T(8,128)(2,1)S(1)}, bf16[8,2,192,512]{3,2,1,0:T(8,128)(2,1)S(1)}) custom-call(f32[1536,512]{1,0:T(8,128)} %bitcast.9), custom_call_target="tpu_custom_call" | custom-call | flops 1000000 | bytes 9000000 | tf_op jit(solution)/shard_map/vectors_parts/pallas_call | solution.py:248
  24.2 1.1 %middle.2 = (f32[4,96,128]{2,1,0:T(8,128)S(1)}, f32[4,96,128]{2,1,0:T(8,128)S(1)}, f32[512,128]{1,0:T(8,128)S(1)}) custom-call(f32[8,96,128]{2,1,0:T(8,128)S(1)} %get-tuple-element.46.rest, f32[8,96,128]{2,1,0:T(8,128)S(1)} %collective-permute-done.near, f32[8,96,128]{2,1,0:T(8,128)S(1)} %collective-permute-done.1.far, f32[4,96,128]{2,1,0:T(8,128)S(1)} %front_faces.2.front, ...), custom_call_target="tpu_custom_call" | custom-call | flops 1000 | bytes 1000 | tf_op jit(solution)/shard_map/middle/pallas_call | solution.py:335
  25.6 0.9 forward_face.2
  26.7 1.3 %collective-permute-done.6.received = f32[256,128]{1,0:T(8,128)S(1)} collective-permute-done((f32[256,128]{1,0:T(8,128)S(1)}, f32[256,128]{1,0:T(8,128)S(1)}, u32[]{:S(2)}, u32[]{:S(2)}) %collective-permute-start.6) | collective-permute-done | bytes 131104 | tf_op jit(solution)/shard_map/ppermute | solution.py:583
  28.0 0.7 collective-permute-start.7
  28.7 1.2 %collective-permute-start.8 = (f32[128,128]{1,0:T(8,128)S(1)}, f32[128,128]{1,0:T(8,128)S(1)}, u32[]{:S(2)}, u32[]{:S(2)}) collective-permute-start(f32[128,128]{1,0:T(8,128)S(1)} %get-tuple-element.60.refs_0_), channel_id=1, source_target_pairs={{0,2},{1,3},{2,0},{3,1},{4,6},{5,7},{6,4},{7,5},{8,10},{9,11},{10,... | collective-permute-start | bytes 196616 | tf_op jit(solution)/shard_map/ppermute | solution.py:583
  30.0 2.5 %collective-permute-start.9 = (f32[128,128]{1,0:T(8,128)S(1)}, f32[128,128]{1,0:T(8,128)S(1)}, u32[]{:S(2)}, u32[]{:S(2)}) collective-permute-start(f32[128,128]{1,0:T(8,128)S(1)} %get-tuple-element.61), channel_id=1, source_target_pairs={{0,10},{1,11},{2,8},{3,9},{4,14},{5,15},{6,12},{7,13},{8,2},{9,3},... | collective-permute-start | bytes 196616 | tf_op jit(solution)/shard_map/ppermute | solution.py:589
  32.6 4.4 %collective-permute-done.8.refs_2_ = f32[128,128]{1,0:T(8,128)S(1)} collective-permute-done((f32[128,128]{1,0:T(8,128)S(1)}, f32[128,128]{1,0:T(8,128)S(1)}, u32[]{:S(2)}, u32[]{:S(2)}) %collective-permute-start.8) | collective-permute-done | bytes 65568 | tf_op jit(solution)/shard_map/ppermute | solution.py:583
  37.0 1.3 %collective-permute-done.9.refs_3_ = f32[128,128]{1,0:T(8,128)S(1)} collective-permute-done((f32[128,128]{1,0:T(8,128)S(1)}, f32[128,128]{1,0:T(8,128)S(1)}, u32[]{:S(2)}, u32[]{:S(2)}) %collective-permute-start.9) | collective-permute-done | bytes 65568 | tf_op jit(solution)/shard_map/ppermute | solution.py:589
  38.3 1.0 %collective-permute-start.11 = (f32[128,128]{1,0:T(8,128)S(1)}, f32[128,128]{1,0:T(8,128)S(1)}, u32[]{:S(2)}, u32[]{:S(2)}) collective-permute-start(f32[128,128]{1,0:T(8,128)S(1)} %scale.2.left), channel_id=1, source_target_pairs={{0,8},{4,12},{8,0},{12,4},{1,9},{5,13},{9,1},{13,5},{2,10},{6,14},... | collective-permute-start | bytes 196616 | tf_op jit(solution)/shard_map/ppermute | solution.py:583
  39.8 2.1 %collective-permute-start.10 = (f32[128,128]{1,0:T(8,128)S(1)}, f32[128,128]{1,0:T(8,128)S(1)}, u32[]{:S(2)}, u32[]{:S(2)}) collective-permute-start(f32[128,128]{1,0:T(8,128)S(1)} %scale.2.left), channel_id=1, source_target_pairs={{0,1},{1,0},{2,3},{3,2},{4,5},{5,4},{6,7},{7,6},{8,9},{9,8},{10,11... | collective-permute-start | bytes 196616 | tf_op jit(solution)/shard_map/ppermute | solution.py:583
  41.9 1.5 %collective-permute-done.11.left = f32[128,128]{1,0:T(8,128)S(1)} collective-permute-done((f32[128,128]{1,0:T(8,128)S(1)}, f32[128,128]{1,0:T(8,128)S(1)}, u32[]{:S(2)}, u32[]{:S(2)}) %collective-permute-start.11) | collective-permute-done | bytes 65568 | tf_op jit(solution)/shard_map/ppermute | solution.py:583
  43.4 1.1 %collective-permute-done.12.right = f32[128,128]{1,0:T(8,128)S(1)} collective-permute-done((f32[128,128]{1,0:T(8,128)S(1)}, f32[128,128]{1,0:T(8,128)S(1)}, u32[]{:S(2)}, u32[]{:S(2)}) %collective-permute-start.12) | collective-permute-done | bytes 65568 | tf_op jit(solution)/shard_map/ppermute | solution.py:589
  45.2 0.7 first_half.3.base
  46.2 0.7 second_half.2
  47.2 1.2 %collective-permute-start.17 = (f32[4,96,128]{2,1,0:T(8,128)S(1)}, f32[4,96,128]{2,1,0:T(8,128)S(1)}, u32[]{:S(2)}, u32[]{:S(2)}) collective-permute-start(f32[4,96,128]{2,1,0:T(8,128)S(1)} %get-tuple-element.68), channel_id=1, source_target_pairs={{0,1},{1,2},{2,3},{3,0},{4,5},{5,6},{6,7},{7,4},{8,9},{9,10},{10,1... | collective-permute-start | bytes 589832 | tf_op jit(solution)/shard_map/ppermute | solution.py:578
  48.4 2.6 %collective-permute-start.18 = (f32[4,96,128]{2,1,0:T(8,128)S(1)}, f32[4,96,128]{2,1,0:T(8,128)S(1)}, u32[]{:S(2)}, u32[]{:S(2)}) collective-permute-start(f32[4,96,128]{2,1,0:T(8,128)S(1)} %get-tuple-element.68), channel_id=1, source_target_pairs={{0,3},{1,0},{2,1},{3,2},{4,7},{5,4},{6,5},{7,6},{8,11},{9,8},{10,9... | collective-permute-start | bytes 589832 | tf_op jit(solution)/shard_map/ppermute | solution.py:578
  51.3 3.8 %collective-permute-start.20 = (f32[4,96,128]{2,1,0:T(8,128)S(1)}, f32[4,96,128]{2,1,0:T(8,128)S(1)}, u32[]{:S(2)}, u32[]{:S(2)}) collective-permute-start(f32[4,96,128]{2,1,0:T(8,128)S(1)} %get-tuple-element.72), channel_id=1, source_target_pairs={{0,3},{1,0},{2,1},{3,2},{4,7},{5,4},{6,5},{7,6},{8,11},{9,8},{10,9... | collective-permute-start | bytes 589832 | tf_op jit(solution)/shard_map/ppermute | solution.py:578
  55.1 1.3 %local_part.1.rest = f32[8,96,128]{2,1,0:T(8,128)S(1)} custom-call(f32[8,96,128]{2,1,0:T(8,128)S(1)} %get-tuple-element.78.x_ref.x, f32[8,96,128]{2,1,0:T(8,128)S(1)} %get-tuple-element.63.source, bf16[5,8,192,192]{3,2,1,0:T(8,128)(2,1)S(1)} %get-tuple-element.64.local), custom_call_target="tpu_custom_call" | custom-call | flops 8000000000 | bytes 8000000 | tf_op jit(solution)/shard_map/local_part/pallas_call | solution.py:195
  56.7 1.5 %collective-permute-start.23 = (f32[8,96,128]{2,1,0:T(8,128)S(1)}, f32[8,96,128]{2,1,0:T(8,128)S(1)}, u32[]{:S(2)}, u32[]{:S(2)}) collective-permute-start(f32[8,96,128]{2,1,0:T(8,128)S(1)} %get-tuple-element.78.x_ref.x), channel_id=1, source_target_pairs={{0,16},{16,0},{1,17},{17,1},{2,18},{18,2},{3,19},{19,3},{4,20},{20... | collective-permute-start | bytes 1179656 | tf_op jit(solution)/shard_map/ppermute | solution.py:583
  58.3 2.7 %collective-permute-done.18.forward = f32[4,96,128]{2,1,0:T(8,128)S(1)} collective-permute-done((f32[4,96,128]{2,1,0:T(8,128)S(1)}, f32[4,96,128]{2,1,0:T(8,128)S(1)}, u32[]{:S(2)}, u32[]{:S(2)}) %collective-permute-start.18) | collective-permute-done | bytes 196640 | tf_op jit(solution)/shard_map/ppermute | solution.py:578
  61.5 0.8 collective-permute-done.16.far
  62.3 1.1 %middle.3 = (f32[4,96,128]{2,1,0:T(8,128)S(1)}, f32[4,96,128]{2,1,0:T(8,128)S(1)}, f32[512,128]{1,0:T(8,128)S(1)}) custom-call(f32[8,96,128]{2,1,0:T(8,128)S(1)} %local_part.1.rest, f32[8,96,128]{2,1,0:T(8,128)S(1)} %collective-permute-done.15.near, f32[8,96,128]{2,1,0:T(8,128)S(1)} %collective-permute-done.16.far, f32[4,96,128]{2,1,0:T(8,128)S(1)} %front_faces.3.front, ...), custom_call_target="tpu_custom_call" | custom-call | flops 1000 | bytes 1000 | tf_op jit(solution)/shard_map/middle/pallas_call | solution.py:335
  63.4 1.9 %collective-permute-done.19.backward = f32[4,96,128]{2,1,0:T(8,128)S(1)} collective-permute-done((f32[4,96,128]{2,1,0:T(8,128)S(1)}, f32[4,96,128]{2,1,0:T(8,128)S(1)}, u32[]{:S(2)}, u32[]{:S(2)}) %collective-permute-start.19) | collective-permute-done | bytes 196640 | tf_op jit(solution)/shard_map/ppermute | solution.py:578
  65.6 2.3 %collective-permute-done.20.forward = f32[4,96,128]{2,1,0:T(8,128)S(1)} collective-permute-done((f32[4,96,128]{2,1,0:T(8,128)S(1)}, f32[4,96,128]{2,1,0:T(8,128)S(1)}, u32[]{:S(2)}, u32[]{:S(2)}) %collective-permute-start.20) | collective-permute-done | bytes 196640 | tf_op jit(solution)/shard_map/ppermute | solution.py:578
  67.9 0.9 forward_face.3
  68.9 1.3 %collective-permute-done.21.received = f32[256,128]{1,0:T(8,128)S(1)} collective-permute-done((f32[256,128]{1,0:T(8,128)S(1)}, f32[256,128]{1,0:T(8,128)S(1)}, u32[]{:S(2)}, u32[]{:S(2)}) %collective-permute-start.21) | collective-permute-done | bytes 131104 | tf_op jit(solution)/shard_map/ppermute | solution.py:583
  70.3 1.0 %collective-permute-start.22 = (f32[128,128]{1,0:T(8,128)S(1)}, f32[128,128]{1,0:T(8,128)S(1)}, u32[]{:S(2)}, u32[]{:S(2)}) collective-permute-start(f32[128,128]{1,0:T(8,128)S(1)} %get-tuple-element.76), channel_id=1, source_target_pairs={{0,8},{4,12},{8,0},{12,4},{1,9},{5,13},{9,1},{13,5},{2,10},{6,14},... | collective-permute-start | bytes 196616 | tf_op jit(solution)/shard_map/ppermute | solution.py:583
  71.3 3.3 %collective-permute-done.22.right = f32[128,128]{1,0:T(8,128)S(1)} collective-permute-done((f32[128,128]{1,0:T(8,128)S(1)}, f32[128,128]{1,0:T(8,128)S(1)}, u32[]{:S(2)}, u32[]{:S(2)}) %collective-permute-start.22) | collective-permute-done | bytes 65568 | tf_op jit(solution)/shard_map/ppermute | solution.py:583
  74.6 1.6 %collective-permute-start.30 = (f32[8,96,128]{2,1,0:T(8,128)S(1)}, f32[8,96,128]{2,1,0:T(8,128)S(1)}, u32[]{:S(2)}, u32[]{:S(2)}) collective-permute-start(f32[8,96,128]{2,1,0:T(8,128)S(1)} %get-tuple-element.80.own.residual), channel_id=1, source_target_pairs={{0,16},{16,0},{1,17},{17,1},{2,18},{18,2},{3,19},{19,3},{4,20},{20... | collective-permute-start | bytes 1179656 | tf_op jit(solution)/shard_map/ppermute | solution.py:583
  76.2 0.7 collective-permute-start.24
  76.9 2.0 %collective-permute-start.25 = (f32[128,128]{1,0:T(8,128)S(1)}, f32[128,128]{1,0:T(8,128)S(1)}, u32[]{:S(2)}, u32[]{:S(2)}) collective-permute-start(f32[128,128]{1,0:T(8,128)S(1)} %add.5.refs_0_), channel_id=1, source_target_pairs={{0,2},{1,3},{2,0},{3,1},{4,6},{5,7},{6,4},{7,5},{8,10},{9,11},{10,... | collective-permute-start | bytes 196616 | tf_op jit(solution)/shard_map/ppermute | solution.py:583
  78.9 1.7 %collective-permute-start.26 = (f32[128,128]{1,0:T(8,128)S(1)}, f32[128,128]{1,0:T(8,128)S(1)}, u32[]{:S(2)}, u32[]{:S(2)}) collective-permute-start(f32[128,128]{1,0:T(8,128)S(1)} %add.5.refs_0_), channel_id=1, source_target_pairs={{0,3},{1,2},{2,1},{3,0},{4,7},{5,6},{6,5},{7,4},{8,11},{9,10},{10,... | collective-permute-start | bytes 196616 | tf_op jit(solution)/shard_map/ppermute | solution.py:583
  80.6 2.8 %collective-permute-done.25.refs_2_ = f32[128,128]{1,0:T(8,128)S(1)} collective-permute-done((f32[128,128]{1,0:T(8,128)S(1)}, f32[128,128]{1,0:T(8,128)S(1)}, u32[]{:S(2)}, u32[]{:S(2)}) %collective-permute-start.25) | collective-permute-done | bytes 65568 | tf_op jit(solution)/shard_map/ppermute | solution.py:583
  83.5 1.5 %collective-permute-done.26.refs_3_ = f32[128,128]{1,0:T(8,128)S(1)} collective-permute-done((f32[128,128]{1,0:T(8,128)S(1)}, f32[128,128]{1,0:T(8,128)S(1)}, u32[]{:S(2)}, u32[]{:S(2)}) %collective-permute-start.26) | collective-permute-done | bytes 65568 | tf_op jit(solution)/shard_map/ppermute | solution.py:583
  85.1 1.0 %collective-permute-start.29 = (f32[128,128]{1,0:T(8,128)S(1)}, f32[128,128]{1,0:T(8,128)S(1)}, u32[]{:S(2)}, u32[]{:S(2)}) collective-permute-start(f32[128,128]{1,0:T(8,128)S(1)} %scale.3.refs_0_), channel_id=1, source_target_pairs={{0,8},{4,12},{8,0},{12,4},{1,9},{5,13},{9,1},{13,5},{2,10},{6,14},... | collective-permute-start | bytes 196616 | tf_op jit(solution)/shard_map/ppermute | solution.py:583
  86.6 2.0 %collective-permute-start.27 = (f32[128,128]{1,0:T(8,128)S(1)}, f32[128,128]{1,0:T(8,128)S(1)}, u32[]{:S(2)}, u32[]{:S(2)}) collective-permute-start(f32[128,128]{1,0:T(8,128)S(1)} %scale.3.refs_0_), channel_id=1, source_target_pairs={{0,24},{4,28},{8,16},{12,20},{16,8},{20,12},{24,0},{28,4},{1,25},{... | collective-permute-start | bytes 196616 | tf_op jit(solution)/shard_map/ppermute | solution.py:589
  88.6 1.0 %join.1 = f32[8,96,256]{2,1,0:T(8,128)} custom-call(f32[8,96,128]{2,1,0:T(8,128)S(1)} %get-tuple-element.80.own.residual, f32[8,96,128]{2,1,0:T(8,128)S(1)} %collective-permute-done.30.other.residual), custom_call_target="tpu_custom_call" | custom-call | flops 1000000 | bytes 2000000 | tf_op jit(solution)/shard_map/join/pallas_call | solution.py:532
  90.0 0.7 first_half.4.base
  91.0 0.7 second_half.3.own
  92.0 0.7 first_half.5.other
  93.3 1.5 %final.1 = f32[8,96,256]{2,1,0:T(8,128)} custom-call(f32[8,96,128]{2,1,0:T(8,128)S(1)} %second_half.3.own, f32[8,96,128]{2,1,0:T(8,128)S(1)} %first_half.5.other, bf16[8,2,192,512]{3,2,1,0:T(8,128)(2,1)S(1)} %get-tuple-element.57.vectors, f32[128,128]{1,0:T(8,128)S(1)} %collective-permute-done.33.refs_0_, f32[128,128]{1,0:T(8,128)S(1)} %collective-permute-done.34.refs_1_), custom_call_target="tpu_custom_call" | custom-call | flops 1000000000 | bytes 4000000 | tf_op jit(solution)/shard_map/final/pallas_call | solution.py:560
  (53 shorter events, 7.4 us)
Async XLA Ops:
  0.6 1.1 %copy-start = (f32[1,1,2,4,96,256]{5,4,3,2,1,0:T(8,128)S(1)}, f32[1,1,2,4,96,256]{5,4,3,2,1,0:T(8,128)}, u32[]{:S(2)}) copy-start(f32[1,1,2,4,96,256]{5,4,3,2,1,0:T(8,128)} %param.7) | copy-start | bytes 2359300
  2.0 6.4 %collective-permute-start = (f32[8,96,128]{2,1,0:T(8,128)S(1)}, f32[8,96,128]{2,1,0:T(8,128)S(1)}, u32[]{:S(2)}, u32[]{:S(2)}) collective-permute-start(f32[8,96,128]{2,1,0:T(8,128)S(1)} %get-tuple-element.45.x_ref.x), channel_id=1, source_target_pairs={{0,4},{4,0},{8,12},{12,8},{1,5},{5,1},{9,13},{13,9},{2,6},{6,2},{1... | collective-permute-start | bytes 1179656 | tf_op jit(solution)/shard_map/ppermute | solution.py:583
  2.6 21.1 %collective-permute-start.2 = (f32[4,96,128]{2,1,0:T(8,128)S(1)}, f32[4,96,128]{2,1,0:T(8,128)S(1)}, u32[]{:S(2)}, u32[]{:S(2)}) collective-permute-start(f32[4,96,128]{2,1,0:T(8,128)S(1)} %get-tuple-element.49), channel_id=1, source_target_pairs={{0,1},{1,2},{2,3},{3,0},{4,5},{5,6},{6,7},{7,4},{8,9},{9,10},{10,1... | collective-permute-start | bytes 589832 | tf_op jit(solution)/shard_map/ppermute | solution.py:578
  5.2 18.5 %collective-permute-start.3 = (f32[4,96,128]{2,1,0:T(8,128)S(1)}, f32[4,96,128]{2,1,0:T(8,128)S(1)}, u32[]{:S(2)}, u32[]{:S(2)}) collective-permute-start(f32[4,96,128]{2,1,0:T(8,128)S(1)} %get-tuple-element.49), channel_id=1, source_target_pairs={{0,3},{1,0},{2,1},{3,2},{4,7},{5,4},{6,5},{7,6},{8,11},{9,8},{10,9... | collective-permute-start | bytes 589832 | tf_op jit(solution)/shard_map/ppermute | solution.py:578
  7.3 16.9 %collective-permute-start.1 = (f32[8,96,128]{2,1,0:T(8,128)S(1)}, f32[8,96,128]{2,1,0:T(8,128)S(1)}, u32[]{:S(2)}, u32[]{:S(2)}) collective-permute-start(f32[8,96,128]{2,1,0:T(8,128)S(1)} %get-tuple-element.45.x_ref.x), channel_id=1, source_target_pairs={{0,12},{4,8},{8,4},{12,0},{1,13},{5,9},{9,5},{13,1},{2,14},{6,10},... | collective-permute-start | bytes 1179656 | tf_op jit(solution)/shard_map/ppermute | solution.py:596
  8.5 16.8 %collective-permute-start.4 = (f32[4,96,128]{2,1,0:T(8,128)S(1)}, f32[4,96,128]{2,1,0:T(8,128)S(1)}, u32[]{:S(2)}, u32[]{:S(2)}) collective-permute-start(f32[4,96,128]{2,1,0:T(8,128)S(1)} %get-tuple-element.55), channel_id=1, source_target_pairs={{0,1},{1,2},{2,3},{3,0},{4,5},{5,6},{6,7},{7,4},{8,9},{9,10},{10,1... | collective-permute-start | bytes 589832 | tf_op jit(solution)/shard_map/ppermute | solution.py:578
  8.5 17.1 %collective-permute-start.5 = (f32[4,96,128]{2,1,0:T(8,128)S(1)}, f32[4,96,128]{2,1,0:T(8,128)S(1)}, u32[]{:S(2)}, u32[]{:S(2)}) collective-permute-start(f32[4,96,128]{2,1,0:T(8,128)S(1)} %get-tuple-element.55), channel_id=1, source_target_pairs={{0,3},{1,0},{2,1},{3,2},{4,7},{5,4},{6,5},{7,6},{8,11},{9,8},{10,9... | collective-permute-start | bytes 589832 | tf_op jit(solution)/shard_map/ppermute | solution.py:578
  25.6 6.8 %copy-start.1 = (f32[2,512]{1,0:T(2,128)S(1)}, f32[2,512]{1,0:T(2,128)}, u32[]{:S(2)}) copy-start(f32[2,512]{1,0:T(2,128)} %inverse.1) | copy-start | bytes 12292
  26.6 1.4 %collective-permute-start.6 = (f32[256,128]{1,0:T(8,128)S(1)}, f32[256,128]{1,0:T(8,128)S(1)}, u32[]{:S(2)}, u32[]{:S(2)}) collective-permute-start(f32[256,128]{1,0:T(8,128)S(1)} %get-tuple-element.59), channel_id=1, source_target_pairs={{0,4},{4,0},{8,12},{12,8},{1,5},{5,1},{9,13},{13,9},{2,6},{6,2},{1... | collective-permute-start | bytes 393224 | tf_op jit(solution)/shard_map/ppermute | solution.py:583
  28.0 4.6 %collective-permute-start.7 = (f32[128,128]{1,0:T(8,128)S(1)}, f32[128,128]{1,0:T(8,128)S(1)}, u32[]{:S(2)}, u32[]{:S(2)}) collective-permute-start(f32[128,128]{1,0:T(8,128)S(1)} %get-tuple-element.61), channel_id=1, source_target_pairs={{0,8},{4,12},{8,0},{12,4},{1,9},{5,13},{9,1},{13,5},{2,10},{6,14},... | collective-permute-start | bytes 196616 | tf_op jit(solution)/shard_map/ppermute | solution.py:583
  28.7 8.2 %collective-permute-start.8 = (f32[128,128]{1,0:T(8,128)S(1)}, f32[128,128]{1,0:T(8,128)S(1)}, u32[]{:S(2)}, u32[]{:S(2)}) collective-permute-start(f32[128,128]{1,0:T(8,128)S(1)} %get-tuple-element.60.refs_0_), channel_id=1, source_target_pairs={{0,2},{1,3},{2,0},{3,1},{4,6},{5,7},{6,4},{7,5},{8,10},{9,11},{10,... | collective-permute-start | bytes 196616 | tf_op jit(solution)/shard_map/ppermute | solution.py:583
  30.0 8.3 %collective-permute-start.9 = (f32[128,128]{1,0:T(8,128)S(1)}, f32[128,128]{1,0:T(8,128)S(1)}, u32[]{:S(2)}, u32[]{:S(2)}) collective-permute-start(f32[128,128]{1,0:T(8,128)S(1)} %get-tuple-element.61), channel_id=1, source_target_pairs={{0,10},{1,11},{2,8},{3,9},{4,14},{5,15},{6,12},{7,13},{8,2},{9,3},... | collective-permute-start | bytes 196616 | tf_op jit(solution)/shard_map/ppermute | solution.py:589
  38.3 5.0 %collective-permute-start.11 = (f32[128,128]{1,0:T(8,128)S(1)}, f32[128,128]{1,0:T(8,128)S(1)}, u32[]{:S(2)}, u32[]{:S(2)}) collective-permute-start(f32[128,128]{1,0:T(8,128)S(1)} %scale.2.left), channel_id=1, source_target_pairs={{0,8},{4,12},{8,0},{12,4},{1,9},{5,13},{9,1},{13,5},{2,10},{6,14},... | collective-permute-start | bytes 196616 | tf_op jit(solution)/shard_map/ppermute | solution.py:583
  39.3 5.2 %collective-permute-start.12 = (f32[128,128]{1,0:T(8,128)S(1)}, f32[128,128]{1,0:T(8,128)S(1)}, u32[]{:S(2)}, u32[]{:S(2)}) collective-permute-start(f32[128,128]{1,0:T(8,128)S(1)} %scale.2.left), channel_id=1, source_target_pairs={{0,9},{1,8},{2,11},{3,10},{4,13},{5,12},{6,15},{7,14},{8,1},{9,0},... | collective-permute-start | bytes 196616 | tf_op jit(solution)/shard_map/ppermute | solution.py:589
  39.8 5.1 %collective-permute-start.10 = (f32[128,128]{1,0:T(8,128)S(1)}, f32[128,128]{1,0:T(8,128)S(1)}, u32[]{:S(2)}, u32[]{:S(2)}) collective-permute-start(f32[128,128]{1,0:T(8,128)S(1)} %scale.2.left), channel_id=1, source_target_pairs={{0,1},{1,0},{2,3},{3,2},{4,5},{5,4},{6,7},{7,6},{8,9},{9,8},{10,11... | collective-permute-start | bytes 196616 | tf_op jit(solution)/shard_map/ppermute | solution.py:583
  44.5 1.3 %collective-permute-start.14 = (f32[128,128]{1,0:T(8,128)S(1)}, f32[128,128]{1,0:T(8,128)S(1)}, u32[]{:S(2)}, u32[]{:S(2)}) collective-permute-start(f32[128,128]{1,0:T(8,128)S(1)} %add.4.refs_1_), channel_id=1, source_target_pairs={{0,4},{4,0},{8,12},{12,8},{1,5},{5,1},{9,13},{13,9},{2,6},{6,2},{1... | collective-permute-start | bytes 196616 | tf_op jit(solution)/shard_map/ppermute | solution.py:583
  44.9 1.3 %collective-permute-start.13 = (f32[128,128]{1,0:T(8,128)S(1)}, f32[128,128]{1,0:T(8,128)S(1)}, u32[]{:S(2)}, u32[]{:S(2)}) collective-permute-start(f32[128,128]{1,0:T(8,128)S(1)} %add.3.refs_0_), channel_id=1, source_target_pairs={{0,4},{4,0},{8,12},{12,8},{1,5},{5,1},{9,13},{13,9},{2,6},{6,2},{1... | collective-permute-start | bytes 196616 | tf_op jit(solution)/shard_map/ppermute | solution.py:583
  46.8 4.4 %collective-permute-start.15 = (f32[8,96,128]{2,1,0:T(8,128)S(1)}, f32[8,96,128]{2,1,0:T(8,128)S(1)}, u32[]{:S(2)}, u32[]{:S(2)}) collective-permute-start(f32[8,96,128]{2,1,0:T(8,128)S(1)} %get-tuple-element.78.x_ref.x), channel_id=1, source_target_pairs={{0,4},{4,0},{8,12},{12,8},{1,5},{5,1},{9,13},{13,9},{2,6},{6,2},{1... | collective-permute-start | bytes 1179656 | tf_op jit(solution)/shard_map/ppermute | solution.py:583
  47.2 9.6 %collective-permute-start.17 = (f32[4,96,128]{2,1,0:T(8,128)S(1)}, f32[4,96,128]{2,1,0:T(8,128)S(1)}, u32[]{:S(2)}, u32[]{:S(2)}) collective-permute-start(f32[4,96,128]{2,1,0:T(8,128)S(1)} %get-tuple-element.68), channel_id=1, source_target_pairs={{0,1},{1,2},{2,3},{3,0},{4,5},{5,6},{6,7},{7,4},{8,9},{9,10},{10,1... | collective-permute-start | bytes 589832 | tf_op jit(solution)/shard_map/ppermute | solution.py:578
  48.4 12.6 %collective-permute-start.18 = (f32[4,96,128]{2,1,0:T(8,128)S(1)}, f32[4,96,128]{2,1,0:T(8,128)S(1)}, u32[]{:S(2)}, u32[]{:S(2)}) collective-permute-start(f32[4,96,128]{2,1,0:T(8,128)S(1)} %get-tuple-element.68), channel_id=1, source_target_pairs={{0,3},{1,0},{2,1},{3,2},{4,7},{5,4},{6,5},{7,6},{8,11},{9,8},{10,9... | collective-permute-start | bytes 589832 | tf_op jit(solution)/shard_map/ppermute | solution.py:578
  51.0 11.3 %collective-permute-start.16 = (f32[8,96,128]{2,1,0:T(8,128)S(1)}, f32[8,96,128]{2,1,0:T(8,128)S(1)}, u32[]{:S(2)}, u32[]{:S(2)}) collective-permute-start(f32[8,96,128]{2,1,0:T(8,128)S(1)} %get-tuple-element.78.x_ref.x), channel_id=1, source_target_pairs={{0,12},{4,8},{8,4},{12,0},{1,13},{5,9},{9,5},{13,1},{2,14},{6,10},... | collective-permute-start | bytes 1179656 | tf_op jit(solution)/shard_map/ppermute | solution.py:596
  51.3 13.9 %collective-permute-start.19 = (f32[4,96,128]{2,1,0:T(8,128)S(1)}, f32[4,96,128]{2,1,0:T(8,128)S(1)}, u32[]{:S(2)}, u32[]{:S(2)}) collective-permute-start(f32[4,96,128]{2,1,0:T(8,128)S(1)} %get-tuple-element.72), channel_id=1, source_target_pairs={{0,1},{1,2},{2,3},{3,0},{4,5},{5,6},{6,7},{7,4},{8,9},{9,10},{10,1... | collective-permute-start | bytes 589832 | tf_op jit(solution)/shard_map/ppermute | solution.py:578
  51.3 16.6 %collective-permute-start.20 = (f32[4,96,128]{2,1,0:T(8,128)S(1)}, f32[4,96,128]{2,1,0:T(8,128)S(1)}, u32[]{:S(2)}, u32[]{:S(2)}) collective-permute-start(f32[4,96,128]{2,1,0:T(8,128)S(1)} %get-tuple-element.72), channel_id=1, source_target_pairs={{0,3},{1,0},{2,1},{3,2},{4,7},{5,4},{6,5},{7,6},{8,11},{9,8},{10,9... | collective-permute-start | bytes 589832 | tf_op jit(solution)/shard_map/ppermute | solution.py:578
  56.7 17.9 %collective-permute-start.23 = (f32[8,96,128]{2,1,0:T(8,128)S(1)}, f32[8,96,128]{2,1,0:T(8,128)S(1)}, u32[]{:S(2)}, u32[]{:S(2)}) collective-permute-start(f32[8,96,128]{2,1,0:T(8,128)S(1)} %get-tuple-element.78.x_ref.x), channel_id=1, source_target_pairs={{0,16},{16,0},{1,17},{17,1},{2,18},{18,2},{3,19},{19,3},{4,20},{20... | collective-permute-start | bytes 1179656 | tf_op jit(solution)/shard_map/ppermute | solution.py:583
  68.8 1.4 %collective-permute-start.21 = (f32[256,128]{1,0:T(8,128)S(1)}, f32[256,128]{1,0:T(8,128)S(1)}, u32[]{:S(2)}, u32[]{:S(2)}) collective-permute-start(f32[256,128]{1,0:T(8,128)S(1)} %get-tuple-element.74), channel_id=1, source_target_pairs={{0,4},{4,0},{8,12},{12,8},{1,5},{5,1},{9,13},{13,9},{2,6},{6,2},{1... | collective-permute-start | bytes 393224 | tf_op jit(solution)/shard_map/ppermute | solution.py:583
  70.3 4.3 %collective-permute-start.22 = (f32[128,128]{1,0:T(8,128)S(1)}, f32[128,128]{1,0:T(8,128)S(1)}, u32[]{:S(2)}, u32[]{:S(2)}) collective-permute-start(f32[128,128]{1,0:T(8,128)S(1)} %get-tuple-element.76), channel_id=1, source_target_pairs={{0,8},{4,12},{8,0},{12,4},{1,9},{5,13},{9,1},{13,5},{2,10},{6,14},... | collective-permute-start | bytes 196616 | tf_op jit(solution)/shard_map/ppermute | solution.py:583
  74.6 14.0 %collective-permute-start.30 = (f32[8,96,128]{2,1,0:T(8,128)S(1)}, f32[8,96,128]{2,1,0:T(8,128)S(1)}, u32[]{:S(2)}, u32[]{:S(2)}) collective-permute-start(f32[8,96,128]{2,1,0:T(8,128)S(1)} %get-tuple-element.80.own.residual), channel_id=1, source_target_pairs={{0,16},{16,0},{1,17},{17,1},{2,18},{18,2},{3,19},{19,3},{4,20},{20... | collective-permute-start | bytes 1179656 | tf_op jit(solution)/shard_map/ppermute | solution.py:583
  76.2 4.4 %collective-permute-start.24 = (f32[128,128]{1,0:T(8,128)S(1)}, f32[128,128]{1,0:T(8,128)S(1)}, u32[]{:S(2)}, u32[]{:S(2)}) collective-permute-start(f32[128,128]{1,0:T(8,128)S(1)} %add.5.refs_0_), channel_id=1, source_target_pairs={{0,1},{1,0},{2,3},{3,2},{4,5},{5,4},{6,7},{7,6},{8,9},{9,8},{10,11... | collective-permute-start | bytes 196616 | tf_op jit(solution)/shard_map/ppermute | solution.py:583
  76.9 6.6 %collective-permute-start.25 = (f32[128,128]{1,0:T(8,128)S(1)}, f32[128,128]{1,0:T(8,128)S(1)}, u32[]{:S(2)}, u32[]{:S(2)}) collective-permute-start(f32[128,128]{1,0:T(8,128)S(1)} %add.5.refs_0_), channel_id=1, source_target_pairs={{0,2},{1,3},{2,0},{3,1},{4,6},{5,7},{6,4},{7,5},{8,10},{9,11},{10,... | collective-permute-start | bytes 196616 | tf_op jit(solution)/shard_map/ppermute | solution.py:583
  78.9 6.1 %collective-permute-start.26 = (f32[128,128]{1,0:T(8,128)S(1)}, f32[128,128]{1,0:T(8,128)S(1)}, u32[]{:S(2)}, u32[]{:S(2)}) collective-permute-start(f32[128,128]{1,0:T(8,128)S(1)} %add.5.refs_0_), channel_id=1, source_target_pairs={{0,3},{1,2},{2,1},{3,0},{4,7},{5,6},{6,5},{7,4},{8,11},{9,10},{10,... | collective-permute-start | bytes 196616 | tf_op jit(solution)/shard_map/ppermute | solution.py:583
  85.1 4.6 %collective-permute-start.29 = (f32[128,128]{1,0:T(8,128)S(1)}, f32[128,128]{1,0:T(8,128)S(1)}, u32[]{:S(2)}, u32[]{:S(2)}) collective-permute-start(f32[128,128]{1,0:T(8,128)S(1)} %scale.3.refs_0_), channel_id=1, source_target_pairs={{0,8},{4,12},{8,0},{12,4},{1,9},{5,13},{9,1},{13,5},{2,10},{6,14},... | collective-permute-start | bytes 196616 | tf_op jit(solution)/shard_map/ppermute | solution.py:583
  86.1 4.6 %collective-permute-start.28 = (f32[128,128]{1,0:T(8,128)S(1)}, f32[128,128]{1,0:T(8,128)S(1)}, u32[]{:S(2)}, u32[]{:S(2)}) collective-permute-start(f32[128,128]{1,0:T(8,128)S(1)} %scale.3.refs_0_), channel_id=1, source_target_pairs={{0,16},{16,0},{1,17},{17,1},{2,18},{18,2},{3,19},{19,3},{4,20},{20... | collective-permute-start | bytes 196616 | tf_op jit(solution)/shard_map/ppermute | solution.py:583
  86.6 4.4 %collective-permute-start.31 = (f32[128,128]{1,0:T(8,128)S(1)}, f32[128,128]{1,0:T(8,128)S(1)}, u32[]{:S(2)}, u32[]{:S(2)}) collective-permute-start(f32[128,128]{1,0:T(8,128)S(1)} %scale.3.refs_0_), channel_id=1, source_target_pairs={{0,4},{4,0},{8,12},{12,8},{1,5},{5,1},{9,13},{13,9},{2,6},{6,2},{1... | collective-permute-start | bytes 196616 | tf_op jit(solution)/shard_map/ppermute | solution.py:583
  86.6 5.4 %collective-permute-start.27 = (f32[128,128]{1,0:T(8,128)S(1)}, f32[128,128]{1,0:T(8,128)S(1)}, u32[]{:S(2)}, u32[]{:S(2)}) collective-permute-start(f32[128,128]{1,0:T(8,128)S(1)} %scale.3.refs_0_), channel_id=1, source_target_pairs={{0,24},{4,28},{8,16},{12,20},{16,8},{20,12},{24,0},{28,4},{1,25},{... | collective-permute-start | bytes 196616 | tf_op jit(solution)/shard_map/ppermute | solution.py:589
  89.7 1.3 %collective-permute-start.32 = (f32[128,128]{1,0:T(8,128)S(1)}, f32[128,128]{1,0:T(8,128)S(1)}, u32[]{:S(2)}, u32[]{:S(2)}) collective-permute-start(f32[128,128]{1,0:T(8,128)S(1)} %collective-permute-done.29.refs_1_), channel_id=1, source_target_pairs={{0,4},{4,0},{8,12},{12,8},{1,5},{5,1},{9,13},{13,9},{2,6},{6,2},{1... | collective-permute-start | bytes 196616 | tf_op jit(solution)/shard_map/ppermute | solution.py:583
  90.7 2.0 %collective-permute-start.33 = (f32[128,128]{1,0:T(8,128)S(1)}, f32[128,128]{1,0:T(8,128)S(1)}, u32[]{:S(2)}, u32[]{:S(2)}) collective-permute-start(f32[128,128]{1,0:T(8,128)S(1)} %collective-permute-done.28.refs_0_), channel_id=1, source_target_pairs={{0,4},{4,0},{8,12},{12,8},{1,5},{5,1},{9,13},{13,9},{2,6},{6,2},{1... | collective-permute-start | bytes 196616 | tf_op jit(solution)/shard_map/ppermute | solution.py:583
  92.0 1.3 %collective-permute-start.34 = (f32[128,128]{1,0:T(8,128)S(1)}, f32[128,128]{1,0:T(8,128)S(1)}, u32[]{:S(2)}, u32[]{:S(2)}) collective-permute-start(f32[128,128]{1,0:T(8,128)S(1)} %collective-permute-done.27.refs_1_), channel_id=1, source_target_pairs={{0,4},{4,0},{8,12},{12,8},{1,5},{5,1},{9,13},{13,9},{2,6},{6,2},{1... | collective-permute-start | bytes 196616 | tf_op jit(solution)/shard_map/ppermute | solution.py:583

commit v13 on v12

--- a/solution.py
+++ b/solution.py
@@ -128,59 +128,6 @@
         term = matmul(local[direction, site], stacks[neighbour])
         total = term if total is None else total + term
     return fold(total)
-
-
-def first_kernel(ny, nx, x_ref, source, couplings, rest, half_source, local, halo, stacks, held, held_source, sems):
-    group = lax.axis_index("groups")
-    sites = x_ref.shape[0]
-    copies = []
-    for site in range(sites):
-        copies.append(pltpu.make_async_copy(couplings.at[:, site], held.at[site], sems.at[site]))
-        copies[-1].start()
-    bring = pltpu.make_async_copy(source, held_source, sems.at[sites])
-    bring.start()
-    for site in range(sites):
-        stacks[site] = stack(x_ref[site], 1.0)
-    bring.wait()
-    for site in range(sites):
-        half_source[site] = pick_half(held_source[site], group)
-    for site in range(sites):
-        copies[site].wait()
-        for direction in range(couplings.shape[0]):
-            high, low = high_low(held[site, direction])
-            both = jnp.concatenate([high, low], axis=0)
-            if direction < LOCAL:
-                local[direction, site] = both
-            else:
-                halo[direction - LOCAL, site] = both
-        rest[site] = half_source[site] - local_sum(site, ny, nx, stacks, local)
-
-
-def first_local(x, source, couplings, ny, nx):
-    sites, rows, lanes = x.shape
-    directions, _, _, columns = couplings.shape
-    outer = directions - LOCAL
-    in_place = pl.BlockSpec(memory_space=pl.ANY)
-    return pl.pallas_call(
-        functools.partial(first_kernel, ny, nx),
-        out_shape=(
-            pltpu.VMEM(x.shape, F32),
-            pltpu.VMEM(x.shape, F32),
-            pltpu.VMEM((LOCAL, sites, 2 * rows, columns), BF16),
-            pltpu.VMEM((outer, sites, 2 * rows, columns), BF16),
-        ),
-        in_specs=vmem(1) + [in_place, in_place],
-        out_specs=tuple(vmem(4)),
-        scratch_shapes=[
-            pltpu.VMEM((sites, 2 * rows, 2 * lanes), BF16),
-            pltpu.VMEM((sites, directions, rows, columns), F32),
-            pltpu.VMEM(source.shape, F32),
-            pltpu.SemaphoreType.DMA((sites + 1,)),
-        ],
-        compiler_params=params(20),
-        cost_estimate=cost(8e9, 16e6),
-        name="first_local",
-    )(x, in_hbm(source), in_hbm(couplings))
 
 
 def local_kernel(ny, nx, x_ref, source, local, rest, stacks):
@@ -221,44 +168,84 @@
     return parts[0] if len(parts) == 1 else jnp.concatenate(parts, axis=0)
 
 
-def vectors_kernel(across, by_rows, by_columns, turned_rows):
-    sites, _, double, number = by_columns.shape
-    rows = double // 2
-    taken = 128
-    turned_rows[...] = across[...].T
-    for chunk in range(number // taken):
-        part = ordered_rows(turned_rows, chunk, taken)
-        high, low = high_low(part)
-        at = slice(chunk * taken, (chunk + 1) * taken)
-        by_rows[at] = high
-        by_rows[number + chunk * taken : number + (chunk + 1) * taken] = low
-        back = part.T
-        for site in range(sites):
-            for half in range(2):
-                start = (2 * site + half) * rows
-                high, low = high_low(back[start : start + rows])
-                by_columns[site, half, :rows, at] = high
-                by_columns[site, half, rows:, at] = low
-
-
-def vectors_parts(across, sites):
+def prepare_kernel(ny, nx, x_ref, source, couplings, across, rest, half_source, local, halo, by_rows, by_columns, stacks, held, held_source, held_across, turned_rows, sems):
+    group = lax.axis_index("groups")
+    sites, directions, rows = held.shape[:3]
+    number = held_across.shape[1]
+    taken, step = 128, turned_rows.shape[1]
+    arriving = []
+    for site in range(sites):
+        arriving.append(pltpu.make_async_copy(couplings.at[:, site], held.at[site], sems.at[site]))
+    arriving.append(pltpu.make_async_copy(source, held_source, sems.at[sites]))
+    for index in range(held_across.shape[0] // step):
+        at = pl.ds(index * step, step)
+        arriving.append(pltpu.make_async_copy(across.at[at], held_across.at[at], sems.at[sites + 1 + index]))
+    for copy in arriving:
+        copy.start()
+    for site in range(sites):
+        stacks[site] = stack(x_ref[site], 1.0)
+    for site in range(sites):
+        arriving[site].wait()
+        for direction in range(directions):
+            high, low = high_low(held[site, direction])
+            both = jnp.concatenate([high, low], axis=0)
+            if direction < LOCAL:
+                local[direction, site] = both
+            else:
+                halo[direction - LOCAL, site] = both
+        if site == 0:
+            arriving[sites].wait()
+        own = pick_half(held_source[site], group)
+        half_source[site] = own
+        rest[site] = own - local_sum(site, ny, nx, stacks, local)
+    for index, copy in enumerate(arriving[sites + 1 :]):
+        copy.wait()
+        at = slice(index * step, (index + 1) * step)
+        turned_rows[...] = held_across[at].T
+        for chunk in range(number // taken):
+            part = ordered_rows(turned_rows, chunk, taken)
+            high, low = high_low(part)
+            by_rows[chunk * taken : (chunk + 1) * taken, at] = high
+            by_rows[number + chunk * taken : number + (chunk + 1) * taken, at] = low
+            back = part.T
+            for half in range(step // rows):
+                high, low = high_low(back[half * rows : (half + 1) * rows])
+                site, which = divmod(index * (step // rows) + half, 2)
+                lanes = slice(chunk * taken, (chunk + 1) * taken)
+                by_columns[site, which, :rows, lanes] = high
+                by_columns[site, which, rows:, lanes] = low
+
+
+def prepare(x, source, couplings, across, ny, nx):
+    sites, rows, lanes = x.shape
+    directions, _, _, columns = couplings.shape
     width, number = across.shape
-    rows = width // sites // 2
-    step = 2
-    return pl.pallas_call(
-        vectors_kernel,
-        grid=(sites // step,),
-        out_shape=(pltpu.VMEM((2 * number, width), BF16), pltpu.VMEM((sites, 2, 2 * rows, number), BF16)),
-        in_specs=[pl.BlockSpec((step * 2 * rows, number), lambda s: (s, 0))],
-        out_specs=(
-            pl.BlockSpec((2 * number, step * 2 * rows), lambda s: (0, s)),
-            pl.BlockSpec((step, 2, 2 * rows, number), lambda s: (s, 0, 0, 0)),
+    outer = directions - LOCAL
+    step = width // (sites // 2)
+    return pl.pallas_call(
+        functools.partial(prepare_kernel, ny, nx),
+        out_shape=(
+            pltpu.VMEM(x.shape, F32),
+            pltpu.VMEM(x.shape, F32),
+            pltpu.VMEM((LOCAL, sites, 2 * rows, columns), BF16),
+            pltpu.VMEM((outer, sites, 2 * rows, columns), BF16),
+            pltpu.VMEM((2 * number, width), BF16),
+            pltpu.VMEM((sites, 2, 2 * rows, number), BF16),
         ),
-        scratch_shapes=[pltpu.VMEM((number, step * 2 * rows), F32)],
-        compiler_params=params(16),
-        cost_estimate=cost(1e6, 9e6),
-        name="vectors_parts",
-    )(in_hbm(across))
+        in_specs=vmem(1) + [pl.BlockSpec(memory_space=pl.ANY)] * 3,
+        out_specs=tuple(vmem(6)),
+        scratch_shapes=[
+            pltpu.VMEM((sites, 2 * rows, 2 * lanes), BF16),
+            pltpu.VMEM((sites, directions, rows, columns), F32),
+            pltpu.VMEM(source.shape, F32),
+            pltpu.VMEM(across.shape, F32),
+            pltpu.VMEM((number, step), F32),
+            pltpu.SemaphoreType.DMA((sites + 1 + width // step,)),
+        ],
+        compiler_params=params(24),
+        cost_estimate=cost(8e9, 25e6),
+        name="prepare",
+    )(x, in_hbm(source), in_hbm(couplings), in_hbm(across))
 
 
 def eigen_kernel(inverse, out):
@@ -647,9 +634,10 @@
     x, early_x, late_x = pack(initial.reshape(sites, rows, lanes))
     faces = faces_of(x, early_x, late_x)
     matrices = couplings.reshape(directions, sites, rows, couplings.shape[-1])
-    rest, half_source, local, halo = first_local(x, source.reshape(sites, rows, lanes), matrices, ny, nx)
     across = jnp.transpose(vectors, (1, 2, 3, 4, 5, 0)).reshape(sites * vectors.shape[-1], number)
-    by_rows, by_columns = vectors_parts(across, sites)
+    rest, half_source, local, halo, by_rows, by_columns = prepare(
+        x, source.reshape(sites, rows, lanes), matrices, across, ny, nx
+    )
     eigen = eigen_of(inverse_eigen, number // blocks, lanes // 2)
 
     for sweep in range(ITERS):

time: 95.1 us -> 95.1 us (level)
  Pallas kernels: 24.7 us -> 22.4 us
  waiting for transfers between devices: 28.2 us -> 29.8 us
    pallas_call x2 -> x1, Pallas kernels: 11.4 us -> 9.08 us  [prepare(): pl.pallas_call(functools.partial(prepare_kernel, ny, nx), out_shape=(pltp...]
    ppermute x22, starting transfers between devices: 17.1 us -> 19.1 us  [crossed(): return lax.ppermute(value, axis, [(i, i ^ mask) for i in range(count)])]
    ppermute x3, starting transfers between devices: 4.98 us -> 3.7 us  [crossed_both(): return lax.ppermute(value, (first, second), pairs)]
  transfers between devices with their start and end apart: 35 -> 35, of which waited for: 18 -> 19; matrix products, arithmetic and copies ran while one was open for 0% -> 0% of each run, Pallas kernels for 22% -> 20%
where the time goes in v13:
time: 95.1 us; the launch traced here: 94.9 us
  starting transfers between devices  40.4 us (42%)
  waiting for transfers between devices  29.8 us (31%)
  Pallas kernels  22.4 us (24%)
  local copies, waits for them, and re-layouts  1.13 us (1%)
  between operations  1.08 us (1%)
    ppermute x22, starting transfers between devices, crossed(): return lax.ppermute(value, axis, [(i, i ^ mask) for i in range(count)])  19.1 us
    ppermute x22, waiting for transfers between devices, crossed(): return lax.ppermute(value, axis, [(i, i ^ mask) for i in range(count)])  17.6 us
    ppermute x8, starting transfers between devices, shifted(): lax.ppermute(value, axis, [(i, (i + step) % count) for i in range(count)])  16.2 us
    pallas_call x1, Pallas kernels, prepare(): pl.pallas_call(functools.partial(prepare_kernel, ny, nx), out_shape=(pltp...  9.08 us
    ppermute x8, waiting for transfers between devices, shifted(): lax.ppermute(value, axis, [(i, (i + step) % count) for i in range(count)])  7.56 us
    ppermute x3, starting transfers between devices, crossed_both(): return lax.ppermute(value, (first, second), pairs)  3.7 us
    ppermute x3, waiting for transfers between devices, crossed_both(): return lax.ppermute(value, (first, second), pairs)  3.16 us
    pallas_call x2, Pallas kernels, middle(): pl.pallas_call(middle_kernel, out_shape=(half, half, pltpu.VMEM((vectors....  2.15 us
  transfers between devices with their start and end apart: 35, of which 19 were waited for; matrix products, arithmetic and copies ran while one was open for 0% of the time, Pallas kernels for 20%

profile of v13, /device:TPU:0, one launch (start us, length us, event | category | flops | bytes accessed | tf_op | source)
XLA Modules:
  0.0 94.9 jit_solution(8987245138758132337)
XLA Ops:
  0.6 1.1 %copy-done = f32[1,1,2,4,96,256]{5,4,3,2,1,0:T(8,128)S(1)} copy-done((f32[1,1,2,4,96,256]{5,4,3,2,1,0:T(8,128)S(1)}, f32[1,1,2,4,96,256]{5,4,3,2,1,0:T(8,128)}, u32[]{:S(2)}) %copy-start) | copy-done | bytes 786456
  2.6 2.6 %collective-permute-start.2 = (f32[4,96,128]{2,1,0:T(8,128)S(1)}, f32[4,96,128]{2,1,0:T(8,128)S(1)}, u32[]{:S(2)}, u32[]{:S(2)}) collective-permute-start(f32[4,96,128]{2,1,0:T(8,128)S(1)} %get-tuple-element.49), channel_id=1, source_target_pairs={{0,1},{1,2},{2,3},{3,0},{4,5},{5,6},{6,7},{7,4},{8,9},{9,10},{10,1... | collective-permute-start | bytes 589832 | tf_op jit(solution)/shard_map/ppermute | solution.py:565
  5.2 2.1 %collective-permute-start.3 = (f32[4,96,128]{2,1,0:T(8,128)S(1)}, f32[4,96,128]{2,1,0:T(8,128)S(1)}, u32[]{:S(2)}, u32[]{:S(2)}) collective-permute-start(f32[4,96,128]{2,1,0:T(8,128)S(1)} %get-tuple-element.49), channel_id=1, source_target_pairs={{0,3},{1,0},{2,1},{3,2},{4,7},{5,4},{6,5},{7,6},{8,11},{9,8},{10,9... | collective-permute-start | bytes 589832 | tf_op jit(solution)/shard_map/ppermute | solution.py:565
  7.3 1.2 %collective-permute-start.1 = (f32[8,96,128]{2,1,0:T(8,128)S(1)}, f32[8,96,128]{2,1,0:T(8,128)S(1)}, u32[]{:S(2)}, u32[]{:S(2)}) collective-permute-start(f32[8,96,128]{2,1,0:T(8,128)S(1)} %get-tuple-element.45.x_ref.x), channel_id=1, source_target_pairs={{0,12},{4,8},{8,4},{12,0},{1,13},{5,9},{9,5},{13,1},{2,14},{6,10},... | collective-permute-start | bytes 1179656 | tf_op jit(solution)/shard_map/ppermute | solution.py:583
  8.5 3.8 %collective-permute-start.5 = (f32[4,96,128]{2,1,0:T(8,128)S(1)}, f32[4,96,128]{2,1,0:T(8,128)S(1)}, u32[]{:S(2)}, u32[]{:S(2)}) collective-permute-start(f32[4,96,128]{2,1,0:T(8,128)S(1)} %get-tuple-element.55), channel_id=1, source_target_pairs={{0,3},{1,0},{2,1},{3,2},{4,7},{5,4},{6,5},{7,6},{8,11},{9,8},{10,9... | collective-permute-start | bytes 589832 | tf_op jit(solution)/shard_map/ppermute | solution.py:565
  12.3 9.1 %prepare.1 = (f32[8,96,128]{2,1,0:T(8,128)S(1)}, f32[8,96,128]{2,1,0:T(8,128)S(1)}, bf16[5,8,192,192]{3,2,1,0:T(8,128)(2,1)S(1)}, bf16[4,8,192,192]{3,2,1,0:T(8,...) custom-call(f32[8,96,128]{2,1,0:T(8,128)S(1)} %get-tuple-element.45.x_ref.x, ...), custom_call_target="tpu_custom_call" | custom-call | flops 8000000000 | bytes 25000000 | tf_op jit(solution)/shard_map/prepare/pallas_call | solution.py:225
  21.9 1.1 %middle.2 = (f32[4,96,128]{2,1,0:T(8,128)S(1)}, f32[4,96,128]{2,1,0:T(8,128)S(1)}, f32[512,128]{1,0:T(8,128)S(1)}) custom-call(f32[8,96,128]{2,1,0:T(8,128)S(1)} %get-tuple-element.46.rest, f32[8,96,128]{2,1,0:T(8,128)S(1)} %collective-permute-done.near, f32[8,96,128]{2,1,0:T(8,128)S(1)} %collective-permute-done.1.far, f32[4,96,128]{2,1,0:T(8,128)S(1)} %front_faces.2.front, ...), custom_call_target="tpu_custom_call" | custom-call | flops 1000 | bytes 1000 | tf_op jit(solution)/shard_map/middle/pallas_call | solution.py:322
  23.3 1.5 %collective-permute-done.5.forward = f32[4,96,128]{2,1,0:T(8,128)S(1)} collective-permute-done((f32[4,96,128]{2,1,0:T(8,128)S(1)}, f32[4,96,128]{2,1,0:T(8,128)S(1)}, u32[]{:S(2)}, u32[]{:S(2)}) %collective-permute-start.5) | collective-permute-done | bytes 196640 | tf_op jit(solution)/shard_map/ppermute | solution.py:565
  24.8 0.9 forward_face.2
  25.8 1.3 %collective-permute-done.6.received = f32[256,128]{1,0:T(8,128)S(1)} collective-permute-done((f32[256,128]{1,0:T(8,128)S(1)}, f32[256,128]{1,0:T(8,128)S(1)}, u32[]{:S(2)}, u32[]{:S(2)}) %collective-permute-start.6) | collective-permute-done | bytes 131104 | tf_op jit(solution)/shard_map/ppermute | solution.py:570
  27.2 1.6 %collective-permute-start.7 = (f32[128,128]{1,0:T(8,128)S(1)}, f32[128,128]{1,0:T(8,128)S(1)}, u32[]{:S(2)}, u32[]{:S(2)}) collective-permute-start(f32[128,128]{1,0:T(8,128)S(1)} %get-tuple-element.61), channel_id=1, source_target_pairs={{0,8},{4,12},{8,0},{12,4},{1,9},{5,13},{9,1},{13,5},{2,10},{6,14},... | collective-permute-start | bytes 196616 | tf_op jit(solution)/shard_map/ppermute | solution.py:570
  28.7 1.2 %collective-permute-start.8 = (f32[128,128]{1,0:T(8,128)S(1)}, f32[128,128]{1,0:T(8,128)S(1)}, u32[]{:S(2)}, u32[]{:S(2)}) collective-permute-start(f32[128,128]{1,0:T(8,128)S(1)} %get-tuple-element.60.refs_0_), channel_id=1, source_target_pairs={{0,2},{1,3},{2,0},{3,1},{4,6},{5,7},{6,4},{7,5},{8,10},{9,11},{10,... | collective-permute-start | bytes 196616 | tf_op jit(solution)/shard_map/ppermute | solution.py:570
  30.0 1.7 %collective-permute-start.9 = (f32[128,128]{1,0:T(8,128)S(1)}, f32[128,128]{1,0:T(8,128)S(1)}, u32[]{:S(2)}, u32[]{:S(2)}) collective-permute-start(f32[128,128]{1,0:T(8,128)S(1)} %get-tuple-element.61), channel_id=1, source_target_pairs={{0,10},{1,11},{2,8},{3,9},{4,14},{5,15},{6,12},{7,13},{8,2},{9,3},... | collective-permute-start | bytes 196616 | tf_op jit(solution)/shard_map/ppermute | solution.py:576
  31.8 5.2 %collective-permute-done.8.refs_2_ = f32[128,128]{1,0:T(8,128)S(1)} collective-permute-done((f32[128,128]{1,0:T(8,128)S(1)}, f32[128,128]{1,0:T(8,128)S(1)}, u32[]{:S(2)}, u32[]{:S(2)}) %collective-permute-start.8) | collective-permute-done | bytes 65568 | tf_op jit(solution)/shard_map/ppermute | solution.py:570
  37.0 0.7 collective-permute-done.9.refs_3_
  37.8 1.6 %collective-permute-start.11 = (f32[128,128]{1,0:T(8,128)S(1)}, f32[128,128]{1,0:T(8,128)S(1)}, u32[]{:S(2)}, u32[]{:S(2)}) collective-permute-start(f32[128,128]{1,0:T(8,128)S(1)} %scale.2.left), channel_id=1, source_target_pairs={{0,8},{4,12},{8,0},{12,4},{1,9},{5,13},{9,1},{13,5},{2,10},{6,14},... | collective-permute-start | bytes 196616 | tf_op jit(solution)/shard_map/ppermute | solution.py:570
  39.8 1.6 %collective-permute-start.10 = (f32[128,128]{1,0:T(8,128)S(1)}, f32[128,128]{1,0:T(8,128)S(1)}, u32[]{:S(2)}, u32[]{:S(2)}) collective-permute-start(f32[128,128]{1,0:T(8,128)S(1)} %scale.2.left), channel_id=1, source_target_pairs={{0,1},{1,0},{2,3},{3,2},{4,5},{5,4},{6,7},{7,6},{8,9},{9,8},{10,11... | collective-permute-start | bytes 196616 | tf_op jit(solution)/shard_map/ppermute | solution.py:570
  41.3 1.5 %collective-permute-done.11.left = f32[128,128]{1,0:T(8,128)S(1)} collective-permute-done((f32[128,128]{1,0:T(8,128)S(1)}, f32[128,128]{1,0:T(8,128)S(1)}, u32[]{:S(2)}, u32[]{:S(2)}) %collective-permute-start.11) | collective-permute-done | bytes 65568 | tf_op jit(solution)/shard_map/ppermute | solution.py:570
  42.8 1.7 %collective-permute-done.12.right = f32[128,128]{1,0:T(8,128)S(1)} collective-permute-done((f32[128,128]{1,0:T(8,128)S(1)}, f32[128,128]{1,0:T(8,128)S(1)}, u32[]{:S(2)}, u32[]{:S(2)}) %collective-permute-start.12) | collective-permute-done | bytes 65568 | tf_op jit(solution)/shard_map/ppermute | solution.py:576
  45.2 0.7 first_half.3.base
  46.1 0.7 second_half.2
  47.2 0.7 collective-permute-start.17
  47.8 3.2 %collective-permute-start.18 = (f32[4,96,128]{2,1,0:T(8,128)S(1)}, f32[4,96,128]{2,1,0:T(8,128)S(1)}, u32[]{:S(2)}, u32[]{:S(2)}) collective-permute-start(f32[4,96,128]{2,1,0:T(8,128)S(1)} %get-tuple-element.68), channel_id=1, source_target_pairs={{0,3},{1,0},{2,1},{3,2},{4,7},{5,4},{6,5},{7,6},{8,11},{9,8},{10,9... | collective-permute-start | bytes 589832 | tf_op jit(solution)/shard_map/ppermute | solution.py:565
  51.2 3.8 %collective-permute-start.20 = (f32[4,96,128]{2,1,0:T(8,128)S(1)}, f32[4,96,128]{2,1,0:T(8,128)S(1)}, u32[]{:S(2)}, u32[]{:S(2)}) collective-permute-start(f32[4,96,128]{2,1,0:T(8,128)S(1)} %get-tuple-element.72), channel_id=1, source_target_pairs={{0,3},{1,0},{2,1},{3,2},{4,7},{5,4},{6,5},{7,6},{8,11},{9,8},{10,9... | collective-permute-start | bytes 589832 | tf_op jit(solution)/shard_map/ppermute | solution.py:565
  55.1 1.3 %local_part.1.rest = f32[8,96,128]{2,1,0:T(8,128)S(1)} custom-call(f32[8,96,128]{2,1,0:T(8,128)S(1)} %get-tuple-element.78.x_ref.x, f32[8,96,128]{2,1,0:T(8,128)S(1)} %get-tuple-element.63.source, bf16[5,8,192,192]{3,2,1,0:T(8,128)(2,1)S(1)} %get-tuple-element.64.local), custom_call_target="tpu_custom_call" | custom-call | flops 8000000000 | bytes 8000000 | tf_op jit(solution)/shard_map/local_part/pallas_call | solution.py:142
  56.8 1.5 %collective-permute-start.23 = (f32[8,96,128]{2,1,0:T(8,128)S(1)}, f32[8,96,128]{2,1,0:T(8,128)S(1)}, u32[]{:S(2)}, u32[]{:S(2)}) collective-permute-start(f32[8,96,128]{2,1,0:T(8,128)S(1)} %get-tuple-element.78.x_ref.x), channel_id=1, source_target_pairs={{0,16},{16,0},{1,17},{17,1},{2,18},{18,2},{3,19},{19,3},{4,20},{20... | collective-permute-start | bytes 1179656 | tf_op jit(solution)/shard_map/ppermute | solution.py:570
  58.3 1.9 %collective-permute-done.18.forward = f32[4,96,128]{2,1,0:T(8,128)S(1)} collective-permute-done((f32[4,96,128]{2,1,0:T(8,128)S(1)}, f32[4,96,128]{2,1,0:T(8,128)S(1)}, u32[]{:S(2)}, u32[]{:S(2)}) %collective-permute-start.18) | collective-permute-done | bytes 196640 | tf_op jit(solution)/shard_map/ppermute | solution.py:565
  60.6 1.5 %collective-permute-done.16.far = f32[8,96,128]{2,1,0:T(8,128)S(1)} collective-permute-done((f32[8,96,128]{2,1,0:T(8,128)S(1)}, f32[8,96,128]{2,1,0:T(8,128)S(1)}, u32[]{:S(2)}, u32[]{:S(2)}) %collective-permute-start.16) | collective-permute-done | bytes 393248 | tf_op jit(solution)/shard_map/ppermute | solution.py:583
  62.2 1.1 %middle.3 = (f32[4,96,128]{2,1,0:T(8,128)S(1)}, f32[4,96,128]{2,1,0:T(8,128)S(1)}, f32[512,128]{1,0:T(8,128)S(1)}) custom-call(f32[8,96,128]{2,1,0:T(8,128)S(1)} %local_part.1.rest, f32[8,96,128]{2,1,0:T(8,128)S(1)} %collective-permute-done.15.near, f32[8,96,128]{2,1,0:T(8,128)S(1)} %collective-permute-done.16.far, f32[4,96,128]{2,1,0:T(8,128)S(1)} %front_faces.3.front, ...), custom_call_target="tpu_custom_call" | custom-call | flops 1000 | bytes 1000 | tf_op jit(solution)/shard_map/middle/pallas_call | solution.py:322
  63.3 2.0 %collective-permute-done.19.backward = f32[4,96,128]{2,1,0:T(8,128)S(1)} collective-permute-done((f32[4,96,128]{2,1,0:T(8,128)S(1)}, f32[4,96,128]{2,1,0:T(8,128)S(1)}, u32[]{:S(2)}, u32[]{:S(2)}) %collective-permute-start.19) | collective-permute-done | bytes 196640 | tf_op jit(solution)/shard_map/ppermute | solution.py:565
  65.6 1.8 %collective-permute-done.20.forward = f32[4,96,128]{2,1,0:T(8,128)S(1)} collective-permute-done((f32[4,96,128]{2,1,0:T(8,128)S(1)}, f32[4,96,128]{2,1,0:T(8,128)S(1)}, u32[]{:S(2)}, u32[]{:S(2)}) %collective-permute-start.20) | collective-permute-done | bytes 196640 | tf_op jit(solution)/shard_map/ppermute | solution.py:565
  67.3 0.9 forward_face.3
  68.4 1.3 %collective-permute-done.21.received = f32[256,128]{1,0:T(8,128)S(1)} collective-permute-done((f32[256,128]{1,0:T(8,128)S(1)}, f32[256,128]{1,0:T(8,128)S(1)}, u32[]{:S(2)}, u32[]{:S(2)}) %collective-permute-start.21) | collective-permute-done | bytes 131104 | tf_op jit(solution)/shard_map/ppermute | solution.py:570
  69.7 1.6 %collective-permute-start.22 = (f32[128,128]{1,0:T(8,128)S(1)}, f32[128,128]{1,0:T(8,128)S(1)}, u32[]{:S(2)}, u32[]{:S(2)}) collective-permute-start(f32[128,128]{1,0:T(8,128)S(1)} %get-tuple-element.76), channel_id=1, source_target_pairs={{0,8},{4,12},{8,0},{12,4},{1,9},{5,13},{9,1},{13,5},{2,10},{6,14},... | collective-permute-start | bytes 196616 | tf_op jit(solution)/shard_map/ppermute | solution.py:570
  71.3 2.8 %collective-permute-done.22.right = f32[128,128]{1,0:T(8,128)S(1)} collective-permute-done((f32[128,128]{1,0:T(8,128)S(1)}, f32[128,128]{1,0:T(8,128)S(1)}, u32[]{:S(2)}, u32[]{:S(2)}) %collective-permute-start.22) | collective-permute-done | bytes 65568 | tf_op jit(solution)/shard_map/ppermute | solution.py:570
  74.1 1.6 %collective-permute-start.30 = (f32[8,96,128]{2,1,0:T(8,128)S(1)}, f32[8,96,128]{2,1,0:T(8,128)S(1)}, u32[]{:S(2)}, u32[]{:S(2)}) collective-permute-start(f32[8,96,128]{2,1,0:T(8,128)S(1)} %get-tuple-element.80.own.residual), channel_id=1, source_target_pairs={{0,16},{16,0},{1,17},{17,1},{2,18},{18,2},{3,19},{19,3},{4,20},{20... | collective-permute-start | bytes 1179656 | tf_op jit(solution)/shard_map/ppermute | solution.py:570
  75.7 1.2 %collective-permute-start.24 = (f32[128,128]{1,0:T(8,128)S(1)}, f32[128,128]{1,0:T(8,128)S(1)}, u32[]{:S(2)}, u32[]{:S(2)}) collective-permute-start(f32[128,128]{1,0:T(8,128)S(1)} %add.5.refs_0_), channel_id=1, source_target_pairs={{0,1},{1,0},{2,3},{3,2},{4,5},{5,4},{6,7},{7,6},{8,9},{9,8},{10,11... | collective-permute-start | bytes 196616 | tf_op jit(solution)/shard_map/ppermute | solution.py:570
  76.9 1.5 %collective-permute-start.25 = (f32[128,128]{1,0:T(8,128)S(1)}, f32[128,128]{1,0:T(8,128)S(1)}, u32[]{:S(2)}, u32[]{:S(2)}) collective-permute-start(f32[128,128]{1,0:T(8,128)S(1)} %add.5.refs_0_), channel_id=1, source_target_pairs={{0,2},{1,3},{2,0},{3,1},{4,6},{5,7},{6,4},{7,5},{8,10},{9,11},{10,... | collective-permute-start | bytes 196616 | tf_op jit(solution)/shard_map/ppermute | solution.py:570
  78.4 1.7 %collective-permute-start.26 = (f32[128,128]{1,0:T(8,128)S(1)}, f32[128,128]{1,0:T(8,128)S(1)}, u32[]{:S(2)}, u32[]{:S(2)}) collective-permute-start(f32[128,128]{1,0:T(8,128)S(1)} %add.5.refs_0_), channel_id=1, source_target_pairs={{0,3},{1,2},{2,1},{3,0},{4,7},{5,6},{6,5},{7,4},{8,11},{9,10},{10,... | collective-permute-start | bytes 196616 | tf_op jit(solution)/shard_map/ppermute | solution.py:570
  80.1 3.1 %collective-permute-done.25.refs_2_ = f32[128,128]{1,0:T(8,128)S(1)} collective-permute-done((f32[128,128]{1,0:T(8,128)S(1)}, f32[128,128]{1,0:T(8,128)S(1)}, u32[]{:S(2)}, u32[]{:S(2)}) %collective-permute-start.25) | collective-permute-done | bytes 65568 | tf_op jit(solution)/shard_map/ppermute | solution.py:570
  83.2 1.3 %collective-permute-done.26.refs_3_ = f32[128,128]{1,0:T(8,128)S(1)} collective-permute-done((f32[128,128]{1,0:T(8,128)S(1)}, f32[128,128]{1,0:T(8,128)S(1)}, u32[]{:S(2)}, u32[]{:S(2)}) %collective-permute-start.26) | collective-permute-done | bytes 65568 | tf_op jit(solution)/shard_map/ppermute | solution.py:570
  84.6 1.5 %collective-permute-start.29 = (f32[128,128]{1,0:T(8,128)S(1)}, f32[128,128]{1,0:T(8,128)S(1)}, u32[]{:S(2)}, u32[]{:S(2)}) collective-permute-start(f32[128,128]{1,0:T(8,128)S(1)} %scale.3.refs_0_), channel_id=1, source_target_pairs={{0,8},{4,12},{8,0},{12,4},{1,9},{5,13},{9,1},{13,5},{2,10},{6,14},... | collective-permute-start | bytes 196616 | tf_op jit(solution)/shard_map/ppermute | solution.py:570
  86.6 1.6 %collective-permute-start.27 = (f32[128,128]{1,0:T(8,128)S(1)}, f32[128,128]{1,0:T(8,128)S(1)}, u32[]{:S(2)}, u32[]{:S(2)}) collective-permute-start(f32[128,128]{1,0:T(8,128)S(1)} %scale.3.refs_0_), channel_id=1, source_target_pairs={{0,24},{4,28},{8,16},{12,20},{16,8},{20,12},{24,0},{28,4},{1,25},{... | collective-permute-start | bytes 196616 | tf_op jit(solution)/shard_map/ppermute | solution.py:576
  88.2 1.0 %join.1 = f32[8,96,256]{2,1,0:T(8,128)} custom-call(f32[8,96,128]{2,1,0:T(8,128)S(1)} %get-tuple-element.80.own.residual, f32[8,96,128]{2,1,0:T(8,128)S(1)} %collective-permute-done.30.other.residual), custom_call_target="tpu_custom_call" | custom-call | flops 1000000 | bytes 2000000 | tf_op jit(solution)/shard_map/join/pallas_call | solution.py:519
  90.6 0.7 second_half.3.own
  91.2 0.8 collective-permute-done.27.refs_1_
  92.0 0.7 first_half.5.other
  93.3 1.5 %final.1 = f32[8,96,256]{2,1,0:T(8,128)} custom-call(f32[8,96,128]{2,1,0:T(8,128)S(1)} %second_half.3.own, f32[8,96,128]{2,1,0:T(8,128)S(1)} %first_half.5.other, bf16[8,2,192,512]{3,2,1,0:T(8,128)(2,1)S(1)} %get-tuple-element.57.vectors, f32[128,128]{1,0:T(8,128)S(1)} %collective-permute-done.33.refs_0_, f32[128,128]{1,0:T(8,128)S(1)} %collective-permute-done.34.refs_1_), custom_call_target="tpu_custom_call" | custom-call | flops 1000000000 | bytes 4000000 | tf_op jit(solution)/shard_map/final/pallas_call | solution.py:547
  (52 shorter events, 7.7 us)
Async XLA Ops:
  0.6 1.1 %copy-start = (f32[1,1,2,4,96,256]{5,4,3,2,1,0:T(8,128)S(1)}, f32[1,1,2,4,96,256]{5,4,3,2,1,0:T(8,128)}, u32[]{:S(2)}) copy-start(f32[1,1,2,4,96,256]{5,4,3,2,1,0:T(8,128)} %param.7) | copy-start | bytes 2359300
  2.0 6.4 %collective-permute-start = (f32[8,96,128]{2,1,0:T(8,128)S(1)}, f32[8,96,128]{2,1,0:T(8,128)S(1)}, u32[]{:S(2)}, u32[]{:S(2)}) collective-permute-start(f32[8,96,128]{2,1,0:T(8,128)S(1)} %get-tuple-element.45.x_ref.x), channel_id=1, source_target_pairs={{0,4},{4,0},{8,12},{12,8},{1,5},{5,1},{9,13},{13,9},{2,6},{6,2},{1... | collective-permute-start | bytes 1179656 | tf_op jit(solution)/shard_map/ppermute | solution.py:570
  2.6 18.8 %collective-permute-start.2 = (f32[4,96,128]{2,1,0:T(8,128)S(1)}, f32[4,96,128]{2,1,0:T(8,128)S(1)}, u32[]{:S(2)}, u32[]{:S(2)}) collective-permute-start(f32[4,96,128]{2,1,0:T(8,128)S(1)} %get-tuple-element.49), channel_id=1, source_target_pairs={{0,1},{1,2},{2,3},{3,0},{4,5},{5,6},{6,7},{7,4},{8,9},{9,10},{10,1... | collective-permute-start | bytes 589832 | tf_op jit(solution)/shard_map/ppermute | solution.py:565
  5.2 16.2 %collective-permute-start.3 = (f32[4,96,128]{2,1,0:T(8,128)S(1)}, f32[4,96,128]{2,1,0:T(8,128)S(1)}, u32[]{:S(2)}, u32[]{:S(2)}) collective-permute-start(f32[4,96,128]{2,1,0:T(8,128)S(1)} %get-tuple-element.49), channel_id=1, source_target_pairs={{0,3},{1,0},{2,1},{3,2},{4,7},{5,4},{6,5},{7,6},{8,11},{9,8},{10,9... | collective-permute-start | bytes 589832 | tf_op jit(solution)/shard_map/ppermute | solution.py:565
  7.3 14.6 %collective-permute-start.1 = (f32[8,96,128]{2,1,0:T(8,128)S(1)}, f32[8,96,128]{2,1,0:T(8,128)S(1)}, u32[]{:S(2)}, u32[]{:S(2)}) collective-permute-start(f32[8,96,128]{2,1,0:T(8,128)S(1)} %get-tuple-element.45.x_ref.x), channel_id=1, source_target_pairs={{0,12},{4,8},{8,4},{12,0},{1,13},{5,9},{9,5},{13,1},{2,14},{6,10},... | collective-permute-start | bytes 1179656 | tf_op jit(solution)/shard_map/ppermute | solution.py:583
  8.5 14.5 %collective-permute-start.4 = (f32[4,96,128]{2,1,0:T(8,128)S(1)}, f32[4,96,128]{2,1,0:T(8,128)S(1)}, u32[]{:S(2)}, u32[]{:S(2)}) collective-permute-start(f32[4,96,128]{2,1,0:T(8,128)S(1)} %get-tuple-element.55), channel_id=1, source_target_pairs={{0,1},{1,2},{2,3},{3,0},{4,5},{5,6},{6,7},{7,4},{8,9},{9,10},{10,1... | collective-permute-start | bytes 589832 | tf_op jit(solution)/shard_map/ppermute | solution.py:565
  8.5 16.3 %collective-permute-start.5 = (f32[4,96,128]{2,1,0:T(8,128)S(1)}, f32[4,96,128]{2,1,0:T(8,128)S(1)}, u32[]{:S(2)}, u32[]{:S(2)}) collective-permute-start(f32[4,96,128]{2,1,0:T(8,128)S(1)} %get-tuple-element.55), channel_id=1, source_target_pairs={{0,3},{1,0},{2,1},{3,2},{4,7},{5,4},{6,5},{7,6},{8,11},{9,8},{10,9... | collective-permute-start | bytes 589832 | tf_op jit(solution)/shard_map/ppermute | solution.py:565
  24.8 6.8 %copy-start.1 = (f32[2,512]{1,0:T(2,128)S(1)}, f32[2,512]{1,0:T(2,128)}, u32[]{:S(2)}) copy-start(f32[2,512]{1,0:T(2,128)} %inverse.1) | copy-start | bytes 12292
  25.8 1.4 %collective-permute-start.6 = (f32[256,128]{1,0:T(8,128)S(1)}, f32[256,128]{1,0:T(8,128)S(1)}, u32[]{:S(2)}, u32[]{:S(2)}) collective-permute-start(f32[256,128]{1,0:T(8,128)S(1)} %get-tuple-element.59), channel_id=1, source_target_pairs={{0,4},{4,0},{8,12},{12,8},{1,5},{5,1},{9,13},{13,9},{2,6},{6,2},{1... | collective-permute-start | bytes 393224 | tf_op jit(solution)/shard_map/ppermute | solution.py:570
  27.2 4.6 %collective-permute-start.7 = (f32[128,128]{1,0:T(8,128)S(1)}, f32[128,128]{1,0:T(8,128)S(1)}, u32[]{:S(2)}, u32[]{:S(2)}) collective-permute-start(f32[128,128]{1,0:T(8,128)S(1)} %get-tuple-element.61), channel_id=1, source_target_pairs={{0,8},{4,12},{8,0},{12,4},{1,9},{5,13},{9,1},{13,5},{2,10},{6,14},... | collective-permute-start | bytes 196616 | tf_op jit(solution)/shard_map/ppermute | solution.py:570
  28.7 8.2 %collective-permute-start.8 = (f32[128,128]{1,0:T(8,128)S(1)}, f32[128,128]{1,0:T(8,128)S(1)}, u32[]{:S(2)}, u32[]{:S(2)}) collective-permute-start(f32[128,128]{1,0:T(8,128)S(1)} %get-tuple-element.60.refs_0_), channel_id=1, source_target_pairs={{0,2},{1,3},{2,0},{3,1},{4,6},{5,7},{6,4},{7,5},{8,10},{9,11},{10,... | collective-permute-start | bytes 196616 | tf_op jit(solution)/shard_map/ppermute | solution.py:570
  30.0 7.7 %collective-permute-start.9 = (f32[128,128]{1,0:T(8,128)S(1)}, f32[128,128]{1,0:T(8,128)S(1)}, u32[]{:S(2)}, u32[]{:S(2)}) collective-permute-start(f32[128,128]{1,0:T(8,128)S(1)} %get-tuple-element.61), channel_id=1, source_target_pairs={{0,10},{1,11},{2,8},{3,9},{4,14},{5,15},{6,12},{7,13},{8,2},{9,3},... | collective-permute-start | bytes 196616 | tf_op jit(solution)/shard_map/ppermute | solution.py:576
  37.8 5.0 %collective-permute-start.11 = (f32[128,128]{1,0:T(8,128)S(1)}, f32[128,128]{1,0:T(8,128)S(1)}, u32[]{:S(2)}, u32[]{:S(2)}) collective-permute-start(f32[128,128]{1,0:T(8,128)S(1)} %scale.2.left), channel_id=1, source_target_pairs={{0,8},{4,12},{8,0},{12,4},{1,9},{5,13},{9,1},{13,5},{2,10},{6,14},... | collective-permute-start | bytes 196616 | tf_op jit(solution)/shard_map/ppermute | solution.py:570
  39.3 5.2 %collective-permute-start.12 = (f32[128,128]{1,0:T(8,128)S(1)}, f32[128,128]{1,0:T(8,128)S(1)}, u32[]{:S(2)}, u32[]{:S(2)}) collective-permute-start(f32[128,128]{1,0:T(8,128)S(1)} %scale.2.left), channel_id=1, source_target_pairs={{0,9},{1,8},{2,11},{3,10},{4,13},{5,12},{6,15},{7,14},{8,1},{9,0},... | collective-permute-start | bytes 196616 | tf_op jit(solution)/shard_map/ppermute | solution.py:576
  39.8 4.8 %collective-permute-start.10 = (f32[128,128]{1,0:T(8,128)S(1)}, f32[128,128]{1,0:T(8,128)S(1)}, u32[]{:S(2)}, u32[]{:S(2)}) collective-permute-start(f32[128,128]{1,0:T(8,128)S(1)} %scale.2.left), channel_id=1, source_target_pairs={{0,1},{1,0},{2,3},{3,2},{4,5},{5,4},{6,7},{7,6},{8,9},{9,8},{10,11... | collective-permute-start | bytes 196616 | tf_op jit(solution)/shard_map/ppermute | solution.py:570
  44.5 1.3 %collective-permute-start.14 = (f32[128,128]{1,0:T(8,128)S(1)}, f32[128,128]{1,0:T(8,128)S(1)}, u32[]{:S(2)}, u32[]{:S(2)}) collective-permute-start(f32[128,128]{1,0:T(8,128)S(1)} %add.4.refs_1_), channel_id=1, source_target_pairs={{0,4},{4,0},{8,12},{12,8},{1,5},{5,1},{9,13},{13,9},{2,6},{6,2},{1... | collective-permute-start | bytes 196616 | tf_op jit(solution)/shard_map/ppermute | solution.py:570
  44.6 1.5 %collective-permute-start.13 = (f32[128,128]{1,0:T(8,128)S(1)}, f32[128,128]{1,0:T(8,128)S(1)}, u32[]{:S(2)}, u32[]{:S(2)}) collective-permute-start(f32[128,128]{1,0:T(8,128)S(1)} %add.3.refs_0_), channel_id=1, source_target_pairs={{0,4},{4,0},{8,12},{12,8},{1,5},{5,1},{9,13},{13,9},{2,6},{6,2},{1... | collective-permute-start | bytes 196616 | tf_op jit(solution)/shard_map/ppermute | solution.py:570
  46.8 4.5 %collective-permute-start.15 = (f32[8,96,128]{2,1,0:T(8,128)S(1)}, f32[8,96,128]{2,1,0:T(8,128)S(1)}, u32[]{:S(2)}, u32[]{:S(2)}) collective-permute-start(f32[8,96,128]{2,1,0:T(8,128)S(1)} %get-tuple-element.78.x_ref.x), channel_id=1, source_target_pairs={{0,4},{4,0},{8,12},{12,8},{1,5},{5,1},{9,13},{13,9},{2,6},{6,2},{1... | collective-permute-start | bytes 1179656 | tf_op jit(solution)/shard_map/ppermute | solution.py:570
  47.2 9.6 %collective-permute-start.17 = (f32[4,96,128]{2,1,0:T(8,128)S(1)}, f32[4,96,128]{2,1,0:T(8,128)S(1)}, u32[]{:S(2)}, u32[]{:S(2)}) collective-permute-start(f32[4,96,128]{2,1,0:T(8,128)S(1)} %get-tuple-element.68), channel_id=1, source_target_pairs={{0,1},{1,2},{2,3},{3,0},{4,5},{5,6},{6,7},{7,4},{8,9},{9,10},{10,1... | collective-permute-start | bytes 589832 | tf_op jit(solution)/shard_map/ppermute | solution.py:565
  47.8 12.3 %collective-permute-start.18 = (f32[4,96,128]{2,1,0:T(8,128)S(1)}, f32[4,96,128]{2,1,0:T(8,128)S(1)}, u32[]{:S(2)}, u32[]{:S(2)}) collective-permute-start(f32[4,96,128]{2,1,0:T(8,128)S(1)} %get-tuple-element.68), channel_id=1, source_target_pairs={{0,3},{1,0},{2,1},{3,2},{4,7},{5,4},{6,5},{7,6},{8,11},{9,8},{10,9... | collective-permute-start | bytes 589832 | tf_op jit(solution)/shard_map/ppermute | solution.py:565
  51.0 11.2 %collective-permute-start.16 = (f32[8,96,128]{2,1,0:T(8,128)S(1)}, f32[8,96,128]{2,1,0:T(8,128)S(1)}, u32[]{:S(2)}, u32[]{:S(2)}) collective-permute-start(f32[8,96,128]{2,1,0:T(8,128)S(1)} %get-tuple-element.78.x_ref.x), channel_id=1, source_target_pairs={{0,12},{4,8},{8,4},{12,0},{1,13},{5,9},{9,5},{13,1},{2,14},{6,10},... | collective-permute-start | bytes 1179656 | tf_op jit(solution)/shard_map/ppermute | solution.py:583
  51.2 14.0 %collective-permute-start.19 = (f32[4,96,128]{2,1,0:T(8,128)S(1)}, f32[4,96,128]{2,1,0:T(8,128)S(1)}, u32[]{:S(2)}, u32[]{:S(2)}) collective-permute-start(f32[4,96,128]{2,1,0:T(8,128)S(1)} %get-tuple-element.72), channel_id=1, source_target_pairs={{0,1},{1,2},{2,3},{3,0},{4,5},{5,6},{6,7},{7,4},{8,9},{9,10},{10,1... | collective-permute-start | bytes 589832 | tf_op jit(solution)/shard_map/ppermute | solution.py:565
  51.2 16.1 %collective-permute-start.20 = (f32[4,96,128]{2,1,0:T(8,128)S(1)}, f32[4,96,128]{2,1,0:T(8,128)S(1)}, u32[]{:S(2)}, u32[]{:S(2)}) collective-permute-start(f32[4,96,128]{2,1,0:T(8,128)S(1)} %get-tuple-element.72), channel_id=1, source_target_pairs={{0,3},{1,0},{2,1},{3,2},{4,7},{5,4},{6,5},{7,6},{8,11},{9,8},{10,9... | collective-permute-start | bytes 589832 | tf_op jit(solution)/shard_map/ppermute | solution.py:565
  56.8 17.3 %collective-permute-start.23 = (f32[8,96,128]{2,1,0:T(8,128)S(1)}, f32[8,96,128]{2,1,0:T(8,128)S(1)}, u32[]{:S(2)}, u32[]{:S(2)}) collective-permute-start(f32[8,96,128]{2,1,0:T(8,128)S(1)} %get-tuple-element.78.x_ref.x), channel_id=1, source_target_pairs={{0,16},{16,0},{1,17},{17,1},{2,18},{18,2},{3,19},{19,3},{4,20},{20... | collective-permute-start | bytes 1179656 | tf_op jit(solution)/shard_map/ppermute | solution.py:570
  68.3 1.4 %collective-permute-start.21 = (f32[256,128]{1,0:T(8,128)S(1)}, f32[256,128]{1,0:T(8,128)S(1)}, u32[]{:S(2)}, u32[]{:S(2)}) collective-permute-start(f32[256,128]{1,0:T(8,128)S(1)} %get-tuple-element.74), channel_id=1, source_target_pairs={{0,4},{4,0},{8,12},{12,8},{1,5},{5,1},{9,13},{13,9},{2,6},{6,2},{1... | collective-permute-start | bytes 393224 | tf_op jit(solution)/shard_map/ppermute | solution.py:570
  69.7 4.3 %collective-permute-start.22 = (f32[128,128]{1,0:T(8,128)S(1)}, f32[128,128]{1,0:T(8,128)S(1)}, u32[]{:S(2)}, u32[]{:S(2)}) collective-permute-start(f32[128,128]{1,0:T(8,128)S(1)} %get-tuple-element.76), channel_id=1, source_target_pairs={{0,8},{4,12},{8,0},{12,4},{1,9},{5,13},{9,1},{13,5},{2,10},{6,14},... | collective-permute-start | bytes 196616 | tf_op jit(solution)/shard_map/ppermute | solution.py:570
  74.1 14.1 %collective-permute-start.30 = (f32[8,96,128]{2,1,0:T(8,128)S(1)}, f32[8,96,128]{2,1,0:T(8,128)S(1)}, u32[]{:S(2)}, u32[]{:S(2)}) collective-permute-start(f32[8,96,128]{2,1,0:T(8,128)S(1)} %get-tuple-element.80.own.residual), channel_id=1, source_target_pairs={{0,16},{16,0},{1,17},{17,1},{2,18},{18,2},{3,19},{19,3},{4,20},{20... | collective-permute-start | bytes 1179656 | tf_op jit(solution)/shard_map/ppermute | solution.py:570
  75.7 4.4 %collective-permute-start.24 = (f32[128,128]{1,0:T(8,128)S(1)}, f32[128,128]{1,0:T(8,128)S(1)}, u32[]{:S(2)}, u32[]{:S(2)}) collective-permute-start(f32[128,128]{1,0:T(8,128)S(1)} %add.5.refs_0_), channel_id=1, source_target_pairs={{0,1},{1,0},{2,3},{3,2},{4,5},{5,4},{6,7},{7,6},{8,9},{9,8},{10,11... | collective-permute-start | bytes 196616 | tf_op jit(solution)/shard_map/ppermute | solution.py:570
  76.9 6.3 %collective-permute-start.25 = (f32[128,128]{1,0:T(8,128)S(1)}, f32[128,128]{1,0:T(8,128)S(1)}, u32[]{:S(2)}, u32[]{:S(2)}) collective-permute-start(f32[128,128]{1,0:T(8,128)S(1)} %add.5.refs_0_), channel_id=1, source_target_pairs={{0,2},{1,3},{2,0},{3,1},{4,6},{5,7},{6,4},{7,5},{8,10},{9,11},{10,... | collective-permute-start | bytes 196616 | tf_op jit(solution)/shard_map/ppermute | solution.py:570
  78.4 6.2 %collective-permute-start.26 = (f32[128,128]{1,0:T(8,128)S(1)}, f32[128,128]{1,0:T(8,128)S(1)}, u32[]{:S(2)}, u32[]{:S(2)}) collective-permute-start(f32[128,128]{1,0:T(8,128)S(1)} %add.5.refs_0_), channel_id=1, source_target_pairs={{0,3},{1,2},{2,1},{3,0},{4,7},{5,6},{6,5},{7,4},{8,11},{9,10},{10,... | collective-permute-start | bytes 196616 | tf_op jit(solution)/shard_map/ppermute | solution.py:570
  84.6 4.6 %collective-permute-start.29 = (f32[128,128]{1,0:T(8,128)S(1)}, f32[128,128]{1,0:T(8,128)S(1)}, u32[]{:S(2)}, u32[]{:S(2)}) collective-permute-start(f32[128,128]{1,0:T(8,128)S(1)} %scale.3.refs_0_), channel_id=1, source_target_pairs={{0,8},{4,12},{8,0},{12,4},{1,9},{5,13},{9,1},{13,5},{2,10},{6,14},... | collective-permute-start | bytes 196616 | tf_op jit(solution)/shard_map/ppermute | solution.py:570
  86.1 4.3 %collective-permute-start.28 = (f32[128,128]{1,0:T(8,128)S(1)}, f32[128,128]{1,0:T(8,128)S(1)}, u32[]{:S(2)}, u32[]{:S(2)}) collective-permute-start(f32[128,128]{1,0:T(8,128)S(1)} %scale.3.refs_0_), channel_id=1, source_target_pairs={{0,16},{16,0},{1,17},{17,1},{2,18},{18,2},{3,19},{19,3},{4,20},{20... | collective-permute-start | bytes 196616 | tf_op jit(solution)/shard_map/ppermute | solution.py:570
  86.6 4.0 %collective-permute-start.31 = (f32[128,128]{1,0:T(8,128)S(1)}, f32[128,128]{1,0:T(8,128)S(1)}, u32[]{:S(2)}, u32[]{:S(2)}) collective-permute-start(f32[128,128]{1,0:T(8,128)S(1)} %scale.3.refs_0_), channel_id=1, source_target_pairs={{0,4},{4,0},{8,12},{12,8},{1,5},{5,1},{9,13},{13,9},{2,6},{6,2},{1... | collective-permute-start | bytes 196616 | tf_op jit(solution)/shard_map/ppermute | solution.py:570
  86.6 5.4 %collective-permute-start.27 = (f32[128,128]{1,0:T(8,128)S(1)}, f32[128,128]{1,0:T(8,128)S(1)}, u32[]{:S(2)}, u32[]{:S(2)}) collective-permute-start(f32[128,128]{1,0:T(8,128)S(1)} %scale.3.refs_0_), channel_id=1, source_target_pairs={{0,24},{4,28},{8,16},{12,20},{16,8},{20,12},{24,0},{28,4},{1,25},{... | collective-permute-start | bytes 196616 | tf_op jit(solution)/shard_map/ppermute | solution.py:576
  89.2 1.3 %collective-permute-start.32 = (f32[128,128]{1,0:T(8,128)S(1)}, f32[128,128]{1,0:T(8,128)S(1)}, u32[]{:S(2)}, u32[]{:S(2)}) collective-permute-start(f32[128,128]{1,0:T(8,128)S(1)} %collective-permute-done.29.refs_1_), channel_id=1, source_target_pairs={{0,4},{4,0},{8,12},{12,8},{1,5},{5,1},{9,13},{13,9},{2,6},{6,2},{1... | collective-permute-start | bytes 196616 | tf_op jit(solution)/shard_map/ppermute | solution.py:570
  90.4 2.3 %collective-permute-start.33 = (f32[128,128]{1,0:T(8,128)S(1)}, f32[128,128]{1,0:T(8,128)S(1)}, u32[]{:S(2)}, u32[]{:S(2)}) collective-permute-start(f32[128,128]{1,0:T(8,128)S(1)} %collective-permute-done.28.refs_0_), channel_id=1, source_target_pairs={{0,4},{4,0},{8,12},{12,8},{1,5},{5,1},{9,13},{13,9},{2,6},{6,2},{1... | collective-permute-start | bytes 196616 | tf_op jit(solution)/shard_map/ppermute | solution.py:570
  92.0 1.3 %collective-permute-start.34 = (f32[128,128]{1,0:T(8,128)S(1)}, f32[128,128]{1,0:T(8,128)S(1)}, u32[]{:S(2)}, u32[]{:S(2)}) collective-permute-start(f32[128,128]{1,0:T(8,128)S(1)} %collective-permute-done.27.refs_1_), channel_id=1, source_target_pairs={{0,4},{4,0},{8,12},{12,8},{1,5},{5,1},{9,13},{13,9},{2,6},{6,2},{1... | collective-permute-start | bytes 196616 | tf_op jit(solution)/shard_map/ppermute | solution.py:570

commit v14 on v13

--- a/solution.py
+++ b/solution.py
@@ -350,13 +350,14 @@
     )(rest, backward, matrix)
 
 
-def forward_kernel(front, partial, rest, forward, matrix, vectors, residual, keep, send, stacks):
+def forward_kernel(front, partial, rest, forward, matrix, vectors, residual, back, keep, send, stacks):
     sign = edge_sign(True)
     sites, rows, _ = forward.shape
     for site in range(sites):
         own = rest[site] - apply_faces((matrix[2, sites + site], sign * forward[site]))
         residual[site] = front[site]
         residual[sites + site] = own
+        back[site] = own
         stacks[site * 2 * rows : (site + 1) * 2 * rows] = stack(own, -1.0)
     whole = partial[...] + fold(matmul(vectors[:, stacks.shape[0] :], stacks[...]))
     half = whole.shape[0] // 2
@@ -369,9 +370,9 @@
     part = pltpu.VMEM((vectors.shape[0] // 4, lanes), F32)
     return pl.pallas_call(
         forward_kernel,
-        out_shape=(pltpu.VMEM((2 * sites, rows, lanes), F32), part, part),
+        out_shape=(pltpu.VMEM((2 * sites, rows, lanes), F32), pltpu.VMEM(forward.shape, F32), part, part),
         in_specs=vmem(6),
-        out_specs=tuple(vmem(3)),
+        out_specs=tuple(vmem(4)),
         scratch_shapes=[pltpu.VMEM((sites * 2 * rows, 2 * lanes), BF16)],
         compiler_params=params(),
         cost_estimate=cost(2e9, 8e6),
@@ -458,24 +459,29 @@
     stacks[...] = stack(values[0] if len(values) == 1 else jnp.concatenate(values, axis=0), 1.0)
 
 
-def first_half_kernel(x, residual, vectors, *refs):
-    pieces, (out, stacks) = refs[:-2], refs[-2:]
+def site_of(parts, site):
+    count = parts[0].shape[0]
+    return parts[site // count][site % count]
+
+
+def first_half_kernel(count, x, vectors, *refs):
+    residual, pieces, (out, stacks) = refs[:count], refs[count:-2], refs[-2:]
     place_pieces(pieces, stacks)
     for site in range(x.shape[0]):
-        out[site] = x[site] + 0.5 * residual[site] + expand(site, vectors, 0, stacks)
+        out[site] = x[site] + 0.5 * site_of(residual, site) + expand(site, vectors, 0, stacks)
 
 
 def first_half(x, residual, pieces, vectors):
     return pl.pallas_call(
-        first_half_kernel,
+        functools.partial(first_half_kernel, len(residual)),
         out_shape=pltpu.VMEM(x.shape, F32),
-        in_specs=vmem(3 + len(pieces)),
+        in_specs=vmem(2 + len(residual) + len(pieces)),
         out_specs=vmem(1)[0],
         scratch_shapes=[pltpu.VMEM((vectors.shape[-1], 2 * x.shape[-1]), BF16)],
         compiler_params=params(),
         cost_estimate=cost(1e9, 4e6),
         name="first_half",
-    )(x, residual, vectors, *pieces)
+    )(x, vectors, *residual, *pieces)
 
 
 def second_half_kernel(count, base, vectors, *refs):
@@ -502,30 +508,30 @@
     )(base, vectors, *pieces)
 
 
-def join_kernel(own, other, full, held, sems):
+def join_kernel(own, front, back, full, held, sems):
     group = lax.axis_index("groups")
     copies = []
     for site in range(own.shape[0]):
-        held[site] = join_halves(own[site], other[site], group)
+        held[site] = join_halves(own[site], site_of((front, back), site), group)
         copies.append(pltpu.make_async_copy(held.at[site], full.at[site], sems.at[site]))
         copies[-1].start()
     for copy in copies:
         copy.wait()
 
 
-def join(own, other):
+def join(own, front, back):
     sites, rows, lanes = own.shape
     shape = (sites, rows, 2 * lanes)
     return pl.pallas_call(
         join_kernel,
         out_shape=jax.ShapeDtypeStruct(shape, F32),
-        in_specs=vmem(2),
+        in_specs=vmem(3),
         out_specs=pl.BlockSpec(memory_space=pl.ANY),
         scratch_shapes=[pltpu.VMEM(shape, F32), pltpu.SemaphoreType.DMA((sites,))],
         compiler_params=params(),
         cost_estimate=cost(1e6, 2e6),
         name="join",
-    )(own, other)
+    )(own, front, back)
 
 
 def final_kernel(own, other, vectors, *refs):
@@ -650,27 +656,29 @@
             other_x = crossed(x, "groups", 1)
         near, far, early, late = faces
         back_rest, own, partial = middle(rest, near, far, front_faces(*early, halo), halo, by_rows)
+        if last:
+            other_front = crossed(own, "groups", 1)
         back_rest = backward_face(back_rest, late[0], halo)
-        residual, keep, send = forward_face(own, partial, back_rest, late[1], halo, by_rows)
+        residual, back, keep, send = forward_face(own, partial, back_rest, late[1], halo, by_rows)
         if not last:
             pieces = scaled_sum(keep, send, eigen)
-            base = first_half(x, residual, pieces, by_columns)
+            base = first_half(x, [residual], pieces, by_columns)
             x, early_x, late_x = second_half(base, paired(pieces), by_columns, True)
-    part, residual, other_x = lax.optimization_barrier((halving(keep, send), residual, other_x))
-    other_residual = crossed(residual, "groups", 1)
-    d = scale(eigen, over_time(part))
+    part, other_x = lax.optimization_barrier((halving(keep, send), other_x))
+    other_back = crossed(back, "groups", 1)
+    d, other_front = lax.optimization_barrier((scale(eigen, over_time(part)), other_front))
     mask = blocks // 2
     other = across_groups(d, mask)
     own = [d, crossed(d, "space", mask)]
     other, own = doubling(other, mask // 2), doubling(own, mask // 2)
-    full_residual = join(residual, other_residual)
+    full_residual = join(residual, other_front, other_back)
     own[-1], full_residual = lax.optimization_barrier((own[-1], full_residual))
-    own_x = first_half(x, residual, own, by_columns)
+    own_x = first_half(x, [residual], own, by_columns)
     other[0], own_x = lax.optimization_barrier((other[0], own_x))
     own_x = second_half(own_x, paired(own), by_columns, False)
     other[-1], own_x = lax.optimization_barrier((other[-1], own_x))
     other_second = paired(other)
-    other_x = first_half(other_x, other_residual, other, by_columns)
+    other_x = first_half(other_x, [other_front, other_back], other, by_columns)
     whole = final(own_x, other_x, other_second, by_columns)
     shape = source.shape
     return whole.reshape(shape), full_residual.reshape(shape)

time: 95.1 us -> 94.7 us (level)
  waiting for transfers between devices: 29.8 us -> 28.2 us
  starting transfers between devices: 40.4 us -> 41.6 us
    ppermute x22 -> x23, waiting for transfers between devices: 17.6 us -> 15.1 us  [crossed(): return lax.ppermute(value, axis, [(i, i ^ mask) for i in range(count)])]
    ppermute x22 -> x23, starting transfers between devices: 19.1 us -> 21.1 us  [crossed(): return lax.ppermute(value, axis, [(i, i ^ mask) for i in range(count)])]
  transfers between devices with their start and end apart: 35 -> 36, of which waited for: 19 -> 19; matrix products, arithmetic and copies ran while one was open for 0% -> 0% of each run, Pallas kernels for 20% -> 20%
where the time goes in v14:
time: 94.7 us; the launch traced here: 94.5 us
  starting transfers between devices  41.6 us (44%)
  waiting for transfers between devices  28.2 us (30%)
  Pallas kernels  22.5 us (24%)
  local copies, waits for them, and re-layouts  1.13 us (1%)
  between operations  1.07 us (1%)
    ppermute x23, starting transfers between devices, crossed(): return lax.ppermute(value, axis, [(i, i ^ mask) for i in range(count)])  21.1 us
    ppermute x8, starting transfers between devices, shifted(): lax.ppermute(value, axis, [(i, (i + step) % count) for i in range(count)])  16.2 us
    ppermute x23, waiting for transfers between devices, crossed(): return lax.ppermute(value, axis, [(i, i ^ mask) for i in range(count)])  15.1 us
    pallas_call x1, Pallas kernels, prepare(): pl.pallas_call(functools.partial(prepare_kernel, ny, nx), out_shape=(pltp...  9.08 us
    ppermute x8, waiting for transfers between devices, shifted(): lax.ppermute(value, axis, [(i, (i + step) % count) for i in range(count)])  7.53 us
    ppermute x3, waiting for transfers between devices, crossed_both(): return lax.ppermute(value, (first, second), pairs)  4 us
    ppermute x3, starting transfers between devices, crossed_both(): return lax.ppermute(value, (first, second), pairs)  2.85 us
    pallas_call x2, Pallas kernels, middle(): pl.pallas_call(middle_kernel, out_shape=(half, half, pltpu.VMEM((vectors....  2.15 us
  transfers between devices with their start and end apart: 36, of which 19 were waited for; matrix products, arithmetic and copies ran while one was open for 0% of the time, Pallas kernels for 20%

profile of v14, /device:TPU:0, one launch (start us, length us, event | category | flops | bytes accessed | tf_op | source)
XLA Modules:
  0.0 94.5 jit_solution(3256857908345829215)
XLA Ops:
  0.6 1.1 %copy-done = f32[1,1,2,4,96,256]{5,4,3,2,1,0:T(8,128)S(1)} copy-done((f32[1,1,2,4,96,256]{5,4,3,2,1,0:T(8,128)S(1)}, f32[1,1,2,4,96,256]{5,4,3,2,1,0:T(8,128)}, u32[]{:S(2)}) %copy-start) | copy-done | bytes 786456
  2.6 2.6 %collective-permute-start.2 = (f32[4,96,128]{2,1,0:T(8,128)S(1)}, f32[4,96,128]{2,1,0:T(8,128)S(1)}, u32[]{:S(2)}, u32[]{:S(2)}) collective-permute-start(f32[4,96,128]{2,1,0:T(8,128)S(1)} %get-tuple-element.52), channel_id=1, source_target_pairs={{0,1},{1,2},{2,3},{3,0},{4,5},{5,6},{6,7},{7,4},{8,9},{9,10},{10,1... | collective-permute-start | bytes 589832 | tf_op jit(solution)/shard_map/ppermute | solution.py:571
  5.2 2.1 %collective-permute-start.3 = (f32[4,96,128]{2,1,0:T(8,128)S(1)}, f32[4,96,128]{2,1,0:T(8,128)S(1)}, u32[]{:S(2)}, u32[]{:S(2)}) collective-permute-start(f32[4,96,128]{2,1,0:T(8,128)S(1)} %get-tuple-element.52), channel_id=1, source_target_pairs={{0,3},{1,0},{2,1},{3,2},{4,7},{5,4},{6,5},{7,6},{8,11},{9,8},{10,9... | collective-permute-start | bytes 589832 | tf_op jit(solution)/shard_map/ppermute | solution.py:571
  7.3 1.2 %collective-permute-start.1 = (f32[8,96,128]{2,1,0:T(8,128)S(1)}, f32[8,96,128]{2,1,0:T(8,128)S(1)}, u32[]{:S(2)}, u32[]{:S(2)}) collective-permute-start(f32[8,96,128]{2,1,0:T(8,128)S(1)} %get-tuple-element.47.x_ref.x), channel_id=1, source_target_pairs={{0,12},{4,8},{8,4},{12,0},{1,13},{5,9},{9,5},{13,1},{2,14},{6,10},... | collective-permute-start | bytes 1179656 | tf_op jit(solution)/shard_map/ppermute | solution.py:589
  8.5 3.8 %collective-permute-start.5 = (f32[4,96,128]{2,1,0:T(8,128)S(1)}, f32[4,96,128]{2,1,0:T(8,128)S(1)}, u32[]{:S(2)}, u32[]{:S(2)}) collective-permute-start(f32[4,96,128]{2,1,0:T(8,128)S(1)} %get-tuple-element.58), channel_id=1, source_target_pairs={{0,3},{1,0},{2,1},{3,2},{4,7},{5,4},{6,5},{7,6},{8,11},{9,8},{10,9... | collective-permute-start | bytes 589832 | tf_op jit(solution)/shard_map/ppermute | solution.py:571
  12.3 9.1 %prepare.1 = (f32[8,96,128]{2,1,0:T(8,128)S(1)}, f32[8,96,128]{2,1,0:T(8,128)S(1)}, bf16[5,8,192,192]{3,2,1,0:T(8,128)(2,1)S(1)}, bf16[4,8,192,192]{3,2,1,0:T(8,...) custom-call(f32[8,96,128]{2,1,0:T(8,128)S(1)} %get-tuple-element.47.x_ref.x, ...), custom_call_target="tpu_custom_call" | custom-call | flops 8000000000 | bytes 25000000 | tf_op jit(solution)/shard_map/prepare/pallas_call | solution.py:225
  21.9 1.1 %middle.2 = (f32[4,96,128]{2,1,0:T(8,128)S(1)}, f32[4,96,128]{2,1,0:T(8,128)S(1)}, f32[512,128]{1,0:T(8,128)S(1)}) custom-call(f32[8,96,128]{2,1,0:T(8,128)S(1)} %get-tuple-element.49.rest, f32[8,96,128]{2,1,0:T(8,128)S(1)} %collective-permute-done.near, f32[8,96,128]{2,1,0:T(8,128)S(1)} %collective-permute-done.1.far, f32[4,96,128]{2,1,0:T(8,128)S(1)} %front_faces.2.front, ...), custom_call_target="tpu_custom_call" | custom-call | flops 1000 | bytes 1000 | tf_op jit(solution)/shard_map/middle/pallas_call | solution.py:322
  23.3 1.5 %collective-permute-done.5.forward = f32[4,96,128]{2,1,0:T(8,128)S(1)} collective-permute-done((f32[4,96,128]{2,1,0:T(8,128)S(1)}, f32[4,96,128]{2,1,0:T(8,128)S(1)}, u32[]{:S(2)}, u32[]{:S(2)}) %collective-permute-start.5) | collective-permute-done | bytes 196640 | tf_op jit(solution)/shard_map/ppermute | solution.py:571
  24.8 1.0 %forward_face.2 = (f32[8,96,128]{2,1,0:T(8,128)S(1)}, f32[4,96,128]{2,1,0:T(8,128)}, f32[256,128]{1,0:T(8,128)S(1)}, f32[256,128]{1,0:T(8,128)S(1)}) custom-call(f32[4,96,128]{2,1,0:T(8,128)S(1)} %get-tuple-element.55.front, f32[512,128]{1,0:T(8,128)S(1)} %get-tuple-element.56.partial, f32[4,96,128]{2,1,0:T(8,128)S(1)} %backward_face.2.rest, ...), custom_call_target="tpu_custom_call" | custom-call | flops 2000000000 | bytes 8000000 | tf_op jit(solution)/shard_map/forward_face/pallas_call | solution.py:371
  25.8 1.3 %collective-permute-done.6.received = f32[256,128]{1,0:T(8,128)S(1)} collective-permute-done((f32[256,128]{1,0:T(8,128)S(1)}, f32[256,128]{1,0:T(8,128)S(1)}, u32[]{:S(2)}, u32[]{:S(2)}) %collective-permute-start.6) | collective-permute-done | bytes 131104 | tf_op jit(solution)/shard_map/ppermute | solution.py:576
  27.2 1.6 %collective-permute-start.7 = (f32[128,128]{1,0:T(8,128)S(1)}, f32[128,128]{1,0:T(8,128)S(1)}, u32[]{:S(2)}, u32[]{:S(2)}) collective-permute-start(f32[128,128]{1,0:T(8,128)S(1)} %get-tuple-element.63), channel_id=1, source_target_pairs={{0,8},{4,12},{8,0},{12,4},{1,9},{5,13},{9,1},{13,5},{2,10},{6,14},... | collective-permute-start | bytes 196616 | tf_op jit(solution)/shard_map/ppermute | solution.py:576
  28.7 1.2 %collective-permute-start.8 = (f32[128,128]{1,0:T(8,128)S(1)}, f32[128,128]{1,0:T(8,128)S(1)}, u32[]{:S(2)}, u32[]{:S(2)}) collective-permute-start(f32[128,128]{1,0:T(8,128)S(1)} %get-tuple-element.62.refs_0_), channel_id=1, source_target_pairs={{0,2},{1,3},{2,0},{3,1},{4,6},{5,7},{6,4},{7,5},{8,10},{9,11},{10,... | collective-permute-start | bytes 196616 | tf_op jit(solution)/shard_map/ppermute | solution.py:576
  30.0 1.7 %collective-permute-start.9 = (f32[128,128]{1,0:T(8,128)S(1)}, f32[128,128]{1,0:T(8,128)S(1)}, u32[]{:S(2)}, u32[]{:S(2)}) collective-permute-start(f32[128,128]{1,0:T(8,128)S(1)} %get-tuple-element.63), channel_id=1, source_target_pairs={{0,10},{1,11},{2,8},{3,9},{4,14},{5,15},{6,12},{7,13},{8,2},{9,3},... | collective-permute-start | bytes 196616 | tf_op jit(solution)/shard_map/ppermute | solution.py:582
  31.8 5.2 %collective-permute-done.8.refs_2_ = f32[128,128]{1,0:T(8,128)S(1)} collective-permute-done((f32[128,128]{1,0:T(8,128)S(1)}, f32[128,128]{1,0:T(8,128)S(1)}, u32[]{:S(2)}, u32[]{:S(2)}) %collective-permute-start.8) | collective-permute-done | bytes 65568 | tf_op jit(solution)/shard_map/ppermute | solution.py:576
  37.0 0.7 collective-permute-done.9.refs_3_
  37.8 1.6 %collective-permute-start.11 = (f32[128,128]{1,0:T(8,128)S(1)}, f32[128,128]{1,0:T(8,128)S(1)}, u32[]{:S(2)}, u32[]{:S(2)}) collective-permute-start(f32[128,128]{1,0:T(8,128)S(1)} %scale.2.left), channel_id=1, source_target_pairs={{0,8},{4,12},{8,0},{12,4},{1,9},{5,13},{9,1},{13,5},{2,10},{6,14},... | collective-permute-start | bytes 196616 | tf_op jit(solution)/shard_map/ppermute | solution.py:576
  39.8 1.6 %collective-permute-start.10 = (f32[128,128]{1,0:T(8,128)S(1)}, f32[128,128]{1,0:T(8,128)S(1)}, u32[]{:S(2)}, u32[]{:S(2)}) collective-permute-start(f32[128,128]{1,0:T(8,128)S(1)} %scale.2.left), channel_id=1, source_target_pairs={{0,1},{1,0},{2,3},{3,2},{4,5},{5,4},{6,7},{7,6},{8,9},{9,8},{10,11... | collective-permute-start | bytes 196616 | tf_op jit(solution)/shard_map/ppermute | solution.py:576
  41.3 1.5 %collective-permute-done.11.left = f32[128,128]{1,0:T(8,128)S(1)} collective-permute-done((f32[128,128]{1,0:T(8,128)S(1)}, f32[128,128]{1,0:T(8,128)S(1)}, u32[]{:S(2)}, u32[]{:S(2)}) %collective-permute-start.11) | collective-permute-done | bytes 65568 | tf_op jit(solution)/shard_map/ppermute | solution.py:576
  42.8 1.7 %collective-permute-done.12.right = f32[128,128]{1,0:T(8,128)S(1)} collective-permute-done((f32[128,128]{1,0:T(8,128)S(1)}, f32[128,128]{1,0:T(8,128)S(1)}, u32[]{:S(2)}, u32[]{:S(2)}) %collective-permute-start.12) | collective-permute-done | bytes 65568 | tf_op jit(solution)/shard_map/ppermute | solution.py:582
  46.1 0.7 second_half.2
  47.2 0.7 collective-permute-start.17
  47.8 3.2 %collective-permute-start.18 = (f32[4,96,128]{2,1,0:T(8,128)S(1)}, f32[4,96,128]{2,1,0:T(8,128)S(1)}, u32[]{:S(2)}, u32[]{:S(2)}) collective-permute-start(f32[4,96,128]{2,1,0:T(8,128)S(1)} %get-tuple-element.70), channel_id=1, source_target_pairs={{0,3},{1,0},{2,1},{3,2},{4,7},{5,4},{6,5},{7,6},{8,11},{9,8},{10,9... | collective-permute-start | bytes 589832 | tf_op jit(solution)/shard_map/ppermute | solution.py:571
  51.2 3.8 %collective-permute-start.20 = (f32[4,96,128]{2,1,0:T(8,128)S(1)}, f32[4,96,128]{2,1,0:T(8,128)S(1)}, u32[]{:S(2)}, u32[]{:S(2)}) collective-permute-start(f32[4,96,128]{2,1,0:T(8,128)S(1)} %get-tuple-element.74), channel_id=1, source_target_pairs={{0,3},{1,0},{2,1},{3,2},{4,7},{5,4},{6,5},{7,6},{8,11},{9,8},{10,9... | collective-permute-start | bytes 589832 | tf_op jit(solution)/shard_map/ppermute | solution.py:571
  55.1 1.3 %local_part.1.rest = f32[8,96,128]{2,1,0:T(8,128)S(1)} custom-call(f32[8,96,128]{2,1,0:T(8,128)S(1)} %get-tuple-element.79.x_ref.x, f32[8,96,128]{2,1,0:T(8,128)S(1)} %get-tuple-element.65.source, bf16[5,8,192,192]{3,2,1,0:T(8,128)(2,1)S(1)} %get-tuple-element.66.local), custom_call_target="tpu_custom_call" | custom-call | flops 8000000000 | bytes 8000000 | tf_op jit(solution)/shard_map/local_part/pallas_call | solution.py:142
  56.8 1.5 %collective-permute-start.23 = (f32[8,96,128]{2,1,0:T(8,128)S(1)}, f32[8,96,128]{2,1,0:T(8,128)S(1)}, u32[]{:S(2)}, u32[]{:S(2)}) collective-permute-start(f32[8,96,128]{2,1,0:T(8,128)S(1)} %get-tuple-element.79.x_ref.x), channel_id=1, source_target_pairs={{0,16},{16,0},{1,17},{17,1},{2,18},{18,2},{3,19},{19,3},{4,20},{20... | collective-permute-start | bytes 1179656 | tf_op jit(solution)/shard_map/ppermute | solution.py:576
  58.3 1.9 %collective-permute-done.18.forward = f32[4,96,128]{2,1,0:T(8,128)S(1)} collective-permute-done((f32[4,96,128]{2,1,0:T(8,128)S(1)}, f32[4,96,128]{2,1,0:T(8,128)S(1)}, u32[]{:S(2)}, u32[]{:S(2)}) %collective-permute-start.18) | collective-permute-done | bytes 196640 | tf_op jit(solution)/shard_map/ppermute | solution.py:571
  60.6 1.6 %collective-permute-done.16.far = f32[8,96,128]{2,1,0:T(8,128)S(1)} collective-permute-done((f32[8,96,128]{2,1,0:T(8,128)S(1)}, f32[8,96,128]{2,1,0:T(8,128)S(1)}, u32[]{:S(2)}, u32[]{:S(2)}) %collective-permute-start.16) | collective-permute-done | bytes 393248 | tf_op jit(solution)/shard_map/ppermute | solution.py:589
  62.2 1.1 %middle.3 = (f32[4,96,128]{2,1,0:T(8,128)S(1)}, f32[4,96,128]{2,1,0:T(8,128)S(1)}, f32[512,128]{1,0:T(8,128)S(1)}) custom-call(f32[8,96,128]{2,1,0:T(8,128)S(1)} %local_part.1.rest, f32[8,96,128]{2,1,0:T(8,128)S(1)} %collective-permute-done.15.near, f32[8,96,128]{2,1,0:T(8,128)S(1)} %collective-permute-done.16.far, f32[4,96,128]{2,1,0:T(8,128)S(1)} %front_faces.3.front, ...), custom_call_target="tpu_custom_call" | custom-call | flops 1000 | bytes 1000 | tf_op jit(solution)/shard_map/middle/pallas_call | solution.py:322
  63.3 1.9 %collective-permute-done.19.backward = f32[4,96,128]{2,1,0:T(8,128)S(1)} collective-permute-done((f32[4,96,128]{2,1,0:T(8,128)S(1)}, f32[4,96,128]{2,1,0:T(8,128)S(1)}, u32[]{:S(2)}, u32[]{:S(2)}) %collective-permute-start.19) | collective-permute-done | bytes 196640 | tf_op jit(solution)/shard_map/ppermute | solution.py:571
  65.6 1.8 %collective-permute-done.20.forward = f32[4,96,128]{2,1,0:T(8,128)S(1)} collective-permute-done((f32[4,96,128]{2,1,0:T(8,128)S(1)}, f32[4,96,128]{2,1,0:T(8,128)S(1)}, u32[]{:S(2)}, u32[]{:S(2)}) %collective-permute-start.20) | collective-permute-done | bytes 196640 | tf_op jit(solution)/shard_map/ppermute | solution.py:571
  67.4 0.9 forward_face.3
  68.4 1.6 %collective-permute-start.27 = (f32[4,96,128]{2,1,0:T(8,128)S(1)}, f32[4,96,128]{2,1,0:T(8,128)S(1)}, u32[]{:S(2)}, u32[]{:S(2)}) collective-permute-start(f32[4,96,128]{2,1,0:T(8,128)S(1)} %get-tuple-element.71.front), channel_id=1, source_target_pairs={{0,16},{16,0},{1,17},{17,1},{2,18},{18,2},{3,19},{19,3},{4,20},{20... | collective-permute-start | bytes 589832 | tf_op jit(solution)/shard_map/ppermute | solution.py:576
  70.0 1.5 %collective-permute-start.22 = (f32[128,128]{1,0:T(8,128)S(1)}, f32[128,128]{1,0:T(8,128)S(1)}, u32[]{:S(2)}, u32[]{:S(2)}) collective-permute-start(f32[128,128]{1,0:T(8,128)S(1)} %get-tuple-element.78), channel_id=1, source_target_pairs={{0,8},{4,12},{8,0},{12,4},{1,9},{5,13},{9,1},{13,5},{2,10},{6,14},... | collective-permute-start | bytes 196616 | tf_op jit(solution)/shard_map/ppermute | solution.py:576
  71.5 1.3 %collective-permute-start.31 = (f32[4,96,128]{2,1,0:T(8,128)S(1)}, f32[4,96,128]{2,1,0:T(8,128)S(1)}, u32[]{:S(2)}, u32[]{:S(2)}) collective-permute-start(f32[4,96,128]{2,1,0:T(8,128)S(1)} %get-tuple-element.84), channel_id=1, source_target_pairs={{0,16},{16,0},{1,17},{17,1},{2,18},{18,2},{3,19},{19,3},{4,20},{20... | collective-permute-start | bytes 589832 | tf_op jit(solution)/shard_map/ppermute | solution.py:576
  72.8 1.5 %collective-permute-done.22.right = f32[128,128]{1,0:T(8,128)S(1)} collective-permute-done((f32[128,128]{1,0:T(8,128)S(1)}, f32[128,128]{1,0:T(8,128)S(1)}, u32[]{:S(2)}, u32[]{:S(2)}) %collective-permute-start.22) | collective-permute-done | bytes 65568 | tf_op jit(solution)/shard_map/ppermute | solution.py:576
  74.4 1.3 %collective-permute-start.24 = (f32[128,128]{1,0:T(8,128)S(1)}, f32[128,128]{1,0:T(8,128)S(1)}, u32[]{:S(2)}, u32[]{:S(2)}) collective-permute-start(f32[128,128]{1,0:T(8,128)S(1)} %add.5.refs_0_), channel_id=1, source_target_pairs={{0,1},{1,0},{2,3},{3,2},{4,5},{5,4},{6,7},{7,6},{8,9},{9,8},{10,11... | collective-permute-start | bytes 196616 | tf_op jit(solution)/shard_map/ppermute | solution.py:576
  75.6 1.5 %collective-permute-start.25 = (f32[128,128]{1,0:T(8,128)S(1)}, f32[128,128]{1,0:T(8,128)S(1)}, u32[]{:S(2)}, u32[]{:S(2)}) collective-permute-start(f32[128,128]{1,0:T(8,128)S(1)} %add.5.refs_0_), channel_id=1, source_target_pairs={{0,2},{1,3},{2,0},{3,1},{4,6},{5,7},{6,4},{7,5},{8,10},{9,11},{10,... | collective-permute-start | bytes 196616 | tf_op jit(solution)/shard_map/ppermute | solution.py:576
  77.1 1.7 %collective-permute-start.26 = (f32[128,128]{1,0:T(8,128)S(1)}, f32[128,128]{1,0:T(8,128)S(1)}, u32[]{:S(2)}, u32[]{:S(2)}) collective-permute-start(f32[128,128]{1,0:T(8,128)S(1)} %add.5.refs_0_), channel_id=1, source_target_pairs={{0,3},{1,2},{2,1},{3,0},{4,7},{5,6},{6,5},{7,4},{8,11},{9,10},{10,... | collective-permute-start | bytes 196616 | tf_op jit(solution)/shard_map/ppermute | solution.py:576
  79.1 3.3 %collective-permute-done.25.refs_2_ = f32[128,128]{1,0:T(8,128)S(1)} collective-permute-done((f32[128,128]{1,0:T(8,128)S(1)}, f32[128,128]{1,0:T(8,128)S(1)}, u32[]{:S(2)}, u32[]{:S(2)}) %collective-permute-start.25) | collective-permute-done | bytes 65568 | tf_op jit(solution)/shard_map/ppermute | solution.py:576
  82.4 0.9 collective-permute-done.26.refs_3_
  83.4 1.5 %collective-permute-start.30 = (f32[128,128]{1,0:T(8,128)S(1)}, f32[128,128]{1,0:T(8,128)S(1)}, u32[]{:S(2)}, u32[]{:S(2)}) collective-permute-start(f32[128,128]{1,0:T(8,128)S(1)} %scale.3.refs_1_), channel_id=1, source_target_pairs={{0,8},{4,12},{8,0},{12,4},{1,9},{5,13},{9,1},{13,5},{2,10},{6,14},... | collective-permute-start | bytes 196616 | tf_op jit(solution)/shard_map/ppermute | solution.py:576
  84.9 1.3 %collective-permute-start.29 = (f32[128,128]{1,0:T(8,128)S(1)}, f32[128,128]{1,0:T(8,128)S(1)}, u32[]{:S(2)}, u32[]{:S(2)}) collective-permute-start(f32[128,128]{1,0:T(8,128)S(1)} %scale.3.refs_1_), channel_id=1, source_target_pairs={{0,16},{16,0},{1,17},{17,1},{2,18},{18,2},{3,19},{19,3},{4,20},{20... | collective-permute-start | bytes 196616 | tf_op jit(solution)/shard_map/ppermute | solution.py:576
  86.2 0.7 collective-permute-start.28
  86.9 1.0 %join.1 = f32[8,96,256]{2,1,0:T(8,128)} custom-call(f32[8,96,128]{2,1,0:T(8,128)S(1)} %get-tuple-element.82.own.refs_0_, f32[4,96,128]{2,1,0:T(8,128)S(1)} %collective-permute-done.27.front.refs_0_, f32[4,96,128]{2,1,0:T(8,128)S(1)} %collective-permute-done.31.back.refs_1_), custom_call_target="tpu_custom_call" | custom-call | flops 1000000 | bytes 2000000 | tf_op jit(solution)/shard_map/join/pallas_call | solution.py:525
  88.3 0.7 first_half.4.base
  89.3 0.7 second_half.3.own
  90.0 1.6 %collective-permute-done.28.refs_3_ = f32[128,128]{1,0:T(8,128)S(1)} collective-permute-done((f32[128,128]{1,0:T(8,128)S(1)}, f32[128,128]{1,0:T(8,128)S(1)}, u32[]{:S(2)}, u32[]{:S(2)}) %collective-permute-start.28) | collective-permute-done | bytes 65568 | tf_op jit(solution)/shard_map/ppermute | solution.py:582
  92.9 1.5 %final.1 = f32[8,96,256]{2,1,0:T(8,128)} custom-call(f32[8,96,128]{2,1,0:T(8,128)S(1)} %second_half.3.own, f32[8,96,128]{2,1,0:T(8,128)S(1)} %first_half.5.other, bf16[8,2,192,512]{3,2,1,0:T(8,128)(2,1)S(1)} %get-tuple-element.48.vectors, f32[128,128]{1,0:T(8,128)S(1)} %collective-permute-done.34.refs_0_, f32[128,128]{1,0:T(8,128)S(1)} %collective-permute-done.35.refs_1_), custom_call_target="tpu_custom_call" | custom-call | flops 1000000000 | bytes 4000000 | tf_op jit(solution)/shard_map/final/pallas_call | solution.py:553
  (54 shorter events, 8.0 us)
Async XLA Ops:
  0.6 1.1 %copy-start = (f32[1,1,2,4,96,256]{5,4,3,2,1,0:T(8,128)S(1)}, f32[1,1,2,4,96,256]{5,4,3,2,1,0:T(8,128)}, u32[]{:S(2)}) copy-start(f32[1,1,2,4,96,256]{5,4,3,2,1,0:T(8,128)} %param.7) | copy-start | bytes 2359300
  2.0 6.4 %collective-permute-start = (f32[8,96,128]{2,1,0:T(8,128)S(1)}, f32[8,96,128]{2,1,0:T(8,128)S(1)}, u32[]{:S(2)}, u32[]{:S(2)}) collective-permute-start(f32[8,96,128]{2,1,0:T(8,128)S(1)} %get-tuple-element.47.x_ref.x), channel_id=1, source_target_pairs={{0,4},{4,0},{8,12},{12,8},{1,5},{5,1},{9,13},{13,9},{2,6},{6,2},{1... | collective-permute-start | bytes 1179656 | tf_op jit(solution)/shard_map/ppermute | solution.py:576
  2.6 18.8 %collective-permute-start.2 = (f32[4,96,128]{2,1,0:T(8,128)S(1)}, f32[4,96,128]{2,1,0:T(8,128)S(1)}, u32[]{:S(2)}, u32[]{:S(2)}) collective-permute-start(f32[4,96,128]{2,1,0:T(8,128)S(1)} %get-tuple-element.52), channel_id=1, source_target_pairs={{0,1},{1,2},{2,3},{3,0},{4,5},{5,6},{6,7},{7,4},{8,9},{9,10},{10,1... | collective-permute-start | bytes 589832 | tf_op jit(solution)/shard_map/ppermute | solution.py:571
  5.2 16.2 %collective-permute-start.3 = (f32[4,96,128]{2,1,0:T(8,128)S(1)}, f32[4,96,128]{2,1,0:T(8,128)S(1)}, u32[]{:S(2)}, u32[]{:S(2)}) collective-permute-start(f32[4,96,128]{2,1,0:T(8,128)S(1)} %get-tuple-element.52), channel_id=1, source_target_pairs={{0,3},{1,0},{2,1},{3,2},{4,7},{5,4},{6,5},{7,6},{8,11},{9,8},{10,9... | collective-permute-start | bytes 589832 | tf_op jit(solution)/shard_map/ppermute | solution.py:571
  7.3 14.6 %collective-permute-start.1 = (f32[8,96,128]{2,1,0:T(8,128)S(1)}, f32[8,96,128]{2,1,0:T(8,128)S(1)}, u32[]{:S(2)}, u32[]{:S(2)}) collective-permute-start(f32[8,96,128]{2,1,0:T(8,128)S(1)} %get-tuple-element.47.x_ref.x), channel_id=1, source_target_pairs={{0,12},{4,8},{8,4},{12,0},{1,13},{5,9},{9,5},{13,1},{2,14},{6,10},... | collective-permute-start | bytes 1179656 | tf_op jit(solution)/shard_map/ppermute | solution.py:589
  8.5 14.5 %collective-permute-start.4 = (f32[4,96,128]{2,1,0:T(8,128)S(1)}, f32[4,96,128]{2,1,0:T(8,128)S(1)}, u32[]{:S(2)}, u32[]{:S(2)}) collective-permute-start(f32[4,96,128]{2,1,0:T(8,128)S(1)} %get-tuple-element.58), channel_id=1, source_target_pairs={{0,1},{1,2},{2,3},{3,0},{4,5},{5,6},{6,7},{7,4},{8,9},{9,10},{10,1... | collective-permute-start | bytes 589832 | tf_op jit(solution)/shard_map/ppermute | solution.py:571
  8.5 16.3 %collective-permute-start.5 = (f32[4,96,128]{2,1,0:T(8,128)S(1)}, f32[4,96,128]{2,1,0:T(8,128)S(1)}, u32[]{:S(2)}, u32[]{:S(2)}) collective-permute-start(f32[4,96,128]{2,1,0:T(8,128)S(1)} %get-tuple-element.58), channel_id=1, source_target_pairs={{0,3},{1,0},{2,1},{3,2},{4,7},{5,4},{6,5},{7,6},{8,11},{9,8},{10,9... | collective-permute-start | bytes 589832 | tf_op jit(solution)/shard_map/ppermute | solution.py:571
  24.8 6.8 %copy-start.1 = (f32[2,512]{1,0:T(2,128)S(1)}, f32[2,512]{1,0:T(2,128)}, u32[]{:S(2)}) copy-start(f32[2,512]{1,0:T(2,128)} %inverse.1) | copy-start | bytes 12292
  25.8 1.3 %collective-permute-start.6 = (f32[256,128]{1,0:T(8,128)S(1)}, f32[256,128]{1,0:T(8,128)S(1)}, u32[]{:S(2)}, u32[]{:S(2)}) collective-permute-start(f32[256,128]{1,0:T(8,128)S(1)} %get-tuple-element.61), channel_id=1, source_target_pairs={{0,4},{4,0},{8,12},{12,8},{1,5},{5,1},{9,13},{13,9},{2,6},{6,2},{1... | collective-permute-start | bytes 393224 | tf_op jit(solution)/shard_map/ppermute | solution.py:576
  27.2 4.6 %collective-permute-start.7 = (f32[128,128]{1,0:T(8,128)S(1)}, f32[128,128]{1,0:T(8,128)S(1)}, u32[]{:S(2)}, u32[]{:S(2)}) collective-permute-start(f32[128,128]{1,0:T(8,128)S(1)} %get-tuple-element.63), channel_id=1, source_target_pairs={{0,8},{4,12},{8,0},{12,4},{1,9},{5,13},{9,1},{13,5},{2,10},{6,14},... | collective-permute-start | bytes 196616 | tf_op jit(solution)/shard_map/ppermute | solution.py:576
  28.7 8.2 %collective-permute-start.8 = (f32[128,128]{1,0:T(8,128)S(1)}, f32[128,128]{1,0:T(8,128)S(1)}, u32[]{:S(2)}, u32[]{:S(2)}) collective-permute-start(f32[128,128]{1,0:T(8,128)S(1)} %get-tuple-element.62.refs_0_), channel_id=1, source_target_pairs={{0,2},{1,3},{2,0},{3,1},{4,6},{5,7},{6,4},{7,5},{8,10},{9,11},{10,... | collective-permute-start | bytes 196616 | tf_op jit(solution)/shard_map/ppermute | solution.py:576
  30.0 7.7 %collective-permute-start.9 = (f32[128,128]{1,0:T(8,128)S(1)}, f32[128,128]{1,0:T(8,128)S(1)}, u32[]{:S(2)}, u32[]{:S(2)}) collective-permute-start(f32[128,128]{1,0:T(8,128)S(1)} %get-tuple-element.63), channel_id=1, source_target_pairs={{0,10},{1,11},{2,8},{3,9},{4,14},{5,15},{6,12},{7,13},{8,2},{9,3},... | collective-permute-start | bytes 196616 | tf_op jit(solution)/shard_map/ppermute | solution.py:582
  37.8 5.0 %collective-permute-start.11 = (f32[128,128]{1,0:T(8,128)S(1)}, f32[128,128]{1,0:T(8,128)S(1)}, u32[]{:S(2)}, u32[]{:S(2)}) collective-permute-start(f32[128,128]{1,0:T(8,128)S(1)} %scale.2.left), channel_id=1, source_target_pairs={{0,8},{4,12},{8,0},{12,4},{1,9},{5,13},{9,1},{13,5},{2,10},{6,14},... | collective-permute-start | bytes 196616 | tf_op jit(solution)/shard_map/ppermute | solution.py:576
  39.4 5.2 %collective-permute-start.12 = (f32[128,128]{1,0:T(8,128)S(1)}, f32[128,128]{1,0:T(8,128)S(1)}, u32[]{:S(2)}, u32[]{:S(2)}) collective-permute-start(f32[128,128]{1,0:T(8,128)S(1)} %scale.2.left), channel_id=1, source_target_pairs={{0,9},{1,8},{2,11},{3,10},{4,13},{5,12},{6,15},{7,14},{8,1},{9,0},... | collective-permute-start | bytes 196616 | tf_op jit(solution)/shard_map/ppermute | solution.py:582
  39.8 4.8 %collective-permute-start.10 = (f32[128,128]{1,0:T(8,128)S(1)}, f32[128,128]{1,0:T(8,128)S(1)}, u32[]{:S(2)}, u32[]{:S(2)}) collective-permute-start(f32[128,128]{1,0:T(8,128)S(1)} %scale.2.left), channel_id=1, source_target_pairs={{0,1},{1,0},{2,3},{3,2},{4,5},{5,4},{6,7},{7,6},{8,9},{9,8},{10,11... | collective-permute-start | bytes 196616 | tf_op jit(solution)/shard_map/ppermute | solution.py:576
  44.5 1.3 %collective-permute-start.14 = (f32[128,128]{1,0:T(8,128)S(1)}, f32[128,128]{1,0:T(8,128)S(1)}, u32[]{:S(2)}, u32[]{:S(2)}) collective-permute-start(f32[128,128]{1,0:T(8,128)S(1)} %add.4.refs_2_), channel_id=1, source_target_pairs={{0,4},{4,0},{8,12},{12,8},{1,5},{5,1},{9,13},{13,9},{2,6},{6,2},{1... | collective-permute-start | bytes 196616 | tf_op jit(solution)/shard_map/ppermute | solution.py:576
  44.6 1.5 %collective-permute-start.13 = (f32[128,128]{1,0:T(8,128)S(1)}, f32[128,128]{1,0:T(8,128)S(1)}, u32[]{:S(2)}, u32[]{:S(2)}) collective-permute-start(f32[128,128]{1,0:T(8,128)S(1)} %add.3.refs_1_), channel_id=1, source_target_pairs={{0,4},{4,0},{8,12},{12,8},{1,5},{5,1},{9,13},{13,9},{2,6},{6,2},{1... | collective-permute-start | bytes 196616 | tf_op jit(solution)/shard_map/ppermute | solution.py:576
  46.8 4.5 %collective-permute-start.15 = (f32[8,96,128]{2,1,0:T(8,128)S(1)}, f32[8,96,128]{2,1,0:T(8,128)S(1)}, u32[]{:S(2)}, u32[]{:S(2)}) collective-permute-start(f32[8,96,128]{2,1,0:T(8,128)S(1)} %get-tuple-element.79.x_ref.x), channel_id=1, source_target_pairs={{0,4},{4,0},{8,12},{12,8},{1,5},{5,1},{9,13},{13,9},{2,6},{6,2},{1... | collective-permute-start | bytes 1179656 | tf_op jit(solution)/shard_map/ppermute | solution.py:576
  47.2 9.6 %collective-permute-start.17 = (f32[4,96,128]{2,1,0:T(8,128)S(1)}, f32[4,96,128]{2,1,0:T(8,128)S(1)}, u32[]{:S(2)}, u32[]{:S(2)}) collective-permute-start(f32[4,96,128]{2,1,0:T(8,128)S(1)} %get-tuple-element.70), channel_id=1, source_target_pairs={{0,1},{1,2},{2,3},{3,0},{4,5},{5,6},{6,7},{7,4},{8,9},{9,10},{10,1... | collective-permute-start | bytes 589832 | tf_op jit(solution)/shard_map/ppermute | solution.py:571
  47.8 12.3 %collective-permute-start.18 = (f32[4,96,128]{2,1,0:T(8,128)S(1)}, f32[4,96,128]{2,1,0:T(8,128)S(1)}, u32[]{:S(2)}, u32[]{:S(2)}) collective-permute-start(f32[4,96,128]{2,1,0:T(8,128)S(1)} %get-tuple-element.70), channel_id=1, source_target_pairs={{0,3},{1,0},{2,1},{3,2},{4,7},{5,4},{6,5},{7,6},{8,11},{9,8},{10,9... | collective-permute-start | bytes 589832 | tf_op jit(solution)/shard_map/ppermute | solution.py:571
  51.0 11.2 %collective-permute-start.16 = (f32[8,96,128]{2,1,0:T(8,128)S(1)}, f32[8,96,128]{2,1,0:T(8,128)S(1)}, u32[]{:S(2)}, u32[]{:S(2)}) collective-permute-start(f32[8,96,128]{2,1,0:T(8,128)S(1)} %get-tuple-element.79.x_ref.x), channel_id=1, source_target_pairs={{0,12},{4,8},{8,4},{12,0},{1,13},{5,9},{9,5},{13,1},{2,14},{6,10},... | collective-permute-start | bytes 1179656 | tf_op jit(solution)/shard_map/ppermute | solution.py:589
  51.2 14.0 %collective-permute-start.19 = (f32[4,96,128]{2,1,0:T(8,128)S(1)}, f32[4,96,128]{2,1,0:T(8,128)S(1)}, u32[]{:S(2)}, u32[]{:S(2)}) collective-permute-start(f32[4,96,128]{2,1,0:T(8,128)S(1)} %get-tuple-element.74), channel_id=1, source_target_pairs={{0,1},{1,2},{2,3},{3,0},{4,5},{5,6},{6,7},{7,4},{8,9},{9,10},{10,1... | collective-permute-start | bytes 589832 | tf_op jit(solution)/shard_map/ppermute | solution.py:571
  51.2 16.1 %collective-permute-start.20 = (f32[4,96,128]{2,1,0:T(8,128)S(1)}, f32[4,96,128]{2,1,0:T(8,128)S(1)}, u32[]{:S(2)}, u32[]{:S(2)}) collective-permute-start(f32[4,96,128]{2,1,0:T(8,128)S(1)} %get-tuple-element.74), channel_id=1, source_target_pairs={{0,3},{1,0},{2,1},{3,2},{4,7},{5,4},{6,5},{7,6},{8,11},{9,8},{10,9... | collective-permute-start | bytes 589832 | tf_op jit(solution)/shard_map/ppermute | solution.py:571
  56.8 17.6 %collective-permute-start.23 = (f32[8,96,128]{2,1,0:T(8,128)S(1)}, f32[8,96,128]{2,1,0:T(8,128)S(1)}, u32[]{:S(2)}, u32[]{:S(2)}) collective-permute-start(f32[8,96,128]{2,1,0:T(8,128)S(1)} %get-tuple-element.79.x_ref.x), channel_id=1, source_target_pairs={{0,16},{16,0},{1,17},{17,1},{2,18},{18,2},{3,19},{19,3},{4,20},{20... | collective-permute-start | bytes 1179656 | tf_op jit(solution)/shard_map/ppermute | solution.py:576
  68.3 1.7 %collective-permute-start.21 = (f32[256,128]{1,0:T(8,128)S(1)}, f32[256,128]{1,0:T(8,128)S(1)}, u32[]{:S(2)}, u32[]{:S(2)}) collective-permute-start(f32[256,128]{1,0:T(8,128)S(1)} %get-tuple-element.76), channel_id=1, source_target_pairs={{0,4},{4,0},{8,12},{12,8},{1,5},{5,1},{9,13},{13,9},{2,6},{6,2},{1... | collective-permute-start | bytes 393224 | tf_op jit(solution)/shard_map/ppermute | solution.py:576
  68.4 15.0 %collective-permute-start.27 = (f32[4,96,128]{2,1,0:T(8,128)S(1)}, f32[4,96,128]{2,1,0:T(8,128)S(1)}, u32[]{:S(2)}, u32[]{:S(2)}) collective-permute-start(f32[4,96,128]{2,1,0:T(8,128)S(1)} %get-tuple-element.71.front), channel_id=1, source_target_pairs={{0,16},{16,0},{1,17},{17,1},{2,18},{18,2},{3,19},{19,3},{4,20},{20... | collective-permute-start | bytes 589832 | tf_op jit(solution)/shard_map/ppermute | solution.py:576
  70.0 4.3 %collective-permute-start.22 = (f32[128,128]{1,0:T(8,128)S(1)}, f32[128,128]{1,0:T(8,128)S(1)}, u32[]{:S(2)}, u32[]{:S(2)}) collective-permute-start(f32[128,128]{1,0:T(8,128)S(1)} %get-tuple-element.78), channel_id=1, source_target_pairs={{0,8},{4,12},{8,0},{12,4},{1,9},{5,13},{9,1},{13,5},{2,10},{6,14},... | collective-permute-start | bytes 196616 | tf_op jit(solution)/shard_map/ppermute | solution.py:576
  71.5 15.4 %collective-permute-start.31 = (f32[4,96,128]{2,1,0:T(8,128)S(1)}, f32[4,96,128]{2,1,0:T(8,128)S(1)}, u32[]{:S(2)}, u32[]{:S(2)}) collective-permute-start(f32[4,96,128]{2,1,0:T(8,128)S(1)} %get-tuple-element.84), channel_id=1, source_target_pairs={{0,16},{16,0},{1,17},{17,1},{2,18},{18,2},{3,19},{19,3},{4,20},{20... | collective-permute-start | bytes 589832 | tf_op jit(solution)/shard_map/ppermute | solution.py:576
  74.4 4.7 %collective-permute-start.24 = (f32[128,128]{1,0:T(8,128)S(1)}, f32[128,128]{1,0:T(8,128)S(1)}, u32[]{:S(2)}, u32[]{:S(2)}) collective-permute-start(f32[128,128]{1,0:T(8,128)S(1)} %add.5.refs_0_), channel_id=1, source_target_pairs={{0,1},{1,0},{2,3},{3,2},{4,5},{5,4},{6,7},{7,6},{8,9},{9,8},{10,11... | collective-permute-start | bytes 196616 | tf_op jit(solution)/shard_map/ppermute | solution.py:576
  75.6 6.7 %collective-permute-start.25 = (f32[128,128]{1,0:T(8,128)S(1)}, f32[128,128]{1,0:T(8,128)S(1)}, u32[]{:S(2)}, u32[]{:S(2)}) collective-permute-start(f32[128,128]{1,0:T(8,128)S(1)} %add.5.refs_0_), channel_id=1, source_target_pairs={{0,2},{1,3},{2,0},{3,1},{4,6},{5,7},{6,4},{7,5},{8,10},{9,11},{10,... | collective-permute-start | bytes 196616 | tf_op jit(solution)/shard_map/ppermute | solution.py:576
  77.1 6.2 %collective-permute-start.26 = (f32[128,128]{1,0:T(8,128)S(1)}, f32[128,128]{1,0:T(8,128)S(1)}, u32[]{:S(2)}, u32[]{:S(2)}) collective-permute-start(f32[128,128]{1,0:T(8,128)S(1)} %add.5.refs_0_), channel_id=1, source_target_pairs={{0,3},{1,2},{2,1},{3,0},{4,7},{5,6},{6,5},{7,4},{8,11},{9,10},{10,... | collective-permute-start | bytes 196616 | tf_op jit(solution)/shard_map/ppermute | solution.py:576
  83.4 4.6 %collective-permute-start.30 = (f32[128,128]{1,0:T(8,128)S(1)}, f32[128,128]{1,0:T(8,128)S(1)}, u32[]{:S(2)}, u32[]{:S(2)}) collective-permute-start(f32[128,128]{1,0:T(8,128)S(1)} %scale.3.refs_1_), channel_id=1, source_target_pairs={{0,8},{4,12},{8,0},{12,4},{1,9},{5,13},{9,1},{13,5},{2,10},{6,14},... | collective-permute-start | bytes 196616 | tf_op jit(solution)/shard_map/ppermute | solution.py:576
  84.9 4.3 %collective-permute-start.29 = (f32[128,128]{1,0:T(8,128)S(1)}, f32[128,128]{1,0:T(8,128)S(1)}, u32[]{:S(2)}, u32[]{:S(2)}) collective-permute-start(f32[128,128]{1,0:T(8,128)S(1)} %scale.3.refs_1_), channel_id=1, source_target_pairs={{0,16},{16,0},{1,17},{17,1},{2,18},{18,2},{3,19},{19,3},{4,20},{20... | collective-permute-start | bytes 196616 | tf_op jit(solution)/shard_map/ppermute | solution.py:576
  86.2 3.1 %collective-permute-start.32 = (f32[128,128]{1,0:T(8,128)S(1)}, f32[128,128]{1,0:T(8,128)S(1)}, u32[]{:S(2)}, u32[]{:S(2)}) collective-permute-start(f32[128,128]{1,0:T(8,128)S(1)} %scale.3.refs_1_), channel_id=1, source_target_pairs={{0,4},{4,0},{8,12},{12,8},{1,5},{5,1},{9,13},{13,9},{2,6},{6,2},{1... | collective-permute-start | bytes 196616 | tf_op jit(solution)/shard_map/ppermute | solution.py:576
  86.2 5.4 %collective-permute-start.28 = (f32[128,128]{1,0:T(8,128)S(1)}, f32[128,128]{1,0:T(8,128)S(1)}, u32[]{:S(2)}, u32[]{:S(2)}) collective-permute-start(f32[128,128]{1,0:T(8,128)S(1)} %scale.3.refs_1_), channel_id=1, source_target_pairs={{0,24},{4,28},{8,16},{12,20},{16,8},{20,12},{24,0},{28,4},{1,25},{... | collective-permute-start | bytes 196616 | tf_op jit(solution)/shard_map/ppermute | solution.py:582
  88.0 1.3 %collective-permute-start.33 = (f32[128,128]{1,0:T(8,128)S(1)}, f32[128,128]{1,0:T(8,128)S(1)}, u32[]{:S(2)}, u32[]{:S(2)}) collective-permute-start(f32[128,128]{1,0:T(8,128)S(1)} %collective-permute-done.30.refs_2_), channel_id=1, source_target_pairs={{0,4},{4,0},{8,12},{12,8},{1,5},{5,1},{9,13},{13,9},{2,6},{6,2},{1... | collective-permute-start | bytes 196616 | tf_op jit(solution)/shard_map/ppermute | solution.py:576
  89.2 3.1 %collective-permute-start.34 = (f32[128,128]{1,0:T(8,128)S(1)}, f32[128,128]{1,0:T(8,128)S(1)}, u32[]{:S(2)}, u32[]{:S(2)}) collective-permute-start(f32[128,128]{1,0:T(8,128)S(1)} %collective-permute-done.29.refs_2_), channel_id=1, source_target_pairs={{0,4},{4,0},{8,12},{12,8},{1,5},{5,1},{9,13},{13,9},{2,6},{6,2},{1... | collective-permute-start | bytes 196616 | tf_op jit(solution)/shard_map/ppermute | solution.py:576
  91.6 1.3 %collective-permute-start.35 = (f32[128,128]{1,0:T(8,128)S(1)}, f32[128,128]{1,0:T(8,128)S(1)}, u32[]{:S(2)}, u32[]{:S(2)}) collective-permute-start(f32[128,128]{1,0:T(8,128)S(1)} %collective-permute-done.28.refs_3_), channel_id=1, source_target_pairs={{0,4},{4,0},{8,12},{12,8},{1,5},{5,1},{9,13},{13,9},{2,6},{6,2},{1... | collective-permute-start | bytes 196616 | tf_op jit(solution)/shard_map/ppermute | solution.py:576

commit v15 on v14

--- a/solution.py
+++ b/solution.py
@@ -674,9 +674,8 @@
     full_residual = join(residual, other_front, other_back)
     own[-1], full_residual = lax.optimization_barrier((own[-1], full_residual))
     own_x = first_half(x, [residual], own, by_columns)
-    other[0], own_x = lax.optimization_barrier((other[0], own_x))
+    other[-1], own_x = lax.optimization_barrier((other[-1], own_x))
     own_x = second_half(own_x, paired(own), by_columns, False)
-    other[-1], own_x = lax.optimization_barrier((other[-1], own_x))
     other_second = paired(other)
     other_x = first_half(other_x, [other_front, other_back], other, by_columns)
     whole = final(own_x, other_x, other_second, by_columns)

time: 94.7 us -> 94.1 us (level)
  transfers between devices with their start and end apart: 36 -> 36, of which waited for: 19 -> 18; matrix products, arithmetic and copies ran while one was open for 0% -> 0% of each run, Pallas kernels for 20% -> 20%
where the time goes in v15:
time: 94.1 us; the launch traced here: 93.9 us
  starting transfers between devices  41.8 us (44%)
  waiting for transfers between devices  27.3 us (29%)
  Pallas kernels  22.5 us (24%)
  local copies, waits for them, and re-layouts  1.13 us (1%)
  between operations  1.1 us (1%)
    ppermute x23, starting transfers between devices, crossed(): return lax.ppermute(value, axis, [(i, i ^ mask) for i in range(count)])  20.8 us
    ppermute x8, starting transfers between devices, shifted(): lax.ppermute(value, axis, [(i, (i + step) % count) for i in range(count)])  16.2 us
    ppermute x23, waiting for transfers between devices, crossed(): return lax.ppermute(value, axis, [(i, i ^ mask) for i in range(count)])  14.9 us
    pallas_call x1, Pallas kernels, prepare(): pl.pallas_call(functools.partial(prepare_kernel, ny, nx), out_shape=(pltp...  9.08 us
    ppermute x8, waiting for transfers between devices, shifted(): lax.ppermute(value, axis, [(i, (i + step) % count) for i in range(count)])  7.53 us
    ppermute x3, starting transfers between devices, crossed_both(): return lax.ppermute(value, (first, second), pairs)  3.35 us
    ppermute x3, waiting for transfers between devices, crossed_both(): return lax.ppermute(value, (first, second), pairs)  3.29 us
    pallas_call x2, Pallas kernels, middle(): pl.pallas_call(middle_kernel, out_shape=(half, half, pltpu.VMEM((vectors....  2.15 us
  transfers between devices with their start and end apart: 36, of which 18 were waited for; matrix products, arithmetic and copies ran while one was open for 0% of the time, Pallas kernels for 20%

profile of v15, /device:TPU:0, one launch (start us, length us, event | category | flops | bytes accessed | tf_op | source)
XLA Modules:
  0.0 93.9 jit_solution(1069421483682704179)
XLA Ops:
  0.6 1.1 %copy-done = f32[1,1,2,4,96,256]{5,4,3,2,1,0:T(8,128)S(1)} copy-done((f32[1,1,2,4,96,256]{5,4,3,2,1,0:T(8,128)S(1)}, f32[1,1,2,4,96,256]{5,4,3,2,1,0:T(8,128)}, u32[]{:S(2)}) %copy-start) | copy-done | bytes 786456
  2.6 2.6 %collective-permute-start.2 = (f32[4,96,128]{2,1,0:T(8,128)S(1)}, f32[4,96,128]{2,1,0:T(8,128)S(1)}, u32[]{:S(2)}, u32[]{:S(2)}) collective-permute-start(f32[4,96,128]{2,1,0:T(8,128)S(1)} %get-tuple-element.50), channel_id=1, source_target_pairs={{0,1},{1,2},{2,3},{3,0},{4,5},{5,6},{6,7},{7,4},{8,9},{9,10},{10,1... | collective-permute-start | bytes 589832 | tf_op jit(solution)/shard_map/ppermute | solution.py:571
  5.2 2.1 %collective-permute-start.3 = (f32[4,96,128]{2,1,0:T(8,128)S(1)}, f32[4,96,128]{2,1,0:T(8,128)S(1)}, u32[]{:S(2)}, u32[]{:S(2)}) collective-permute-start(f32[4,96,128]{2,1,0:T(8,128)S(1)} %get-tuple-element.50), channel_id=1, source_target_pairs={{0,3},{1,0},{2,1},{3,2},{4,7},{5,4},{6,5},{7,6},{8,11},{9,8},{10,9... | collective-permute-start | bytes 589832 | tf_op jit(solution)/shard_map/ppermute | solution.py:571
  7.3 1.2 %collective-permute-start.1 = (f32[8,96,128]{2,1,0:T(8,128)S(1)}, f32[8,96,128]{2,1,0:T(8,128)S(1)}, u32[]{:S(2)}, u32[]{:S(2)}) collective-permute-start(f32[8,96,128]{2,1,0:T(8,128)S(1)} %get-tuple-element.45.x_ref.x), channel_id=1, source_target_pairs={{0,12},{4,8},{8,4},{12,0},{1,13},{5,9},{9,5},{13,1},{2,14},{6,10},... | collective-permute-start | bytes 1179656 | tf_op jit(solution)/shard_map/ppermute | solution.py:589
  8.5 3.8 %collective-permute-start.5 = (f32[4,96,128]{2,1,0:T(8,128)S(1)}, f32[4,96,128]{2,1,0:T(8,128)S(1)}, u32[]{:S(2)}, u32[]{:S(2)}) collective-permute-start(f32[4,96,128]{2,1,0:T(8,128)S(1)} %get-tuple-element.56), channel_id=1, source_target_pairs={{0,3},{1,0},{2,1},{3,2},{4,7},{5,4},{6,5},{7,6},{8,11},{9,8},{10,9... | collective-permute-start | bytes 589832 | tf_op jit(solution)/shard_map/ppermute | solution.py:571
  12.3 9.1 %prepare.1 = (f32[8,96,128]{2,1,0:T(8,128)S(1)}, f32[8,96,128]{2,1,0:T(8,128)S(1)}, bf16[5,8,192,192]{3,2,1,0:T(8,128)(2,1)S(1)}, bf16[4,8,192,192]{3,2,1,0:T(8,...) custom-call(f32[8,96,128]{2,1,0:T(8,128)S(1)} %get-tuple-element.45.x_ref.x, ...), custom_call_target="tpu_custom_call" | custom-call | flops 8000000000 | bytes 25000000 | tf_op jit(solution)/shard_map/prepare/pallas_call | solution.py:225
  21.9 1.1 %middle.2 = (f32[4,96,128]{2,1,0:T(8,128)S(1)}, f32[4,96,128]{2,1,0:T(8,128)S(1)}, f32[512,128]{1,0:T(8,128)S(1)}) custom-call(f32[8,96,128]{2,1,0:T(8,128)S(1)} %get-tuple-element.47.rest, f32[8,96,128]{2,1,0:T(8,128)S(1)} %collective-permute-done.near, f32[8,96,128]{2,1,0:T(8,128)S(1)} %collective-permute-done.1.far, f32[4,96,128]{2,1,0:T(8,128)S(1)} %front_faces.2.front, ...), custom_call_target="tpu_custom_call" | custom-call | flops 1000 | bytes 1000 | tf_op jit(solution)/shard_map/middle/pallas_call | solution.py:322
  23.3 1.5 %collective-permute-done.5.forward = f32[4,96,128]{2,1,0:T(8,128)S(1)} collective-permute-done((f32[4,96,128]{2,1,0:T(8,128)S(1)}, f32[4,96,128]{2,1,0:T(8,128)S(1)}, u32[]{:S(2)}, u32[]{:S(2)}) %collective-permute-start.5) | collective-permute-done | bytes 196640 | tf_op jit(solution)/shard_map/ppermute | solution.py:571
  24.8 1.0 %forward_face.2 = (f32[8,96,128]{2,1,0:T(8,128)S(1)}, f32[4,96,128]{2,1,0:T(8,128)}, f32[256,128]{1,0:T(8,128)S(1)}, f32[256,128]{1,0:T(8,128)S(1)}) custom-call(f32[4,96,128]{2,1,0:T(8,128)S(1)} %get-tuple-element.53.front, f32[512,128]{1,0:T(8,128)S(1)} %get-tuple-element.54.partial, f32[4,96,128]{2,1,0:T(8,128)S(1)} %backward_face.2.rest, ...), custom_call_target="tpu_custom_call" | custom-call | flops 2000000000 | bytes 8000000 | tf_op jit(solution)/shard_map/forward_face/pallas_call | solution.py:371
  25.8 1.3 %collective-permute-done.6.received = f32[256,128]{1,0:T(8,128)S(1)} collective-permute-done((f32[256,128]{1,0:T(8,128)S(1)}, f32[256,128]{1,0:T(8,128)S(1)}, u32[]{:S(2)}, u32[]{:S(2)}) %collective-permute-start.6) | collective-permute-done | bytes 131104 | tf_op jit(solution)/shard_map/ppermute | solution.py:576
  27.2 1.6 %collective-permute-start.7 = (f32[128,128]{1,0:T(8,128)S(1)}, f32[128,128]{1,0:T(8,128)S(1)}, u32[]{:S(2)}, u32[]{:S(2)}) collective-permute-start(f32[128,128]{1,0:T(8,128)S(1)} %get-tuple-element.61), channel_id=1, source_target_pairs={{0,8},{4,12},{8,0},{12,4},{1,9},{5,13},{9,1},{13,5},{2,10},{6,14},... | collective-permute-start | bytes 196616 | tf_op jit(solution)/shard_map/ppermute | solution.py:576
  28.7 1.2 %collective-permute-start.8 = (f32[128,128]{1,0:T(8,128)S(1)}, f32[128,128]{1,0:T(8,128)S(1)}, u32[]{:S(2)}, u32[]{:S(2)}) collective-permute-start(f32[128,128]{1,0:T(8,128)S(1)} %get-tuple-element.60.refs_0_), channel_id=1, source_target_pairs={{0,2},{1,3},{2,0},{3,1},{4,6},{5,7},{6,4},{7,5},{8,10},{9,11},{10,... | collective-permute-start | bytes 196616 | tf_op jit(solution)/shard_map/ppermute | solution.py:576
  30.0 1.7 %collective-permute-start.9 = (f32[128,128]{1,0:T(8,128)S(1)}, f32[128,128]{1,0:T(8,128)S(1)}, u32[]{:S(2)}, u32[]{:S(2)}) collective-permute-start(f32[128,128]{1,0:T(8,128)S(1)} %get-tuple-element.61), channel_id=1, source_target_pairs={{0,10},{1,11},{2,8},{3,9},{4,14},{5,15},{6,12},{7,13},{8,2},{9,3},... | collective-permute-start | bytes 196616 | tf_op jit(solution)/shard_map/ppermute | solution.py:582
  31.8 5.2 %collective-permute-done.8.refs_2_ = f32[128,128]{1,0:T(8,128)S(1)} collective-permute-done((f32[128,128]{1,0:T(8,128)S(1)}, f32[128,128]{1,0:T(8,128)S(1)}, u32[]{:S(2)}, u32[]{:S(2)}) %collective-permute-start.8) | collective-permute-done | bytes 65568 | tf_op jit(solution)/shard_map/ppermute | solution.py:576
  37.0 0.7 collective-permute-done.9.refs_3_
  37.8 1.6 %collective-permute-start.11 = (f32[128,128]{1,0:T(8,128)S(1)}, f32[128,128]{1,0:T(8,128)S(1)}, u32[]{:S(2)}, u32[]{:S(2)}) collective-permute-start(f32[128,128]{1,0:T(8,128)S(1)} %scale.2.left), channel_id=1, source_target_pairs={{0,8},{4,12},{8,0},{12,4},{1,9},{5,13},{9,1},{13,5},{2,10},{6,14},... | collective-permute-start | bytes 196616 | tf_op jit(solution)/shard_map/ppermute | solution.py:576
  39.8 1.6 %collective-permute-start.10 = (f32[128,128]{1,0:T(8,128)S(1)}, f32[128,128]{1,0:T(8,128)S(1)}, u32[]{:S(2)}, u32[]{:S(2)}) collective-permute-start(f32[128,128]{1,0:T(8,128)S(1)} %scale.2.left), channel_id=1, source_target_pairs={{0,1},{1,0},{2,3},{3,2},{4,5},{5,4},{6,7},{7,6},{8,9},{9,8},{10,11... | collective-permute-start | bytes 196616 | tf_op jit(solution)/shard_map/ppermute | solution.py:576
  41.3 1.5 %collective-permute-done.11.left = f32[128,128]{1,0:T(8,128)S(1)} collective-permute-done((f32[128,128]{1,0:T(8,128)S(1)}, f32[128,128]{1,0:T(8,128)S(1)}, u32[]{:S(2)}, u32[]{:S(2)}) %collective-permute-start.11) | collective-permute-done | bytes 65568 | tf_op jit(solution)/shard_map/ppermute | solution.py:576
  42.8 1.7 %collective-permute-done.12.right = f32[128,128]{1,0:T(8,128)S(1)} collective-permute-done((f32[128,128]{1,0:T(8,128)S(1)}, f32[128,128]{1,0:T(8,128)S(1)}, u32[]{:S(2)}, u32[]{:S(2)}) %collective-permute-start.12) | collective-permute-done | bytes 65568 | tf_op jit(solution)/shard_map/ppermute | solution.py:582
  46.1 0.7 second_half.2
  47.2 0.7 collective-permute-start.17
  47.8 3.2 %collective-permute-start.18 = (f32[4,96,128]{2,1,0:T(8,128)S(1)}, f32[4,96,128]{2,1,0:T(8,128)S(1)}, u32[]{:S(2)}, u32[]{:S(2)}) collective-permute-start(f32[4,96,128]{2,1,0:T(8,128)S(1)} %get-tuple-element.68), channel_id=1, source_target_pairs={{0,3},{1,0},{2,1},{3,2},{4,7},{5,4},{6,5},{7,6},{8,11},{9,8},{10,9... | collective-permute-start | bytes 589832 | tf_op jit(solution)/shard_map/ppermute | solution.py:571
  51.2 3.8 %collective-permute-start.20 = (f32[4,96,128]{2,1,0:T(8,128)S(1)}, f32[4,96,128]{2,1,0:T(8,128)S(1)}, u32[]{:S(2)}, u32[]{:S(2)}) collective-permute-start(f32[4,96,128]{2,1,0:T(8,128)S(1)} %get-tuple-element.72), channel_id=1, source_target_pairs={{0,3},{1,0},{2,1},{3,2},{4,7},{5,4},{6,5},{7,6},{8,11},{9,8},{10,9... | collective-permute-start | bytes 589832 | tf_op jit(solution)/shard_map/ppermute | solution.py:571
  55.1 1.3 %local_part.1.rest = f32[8,96,128]{2,1,0:T(8,128)S(1)} custom-call(f32[8,96,128]{2,1,0:T(8,128)S(1)} %get-tuple-element.77.x_ref.x, f32[8,96,128]{2,1,0:T(8,128)S(1)} %get-tuple-element.63.source, bf16[5,8,192,192]{3,2,1,0:T(8,128)(2,1)S(1)} %get-tuple-element.64.local), custom_call_target="tpu_custom_call" | custom-call | flops 8000000000 | bytes 8000000 | tf_op jit(solution)/shard_map/local_part/pallas_call | solution.py:142
  56.8 1.5 %collective-permute-start.23 = (f32[8,96,128]{2,1,0:T(8,128)S(1)}, f32[8,96,128]{2,1,0:T(8,128)S(1)}, u32[]{:S(2)}, u32[]{:S(2)}) collective-permute-start(f32[8,96,128]{2,1,0:T(8,128)S(1)} %get-tuple-element.77.x_ref.x), channel_id=1, source_target_pairs={{0,16},{16,0},{1,17},{17,1},{2,18},{18,2},{3,19},{19,3},{4,20},{20... | collective-permute-start | bytes 1179656 | tf_op jit(solution)/shard_map/ppermute | solution.py:576
  58.3 1.9 %collective-permute-done.18.forward = f32[4,96,128]{2,1,0:T(8,128)S(1)} collective-permute-done((f32[4,96,128]{2,1,0:T(8,128)S(1)}, f32[4,96,128]{2,1,0:T(8,128)S(1)}, u32[]{:S(2)}, u32[]{:S(2)}) %collective-permute-start.18) | collective-permute-done | bytes 196640 | tf_op jit(solution)/shard_map/ppermute | solution.py:571
  60.6 1.6 %collective-permute-done.16.far = f32[8,96,128]{2,1,0:T(8,128)S(1)} collective-permute-done((f32[8,96,128]{2,1,0:T(8,128)S(1)}, f32[8,96,128]{2,1,0:T(8,128)S(1)}, u32[]{:S(2)}, u32[]{:S(2)}) %collective-permute-start.16) | collective-permute-done | bytes 393248 | tf_op jit(solution)/shard_map/ppermute | solution.py:589
  62.2 1.1 %middle.3 = (f32[4,96,128]{2,1,0:T(8,128)S(1)}, f32[4,96,128]{2,1,0:T(8,128)S(1)}, f32[512,128]{1,0:T(8,128)S(1)}) custom-call(f32[8,96,128]{2,1,0:T(8,128)S(1)} %local_part.1.rest, f32[8,96,128]{2,1,0:T(8,128)S(1)} %collective-permute-done.15.near, f32[8,96,128]{2,1,0:T(8,128)S(1)} %collective-permute-done.16.far, f32[4,96,128]{2,1,0:T(8,128)S(1)} %front_faces.3.front, ...), custom_call_target="tpu_custom_call" | custom-call | flops 1000 | bytes 1000 | tf_op jit(solution)/shard_map/middle/pallas_call | solution.py:322
  63.3 1.9 %collective-permute-done.19.backward = f32[4,96,128]{2,1,0:T(8,128)S(1)} collective-permute-done((f32[4,96,128]{2,1,0:T(8,128)S(1)}, f32[4,96,128]{2,1,0:T(8,128)S(1)}, u32[]{:S(2)}, u32[]{:S(2)}) %collective-permute-start.19) | collective-permute-done | bytes 196640 | tf_op jit(solution)/shard_map/ppermute | solution.py:571
  65.6 1.8 %collective-permute-done.20.forward = f32[4,96,128]{2,1,0:T(8,128)S(1)} collective-permute-done((f32[4,96,128]{2,1,0:T(8,128)S(1)}, f32[4,96,128]{2,1,0:T(8,128)S(1)}, u32[]{:S(2)}, u32[]{:S(2)}) %collective-permute-start.20) | collective-permute-done | bytes 196640 | tf_op jit(solution)/shard_map/ppermute | solution.py:571
  67.4 0.9 forward_face.3
  68.4 1.6 %collective-permute-start.27 = (f32[4,96,128]{2,1,0:T(8,128)S(1)}, f32[4,96,128]{2,1,0:T(8,128)S(1)}, u32[]{:S(2)}, u32[]{:S(2)}) collective-permute-start(f32[4,96,128]{2,1,0:T(8,128)S(1)} %get-tuple-element.69.front), channel_id=1, source_target_pairs={{0,16},{16,0},{1,17},{17,1},{2,18},{18,2},{3,19},{19,3},{4,20},{20... | collective-permute-start | bytes 589832 | tf_op jit(solution)/shard_map/ppermute | solution.py:576
  70.0 1.5 %collective-permute-start.22 = (f32[128,128]{1,0:T(8,128)S(1)}, f32[128,128]{1,0:T(8,128)S(1)}, u32[]{:S(2)}, u32[]{:S(2)}) collective-permute-start(f32[128,128]{1,0:T(8,128)S(1)} %get-tuple-element.76), channel_id=1, source_target_pairs={{0,8},{4,12},{8,0},{12,4},{1,9},{5,13},{9,1},{13,5},{2,10},{6,14},... | collective-permute-start | bytes 196616 | tf_op jit(solution)/shard_map/ppermute | solution.py:576
  71.5 1.3 %collective-permute-start.30 = (f32[4,96,128]{2,1,0:T(8,128)S(1)}, f32[4,96,128]{2,1,0:T(8,128)S(1)}, u32[]{:S(2)}, u32[]{:S(2)}) collective-permute-start(f32[4,96,128]{2,1,0:T(8,128)S(1)} %get-tuple-element.82), channel_id=1, source_target_pairs={{0,16},{16,0},{1,17},{17,1},{2,18},{18,2},{3,19},{19,3},{4,20},{20... | collective-permute-start | bytes 589832 | tf_op jit(solution)/shard_map/ppermute | solution.py:576
  72.8 1.5 %collective-permute-done.22.right = f32[128,128]{1,0:T(8,128)S(1)} collective-permute-done((f32[128,128]{1,0:T(8,128)S(1)}, f32[128,128]{1,0:T(8,128)S(1)}, u32[]{:S(2)}, u32[]{:S(2)}) %collective-permute-start.22) | collective-permute-done | bytes 65568 | tf_op jit(solution)/shard_map/ppermute | solution.py:576
  74.4 1.3 %collective-permute-start.24 = (f32[128,128]{1,0:T(8,128)S(1)}, f32[128,128]{1,0:T(8,128)S(1)}, u32[]{:S(2)}, u32[]{:S(2)}) collective-permute-start(f32[128,128]{1,0:T(8,128)S(1)} %add.5.refs_0_), channel_id=1, source_target_pairs={{0,1},{1,0},{2,3},{3,2},{4,5},{5,4},{6,7},{7,6},{8,9},{9,8},{10,11... | collective-permute-start | bytes 196616 | tf_op jit(solution)/shard_map/ppermute | solution.py:576
  75.6 1.5 %collective-permute-start.25 = (f32[128,128]{1,0:T(8,128)S(1)}, f32[128,128]{1,0:T(8,128)S(1)}, u32[]{:S(2)}, u32[]{:S(2)}) collective-permute-start(f32[128,128]{1,0:T(8,128)S(1)} %add.5.refs_0_), channel_id=1, source_target_pairs={{0,2},{1,3},{2,0},{3,1},{4,6},{5,7},{6,4},{7,5},{8,10},{9,11},{10,... | collective-permute-start | bytes 196616 | tf_op jit(solution)/shard_map/ppermute | solution.py:576
  77.1 1.7 %collective-permute-start.26 = (f32[128,128]{1,0:T(8,128)S(1)}, f32[128,128]{1,0:T(8,128)S(1)}, u32[]{:S(2)}, u32[]{:S(2)}) collective-permute-start(f32[128,128]{1,0:T(8,128)S(1)} %add.5.refs_0_), channel_id=1, source_target_pairs={{0,3},{1,2},{2,1},{3,0},{4,7},{5,6},{6,5},{7,4},{8,11},{9,10},{10,... | collective-permute-start | bytes 196616 | tf_op jit(solution)/shard_map/ppermute | solution.py:576
  79.1 3.3 %collective-permute-done.25.refs_2_ = f32[128,128]{1,0:T(8,128)S(1)} collective-permute-done((f32[128,128]{1,0:T(8,128)S(1)}, f32[128,128]{1,0:T(8,128)S(1)}, u32[]{:S(2)}, u32[]{:S(2)}) %collective-permute-start.25) | collective-permute-done | bytes 65568 | tf_op jit(solution)/shard_map/ppermute | solution.py:576
  82.4 0.9 collective-permute-done.26.refs_3_
  83.4 1.5 %collective-permute-start.29 = (f32[128,128]{1,0:T(8,128)S(1)}, f32[128,128]{1,0:T(8,128)S(1)}, u32[]{:S(2)}, u32[]{:S(2)}) collective-permute-start(f32[128,128]{1,0:T(8,128)S(1)} %scale.3.refs_1_), channel_id=1, source_target_pairs={{0,8},{4,12},{8,0},{12,4},{1,9},{5,13},{9,1},{13,5},{2,10},{6,14},... | collective-permute-start | bytes 196616 | tf_op jit(solution)/shard_map/ppermute | solution.py:576
  84.9 1.2 %collective-permute-start.28 = (f32[128,128]{1,0:T(8,128)S(1)}, f32[128,128]{1,0:T(8,128)S(1)}, u32[]{:S(2)}, u32[]{:S(2)}) collective-permute-start(f32[128,128]{1,0:T(8,128)S(1)} %scale.3.refs_1_), channel_id=1, source_target_pairs={{0,24},{4,28},{8,16},{12,20},{16,8},{20,12},{24,0},{28,4},{1,25},{... | collective-permute-start | bytes 196616 | tf_op jit(solution)/shard_map/ppermute | solution.py:582
  86.2 0.8 collective-permute-start.33
  86.9 1.0 %join.1 = f32[8,96,256]{2,1,0:T(8,128)} custom-call(f32[8,96,128]{2,1,0:T(8,128)S(1)} %get-tuple-element.80.own.refs_0_, f32[4,96,128]{2,1,0:T(8,128)S(1)} %collective-permute-done.27.front.refs_0_, f32[4,96,128]{2,1,0:T(8,128)S(1)} %collective-permute-done.30.back.refs_1_), custom_call_target="tpu_custom_call" | custom-call | flops 1000000 | bytes 2000000 | tf_op jit(solution)/shard_map/join/pallas_call | solution.py:525
  89.2 0.9 collective-permute-done.28.refs_3_
  90.1 0.7 collective-permute-done.33.refs_2_
  91.5 0.7 second_half.3.own
  92.2 1.5 %final.1 = f32[8,96,256]{2,1,0:T(8,128)} custom-call(f32[8,96,128]{2,1,0:T(8,128)S(1)} %second_half.3.own, f32[8,96,128]{2,1,0:T(8,128)S(1)} %first_half.5.other, bf16[8,2,192,512]{3,2,1,0:T(8,128)(2,1)S(1)} %get-tuple-element.46.vectors, f32[128,128]{1,0:T(8,128)S(1)} %collective-permute-done.34.refs_0_, f32[128,128]{1,0:T(8,128)S(1)} %collective-permute-done.35.refs_1_), custom_call_target="tpu_custom_call" | custom-call | flops 1000000000 | bytes 4000000 | tf_op jit(solution)/shard_map/final/pallas_call | solution.py:553
  (54 shorter events, 8.0 us)
Async XLA Ops:
  0.6 1.1 %copy-start = (f32[1,1,2,4,96,256]{5,4,3,2,1,0:T(8,128)S(1)}, f32[1,1,2,4,96,256]{5,4,3,2,1,0:T(8,128)}, u32[]{:S(2)}) copy-start(f32[1,1,2,4,96,256]{5,4,3,2,1,0:T(8,128)} %param.7) | copy-start | bytes 2359300
  2.0 6.4 %collective-permute-start = (f32[8,96,128]{2,1,0:T(8,128)S(1)}, f32[8,96,128]{2,1,0:T(8,128)S(1)}, u32[]{:S(2)}, u32[]{:S(2)}) collective-permute-start(f32[8,96,128]{2,1,0:T(8,128)S(1)} %get-tuple-element.45.x_ref.x), channel_id=1, source_target_pairs={{0,4},{4,0},{8,12},{12,8},{1,5},{5,1},{9,13},{13,9},{2,6},{6,2},{1... | collective-permute-start | bytes 1179656 | tf_op jit(solution)/shard_map/ppermute | solution.py:576
  2.6 18.8 %collective-permute-start.2 = (f32[4,96,128]{2,1,0:T(8,128)S(1)}, f32[4,96,128]{2,1,0:T(8,128)S(1)}, u32[]{:S(2)}, u32[]{:S(2)}) collective-permute-start(f32[4,96,128]{2,1,0:T(8,128)S(1)} %get-tuple-element.50), channel_id=1, source_target_pairs={{0,1},{1,2},{2,3},{3,0},{4,5},{5,6},{6,7},{7,4},{8,9},{9,10},{10,1... | collective-permute-start | bytes 589832 | tf_op jit(solution)/shard_map/ppermute | solution.py:571
  5.2 16.2 %collective-permute-start.3 = (f32[4,96,128]{2,1,0:T(8,128)S(1)}, f32[4,96,128]{2,1,0:T(8,128)S(1)}, u32[]{:S(2)}, u32[]{:S(2)}) collective-permute-start(f32[4,96,128]{2,1,0:T(8,128)S(1)} %get-tuple-element.50), channel_id=1, source_target_pairs={{0,3},{1,0},{2,1},{3,2},{4,7},{5,4},{6,5},{7,6},{8,11},{9,8},{10,9... | collective-permute-start | bytes 589832 | tf_op jit(solution)/shard_map/ppermute | solution.py:571
  7.3 14.6 %collective-permute-start.1 = (f32[8,96,128]{2,1,0:T(8,128)S(1)}, f32[8,96,128]{2,1,0:T(8,128)S(1)}, u32[]{:S(2)}, u32[]{:S(2)}) collective-permute-start(f32[8,96,128]{2,1,0:T(8,128)S(1)} %get-tuple-element.45.x_ref.x), channel_id=1, source_target_pairs={{0,12},{4,8},{8,4},{12,0},{1,13},{5,9},{9,5},{13,1},{2,14},{6,10},... | collective-permute-start | bytes 1179656 | tf_op jit(solution)/shard_map/ppermute | solution.py:589
  8.5 14.5 %collective-permute-start.4 = (f32[4,96,128]{2,1,0:T(8,128)S(1)}, f32[4,96,128]{2,1,0:T(8,128)S(1)}, u32[]{:S(2)}, u32[]{:S(2)}) collective-permute-start(f32[4,96,128]{2,1,0:T(8,128)S(1)} %get-tuple-element.56), channel_id=1, source_target_pairs={{0,1},{1,2},{2,3},{3,0},{4,5},{5,6},{6,7},{7,4},{8,9},{9,10},{10,1... | collective-permute-start | bytes 589832 | tf_op jit(solution)/shard_map/ppermute | solution.py:571
  8.5 16.3 %collective-permute-start.5 = (f32[4,96,128]{2,1,0:T(8,128)S(1)}, f32[4,96,128]{2,1,0:T(8,128)S(1)}, u32[]{:S(2)}, u32[]{:S(2)}) collective-permute-start(f32[4,96,128]{2,1,0:T(8,128)S(1)} %get-tuple-element.56), channel_id=1, source_target_pairs={{0,3},{1,0},{2,1},{3,2},{4,7},{5,4},{6,5},{7,6},{8,11},{9,8},{10,9... | collective-permute-start | bytes 589832 | tf_op jit(solution)/shard_map/ppermute | solution.py:571
  24.8 6.8 %copy-start.1 = (f32[2,512]{1,0:T(2,128)S(1)}, f32[2,512]{1,0:T(2,128)}, u32[]{:S(2)}) copy-start(f32[2,512]{1,0:T(2,128)} %inverse.1) | copy-start | bytes 12292
  25.8 1.3 %collective-permute-start.6 = (f32[256,128]{1,0:T(8,128)S(1)}, f32[256,128]{1,0:T(8,128)S(1)}, u32[]{:S(2)}, u32[]{:S(2)}) collective-permute-start(f32[256,128]{1,0:T(8,128)S(1)} %get-tuple-element.59), channel_id=1, source_target_pairs={{0,4},{4,0},{8,12},{12,8},{1,5},{5,1},{9,13},{13,9},{2,6},{6,2},{1... | collective-permute-start | bytes 393224 | tf_op jit(solution)/shard_map/ppermute | solution.py:576
  27.2 4.6 %collective-permute-start.7 = (f32[128,128]{1,0:T(8,128)S(1)}, f32[128,128]{1,0:T(8,128)S(1)}, u32[]{:S(2)}, u32[]{:S(2)}) collective-permute-start(f32[128,128]{1,0:T(8,128)S(1)} %get-tuple-element.61), channel_id=1, source_target_pairs={{0,8},{4,12},{8,0},{12,4},{1,9},{5,13},{9,1},{13,5},{2,10},{6,14},... | collective-permute-start | bytes 196616 | tf_op jit(solution)/shard_map/ppermute | solution.py:576
  28.7 8.2 %collective-permute-start.8 = (f32[128,128]{1,0:T(8,128)S(1)}, f32[128,128]{1,0:T(8,128)S(1)}, u32[]{:S(2)}, u32[]{:S(2)}) collective-permute-start(f32[128,128]{1,0:T(8,128)S(1)} %get-tuple-element.60.refs_0_), channel_id=1, source_target_pairs={{0,2},{1,3},{2,0},{3,1},{4,6},{5,7},{6,4},{7,5},{8,10},{9,11},{10,... | collective-permute-start | bytes 196616 | tf_op jit(solution)/shard_map/ppermute | solution.py:576
  30.0 7.7 %collective-permute-start.9 = (f32[128,128]{1,0:T(8,128)S(1)}, f32[128,128]{1,0:T(8,128)S(1)}, u32[]{:S(2)}, u32[]{:S(2)}) collective-permute-start(f32[128,128]{1,0:T(8,128)S(1)} %get-tuple-element.61), channel_id=1, source_target_pairs={{0,10},{1,11},{2,8},{3,9},{4,14},{5,15},{6,12},{7,13},{8,2},{9,3},... | collective-permute-start | bytes 196616 | tf_op jit(solution)/shard_map/ppermute | solution.py:582
  37.8 5.0 %collective-permute-start.11 = (f32[128,128]{1,0:T(8,128)S(1)}, f32[128,128]{1,0:T(8,128)S(1)}, u32[]{:S(2)}, u32[]{:S(2)}) collective-permute-start(f32[128,128]{1,0:T(8,128)S(1)} %scale.2.left), channel_id=1, source_target_pairs={{0,8},{4,12},{8,0},{12,4},{1,9},{5,13},{9,1},{13,5},{2,10},{6,14},... | collective-permute-start | bytes 196616 | tf_op jit(solution)/shard_map/ppermute | solution.py:576
  39.4 5.2 %collective-permute-start.12 = (f32[128,128]{1,0:T(8,128)S(1)}, f32[128,128]{1,0:T(8,128)S(1)}, u32[]{:S(2)}, u32[]{:S(2)}) collective-permute-start(f32[128,128]{1,0:T(8,128)S(1)} %scale.2.left), channel_id=1, source_target_pairs={{0,9},{1,8},{2,11},{3,10},{4,13},{5,12},{6,15},{7,14},{8,1},{9,0},... | collective-permute-start | bytes 196616 | tf_op jit(solution)/shard_map/ppermute | solution.py:582
  39.8 4.8 %collective-permute-start.10 = (f32[128,128]{1,0:T(8,128)S(1)}, f32[128,128]{1,0:T(8,128)S(1)}, u32[]{:S(2)}, u32[]{:S(2)}) collective-permute-start(f32[128,128]{1,0:T(8,128)S(1)} %scale.2.left), channel_id=1, source_target_pairs={{0,1},{1,0},{2,3},{3,2},{4,5},{5,4},{6,7},{7,6},{8,9},{9,8},{10,11... | collective-permute-start | bytes 196616 | tf_op jit(solution)/shard_map/ppermute | solution.py:576
  44.5 1.3 %collective-permute-start.14 = (f32[128,128]{1,0:T(8,128)S(1)}, f32[128,128]{1,0:T(8,128)S(1)}, u32[]{:S(2)}, u32[]{:S(2)}) collective-permute-start(f32[128,128]{1,0:T(8,128)S(1)} %add.4.refs_2_), channel_id=1, source_target_pairs={{0,4},{4,0},{8,12},{12,8},{1,5},{5,1},{9,13},{13,9},{2,6},{6,2},{1... | collective-permute-start | bytes 196616 | tf_op jit(solution)/shard_map/ppermute | solution.py:576
  44.6 1.5 %collective-permute-start.13 = (f32[128,128]{1,0:T(8,128)S(1)}, f32[128,128]{1,0:T(8,128)S(1)}, u32[]{:S(2)}, u32[]{:S(2)}) collective-permute-start(f32[128,128]{1,0:T(8,128)S(1)} %add.3.refs_1_), channel_id=1, source_target_pairs={{0,4},{4,0},{8,12},{12,8},{1,5},{5,1},{9,13},{13,9},{2,6},{6,2},{1... | collective-permute-start | bytes 196616 | tf_op jit(solution)/shard_map/ppermute | solution.py:576
  46.8 4.5 %collective-permute-start.15 = (f32[8,96,128]{2,1,0:T(8,128)S(1)}, f32[8,96,128]{2,1,0:T(8,128)S(1)}, u32[]{:S(2)}, u32[]{:S(2)}) collective-permute-start(f32[8,96,128]{2,1,0:T(8,128)S(1)} %get-tuple-element.77.x_ref.x), channel_id=1, source_target_pairs={{0,4},{4,0},{8,12},{12,8},{1,5},{5,1},{9,13},{13,9},{2,6},{6,2},{1... | collective-permute-start | bytes 1179656 | tf_op jit(solution)/shard_map/ppermute | solution.py:576
  47.2 9.6 %collective-permute-start.17 = (f32[4,96,128]{2,1,0:T(8,128)S(1)}, f32[4,96,128]{2,1,0:T(8,128)S(1)}, u32[]{:S(2)}, u32[]{:S(2)}) collective-permute-start(f32[4,96,128]{2,1,0:T(8,128)S(1)} %get-tuple-element.68), channel_id=1, source_target_pairs={{0,1},{1,2},{2,3},{3,0},{4,5},{5,6},{6,7},{7,4},{8,9},{9,10},{10,1... | collective-permute-start | bytes 589832 | tf_op jit(solution)/shard_map/ppermute | solution.py:571
  47.8 12.3 %collective-permute-start.18 = (f32[4,96,128]{2,1,0:T(8,128)S(1)}, f32[4,96,128]{2,1,0:T(8,128)S(1)}, u32[]{:S(2)}, u32[]{:S(2)}) collective-permute-start(f32[4,96,128]{2,1,0:T(8,128)S(1)} %get-tuple-element.68), channel_id=1, source_target_pairs={{0,3},{1,0},{2,1},{3,2},{4,7},{5,4},{6,5},{7,6},{8,11},{9,8},{10,9... | collective-permute-start | bytes 589832 | tf_op jit(solution)/shard_map/ppermute | solution.py:571
  51.0 11.2 %collective-permute-start.16 = (f32[8,96,128]{2,1,0:T(8,128)S(1)}, f32[8,96,128]{2,1,0:T(8,128)S(1)}, u32[]{:S(2)}, u32[]{:S(2)}) collective-permute-start(f32[8,96,128]{2,1,0:T(8,128)S(1)} %get-tuple-element.77.x_ref.x), channel_id=1, source_target_pairs={{0,12},{4,8},{8,4},{12,0},{1,13},{5,9},{9,5},{13,1},{2,14},{6,10},... | collective-permute-start | bytes 1179656 | tf_op jit(solution)/shard_map/ppermute | solution.py:589
  51.2 14.0 %collective-permute-start.19 = (f32[4,96,128]{2,1,0:T(8,128)S(1)}, f32[4,96,128]{2,1,0:T(8,128)S(1)}, u32[]{:S(2)}, u32[]{:S(2)}) collective-permute-start(f32[4,96,128]{2,1,0:T(8,128)S(1)} %get-tuple-element.72), channel_id=1, source_target_pairs={{0,1},{1,2},{2,3},{3,0},{4,5},{5,6},{6,7},{7,4},{8,9},{9,10},{10,1... | collective-permute-start | bytes 589832 | tf_op jit(solution)/shard_map/ppermute | solution.py:571
  51.2 16.1 %collective-permute-start.20 = (f32[4,96,128]{2,1,0:T(8,128)S(1)}, f32[4,96,128]{2,1,0:T(8,128)S(1)}, u32[]{:S(2)}, u32[]{:S(2)}) collective-permute-start(f32[4,96,128]{2,1,0:T(8,128)S(1)} %get-tuple-element.72), channel_id=1, source_target_pairs={{0,3},{1,0},{2,1},{3,2},{4,7},{5,4},{6,5},{7,6},{8,11},{9,8},{10,9... | collective-permute-start | bytes 589832 | tf_op jit(solution)/shard_map/ppermute | solution.py:571
  56.8 17.6 %collective-permute-start.23 = (f32[8,96,128]{2,1,0:T(8,128)S(1)}, f32[8,96,128]{2,1,0:T(8,128)S(1)}, u32[]{:S(2)}, u32[]{:S(2)}) collective-permute-start(f32[8,96,128]{2,1,0:T(8,128)S(1)} %get-tuple-element.77.x_ref.x), channel_id=1, source_target_pairs={{0,16},{16,0},{1,17},{17,1},{2,18},{18,2},{3,19},{19,3},{4,20},{20... | collective-permute-start | bytes 1179656 | tf_op jit(solution)/shard_map/ppermute | solution.py:576
  68.3 1.7 %collective-permute-start.21 = (f32[256,128]{1,0:T(8,128)S(1)}, f32[256,128]{1,0:T(8,128)S(1)}, u32[]{:S(2)}, u32[]{:S(2)}) collective-permute-start(f32[256,128]{1,0:T(8,128)S(1)} %get-tuple-element.74), channel_id=1, source_target_pairs={{0,4},{4,0},{8,12},{12,8},{1,5},{5,1},{9,13},{13,9},{2,6},{6,2},{1... | collective-permute-start | bytes 393224 | tf_op jit(solution)/shard_map/ppermute | solution.py:576
  68.4 15.0 %collective-permute-start.27 = (f32[4,96,128]{2,1,0:T(8,128)S(1)}, f32[4,96,128]{2,1,0:T(8,128)S(1)}, u32[]{:S(2)}, u32[]{:S(2)}) collective-permute-start(f32[4,96,128]{2,1,0:T(8,128)S(1)} %get-tuple-element.69.front), channel_id=1, source_target_pairs={{0,16},{16,0},{1,17},{17,1},{2,18},{18,2},{3,19},{19,3},{4,20},{20... | collective-permute-start | bytes 589832 | tf_op jit(solution)/shard_map/ppermute | solution.py:576
  70.0 4.3 %collective-permute-start.22 = (f32[128,128]{1,0:T(8,128)S(1)}, f32[128,128]{1,0:T(8,128)S(1)}, u32[]{:S(2)}, u32[]{:S(2)}) collective-permute-start(f32[128,128]{1,0:T(8,128)S(1)} %get-tuple-element.76), channel_id=1, source_target_pairs={{0,8},{4,12},{8,0},{12,4},{1,9},{5,13},{9,1},{13,5},{2,10},{6,14},... | collective-permute-start | bytes 196616 | tf_op jit(solution)/shard_map/ppermute | solution.py:576
  71.5 15.4 %collective-permute-start.30 = (f32[4,96,128]{2,1,0:T(8,128)S(1)}, f32[4,96,128]{2,1,0:T(8,128)S(1)}, u32[]{:S(2)}, u32[]{:S(2)}) collective-permute-start(f32[4,96,128]{2,1,0:T(8,128)S(1)} %get-tuple-element.82), channel_id=1, source_target_pairs={{0,16},{16,0},{1,17},{17,1},{2,18},{18,2},{3,19},{19,3},{4,20},{20... | collective-permute-start | bytes 589832 | tf_op jit(solution)/shard_map/ppermute | solution.py:576
  74.4 4.7 %collective-permute-start.24 = (f32[128,128]{1,0:T(8,128)S(1)}, f32[128,128]{1,0:T(8,128)S(1)}, u32[]{:S(2)}, u32[]{:S(2)}) collective-permute-start(f32[128,128]{1,0:T(8,128)S(1)} %add.5.refs_0_), channel_id=1, source_target_pairs={{0,1},{1,0},{2,3},{3,2},{4,5},{5,4},{6,7},{7,6},{8,9},{9,8},{10,11... | collective-permute-start | bytes 196616 | tf_op jit(solution)/shard_map/ppermute | solution.py:576
  75.6 6.7 %collective-permute-start.25 = (f32[128,128]{1,0:T(8,128)S(1)}, f32[128,128]{1,0:T(8,128)S(1)}, u32[]{:S(2)}, u32[]{:S(2)}) collective-permute-start(f32[128,128]{1,0:T(8,128)S(1)} %add.5.refs_0_), channel_id=1, source_target_pairs={{0,2},{1,3},{2,0},{3,1},{4,6},{5,7},{6,4},{7,5},{8,10},{9,11},{10,... | collective-permute-start | bytes 196616 | tf_op jit(solution)/shard_map/ppermute | solution.py:576
  77.1 6.2 %collective-permute-start.26 = (f32[128,128]{1,0:T(8,128)S(1)}, f32[128,128]{1,0:T(8,128)S(1)}, u32[]{:S(2)}, u32[]{:S(2)}) collective-permute-start(f32[128,128]{1,0:T(8,128)S(1)} %add.5.refs_0_), channel_id=1, source_target_pairs={{0,3},{1,2},{2,1},{3,0},{4,7},{5,6},{6,5},{7,4},{8,11},{9,10},{10,... | collective-permute-start | bytes 196616 | tf_op jit(solution)/shard_map/ppermute | solution.py:576
  83.4 4.6 %collective-permute-start.29 = (f32[128,128]{1,0:T(8,128)S(1)}, f32[128,128]{1,0:T(8,128)S(1)}, u32[]{:S(2)}, u32[]{:S(2)}) collective-permute-start(f32[128,128]{1,0:T(8,128)S(1)} %scale.3.refs_1_), channel_id=1, source_target_pairs={{0,8},{4,12},{8,0},{12,4},{1,9},{5,13},{9,1},{13,5},{2,10},{6,14},... | collective-permute-start | bytes 196616 | tf_op jit(solution)/shard_map/ppermute | solution.py:576
  84.9 5.2 %collective-permute-start.28 = (f32[128,128]{1,0:T(8,128)S(1)}, f32[128,128]{1,0:T(8,128)S(1)}, u32[]{:S(2)}, u32[]{:S(2)}) collective-permute-start(f32[128,128]{1,0:T(8,128)S(1)} %scale.3.refs_1_), channel_id=1, source_target_pairs={{0,24},{4,28},{8,16},{12,20},{16,8},{20,12},{24,0},{28,4},{1,25},{... | collective-permute-start | bytes 196616 | tf_op jit(solution)/shard_map/ppermute | solution.py:582
  86.2 4.6 %collective-permute-start.33 = (f32[128,128]{1,0:T(8,128)S(1)}, f32[128,128]{1,0:T(8,128)S(1)}, u32[]{:S(2)}, u32[]{:S(2)}) collective-permute-start(f32[128,128]{1,0:T(8,128)S(1)} %scale.3.refs_1_), channel_id=1, source_target_pairs={{0,16},{16,0},{1,17},{17,1},{2,18},{18,2},{3,19},{19,3},{4,20},{20... | collective-permute-start | bytes 196616 | tf_op jit(solution)/shard_map/ppermute | solution.py:576
  86.9 4.5 %collective-permute-start.31 = (f32[128,128]{1,0:T(8,128)S(1)}, f32[128,128]{1,0:T(8,128)S(1)}, u32[]{:S(2)}, u32[]{:S(2)}) collective-permute-start(f32[128,128]{1,0:T(8,128)S(1)} %scale.3.refs_1_), channel_id=1, source_target_pairs={{0,4},{4,0},{8,12},{12,8},{1,5},{5,1},{9,13},{13,9},{2,6},{6,2},{1... | collective-permute-start | bytes 196616 | tf_op jit(solution)/shard_map/ppermute | solution.py:576
  88.0 3.5 %collective-permute-start.32 = (f32[128,128]{1,0:T(8,128)S(1)}, f32[128,128]{1,0:T(8,128)S(1)}, u32[]{:S(2)}, u32[]{:S(2)}) collective-permute-start(f32[128,128]{1,0:T(8,128)S(1)} %collective-permute-done.29.refs_2_), channel_id=1, source_target_pairs={{0,4},{4,0},{8,12},{12,8},{1,5},{5,1},{9,13},{13,9},{2,6},{6,2},{1... | collective-permute-start | bytes 196616 | tf_op jit(solution)/shard_map/ppermute | solution.py:576
  90.1 2.0 %collective-permute-start.35 = (f32[128,128]{1,0:T(8,128)S(1)}, f32[128,128]{1,0:T(8,128)S(1)}, u32[]{:S(2)}, u32[]{:S(2)}) collective-permute-start(f32[128,128]{1,0:T(8,128)S(1)} %collective-permute-done.28.refs_3_), channel_id=1, source_target_pairs={{0,4},{4,0},{8,12},{12,8},{1,5},{5,1},{9,13},{13,9},{2,6},{6,2},{1... | collective-permute-start | bytes 196616 | tf_op jit(solution)/shard_map/ppermute | solution.py:576
  90.8 1.4 %collective-permute-start.34 = (f32[128,128]{1,0:T(8,128)S(1)}, f32[128,128]{1,0:T(8,128)S(1)}, u32[]{:S(2)}, u32[]{:S(2)}) collective-permute-start(f32[128,128]{1,0:T(8,128)S(1)} %collective-permute-done.33.refs_2_), channel_id=1, source_target_pairs={{0,4},{4,0},{8,12},{12,8},{1,5},{5,1},{9,13},{13,9},{2,6},{6,2},{1... | collective-permute-start | bytes 196616 | tf_op jit(solution)/shard_map/ppermute | solution.py:576

commit v16 on v15

--- a/solution.py
+++ b/solution.py
@@ -419,7 +419,7 @@
     if blocks != 4 or slices != 4:
         return doubling([scale(eigen, over_time(halving(keep, send)))], blocks // 2)
     keep, send = add_split(keep, crossed(send, "space", 1))
-    parts = [crossed(send, "space", 2), crossed(keep, "tm", 2), crossed_both(send, "space", 2, "tm", 2)]
+    parts = [crossed_both(send, "space", 2, "tm", 2), crossed(keep, "tm", 2), crossed(send, "space", 2)]
     d = scale(eigen, [keep] + parts)
     moved, across = crossed(d, "space", 2), crossed_both(d, "space", 2, "tm", 1)
     return [add(d, crossed(d, "tm", 1)), add(moved, across)]

time: 94.1 us -> 93.4 us (level)
  starting transfers between devices: 41.8 us -> 40.5 us
    ppermute x3, waiting for transfers between devices: 3.29 us -> 6.14 us  [crossed_both(): return lax.ppermute(value, (first, second), pairs)]
    ppermute x23, waiting for transfers between devices: 14.9 us -> 12.3 us  [crossed(): return lax.ppermute(value, axis, [(i, i ^ mask) for i in range(count)])]
    ppermute x23, starting transfers between devices: 20.8 us -> 18.4 us  [crossed(): return lax.ppermute(value, axis, [(i, i ^ mask) for i in range(count)])]
    ppermute x8, waiting for transfers between devices: 7.53 us -> 8.7 us  [shifted(): lax.ppermute(value, axis, [(i, (i + step) % count) for i in range(count)])]
    ppermute x3, starting transfers between devices: 3.35 us -> 4.31 us  [crossed_both(): return lax.ppermute(value, (first, second), pairs)]
  transfers between devices with their start and end apart: 36 -> 36, of which waited for: 18 -> 19; matrix products, arithmetic and copies ran while one was open for 0% -> 0% of each run, Pallas kernels for 20% -> 20%
where the time goes in v16:
time: 93.4 us; the launch traced here: 93.3 us
  starting transfers between devices  40.5 us (43%)
  waiting for transfers between devices  28 us (30%)
  Pallas kernels  22.5 us (24%)
  local copies, waits for them, and re-layouts  1.13 us (1%)
  between operations  1.08 us (1%)
    ppermute x23, starting transfers between devices, crossed(): return lax.ppermute(value, axis, [(i, i ^ mask) for i in range(count)])  18.4 us
    ppermute x8, starting transfers between devices, shifted(): lax.ppermute(value, axis, [(i, (i + step) % count) for i in range(count)])  16.2 us
    ppermute x23, waiting for transfers between devices, crossed(): return lax.ppermute(value, axis, [(i, i ^ mask) for i in range(count)])  12.3 us
    pallas_call x1, Pallas kernels, prepare(): pl.pallas_call(functools.partial(prepare_kernel, ny, nx), out_shape=(pltp...  9.08 us
    ppermute x8, waiting for transfers between devices, shifted(): lax.ppermute(value, axis, [(i, (i + step) % count) for i in range(count)])  8.7 us
    ppermute x3, waiting for transfers between devices, crossed_both(): return lax.ppermute(value, (first, second), pairs)  6.14 us
    ppermute x3, starting transfers between devices, crossed_both(): return lax.ppermute(value, (first, second), pairs)  4.31 us
    pallas_call x2, Pallas kernels, middle(): pl.pallas_call(middle_kernel, out_shape=(half, half, pltpu.VMEM((vectors....  2.15 us
  transfers between devices with their start and end apart: 36, of which 19 were waited for; matrix products, arithmetic and copies ran while one was open for 0% of the time, Pallas kernels for 20%

profile of v16, /device:TPU:0, one launch (start us, length us, event | category | flops | bytes accessed | tf_op | source)
XLA Modules:
  0.0 93.3 jit_solution(18350115985103972344)
XLA Ops:
  0.6 1.1 %copy-done = f32[1,1,2,4,96,256]{5,4,3,2,1,0:T(8,128)S(1)} copy-done((f32[1,1,2,4,96,256]{5,4,3,2,1,0:T(8,128)S(1)}, f32[1,1,2,4,96,256]{5,4,3,2,1,0:T(8,128)}, u32[]{:S(2)}) %copy-start) | copy-done | bytes 786456
  2.6 2.6 %collective-permute-start.2 = (f32[4,96,128]{2,1,0:T(8,128)S(1)}, f32[4,96,128]{2,1,0:T(8,128)S(1)}, u32[]{:S(2)}, u32[]{:S(2)}) collective-permute-start(f32[4,96,128]{2,1,0:T(8,128)S(1)} %get-tuple-element.50), channel_id=1, source_target_pairs={{0,1},{1,2},{2,3},{3,0},{4,5},{5,6},{6,7},{7,4},{8,9},{9,10},{10,1... | collective-permute-start | bytes 589832 | tf_op jit(solution)/shard_map/ppermute | solution.py:571
  5.2 2.1 %collective-permute-start.3 = (f32[4,96,128]{2,1,0:T(8,128)S(1)}, f32[4,96,128]{2,1,0:T(8,128)S(1)}, u32[]{:S(2)}, u32[]{:S(2)}) collective-permute-start(f32[4,96,128]{2,1,0:T(8,128)S(1)} %get-tuple-element.50), channel_id=1, source_target_pairs={{0,3},{1,0},{2,1},{3,2},{4,7},{5,4},{6,5},{7,6},{8,11},{9,8},{10,9... | collective-permute-start | bytes 589832 | tf_op jit(solution)/shard_map/ppermute | solution.py:571
  7.3 1.2 %collective-permute-start.1 = (f32[8,96,128]{2,1,0:T(8,128)S(1)}, f32[8,96,128]{2,1,0:T(8,128)S(1)}, u32[]{:S(2)}, u32[]{:S(2)}) collective-permute-start(f32[8,96,128]{2,1,0:T(8,128)S(1)} %get-tuple-element.45.x_ref.x), channel_id=1, source_target_pairs={{0,12},{4,8},{8,4},{12,0},{1,13},{5,9},{9,5},{13,1},{2,14},{6,10},... | collective-permute-start | bytes 1179656 | tf_op jit(solution)/shard_map/ppermute | solution.py:589
  8.5 3.8 %collective-permute-start.5 = (f32[4,96,128]{2,1,0:T(8,128)S(1)}, f32[4,96,128]{2,1,0:T(8,128)S(1)}, u32[]{:S(2)}, u32[]{:S(2)}) collective-permute-start(f32[4,96,128]{2,1,0:T(8,128)S(1)} %get-tuple-element.56), channel_id=1, source_target_pairs={{0,3},{1,0},{2,1},{3,2},{4,7},{5,4},{6,5},{7,6},{8,11},{9,8},{10,9... | collective-permute-start | bytes 589832 | tf_op jit(solution)/shard_map/ppermute | solution.py:571
  12.3 9.1 %prepare.1 = (f32[8,96,128]{2,1,0:T(8,128)S(1)}, f32[8,96,128]{2,1,0:T(8,128)S(1)}, bf16[5,8,192,192]{3,2,1,0:T(8,128)(2,1)S(1)}, bf16[4,8,192,192]{3,2,1,0:T(8,...) custom-call(f32[8,96,128]{2,1,0:T(8,128)S(1)} %get-tuple-element.45.x_ref.x, ...), custom_call_target="tpu_custom_call" | custom-call | flops 8000000000 | bytes 25000000 | tf_op jit(solution)/shard_map/prepare/pallas_call | solution.py:225
  21.9 1.1 %middle.2 = (f32[4,96,128]{2,1,0:T(8,128)S(1)}, f32[4,96,128]{2,1,0:T(8,128)S(1)}, f32[512,128]{1,0:T(8,128)S(1)}) custom-call(f32[8,96,128]{2,1,0:T(8,128)S(1)} %get-tuple-element.47.rest, f32[8,96,128]{2,1,0:T(8,128)S(1)} %collective-permute-done.near, f32[8,96,128]{2,1,0:T(8,128)S(1)} %collective-permute-done.1.far, f32[4,96,128]{2,1,0:T(8,128)S(1)} %front_faces.2.front, ...), custom_call_target="tpu_custom_call" | custom-call | flops 1000 | bytes 1000 | tf_op jit(solution)/shard_map/middle/pallas_call | solution.py:322
  23.3 1.5 %collective-permute-done.5.forward = f32[4,96,128]{2,1,0:T(8,128)S(1)} collective-permute-done((f32[4,96,128]{2,1,0:T(8,128)S(1)}, f32[4,96,128]{2,1,0:T(8,128)S(1)}, u32[]{:S(2)}, u32[]{:S(2)}) %collective-permute-start.5) | collective-permute-done | bytes 196640 | tf_op jit(solution)/shard_map/ppermute | solution.py:571
  24.8 1.0 %forward_face.2 = (f32[8,96,128]{2,1,0:T(8,128)S(1)}, f32[4,96,128]{2,1,0:T(8,128)}, f32[256,128]{1,0:T(8,128)S(1)}, f32[256,128]{1,0:T(8,128)S(1)}) custom-call(f32[4,96,128]{2,1,0:T(8,128)S(1)} %get-tuple-element.53.front, f32[512,128]{1,0:T(8,128)S(1)} %get-tuple-element.54.partial, f32[4,96,128]{2,1,0:T(8,128)S(1)} %backward_face.2.rest, ...), custom_call_target="tpu_custom_call" | custom-call | flops 2000000000 | bytes 8000000 | tf_op jit(solution)/shard_map/forward_face/pallas_call | solution.py:371
  25.8 1.3 %collective-permute-done.6.received = f32[256,128]{1,0:T(8,128)S(1)} collective-permute-done((f32[256,128]{1,0:T(8,128)S(1)}, f32[256,128]{1,0:T(8,128)S(1)}, u32[]{:S(2)}, u32[]{:S(2)}) %collective-permute-start.6) | collective-permute-done | bytes 131104 | tf_op jit(solution)/shard_map/ppermute | solution.py:576
  27.2 2.2 %collective-permute-start.7 = (f32[128,128]{1,0:T(8,128)S(1)}, f32[128,128]{1,0:T(8,128)S(1)}, u32[]{:S(2)}, u32[]{:S(2)}) collective-permute-start(f32[128,128]{1,0:T(8,128)S(1)} %get-tuple-element.61), channel_id=1, source_target_pairs={{0,10},{1,11},{2,8},{3,9},{4,14},{5,15},{6,12},{7,13},{8,2},{9,3},... | collective-permute-start | bytes 196616 | tf_op jit(solution)/shard_map/ppermute | solution.py:582
  29.4 1.7 %collective-permute-start.8 = (f32[128,128]{1,0:T(8,128)S(1)}, f32[128,128]{1,0:T(8,128)S(1)}, u32[]{:S(2)}, u32[]{:S(2)}) collective-permute-start(f32[128,128]{1,0:T(8,128)S(1)} %get-tuple-element.60.refs_0_), channel_id=1, source_target_pairs={{0,2},{1,3},{2,0},{3,1},{4,6},{5,7},{6,4},{7,5},{8,10},{9,11},{10,... | collective-permute-start | bytes 196616 | tf_op jit(solution)/shard_map/ppermute | solution.py:576
  31.8 4.9 %collective-permute-done.7.refs_1_ = f32[128,128]{1,0:T(8,128)S(1)} collective-permute-done((f32[128,128]{1,0:T(8,128)S(1)}, f32[128,128]{1,0:T(8,128)S(1)}, u32[]{:S(2)}, u32[]{:S(2)}) %collective-permute-start.7) | collective-permute-done | bytes 65568 | tf_op jit(solution)/shard_map/ppermute | solution.py:582
  36.6 0.8 collective-permute-done.8.refs_2_
  37.5 0.8 collective-permute-start.11
  38.4 2.7 %collective-permute-start.10 = (f32[128,128]{1,0:T(8,128)S(1)}, f32[128,128]{1,0:T(8,128)S(1)}, u32[]{:S(2)}, u32[]{:S(2)}) collective-permute-start(f32[128,128]{1,0:T(8,128)S(1)} %scale.2.left), channel_id=1, source_target_pairs={{0,1},{1,0},{2,3},{3,2},{4,5},{5,4},{6,7},{7,6},{8,9},{9,8},{10,11... | collective-permute-start | bytes 196616 | tf_op jit(solution)/shard_map/ppermute | solution.py:576
  41.1 1.1 %collective-permute-done.11.left = f32[128,128]{1,0:T(8,128)S(1)} collective-permute-done((f32[128,128]{1,0:T(8,128)S(1)}, f32[128,128]{1,0:T(8,128)S(1)}, u32[]{:S(2)}, u32[]{:S(2)}) %collective-permute-start.11) | collective-permute-done | bytes 65568 | tf_op jit(solution)/shard_map/ppermute | solution.py:576
  42.2 1.2 %collective-permute-done.12.right = f32[128,128]{1,0:T(8,128)S(1)} collective-permute-done((f32[128,128]{1,0:T(8,128)S(1)}, f32[128,128]{1,0:T(8,128)S(1)}, u32[]{:S(2)}, u32[]{:S(2)}) %collective-permute-start.12) | collective-permute-done | bytes 65568 | tf_op jit(solution)/shard_map/ppermute | solution.py:582
  44.1 0.7 first_half.3.base
  45.4 0.7 second_half.2
  46.3 1.3 %collective-permute-start.17 = (f32[4,96,128]{2,1,0:T(8,128)S(1)}, f32[4,96,128]{2,1,0:T(8,128)S(1)}, u32[]{:S(2)}, u32[]{:S(2)}) collective-permute-start(f32[4,96,128]{2,1,0:T(8,128)S(1)} %get-tuple-element.68), channel_id=1, source_target_pairs={{0,1},{1,2},{2,3},{3,0},{4,5},{5,6},{6,7},{7,4},{8,9},{9,10},{10,1... | collective-permute-start | bytes 589832 | tf_op jit(solution)/shard_map/ppermute | solution.py:571
  47.6 2.5 %collective-permute-start.18 = (f32[4,96,128]{2,1,0:T(8,128)S(1)}, f32[4,96,128]{2,1,0:T(8,128)S(1)}, u32[]{:S(2)}, u32[]{:S(2)}) collective-permute-start(f32[4,96,128]{2,1,0:T(8,128)S(1)} %get-tuple-element.68), channel_id=1, source_target_pairs={{0,3},{1,0},{2,1},{3,2},{4,7},{5,4},{6,5},{7,6},{8,11},{9,8},{10,9... | collective-permute-start | bytes 589832 | tf_op jit(solution)/shard_map/ppermute | solution.py:571
  50.5 3.8 %collective-permute-start.20 = (f32[4,96,128]{2,1,0:T(8,128)S(1)}, f32[4,96,128]{2,1,0:T(8,128)S(1)}, u32[]{:S(2)}, u32[]{:S(2)}) collective-permute-start(f32[4,96,128]{2,1,0:T(8,128)S(1)} %get-tuple-element.72), channel_id=1, source_target_pairs={{0,3},{1,0},{2,1},{3,2},{4,7},{5,4},{6,5},{7,6},{8,11},{9,8},{10,9... | collective-permute-start | bytes 589832 | tf_op jit(solution)/shard_map/ppermute | solution.py:571
  54.3 1.3 %local_part.1.rest = f32[8,96,128]{2,1,0:T(8,128)S(1)} custom-call(f32[8,96,128]{2,1,0:T(8,128)S(1)} %get-tuple-element.77.x_ref.x, f32[8,96,128]{2,1,0:T(8,128)S(1)} %get-tuple-element.63.source, bf16[5,8,192,192]{3,2,1,0:T(8,128)(2,1)S(1)} %get-tuple-element.64.local), custom_call_target="tpu_custom_call" | custom-call | flops 8000000000 | bytes 8000000 | tf_op jit(solution)/shard_map/local_part/pallas_call | solution.py:142
  55.8 1.5 %collective-permute-start.23 = (f32[8,96,128]{2,1,0:T(8,128)S(1)}, f32[8,96,128]{2,1,0:T(8,128)S(1)}, u32[]{:S(2)}, u32[]{:S(2)}) collective-permute-start(f32[8,96,128]{2,1,0:T(8,128)S(1)} %get-tuple-element.77.x_ref.x), channel_id=1, source_target_pairs={{0,16},{16,0},{1,17},{17,1},{2,18},{18,2},{3,19},{19,3},{4,20},{20... | collective-permute-start | bytes 1179656 | tf_op jit(solution)/shard_map/ppermute | solution.py:576
  57.4 2.8 %collective-permute-done.18.forward = f32[4,96,128]{2,1,0:T(8,128)S(1)} collective-permute-done((f32[4,96,128]{2,1,0:T(8,128)S(1)}, f32[4,96,128]{2,1,0:T(8,128)S(1)}, u32[]{:S(2)}, u32[]{:S(2)}) %collective-permute-start.18) | collective-permute-done | bytes 196640 | tf_op jit(solution)/shard_map/ppermute | solution.py:571
  60.6 0.9 collective-permute-done.16.far
  61.5 1.1 %middle.3 = (f32[4,96,128]{2,1,0:T(8,128)S(1)}, f32[4,96,128]{2,1,0:T(8,128)S(1)}, f32[512,128]{1,0:T(8,128)S(1)}) custom-call(f32[8,96,128]{2,1,0:T(8,128)S(1)} %local_part.1.rest, f32[8,96,128]{2,1,0:T(8,128)S(1)} %collective-permute-done.15.near, f32[8,96,128]{2,1,0:T(8,128)S(1)} %collective-permute-done.16.far, f32[4,96,128]{2,1,0:T(8,128)S(1)} %front_faces.3.front, ...), custom_call_target="tpu_custom_call" | custom-call | flops 1000 | bytes 1000 | tf_op jit(solution)/shard_map/middle/pallas_call | solution.py:322
  62.6 1.8 %collective-permute-done.19.backward = f32[4,96,128]{2,1,0:T(8,128)S(1)} collective-permute-done((f32[4,96,128]{2,1,0:T(8,128)S(1)}, f32[4,96,128]{2,1,0:T(8,128)S(1)}, u32[]{:S(2)}, u32[]{:S(2)}) %collective-permute-start.19) | collective-permute-done | bytes 196640 | tf_op jit(solution)/shard_map/ppermute | solution.py:571
  64.7 2.4 %collective-permute-done.20.forward = f32[4,96,128]{2,1,0:T(8,128)S(1)} collective-permute-done((f32[4,96,128]{2,1,0:T(8,128)S(1)}, f32[4,96,128]{2,1,0:T(8,128)S(1)}, u32[]{:S(2)}, u32[]{:S(2)}) %collective-permute-start.20) | collective-permute-done | bytes 196640 | tf_op jit(solution)/shard_map/ppermute | solution.py:571
  67.1 0.9 %forward_face.3 = (f32[8,96,128]{2,1,0:T(8,128)S(1)}, f32[4,96,128]{2,1,0:T(8,128)S(1)}, f32[256,128]{1,0:T(8,128)S(1)}, f32[256,128]{1,0:T(8,128)S(1)}) custom-call(f32[4,96,128]{2,1,0:T(8,128)S(1)} %get-tuple-element.69.front, f32[512,128]{1,0:T(8,128)S(1)} %get-tuple-element.70.partial, f32[4,96,128]{2,1,0:T(8,128)S(1)} %backward_face.3.rest, ...), custom_call_target="tpu_custom_call" | custom-call | flops 2000000000 | bytes 8000000 | tf_op jit(solution)/shard_map/forward_face/pallas_call | solution.py:371
  68.1 1.6 %collective-permute-start.27 = (f32[4,96,128]{2,1,0:T(8,128)S(1)}, f32[4,96,128]{2,1,0:T(8,128)S(1)}, u32[]{:S(2)}, u32[]{:S(2)}) collective-permute-start(f32[4,96,128]{2,1,0:T(8,128)S(1)} %get-tuple-element.69.front), channel_id=1, source_target_pairs={{0,16},{16,0},{1,17},{17,1},{2,18},{18,2},{3,19},{19,3},{4,20},{20... | collective-permute-start | bytes 589832 | tf_op jit(solution)/shard_map/ppermute | solution.py:576
  69.8 0.7 collective-permute-start.22
  70.5 1.3 %collective-permute-start.30 = (f32[4,96,128]{2,1,0:T(8,128)S(1)}, f32[4,96,128]{2,1,0:T(8,128)S(1)}, u32[]{:S(2)}, u32[]{:S(2)}) collective-permute-start(f32[4,96,128]{2,1,0:T(8,128)S(1)} %get-tuple-element.82), channel_id=1, source_target_pairs={{0,16},{16,0},{1,17},{17,1},{2,18},{18,2},{3,19},{19,3},{4,20},{20... | collective-permute-start | bytes 589832 | tf_op jit(solution)/shard_map/ppermute | solution.py:576
  71.8 2.3 %collective-permute-done.22.right = f32[128,128]{1,0:T(8,128)S(1)} collective-permute-done((f32[128,128]{1,0:T(8,128)S(1)}, f32[128,128]{1,0:T(8,128)S(1)}, u32[]{:S(2)}, u32[]{:S(2)}) %collective-permute-start.22) | collective-permute-done | bytes 65568 | tf_op jit(solution)/shard_map/ppermute | solution.py:576
  74.1 1.3 %collective-permute-start.24 = (f32[128,128]{1,0:T(8,128)S(1)}, f32[128,128]{1,0:T(8,128)S(1)}, u32[]{:S(2)}, u32[]{:S(2)}) collective-permute-start(f32[128,128]{1,0:T(8,128)S(1)} %add.5.refs_0_), channel_id=1, source_target_pairs={{0,1},{1,0},{2,3},{3,2},{4,5},{5,4},{6,7},{7,6},{8,9},{9,8},{10,11... | collective-permute-start | bytes 196616 | tf_op jit(solution)/shard_map/ppermute | solution.py:576
  75.4 1.5 %collective-permute-start.25 = (f32[128,128]{1,0:T(8,128)S(1)}, f32[128,128]{1,0:T(8,128)S(1)}, u32[]{:S(2)}, u32[]{:S(2)}) collective-permute-start(f32[128,128]{1,0:T(8,128)S(1)} %add.5.refs_0_), channel_id=1, source_target_pairs={{0,2},{1,3},{2,0},{3,1},{4,6},{5,7},{6,4},{7,5},{8,10},{9,11},{10,... | collective-permute-start | bytes 196616 | tf_op jit(solution)/shard_map/ppermute | solution.py:576
  76.9 1.7 %collective-permute-start.26 = (f32[128,128]{1,0:T(8,128)S(1)}, f32[128,128]{1,0:T(8,128)S(1)}, u32[]{:S(2)}, u32[]{:S(2)}) collective-permute-start(f32[128,128]{1,0:T(8,128)S(1)} %add.5.refs_0_), channel_id=1, source_target_pairs={{0,3},{1,2},{2,1},{3,0},{4,7},{5,6},{6,5},{7,4},{8,11},{9,10},{10,... | collective-permute-start | bytes 196616 | tf_op jit(solution)/shard_map/ppermute | solution.py:576
  78.9 3.2 %collective-permute-done.25.refs_2_ = f32[128,128]{1,0:T(8,128)S(1)} collective-permute-done((f32[128,128]{1,0:T(8,128)S(1)}, f32[128,128]{1,0:T(8,128)S(1)}, u32[]{:S(2)}, u32[]{:S(2)}) %collective-permute-start.25) | collective-permute-done | bytes 65568 | tf_op jit(solution)/shard_map/ppermute | solution.py:576
  82.1 0.9 collective-permute-done.26.refs_3_
  83.1 0.7 collective-permute-start.29
  83.9 2.0 %collective-permute-start.28 = (f32[128,128]{1,0:T(8,128)S(1)}, f32[128,128]{1,0:T(8,128)S(1)}, u32[]{:S(2)}, u32[]{:S(2)}) collective-permute-start(f32[128,128]{1,0:T(8,128)S(1)} %scale.3.refs_1_), channel_id=1, source_target_pairs={{0,24},{4,28},{8,16},{12,20},{16,8},{20,12},{24,0},{28,4},{1,25},{... | collective-permute-start | bytes 196616 | tf_op jit(solution)/shard_map/ppermute | solution.py:582
  85.9 0.8 collective-permute-start.33
  86.7 1.0 %join.1 = f32[8,96,256]{2,1,0:T(8,128)} custom-call(f32[8,96,128]{2,1,0:T(8,128)S(1)} %get-tuple-element.80.own.refs_0_, f32[4,96,128]{2,1,0:T(8,128)S(1)} %collective-permute-done.27.front.refs_0_, f32[4,96,128]{2,1,0:T(8,128)S(1)} %collective-permute-done.30.back.refs_1_), custom_call_target="tpu_custom_call" | custom-call | flops 1000000 | bytes 2000000 | tf_op jit(solution)/shard_map/join/pallas_call | solution.py:525
  88.3 0.7 first_half.4.base
  89.1 1.1 %collective-permute-done.33.refs_2_ = f32[128,128]{1,0:T(8,128)S(1)} collective-permute-done((f32[128,128]{1,0:T(8,128)S(1)}, f32[128,128]{1,0:T(8,128)S(1)}, u32[]{:S(2)}, u32[]{:S(2)}) %collective-permute-start.33) | collective-permute-done | bytes 65568 | tf_op jit(solution)/shard_map/ppermute | solution.py:576
  90.2 0.7 first_half.5.other
  91.6 1.5 %final.1 = f32[8,96,256]{2,1,0:T(8,128)} custom-call(f32[8,96,128]{2,1,0:T(8,128)S(1)} %second_half.3.own, f32[8,96,128]{2,1,0:T(8,128)S(1)} %first_half.5.other, bf16[8,2,192,512]{3,2,1,0:T(8,128)(2,1)S(1)} %get-tuple-element.46.vectors, f32[128,128]{1,0:T(8,128)S(1)} %collective-permute-done.34.refs_0_, f32[128,128]{1,0:T(8,128)S(1)} %collective-permute-done.35.refs_1_), custom_call_target="tpu_custom_call" | custom-call | flops 1000000000 | bytes 4000000 | tf_op jit(solution)/shard_map/final/pallas_call | solution.py:553
  (54 shorter events, 7.2 us)
Async XLA Ops:
  0.6 1.1 %copy-start = (f32[1,1,2,4,96,256]{5,4,3,2,1,0:T(8,128)S(1)}, f32[1,1,2,4,96,256]{5,4,3,2,1,0:T(8,128)}, u32[]{:S(2)}) copy-start(f32[1,1,2,4,96,256]{5,4,3,2,1,0:T(8,128)} %param.7) | copy-start | bytes 2359300
  2.0 6.4 %collective-permute-start = (f32[8,96,128]{2,1,0:T(8,128)S(1)}, f32[8,96,128]{2,1,0:T(8,128)S(1)}, u32[]{:S(2)}, u32[]{:S(2)}) collective-permute-start(f32[8,96,128]{2,1,0:T(8,128)S(1)} %get-tuple-element.45.x_ref.x), channel_id=1, source_target_pairs={{0,4},{4,0},{8,12},{12,8},{1,5},{5,1},{9,13},{13,9},{2,6},{6,2},{1... | collective-permute-start | bytes 1179656 | tf_op jit(solution)/shard_map/ppermute | solution.py:576
  2.6 18.8 %collective-permute-start.2 = (f32[4,96,128]{2,1,0:T(8,128)S(1)}, f32[4,96,128]{2,1,0:T(8,128)S(1)}, u32[]{:S(2)}, u32[]{:S(2)}) collective-permute-start(f32[4,96,128]{2,1,0:T(8,128)S(1)} %get-tuple-element.50), channel_id=1, source_target_pairs={{0,1},{1,2},{2,3},{3,0},{4,5},{5,6},{6,7},{7,4},{8,9},{9,10},{10,1... | collective-permute-start | bytes 589832 | tf_op jit(solution)/shard_map/ppermute | solution.py:571
  5.2 16.2 %collective-permute-start.3 = (f32[4,96,128]{2,1,0:T(8,128)S(1)}, f32[4,96,128]{2,1,0:T(8,128)S(1)}, u32[]{:S(2)}, u32[]{:S(2)}) collective-permute-start(f32[4,96,128]{2,1,0:T(8,128)S(1)} %get-tuple-element.50), channel_id=1, source_target_pairs={{0,3},{1,0},{2,1},{3,2},{4,7},{5,4},{6,5},{7,6},{8,11},{9,8},{10,9... | collective-permute-start | bytes 589832 | tf_op jit(solution)/shard_map/ppermute | solution.py:571
  7.3 14.6 %collective-permute-start.1 = (f32[8,96,128]{2,1,0:T(8,128)S(1)}, f32[8,96,128]{2,1,0:T(8,128)S(1)}, u32[]{:S(2)}, u32[]{:S(2)}) collective-permute-start(f32[8,96,128]{2,1,0:T(8,128)S(1)} %get-tuple-element.45.x_ref.x), channel_id=1, source_target_pairs={{0,12},{4,8},{8,4},{12,0},{1,13},{5,9},{9,5},{13,1},{2,14},{6,10},... | collective-permute-start | bytes 1179656 | tf_op jit(solution)/shard_map/ppermute | solution.py:589
  8.5 14.5 %collective-permute-start.4 = (f32[4,96,128]{2,1,0:T(8,128)S(1)}, f32[4,96,128]{2,1,0:T(8,128)S(1)}, u32[]{:S(2)}, u32[]{:S(2)}) collective-permute-start(f32[4,96,128]{2,1,0:T(8,128)S(1)} %get-tuple-element.56), channel_id=1, source_target_pairs={{0,1},{1,2},{2,3},{3,0},{4,5},{5,6},{6,7},{7,4},{8,9},{9,10},{10,1... | collective-permute-start | bytes 589832 | tf_op jit(solution)/shard_map/ppermute | solution.py:571
  8.5 16.3 %collective-permute-start.5 = (f32[4,96,128]{2,1,0:T(8,128)S(1)}, f32[4,96,128]{2,1,0:T(8,128)S(1)}, u32[]{:S(2)}, u32[]{:S(2)}) collective-permute-start(f32[4,96,128]{2,1,0:T(8,128)S(1)} %get-tuple-element.56), channel_id=1, source_target_pairs={{0,3},{1,0},{2,1},{3,2},{4,7},{5,4},{6,5},{7,6},{8,11},{9,8},{10,9... | collective-permute-start | bytes 589832 | tf_op jit(solution)/shard_map/ppermute | solution.py:571
  24.8 6.8 %copy-start.1 = (f32[2,512]{1,0:T(2,128)S(1)}, f32[2,512]{1,0:T(2,128)}, u32[]{:S(2)}) copy-start(f32[2,512]{1,0:T(2,128)} %inverse.1) | copy-start | bytes 12292
  25.8 1.3 %collective-permute-start.6 = (f32[256,128]{1,0:T(8,128)S(1)}, f32[256,128]{1,0:T(8,128)S(1)}, u32[]{:S(2)}, u32[]{:S(2)}) collective-permute-start(f32[256,128]{1,0:T(8,128)S(1)} %get-tuple-element.59), channel_id=1, source_target_pairs={{0,4},{4,0},{8,12},{12,8},{1,5},{5,1},{9,13},{13,9},{2,6},{6,2},{1... | collective-permute-start | bytes 393224 | tf_op jit(solution)/shard_map/ppermute | solution.py:576
  27.2 9.4 %collective-permute-start.7 = (f32[128,128]{1,0:T(8,128)S(1)}, f32[128,128]{1,0:T(8,128)S(1)}, u32[]{:S(2)}, u32[]{:S(2)}) collective-permute-start(f32[128,128]{1,0:T(8,128)S(1)} %get-tuple-element.61), channel_id=1, source_target_pairs={{0,10},{1,11},{2,8},{3,9},{4,14},{5,15},{6,12},{7,13},{8,2},{9,3},... | collective-permute-start | bytes 196616 | tf_op jit(solution)/shard_map/ppermute | solution.py:582
  29.4 8.0 %collective-permute-start.8 = (f32[128,128]{1,0:T(8,128)S(1)}, f32[128,128]{1,0:T(8,128)S(1)}, u32[]{:S(2)}, u32[]{:S(2)}) collective-permute-start(f32[128,128]{1,0:T(8,128)S(1)} %get-tuple-element.60.refs_0_), channel_id=1, source_target_pairs={{0,2},{1,3},{2,0},{3,1},{4,6},{5,7},{6,4},{7,5},{8,10},{9,11},{10,... | collective-permute-start | bytes 196616 | tf_op jit(solution)/shard_map/ppermute | solution.py:576
  31.1 6.3 %collective-permute-start.9 = (f32[128,128]{1,0:T(8,128)S(1)}, f32[128,128]{1,0:T(8,128)S(1)}, u32[]{:S(2)}, u32[]{:S(2)}) collective-permute-start(f32[128,128]{1,0:T(8,128)S(1)} %get-tuple-element.61), channel_id=1, source_target_pairs={{0,8},{4,12},{8,0},{12,4},{1,9},{5,13},{9,1},{13,5},{2,10},{6,14},... | collective-permute-start | bytes 196616 | tf_op jit(solution)/shard_map/ppermute | solution.py:576
  37.5 4.7 %collective-permute-start.11 = (f32[128,128]{1,0:T(8,128)S(1)}, f32[128,128]{1,0:T(8,128)S(1)}, u32[]{:S(2)}, u32[]{:S(2)}) collective-permute-start(f32[128,128]{1,0:T(8,128)S(1)} %scale.2.left), channel_id=1, source_target_pairs={{0,8},{4,12},{8,0},{12,4},{1,9},{5,13},{9,1},{13,5},{2,10},{6,14},... | collective-permute-start | bytes 196616 | tf_op jit(solution)/shard_map/ppermute | solution.py:576
  38.3 5.2 %collective-permute-start.12 = (f32[128,128]{1,0:T(8,128)S(1)}, f32[128,128]{1,0:T(8,128)S(1)}, u32[]{:S(2)}, u32[]{:S(2)}) collective-permute-start(f32[128,128]{1,0:T(8,128)S(1)} %scale.2.left), channel_id=1, source_target_pairs={{0,9},{1,8},{2,11},{3,10},{4,13},{5,12},{6,15},{7,14},{8,1},{9,0},... | collective-permute-start | bytes 196616 | tf_op jit(solution)/shard_map/ppermute | solution.py:582
  38.4 5.7 %collective-permute-start.10 = (f32[128,128]{1,0:T(8,128)S(1)}, f32[128,128]{1,0:T(8,128)S(1)}, u32[]{:S(2)}, u32[]{:S(2)}) collective-permute-start(f32[128,128]{1,0:T(8,128)S(1)} %scale.2.left), channel_id=1, source_target_pairs={{0,1},{1,0},{2,3},{3,2},{4,5},{5,4},{6,7},{7,6},{8,9},{9,8},{10,11... | collective-permute-start | bytes 196616 | tf_op jit(solution)/shard_map/ppermute | solution.py:576
  43.5 1.3 %collective-permute-start.14 = (f32[128,128]{1,0:T(8,128)S(1)}, f32[128,128]{1,0:T(8,128)S(1)}, u32[]{:S(2)}, u32[]{:S(2)}) collective-permute-start(f32[128,128]{1,0:T(8,128)S(1)} %add.4.refs_2_), channel_id=1, source_target_pairs={{0,4},{4,0},{8,12},{12,8},{1,5},{5,1},{9,13},{13,9},{2,6},{6,2},{1... | collective-permute-start | bytes 196616 | tf_op jit(solution)/shard_map/ppermute | solution.py:576
  44.1 1.3 %collective-permute-start.13 = (f32[128,128]{1,0:T(8,128)S(1)}, f32[128,128]{1,0:T(8,128)S(1)}, u32[]{:S(2)}, u32[]{:S(2)}) collective-permute-start(f32[128,128]{1,0:T(8,128)S(1)} %add.3.refs_1_), channel_id=1, source_target_pairs={{0,4},{4,0},{8,12},{12,8},{1,5},{5,1},{9,13},{13,9},{2,6},{6,2},{1... | collective-permute-start | bytes 196616 | tf_op jit(solution)/shard_map/ppermute | solution.py:576
  46.0 4.4 %collective-permute-start.15 = (f32[8,96,128]{2,1,0:T(8,128)S(1)}, f32[8,96,128]{2,1,0:T(8,128)S(1)}, u32[]{:S(2)}, u32[]{:S(2)}) collective-permute-start(f32[8,96,128]{2,1,0:T(8,128)S(1)} %get-tuple-element.77.x_ref.x), channel_id=1, source_target_pairs={{0,4},{4,0},{8,12},{12,8},{1,5},{5,1},{9,13},{13,9},{2,6},{6,2},{1... | collective-permute-start | bytes 1179656 | tf_op jit(solution)/shard_map/ppermute | solution.py:576
  46.3 9.6 %collective-permute-start.17 = (f32[4,96,128]{2,1,0:T(8,128)S(1)}, f32[4,96,128]{2,1,0:T(8,128)S(1)}, u32[]{:S(2)}, u32[]{:S(2)}) collective-permute-start(f32[4,96,128]{2,1,0:T(8,128)S(1)} %get-tuple-element.68), channel_id=1, source_target_pairs={{0,1},{1,2},{2,3},{3,0},{4,5},{5,6},{6,7},{7,4},{8,9},{9,10},{10,1... | collective-permute-start | bytes 589832 | tf_op jit(solution)/shard_map/ppermute | solution.py:571
  47.6 12.5 %collective-permute-start.18 = (f32[4,96,128]{2,1,0:T(8,128)S(1)}, f32[4,96,128]{2,1,0:T(8,128)S(1)}, u32[]{:S(2)}, u32[]{:S(2)}) collective-permute-start(f32[4,96,128]{2,1,0:T(8,128)S(1)} %get-tuple-element.68), channel_id=1, source_target_pairs={{0,3},{1,0},{2,1},{3,2},{4,7},{5,4},{6,5},{7,6},{8,11},{9,8},{10,9... | collective-permute-start | bytes 589832 | tf_op jit(solution)/shard_map/ppermute | solution.py:571
  50.1 11.4 %collective-permute-start.16 = (f32[8,96,128]{2,1,0:T(8,128)S(1)}, f32[8,96,128]{2,1,0:T(8,128)S(1)}, u32[]{:S(2)}, u32[]{:S(2)}) collective-permute-start(f32[8,96,128]{2,1,0:T(8,128)S(1)} %get-tuple-element.77.x_ref.x), channel_id=1, source_target_pairs={{0,12},{4,8},{8,4},{12,0},{1,13},{5,9},{9,5},{13,1},{2,14},{6,10},... | collective-permute-start | bytes 1179656 | tf_op jit(solution)/shard_map/ppermute | solution.py:589
  50.5 13.8 %collective-permute-start.19 = (f32[4,96,128]{2,1,0:T(8,128)S(1)}, f32[4,96,128]{2,1,0:T(8,128)S(1)}, u32[]{:S(2)}, u32[]{:S(2)}) collective-permute-start(f32[4,96,128]{2,1,0:T(8,128)S(1)} %get-tuple-element.72), channel_id=1, source_target_pairs={{0,1},{1,2},{2,3},{3,0},{4,5},{5,6},{6,7},{7,4},{8,9},{9,10},{10,1... | collective-permute-start | bytes 589832 | tf_op jit(solution)/shard_map/ppermute | solution.py:571
  50.5 16.6 %collective-permute-start.20 = (f32[4,96,128]{2,1,0:T(8,128)S(1)}, f32[4,96,128]{2,1,0:T(8,128)S(1)}, u32[]{:S(2)}, u32[]{:S(2)}) collective-permute-start(f32[4,96,128]{2,1,0:T(8,128)S(1)} %get-tuple-element.72), channel_id=1, source_target_pairs={{0,3},{1,0},{2,1},{3,2},{4,7},{5,4},{6,5},{7,6},{8,11},{9,8},{10,9... | collective-permute-start | bytes 589832 | tf_op jit(solution)/shard_map/ppermute | solution.py:571
  55.8 18.3 %collective-permute-start.23 = (f32[8,96,128]{2,1,0:T(8,128)S(1)}, f32[8,96,128]{2,1,0:T(8,128)S(1)}, u32[]{:S(2)}, u32[]{:S(2)}) collective-permute-start(f32[8,96,128]{2,1,0:T(8,128)S(1)} %get-tuple-element.77.x_ref.x), channel_id=1, source_target_pairs={{0,16},{16,0},{1,17},{17,1},{2,18},{18,2},{3,19},{19,3},{4,20},{20... | collective-permute-start | bytes 1179656 | tf_op jit(solution)/shard_map/ppermute | solution.py:576
  68.1 1.7 %collective-permute-start.21 = (f32[256,128]{1,0:T(8,128)S(1)}, f32[256,128]{1,0:T(8,128)S(1)}, u32[]{:S(2)}, u32[]{:S(2)}) collective-permute-start(f32[256,128]{1,0:T(8,128)S(1)} %get-tuple-element.74), channel_id=1, source_target_pairs={{0,4},{4,0},{8,12},{12,8},{1,5},{5,1},{9,13},{13,9},{2,6},{6,2},{1... | collective-permute-start | bytes 393224 | tf_op jit(solution)/shard_map/ppermute | solution.py:576
  68.1 15.0 %collective-permute-start.27 = (f32[4,96,128]{2,1,0:T(8,128)S(1)}, f32[4,96,128]{2,1,0:T(8,128)S(1)}, u32[]{:S(2)}, u32[]{:S(2)}) collective-permute-start(f32[4,96,128]{2,1,0:T(8,128)S(1)} %get-tuple-element.69.front), channel_id=1, source_target_pairs={{0,16},{16,0},{1,17},{17,1},{2,18},{18,2},{3,19},{19,3},{4,20},{20... | collective-permute-start | bytes 589832 | tf_op jit(solution)/shard_map/ppermute | solution.py:576
  69.8 4.3 %collective-permute-start.22 = (f32[128,128]{1,0:T(8,128)S(1)}, f32[128,128]{1,0:T(8,128)S(1)}, u32[]{:S(2)}, u32[]{:S(2)}) collective-permute-start(f32[128,128]{1,0:T(8,128)S(1)} %get-tuple-element.76), channel_id=1, source_target_pairs={{0,8},{4,12},{8,0},{12,4},{1,9},{5,13},{9,1},{13,5},{2,10},{6,14},... | collective-permute-start | bytes 196616 | tf_op jit(solution)/shard_map/ppermute | solution.py:576
  70.5 16.2 %collective-permute-start.30 = (f32[4,96,128]{2,1,0:T(8,128)S(1)}, f32[4,96,128]{2,1,0:T(8,128)S(1)}, u32[]{:S(2)}, u32[]{:S(2)}) collective-permute-start(f32[4,96,128]{2,1,0:T(8,128)S(1)} %get-tuple-element.82), channel_id=1, source_target_pairs={{0,16},{16,0},{1,17},{17,1},{2,18},{18,2},{3,19},{19,3},{4,20},{20... | collective-permute-start | bytes 589832 | tf_op jit(solution)/shard_map/ppermute | solution.py:576
  74.1 4.8 %collective-permute-start.24 = (f32[128,128]{1,0:T(8,128)S(1)}, f32[128,128]{1,0:T(8,128)S(1)}, u32[]{:S(2)}, u32[]{:S(2)}) collective-permute-start(f32[128,128]{1,0:T(8,128)S(1)} %add.5.refs_0_), channel_id=1, source_target_pairs={{0,1},{1,0},{2,3},{3,2},{4,5},{5,4},{6,7},{7,6},{8,9},{9,8},{10,11... | collective-permute-start | bytes 196616 | tf_op jit(solution)/shard_map/ppermute | solution.py:576
  75.4 6.7 %collective-permute-start.25 = (f32[128,128]{1,0:T(8,128)S(1)}, f32[128,128]{1,0:T(8,128)S(1)}, u32[]{:S(2)}, u32[]{:S(2)}) collective-permute-start(f32[128,128]{1,0:T(8,128)S(1)} %add.5.refs_0_), channel_id=1, source_target_pairs={{0,2},{1,3},{2,0},{3,1},{4,6},{5,7},{6,4},{7,5},{8,10},{9,11},{10,... | collective-permute-start | bytes 196616 | tf_op jit(solution)/shard_map/ppermute | solution.py:576
  76.9 6.2 %collective-permute-start.26 = (f32[128,128]{1,0:T(8,128)S(1)}, f32[128,128]{1,0:T(8,128)S(1)}, u32[]{:S(2)}, u32[]{:S(2)}) collective-permute-start(f32[128,128]{1,0:T(8,128)S(1)} %add.5.refs_0_), channel_id=1, source_target_pairs={{0,3},{1,2},{2,1},{3,0},{4,7},{5,6},{6,5},{7,4},{8,11},{9,10},{10,... | collective-permute-start | bytes 196616 | tf_op jit(solution)/shard_map/ppermute | solution.py:576
  83.1 4.6 %collective-permute-start.29 = (f32[128,128]{1,0:T(8,128)S(1)}, f32[128,128]{1,0:T(8,128)S(1)}, u32[]{:S(2)}, u32[]{:S(2)}) collective-permute-start(f32[128,128]{1,0:T(8,128)S(1)} %scale.3.refs_1_), channel_id=1, source_target_pairs={{0,8},{4,12},{8,0},{12,4},{1,9},{5,13},{9,1},{13,5},{2,10},{6,14},... | collective-permute-start | bytes 196616 | tf_op jit(solution)/shard_map/ppermute | solution.py:576
  83.9 5.2 %collective-permute-start.28 = (f32[128,128]{1,0:T(8,128)S(1)}, f32[128,128]{1,0:T(8,128)S(1)}, u32[]{:S(2)}, u32[]{:S(2)}) collective-permute-start(f32[128,128]{1,0:T(8,128)S(1)} %scale.3.refs_1_), channel_id=1, source_target_pairs={{0,24},{4,28},{8,16},{12,20},{16,8},{20,12},{24,0},{28,4},{1,25},{... | collective-permute-start | bytes 196616 | tf_op jit(solution)/shard_map/ppermute | solution.py:582
  85.9 4.3 %collective-permute-start.33 = (f32[128,128]{1,0:T(8,128)S(1)}, f32[128,128]{1,0:T(8,128)S(1)}, u32[]{:S(2)}, u32[]{:S(2)}) collective-permute-start(f32[128,128]{1,0:T(8,128)S(1)} %scale.3.refs_1_), channel_id=1, source_target_pairs={{0,16},{16,0},{1,17},{17,1},{2,18},{18,2},{3,19},{19,3},{4,20},{20... | collective-permute-start | bytes 196616 | tf_op jit(solution)/shard_map/ppermute | solution.py:576
  86.7 4.2 %collective-permute-start.31 = (f32[128,128]{1,0:T(8,128)S(1)}, f32[128,128]{1,0:T(8,128)S(1)}, u32[]{:S(2)}, u32[]{:S(2)}) collective-permute-start(f32[128,128]{1,0:T(8,128)S(1)} %scale.3.refs_1_), channel_id=1, source_target_pairs={{0,4},{4,0},{8,12},{12,8},{1,5},{5,1},{9,13},{13,9},{2,6},{6,2},{1... | collective-permute-start | bytes 196616 | tf_op jit(solution)/shard_map/ppermute | solution.py:576
  87.8 3.1 %collective-permute-start.32 = (f32[128,128]{1,0:T(8,128)S(1)}, f32[128,128]{1,0:T(8,128)S(1)}, u32[]{:S(2)}, u32[]{:S(2)}) collective-permute-start(f32[128,128]{1,0:T(8,128)S(1)} %collective-permute-done.29.refs_2_), channel_id=1, source_target_pairs={{0,4},{4,0},{8,12},{12,8},{1,5},{5,1},{9,13},{13,9},{2,6},{6,2},{1... | collective-permute-start | bytes 196616 | tf_op jit(solution)/shard_map/ppermute | solution.py:576
  89.0 2.5 %collective-permute-start.35 = (f32[128,128]{1,0:T(8,128)S(1)}, f32[128,128]{1,0:T(8,128)S(1)}, u32[]{:S(2)}, u32[]{:S(2)}) collective-permute-start(f32[128,128]{1,0:T(8,128)S(1)} %collective-permute-done.28.refs_3_), channel_id=1, source_target_pairs={{0,4},{4,0},{8,12},{12,8},{1,5},{5,1},{9,13},{13,9},{2,6},{6,2},{1... | collective-permute-start | bytes 196616 | tf_op jit(solution)/shard_map/ppermute | solution.py:576
  90.2 1.4 %collective-permute-start.34 = (f32[128,128]{1,0:T(8,128)S(1)}, f32[128,128]{1,0:T(8,128)S(1)}, u32[]{:S(2)}, u32[]{:S(2)}) collective-permute-start(f32[128,128]{1,0:T(8,128)S(1)} %collective-permute-done.33.refs_2_), channel_id=1, source_target_pairs={{0,4},{4,0},{8,12},{12,8},{1,5},{5,1},{9,13},{13,9},{2,6},{6,2},{1... | collective-permute-start | bytes 196616 | tf_op jit(solution)/shard_map/ppermute | solution.py:576

commit v17 on v16

--- a/solution.py
+++ b/solution.py
@@ -622,7 +622,7 @@
 def over_time(part):
     count = lax.axis_size("tm")
     if count <= 4:
-        return [part] + [crossed(part, "tm", mask) for mask in range(1, count)]
+        return [part] + [crossed(part, "tm", mask) for mask in reversed(range(1, count))]
     mask = 1
     while mask < count:
         part = part + crossed(part, "tm", mask)

time: 93.4 us -> 93.2 us (level)
  transfers between devices with their start and end apart: 36 -> 36, of which waited for: 19 -> 18; matrix products, arithmetic and copies ran while one was open for 0% -> 0% of each run, Pallas kernels for 20% -> 20%
where the time goes in v17:
time: 93.2 us; the launch traced here: 93 us
  starting transfers between devices  40.5 us (43%)
  waiting for transfers between devices  27.8 us (30%)
  Pallas kernels  22.5 us (24%)
  local copies, waits for them, and re-layouts  1.13 us (1%)
  between operations  1.08 us (1%)
    ppermute x23, starting transfers between devices, crossed(): return lax.ppermute(value, axis, [(i, i ^ mask) for i in range(count)])  18.4 us
    ppermute x8, starting transfers between devices, shifted(): lax.ppermute(value, axis, [(i, (i + step) % count) for i in range(count)])  16.2 us
    ppermute x23, waiting for transfers between devices, crossed(): return lax.ppermute(value, axis, [(i, i ^ mask) for i in range(count)])  12 us
    pallas_call x1, Pallas kernels, prepare(): pl.pallas_call(functools.partial(prepare_kernel, ny, nx), out_shape=(pltp...  9.08 us
    ppermute x8, waiting for transfers between devices, shifted(): lax.ppermute(value, axis, [(i, (i + step) % count) for i in range(count)])  8.7 us
    ppermute x3, waiting for transfers between devices, crossed_both(): return lax.ppermute(value, (first, second), pairs)  6.14 us
    ppermute x3, starting transfers between devices, crossed_both(): return lax.ppermute(value, (first, second), pairs)  4.3 us
    pallas_call x2, Pallas kernels, middle(): pl.pallas_call(middle_kernel, out_shape=(half, half, pltpu.VMEM((vectors....  2.15 us
  transfers between devices with their start and end apart: 36, of which 18 were waited for; matrix products, arithmetic and copies ran while one was open for 0% of the time, Pallas kernels for 20%

profile of v17, /device:TPU:0, one launch (start us, length us, event | category | flops | bytes accessed | tf_op | source)
XLA Modules:
  0.0 93.0 jit_solution(13904178943333113073)
XLA Ops:
  0.6 1.1 %copy-done = f32[1,1,2,4,96,256]{5,4,3,2,1,0:T(8,128)S(1)} copy-done((f32[1,1,2,4,96,256]{5,4,3,2,1,0:T(8,128)S(1)}, f32[1,1,2,4,96,256]{5,4,3,2,1,0:T(8,128)}, u32[]{:S(2)}) %copy-start) | copy-done | bytes 786456
  2.6 2.6 %collective-permute-start.2 = (f32[4,96,128]{2,1,0:T(8,128)S(1)}, f32[4,96,128]{2,1,0:T(8,128)S(1)}, u32[]{:S(2)}, u32[]{:S(2)}) collective-permute-start(f32[4,96,128]{2,1,0:T(8,128)S(1)} %get-tuple-element.50), channel_id=1, source_target_pairs={{0,1},{1,2},{2,3},{3,0},{4,5},{5,6},{6,7},{7,4},{8,9},{9,10},{10,1... | collective-permute-start | bytes 589832 | tf_op jit(solution)/shard_map/ppermute | solution.py:571
  5.2 2.1 %collective-permute-start.3 = (f32[4,96,128]{2,1,0:T(8,128)S(1)}, f32[4,96,128]{2,1,0:T(8,128)S(1)}, u32[]{:S(2)}, u32[]{:S(2)}) collective-permute-start(f32[4,96,128]{2,1,0:T(8,128)S(1)} %get-tuple-element.50), channel_id=1, source_target_pairs={{0,3},{1,0},{2,1},{3,2},{4,7},{5,4},{6,5},{7,6},{8,11},{9,8},{10,9... | collective-permute-start | bytes 589832 | tf_op jit(solution)/shard_map/ppermute | solution.py:571
  7.3 1.2 %collective-permute-start.1 = (f32[8,96,128]{2,1,0:T(8,128)S(1)}, f32[8,96,128]{2,1,0:T(8,128)S(1)}, u32[]{:S(2)}, u32[]{:S(2)}) collective-permute-start(f32[8,96,128]{2,1,0:T(8,128)S(1)} %get-tuple-element.45.x_ref.x), channel_id=1, source_target_pairs={{0,12},{4,8},{8,4},{12,0},{1,13},{5,9},{9,5},{13,1},{2,14},{6,10},... | collective-permute-start | bytes 1179656 | tf_op jit(solution)/shard_map/ppermute | solution.py:589
  8.5 3.8 %collective-permute-start.5 = (f32[4,96,128]{2,1,0:T(8,128)S(1)}, f32[4,96,128]{2,1,0:T(8,128)S(1)}, u32[]{:S(2)}, u32[]{:S(2)}) collective-permute-start(f32[4,96,128]{2,1,0:T(8,128)S(1)} %get-tuple-element.56), channel_id=1, source_target_pairs={{0,3},{1,0},{2,1},{3,2},{4,7},{5,4},{6,5},{7,6},{8,11},{9,8},{10,9... | collective-permute-start | bytes 589832 | tf_op jit(solution)/shard_map/ppermute | solution.py:571
  12.3 9.1 %prepare.1 = (f32[8,96,128]{2,1,0:T(8,128)S(1)}, f32[8,96,128]{2,1,0:T(8,128)S(1)}, bf16[5,8,192,192]{3,2,1,0:T(8,128)(2,1)S(1)}, bf16[4,8,192,192]{3,2,1,0:T(8,...) custom-call(f32[8,96,128]{2,1,0:T(8,128)S(1)} %get-tuple-element.45.x_ref.x, ...), custom_call_target="tpu_custom_call" | custom-call | flops 8000000000 | bytes 25000000 | tf_op jit(solution)/shard_map/prepare/pallas_call | solution.py:225
  21.9 1.1 %middle.2 = (f32[4,96,128]{2,1,0:T(8,128)S(1)}, f32[4,96,128]{2,1,0:T(8,128)S(1)}, f32[512,128]{1,0:T(8,128)S(1)}) custom-call(f32[8,96,128]{2,1,0:T(8,128)S(1)} %get-tuple-element.47.rest, f32[8,96,128]{2,1,0:T(8,128)S(1)} %collective-permute-done.near, f32[8,96,128]{2,1,0:T(8,128)S(1)} %collective-permute-done.1.far, f32[4,96,128]{2,1,0:T(8,128)S(1)} %front_faces.2.front, ...), custom_call_target="tpu_custom_call" | custom-call | flops 1000 | bytes 1000 | tf_op jit(solution)/shard_map/middle/pallas_call | solution.py:322
  23.3 1.5 %collective-permute-done.5.forward = f32[4,96,128]{2,1,0:T(8,128)S(1)} collective-permute-done((f32[4,96,128]{2,1,0:T(8,128)S(1)}, f32[4,96,128]{2,1,0:T(8,128)S(1)}, u32[]{:S(2)}, u32[]{:S(2)}) %collective-permute-start.5) | collective-permute-done | bytes 196640 | tf_op jit(solution)/shard_map/ppermute | solution.py:571
  24.8 1.0 %forward_face.2 = (f32[8,96,128]{2,1,0:T(8,128)S(1)}, f32[4,96,128]{2,1,0:T(8,128)}, f32[256,128]{1,0:T(8,128)S(1)}, f32[256,128]{1,0:T(8,128)S(1)}) custom-call(f32[4,96,128]{2,1,0:T(8,128)S(1)} %get-tuple-element.53.front, f32[512,128]{1,0:T(8,128)S(1)} %get-tuple-element.54.partial, f32[4,96,128]{2,1,0:T(8,128)S(1)} %backward_face.2.rest, ...), custom_call_target="tpu_custom_call" | custom-call | flops 2000000000 | bytes 8000000 | tf_op jit(solution)/shard_map/forward_face/pallas_call | solution.py:371
  25.8 1.3 %collective-permute-done.6.received = f32[256,128]{1,0:T(8,128)S(1)} collective-permute-done((f32[256,128]{1,0:T(8,128)S(1)}, f32[256,128]{1,0:T(8,128)S(1)}, u32[]{:S(2)}, u32[]{:S(2)}) %collective-permute-start.6) | collective-permute-done | bytes 131104 | tf_op jit(solution)/shard_map/ppermute | solution.py:576
  27.2 2.2 %collective-permute-start.7 = (f32[128,128]{1,0:T(8,128)S(1)}, f32[128,128]{1,0:T(8,128)S(1)}, u32[]{:S(2)}, u32[]{:S(2)}) collective-permute-start(f32[128,128]{1,0:T(8,128)S(1)} %get-tuple-element.61), channel_id=1, source_target_pairs={{0,10},{1,11},{2,8},{3,9},{4,14},{5,15},{6,12},{7,13},{8,2},{9,3},... | collective-permute-start | bytes 196616 | tf_op jit(solution)/shard_map/ppermute | solution.py:582
  29.4 1.7 %collective-permute-start.8 = (f32[128,128]{1,0:T(8,128)S(1)}, f32[128,128]{1,0:T(8,128)S(1)}, u32[]{:S(2)}, u32[]{:S(2)}) collective-permute-start(f32[128,128]{1,0:T(8,128)S(1)} %get-tuple-element.60.refs_0_), channel_id=1, source_target_pairs={{0,2},{1,3},{2,0},{3,1},{4,6},{5,7},{6,4},{7,5},{8,10},{9,11},{10,... | collective-permute-start | bytes 196616 | tf_op jit(solution)/shard_map/ppermute | solution.py:576
  31.8 4.9 %collective-permute-done.7.refs_1_ = f32[128,128]{1,0:T(8,128)S(1)} collective-permute-done((f32[128,128]{1,0:T(8,128)S(1)}, f32[128,128]{1,0:T(8,128)S(1)}, u32[]{:S(2)}, u32[]{:S(2)}) %collective-permute-start.7) | collective-permute-done | bytes 65568 | tf_op jit(solution)/shard_map/ppermute | solution.py:582
  36.6 0.8 collective-permute-done.8.refs_2_
  37.5 0.8 collective-permute-start.11
  38.4 2.7 %collective-permute-start.10 = (f32[128,128]{1,0:T(8,128)S(1)}, f32[128,128]{1,0:T(8,128)S(1)}, u32[]{:S(2)}, u32[]{:S(2)}) collective-permute-start(f32[128,128]{1,0:T(8,128)S(1)} %scale.2.left), channel_id=1, source_target_pairs={{0,1},{1,0},{2,3},{3,2},{4,5},{5,4},{6,7},{7,6},{8,9},{9,8},{10,11... | collective-permute-start | bytes 196616 | tf_op jit(solution)/shard_map/ppermute | solution.py:576
  41.1 1.1 %collective-permute-done.11.left = f32[128,128]{1,0:T(8,128)S(1)} collective-permute-done((f32[128,128]{1,0:T(8,128)S(1)}, f32[128,128]{1,0:T(8,128)S(1)}, u32[]{:S(2)}, u32[]{:S(2)}) %collective-permute-start.11) | collective-permute-done | bytes 65568 | tf_op jit(solution)/shard_map/ppermute | solution.py:576
  42.2 1.2 %collective-permute-done.12.right = f32[128,128]{1,0:T(8,128)S(1)} collective-permute-done((f32[128,128]{1,0:T(8,128)S(1)}, f32[128,128]{1,0:T(8,128)S(1)}, u32[]{:S(2)}, u32[]{:S(2)}) %collective-permute-start.12) | collective-permute-done | bytes 65568 | tf_op jit(solution)/shard_map/ppermute | solution.py:582
  44.1 0.7 first_half.3.base
  45.4 0.7 second_half.2
  46.3 1.3 %collective-permute-start.17 = (f32[4,96,128]{2,1,0:T(8,128)S(1)}, f32[4,96,128]{2,1,0:T(8,128)S(1)}, u32[]{:S(2)}, u32[]{:S(2)}) collective-permute-start(f32[4,96,128]{2,1,0:T(8,128)S(1)} %get-tuple-element.68), channel_id=1, source_target_pairs={{0,1},{1,2},{2,3},{3,0},{4,5},{5,6},{6,7},{7,4},{8,9},{9,10},{10,1... | collective-permute-start | bytes 589832 | tf_op jit(solution)/shard_map/ppermute | solution.py:571
  47.6 2.5 %collective-permute-start.18 = (f32[4,96,128]{2,1,0:T(8,128)S(1)}, f32[4,96,128]{2,1,0:T(8,128)S(1)}, u32[]{:S(2)}, u32[]{:S(2)}) collective-permute-start(f32[4,96,128]{2,1,0:T(8,128)S(1)} %get-tuple-element.68), channel_id=1, source_target_pairs={{0,3},{1,0},{2,1},{3,2},{4,7},{5,4},{6,5},{7,6},{8,11},{9,8},{10,9... | collective-permute-start | bytes 589832 | tf_op jit(solution)/shard_map/ppermute | solution.py:571
  50.5 3.8 %collective-permute-start.20 = (f32[4,96,128]{2,1,0:T(8,128)S(1)}, f32[4,96,128]{2,1,0:T(8,128)S(1)}, u32[]{:S(2)}, u32[]{:S(2)}) collective-permute-start(f32[4,96,128]{2,1,0:T(8,128)S(1)} %get-tuple-element.72), channel_id=1, source_target_pairs={{0,3},{1,0},{2,1},{3,2},{4,7},{5,4},{6,5},{7,6},{8,11},{9,8},{10,9... | collective-permute-start | bytes 589832 | tf_op jit(solution)/shard_map/ppermute | solution.py:571
  54.3 1.3 %local_part.1.rest = f32[8,96,128]{2,1,0:T(8,128)S(1)} custom-call(f32[8,96,128]{2,1,0:T(8,128)S(1)} %get-tuple-element.77.x_ref.x, f32[8,96,128]{2,1,0:T(8,128)S(1)} %get-tuple-element.63.source, bf16[5,8,192,192]{3,2,1,0:T(8,128)(2,1)S(1)} %get-tuple-element.64.local), custom_call_target="tpu_custom_call" | custom-call | flops 8000000000 | bytes 8000000 | tf_op jit(solution)/shard_map/local_part/pallas_call | solution.py:142
  55.8 1.5 %collective-permute-start.23 = (f32[8,96,128]{2,1,0:T(8,128)S(1)}, f32[8,96,128]{2,1,0:T(8,128)S(1)}, u32[]{:S(2)}, u32[]{:S(2)}) collective-permute-start(f32[8,96,128]{2,1,0:T(8,128)S(1)} %get-tuple-element.77.x_ref.x), channel_id=1, source_target_pairs={{0,16},{16,0},{1,17},{17,1},{2,18},{18,2},{3,19},{19,3},{4,20},{20... | collective-permute-start | bytes 1179656 | tf_op jit(solution)/shard_map/ppermute | solution.py:576
  57.4 2.8 %collective-permute-done.18.forward = f32[4,96,128]{2,1,0:T(8,128)S(1)} collective-permute-done((f32[4,96,128]{2,1,0:T(8,128)S(1)}, f32[4,96,128]{2,1,0:T(8,128)S(1)}, u32[]{:S(2)}, u32[]{:S(2)}) %collective-permute-start.18) | collective-permute-done | bytes 196640 | tf_op jit(solution)/shard_map/ppermute | solution.py:571
  60.6 0.9 collective-permute-done.16.far
  61.5 1.1 %middle.3 = (f32[4,96,128]{2,1,0:T(8,128)S(1)}, f32[4,96,128]{2,1,0:T(8,128)S(1)}, f32[512,128]{1,0:T(8,128)S(1)}) custom-call(f32[8,96,128]{2,1,0:T(8,128)S(1)} %local_part.1.rest, f32[8,96,128]{2,1,0:T(8,128)S(1)} %collective-permute-done.15.near, f32[8,96,128]{2,1,0:T(8,128)S(1)} %collective-permute-done.16.far, f32[4,96,128]{2,1,0:T(8,128)S(1)} %front_faces.3.front, ...), custom_call_target="tpu_custom_call" | custom-call | flops 1000 | bytes 1000 | tf_op jit(solution)/shard_map/middle/pallas_call | solution.py:322
  62.6 1.8 %collective-permute-done.19.backward = f32[4,96,128]{2,1,0:T(8,128)S(1)} collective-permute-done((f32[4,96,128]{2,1,0:T(8,128)S(1)}, f32[4,96,128]{2,1,0:T(8,128)S(1)}, u32[]{:S(2)}, u32[]{:S(2)}) %collective-permute-start.19) | collective-permute-done | bytes 196640 | tf_op jit(solution)/shard_map/ppermute | solution.py:571
  64.7 2.4 %collective-permute-done.20.forward = f32[4,96,128]{2,1,0:T(8,128)S(1)} collective-permute-done((f32[4,96,128]{2,1,0:T(8,128)S(1)}, f32[4,96,128]{2,1,0:T(8,128)S(1)}, u32[]{:S(2)}, u32[]{:S(2)}) %collective-permute-start.20) | collective-permute-done | bytes 196640 | tf_op jit(solution)/shard_map/ppermute | solution.py:571
  67.1 0.9 %forward_face.3 = (f32[8,96,128]{2,1,0:T(8,128)S(1)}, f32[4,96,128]{2,1,0:T(8,128)S(1)}, f32[256,128]{1,0:T(8,128)S(1)}, f32[256,128]{1,0:T(8,128)S(1)}) custom-call(f32[4,96,128]{2,1,0:T(8,128)S(1)} %get-tuple-element.69.front, f32[512,128]{1,0:T(8,128)S(1)} %get-tuple-element.70.partial, f32[4,96,128]{2,1,0:T(8,128)S(1)} %backward_face.3.rest, ...), custom_call_target="tpu_custom_call" | custom-call | flops 2000000000 | bytes 8000000 | tf_op jit(solution)/shard_map/forward_face/pallas_call | solution.py:371
  68.1 1.6 %collective-permute-start.27 = (f32[4,96,128]{2,1,0:T(8,128)S(1)}, f32[4,96,128]{2,1,0:T(8,128)S(1)}, u32[]{:S(2)}, u32[]{:S(2)}) collective-permute-start(f32[4,96,128]{2,1,0:T(8,128)S(1)} %get-tuple-element.69.front), channel_id=1, source_target_pairs={{0,16},{16,0},{1,17},{17,1},{2,18},{18,2},{3,19},{19,3},{4,20},{20... | collective-permute-start | bytes 589832 | tf_op jit(solution)/shard_map/ppermute | solution.py:576
  69.8 0.7 collective-permute-start.22
  70.5 1.3 %collective-permute-start.30 = (f32[4,96,128]{2,1,0:T(8,128)S(1)}, f32[4,96,128]{2,1,0:T(8,128)S(1)}, u32[]{:S(2)}, u32[]{:S(2)}) collective-permute-start(f32[4,96,128]{2,1,0:T(8,128)S(1)} %get-tuple-element.82), channel_id=1, source_target_pairs={{0,16},{16,0},{1,17},{17,1},{2,18},{18,2},{3,19},{19,3},{4,20},{20... | collective-permute-start | bytes 589832 | tf_op jit(solution)/shard_map/ppermute | solution.py:576
  71.8 2.3 %collective-permute-done.22.right = f32[128,128]{1,0:T(8,128)S(1)} collective-permute-done((f32[128,128]{1,0:T(8,128)S(1)}, f32[128,128]{1,0:T(8,128)S(1)}, u32[]{:S(2)}, u32[]{:S(2)}) %collective-permute-start.22) | collective-permute-done | bytes 65568 | tf_op jit(solution)/shard_map/ppermute | solution.py:576
  74.1 2.2 %collective-permute-start.24 = (f32[128,128]{1,0:T(8,128)S(1)}, f32[128,128]{1,0:T(8,128)S(1)}, u32[]{:S(2)}, u32[]{:S(2)}) collective-permute-start(f32[128,128]{1,0:T(8,128)S(1)} %add.5.refs_0_), channel_id=1, source_target_pairs={{0,3},{1,2},{2,1},{3,0},{4,7},{5,6},{6,5},{7,4},{8,11},{9,10},{10,... | collective-permute-start | bytes 196616 | tf_op jit(solution)/shard_map/ppermute | solution.py:576
  76.8 1.7 %collective-permute-start.26 = (f32[128,128]{1,0:T(8,128)S(1)}, f32[128,128]{1,0:T(8,128)S(1)}, u32[]{:S(2)}, u32[]{:S(2)}) collective-permute-start(f32[128,128]{1,0:T(8,128)S(1)} %add.5.refs_0_), channel_id=1, source_target_pairs={{0,1},{1,0},{2,3},{3,2},{4,5},{5,4},{6,7},{7,6},{8,9},{9,8},{10,11... | collective-permute-start | bytes 196616 | tf_op jit(solution)/shard_map/ppermute | solution.py:576
  78.6 2.0 %collective-permute-done.24.refs_1_ = f32[128,128]{1,0:T(8,128)S(1)} collective-permute-done((f32[128,128]{1,0:T(8,128)S(1)}, f32[128,128]{1,0:T(8,128)S(1)}, u32[]{:S(2)}, u32[]{:S(2)}) %collective-permute-start.24) | collective-permute-done | bytes 65568 | tf_op jit(solution)/shard_map/ppermute | solution.py:576
  80.6 2.2 %collective-permute-done.25.refs_2_ = f32[128,128]{1,0:T(8,128)S(1)} collective-permute-done((f32[128,128]{1,0:T(8,128)S(1)}, f32[128,128]{1,0:T(8,128)S(1)}, u32[]{:S(2)}, u32[]{:S(2)}) %collective-permute-start.25) | collective-permute-done | bytes 65568 | tf_op jit(solution)/shard_map/ppermute | solution.py:576
  82.9 0.7 collective-permute-start.29
  83.6 2.0 %collective-permute-start.28 = (f32[128,128]{1,0:T(8,128)S(1)}, f32[128,128]{1,0:T(8,128)S(1)}, u32[]{:S(2)}, u32[]{:S(2)}) collective-permute-start(f32[128,128]{1,0:T(8,128)S(1)} %scale.3.refs_1_), channel_id=1, source_target_pairs={{0,24},{4,28},{8,16},{12,20},{16,8},{20,12},{24,0},{28,4},{1,25},{... | collective-permute-start | bytes 196616 | tf_op jit(solution)/shard_map/ppermute | solution.py:582
  85.7 0.8 collective-permute-start.33
  86.5 1.0 %join.1 = f32[8,96,256]{2,1,0:T(8,128)} custom-call(f32[8,96,128]{2,1,0:T(8,128)S(1)} %get-tuple-element.80.own.refs_0_, f32[4,96,128]{2,1,0:T(8,128)S(1)} %collective-permute-done.27.front.refs_0_, f32[4,96,128]{2,1,0:T(8,128)S(1)} %collective-permute-done.30.back.refs_1_), custom_call_target="tpu_custom_call" | custom-call | flops 1000000 | bytes 2000000 | tf_op jit(solution)/shard_map/join/pallas_call | solution.py:525
  88.1 0.7 first_half.4.base
  88.8 1.1 %collective-permute-done.33.refs_2_ = f32[128,128]{1,0:T(8,128)S(1)} collective-permute-done((f32[128,128]{1,0:T(8,128)S(1)}, f32[128,128]{1,0:T(8,128)S(1)}, u32[]{:S(2)}, u32[]{:S(2)}) %collective-permute-start.33) | collective-permute-done | bytes 65568 | tf_op jit(solution)/shard_map/ppermute | solution.py:576
  89.9 0.7 first_half.5.other
  90.6 0.7 second_half.3.own
  91.3 1.5 %final.1 = f32[8,96,256]{2,1,0:T(8,128)} custom-call(f32[8,96,128]{2,1,0:T(8,128)S(1)} %second_half.3.own, f32[8,96,128]{2,1,0:T(8,128)S(1)} %first_half.5.other, bf16[8,2,192,512]{3,2,1,0:T(8,128)(2,1)S(1)} %get-tuple-element.46.vectors, f32[128,128]{1,0:T(8,128)S(1)} %collective-permute-done.34.refs_0_, f32[128,128]{1,0:T(8,128)S(1)} %collective-permute-done.35.refs_1_), custom_call_target="tpu_custom_call" | custom-call | flops 1000000000 | bytes 4000000 | tf_op jit(solution)/shard_map/final/pallas_call | solution.py:553
  (54 shorter events, 6.8 us)
Async XLA Ops:
  0.6 1.1 %copy-start = (f32[1,1,2,4,96,256]{5,4,3,2,1,0:T(8,128)S(1)}, f32[1,1,2,4,96,256]{5,4,3,2,1,0:T(8,128)}, u32[]{:S(2)}) copy-start(f32[1,1,2,4,96,256]{5,4,3,2,1,0:T(8,128)} %param.7) | copy-start | bytes 2359300
  2.0 6.4 %collective-permute-start = (f32[8,96,128]{2,1,0:T(8,128)S(1)}, f32[8,96,128]{2,1,0:T(8,128)S(1)}, u32[]{:S(2)}, u32[]{:S(2)}) collective-permute-start(f32[8,96,128]{2,1,0:T(8,128)S(1)} %get-tuple-element.45.x_ref.x), channel_id=1, source_target_pairs={{0,4},{4,0},{8,12},{12,8},{1,5},{5,1},{9,13},{13,9},{2,6},{6,2},{1... | collective-permute-start | bytes 1179656 | tf_op jit(solution)/shard_map/ppermute | solution.py:576
  2.6 18.8 %collective-permute-start.2 = (f32[4,96,128]{2,1,0:T(8,128)S(1)}, f32[4,96,128]{2,1,0:T(8,128)S(1)}, u32[]{:S(2)}, u32[]{:S(2)}) collective-permute-start(f32[4,96,128]{2,1,0:T(8,128)S(1)} %get-tuple-element.50), channel_id=1, source_target_pairs={{0,1},{1,2},{2,3},{3,0},{4,5},{5,6},{6,7},{7,4},{8,9},{9,10},{10,1... | collective-permute-start | bytes 589832 | tf_op jit(solution)/shard_map/ppermute | solution.py:571
  5.2 16.2 %collective-permute-start.3 = (f32[4,96,128]{2,1,0:T(8,128)S(1)}, f32[4,96,128]{2,1,0:T(8,128)S(1)}, u32[]{:S(2)}, u32[]{:S(2)}) collective-permute-start(f32[4,96,128]{2,1,0:T(8,128)S(1)} %get-tuple-element.50), channel_id=1, source_target_pairs={{0,3},{1,0},{2,1},{3,2},{4,7},{5,4},{6,5},{7,6},{8,11},{9,8},{10,9... | collective-permute-start | bytes 589832 | tf_op jit(solution)/shard_map/ppermute | solution.py:571
  7.3 14.6 %collective-permute-start.1 = (f32[8,96,128]{2,1,0:T(8,128)S(1)}, f32[8,96,128]{2,1,0:T(8,128)S(1)}, u32[]{:S(2)}, u32[]{:S(2)}) collective-permute-start(f32[8,96,128]{2,1,0:T(8,128)S(1)} %get-tuple-element.45.x_ref.x), channel_id=1, source_target_pairs={{0,12},{4,8},{8,4},{12,0},{1,13},{5,9},{9,5},{13,1},{2,14},{6,10},... | collective-permute-start | bytes 1179656 | tf_op jit(solution)/shard_map/ppermute | solution.py:589
  8.5 14.5 %collective-permute-start.4 = (f32[4,96,128]{2,1,0:T(8,128)S(1)}, f32[4,96,128]{2,1,0:T(8,128)S(1)}, u32[]{:S(2)}, u32[]{:S(2)}) collective-permute-start(f32[4,96,128]{2,1,0:T(8,128)S(1)} %get-tuple-element.56), channel_id=1, source_target_pairs={{0,1},{1,2},{2,3},{3,0},{4,5},{5,6},{6,7},{7,4},{8,9},{9,10},{10,1... | collective-permute-start | bytes 589832 | tf_op jit(solution)/shard_map/ppermute | solution.py:571
  8.5 16.3 %collective-permute-start.5 = (f32[4,96,128]{2,1,0:T(8,128)S(1)}, f32[4,96,128]{2,1,0:T(8,128)S(1)}, u32[]{:S(2)}, u32[]{:S(2)}) collective-permute-start(f32[4,96,128]{2,1,0:T(8,128)S(1)} %get-tuple-element.56), channel_id=1, source_target_pairs={{0,3},{1,0},{2,1},{3,2},{4,7},{5,4},{6,5},{7,6},{8,11},{9,8},{10,9... | collective-permute-start | bytes 589832 | tf_op jit(solution)/shard_map/ppermute | solution.py:571
  24.8 6.8 %copy-start.1 = (f32[2,512]{1,0:T(2,128)S(1)}, f32[2,512]{1,0:T(2,128)}, u32[]{:S(2)}) copy-start(f32[2,512]{1,0:T(2,128)} %inverse.1) | copy-start | bytes 12292
  25.8 1.3 %collective-permute-start.6 = (f32[256,128]{1,0:T(8,128)S(1)}, f32[256,128]{1,0:T(8,128)S(1)}, u32[]{:S(2)}, u32[]{:S(2)}) collective-permute-start(f32[256,128]{1,0:T(8,128)S(1)} %get-tuple-element.59), channel_id=1, source_target_pairs={{0,4},{4,0},{8,12},{12,8},{1,5},{5,1},{9,13},{13,9},{2,6},{6,2},{1... | collective-permute-start | bytes 393224 | tf_op jit(solution)/shard_map/ppermute | solution.py:576
  27.2 9.4 %collective-permute-start.7 = (f32[128,128]{1,0:T(8,128)S(1)}, f32[128,128]{1,0:T(8,128)S(1)}, u32[]{:S(2)}, u32[]{:S(2)}) collective-permute-start(f32[128,128]{1,0:T(8,128)S(1)} %get-tuple-element.61), channel_id=1, source_target_pairs={{0,10},{1,11},{2,8},{3,9},{4,14},{5,15},{6,12},{7,13},{8,2},{9,3},... | collective-permute-start | bytes 196616 | tf_op jit(solution)/shard_map/ppermute | solution.py:582
  29.4 8.0 %collective-permute-start.8 = (f32[128,128]{1,0:T(8,128)S(1)}, f32[128,128]{1,0:T(8,128)S(1)}, u32[]{:S(2)}, u32[]{:S(2)}) collective-permute-start(f32[128,128]{1,0:T(8,128)S(1)} %get-tuple-element.60.refs_0_), channel_id=1, source_target_pairs={{0,2},{1,3},{2,0},{3,1},{4,6},{5,7},{6,4},{7,5},{8,10},{9,11},{10,... | collective-permute-start | bytes 196616 | tf_op jit(solution)/shard_map/ppermute | solution.py:576
  31.1 6.3 %collective-permute-start.9 = (f32[128,128]{1,0:T(8,128)S(1)}, f32[128,128]{1,0:T(8,128)S(1)}, u32[]{:S(2)}, u32[]{:S(2)}) collective-permute-start(f32[128,128]{1,0:T(8,128)S(1)} %get-tuple-element.61), channel_id=1, source_target_pairs={{0,8},{4,12},{8,0},{12,4},{1,9},{5,13},{9,1},{13,5},{2,10},{6,14},... | collective-permute-start | bytes 196616 | tf_op jit(solution)/shard_map/ppermute | solution.py:576
  37.5 4.7 %collective-permute-start.11 = (f32[128,128]{1,0:T(8,128)S(1)}, f32[128,128]{1,0:T(8,128)S(1)}, u32[]{:S(2)}, u32[]{:S(2)}) collective-permute-start(f32[128,128]{1,0:T(8,128)S(1)} %scale.2.left), channel_id=1, source_target_pairs={{0,8},{4,12},{8,0},{12,4},{1,9},{5,13},{9,1},{13,5},{2,10},{6,14},... | collective-permute-start | bytes 196616 | tf_op jit(solution)/shard_map/ppermute | solution.py:576
  38.3 5.2 %collective-permute-start.12 = (f32[128,128]{1,0:T(8,128)S(1)}, f32[128,128]{1,0:T(8,128)S(1)}, u32[]{:S(2)}, u32[]{:S(2)}) collective-permute-start(f32[128,128]{1,0:T(8,128)S(1)} %scale.2.left), channel_id=1, source_target_pairs={{0,9},{1,8},{2,11},{3,10},{4,13},{5,12},{6,15},{7,14},{8,1},{9,0},... | collective-permute-start | bytes 196616 | tf_op jit(solution)/shard_map/ppermute | solution.py:582
  38.4 5.7 %collective-permute-start.10 = (f32[128,128]{1,0:T(8,128)S(1)}, f32[128,128]{1,0:T(8,128)S(1)}, u32[]{:S(2)}, u32[]{:S(2)}) collective-permute-start(f32[128,128]{1,0:T(8,128)S(1)} %scale.2.left), channel_id=1, source_target_pairs={{0,1},{1,0},{2,3},{3,2},{4,5},{5,4},{6,7},{7,6},{8,9},{9,8},{10,11... | collective-permute-start | bytes 196616 | tf_op jit(solution)/shard_map/ppermute | solution.py:576
  43.5 1.3 %collective-permute-start.14 = (f32[128,128]{1,0:T(8,128)S(1)}, f32[128,128]{1,0:T(8,128)S(1)}, u32[]{:S(2)}, u32[]{:S(2)}) collective-permute-start(f32[128,128]{1,0:T(8,128)S(1)} %add.4.refs_2_), channel_id=1, source_target_pairs={{0,4},{4,0},{8,12},{12,8},{1,5},{5,1},{9,13},{13,9},{2,6},{6,2},{1... | collective-permute-start | bytes 196616 | tf_op jit(solution)/shard_map/ppermute | solution.py:576
  44.1 1.3 %collective-permute-start.13 = (f32[128,128]{1,0:T(8,128)S(1)}, f32[128,128]{1,0:T(8,128)S(1)}, u32[]{:S(2)}, u32[]{:S(2)}) collective-permute-start(f32[128,128]{1,0:T(8,128)S(1)} %add.3.refs_1_), channel_id=1, source_target_pairs={{0,4},{4,0},{8,12},{12,8},{1,5},{5,1},{9,13},{13,9},{2,6},{6,2},{1... | collective-permute-start | bytes 196616 | tf_op jit(solution)/shard_map/ppermute | solution.py:576
  46.0 4.4 %collective-permute-start.15 = (f32[8,96,128]{2,1,0:T(8,128)S(1)}, f32[8,96,128]{2,1,0:T(8,128)S(1)}, u32[]{:S(2)}, u32[]{:S(2)}) collective-permute-start(f32[8,96,128]{2,1,0:T(8,128)S(1)} %get-tuple-element.77.x_ref.x), channel_id=1, source_target_pairs={{0,4},{4,0},{8,12},{12,8},{1,5},{5,1},{9,13},{13,9},{2,6},{6,2},{1... | collective-permute-start | bytes 1179656 | tf_op jit(solution)/shard_map/ppermute | solution.py:576
  46.3 9.6 %collective-permute-start.17 = (f32[4,96,128]{2,1,0:T(8,128)S(1)}, f32[4,96,128]{2,1,0:T(8,128)S(1)}, u32[]{:S(2)}, u32[]{:S(2)}) collective-permute-start(f32[4,96,128]{2,1,0:T(8,128)S(1)} %get-tuple-element.68), channel_id=1, source_target_pairs={{0,1},{1,2},{2,3},{3,0},{4,5},{5,6},{6,7},{7,4},{8,9},{9,10},{10,1... | collective-permute-start | bytes 589832 | tf_op jit(solution)/shard_map/ppermute | solution.py:571
  47.6 12.5 %collective-permute-start.18 = (f32[4,96,128]{2,1,0:T(8,128)S(1)}, f32[4,96,128]{2,1,0:T(8,128)S(1)}, u32[]{:S(2)}, u32[]{:S(2)}) collective-permute-start(f32[4,96,128]{2,1,0:T(8,128)S(1)} %get-tuple-element.68), channel_id=1, source_target_pairs={{0,3},{1,0},{2,1},{3,2},{4,7},{5,4},{6,5},{7,6},{8,11},{9,8},{10,9... | collective-permute-start | bytes 589832 | tf_op jit(solution)/shard_map/ppermute | solution.py:571
  50.1 11.4 %collective-permute-start.16 = (f32[8,96,128]{2,1,0:T(8,128)S(1)}, f32[8,96,128]{2,1,0:T(8,128)S(1)}, u32[]{:S(2)}, u32[]{:S(2)}) collective-permute-start(f32[8,96,128]{2,1,0:T(8,128)S(1)} %get-tuple-element.77.x_ref.x), channel_id=1, source_target_pairs={{0,12},{4,8},{8,4},{12,0},{1,13},{5,9},{9,5},{13,1},{2,14},{6,10},... | collective-permute-start | bytes 1179656 | tf_op jit(solution)/shard_map/ppermute | solution.py:589
  50.5 13.8 %collective-permute-start.19 = (f32[4,96,128]{2,1,0:T(8,128)S(1)}, f32[4,96,128]{2,1,0:T(8,128)S(1)}, u32[]{:S(2)}, u32[]{:S(2)}) collective-permute-start(f32[4,96,128]{2,1,0:T(8,128)S(1)} %get-tuple-element.72), channel_id=1, source_target_pairs={{0,1},{1,2},{2,3},{3,0},{4,5},{5,6},{6,7},{7,4},{8,9},{9,10},{10,1... | collective-permute-start | bytes 589832 | tf_op jit(solution)/shard_map/ppermute | solution.py:571
  50.5 16.6 %collective-permute-start.20 = (f32[4,96,128]{2,1,0:T(8,128)S(1)}, f32[4,96,128]{2,1,0:T(8,128)S(1)}, u32[]{:S(2)}, u32[]{:S(2)}) collective-permute-start(f32[4,96,128]{2,1,0:T(8,128)S(1)} %get-tuple-element.72), channel_id=1, source_target_pairs={{0,3},{1,0},{2,1},{3,2},{4,7},{5,4},{6,5},{7,6},{8,11},{9,8},{10,9... | collective-permute-start | bytes 589832 | tf_op jit(solution)/shard_map/ppermute | solution.py:571
  55.8 18.3 %collective-permute-start.23 = (f32[8,96,128]{2,1,0:T(8,128)S(1)}, f32[8,96,128]{2,1,0:T(8,128)S(1)}, u32[]{:S(2)}, u32[]{:S(2)}) collective-permute-start(f32[8,96,128]{2,1,0:T(8,128)S(1)} %get-tuple-element.77.x_ref.x), channel_id=1, source_target_pairs={{0,16},{16,0},{1,17},{17,1},{2,18},{18,2},{3,19},{19,3},{4,20},{20... | collective-permute-start | bytes 1179656 | tf_op jit(solution)/shard_map/ppermute | solution.py:576
  68.1 1.7 %collective-permute-start.21 = (f32[256,128]{1,0:T(8,128)S(1)}, f32[256,128]{1,0:T(8,128)S(1)}, u32[]{:S(2)}, u32[]{:S(2)}) collective-permute-start(f32[256,128]{1,0:T(8,128)S(1)} %get-tuple-element.74), channel_id=1, source_target_pairs={{0,4},{4,0},{8,12},{12,8},{1,5},{5,1},{9,13},{13,9},{2,6},{6,2},{1... | collective-permute-start | bytes 393224 | tf_op jit(solution)/shard_map/ppermute | solution.py:576
  68.1 14.8 %collective-permute-start.27 = (f32[4,96,128]{2,1,0:T(8,128)S(1)}, f32[4,96,128]{2,1,0:T(8,128)S(1)}, u32[]{:S(2)}, u32[]{:S(2)}) collective-permute-start(f32[4,96,128]{2,1,0:T(8,128)S(1)} %get-tuple-element.69.front), channel_id=1, source_target_pairs={{0,16},{16,0},{1,17},{17,1},{2,18},{18,2},{3,19},{19,3},{4,20},{20... | collective-permute-start | bytes 589832 | tf_op jit(solution)/shard_map/ppermute | solution.py:576
  69.8 4.3 %collective-permute-start.22 = (f32[128,128]{1,0:T(8,128)S(1)}, f32[128,128]{1,0:T(8,128)S(1)}, u32[]{:S(2)}, u32[]{:S(2)}) collective-permute-start(f32[128,128]{1,0:T(8,128)S(1)} %get-tuple-element.76), channel_id=1, source_target_pairs={{0,8},{4,12},{8,0},{12,4},{1,9},{5,13},{9,1},{13,5},{2,10},{6,14},... | collective-permute-start | bytes 196616 | tf_op jit(solution)/shard_map/ppermute | solution.py:576
  70.5 16.0 %collective-permute-start.30 = (f32[4,96,128]{2,1,0:T(8,128)S(1)}, f32[4,96,128]{2,1,0:T(8,128)S(1)}, u32[]{:S(2)}, u32[]{:S(2)}) collective-permute-start(f32[4,96,128]{2,1,0:T(8,128)S(1)} %get-tuple-element.82), channel_id=1, source_target_pairs={{0,16},{16,0},{1,17},{17,1},{2,18},{18,2},{3,19},{19,3},{4,20},{20... | collective-permute-start | bytes 589832 | tf_op jit(solution)/shard_map/ppermute | solution.py:576
  74.1 6.4 %collective-permute-start.24 = (f32[128,128]{1,0:T(8,128)S(1)}, f32[128,128]{1,0:T(8,128)S(1)}, u32[]{:S(2)}, u32[]{:S(2)}) collective-permute-start(f32[128,128]{1,0:T(8,128)S(1)} %add.5.refs_0_), channel_id=1, source_target_pairs={{0,3},{1,2},{2,1},{3,0},{4,7},{5,6},{6,5},{7,4},{8,11},{9,10},{10,... | collective-permute-start | bytes 196616 | tf_op jit(solution)/shard_map/ppermute | solution.py:576
  76.3 6.5 %collective-permute-start.25 = (f32[128,128]{1,0:T(8,128)S(1)}, f32[128,128]{1,0:T(8,128)S(1)}, u32[]{:S(2)}, u32[]{:S(2)}) collective-permute-start(f32[128,128]{1,0:T(8,128)S(1)} %add.5.refs_0_), channel_id=1, source_target_pairs={{0,2},{1,3},{2,0},{3,1},{4,6},{5,7},{6,4},{7,5},{8,10},{9,11},{10,... | collective-permute-start | bytes 196616 | tf_op jit(solution)/shard_map/ppermute | solution.py:576
  76.8 6.0 %collective-permute-start.26 = (f32[128,128]{1,0:T(8,128)S(1)}, f32[128,128]{1,0:T(8,128)S(1)}, u32[]{:S(2)}, u32[]{:S(2)}) collective-permute-start(f32[128,128]{1,0:T(8,128)S(1)} %add.5.refs_0_), channel_id=1, source_target_pairs={{0,1},{1,0},{2,3},{3,2},{4,5},{5,4},{6,7},{7,6},{8,9},{9,8},{10,11... | collective-permute-start | bytes 196616 | tf_op jit(solution)/shard_map/ppermute | solution.py:576
  82.9 4.6 %collective-permute-start.29 = (f32[128,128]{1,0:T(8,128)S(1)}, f32[128,128]{1,0:T(8,128)S(1)}, u32[]{:S(2)}, u32[]{:S(2)}) collective-permute-start(f32[128,128]{1,0:T(8,128)S(1)} %scale.3.refs_1_), channel_id=1, source_target_pairs={{0,8},{4,12},{8,0},{12,4},{1,9},{5,13},{9,1},{13,5},{2,10},{6,14},... | collective-permute-start | bytes 196616 | tf_op jit(solution)/shard_map/ppermute | solution.py:576
  83.6 5.2 %collective-permute-start.28 = (f32[128,128]{1,0:T(8,128)S(1)}, f32[128,128]{1,0:T(8,128)S(1)}, u32[]{:S(2)}, u32[]{:S(2)}) collective-permute-start(f32[128,128]{1,0:T(8,128)S(1)} %scale.3.refs_1_), channel_id=1, source_target_pairs={{0,24},{4,28},{8,16},{12,20},{16,8},{20,12},{24,0},{28,4},{1,25},{... | collective-permute-start | bytes 196616 | tf_op jit(solution)/shard_map/ppermute | solution.py:582
  85.7 4.3 %collective-permute-start.33 = (f32[128,128]{1,0:T(8,128)S(1)}, f32[128,128]{1,0:T(8,128)S(1)}, u32[]{:S(2)}, u32[]{:S(2)}) collective-permute-start(f32[128,128]{1,0:T(8,128)S(1)} %scale.3.refs_1_), channel_id=1, source_target_pairs={{0,16},{16,0},{1,17},{17,1},{2,18},{18,2},{3,19},{19,3},{4,20},{20... | collective-permute-start | bytes 196616 | tf_op jit(solution)/shard_map/ppermute | solution.py:576
  86.5 4.2 %collective-permute-start.31 = (f32[128,128]{1,0:T(8,128)S(1)}, f32[128,128]{1,0:T(8,128)S(1)}, u32[]{:S(2)}, u32[]{:S(2)}) collective-permute-start(f32[128,128]{1,0:T(8,128)S(1)} %scale.3.refs_1_), channel_id=1, source_target_pairs={{0,4},{4,0},{8,12},{12,8},{1,5},{5,1},{9,13},{13,9},{2,6},{6,2},{1... | collective-permute-start | bytes 196616 | tf_op jit(solution)/shard_map/ppermute | solution.py:576
  87.5 3.1 %collective-permute-start.32 = (f32[128,128]{1,0:T(8,128)S(1)}, f32[128,128]{1,0:T(8,128)S(1)}, u32[]{:S(2)}, u32[]{:S(2)}) collective-permute-start(f32[128,128]{1,0:T(8,128)S(1)} %collective-permute-done.29.refs_2_), channel_id=1, source_target_pairs={{0,4},{4,0},{8,12},{12,8},{1,5},{5,1},{9,13},{13,9},{2,6},{6,2},{1... | collective-permute-start | bytes 196616 | tf_op jit(solution)/shard_map/ppermute | solution.py:576
  88.8 2.5 %collective-permute-start.35 = (f32[128,128]{1,0:T(8,128)S(1)}, f32[128,128]{1,0:T(8,128)S(1)}, u32[]{:S(2)}, u32[]{:S(2)}) collective-permute-start(f32[128,128]{1,0:T(8,128)S(1)} %collective-permute-done.28.refs_3_), channel_id=1, source_target_pairs={{0,4},{4,0},{8,12},{12,8},{1,5},{5,1},{9,13},{13,9},{2,6},{6,2},{1... | collective-permute-start | bytes 196616 | tf_op jit(solution)/shard_map/ppermute | solution.py:576
  89.9 1.4 %collective-permute-start.34 = (f32[128,128]{1,0:T(8,128)S(1)}, f32[128,128]{1,0:T(8,128)S(1)}, u32[]{:S(2)}, u32[]{:S(2)}) collective-permute-start(f32[128,128]{1,0:T(8,128)S(1)} %collective-permute-done.33.refs_2_), channel_id=1, source_target_pairs={{0,4},{4,0},{8,12},{12,8},{1,5},{5,1},{9,13},{13,9},{2,6},{6,2},{1... | collective-permute-start | bytes 196616 | tf_op jit(solution)/shard_map/ppermute | solution.py:576

commit v18 on v17

--- a/solution.py
+++ b/solution.py
@@ -422,7 +422,7 @@
     parts = [crossed_both(send, "space", 2, "tm", 2), crossed(keep, "tm", 2), crossed(send, "space", 2)]
     d = scale(eigen, [keep] + parts)
     moved, across = crossed(d, "space", 2), crossed_both(d, "space", 2, "tm", 1)
-    return [add(d, crossed(d, "tm", 1)), add(moved, across)]
+    return [add(d, crossed(d, "tm", 1)), add(across, moved)]
 
 
 def scale_kernel(eigen, *refs):

time: 93.2 us -> 93.1 us (level)
    ppermute x23, waiting for transfers between devices: 12 us -> 10.9 us  [crossed(): return lax.ppermute(value, axis, [(i, i ^ mask) for i in range(count)])]
    ppermute x8, waiting for transfers between devices: 8.7 us -> 9.7 us  [shifted(): lax.ppermute(value, axis, [(i, (i + step) % count) for i in range(count)])]
where the time goes in v18:
time: 93.1 us; the launch traced here: 92.9 us
  starting transfers between devices  40.1 us (43%)
  waiting for transfers between devices  28.1 us (30%)
  Pallas kernels  22.5 us (24%)
  local copies, waits for them, and re-layouts  1.13 us (1%)
  between operations  1.08 us (1%)
    ppermute x23, starting transfers between devices, crossed(): return lax.ppermute(value, axis, [(i, i ^ mask) for i in range(count)])  18.3 us
    ppermute x8, starting transfers between devices, shifted(): lax.ppermute(value, axis, [(i, (i + step) % count) for i in range(count)])  16.2 us
    ppermute x23, waiting for transfers between devices, crossed(): return lax.ppermute(value, axis, [(i, i ^ mask) for i in range(count)])  10.9 us
    ppermute x8, waiting for transfers between devices, shifted(): lax.ppermute(value, axis, [(i, (i + step) % count) for i in range(count)])  9.7 us
    pallas_call x1, Pallas kernels, prepare(): pl.pallas_call(functools.partial(prepare_kernel, ny, nx), out_shape=(pltp...  9.08 us
    ppermute x3, waiting for transfers between devices, crossed_both(): return lax.ppermute(value, (first, second), pairs)  6.59 us
    ppermute x3, starting transfers between devices, crossed_both(): return lax.ppermute(value, (first, second), pairs)  4.31 us
    pallas_call x2, Pallas kernels, middle(): pl.pallas_call(middle_kernel, out_shape=(half, half, pltpu.VMEM((vectors....  2.15 us
  transfers between devices with their start and end apart: 36, of which 18 were waited for; matrix products, arithmetic and copies ran while one was open for 0% of the time, Pallas kernels for 20%

profile of v18, /device:TPU:0, one launch (start us, length us, event | category | flops | bytes accessed | tf_op | source)
XLA Modules:
  0.0 92.9 jit_solution(1118924034397374590)
XLA Ops:
  0.6 1.1 %copy-done = f32[1,1,2,4,96,256]{5,4,3,2,1,0:T(8,128)S(1)} copy-done((f32[1,1,2,4,96,256]{5,4,3,2,1,0:T(8,128)S(1)}, f32[1,1,2,4,96,256]{5,4,3,2,1,0:T(8,128)}, u32[]{:S(2)}) %copy-start) | copy-done | bytes 786456
  2.6 2.6 %collective-permute-start.2 = (f32[4,96,128]{2,1,0:T(8,128)S(1)}, f32[4,96,128]{2,1,0:T(8,128)S(1)}, u32[]{:S(2)}, u32[]{:S(2)}) collective-permute-start(f32[4,96,128]{2,1,0:T(8,128)S(1)} %get-tuple-element.50), channel_id=1, source_target_pairs={{0,1},{1,2},{2,3},{3,0},{4,5},{5,6},{6,7},{7,4},{8,9},{9,10},{10,1... | collective-permute-start | bytes 589832 | tf_op jit(solution)/shard_map/ppermute | solution.py:571
  5.2 2.1 %collective-permute-start.3 = (f32[4,96,128]{2,1,0:T(8,128)S(1)}, f32[4,96,128]{2,1,0:T(8,128)S(1)}, u32[]{:S(2)}, u32[]{:S(2)}) collective-permute-start(f32[4,96,128]{2,1,0:T(8,128)S(1)} %get-tuple-element.50), channel_id=1, source_target_pairs={{0,3},{1,0},{2,1},{3,2},{4,7},{5,4},{6,5},{7,6},{8,11},{9,8},{10,9... | collective-permute-start | bytes 589832 | tf_op jit(solution)/shard_map/ppermute | solution.py:571
  7.3 1.2 %collective-permute-start.1 = (f32[8,96,128]{2,1,0:T(8,128)S(1)}, f32[8,96,128]{2,1,0:T(8,128)S(1)}, u32[]{:S(2)}, u32[]{:S(2)}) collective-permute-start(f32[8,96,128]{2,1,0:T(8,128)S(1)} %get-tuple-element.45.x_ref.x), channel_id=1, source_target_pairs={{0,12},{4,8},{8,4},{12,0},{1,13},{5,9},{9,5},{13,1},{2,14},{6,10},... | collective-permute-start | bytes 1179656 | tf_op jit(solution)/shard_map/ppermute | solution.py:589
  8.5 3.8 %collective-permute-start.5 = (f32[4,96,128]{2,1,0:T(8,128)S(1)}, f32[4,96,128]{2,1,0:T(8,128)S(1)}, u32[]{:S(2)}, u32[]{:S(2)}) collective-permute-start(f32[4,96,128]{2,1,0:T(8,128)S(1)} %get-tuple-element.56), channel_id=1, source_target_pairs={{0,3},{1,0},{2,1},{3,2},{4,7},{5,4},{6,5},{7,6},{8,11},{9,8},{10,9... | collective-permute-start | bytes 589832 | tf_op jit(solution)/shard_map/ppermute | solution.py:571
  12.3 9.1 %prepare.1 = (f32[8,96,128]{2,1,0:T(8,128)S(1)}, f32[8,96,128]{2,1,0:T(8,128)S(1)}, bf16[5,8,192,192]{3,2,1,0:T(8,128)(2,1)S(1)}, bf16[4,8,192,192]{3,2,1,0:T(8,...) custom-call(f32[8,96,128]{2,1,0:T(8,128)S(1)} %get-tuple-element.45.x_ref.x, ...), custom_call_target="tpu_custom_call" | custom-call | flops 8000000000 | bytes 25000000 | tf_op jit(solution)/shard_map/prepare/pallas_call | solution.py:225
  21.9 1.1 %middle.2 = (f32[4,96,128]{2,1,0:T(8,128)S(1)}, f32[4,96,128]{2,1,0:T(8,128)S(1)}, f32[512,128]{1,0:T(8,128)S(1)}) custom-call(f32[8,96,128]{2,1,0:T(8,128)S(1)} %get-tuple-element.47.rest, f32[8,96,128]{2,1,0:T(8,128)S(1)} %collective-permute-done.near, f32[8,96,128]{2,1,0:T(8,128)S(1)} %collective-permute-done.1.far, f32[4,96,128]{2,1,0:T(8,128)S(1)} %front_faces.2.front, ...), custom_call_target="tpu_custom_call" | custom-call | flops 1000 | bytes 1000 | tf_op jit(solution)/shard_map/middle/pallas_call | solution.py:322
  23.3 1.5 %collective-permute-done.5.forward = f32[4,96,128]{2,1,0:T(8,128)S(1)} collective-permute-done((f32[4,96,128]{2,1,0:T(8,128)S(1)}, f32[4,96,128]{2,1,0:T(8,128)S(1)}, u32[]{:S(2)}, u32[]{:S(2)}) %collective-permute-start.5) | collective-permute-done | bytes 196640 | tf_op jit(solution)/shard_map/ppermute | solution.py:571
  24.8 1.0 %forward_face.2 = (f32[8,96,128]{2,1,0:T(8,128)S(1)}, f32[4,96,128]{2,1,0:T(8,128)}, f32[256,128]{1,0:T(8,128)S(1)}, f32[256,128]{1,0:T(8,128)S(1)}) custom-call(f32[4,96,128]{2,1,0:T(8,128)S(1)} %get-tuple-element.53.front, f32[512,128]{1,0:T(8,128)S(1)} %get-tuple-element.54.partial, f32[4,96,128]{2,1,0:T(8,128)S(1)} %backward_face.2.rest, ...), custom_call_target="tpu_custom_call" | custom-call | flops 2000000000 | bytes 8000000 | tf_op jit(solution)/shard_map/forward_face/pallas_call | solution.py:371
  25.8 1.3 %collective-permute-done.6.received = f32[256,128]{1,0:T(8,128)S(1)} collective-permute-done((f32[256,128]{1,0:T(8,128)S(1)}, f32[256,128]{1,0:T(8,128)S(1)}, u32[]{:S(2)}, u32[]{:S(2)}) %collective-permute-start.6) | collective-permute-done | bytes 131104 | tf_op jit(solution)/shard_map/ppermute | solution.py:576
  27.2 2.2 %collective-permute-start.7 = (f32[128,128]{1,0:T(8,128)S(1)}, f32[128,128]{1,0:T(8,128)S(1)}, u32[]{:S(2)}, u32[]{:S(2)}) collective-permute-start(f32[128,128]{1,0:T(8,128)S(1)} %get-tuple-element.61), channel_id=1, source_target_pairs={{0,10},{1,11},{2,8},{3,9},{4,14},{5,15},{6,12},{7,13},{8,2},{9,3},... | collective-permute-start | bytes 196616 | tf_op jit(solution)/shard_map/ppermute | solution.py:582
  29.4 1.7 %collective-permute-start.8 = (f32[128,128]{1,0:T(8,128)S(1)}, f32[128,128]{1,0:T(8,128)S(1)}, u32[]{:S(2)}, u32[]{:S(2)}) collective-permute-start(f32[128,128]{1,0:T(8,128)S(1)} %get-tuple-element.60.refs_0_), channel_id=1, source_target_pairs={{0,2},{1,3},{2,0},{3,1},{4,6},{5,7},{6,4},{7,5},{8,10},{9,11},{10,... | collective-permute-start | bytes 196616 | tf_op jit(solution)/shard_map/ppermute | solution.py:576
  31.8 4.9 %collective-permute-done.7.refs_1_ = f32[128,128]{1,0:T(8,128)S(1)} collective-permute-done((f32[128,128]{1,0:T(8,128)S(1)}, f32[128,128]{1,0:T(8,128)S(1)}, u32[]{:S(2)}, u32[]{:S(2)}) %collective-permute-start.7) | collective-permute-done | bytes 65568 | tf_op jit(solution)/shard_map/ppermute | solution.py:582
  36.6 0.8 collective-permute-done.8.refs_2_
  37.6 0.8 collective-permute-start.12
  38.4 2.7 %collective-permute-start.10 = (f32[128,128]{1,0:T(8,128)S(1)}, f32[128,128]{1,0:T(8,128)S(1)}, u32[]{:S(2)}, u32[]{:S(2)}) collective-permute-start(f32[128,128]{1,0:T(8,128)S(1)} %scale.2.left), channel_id=1, source_target_pairs={{0,1},{1,0},{2,3},{3,2},{4,5},{5,4},{6,7},{7,6},{8,9},{9,8},{10,11... | collective-permute-start | bytes 196616 | tf_op jit(solution)/shard_map/ppermute | solution.py:576
  41.1 1.7 %collective-permute-done.11.left = f32[128,128]{1,0:T(8,128)S(1)} collective-permute-done((f32[128,128]{1,0:T(8,128)S(1)}, f32[128,128]{1,0:T(8,128)S(1)}, u32[]{:S(2)}, u32[]{:S(2)}) %collective-permute-start.11) | collective-permute-done | bytes 65568 | tf_op jit(solution)/shard_map/ppermute | solution.py:582
  43.4 0.7 first_half.3.base
  44.7 0.7 second_half.2
  45.6 2.0 %collective-permute-start.17 = (f32[4,96,128]{2,1,0:T(8,128)S(1)}, f32[4,96,128]{2,1,0:T(8,128)S(1)}, u32[]{:S(2)}, u32[]{:S(2)}) collective-permute-start(f32[4,96,128]{2,1,0:T(8,128)S(1)} %get-tuple-element.68), channel_id=1, source_target_pairs={{0,1},{1,2},{2,3},{3,0},{4,5},{5,6},{6,7},{7,4},{8,9},{9,10},{10,1... | collective-permute-start | bytes 589832 | tf_op jit(solution)/shard_map/ppermute | solution.py:571
  47.6 1.8 %collective-permute-start.18 = (f32[4,96,128]{2,1,0:T(8,128)S(1)}, f32[4,96,128]{2,1,0:T(8,128)S(1)}, u32[]{:S(2)}, u32[]{:S(2)}) collective-permute-start(f32[4,96,128]{2,1,0:T(8,128)S(1)} %get-tuple-element.68), channel_id=1, source_target_pairs={{0,3},{1,0},{2,1},{3,2},{4,7},{5,4},{6,5},{7,6},{8,11},{9,8},{10,9... | collective-permute-start | bytes 589832 | tf_op jit(solution)/shard_map/ppermute | solution.py:571
  49.7 3.6 %collective-permute-start.20 = (f32[4,96,128]{2,1,0:T(8,128)S(1)}, f32[4,96,128]{2,1,0:T(8,128)S(1)}, u32[]{:S(2)}, u32[]{:S(2)}) collective-permute-start(f32[4,96,128]{2,1,0:T(8,128)S(1)} %get-tuple-element.72), channel_id=1, source_target_pairs={{0,3},{1,0},{2,1},{3,2},{4,7},{5,4},{6,5},{7,6},{8,11},{9,8},{10,9... | collective-permute-start | bytes 589832 | tf_op jit(solution)/shard_map/ppermute | solution.py:571
  53.3 1.3 %local_part.1.rest = f32[8,96,128]{2,1,0:T(8,128)S(1)} custom-call(f32[8,96,128]{2,1,0:T(8,128)S(1)} %get-tuple-element.77.x_ref.x, f32[8,96,128]{2,1,0:T(8,128)S(1)} %get-tuple-element.63.source, bf16[5,8,192,192]{3,2,1,0:T(8,128)(2,1)S(1)} %get-tuple-element.64.local), custom_call_target="tpu_custom_call" | custom-call | flops 8000000000 | bytes 8000000 | tf_op jit(solution)/shard_map/local_part/pallas_call | solution.py:142
  54.6 0.6 collective-permute-done.17.backward
  55.1 1.5 %collective-permute-start.23 = (f32[8,96,128]{2,1,0:T(8,128)S(1)}, f32[8,96,128]{2,1,0:T(8,128)S(1)}, u32[]{:S(2)}, u32[]{:S(2)}) collective-permute-start(f32[8,96,128]{2,1,0:T(8,128)S(1)} %get-tuple-element.77.x_ref.x), channel_id=1, source_target_pairs={{0,16},{16,0},{1,17},{17,1},{2,18},{18,2},{3,19},{19,3},{4,20},{20... | collective-permute-start | bytes 1179656 | tf_op jit(solution)/shard_map/ppermute | solution.py:576
  56.7 2.8 %collective-permute-done.18.forward = f32[4,96,128]{2,1,0:T(8,128)S(1)} collective-permute-done((f32[4,96,128]{2,1,0:T(8,128)S(1)}, f32[4,96,128]{2,1,0:T(8,128)S(1)}, u32[]{:S(2)}, u32[]{:S(2)}) %collective-permute-start.18) | collective-permute-done | bytes 196640 | tf_op jit(solution)/shard_map/ppermute | solution.py:571
  59.9 0.9 collective-permute-done.16.far
  60.8 1.1 %middle.3 = (f32[4,96,128]{2,1,0:T(8,128)S(1)}, f32[4,96,128]{2,1,0:T(8,128)S(1)}, f32[512,128]{1,0:T(8,128)S(1)}) custom-call(f32[8,96,128]{2,1,0:T(8,128)S(1)} %local_part.1.rest, f32[8,96,128]{2,1,0:T(8,128)S(1)} %collective-permute-done.15.near, f32[8,96,128]{2,1,0:T(8,128)S(1)} %collective-permute-done.16.far, f32[4,96,128]{2,1,0:T(8,128)S(1)} %front_faces.3.front, ...), custom_call_target="tpu_custom_call" | custom-call | flops 1000 | bytes 1000 | tf_op jit(solution)/shard_map/middle/pallas_call | solution.py:322
  61.9 1.7 %collective-permute-done.19.backward = f32[4,96,128]{2,1,0:T(8,128)S(1)} collective-permute-done((f32[4,96,128]{2,1,0:T(8,128)S(1)}, f32[4,96,128]{2,1,0:T(8,128)S(1)}, u32[]{:S(2)}, u32[]{:S(2)}) %collective-permute-start.19) | collective-permute-done | bytes 196640 | tf_op jit(solution)/shard_map/ppermute | solution.py:571
  64.0 3.2 %collective-permute-done.20.forward = f32[4,96,128]{2,1,0:T(8,128)S(1)} collective-permute-done((f32[4,96,128]{2,1,0:T(8,128)S(1)}, f32[4,96,128]{2,1,0:T(8,128)S(1)}, u32[]{:S(2)}, u32[]{:S(2)}) %collective-permute-start.20) | collective-permute-done | bytes 196640 | tf_op jit(solution)/shard_map/ppermute | solution.py:571
  67.1 0.9 %forward_face.3 = (f32[8,96,128]{2,1,0:T(8,128)S(1)}, f32[4,96,128]{2,1,0:T(8,128)S(1)}, f32[256,128]{1,0:T(8,128)S(1)}, f32[256,128]{1,0:T(8,128)S(1)}) custom-call(f32[4,96,128]{2,1,0:T(8,128)S(1)} %get-tuple-element.69.front, f32[512,128]{1,0:T(8,128)S(1)} %get-tuple-element.70.partial, f32[4,96,128]{2,1,0:T(8,128)S(1)} %backward_face.3.rest, ...), custom_call_target="tpu_custom_call" | custom-call | flops 2000000000 | bytes 8000000 | tf_op jit(solution)/shard_map/forward_face/pallas_call | solution.py:371
  68.1 1.6 %collective-permute-start.27 = (f32[4,96,128]{2,1,0:T(8,128)S(1)}, f32[4,96,128]{2,1,0:T(8,128)S(1)}, u32[]{:S(2)}, u32[]{:S(2)}) collective-permute-start(f32[4,96,128]{2,1,0:T(8,128)S(1)} %get-tuple-element.69.front), channel_id=1, source_target_pairs={{0,16},{16,0},{1,17},{17,1},{2,18},{18,2},{3,19},{19,3},{4,20},{20... | collective-permute-start | bytes 589832 | tf_op jit(solution)/shard_map/ppermute | solution.py:576
  69.7 0.8 collective-permute-start.22
  70.5 1.3 %collective-permute-start.30 = (f32[4,96,128]{2,1,0:T(8,128)S(1)}, f32[4,96,128]{2,1,0:T(8,128)S(1)}, u32[]{:S(2)}, u32[]{:S(2)}) collective-permute-start(f32[4,96,128]{2,1,0:T(8,128)S(1)} %get-tuple-element.82), channel_id=1, source_target_pairs={{0,16},{16,0},{1,17},{17,1},{2,18},{18,2},{3,19},{19,3},{4,20},{20... | collective-permute-start | bytes 589832 | tf_op jit(solution)/shard_map/ppermute | solution.py:576
  71.8 2.3 %collective-permute-done.22.right = f32[128,128]{1,0:T(8,128)S(1)} collective-permute-done((f32[128,128]{1,0:T(8,128)S(1)}, f32[128,128]{1,0:T(8,128)S(1)}, u32[]{:S(2)}, u32[]{:S(2)}) %collective-permute-start.22) | collective-permute-done | bytes 65568 | tf_op jit(solution)/shard_map/ppermute | solution.py:576
  74.1 2.2 %collective-permute-start.24 = (f32[128,128]{1,0:T(8,128)S(1)}, f32[128,128]{1,0:T(8,128)S(1)}, u32[]{:S(2)}, u32[]{:S(2)}) collective-permute-start(f32[128,128]{1,0:T(8,128)S(1)} %add.5.refs_0_), channel_id=1, source_target_pairs={{0,3},{1,2},{2,1},{3,0},{4,7},{5,6},{6,5},{7,4},{8,11},{9,10},{10,... | collective-permute-start | bytes 196616 | tf_op jit(solution)/shard_map/ppermute | solution.py:576
  76.3 2.3 %collective-permute-start.26 = (f32[128,128]{1,0:T(8,128)S(1)}, f32[128,128]{1,0:T(8,128)S(1)}, u32[]{:S(2)}, u32[]{:S(2)}) collective-permute-start(f32[128,128]{1,0:T(8,128)S(1)} %add.5.refs_0_), channel_id=1, source_target_pairs={{0,1},{1,0},{2,3},{3,2},{4,5},{5,4},{6,7},{7,6},{8,9},{9,8},{10,11... | collective-permute-start | bytes 196616 | tf_op jit(solution)/shard_map/ppermute | solution.py:576
  78.5 2.0 %collective-permute-done.24.refs_1_ = f32[128,128]{1,0:T(8,128)S(1)} collective-permute-done((f32[128,128]{1,0:T(8,128)S(1)}, f32[128,128]{1,0:T(8,128)S(1)}, u32[]{:S(2)}, u32[]{:S(2)}) %collective-permute-start.24) | collective-permute-done | bytes 65568 | tf_op jit(solution)/shard_map/ppermute | solution.py:576
  80.5 2.1 %collective-permute-done.25.refs_2_ = f32[128,128]{1,0:T(8,128)S(1)} collective-permute-done((f32[128,128]{1,0:T(8,128)S(1)}, f32[128,128]{1,0:T(8,128)S(1)}, u32[]{:S(2)}, u32[]{:S(2)}) %collective-permute-start.25) | collective-permute-done | bytes 65568 | tf_op jit(solution)/shard_map/ppermute | solution.py:576
  82.8 0.8 collective-permute-start.29
  83.6 2.0 %collective-permute-start.28 = (f32[128,128]{1,0:T(8,128)S(1)}, f32[128,128]{1,0:T(8,128)S(1)}, u32[]{:S(2)}, u32[]{:S(2)}) collective-permute-start(f32[128,128]{1,0:T(8,128)S(1)} %scale.3.refs_1_), channel_id=1, source_target_pairs={{0,24},{4,28},{8,16},{12,20},{16,8},{20,12},{24,0},{28,4},{1,25},{... | collective-permute-start | bytes 196616 | tf_op jit(solution)/shard_map/ppermute | solution.py:582
  85.6 0.8 collective-permute-start.33
  86.4 1.0 %join.1 = f32[8,96,256]{2,1,0:T(8,128)} custom-call(f32[8,96,128]{2,1,0:T(8,128)S(1)} %get-tuple-element.80.own.refs_0_, f32[4,96,128]{2,1,0:T(8,128)S(1)} %collective-permute-done.27.front.refs_0_, f32[4,96,128]{2,1,0:T(8,128)S(1)} %collective-permute-done.30.back.refs_1_), custom_call_target="tpu_custom_call" | custom-call | flops 1000000 | bytes 2000000 | tf_op jit(solution)/shard_map/join/pallas_call | solution.py:525
  88.0 0.7 first_half.4.base
  88.8 1.1 %collective-permute-done.33.refs_2_ = f32[128,128]{1,0:T(8,128)S(1)} collective-permute-done((f32[128,128]{1,0:T(8,128)S(1)}, f32[128,128]{1,0:T(8,128)S(1)}, u32[]{:S(2)}, u32[]{:S(2)}) %collective-permute-start.33) | collective-permute-done | bytes 65568 | tf_op jit(solution)/shard_map/ppermute | solution.py:576
  89.9 0.7 first_half.5.other
  90.5 0.7 second_half.3.own
  91.2 1.5 %final.1 = f32[8,96,256]{2,1,0:T(8,128)} custom-call(f32[8,96,128]{2,1,0:T(8,128)S(1)} %second_half.3.own, f32[8,96,128]{2,1,0:T(8,128)S(1)} %first_half.5.other, bf16[8,2,192,512]{3,2,1,0:T(8,128)(2,1)S(1)} %get-tuple-element.46.vectors, f32[128,128]{1,0:T(8,128)S(1)} %collective-permute-done.34.refs_0_, f32[128,128]{1,0:T(8,128)S(1)} %collective-permute-done.35.refs_1_), custom_call_target="tpu_custom_call" | custom-call | flops 1000000000 | bytes 4000000 | tf_op jit(solution)/shard_map/final/pallas_call | solution.py:553
  (54 shorter events, 5.9 us)
Async XLA Ops:
  0.6 1.1 %copy-start = (f32[1,1,2,4,96,256]{5,4,3,2,1,0:T(8,128)S(1)}, f32[1,1,2,4,96,256]{5,4,3,2,1,0:T(8,128)}, u32[]{:S(2)}) copy-start(f32[1,1,2,4,96,256]{5,4,3,2,1,0:T(8,128)} %param.7) | copy-start | bytes 2359300
  2.0 6.4 %collective-permute-start = (f32[8,96,128]{2,1,0:T(8,128)S(1)}, f32[8,96,128]{2,1,0:T(8,128)S(1)}, u32[]{:S(2)}, u32[]{:S(2)}) collective-permute-start(f32[8,96,128]{2,1,0:T(8,128)S(1)} %get-tuple-element.45.x_ref.x), channel_id=1, source_target_pairs={{0,4},{4,0},{8,12},{12,8},{1,5},{5,1},{9,13},{13,9},{2,6},{6,2},{1... | collective-permute-start | bytes 1179656 | tf_op jit(solution)/shard_map/ppermute | solution.py:576
  2.6 18.8 %collective-permute-start.2 = (f32[4,96,128]{2,1,0:T(8,128)S(1)}, f32[4,96,128]{2,1,0:T(8,128)S(1)}, u32[]{:S(2)}, u32[]{:S(2)}) collective-permute-start(f32[4,96,128]{2,1,0:T(8,128)S(1)} %get-tuple-element.50), channel_id=1, source_target_pairs={{0,1},{1,2},{2,3},{3,0},{4,5},{5,6},{6,7},{7,4},{8,9},{9,10},{10,1... | collective-permute-start | bytes 589832 | tf_op jit(solution)/shard_map/ppermute | solution.py:571
  5.2 16.2 %collective-permute-start.3 = (f32[4,96,128]{2,1,0:T(8,128)S(1)}, f32[4,96,128]{2,1,0:T(8,128)S(1)}, u32[]{:S(2)}, u32[]{:S(2)}) collective-permute-start(f32[4,96,128]{2,1,0:T(8,128)S(1)} %get-tuple-element.50), channel_id=1, source_target_pairs={{0,3},{1,0},{2,1},{3,2},{4,7},{5,4},{6,5},{7,6},{8,11},{9,8},{10,9... | collective-permute-start | bytes 589832 | tf_op jit(solution)/shard_map/ppermute | solution.py:571
  7.3 14.6 %collective-permute-start.1 = (f32[8,96,128]{2,1,0:T(8,128)S(1)}, f32[8,96,128]{2,1,0:T(8,128)S(1)}, u32[]{:S(2)}, u32[]{:S(2)}) collective-permute-start(f32[8,96,128]{2,1,0:T(8,128)S(1)} %get-tuple-element.45.x_ref.x), channel_id=1, source_target_pairs={{0,12},{4,8},{8,4},{12,0},{1,13},{5,9},{9,5},{13,1},{2,14},{6,10},... | collective-permute-start | bytes 1179656 | tf_op jit(solution)/shard_map/ppermute | solution.py:589
  8.5 14.5 %collective-permute-start.4 = (f32[4,96,128]{2,1,0:T(8,128)S(1)}, f32[4,96,128]{2,1,0:T(8,128)S(1)}, u32[]{:S(2)}, u32[]{:S(2)}) collective-permute-start(f32[4,96,128]{2,1,0:T(8,128)S(1)} %get-tuple-element.56), channel_id=1, source_target_pairs={{0,1},{1,2},{2,3},{3,0},{4,5},{5,6},{6,7},{7,4},{8,9},{9,10},{10,1... | collective-permute-start | bytes 589832 | tf_op jit(solution)/shard_map/ppermute | solution.py:571
  8.5 16.3 %collective-permute-start.5 = (f32[4,96,128]{2,1,0:T(8,128)S(1)}, f32[4,96,128]{2,1,0:T(8,128)S(1)}, u32[]{:S(2)}, u32[]{:S(2)}) collective-permute-start(f32[4,96,128]{2,1,0:T(8,128)S(1)} %get-tuple-element.56), channel_id=1, source_target_pairs={{0,3},{1,0},{2,1},{3,2},{4,7},{5,4},{6,5},{7,6},{8,11},{9,8},{10,9... | collective-permute-start | bytes 589832 | tf_op jit(solution)/shard_map/ppermute | solution.py:571
  24.8 6.8 %copy-start.1 = (f32[2,512]{1,0:T(2,128)S(1)}, f32[2,512]{1,0:T(2,128)}, u32[]{:S(2)}) copy-start(f32[2,512]{1,0:T(2,128)} %inverse.1) | copy-start | bytes 12292
  25.8 1.3 %collective-permute-start.6 = (f32[256,128]{1,0:T(8,128)S(1)}, f32[256,128]{1,0:T(8,128)S(1)}, u32[]{:S(2)}, u32[]{:S(2)}) collective-permute-start(f32[256,128]{1,0:T(8,128)S(1)} %get-tuple-element.59), channel_id=1, source_target_pairs={{0,4},{4,0},{8,12},{12,8},{1,5},{5,1},{9,13},{13,9},{2,6},{6,2},{1... | collective-permute-start | bytes 393224 | tf_op jit(solution)/shard_map/ppermute | solution.py:576
  27.2 9.4 %collective-permute-start.7 = (f32[128,128]{1,0:T(8,128)S(1)}, f32[128,128]{1,0:T(8,128)S(1)}, u32[]{:S(2)}, u32[]{:S(2)}) collective-permute-start(f32[128,128]{1,0:T(8,128)S(1)} %get-tuple-element.61), channel_id=1, source_target_pairs={{0,10},{1,11},{2,8},{3,9},{4,14},{5,15},{6,12},{7,13},{8,2},{9,3},... | collective-permute-start | bytes 196616 | tf_op jit(solution)/shard_map/ppermute | solution.py:582
  29.4 8.0 %collective-permute-start.8 = (f32[128,128]{1,0:T(8,128)S(1)}, f32[128,128]{1,0:T(8,128)S(1)}, u32[]{:S(2)}, u32[]{:S(2)}) collective-permute-start(f32[128,128]{1,0:T(8,128)S(1)} %get-tuple-element.60.refs_0_), channel_id=1, source_target_pairs={{0,2},{1,3},{2,0},{3,1},{4,6},{5,7},{6,4},{7,5},{8,10},{9,11},{10,... | collective-permute-start | bytes 196616 | tf_op jit(solution)/shard_map/ppermute | solution.py:576
  31.1 6.3 %collective-permute-start.9 = (f32[128,128]{1,0:T(8,128)S(1)}, f32[128,128]{1,0:T(8,128)S(1)}, u32[]{:S(2)}, u32[]{:S(2)}) collective-permute-start(f32[128,128]{1,0:T(8,128)S(1)} %get-tuple-element.61), channel_id=1, source_target_pairs={{0,8},{4,12},{8,0},{12,4},{1,9},{5,13},{9,1},{13,5},{2,10},{6,14},... | collective-permute-start | bytes 196616 | tf_op jit(solution)/shard_map/ppermute | solution.py:576
  37.5 5.2 %collective-permute-start.11 = (f32[128,128]{1,0:T(8,128)S(1)}, f32[128,128]{1,0:T(8,128)S(1)}, u32[]{:S(2)}, u32[]{:S(2)}) collective-permute-start(f32[128,128]{1,0:T(8,128)S(1)} %scale.2.left), channel_id=1, source_target_pairs={{0,9},{1,8},{2,11},{3,10},{4,13},{5,12},{6,15},{7,14},{8,1},{9,0},... | collective-permute-start | bytes 196616 | tf_op jit(solution)/shard_map/ppermute | solution.py:582
  37.6 5.2 %collective-permute-start.12 = (f32[128,128]{1,0:T(8,128)S(1)}, f32[128,128]{1,0:T(8,128)S(1)}, u32[]{:S(2)}, u32[]{:S(2)}) collective-permute-start(f32[128,128]{1,0:T(8,128)S(1)} %scale.2.left), channel_id=1, source_target_pairs={{0,8},{4,12},{8,0},{12,4},{1,9},{5,13},{9,1},{13,5},{2,10},{6,14},... | collective-permute-start | bytes 196616 | tf_op jit(solution)/shard_map/ppermute | solution.py:576
  38.4 5.0 %collective-permute-start.10 = (f32[128,128]{1,0:T(8,128)S(1)}, f32[128,128]{1,0:T(8,128)S(1)}, u32[]{:S(2)}, u32[]{:S(2)}) collective-permute-start(f32[128,128]{1,0:T(8,128)S(1)} %scale.2.left), channel_id=1, source_target_pairs={{0,1},{1,0},{2,3},{3,2},{4,5},{5,4},{6,7},{7,6},{8,9},{9,8},{10,11... | collective-permute-start | bytes 196616 | tf_op jit(solution)/shard_map/ppermute | solution.py:576
  42.8 1.3 %collective-permute-start.14 = (f32[128,128]{1,0:T(8,128)S(1)}, f32[128,128]{1,0:T(8,128)S(1)}, u32[]{:S(2)}, u32[]{:S(2)}) collective-permute-start(f32[128,128]{1,0:T(8,128)S(1)} %add.4.refs_2_), channel_id=1, source_target_pairs={{0,4},{4,0},{8,12},{12,8},{1,5},{5,1},{9,13},{13,9},{2,6},{6,2},{1... | collective-permute-start | bytes 196616 | tf_op jit(solution)/shard_map/ppermute | solution.py:576
  43.4 1.3 %collective-permute-start.13 = (f32[128,128]{1,0:T(8,128)S(1)}, f32[128,128]{1,0:T(8,128)S(1)}, u32[]{:S(2)}, u32[]{:S(2)}) collective-permute-start(f32[128,128]{1,0:T(8,128)S(1)} %add.3.refs_1_), channel_id=1, source_target_pairs={{0,4},{4,0},{8,12},{12,8},{1,5},{5,1},{9,13},{13,9},{2,6},{6,2},{1... | collective-permute-start | bytes 196616 | tf_op jit(solution)/shard_map/ppermute | solution.py:576
  45.4 4.2 %collective-permute-start.15 = (f32[8,96,128]{2,1,0:T(8,128)S(1)}, f32[8,96,128]{2,1,0:T(8,128)S(1)}, u32[]{:S(2)}, u32[]{:S(2)}) collective-permute-start(f32[8,96,128]{2,1,0:T(8,128)S(1)} %get-tuple-element.77.x_ref.x), channel_id=1, source_target_pairs={{0,4},{4,0},{8,12},{12,8},{1,5},{5,1},{9,13},{13,9},{2,6},{6,2},{1... | collective-permute-start | bytes 1179656 | tf_op jit(solution)/shard_map/ppermute | solution.py:576
  45.6 9.6 %collective-permute-start.17 = (f32[4,96,128]{2,1,0:T(8,128)S(1)}, f32[4,96,128]{2,1,0:T(8,128)S(1)}, u32[]{:S(2)}, u32[]{:S(2)}) collective-permute-start(f32[4,96,128]{2,1,0:T(8,128)S(1)} %get-tuple-element.68), channel_id=1, source_target_pairs={{0,1},{1,2},{2,3},{3,0},{4,5},{5,6},{6,7},{7,4},{8,9},{9,10},{10,1... | collective-permute-start | bytes 589832 | tf_op jit(solution)/shard_map/ppermute | solution.py:571
  47.6 11.8 %collective-permute-start.18 = (f32[4,96,128]{2,1,0:T(8,128)S(1)}, f32[4,96,128]{2,1,0:T(8,128)S(1)}, u32[]{:S(2)}, u32[]{:S(2)}) collective-permute-start(f32[4,96,128]{2,1,0:T(8,128)S(1)} %get-tuple-element.68), channel_id=1, source_target_pairs={{0,3},{1,0},{2,1},{3,2},{4,7},{5,4},{6,5},{7,6},{8,11},{9,8},{10,9... | collective-permute-start | bytes 589832 | tf_op jit(solution)/shard_map/ppermute | solution.py:571
  49.4 11.4 %collective-permute-start.16 = (f32[8,96,128]{2,1,0:T(8,128)S(1)}, f32[8,96,128]{2,1,0:T(8,128)S(1)}, u32[]{:S(2)}, u32[]{:S(2)}) collective-permute-start(f32[8,96,128]{2,1,0:T(8,128)S(1)} %get-tuple-element.77.x_ref.x), channel_id=1, source_target_pairs={{0,12},{4,8},{8,4},{12,0},{1,13},{5,9},{9,5},{13,1},{2,14},{6,10},... | collective-permute-start | bytes 1179656 | tf_op jit(solution)/shard_map/ppermute | solution.py:589
  49.5 14.1 %collective-permute-start.19 = (f32[4,96,128]{2,1,0:T(8,128)S(1)}, f32[4,96,128]{2,1,0:T(8,128)S(1)}, u32[]{:S(2)}, u32[]{:S(2)}) collective-permute-start(f32[4,96,128]{2,1,0:T(8,128)S(1)} %get-tuple-element.72), channel_id=1, source_target_pairs={{0,1},{1,2},{2,3},{3,0},{4,5},{5,6},{6,7},{7,4},{8,9},{9,10},{10,1... | collective-permute-start | bytes 589832 | tf_op jit(solution)/shard_map/ppermute | solution.py:571
  49.7 17.4 %collective-permute-start.20 = (f32[4,96,128]{2,1,0:T(8,128)S(1)}, f32[4,96,128]{2,1,0:T(8,128)S(1)}, u32[]{:S(2)}, u32[]{:S(2)}) collective-permute-start(f32[4,96,128]{2,1,0:T(8,128)S(1)} %get-tuple-element.72), channel_id=1, source_target_pairs={{0,3},{1,0},{2,1},{3,2},{4,7},{5,4},{6,5},{7,6},{8,11},{9,8},{10,9... | collective-permute-start | bytes 589832 | tf_op jit(solution)/shard_map/ppermute | solution.py:571
  55.1 18.9 %collective-permute-start.23 = (f32[8,96,128]{2,1,0:T(8,128)S(1)}, f32[8,96,128]{2,1,0:T(8,128)S(1)}, u32[]{:S(2)}, u32[]{:S(2)}) collective-permute-start(f32[8,96,128]{2,1,0:T(8,128)S(1)} %get-tuple-element.77.x_ref.x), channel_id=1, source_target_pairs={{0,16},{16,0},{1,17},{17,1},{2,18},{18,2},{3,19},{19,3},{4,20},{20... | collective-permute-start | bytes 1179656 | tf_op jit(solution)/shard_map/ppermute | solution.py:576
  68.1 1.7 %collective-permute-start.21 = (f32[256,128]{1,0:T(8,128)S(1)}, f32[256,128]{1,0:T(8,128)S(1)}, u32[]{:S(2)}, u32[]{:S(2)}) collective-permute-start(f32[256,128]{1,0:T(8,128)S(1)} %get-tuple-element.74), channel_id=1, source_target_pairs={{0,4},{4,0},{8,12},{12,8},{1,5},{5,1},{9,13},{13,9},{2,6},{6,2},{1... | collective-permute-start | bytes 393224 | tf_op jit(solution)/shard_map/ppermute | solution.py:576
  68.1 14.7 %collective-permute-start.27 = (f32[4,96,128]{2,1,0:T(8,128)S(1)}, f32[4,96,128]{2,1,0:T(8,128)S(1)}, u32[]{:S(2)}, u32[]{:S(2)}) collective-permute-start(f32[4,96,128]{2,1,0:T(8,128)S(1)} %get-tuple-element.69.front), channel_id=1, source_target_pairs={{0,16},{16,0},{1,17},{17,1},{2,18},{18,2},{3,19},{19,3},{4,20},{20... | collective-permute-start | bytes 589832 | tf_op jit(solution)/shard_map/ppermute | solution.py:576
  69.7 4.3 %collective-permute-start.22 = (f32[128,128]{1,0:T(8,128)S(1)}, f32[128,128]{1,0:T(8,128)S(1)}, u32[]{:S(2)}, u32[]{:S(2)}) collective-permute-start(f32[128,128]{1,0:T(8,128)S(1)} %get-tuple-element.76), channel_id=1, source_target_pairs={{0,8},{4,12},{8,0},{12,4},{1,9},{5,13},{9,1},{13,5},{2,10},{6,14},... | collective-permute-start | bytes 196616 | tf_op jit(solution)/shard_map/ppermute | solution.py:576
  70.5 15.9 %collective-permute-start.30 = (f32[4,96,128]{2,1,0:T(8,128)S(1)}, f32[4,96,128]{2,1,0:T(8,128)S(1)}, u32[]{:S(2)}, u32[]{:S(2)}) collective-permute-start(f32[4,96,128]{2,1,0:T(8,128)S(1)} %get-tuple-element.82), channel_id=1, source_target_pairs={{0,16},{16,0},{1,17},{17,1},{2,18},{18,2},{3,19},{19,3},{4,20},{20... | collective-permute-start | bytes 589832 | tf_op jit(solution)/shard_map/ppermute | solution.py:576
  74.1 6.4 %collective-permute-start.24 = (f32[128,128]{1,0:T(8,128)S(1)}, f32[128,128]{1,0:T(8,128)S(1)}, u32[]{:S(2)}, u32[]{:S(2)}) collective-permute-start(f32[128,128]{1,0:T(8,128)S(1)} %add.5.refs_0_), channel_id=1, source_target_pairs={{0,3},{1,2},{2,1},{3,0},{4,7},{5,6},{6,5},{7,4},{8,11},{9,10},{10,... | collective-permute-start | bytes 196616 | tf_op jit(solution)/shard_map/ppermute | solution.py:576
  76.3 6.4 %collective-permute-start.25 = (f32[128,128]{1,0:T(8,128)S(1)}, f32[128,128]{1,0:T(8,128)S(1)}, u32[]{:S(2)}, u32[]{:S(2)}) collective-permute-start(f32[128,128]{1,0:T(8,128)S(1)} %add.5.refs_0_), channel_id=1, source_target_pairs={{0,2},{1,3},{2,0},{3,1},{4,6},{5,7},{6,4},{7,5},{8,10},{9,11},{10,... | collective-permute-start | bytes 196616 | tf_op jit(solution)/shard_map/ppermute | solution.py:576
  76.3 6.4 %collective-permute-start.26 = (f32[128,128]{1,0:T(8,128)S(1)}, f32[128,128]{1,0:T(8,128)S(1)}, u32[]{:S(2)}, u32[]{:S(2)}) collective-permute-start(f32[128,128]{1,0:T(8,128)S(1)} %add.5.refs_0_), channel_id=1, source_target_pairs={{0,1},{1,0},{2,3},{3,2},{4,5},{5,4},{6,7},{7,6},{8,9},{9,8},{10,11... | collective-permute-start | bytes 196616 | tf_op jit(solution)/shard_map/ppermute | solution.py:576
  82.8 4.8 %collective-permute-start.29 = (f32[128,128]{1,0:T(8,128)S(1)}, f32[128,128]{1,0:T(8,128)S(1)}, u32[]{:S(2)}, u32[]{:S(2)}) collective-permute-start(f32[128,128]{1,0:T(8,128)S(1)} %scale.3.refs_1_), channel_id=1, source_target_pairs={{0,8},{4,12},{8,0},{12,4},{1,9},{5,13},{9,1},{13,5},{2,10},{6,14},... | collective-permute-start | bytes 196616 | tf_op jit(solution)/shard_map/ppermute | solution.py:576
  83.6 5.2 %collective-permute-start.28 = (f32[128,128]{1,0:T(8,128)S(1)}, f32[128,128]{1,0:T(8,128)S(1)}, u32[]{:S(2)}, u32[]{:S(2)}) collective-permute-start(f32[128,128]{1,0:T(8,128)S(1)} %scale.3.refs_1_), channel_id=1, source_target_pairs={{0,24},{4,28},{8,16},{12,20},{16,8},{20,12},{24,0},{28,4},{1,25},{... | collective-permute-start | bytes 196616 | tf_op jit(solution)/shard_map/ppermute | solution.py:582
  85.6 4.3 %collective-permute-start.33 = (f32[128,128]{1,0:T(8,128)S(1)}, f32[128,128]{1,0:T(8,128)S(1)}, u32[]{:S(2)}, u32[]{:S(2)}) collective-permute-start(f32[128,128]{1,0:T(8,128)S(1)} %scale.3.refs_1_), channel_id=1, source_target_pairs={{0,16},{16,0},{1,17},{17,1},{2,18},{18,2},{3,19},{19,3},{4,20},{20... | collective-permute-start | bytes 196616 | tf_op jit(solution)/shard_map/ppermute | solution.py:576
  86.4 4.2 %collective-permute-start.31 = (f32[128,128]{1,0:T(8,128)S(1)}, f32[128,128]{1,0:T(8,128)S(1)}, u32[]{:S(2)}, u32[]{:S(2)}) collective-permute-start(f32[128,128]{1,0:T(8,128)S(1)} %scale.3.refs_1_), channel_id=1, source_target_pairs={{0,4},{4,0},{8,12},{12,8},{1,5},{5,1},{9,13},{13,9},{2,6},{6,2},{1... | collective-permute-start | bytes 196616 | tf_op jit(solution)/shard_map/ppermute | solution.py:576
  87.5 3.0 %collective-permute-start.32 = (f32[128,128]{1,0:T(8,128)S(1)}, f32[128,128]{1,0:T(8,128)S(1)}, u32[]{:S(2)}, u32[]{:S(2)}) collective-permute-start(f32[128,128]{1,0:T(8,128)S(1)} %collective-permute-done.29.refs_2_), channel_id=1, source_target_pairs={{0,4},{4,0},{8,12},{12,8},{1,5},{5,1},{9,13},{13,9},{2,6},{6,2},{1... | collective-permute-start | bytes 196616 | tf_op jit(solution)/shard_map/ppermute | solution.py:576
  88.7 2.5 %collective-permute-start.35 = (f32[128,128]{1,0:T(8,128)S(1)}, f32[128,128]{1,0:T(8,128)S(1)}, u32[]{:S(2)}, u32[]{:S(2)}) collective-permute-start(f32[128,128]{1,0:T(8,128)S(1)} %collective-permute-done.28.refs_3_), channel_id=1, source_target_pairs={{0,4},{4,0},{8,12},{12,8},{1,5},{5,1},{9,13},{13,9},{2,6},{6,2},{1... | collective-permute-start | bytes 196616 | tf_op jit(solution)/shard_map/ppermute | solution.py:576
  89.9 1.4 %collective-permute-start.34 = (f32[128,128]{1,0:T(8,128)S(1)}, f32[128,128]{1,0:T(8,128)S(1)}, u32[]{:S(2)}, u32[]{:S(2)}) collective-permute-start(f32[128,128]{1,0:T(8,128)S(1)} %collective-permute-done.33.refs_2_), channel_id=1, source_target_pairs={{0,4},{4,0},{8,12},{12,8},{1,5},{5,1},{9,13},{13,9},{2,6},{6,2},{1... | collective-permute-start | bytes 196616 | tf_op jit(solution)/shard_map/ppermute | solution.py:576
